TPU v7x, 32 devices: a whole 2x2x4 slice. The times are simulated.
32 devices in a mesh: section: 2 (over x), gy: 4 (over z), gz: 4 (over y, core).
Axes of the slice: x: 2, y: 2, z: 4, core: 2. Of those that a mesh axis runs over, the one named last changes fastest.
Arguments:
- inflow: float32 [2, 64, 2, 8, 512], P(None, None, None, 'gy', 'gz'), may hold values from -6 to 6
- weights: float32 [4, 27, 64, 64], P('section'), may hold values from -0.15625 to 0.15625
- biases: float32 [4, 64], P('section'), may hold values from -3 to 3
- cotangent: float32 [2, 64, 2, 8, 512], P(None, None, None, 'gy', 'gz'), may hold values from -6 to 6
Outputs:
- section_out: float32 [2, 2, 64, 2, 8, 512], P('section', None, None, None, 'gy', 'gz')
- section_grad: float32 [2, 2, 64, 2, 8, 512], P('section', None, None, None, 'gy', 'gz')
- weight_grad: float32 [4, 27, 64, 64], P('section')
- bias_grad: float32 [4, 64], P('section')
All inputs are finite; a program needn't handle non-finite values.
Results may differ from a plain program's by a relative error of at most 0.0001.
Values sent between devices are 32-bit elements; how exact they have to be, the bound alone decides.
No kernel may reach another device: no remote copies, remote signals or barrier semaphores. Data moves between devices by JAX's collectives and lax.ppermute only.
A program may use at most 128 MiB of HBM per device.

v0:
```python
import math

import jax
import jax.numpy as jnp
from jax import lax
from jax.sharding import PartitionSpec as P


def extended(block, sides, width):
    for axis, dim in sides:
        count = lax.axis_size(axis)
        forward = [(i, i + 1) for i in range(count - 1)]
        backward = [(target, source) for source, target in forward]
        low = lax.ppermute(
            lax.slice_in_dim(block, block.shape[dim] - width, None, axis=dim), axis, forward
        )
        high = lax.ppermute(lax.slice_in_dim(block, 0, width, axis=dim), axis, backward)
        block = jnp.concatenate([low, block, high], axis=dim)
    return block


def passed_along(block, axis, distance):
    devices = range(lax.axis_size(axis))
    route = [(i - distance, i) for i in devices if i - distance in devices]
    return lax.ppermute(block, axis, route)


def stacked_taps(padded, out_sizes, flipped):
    size_x, size_y, size_z = out_sizes
    pieces = []
    for offset in range(27):
        start_x, start_y, start_z = (offset // 9, offset // 3 % 3, offset % 3)
        if flipped:
            start_x, start_y, start_z = (2 - start_x, 2 - start_y, 2 - start_z)
        pieces.append(
            padded[
                :,
                start_x : start_x + size_x,
                start_y : start_y + size_y,
                start_z : start_z + size_z,
            ]
        )
    return jnp.stack(pieces)


def convolve(weight, padded, out_sizes):
    return jnp.einsum(
        "toc,tcxyz->oxyz",
        weight,
        stacked_taps(padded, out_sizes, False),
        precision=lax.Precision.HIGHEST,
    )


def face_rim(values):
    rimmed = extended(values, (("gy", 2), ("gz", 3)), 1)
    return jnp.pad(rimmed, ((0, 0), (1, 1), (0, 0), (0, 0)))


def slope_rim(values):
    rimmed = extended(values, (("gy", 2), ("gz", 3)), 1)
    return jnp.pad(rimmed, ((0, 0), (1, 1), (0, 0), (0, 0)))


def section_forward(weights, biases, current, extents):
    stored = []
    for layer_index in range(weights.shape[0]):
        padded = face_rim(current)
        pre_act = (
            convolve(weights[layer_index], padded, extents)
            + biases[layer_index][:, None, None, None]
        )
        stored.append((padded, pre_act))
        current = jax.nn.silu(pre_act)
    return (stored, current)


def per_device(inflow, weights, biases, cotangent):
    highest = lax.Precision.HIGHEST
    first_section = lax.axis_index("section") == 0
    micro_count = inflow.shape[0]
    layer_count = weights.shape[0]
    extents = inflow.shape[2:]
    blank = jnp.zeros(inflow.shape[1:], jnp.float32)
    received = blank
    stored_all = []
    produced = []
    for step_index in range(micro_count + 1):
        own_input = inflow[step_index] if step_index < micro_count else blank
        current = jnp.where(first_section, own_input, received)
        stored, current = section_forward(weights, biases, current, extents)
        stored_all.append(stored)
        produced.append(current)
        if step_index < micro_count:
            received = passed_along(current, "section", 1)
    section_out = jnp.stack(
        [
            jnp.where(first_section, produced[micro], produced[micro + 1])
            for micro in range(micro_count)
        ]
    )
    cell_count = (
        micro_count
        * extents[0]
        * extents[1]
        * lax.axis_size("gy")
        * extents[2]
        * lax.axis_size("gz")
    )
    grad_scale = 1.0 / math.sqrt(cell_count)
    weight_grads = [jnp.zeros(weights.shape[1:], jnp.float32) for layer_index in range(layer_count)]
    bias_grads = [jnp.zeros(biases.shape[1:], jnp.float32) for layer_index in range(layer_count)]
    returned = blank
    collected = []
    for step_index in range(micro_count + 1):
        later = micro_count - 1 - step_index
        own_grad = cotangent[later] if later >= 0 else blank
        gradient = jnp.where(first_section, returned, own_grad)
        stored = stored_all[micro_count - step_index]
        for layer_index in reversed(range(layer_count)):
            padded, pre_act = stored[layer_index]
            sigmoid_value = jax.nn.sigmoid(pre_act)
            slope_grad = gradient * sigmoid_value * (1.0 + pre_act * (1.0 - sigmoid_value))
            weight_grads[layer_index] = weight_grads[layer_index] + jnp.einsum(
                "oxyz,tcxyz->toc",
                slope_grad,
                stacked_taps(padded, extents, False),
                precision=highest,
            )
            bias_grads[layer_index] = bias_grads[layer_index] + jnp.sum(slope_grad, axis=(1, 2, 3))
            gradient = jnp.einsum(
                "toc,toxyz->cxyz",
                weights[layer_index],
                stacked_taps(slope_rim(slope_grad), extents, True),
                precision=highest,
            )
        collected.append(gradient)
        if step_index < micro_count:
            returned = passed_along(gradient, "section", -1)
    section_grad = jnp.stack(
        [
            jnp.where(
                first_section, collected[micro_count - micro], collected[micro_count - 1 - micro]
            )
            for micro in range(micro_count)
        ]
    )
    weight_total, bias_total = lax.psum(
        (jnp.stack(weight_grads) * grad_scale, jnp.stack(bias_grads) * grad_scale), ("gy", "gz")
    )
    return (section_out[None], section_grad[None], weight_total, bias_total)


def solution(mesh):
    return jax.shard_map(
        per_device,
        mesh=mesh,
        in_specs=(
            P(None, None, None, "gy", "gz"),
            P("section", None, None, None),
            P("section", None),
            P(None, None, None, "gy", "gz"),
        ),
        out_specs=(
            P("section", None, None, None, "gy", "gz"),
            P("section", None, None, None, "gy", "gz"),
            P("section", None, None, None),
            P("section", None),
        ),
        check_vma=False,
    )
```

profile of v0, /device:TPU:0, one launch (start us, length us, event | category | flops | bytes accessed | tf_op | source)
XLA Modules:
  0.0 402.8 jit_solution(9476542956862868853)
XLA Ops:
  8.3 4.9 %collective-permute-start = (f32[64,2,1,128]{3,0,2,1:T(8,128)S(1)}, f32[64,2,1,128]{3,0,2,1:T(8,128)S(1)}, u32[]{:S(2)}, u32[]{:S(2)}) collective-permute-start(f32[64,2,1,128]{3,0,2,1:T(8,128)S(1)} %get-tuple-element.75), channel_id=1, source_target_pairs={{0,4},{4,8},{8,12},{1,5},{5,9},{9,13},{2,6},{6,10},{10,14},{3,7},{... | collective-permute-start | bytes 196616 | tf_op jit(solution)/shard_map/ppermute | solution.py:14
  15.1 4.3 %collective-permute-done.1 = f32[64,2,1,128]{3,0,2,1:T(8,128)S(1)} collective-permute-done((f32[64,2,1,128]{3,0,2,1:T(8,128)S(1)}, f32[64,2,1,128]{3,0,2,1:T(8,128)S(1)}, u32[]{:S(2)}, u32[]{:S(2)}) %collective-permute-start.1) | collective-permute-done | bytes 65568 | tf_op jit(solution)/shard_map/ppermute | solution.py:17
  22.9 3.1 collective-permute-done.3
  28.4 2.5 fusion.143
  31.0 3.5 collective-permute-start.4
  36.3 4.3 %collective-permute-done.5 = f32[64,2,1,128]{3,0,2,1:T(8,128)S(1)} collective-permute-done((f32[64,2,1,128]{3,0,2,1:T(8,128)S(1)}, f32[64,2,1,128]{3,0,2,1:T(8,128)S(1)}, u32[]{:S(2)}, u32[]{:S(2)}) %collective-permute-start.5) | collective-permute-done | bytes 65568 | tf_op jit(solution)/shard_map/ppermute | solution.py:17
  40.8 5.3 %collective-permute-start.6 = (f32[64,2,4,1]{3,0,2,1:T(8,128)S(1)}, f32[64,2,4,1]{3,0,2,1:T(8,128)S(1)}, u32[]{:S(2)}, u32[]{:S(2)}) collective-permute-start(f32[64,2,4,1]{3,0,2,1:T(8,128)S(1)} %get-tuple-element.46), channel_id=1, source_target_pairs={{0,1},{1,2},{2,3},{4,5},{5,6},{6,7},{8,9},{9,10},{10,11},{12,13},{... | collective-permute-start | bytes 6152 | tf_op jit(solution)/shard_map/ppermute | solution.py:14
  47.3 2.9 collective-permute-done.7
  52.7 2.5 fusion.20
  55.3 3.4 collective-permute-start.8
  58.7 2.5 collective-permute-done.8
  61.2 3.5 collective-permute-start.9
  66.6 4.3 %collective-permute-done.10 = f32[64,2,1,128]{3,0,2,1:T(8,128)S(1)} collective-permute-done((f32[64,2,1,128]{3,0,2,1:T(8,128)S(1)}, f32[64,2,1,128]{3,0,2,1:T(8,128)S(1)}, u32[]{:S(2)}, u32[]{:S(2)}) %collective-permute-start.10) | collective-permute-done | bytes 65568 | tf_op jit(solution)/shard_map/ppermute | solution.py:17
  71.0 4.4 %collective-permute-start.11 = (f32[64,2,4,1]{3,0,2,1:T(8,128)S(1)}, f32[64,2,4,1]{3,0,2,1:T(8,128)S(1)}, u32[]{:S(2)}, u32[]{:S(2)}) collective-permute-start(f32[64,2,4,1]{3,0,2,1:T(8,128)S(1)} %get-tuple-element.42), channel_id=1, source_target_pairs={{0,1},{1,2},{2,3},{4,5},{5,6},{6,7},{8,9},{9,10},{10,11},{12,13},{... | collective-permute-start | bytes 6152 | tf_op jit(solution)/shard_map/ppermute | solution.py:14
  77.0 3.5 collective-permute-done.12
  82.9 2.5 fusion.18
  89.3 4.3 %collective-permute-done.14 = f32[64,2,1,128]{3,0,2,1:T(8,128)S(1)} collective-permute-done((f32[64,2,1,128]{3,0,2,1:T(8,128)S(1)}, f32[64,2,1,128]{3,0,2,1:T(8,128)S(1)}, u32[]{:S(2)}, u32[]{:S(2)}) %collective-permute-start.14) | collective-permute-done | bytes 65568 | tf_op jit(solution)/shard_map/ppermute | solution.py:17
  93.8 5.2 %collective-permute-start.15 = (f32[64,2,4,1]{3,0,2,1:T(8,128)S(1)}, f32[64,2,4,1]{3,0,2,1:T(8,128)S(1)}, u32[]{:S(2)}, u32[]{:S(2)}) collective-permute-start(f32[64,2,4,1]{3,0,2,1:T(8,128)S(1)} %get-tuple-element.40), channel_id=1, source_target_pairs={{0,1},{1,2},{2,3},{4,5},{5,6},{6,7},{8,9},{9,10},{10,11},{12,13},{... | collective-permute-start | bytes 6152 | tf_op jit(solution)/shard_map/ppermute | solution.py:14
  100.3 2.9 collective-permute-done.16
  105.7 2.5 fusion.16
  108.4 4.4 %collective-permute-start.17 = (f32[64,2,2,128]{3,0,2,1:T(8,128)S(1)}, f32[64,2,2,128]{3,0,2,1:T(8,128)S(1)}, u32[]{:S(2)}, u32[]{:S(2)}) collective-permute-start(f32[64,2,2,128]{3,0,2,1:T(8,128)S(1)} %get-tuple-element.21), channel_id=1, source_target_pairs={{0,16},{1,17},{2,18},{3,19},{4,20},{5,21},{6,22},{7,23},{8,24},{9,... | collective-permute-start | bytes 393224 | tf_op jit(solution)/shard_map/ppermute | solution.py:25
  112.7 2.5 collective-permute-done.17
  119.1 4.3 %collective-permute-done.19 = f32[64,2,1,128]{3,0,2,1:T(8,128)S(1)} collective-permute-done((f32[64,2,1,128]{3,0,2,1:T(8,128)S(1)}, f32[64,2,1,128]{3,0,2,1:T(8,128)S(1)}, u32[]{:S(2)}, u32[]{:S(2)}) %collective-permute-start.19) | collective-permute-done | bytes 65568 | tf_op jit(solution)/shard_map/ppermute | solution.py:17
  123.5 4.4 %collective-permute-start.20 = (f32[64,2,4,1]{3,0,2,1:T(8,128)S(1)}, f32[64,2,4,1]{3,0,2,1:T(8,128)S(1)}, u32[]{:S(2)}, u32[]{:S(2)}) collective-permute-start(f32[64,2,4,1]{3,0,2,1:T(8,128)S(1)} %get-tuple-element.38), channel_id=1, source_target_pairs={{0,1},{1,2},{2,3},{4,5},{5,6},{6,7},{8,9},{9,10},{10,11},{12,13},{... | collective-permute-start | bytes 6152 | tf_op jit(solution)/shard_map/ppermute | solution.py:14
  129.2 3.7 collective-permute-done.21
  135.4 2.5 fusion.14
  141.8 4.3 %collective-permute-done.23 = f32[64,2,1,128]{3,0,2,1:T(8,128)S(1)} collective-permute-done((f32[64,2,1,128]{3,0,2,1:T(8,128)S(1)}, f32[64,2,1,128]{3,0,2,1:T(8,128)S(1)}, u32[]{:S(2)}, u32[]{:S(2)}) %collective-permute-start.23) | collective-permute-done | bytes 65568 | tf_op jit(solution)/shard_map/ppermute | solution.py:17
  146.2 5.2 %collective-permute-start.24 = (f32[64,2,4,1]{3,0,2,1:T(8,128)S(1)}, f32[64,2,4,1]{3,0,2,1:T(8,128)S(1)}, u32[]{:S(2)}, u32[]{:S(2)}) collective-permute-start(f32[64,2,4,1]{3,0,2,1:T(8,128)S(1)} %get-tuple-element.36), channel_id=1, source_target_pairs={{0,1},{1,2},{2,3},{4,5},{5,6},{6,7},{8,9},{9,10},{10,11},{12,13},{... | collective-permute-start | bytes 6152 | tf_op jit(solution)/shard_map/ppermute | solution.py:14
  153.3 2.4 collective-permute-done.25
  158.2 2.5 fusion.12
  164.7 4.3 %collective-permute-done.27 = f32[64,2,1,128]{3,0,2,1:T(8,128)S(1)} collective-permute-done((f32[64,2,1,128]{3,0,2,1:T(8,128)S(1)}, f32[64,2,1,128]{3,0,2,1:T(8,128)S(1)}, u32[]{:S(2)}, u32[]{:S(2)}) %collective-permute-start.27) | collective-permute-done | bytes 65568 | tf_op jit(solution)/shard_map/ppermute | solution.py:17
  169.2 5.2 %collective-permute-start.28 = (f32[64,2,4,1]{3,0,2,1:T(8,128)S(1)}, f32[64,2,4,1]{3,0,2,1:T(8,128)S(1)}, u32[]{:S(2)}, u32[]{:S(2)}) collective-permute-start(f32[64,2,4,1]{3,0,2,1:T(8,128)S(1)} %get-tuple-element.34), channel_id=1, source_target_pairs={{0,1},{1,2},{2,3},{4,5},{5,6},{6,7},{8,9},{9,10},{10,11},{12,13},{... | collective-permute-start | bytes 6152 | tf_op jit(solution)/shard_map/ppermute | solution.py:14
  175.7 2.9 collective-permute-done.29
  181.0 2.2 fusion.10
  187.3 4.3 %collective-permute-done.31 = f32[64,2,1,128]{3,0,2,1:T(8,128)S(1)} collective-permute-done((f32[64,2,1,128]{3,0,2,1:T(8,128)S(1)}, f32[64,2,1,128]{3,0,2,1:T(8,128)S(1)}, u32[]{:S(2)}, u32[]{:S(2)}) %collective-permute-start.31) | collective-permute-done | bytes 65568 | tf_op jit(solution)/shard_map/ppermute | solution.py:17
  191.7 5.3 %collective-permute-start.32 = (f32[64,2,4,1]{3,0,2,1:T(8,128)S(1)}, f32[64,2,4,1]{3,0,2,1:T(8,128)S(1)}, u32[]{:S(2)}, u32[]{:S(2)}) collective-permute-start(f32[64,2,4,1]{3,0,2,1:T(8,128)S(1)} %get-tuple-element.32), channel_id=1, source_target_pairs={{0,1},{1,2},{2,3},{4,5},{5,6},{6,7},{8,9},{9,10},{10,11},{12,13},{... | collective-permute-start | bytes 6152 | tf_op jit(solution)/shard_map/ppermute | solution.py:14
  198.3 2.9 collective-permute-done.33
  203.6 2.2 fusion.8
  207.1 5.6 %collective-permute-done.34 = f32[64,2,2,128]{3,0,2,1:T(8,128)S(1)} collective-permute-done((f32[64,2,2,128]{3,0,2,1:T(8,128)S(1)}, f32[64,2,2,128]{3,0,2,1:T(8,128)S(1)}, u32[]{:S(2)}, u32[]{:S(2)}) %collective-permute-start.34) | collective-permute-done | bytes 131104 | tf_op jit(solution)/shard_map/ppermute | solution.py:25
  216.7 4.3 %collective-permute-done.36 = f32[64,2,1,128]{3,0,2,1:T(8,128)S(1)} collective-permute-done((f32[64,2,1,128]{3,0,2,1:T(8,128)S(1)}, f32[64,2,1,128]{3,0,2,1:T(8,128)S(1)}, u32[]{:S(2)}, u32[]{:S(2)}) %collective-permute-start.36) | collective-permute-done | bytes 65568 | tf_op jit(solution)/shard_map/ppermute | solution.py:17
  221.2 4.2 %collective-permute-start.37 = (f32[64,2,4,1]{3,0,2,1:T(8,128)S(1)}, f32[64,2,4,1]{3,0,2,1:T(8,128)S(1)}, u32[]{:S(2)}, u32[]{:S(2)}) collective-permute-start(f32[64,2,4,1]{3,0,2,1:T(8,128)S(1)} %get-tuple-element.28), channel_id=1, source_target_pairs={{0,1},{1,2},{2,3},{4,5},{5,6},{6,7},{8,9},{9,10},{10,11},{12,13},{... | collective-permute-start | bytes 6152 | tf_op jit(solution)/shard_map/ppermute | solution.py:14
  226.8 3.0 convolution_bitcast_fusion.2
  233.0 2.2 fusion.6
  235.5 1.9 collective-permute-start.39
  239.7 3.9 collective-permute-done.40
  243.7 5.2 %collective-permute-start.41 = (f32[64,2,4,1]{3,0,2,1:T(8,128)S(1)}, f32[64,2,4,1]{3,0,2,1:T(8,128)S(1)}, u32[]{:S(2)}, u32[]{:S(2)}) collective-permute-start(f32[64,2,4,1]{3,0,2,1:T(8,128)S(1)} %get-tuple-element.26), channel_id=1, source_target_pairs={{0,1},{1,2},{2,3},{4,5},{5,6},{6,7},{8,9},{9,10},{10,11},{12,13},{... | collective-permute-start | bytes 6152 | tf_op jit(solution)/shard_map/ppermute | solution.py:14
  250.3 3.0 convolution_bitcast_fusion.3
  255.7 2.2 fusion.4
  259.5 3.0 fusion.24
  262.5 2.3 collective-permute-done.43
  265.0 3.0 convolution_bitcast_fusion
  268.0 2.2 collective-permute-start.44
  271.5 3.0 fusion.27
  276.6 3.7 collective-permute-start.46
  281.8 3.8 collective-permute-done.47
  288.0 2.2 fusion.2
  290.4 3.0 fusion.23
  294.9 2.7 collective-permute-start.48
  299.5 5.0 %collective-permute-done.49 = f32[64,2,1,128]{3,0,2,1:T(8,128)S(1)} collective-permute-done((f32[64,2,1,128]{3,0,2,1:T(8,128)S(1)}, f32[64,2,1,128]{3,0,2,1:T(8,128)S(1)}, u32[]{:S(2)}, u32[]{:S(2)}) %collective-permute-start.49) | collective-permute-done | bytes 65568 | tf_op jit(solution)/shard_map/ppermute | solution.py:17
  304.7 5.6 %collective-permute-start.50 = (f32[64,2,4,1]{3,0,2,1:T(8,128)S(1)}, f32[64,2,4,1]{3,0,2,1:T(8,128)S(1)}, u32[]{:S(2)}, u32[]{:S(2)}) collective-permute-start(f32[64,2,4,1]{3,0,2,1:T(8,128)S(1)} %get-tuple-element.22), channel_id=1, source_target_pairs={{0,1},{1,2},{2,3},{4,5},{5,6},{6,7},{8,9},{9,10},{10,11},{12,13},{... | collective-permute-start | bytes 6152 | tf_op jit(solution)/shard_map/ppermute | solution.py:14
  311.6 31.5 %psum.15 = f32[2,64]{1,0:T(2,128)} all-reduce(f32[2,64]{1,0:T(2,128)S(1)} %maximum_multiply_fusion.1), channel_id=1, replica_groups=mesh['section'=2,'gy'=4,'gz'=4] {'gy','gz'}, use_global_device_ids=true, to_apply=%region_7.8 | all-reduce | flops 128 | bytes 1024 | tf_op jit(solution)/shard_map/psum | solution.py:148
  345.5 2.2 fusion
  348.7 44.1 %all-reduce.14.cloned.1.call-done = f32[2,27,64,64]{2,3,1,0:T(8,128)} async-done(((f32[2,27,64,64]{2,3,1,0:T(8,128)}), f32[2,27,64,64]{2,3,1,0:T(8,128)}) %all-reduce.14.cloned.1.call-update) | async-done | bytes 884752 | tf_op jit(solution)/shard_map/psum | solution.py:148
  392.8 2.7 copy.58
  (466 shorter events, 91.9 us)
Async XLA Ops:
  7.2 385.6 %all-reduce.14.cloned.1.call-start = ((), (), s32[]{:S(2)}) async-start(), calls=%async_computation | async-start | bytes 3538944 | tf_op jit(solution)/shard_map/psum | solution.py:148
  8.3 6.8 %collective-permute-start = (f32[64,2,1,128]{3,0,2,1:T(8,128)S(1)}, f32[64,2,1,128]{3,0,2,1:T(8,128)S(1)}, u32[]{:S(2)}, u32[]{:S(2)}) collective-permute-start(f32[64,2,1,128]{3,0,2,1:T(8,128)S(1)} %get-tuple-element.75), channel_id=1, source_target_pairs={{0,4},{4,8},{8,12},{1,5},{5,9},{9,13},{2,6},{6,10},{10,14},{3,7},{... | collective-permute-start | bytes 196616 | tf_op jit(solution)/shard_map/ppermute | solution.py:14
  13.2 6.2 %collective-permute-start.1 = (f32[64,2,1,128]{3,0,2,1:T(8,128)S(1)}, f32[64,2,1,128]{3,0,2,1:T(8,128)S(1)}, u32[]{:S(2)}, u32[]{:S(2)}) collective-permute-start(f32[64,2,1,128]{3,0,2,1:T(8,128)S(1)} %get-tuple-element.76), channel_id=1, source_target_pairs={{4,0},{8,4},{12,8},{5,1},{9,5},{13,9},{6,2},{10,6},{14,10},{7,3},{... | collective-permute-start | bytes 196616 | tf_op jit(solution)/shard_map/ppermute | solution.py:17
  19.5 3.4 collective-permute-start.2
  20.8 5.2 %collective-permute-start.3 = (f32[64,2,4,1]{3,0,2,1:T(8,128)S(1)}, f32[64,2,4,1]{3,0,2,1:T(8,128)S(1)}, u32[]{:S(2)}, u32[]{:S(2)}) collective-permute-start(f32[64,2,4,1]{3,0,2,1:T(8,128)S(1)} %get-tuple-element.49), channel_id=1, source_target_pairs={{1,0},{2,1},{3,2},{5,4},{6,5},{7,6},{9,8},{10,9},{11,10},{13,12},{... | collective-permute-start | bytes 6152 | tf_op jit(solution)/shard_map/ppermute | solution.py:17
  26.9 1.5 copy-start
  31.0 5.4 %collective-permute-start.4 = (f32[64,2,1,128]{3,0,2,1:T(8,128)S(1)}, f32[64,2,1,128]{3,0,2,1:T(8,128)S(1)}, u32[]{:S(2)}, u32[]{:S(2)}) collective-permute-start(f32[64,2,1,128]{3,0,2,1:T(8,128)S(1)} %get-tuple-element.73), channel_id=1, source_target_pairs={{0,4},{4,8},{8,12},{1,5},{5,9},{9,13},{2,6},{6,10},{10,14},{3,7},{... | collective-permute-start | bytes 196616 | tf_op jit(solution)/shard_map/ppermute | solution.py:14
  34.4 6.2 %collective-permute-start.5 = (f32[64,2,1,128]{3,0,2,1:T(8,128)S(1)}, f32[64,2,1,128]{3,0,2,1:T(8,128)S(1)}, u32[]{:S(2)}, u32[]{:S(2)}) collective-permute-start(f32[64,2,1,128]{3,0,2,1:T(8,128)S(1)} %get-tuple-element.74), channel_id=1, source_target_pairs={{4,0},{8,4},{12,8},{5,1},{9,5},{13,9},{6,2},{10,6},{14,10},{7,3},{... | collective-permute-start | bytes 196616 | tf_op jit(solution)/shard_map/ppermute | solution.py:17
  40.8 6.6 %collective-permute-start.6 = (f32[64,2,4,1]{3,0,2,1:T(8,128)S(1)}, f32[64,2,4,1]{3,0,2,1:T(8,128)S(1)}, u32[]{:S(2)}, u32[]{:S(2)}) collective-permute-start(f32[64,2,4,1]{3,0,2,1:T(8,128)S(1)} %get-tuple-element.46), channel_id=1, source_target_pairs={{0,1},{1,2},{2,3},{4,5},{5,6},{6,7},{8,9},{9,10},{10,11},{12,13},{... | collective-permute-start | bytes 6152 | tf_op jit(solution)/shard_map/ppermute | solution.py:14
  46.0 4.2 %collective-permute-start.7 = (f32[64,2,4,1]{3,0,2,1:T(8,128)S(1)}, f32[64,2,4,1]{3,0,2,1:T(8,128)S(1)}, u32[]{:S(2)}, u32[]{:S(2)}) collective-permute-start(f32[64,2,4,1]{3,0,2,1:T(8,128)S(1)} %get-tuple-element.47), channel_id=1, source_target_pairs={{1,0},{2,1},{3,2},{5,4},{6,5},{7,6},{9,8},{10,9},{11,10},{13,12},{... | collective-permute-start | bytes 6152 | tf_op jit(solution)/shard_map/ppermute | solution.py:17
  55.3 5.9 %collective-permute-start.8 = (f32[64,2,2,128]{3,0,2,1:T(8,128)S(1)}, f32[64,2,2,128]{3,0,2,1:T(8,128)S(1)}, u32[]{:S(2)}, u32[]{:S(2)}) collective-permute-start(f32[64,2,2,128]{3,0,2,1:T(8,128)S(1)} %bitcast_multiply_fusion.12), channel_id=1, source_target_pairs={{0,16},{1,17},{2,18},{3,19},{4,20},{5,21},{6,22},{7,23},{8,24},{9,... | collective-permute-start | bytes 393224 | tf_op jit(solution)/shard_map/ppermute | solution.py:25
  61.2 5.4 %collective-permute-start.9 = (f32[64,2,1,128]{3,0,2,1:T(8,128)S(1)}, f32[64,2,1,128]{3,0,2,1:T(8,128)S(1)}, u32[]{:S(2)}, u32[]{:S(2)}) collective-permute-start(f32[64,2,1,128]{3,0,2,1:T(8,128)S(1)} %get-tuple-element.71), channel_id=1, source_target_pairs={{0,4},{4,8},{8,12},{1,5},{5,9},{9,13},{2,6},{6,10},{10,14},{3,7},{... | collective-permute-start | bytes 196616 | tf_op jit(solution)/shard_map/ppermute | solution.py:14
  64.7 6.2 %collective-permute-start.10 = (f32[64,2,1,128]{3,0,2,1:T(8,128)S(1)}, f32[64,2,1,128]{3,0,2,1:T(8,128)S(1)}, u32[]{:S(2)}, u32[]{:S(2)}) collective-permute-start(f32[64,2,1,128]{3,0,2,1:T(8,128)S(1)} %get-tuple-element.72), channel_id=1, source_target_pairs={{4,0},{8,4},{12,8},{5,1},{9,5},{13,9},{6,2},{10,6},{14,10},{7,3},{... | collective-permute-start | bytes 196616 | tf_op jit(solution)/shard_map/ppermute | solution.py:17
  71.0 5.9 %collective-permute-start.11 = (f32[64,2,4,1]{3,0,2,1:T(8,128)S(1)}, f32[64,2,4,1]{3,0,2,1:T(8,128)S(1)}, u32[]{:S(2)}, u32[]{:S(2)}) collective-permute-start(f32[64,2,4,1]{3,0,2,1:T(8,128)S(1)} %get-tuple-element.42), channel_id=1, source_target_pairs={{0,1},{1,2},{2,3},{4,5},{5,6},{6,7},{8,9},{9,10},{10,11},{12,13},{... | collective-permute-start | bytes 6152 | tf_op jit(solution)/shard_map/ppermute | solution.py:14
  75.4 5.0 %collective-permute-start.12 = (f32[64,2,4,1]{3,0,2,1:T(8,128)S(1)}, f32[64,2,4,1]{3,0,2,1:T(8,128)S(1)}, u32[]{:S(2)}, u32[]{:S(2)}) collective-permute-start(f32[64,2,4,1]{3,0,2,1:T(8,128)S(1)} %get-tuple-element.43), channel_id=1, source_target_pairs={{1,0},{2,1},{3,2},{5,4},{6,5},{7,6},{9,8},{10,9},{11,10},{13,12},{... | collective-permute-start | bytes 6152 | tf_op jit(solution)/shard_map/ppermute | solution.py:17
  85.5 3.8 collective-permute-start.13
  87.4 6.2 %collective-permute-start.14 = (f32[64,2,1,128]{3,0,2,1:T(8,128)S(1)}, f32[64,2,1,128]{3,0,2,1:T(8,128)S(1)}, u32[]{:S(2)}, u32[]{:S(2)}) collective-permute-start(f32[64,2,1,128]{3,0,2,1:T(8,128)S(1)} %get-tuple-element.70), channel_id=1, source_target_pairs={{4,0},{8,4},{12,8},{5,1},{9,5},{13,9},{6,2},{10,6},{14,10},{7,3},{... | collective-permute-start | bytes 196616 | tf_op jit(solution)/shard_map/ppermute | solution.py:17
  93.8 6.6 %collective-permute-start.15 = (f32[64,2,4,1]{3,0,2,1:T(8,128)S(1)}, f32[64,2,4,1]{3,0,2,1:T(8,128)S(1)}, u32[]{:S(2)}, u32[]{:S(2)}) collective-permute-start(f32[64,2,4,1]{3,0,2,1:T(8,128)S(1)} %get-tuple-element.40), channel_id=1, source_target_pairs={{0,1},{1,2},{2,3},{4,5},{5,6},{6,7},{8,9},{9,10},{10,11},{12,13},{... | collective-permute-start | bytes 6152 | tf_op jit(solution)/shard_map/ppermute | solution.py:14
  99.0 4.2 %collective-permute-start.16 = (f32[64,2,4,1]{3,0,2,1:T(8,128)S(1)}, f32[64,2,4,1]{3,0,2,1:T(8,128)S(1)}, u32[]{:S(2)}, u32[]{:S(2)}) collective-permute-start(f32[64,2,4,1]{3,0,2,1:T(8,128)S(1)} %get-tuple-element.41), channel_id=1, source_target_pairs={{1,0},{2,1},{3,2},{5,4},{6,5},{7,6},{9,8},{10,9},{11,10},{13,12},{... | collective-permute-start | bytes 6152 | tf_op jit(solution)/shard_map/ppermute | solution.py:17
  108.4 6.9 %collective-permute-start.17 = (f32[64,2,2,128]{3,0,2,1:T(8,128)S(1)}, f32[64,2,2,128]{3,0,2,1:T(8,128)S(1)}, u32[]{:S(2)}, u32[]{:S(2)}) collective-permute-start(f32[64,2,2,128]{3,0,2,1:T(8,128)S(1)} %get-tuple-element.21), channel_id=1, source_target_pairs={{0,16},{1,17},{2,18},{3,19},{4,20},{5,21},{6,22},{7,23},{8,24},{9,... | collective-permute-start | bytes 393224 | tf_op jit(solution)/shard_map/ppermute | solution.py:25
  115.2 3.8 collective-permute-start.18
  117.2 6.2 %collective-permute-start.19 = (f32[64,2,1,128]{3,0,2,1:T(8,128)S(1)}, f32[64,2,1,128]{3,0,2,1:T(8,128)S(1)}, u32[]{:S(2)}, u32[]{:S(2)}) collective-permute-start(f32[64,2,1,128]{3,0,2,1:T(8,128)S(1)} %get-tuple-element.68), channel_id=1, source_target_pairs={{4,0},{8,4},{12,8},{5,1},{9,5},{13,9},{6,2},{10,6},{14,10},{7,3},{... | collective-permute-start | bytes 196616 | tf_op jit(solution)/shard_map/ppermute | solution.py:17
  123.5 5.7 %collective-permute-start.20 = (f32[64,2,4,1]{3,0,2,1:T(8,128)S(1)}, f32[64,2,4,1]{3,0,2,1:T(8,128)S(1)}, u32[]{:S(2)}, u32[]{:S(2)}) collective-permute-start(f32[64,2,4,1]{3,0,2,1:T(8,128)S(1)} %get-tuple-element.38), channel_id=1, source_target_pairs={{0,1},{1,2},{2,3},{4,5},{5,6},{6,7},{8,9},{9,10},{10,11},{12,13},{... | collective-permute-start | bytes 6152 | tf_op jit(solution)/shard_map/ppermute | solution.py:14
  127.9 5.0 %collective-permute-start.21 = (f32[64,2,4,1]{3,0,2,1:T(8,128)S(1)}, f32[64,2,4,1]{3,0,2,1:T(8,128)S(1)}, u32[]{:S(2)}, u32[]{:S(2)}) collective-permute-start(f32[64,2,4,1]{3,0,2,1:T(8,128)S(1)} %get-tuple-element.39), channel_id=1, source_target_pairs={{1,0},{2,1},{3,2},{5,4},{6,5},{7,6},{9,8},{10,9},{11,10},{13,12},{... | collective-permute-start | bytes 6152 | tf_op jit(solution)/shard_map/ppermute | solution.py:17
  135.2 18.1 %copy-start.1 = (f32[2,64,2,2,128]{4,3,2,1,0:T(2,128)S(1)}, f32[2,64,2,2,128]{4,3,2,1,0:T(2,128)}, u32[]{:S(2)}) copy-start(f32[2,64,2,2,128]{4,3,2,1,0:T(2,128)} %param.7) | copy-start | bytes 786436
  138.0 3.8 collective-permute-start.22
  139.9 6.2 %collective-permute-start.23 = (f32[64,2,1,128]{3,0,2,1:T(8,128)S(1)}, f32[64,2,1,128]{3,0,2,1:T(8,128)S(1)}, u32[]{:S(2)}, u32[]{:S(2)}) collective-permute-start(f32[64,2,1,128]{3,0,2,1:T(8,128)S(1)} %get-tuple-element.66), channel_id=1, source_target_pairs={{4,0},{8,4},{12,8},{5,1},{9,5},{13,9},{6,2},{10,6},{14,10},{7,3},{... | collective-permute-start | bytes 196616 | tf_op jit(solution)/shard_map/ppermute | solution.py:17
  146.2 7.1 %collective-permute-start.24 = (f32[64,2,4,1]{3,0,2,1:T(8,128)S(1)}, f32[64,2,4,1]{3,0,2,1:T(8,128)S(1)}, u32[]{:S(2)}, u32[]{:S(2)}) collective-permute-start(f32[64,2,4,1]{3,0,2,1:T(8,128)S(1)} %get-tuple-element.36), channel_id=1, source_target_pairs={{0,1},{1,2},{2,3},{4,5},{5,6},{6,7},{8,9},{9,10},{10,11},{12,13},{... | collective-permute-start | bytes 6152 | tf_op jit(solution)/shard_map/ppermute | solution.py:14
  151.5 4.2 %collective-permute-start.25 = (f32[64,2,4,1]{3,0,2,1:T(8,128)S(1)}, f32[64,2,4,1]{3,0,2,1:T(8,128)S(1)}, u32[]{:S(2)}, u32[]{:S(2)}) collective-permute-start(f32[64,2,4,1]{3,0,2,1:T(8,128)S(1)} %get-tuple-element.37), channel_id=1, source_target_pairs={{1,0},{2,1},{3,2},{5,4},{6,5},{7,6},{9,8},{10,9},{11,10},{13,12},{... | collective-permute-start | bytes 6152 | tf_op jit(solution)/shard_map/ppermute | solution.py:17
  160.9 3.8 collective-permute-start.26
  162.9 6.2 %collective-permute-start.27 = (f32[64,2,1,128]{3,0,2,1:T(8,128)S(1)}, f32[64,2,1,128]{3,0,2,1:T(8,128)S(1)}, u32[]{:S(2)}, u32[]{:S(2)}) collective-permute-start(f32[64,2,1,128]{3,0,2,1:T(8,128)S(1)} %get-tuple-element.64), channel_id=1, source_target_pairs={{4,0},{8,4},{12,8},{5,1},{9,5},{13,9},{6,2},{10,6},{14,10},{7,3},{... | collective-permute-start | bytes 196616 | tf_op jit(solution)/shard_map/ppermute | solution.py:17
  169.2 6.6 %collective-permute-start.28 = (f32[64,2,4,1]{3,0,2,1:T(8,128)S(1)}, f32[64,2,4,1]{3,0,2,1:T(8,128)S(1)}, u32[]{:S(2)}, u32[]{:S(2)}) collective-permute-start(f32[64,2,4,1]{3,0,2,1:T(8,128)S(1)} %get-tuple-element.34), channel_id=1, source_target_pairs={{0,1},{1,2},{2,3},{4,5},{5,6},{6,7},{8,9},{9,10},{10,11},{12,13},{... | collective-permute-start | bytes 6152 | tf_op jit(solution)/shard_map/ppermute | solution.py:14
  174.4 4.2 %collective-permute-start.29 = (f32[64,2,4,1]{3,0,2,1:T(8,128)S(1)}, f32[64,2,4,1]{3,0,2,1:T(8,128)S(1)}, u32[]{:S(2)}, u32[]{:S(2)}) collective-permute-start(f32[64,2,4,1]{3,0,2,1:T(8,128)S(1)} %get-tuple-element.35), channel_id=1, source_target_pairs={{1,0},{2,1},{3,2},{5,4},{6,5},{7,6},{9,8},{10,9},{11,10},{13,12},{... | collective-permute-start | bytes 6152 | tf_op jit(solution)/shard_map/ppermute | solution.py:17
  183.5 3.8 collective-permute-start.30
  185.4 6.2 %collective-permute-start.31 = (f32[64,2,1,128]{3,0,2,1:T(8,128)S(1)}, f32[64,2,1,128]{3,0,2,1:T(8,128)S(1)}, u32[]{:S(2)}, u32[]{:S(2)}) collective-permute-start(f32[64,2,1,128]{3,0,2,1:T(8,128)S(1)} %get-tuple-element.62), channel_id=1, source_target_pairs={{4,0},{8,4},{12,8},{5,1},{9,5},{13,9},{6,2},{10,6},{14,10},{7,3},{... | collective-permute-start | bytes 196616 | tf_op jit(solution)/shard_map/ppermute | solution.py:17
  191.7 6.6 %collective-permute-start.32 = (f32[64,2,4,1]{3,0,2,1:T(8,128)S(1)}, f32[64,2,4,1]{3,0,2,1:T(8,128)S(1)}, u32[]{:S(2)}, u32[]{:S(2)}) collective-permute-start(f32[64,2,4,1]{3,0,2,1:T(8,128)S(1)} %get-tuple-element.32), channel_id=1, source_target_pairs={{0,1},{1,2},{2,3},{4,5},{5,6},{6,7},{8,9},{9,10},{10,11},{12,13},{... | collective-permute-start | bytes 6152 | tf_op jit(solution)/shard_map/ppermute | solution.py:14
  197.0 4.2 %collective-permute-start.33 = (f32[64,2,4,1]{3,0,2,1:T(8,128)S(1)}, f32[64,2,4,1]{3,0,2,1:T(8,128)S(1)}, u32[]{:S(2)}, u32[]{:S(2)}) collective-permute-start(f32[64,2,4,1]{3,0,2,1:T(8,128)S(1)} %get-tuple-element.33), channel_id=1, source_target_pairs={{1,0},{2,1},{3,2},{5,4},{6,5},{7,6},{9,8},{10,9},{11,10},{13,12},{... | collective-permute-start | bytes 6152 | tf_op jit(solution)/shard_map/ppermute | solution.py:17
  205.8 6.9 %collective-permute-start.34 = (f32[64,2,2,128]{3,0,2,1:T(8,128)S(1)}, f32[64,2,2,128]{3,0,2,1:T(8,128)S(1)}, u32[]{:S(2)}, u32[]{:S(2)}) collective-permute-start(f32[64,2,2,128]{3,0,2,1:T(8,128)S(1)} %bitcast.1716), channel_id=1, source_target_pairs={{16,0},{17,1},{18,2},{19,3},{20,4},{21,5},{22,6},{23,7},{24,8},{25... | collective-permute-start | bytes 393224 | tf_op jit(solution)/shard_map/ppermute | solution.py:25
  212.9 3.8 collective-permute-start.35
  214.9 6.2 %collective-permute-start.36 = (f32[64,2,1,128]{3,0,2,1:T(8,128)S(1)}, f32[64,2,1,128]{3,0,2,1:T(8,128)S(1)}, u32[]{:S(2)}, u32[]{:S(2)}) collective-permute-start(f32[64,2,1,128]{3,0,2,1:T(8,128)S(1)} %get-tuple-element.60), channel_id=1, source_target_pairs={{4,0},{8,4},{12,8},{5,1},{9,5},{13,9},{6,2},{10,6},{14,10},{7,3},{... | collective-permute-start | bytes 196616 | tf_op jit(solution)/shard_map/ppermute | solution.py:17
  221.2 8.7 %collective-permute-start.37 = (f32[64,2,4,1]{3,0,2,1:T(8,128)S(1)}, f32[64,2,4,1]{3,0,2,1:T(8,128)S(1)}, u32[]{:S(2)}, u32[]{:S(2)}) collective-permute-start(f32[64,2,4,1]{3,0,2,1:T(8,128)S(1)} %get-tuple-element.28), channel_id=1, source_target_pairs={{0,1},{1,2},{2,3},{4,5},{5,6},{6,7},{8,9},{9,10},{10,11},{12,13},{... | collective-permute-start | bytes 6152 | tf_op jit(solution)/shard_map/ppermute | solution.py:14
  225.4 5.3 %collective-permute-start.38 = (f32[64,2,4,1]{3,0,2,1:T(8,128)S(1)}, f32[64,2,4,1]{3,0,2,1:T(8,128)S(1)}, u32[]{:S(2)}, u32[]{:S(2)}) collective-permute-start(f32[64,2,4,1]{3,0,2,1:T(8,128)S(1)} %get-tuple-element.29), channel_id=1, source_target_pairs={{1,0},{2,1},{3,2},{5,4},{6,5},{7,6},{9,8},{10,9},{11,10},{13,12},{... | collective-permute-start | bytes 6152 | tf_op jit(solution)/shard_map/ppermute | solution.py:17
  235.5 4.2 %collective-permute-start.39 = (f32[64,2,1,128]{3,0,2,1:T(8,128)S(1)}, f32[64,2,1,128]{3,0,2,1:T(8,128)S(1)}, u32[]{:S(2)}, u32[]{:S(2)}) collective-permute-start(f32[64,2,1,128]{3,0,2,1:T(8,128)S(1)} %get-tuple-element.57), channel_id=1, source_target_pairs={{0,4},{4,8},{8,12},{1,5},{5,9},{9,13},{2,6},{6,10},{10,14},{3,7},{... | collective-permute-start | bytes 196616 | tf_op jit(solution)/shard_map/ppermute | solution.py:14
  237.4 6.2 %collective-permute-start.40 = (f32[64,2,1,128]{3,0,2,1:T(8,128)S(1)}, f32[64,2,1,128]{3,0,2,1:T(8,128)S(1)}, u32[]{:S(2)}, u32[]{:S(2)}) collective-permute-start(f32[64,2,1,128]{3,0,2,1:T(8,128)S(1)} %get-tuple-element.58), channel_id=1, source_target_pairs={{4,0},{8,4},{12,8},{5,1},{9,5},{13,9},{6,2},{10,6},{14,10},{7,3},{... | collective-permute-start | bytes 196616 | tf_op jit(solution)/shard_map/ppermute | solution.py:17
  243.7 9.5 %collective-permute-start.41 = (f32[64,2,4,1]{3,0,2,1:T(8,128)S(1)}, f32[64,2,4,1]{3,0,2,1:T(8,128)S(1)}, u32[]{:S(2)}, u32[]{:S(2)}) collective-permute-start(f32[64,2,4,1]{3,0,2,1:T(8,128)S(1)} %get-tuple-element.26), channel_id=1, source_target_pairs={{0,1},{1,2},{2,3},{4,5},{5,6},{6,7},{8,9},{9,10},{10,11},{12,13},{... | collective-permute-start | bytes 6152 | tf_op jit(solution)/shard_map/ppermute | solution.py:14
  249.0 4.3 %collective-permute-start.42 = (f32[64,2,4,1]{3,0,2,1:T(8,128)S(1)}, f32[64,2,4,1]{3,0,2,1:T(8,128)S(1)}, u32[]{:S(2)}, u32[]{:S(2)}) collective-permute-start(f32[64,2,4,1]{3,0,2,1:T(8,128)S(1)} %get-tuple-element.27), channel_id=1, source_target_pairs={{1,0},{2,1},{3,2},{5,4},{6,5},{7,6},{9,8},{10,9},{11,10},{13,12},{... | collective-permute-start | bytes 6152 | tf_op jit(solution)/shard_map/ppermute | solution.py:17
  257.9 6.9 %collective-permute-start.43 = (f32[64,2,2,128]{3,0,2,1:T(8,128)S(1)}, f32[64,2,2,128]{3,0,2,1:T(8,128)S(1)}, u32[]{:S(2)}, u32[]{:S(2)}) collective-permute-start(f32[64,2,2,128]{3,0,2,1:T(8,128)S(1)} %bitcast.1715), channel_id=1, source_target_pairs={{16,0},{17,1},{18,2},{19,3},{20,4},{21,5},{22,6},{23,7},{24,8},{25... | collective-permute-start | bytes 393224 | tf_op jit(solution)/shard_map/ppermute | solution.py:25
  268.0 6.5 %collective-permute-start.44 = (f32[64,2,1,128]{3,0,2,1:T(8,128)S(1)}, f32[64,2,1,128]{3,0,2,1:T(8,128)S(1)}, u32[]{:S(2)}, u32[]{:S(2)}) collective-permute-start(f32[64,2,1,128]{3,0,2,1:T(8,128)S(1)} %get-tuple-element.55), channel_id=1, source_target_pairs={{0,4},{4,8},{8,12},{1,5},{5,9},{9,13},{2,6},{6,10},{10,14},{3,7},{... | collective-permute-start | bytes 196616 | tf_op jit(solution)/shard_map/ppermute | solution.py:14
  270.2 6.2 %collective-permute-start.45 = (f32[64,2,1,128]{3,0,2,1:T(8,128)S(1)}, f32[64,2,1,128]{3,0,2,1:T(8,128)S(1)}, u32[]{:S(2)}, u32[]{:S(2)}) collective-permute-start(f32[64,2,1,128]{3,0,2,1:T(8,128)S(1)} %get-tuple-element.56), channel_id=1, source_target_pairs={{4,0},{8,4},{12,8},{5,1},{9,5},{13,9},{6,2},{10,6},{14,10},{7,3},{... | collective-permute-start | bytes 196616 | tf_op jit(solution)/shard_map/ppermute | solution.py:17
  276.6 5.3 %collective-permute-start.46 = (f32[64,2,4,1]{3,0,2,1:T(8,128)S(1)}, f32[64,2,4,1]{3,0,2,1:T(8,128)S(1)}, u32[]{:S(2)}, u32[]{:S(2)}) collective-permute-start(f32[64,2,4,1]{3,0,2,1:T(8,128)S(1)} %get-tuple-element.24), channel_id=1, source_target_pairs={{0,1},{1,2},{2,3},{4,5},{5,6},{6,7},{8,9},{9,10},{10,11},{12,13},{... | collective-permute-start | bytes 6152 | tf_op jit(solution)/shard_map/ppermute | solution.py:14
  280.3 5.3 %collective-permute-start.47 = (f32[64,2,4,1]{3,0,2,1:T(8,128)S(1)}, f32[64,2,4,1]{3,0,2,1:T(8,128)S(1)}, u32[]{:S(2)}, u32[]{:S(2)}) collective-permute-start(f32[64,2,4,1]{3,0,2,1:T(8,128)S(1)} %get-tuple-element.25), channel_id=1, source_target_pairs={{1,0},{2,1},{3,2},{5,4},{6,5},{7,6},{9,8},{10,9},{11,10},{13,12},{... | collective-permute-start | bytes 6152 | tf_op jit(solution)/shard_map/ppermute | solution.py:17
  294.9 4.6 %collective-permute-start.48 = (f32[64,2,1,128]{3,0,2,1:T(8,128)S(1)}, f32[64,2,1,128]{3,0,2,1:T(8,128)S(1)}, u32[]{:S(2)}, u32[]{:S(2)}) collective-permute-start(f32[64,2,1,128]{3,0,2,1:T(8,128)S(1)} %get-tuple-element.53), channel_id=1, source_target_pairs={{0,4},{4,8},{8,12},{1,5},{5,9},{9,13},{2,6},{6,10},{10,14},{3,7},{... | collective-permute-start | bytes 196616 | tf_op jit(solution)/shard_map/ppermute | solution.py:14
  297.7 6.9 %collective-permute-start.49 = (f32[64,2,1,128]{3,0,2,1:T(8,128)S(1)}, f32[64,2,1,128]{3,0,2,1:T(8,128)S(1)}, u32[]{:S(2)}, u32[]{:S(2)}) collective-permute-start(f32[64,2,1,128]{3,0,2,1:T(8,128)S(1)} %get-tuple-element.54), channel_id=1, source_target_pairs={{4,0},{8,4},{12,8},{5,1},{9,5},{13,9},{6,2},{10,6},{14,10},{7,3},{... | collective-permute-start | bytes 196616 | tf_op jit(solution)/shard_map/ppermute | solution.py:17
  304.7 38.4 %collective-permute-start.50 = (f32[64,2,4,1]{3,0,2,1:T(8,128)S(1)}, f32[64,2,4,1]{3,0,2,1:T(8,128)S(1)}, u32[]{:S(2)}, u32[]{:S(2)}) collective-permute-start(f32[64,2,4,1]{3,0,2,1:T(8,128)S(1)} %get-tuple-element.22), channel_id=1, source_target_pairs={{0,1},{1,2},{2,3},{4,5},{5,6},{6,7},{8,9},{9,10},{10,11},{12,13},{... | collective-permute-start | bytes 6152 | tf_op jit(solution)/shard_map/ppermute | solution.py:14
  310.3 32.8 %collective-permute-start.51 = (f32[64,2,4,1]{3,0,2,1:T(8,128)S(1)}, f32[64,2,4,1]{3,0,2,1:T(8,128)S(1)}, u32[]{:S(2)}, u32[]{:S(2)}) collective-permute-start(f32[64,2,4,1]{3,0,2,1:T(8,128)S(1)} %get-tuple-element.23), channel_id=1, source_target_pairs={{1,0},{2,1},{3,2},{5,4},{6,5},{7,6},{9,8},{10,9},{11,10},{13,12},{... | collective-permute-start | bytes 6152 | tf_op jit(solution)/shard_map/ppermute | solution.py:17
Sparse Core Ops, SparseCore 0:
  295.0 97.6 all-reduce.13
where the time goes:
time: 411 us; the launch traced here: 403 us
  waiting for transfers between devices  141 us (34%)
  starting transfers between devices  128 us (31%)
  matrix products  46.1 us (11%)
  blocking collectives  31.5 us (8%)
  local copies, waits for them, and re-layouts  22.3 us (5%)
  between operations  18 us (4%)
  other arithmetic  15.9 us (4%)
    ppermute x24, starting transfers between devices, extended(): lax.ppermute(lax.slice_in_dim(block, block.shape[dim] - width, None, axis...  85.4 us
    ppermute x24, waiting for transfers between devices, extended(): lax.ppermute(lax.slice_in_dim(block, 0, width, axis=dim), axis, backward)  78 us
    psum x1, waiting for transfers between devices, per_device(): lax.psum((jnp.stack(weight_grads) * grad_scale, jnp.stack(bias_grads) * g...  44.1 us
    ppermute x24, starting transfers between devices, extended(): lax.ppermute(lax.slice_in_dim(block, 0, width, axis=dim), axis, backward)  32.1 us
    psum x1, blocking collectives, per_device(): lax.psum((jnp.stack(weight_grads) * grad_scale, jnp.stack(bias_grads) * g...  31.5 us
    unnamed x218, local copies, waits for them, and re-layouts  18.2 us
    dot_general x6, matrix products, per_device(): jnp.einsum('oxyz,tcxyz->toc', slope_grad, stacked_taps(padded, extents, F...  18 us
    dot_general x6, matrix products, convolve(): jnp.einsum('toc,tcxyz->oxyz', weight, stacked_taps(padded, out_sizes, Fal...  14.9 us
  transfers between devices with their start and end apart: 53, of which 37 were waited for; matrix products, arithmetic and copies ran while one was open for 5% of the time, Pallas kernels for 0%

commit v1 on v0

v1 whole, which is shorter than its diff:
```python
import functools
import math

import jax
import jax.numpy as jnp
from jax import lax
from jax.experimental import pallas as pl
from jax.experimental.pallas import tpu as pltpu
from jax.sharding import PartitionSpec as P

HALO = 8
LANES = 128
BF16 = jnp.bfloat16
F32 = jnp.float32


def shifted(block, axis, distance):
    count = lax.axis_size(axis)
    route = [(i, i + distance) for i in range(count) if 0 <= i + distance < count]
    return lax.ppermute(block, axis, route)


def split_terms(values):
    high = values.astype(BF16)
    return high, (values - high.astype(F32)).astype(BF16)


def slab_kernel(dims, place, own, other, cells, outs, sums, fwd, bwd, acts, rim, kept, slopes, acc):
    micros, rows_y, depth, width, chunk_y, chans, limit_z, scale = dims
    section = place[0]
    origin = place[1]
    chunk = chunk_y * depth
    chunks = rows_y // chunk_y
    per_owner = rows_y // cells.shape[0]
    zs = lax.broadcasted_iota(jnp.int32, (depth, LANES), 0)
    in_grid = ((zs + origin >= 0) & (zs + origin < limit_z)).astype(F32)[None]
    mine = ((zs >= HALO) & (zs < HALO + width)).astype(F32)[None]

    def prepare(pair, carry):
        for half in range(2):
            layer = 2 * pair + half
            for b in range(3):
                for c in range(3):
                    taps = []
                    for a in range(3):
                        tap = 9 * a + 3 * b + c
                        both = jnp.where(pair == section, own[tap], other[tap])
                        taps.append(both[:, half * chans : (half + 1) * chans])
                    top = jnp.concatenate([taps[1], taps[2]], axis=1)
                    low = jnp.concatenate([taps[0], taps[1]], axis=1)
                    block = jnp.concatenate([top, low], axis=0)
                    for target, value, row, col in (
                        (fwd, block.T, b, c),
                        (bwd, block, 2 - b, 2 - c),
                    ):
                        hi, lo = split_terms(value)
                        at = slice(col * LANES, (col + 1) * LANES)
                        target[layer, 2 * row * LANES : (2 * row + 1) * LANES, at] = hi
                        target[layer, (2 * row + 1) * LANES : (2 * row + 2) * LANES, at] = hi
                        target[layer, (6 + row) * LANES : (7 + row) * LANES, at] = lo
        return carry

    lax.fori_loop(0, 2, prepare, 0)

    def over_chunks(body):
        if chunks == 1:
            for micro in range(micros):
                body(micro, 0, 0)
        else:

            def step(index, carry):
                part = index % chunks
                body(index // chunks, part, pl.multiple_of(part * chunk, 16))
                return carry

            lax.fori_loop(0, micros * chunks, step, 0)

    def put_rows(target, lead, start, values):
        hi, lo = split_terms(values)
        at = pl.ds(start + depth, chunk)
        target[(*lead, at, slice(0, LANES))] = hi
        target[(*lead, at, slice(LANES, 2 * LANES))] = lo

    def pieces_of(source, lead, start):
        return [source[(*lead, pl.ds(start + b * depth, chunk), slice(None))] for b in range(3)]

    def conv(source, lead, start, table):
        pieces = pieces_of(source, lead, start)
        left = jnp.concatenate(pieces + [piece[:, :LANES] for piece in pieces], axis=1)
        out = jnp.dot(left, table[...], preferred_element_type=F32)
        before = pltpu.roll(out[:, :LANES], 1, 0)
        after = pltpu.roll(out[:, 2 * LANES :], chunk - 1, 0)
        return before + out[:, LANES : 2 * LANES] + after

    def masked(values, mask):
        return (values.reshape(chunk_y, depth, LANES) * mask).reshape(chunk, LANES)

    blank = jnp.zeros((depth, 2 * LANES), BF16)
    for micro in range(micros):
        for edge in (0, rows_y + 1):
            at = slice(edge * depth, (edge + 1) * depth)
            for layer in range(4):
                acts[layer, micro, at, :] = blank
            for side in range(2):
                rim[side, micro, at, :] = blank

    def load(micro, part, which):
        rows = [part * chunk_y + y for y in range(chunk_y)]
        pieces = [cells[row // per_owner, which, micro, row % per_owner] for row in rows]
        return jnp.concatenate(pieces, axis=0)

    def emit(slot, micro, part, values):
        inner = values.reshape(chunk_y, depth, LANES)[:, HALO : HALO + width, :]
        outs[slot, micro, pl.ds(part * chunk_y, chunk_y)] = inner

    over_chunks(lambda micro, part, start: put_rows(acts, (0, micro), start, load(micro, part, 0)))

    for layer in range(4):
        source = own if layer < 2 else other
        half = layer % 2

        def forward(micro, part, start):
            row = jnp.where(section == layer // 2, own[27, 0:1, :], other[27, 0:1, :])
            bias = row[:, half * chans : (half + 1) * chans]
            bias = jnp.concatenate([bias, bias], axis=1)
            pre = conv(acts, (layer, micro), start, fwd.at[layer]) + bias
            grown = 1.0 + jnp.exp(-pre)
            sigma = 1.0 / grown
            kept[layer, micro, pl.ds(start, chunk), :] = sigma * (1.0 + pre * (1.0 - sigma))
            out = masked(pre / grown, in_grid)
            if layer < 3:
                put_rows(acts, (layer + 1, micro), start, out)
            if half == 1:
                pl.when(section == layer // 2)(lambda: emit(0, micro, part, out))

        over_chunks(forward)

    def take_gradient(layer, micro, start, gradient):
        slope = masked(gradient * kept[layer, micro, pl.ds(start, chunk), :], in_grid)
        slopes[layer, micro, pl.ds(start, chunk), :] = masked(slope, mine)
        put_rows(rim, (layer % 2, micro), start, slope)

    over_chunks(lambda micro, part, start: take_gradient(3, micro, start, load(micro, part, 1)))

    def backward(layer):
        def pull(micro, part, start):
            gradient = conv(rim, (layer % 2, micro), start, bwd.at[layer])
            if layer > 0:
                take_gradient(layer - 1, micro, start, gradient)
            if layer % 2 == 0:
                pl.when(section == layer // 2)(lambda: emit(1, micro, part, gradient))

        over_chunks(pull)

    backward(3)
    backward(2)

    @pl.when(section == 0)
    def _():
        backward(1)
        backward(0)

    sums[27] = jnp.zeros((chans, LANES), F32)
    for slot in range(2):
        layer = 2 * section + slot
        acc[...] = jnp.zeros(acc.shape, F32)

        def gather(micro, part, start):
            slope = slopes[layer, micro, pl.ds(start, chunk), :]
            moved = [pltpu.roll(slope, 1 if c == 0 else chunk - 1, 0) if c != 1 else slope for c in (2, 1, 0)]
            terms = [split_terms(value) for value in moved]
            left_hi = jnp.concatenate([hi for hi, lo in terms], axis=1)
            left_lo = jnp.concatenate([lo for hi, lo in terms], axis=1)
            pieces = pieces_of(acts, (layer, micro), start)
            full = jnp.concatenate(pieces, axis=1)
            high = jnp.concatenate([piece[:, :LANES] for piece in pieces], axis=1)
            over_rows = (((0,), (0,)), ((), ()))
            one = lax.dot_general(left_hi, full, over_rows, preferred_element_type=F32)
            two = lax.dot_general(left_lo, high, over_rows, preferred_element_type=F32)
            for b in range(3):
                at = slice(b * LANES, (b + 1) * LANES)
                acc[0 : 3 * LANES, at] += (
                    one[:, 2 * b * LANES : (2 * b + 1) * LANES]
                    + one[:, (2 * b + 1) * LANES : (2 * b + 2) * LANES]
                    + two[:, at]
                )
            acc[3 * LANES : 3 * LANES + 1, 0:LANES] += jnp.sum(slope, axis=0, keepdims=True)

        over_chunks(gather)
        lanes = slice(slot * chans, (slot + 1) * chans)
        for b in range(3):
            for c in range(3):
                block = acc[c * LANES : (c + 1) * LANES, b * LANES : (b + 1) * LANES] * scale
                tap = 3 * b + c
                sums[tap, :, lanes] = block[chans:, :chans]
                sums[9 + tap, :, lanes] = block[:chans, :chans] + block[chans:, chans:]
                sums[18 + tap, :, lanes] = block[:chans, chans:]
        row = acc[3 * LANES : 3 * LANES + 1, 0:LANES] * scale
        sums[27, 0:1, lanes] = row[:, :chans] + row[:, chans:]


def packed(weights, biases):
    pair = jnp.concatenate([weights[0], weights[1]], axis=-1)
    row = jnp.concatenate([biases[0], biases[1]])[None, None, :]
    tail = jnp.pad(row, ((0, 0), (0, pair.shape[1] - 1), (0, 0)))
    return jnp.concatenate([pair, tail], axis=0)


def summed_over_grid(block):
    rows = block.shape[0]
    gy, gz = lax.axis_size("gy"), lax.axis_size("gz")
    even = -(-rows // (gy * gz * 8)) * gy * gz * 8
    block = jnp.pad(block, ((0, even - rows), (0, 0)))
    for axis, count in (("gz", gz), ("gy", gy)):
        parts = block.reshape(count, block.shape[0] // count, LANES)
        block = jnp.sum(lax.all_to_all(parts, axis, 0, 0), axis=0)
    for axis in ("gy", "gz"):
        block = lax.all_gather(block, axis, tiled=True)
    return block[:rows]


def per_device(inflow, weights, biases, cotangent):
    micros, chans, size_x, local_y, local_z = inflow.shape
    gy, gz = lax.axis_size("gy"), lax.axis_size("gz")
    rows_y = local_y * gy
    width = local_z // gy
    depth = -(-(width + 2 * HALO) // 16) * 16
    chunk_y = max(n for n in range(1, rows_y + 1) if rows_y % n == 0 and n * depth <= 384)
    scale = 1.0 / math.sqrt(micros * size_x * rows_y * local_z * gz)
    section = lax.axis_index("section")

    own = packed(weights, biases)
    other = lax.ppermute(own, "section", [(0, 1), (1, 0)])

    fields = jnp.stack([inflow, cotangent]).transpose(0, 1, 4, 5, 3, 2)
    fields = fields.reshape(2, micros, local_y, local_z, size_x * chans)
    before = shifted(fields[:, :, :, local_z - HALO :], "gz", 1)
    after = shifted(fields[:, :, :, :HALO], "gz", -1)
    span = width * (gy - 1) + depth
    fields = jnp.concatenate([before, fields, after], axis=3)
    fields = jnp.pad(fields, ((0, 0),) * 3 + ((0, max(0, span - fields.shape[3])), (0, 0)))
    windows = jnp.stack(
        [lax.slice_in_dim(fields, i * width, i * width + depth, axis=3) for i in range(gy)]
    )
    cells = lax.all_to_all(windows, "gy", 0, 0)

    origin = lax.axis_index("gz") * local_z + lax.axis_index("gy") * width - HALO
    place = jnp.stack([section, origin]).astype(jnp.int32)
    dims = (micros, rows_y, depth, width, chunk_y, chans, local_z * gz, scale)
    padded = (rows_y + 2) * depth
    full = rows_y * depth
    vmem = pl.BlockSpec(memory_space=pltpu.VMEM)
    outs, sums = pl.pallas_call(
        functools.partial(slab_kernel, dims),
        out_shape=(
            jax.ShapeDtypeStruct((2, micros, rows_y, width, LANES), F32),
            jax.ShapeDtypeStruct((28, chans, LANES), F32),
        ),
        in_specs=[pl.BlockSpec(memory_space=pltpu.SMEM), vmem, vmem, vmem],
        out_specs=(vmem, vmem),
        scratch_shapes=[
            pltpu.VMEM((4, 9 * LANES, 3 * LANES), BF16),
            pltpu.VMEM((4, 9 * LANES, 3 * LANES), BF16),
            pltpu.VMEM((4, micros, padded, 2 * LANES), BF16),
            pltpu.VMEM((2, micros, padded, 2 * LANES), BF16),
            pltpu.VMEM((4, micros, full, LANES), F32),
            pltpu.VMEM((4, micros, full, LANES), F32),
            pltpu.VMEM((3 * LANES + 8, 3 * LANES), F32),
        ],
        compiler_params=pltpu.CompilerParams(vmem_limit_bytes=56 * 1024 * 1024),
        name="slab",
    )(place, own, other, cells)

    total = summed_over_grid(sums.reshape(28 * chans, LANES)).reshape(28, chans, LANES)
    weight_total = jnp.stack([total[:27, :, :chans], total[:27, :, chans:]])
    bias_total = total[27, 0].reshape(2, chans)

    parts = outs.reshape(2, micros, gy, local_y, width, LANES).transpose(2, 0, 1, 3, 4, 5)
    parts = lax.all_to_all(parts, "gy", 0, 0)
    parts = parts.reshape(gy, 2, micros, local_y, width, size_x, chans)
    parts = parts.transpose(1, 2, 6, 5, 3, 0, 4)
    parts = parts.reshape(2, micros, chans, size_x, local_y, local_z)
    return (parts[0][None], parts[1][None], weight_total, bias_total)


def solution(mesh):
    grid = P(None, None, None, "gy", "gz")
    section_grid = P("section", None, None, None, "gy", "gz")
    return jax.shard_map(
        per_device,
        mesh=mesh,
        in_specs=(grid, P("section", None, None, None), P("section", None), grid),
        out_specs=(section_grid, section_grid, P("section", None, None, None), P("section", None)),
        check_vma=False,
    )
```

time: 411 us -> 129 us (0.31); the launches traced: 403 us -> 128 us
  starting transfers between devices: 128 us -> 22.5 us
  waiting for transfers between devices: 141 us -> 52.9 us
  matrix products: 46.1 us -> 0 us
  between operations: 18 us -> 0.8 us
  Pallas kernels: 0 us -> 15.8 us
  local copies, waits for them, and re-layouts: 22.3 us -> 9.1 us
  other arithmetic: 15.9 us -> 4.15 us
  blocking collectives: 31.5 us -> 22.8 us
    ppermute x52 -> x3, starting transfers between devices: 128 us -> 5.21 us  [the longest x2 3.65 us: shifted(): return lax.ppermute(block, axis, route)]
    ppermute x52 -> x3, waiting for transfers between devices: 96.8 us -> 22.1 us  [the longest x1 19.7 us: per_device(): other = lax.ppermute(own, 'section', [(0, 1), (1, 0)])]
    dot_general x18 -> x0, matrix products: 46.1 us -> none  [the longest x6 18 us: per_device(): jnp.einsum('oxyz,tcxyz->toc', slope_grad, stacked_taps(padded, extents, F...]
    psum x1 -> x0, waiting for transfers between devices: 44.1 us -> none  [per_device(): lax.psum((jnp.stack(weight_grads) * grad_scale, jnp.stack(bias_grads) * g...]
    psum x1 -> x0, blocking collectives: 31.5 us -> none  [per_device(): lax.psum((jnp.stack(weight_grads) * grad_scale, jnp.stack(bias_grads) * g...]
    all_to_all x0 -> x4, waiting for transfers between devices: none -> 30.8 us  [the longest x2 17.2 us: summed_over_grid(): block = jnp.sum(lax.all_to_all(parts, axis, 0, 0), axis=0)]
    all_gather x0 -> x2, blocking collectives: none -> 22.8 us  [summed_over_grid(): block = lax.all_gather(block, axis, tiled=True)]
    all_to_all x0 -> x4, starting transfers between devices: none -> 17.3 us  [the longest x2 7.02 us: summed_over_grid(): block = jnp.sum(lax.all_to_all(parts, axis, 0, 0), axis=0)]
  transfers between devices with their start and end apart: 53 -> 7, of which waited for: 37 -> 5; matrix products, arithmetic and copies ran while one was open for 5% -> 5% of each run, Pallas kernels for 0% -> 0%
where the time goes in v1:
time: 129 us; the launch traced here: 128 us
  waiting for transfers between devices  52.9 us (41%)
  blocking collectives  22.8 us (18%)
  starting transfers between devices  22.5 us (17%)
  Pallas kernels  15.8 us (12%)
  local copies, waits for them, and re-layouts  9.1 us (7%)
  other arithmetic  4.15 us (3%)
    all_gather x2, blocking collectives, summed_over_grid(): block = lax.all_gather(block, axis, tiled=True)  22.8 us
    ppermute x1, waiting for transfers between devices, per_device(): other = lax.ppermute(own, 'section', [(0, 1), (1, 0)])  19.7 us
    all_to_all x2, waiting for transfers between devices, summed_over_grid(): block = jnp.sum(lax.all_to_all(parts, axis, 0, 0), axis=0)  17.2 us
    pallas_call x1, Pallas kernels, per_device(): pl.pallas_call(functools.partial(slab_kernel, dims), out_shape=(jax.Shape...  15.8 us
    all_to_all x1, waiting for transfers between devices, per_device(): parts = lax.all_to_all(parts, 'gy', 0, 0)  13.6 us
    all_to_all x2, starting transfers between devices, summed_over_grid(): block = jnp.sum(lax.all_to_all(parts, axis, 0, 0), axis=0)  7.02 us
    all_to_all x1, starting transfers between devices, per_device(): parts = lax.all_to_all(parts, 'gy', 0, 0)  5.4 us
    all_to_all x1, starting transfers between devices, per_device(): cells = lax.all_to_all(windows, 'gy', 0, 0)  4.87 us
  transfers between devices with their start and end apart: 7, of which 5 were waited for; matrix products, arithmetic and copies ran while one was open for 5% of the time, Pallas kernels for 0%

profile of v1, /device:TPU:0, one launch (start us, length us, event | category | flops | bytes accessed | tf_op | source)
XLA Modules:
  0.0 128.1 jit_solution(11446427372991493583)
XLA Ops:
  0.6 1.1 copy_bitcast_fusion.1
  1.8 0.2 copy.35
  2.0 2.4 %collective-permute-start.1 = (f32[2,2,2,8,128]{4,3,2,1,0:T(8,128)S(1)}, f32[2,2,2,8,128]{4,3,2,1,0:T(8,128)S(1)}, u32[]{:S(2)}, u32[]{:S(2)}) collective-permute-start(f32[2,2,2,8,128]{4,3,2,1,0:T(8,128)S(1)} %get-tuple-element.30), channel_id=1, source_target_pairs={{0,1},{1,2},{2,3},{4,5},{5,6},{6,7},{8,9},{9,10},{10,11},{12,13},{... | collective-permute-start | bytes 98312 | tf_op jit(solution)/shard_map/ppermute | solution.py:20
  4.4 1.3 %collective-permute-start.2 = (f32[2,2,2,8,128]{4,3,2,1,0:T(8,128)S(1)}, f32[2,2,2,8,128]{4,3,2,1,0:T(8,128)S(1)}, u32[]{:S(2)}, u32[]{:S(2)}) collective-permute-start(f32[2,2,2,8,128]{4,3,2,1,0:T(8,128)S(1)} %get-tuple-element.31), channel_id=1, source_target_pairs={{1,0},{2,1},{3,2},{5,4},{6,5},{7,6},{9,8},{10,9},{11,10},{13,12},{... | collective-permute-start | bytes 98312 | tf_op jit(solution)/shard_map/ppermute | solution.py:20
  5.7 1.6 %slice_bitcast_fusion.3 = (f32[27,64,64]{2,1,0:T(8,128)S(1)}, f32[27,64,64]{2,1,0:T(8,128)S(1)}) fusion(f32[2,27,64,64]{3,2,1,0:T(8,128)} %param.5), kind=kLoop, calls=%fused_computation.6 | loop fusion | bytes 1769472 | tf_op jit(solution)/shard_map/squeeze | solution.py:203
  7.2 0.0 collective-permute-done.1
  7.2 2.4 %collective-permute-done.2 = f32[2,2,2,8,128]{4,3,2,1,0:T(8,128)S(1)} collective-permute-done((f32[2,2,2,8,128]{4,3,2,1,0:T(8,128)S(1)}, f32[2,2,2,8,128]{4,3,2,1,0:T(8,128)S(1)}, u32[]{:S(2)}, u32[]{:S(2)}) %collective-permute-start.2) | collective-permute-done | bytes 32800 | tf_op jit(solution)/shard_map/ppermute | solution.py:20
  9.6 0.1 fusion.1
  9.7 0.0 copy-start.4
  9.7 1.0 pad_maximum_fusion.1
  10.7 4.9 %all-to-all-start = ((f32[4,2,2,2,48,128]{5,4,3,2,1,0:T(8,128)}), f32[4,2,2,2,48,128]{5,4,3,2,1,0:T(8,128)S(1)}, u32[]{:S(2)}, u32[]{:S(2)}) async-start(f32[4,2,2,2,48,128]{5,4,3,2,1,0:T(8,128)} %pad_maximum_fusion.1), calls=%async_computation | async-start | bytes 1572864 | tf_op jit(solution)/shard_map/all_to_all | solution.py:245
  15.6 0.0 copy-done.4
  15.6 0.1 maximum_bitcast_fusion
  15.6 0.3 select_maximum_fusion.own
  15.9 0.0 copy-start
  16.0 1.6 %collective-permute-start = (f32[28,64,128]{2,1,0:T(8,128)S(1)}, f32[28,64,128]{2,1,0:T(8,128)S(1)}, u32[]{:S(2)}, u32[]{:S(2)}) collective-permute-start(f32[28,64,128]{2,1,0:T(8,128)S(1)} %select_maximum_fusion.own), channel_id=1, source_target_pairs={{0,16},{16,0},{1,17},{17,1},{2,18},{18,2},{3,19},{19,3},{4,20},{20... | collective-permute-start | bytes 2752520 | tf_op jit(solution)/shard_map/ppermute | solution.py:233
  17.5 0.6 pad_add_fusion.place
  18.1 19.7 %collective-permute-done.other = f32[28,64,128]{2,1,0:T(8,128)S(1)} collective-permute-done((f32[28,64,128]{2,1,0:T(8,128)S(1)}, f32[28,64,128]{2,1,0:T(8,128)S(1)}, u32[]{:S(2)}, u32[]{:S(2)}) %collective-permute-start) | collective-permute-done | bytes 917536 | tf_op jit(solution)/shard_map/ppermute | solution.py:233
  37.8 0.0 copy-start.2
  37.8 0.0 all-to-all-done.cells
  37.8 0.0 copy-done
  37.8 0.9 copy-done.2
  38.7 0.0 copy-start.1
  38.7 0.9 copy-done.1
  39.6 15.8 %slab.1 = (f32[2,2,8,32,128]{4,3,2,1,0:T(8,128)}, f32[28,64,128]{2,1,0:T(8,128)}) custom-call(s32[2]{0:T(128)} %pad_add_fusion.place, f32[28,64,128]{2,1,0:T(8,128)} %copy-done, f32[28,64,128]{2,1,0:T(8,128)} %copy-done.2, f32[4,2,2,2,48,128]{5,4,3,2,1,0:T(8,128)} %copy-done.1), custom_call_target="tpu_custom_call" | custom-call | tf_op jit(solution)/shard_map/slab/pallas_call | solution.py:253
  55.5 0.0 copy-start.3
  55.5 3.6 %all-to-all-start.2 = ((f32[4,448,128]{2,1,0:T(8,128)}), f32[4,448,128]{2,1,0:T(8,128)S(1)}, u32[]{:S(2)}, u32[]{:S(2)}) async-start(f32[4,448,128]{2,1,0:T(8,128)} %bitcast.49), calls=%async_computation.2 | async-start | bytes 1835008 | tf_op jit(solution)/shard_map/all_to_all | solution.py:216
  59.1 0.0 copy-done.3
  59.1 0.8 copy.49
  60.0 12.2 %all-to-all-done.2 = f32[4,448,128]{2,1,0:T(8,128)S(1)} async-done(((f32[4,448,128]{2,1,0:T(8,128)}), f32[4,448,128]{2,1,0:T(8,128)S(1)}, u32[]{:S(2)}, u32[]{:S(2)}) %all-to-all-start.2) | async-done | bytes 917536 | tf_op jit(solution)/shard_map/all_to_all | solution.py:216
  72.2 5.4 %all-to-all-start.1 = ((f32[4,2,2,2,32,128]{5,4,3,2,1,0:T(8,128)}), f32[4,2,2,2,32,128]{5,4,3,2,1,0:T(8,128)S(1)}, u32[]{:S(2)}, u32[]{:S(2)}) async-start(f32[4,2,2,2,32,128]{5,4,3,2,1,0:T(8,128)} %bitcast.42), calls=%async_computation.1 | async-start | bytes 1048576 | tf_op jit(solution)/shard_map/all_to_all | solution.py:279
  77.6 0.7 reduce_sum.18
  78.3 13.6 %all-to-all-done.1 = f32[4,2,2,2,32,128]{5,4,3,2,1,0:T(8,128)S(1)} async-done(((f32[4,2,2,2,32,128]{5,4,3,2,1,0:T(8,128)}), f32[4,2,2,2,32,128]{5,4,3,2,1,0:T(8,128)S(1)}, u32[]{:S(2)}, u32[]{:S(2)}) %all-to-all-start.1) | async-done | bytes 524320 | tf_op jit(solution)/shard_map/all_to_all | solution.py:279
  91.9 3.4 %all-to-all-start.3 = ((f32[4,112,128]{2,1,0:T(8,128)}), f32[4,112,128]{2,1,0:T(8,128)S(1)}, u32[]{:S(2)}, u32[]{:S(2)}) async-start(f32[4,112,128]{2,1,0:T(8,128)} %bitcast.21), calls=%async_computation.3 | async-start | bytes 458752 | tf_op jit(solution)/shard_map/all_to_all | solution.py:216
  95.2 0.6 reshape.33
  95.9 0.1 fusion.2
  96.0 0.1 copy.43
  96.0 0.9 copy.45
  96.9 0.1 copy.42
  97.0 0.9 copy.44
  97.9 5.1 %all-to-all-done.3 = f32[4,112,128]{2,1,0:T(8,128)S(1)} async-done(((f32[4,112,128]{2,1,0:T(8,128)}), f32[4,112,128]{2,1,0:T(8,128)S(1)}, u32[]{:S(2)}, u32[]{:S(2)}) %all-to-all-start.3) | async-done | bytes 229408 | tf_op jit(solution)/shard_map/all_to_all | solution.py:216
  103.0 14.2 %all_gather.6 = f32[448,128]{1,0:T(8,128)S(1)} all-gather(f32[112,128]{1,0:T(8,128)S(1)} %reduce_sum.19), channel_id=1, replica_groups=mesh['section'=2,'gy'=4,'gz'=4] {'gy'}, dimensions={0}, use_global_device_ids=true | all-gather | bytes 286720 | tf_op jit(solution)/shard_map/all_gather | solution.py:218
  117.2 8.6 %all_gather.7 = f32[1792,128]{1,0:T(8,128)S(1)} all-gather(f32[448,128]{1,0:T(8,128)S(1)} %all_gather.6), channel_id=1, replica_groups=mesh['section'=2,'gy'=4,'gz'=4] {'gz'}, dimensions={0}, use_global_device_ids=true | all-gather | bytes 1146880 | tf_op jit(solution)/shard_map/all_gather | solution.py:218
  125.8 0.3 slice_bitcast_fusion.1
  126.1 0.6 reshape_squeeze.3
  126.8 1.3 %pad_maximum_fusion = f32[2,27,64,64]{3,2,1,0:T(8,128)} fusion(f32[1,27,64,64]{3,2,1,0:T(8,128)S(1)} %get-tuple-element.25, f32[1,27,64,64]{3,2,1,0:T(8,128)S(1)} %get-tuple-element.24), kind=kLoop, calls=%fused_computation | loop fusion | flops 221184 | bytes 1769472 | tf_op jit(solution)/shard_map/stack | solution.py:275
  (5 shorter events, 0.1 us)
Async XLA Ops:
  2.0 5.2 %collective-permute-start.1 = (f32[2,2,2,8,128]{4,3,2,1,0:T(8,128)S(1)}, f32[2,2,2,8,128]{4,3,2,1,0:T(8,128)S(1)}, u32[]{:S(2)}, u32[]{:S(2)}) collective-permute-start(f32[2,2,2,8,128]{4,3,2,1,0:T(8,128)S(1)} %get-tuple-element.30), channel_id=1, source_target_pairs={{0,1},{1,2},{2,3},{4,5},{5,6},{6,7},{8,9},{9,10},{10,11},{12,13},{... | collective-permute-start | bytes 98312 | tf_op jit(solution)/shard_map/ppermute | solution.py:20
  4.4 5.2 %collective-permute-start.2 = (f32[2,2,2,8,128]{4,3,2,1,0:T(8,128)S(1)}, f32[2,2,2,8,128]{4,3,2,1,0:T(8,128)S(1)}, u32[]{:S(2)}, u32[]{:S(2)}) collective-permute-start(f32[2,2,2,8,128]{4,3,2,1,0:T(8,128)S(1)} %get-tuple-element.31), channel_id=1, source_target_pairs={{1,0},{2,1},{3,2},{5,4},{6,5},{7,6},{9,8},{10,9},{11,10},{13,12},{... | collective-permute-start | bytes 98312 | tf_op jit(solution)/shard_map/ppermute | solution.py:20
  9.7 5.9 %copy-start.4 = (f32[2,64]{1,0:T(2,128)S(1)}, f32[2,64]{1,0:T(2,128)}, u32[]{:S(2)}) copy-start(f32[2,64]{1,0:T(2,128)} %param.6) | copy-start | bytes 1540
  10.7 27.1 %all-to-all-start = ((f32[4,2,2,2,48,128]{5,4,3,2,1,0:T(8,128)}), f32[4,2,2,2,48,128]{5,4,3,2,1,0:T(8,128)S(1)}, u32[]{:S(2)}, u32[]{:S(2)}) async-start(f32[4,2,2,2,48,128]{5,4,3,2,1,0:T(8,128)} %pad_maximum_fusion.1), calls=%async_computation | async-start | bytes 1572864 | tf_op jit(solution)/shard_map/all_to_all | solution.py:245
  15.9 21.9 %copy-start = (f32[28,64,128]{2,1,0:T(8,128)}, f32[28,64,128]{2,1,0:T(8,128)S(1)}, u32[]{:S(2)}) copy-start(f32[28,64,128]{2,1,0:T(8,128)S(1)} %select_maximum_fusion.own) | copy-start | bytes 2752516
  16.0 21.9 %collective-permute-start = (f32[28,64,128]{2,1,0:T(8,128)S(1)}, f32[28,64,128]{2,1,0:T(8,128)S(1)}, u32[]{:S(2)}, u32[]{:S(2)}) collective-permute-start(f32[28,64,128]{2,1,0:T(8,128)S(1)} %select_maximum_fusion.own), channel_id=1, source_target_pairs={{0,16},{16,0},{1,17},{17,1},{2,18},{18,2},{3,19},{19,3},{4,20},{20... | collective-permute-start | bytes 2752520 | tf_op jit(solution)/shard_map/ppermute | solution.py:233
  37.8 0.9 copy-start.2
  38.7 0.9 copy-start.1
  55.5 3.6 %copy-start.3 = (f32[2,2,8,32,128]{4,3,2,1,0:T(8,128)S(1)}, f32[2,2,8,32,128]{4,3,2,1,0:T(8,128)}, u32[]{:S(2)}) copy-start(f32[2,2,8,32,128]{4,3,2,1,0:T(8,128)} %get-tuple-element.6) | copy-start | bytes 1572868
  55.5 16.7 %all-to-all-start.2 = ((f32[4,448,128]{2,1,0:T(8,128)}), f32[4,448,128]{2,1,0:T(8,128)S(1)}, u32[]{:S(2)}, u32[]{:S(2)}) async-start(f32[4,448,128]{2,1,0:T(8,128)} %bitcast.49), calls=%async_computation.2 | async-start | bytes 1835008 | tf_op jit(solution)/shard_map/all_to_all | solution.py:216
  72.2 19.7 %all-to-all-start.1 = ((f32[4,2,2,2,32,128]{5,4,3,2,1,0:T(8,128)}), f32[4,2,2,2,32,128]{5,4,3,2,1,0:T(8,128)S(1)}, u32[]{:S(2)}, u32[]{:S(2)}) async-start(f32[4,2,2,2,32,128]{5,4,3,2,1,0:T(8,128)} %bitcast.42), calls=%async_computation.1 | async-start | bytes 1048576 | tf_op jit(solution)/shard_map/all_to_all | solution.py:279
  91.9 11.1 %all-to-all-start.3 = ((f32[4,112,128]{2,1,0:T(8,128)}), f32[4,112,128]{2,1,0:T(8,128)S(1)}, u32[]{:S(2)}, u32[]{:S(2)}) async-start(f32[4,112,128]{2,1,0:T(8,128)} %bitcast.21), calls=%async_computation.3 | async-start | bytes 458752 | tf_op jit(solution)/shard_map/all_to_all | solution.py:216

commit v2 on v1

v2 whole, which is shorter than its diff:
```python
import functools
import math

import jax
import jax.numpy as jnp
from jax import lax
from jax.experimental import pallas as pl
from jax.experimental.pallas import tpu as pltpu
from jax.sharding import PartitionSpec as P

HALO = 8
LANES = 128
BF16 = jnp.bfloat16
F32 = jnp.float32


def split_terms(values):
    high = values.astype(BF16)
    return high, (values - high.astype(F32)).astype(BF16)


def slab_kernel(dims, place, own, first, second, *rest):
    micros, rows_y, depth, width, chunk_y, chans, limit_z, scale, slabs, reach = dims
    windows, rest = rest[:slabs], rest[slabs:]
    edges, rest = rest[:-11], rest[-11:]
    front, back, sums, fwd, bwd, acts, rim, kept, slopes, field, acc = rest
    section, slab, swap = place[0], place[1], place[2]
    origin = place[3]
    chunk = chunk_y * depth
    chunks = rows_y // chunk_y
    per_owner = rows_y // slabs
    span = windows[0].shape[3]
    half_taps = first.shape[0]
    zs = lax.broadcasted_iota(jnp.int32, (depth, LANES), 0)
    in_grid = ((zs + origin >= 0) & (zs + origin < limit_z)).astype(F32)[None]
    mine = ((zs >= HALO) & (zs < HALO + width)).astype(F32)[None]

    def other(tap):
        index = tap % half_taps
        return jnp.where(swap // 2 == tap // half_taps, first[index], second[index])

    def prepare(pair, carry):
        for half in range(2):
            layer = 2 * pair + half
            for b in range(3):
                for c in range(3):
                    taps = []
                    for a in range(3):
                        tap = 9 * a + 3 * b + c
                        both = jnp.where(pair == section, own[tap], other(tap))
                        taps.append(both[:, half * chans : (half + 1) * chans])
                    top = jnp.concatenate([taps[1], taps[2]], axis=1)
                    low = jnp.concatenate([taps[0], taps[1]], axis=1)
                    block = jnp.concatenate([top, low], axis=0)
                    for target, value, row, col in (
                        (fwd, block.T, b, c),
                        (bwd, block, 2 - b, 2 - c),
                    ):
                        hi, lo = split_terms(value)
                        at = slice(col * LANES, (col + 1) * LANES)
                        target[layer, 2 * row * LANES : (2 * row + 1) * LANES, at] = hi
                        target[layer, (2 * row + 1) * LANES : (2 * row + 2) * LANES, at] = hi
                        target[layer, (6 + row) * LANES : (7 + row) * LANES, at] = lo
        return carry

    lax.fori_loop(0, 2, prepare, 0)

    def over_chunks(body):
        if chunks == 1:
            for micro in range(micros):
                body(micro, 0, 0)
        else:

            def step(index, carry):
                part = index % chunks
                body(index // chunks, part, pl.multiple_of(part * chunk, 16))
                return carry

            lax.fori_loop(0, micros * chunks, step, 0)

    def put_rows(target, lead, start, values):
        hi, lo = split_terms(values)
        at = pl.ds(start + depth, chunk)
        target[(*lead, at, slice(0, LANES))] = hi
        target[(*lead, at, slice(LANES, 2 * LANES))] = lo

    def pieces_of(source, lead, start):
        return [source[(*lead, pl.ds(start + b * depth, chunk), slice(None))] for b in range(3)]

    def conv(source, lead, start, table):
        pieces = pieces_of(source, lead, start)
        left = jnp.concatenate(pieces + [piece[:, :LANES] for piece in pieces], axis=1)
        out = jnp.dot(left, table[...], preferred_element_type=F32)
        before = pltpu.roll(out[:, :LANES], 1, 0)
        after = pltpu.roll(out[:, 2 * LANES :], chunk - 1, 0)
        return before + out[:, LANES : 2 * LANES] + after

    def masked(values, mask):
        return (values.reshape(chunk_y, depth, LANES) * mask).reshape(chunk, LANES)

    blank = jnp.zeros((depth, 2 * LANES), BF16)
    for micro in range(micros):
        for edge in (0, rows_y + 1):
            at = slice(edge * depth, (edge + 1) * depth)
            for layer in range(4):
                acts[layer, micro, at, :] = blank
            for side in range(2):
                rim[side, micro, at, :] = blank

    def emit(target, micro, part, values):
        inner = values.reshape(chunk_y, depth, LANES)[:, HALO : HALO + width, :]
        for y in range(chunk_y):
            row = part * chunk_y + y
            to = lax.rem(row // per_owner + slabs - slab, slabs)
            target[to, micro, row % per_owner] = inner[y]

    def place_cells(which, write):
        for micro in range(micros):
            for turn, window in enumerate(windows):
                owner = lax.rem(slab + slabs - turn, slabs)
                for y in range(per_owner):
                    value = window[which, micro, y]
                    if span < depth:
                        value = jnp.concatenate(
                            [value, jnp.zeros((depth - span, LANES), F32)], axis=0
                        )
                    row = owner * per_owner + y
                    write(micro, pl.multiple_of(row * depth, 16), value)

    def place_edges(which, add):
        left = slab < reach
        at = jnp.where(left, 0, HALO + width)

        @pl.when(left | (slab >= slabs - reach))
        def _():
            for m, edge in enumerate(edges):
                owner = jnp.where(left, m, (m + 1) % slabs)
                for micro in range(micros):
                    for y in range(per_owner):
                        start = (owner * per_owner + y) * depth + at
                        add(micro, pl.multiple_of(start, 8), edge[which, micro, y])

    def fill(which):
        def write(micro, start, value):
            field[micro, pl.ds(start, depth), :] = value

        def add(micro, start, value):
            field[micro, pl.ds(start, HALO), :] += value

        place_cells(which, write)
        place_edges(which, add)

    fill(0)
    over_chunks(
        lambda micro, part, start: put_rows(
            acts, (0, micro), start, field[micro, pl.ds(start, chunk), :]
        )
    )

    for layer in range(4):
        half = layer % 2

        def forward(micro, part, start):
            row = jnp.where(section == layer // 2, own[27, 0:1, :], other(27)[0:1, :])
            bias = row[:, half * chans : (half + 1) * chans]
            bias = jnp.concatenate([bias, bias], axis=1)
            pre = conv(acts, (layer, micro), start, fwd.at[layer]) + bias
            grown = 1.0 + jnp.exp(-pre)
            sigma = 1.0 / grown
            kept[layer, micro, pl.ds(start, chunk), :] = sigma * (1.0 + pre * (1.0 - sigma))
            out = masked(pre / grown, in_grid)
            if layer < 3:
                put_rows(acts, (layer + 1, micro), start, out)
            if half == 1:
                pl.when(section == layer // 2)(lambda: emit(front, micro, part, out))

        over_chunks(forward)

    def take_gradient(layer, micro, start, gradient):
        slope = masked(gradient * kept[layer, micro, pl.ds(start, chunk), :], in_grid)
        slopes[layer, micro, pl.ds(start, chunk), :] = masked(slope, mine)
        put_rows(rim, (layer % 2, micro), start, slope)

    fill(1)
    over_chunks(
        lambda micro, part, start: take_gradient(
            3, micro, start, field[micro, pl.ds(start, chunk), :]
        )
    )

    def backward(layer):
        def pull(micro, part, start):
            gradient = conv(rim, (layer % 2, micro), start, bwd.at[layer])
            if layer > 0:
                take_gradient(layer - 1, micro, start, gradient)
            if layer % 2 == 0:
                pl.when(section == layer // 2)(lambda: emit(back, micro, part, gradient))

        over_chunks(pull)

    backward(3)
    backward(2)

    @pl.when(section == 0)
    def _():
        backward(1)
        backward(0)

    def spot(tap):
        quarter = sums.shape[0] // 4
        return (tap // quarter ^ swap) * quarter + tap % quarter

    sums[spot(27)] = jnp.zeros((chans, LANES), F32)
    for slot in range(2):
        layer = 2 * section + slot
        acc[...] = jnp.zeros(acc.shape, F32)

        def gather(micro, part, start):
            slope = slopes[layer, micro, pl.ds(start, chunk), :]
            moved = [pltpu.roll(slope, 1 if c == 0 else chunk - 1, 0) if c != 1 else slope for c in (2, 1, 0)]
            terms = [split_terms(value) for value in moved]
            left_hi = jnp.concatenate([hi for hi, lo in terms], axis=1)
            left_lo = jnp.concatenate([lo for hi, lo in terms], axis=1)
            pieces = pieces_of(acts, (layer, micro), start)
            full = jnp.concatenate(pieces, axis=1)
            high = jnp.concatenate([piece[:, :LANES] for piece in pieces], axis=1)
            over_rows = (((0,), (0,)), ((), ()))
            one = lax.dot_general(left_hi, full, over_rows, preferred_element_type=F32)
            two = lax.dot_general(left_lo, high, over_rows, preferred_element_type=F32)
            for b in range(3):
                at = slice(b * LANES, (b + 1) * LANES)
                acc[0 : 3 * LANES, at] += (
                    one[:, 2 * b * LANES : (2 * b + 1) * LANES]
                    + one[:, (2 * b + 1) * LANES : (2 * b + 2) * LANES]
                    + two[:, at]
                )
            acc[3 * LANES : 3 * LANES + 1, 0:LANES] += jnp.sum(slope, axis=0, keepdims=True)

        over_chunks(gather)
        lanes = slice(slot * chans, (slot + 1) * chans)
        for b in range(3):
            for c in range(3):
                block = acc[c * LANES : (c + 1) * LANES, b * LANES : (b + 1) * LANES] * scale
                tap = 3 * b + c
                sums[spot(tap), :, lanes] = block[chans:, :chans]
                sums[spot(9 + tap), :, lanes] = block[:chans, :chans] + block[chans:, chans:]
                sums[spot(18 + tap), :, lanes] = block[:chans, chans:]
        row = acc[3 * LANES : 3 * LANES + 1, 0:LANES] * scale
        sums[spot(27), 0:1, lanes] = row[:, :chans] + row[:, chans:]


def packed(weights, biases):
    pair = jnp.concatenate([weights[0], weights[1]], axis=-1)
    row = jnp.concatenate([biases[0], biases[1]])[None, None, :]
    tail = jnp.pad(row, ((0, 0), (0, pair.shape[1] - 1), (0, 0)))
    return jnp.concatenate([pair, tail], axis=0)


def turned(block, distance):
    count = lax.axis_size("gy")
    return lax.ppermute(block, "gy", [(i, (i + distance) % count) for i in range(count)])


def spread(blocks):
    slabs = len(blocks)
    if slabs <= 8:
        return [blocks[0]] + [turned(blocks[turn], turn) for turn in range(1, slabs)]
    slab = lax.axis_index("gy")
    got = lax.all_to_all(jnp.roll(jnp.stack(blocks), slab, axis=0), "gy", 0, 0)
    got = jnp.roll(got[::-1], slab + 1, axis=0)
    return [got[turn] for turn in range(slabs)]


def swapped(block, bit):
    count = lax.axis_size("gz")
    return lax.ppermute(block, "gz", [(i, i ^ bit) for i in range(count)])


def unpack_kernel(chunk, place, *rest):
    slab, swap = place[1], place[2]
    near, rest = rest[:-5], rest[-5:]
    beside, across, weight, bias, whole = rest
    slabs = len(near)
    quarter = slabs * chunk
    chans = weight.shape[-1]

    def put(relative, turn, values):
        at = (relative ^ swap) * quarter + lax.rem(slab + slabs - turn, slabs) * chunk
        whole[pl.ds(pl.multiple_of(at, 8), chunk), :] = values

    for turn in range(slabs):
        rows = slice(turn * chunk, (turn + 1) * chunk)
        put(0, turn, near[turn][...])
        put(1, turn, beside[rows, :])
        for part in range(2):
            put(2 + part, turn, across[part * quarter + rows.start : part * quarter + rows.stop, :])
    for layer in range(2):
        lanes = slice(layer * chans, (layer + 1) * chans)
        for tap in range(28):
            at = tap // 7 * quarter + tap % 7 * chans
            if tap < 27:
                weight[layer, tap] = whole[at : at + chans, lanes]
            else:
                bias[layer : layer + 1, :] = whole[at : at + 1, lanes]


def summed_over_grid(block, place, chans):
    slabs = lax.axis_size("gy")
    slab = lax.axis_index("gy")
    for bit in (1, 2):
        rows = block.shape[0] // 2
        block = block[:rows] + swapped(block[rows:], bit)
    chunk = -(-block.shape[0] // (8 * slabs)) * 8
    block = jnp.pad(block, ((0, slabs * chunk - block.shape[0]), (0, 0)))
    parts = block.reshape(slabs, chunk, LANES)

    def part_for(turn):
        return lax.dynamic_index_in_dim(parts, (slab + turn) % slabs, 0, keepdims=False)

    mine = sum(spread([part_for(turn) for turn in range(slabs)]))
    near = spread([mine] * slabs)
    quarter = jnp.concatenate(near, axis=0)
    beside = swapped(quarter, 2)
    across = swapped(jnp.concatenate([quarter, beside], axis=0), 1)
    vmem = pl.BlockSpec(memory_space=pltpu.VMEM)
    return pl.pallas_call(
        functools.partial(unpack_kernel, chunk),
        out_shape=(
            jax.ShapeDtypeStruct((2, 27, chans, chans), F32),
            jax.ShapeDtypeStruct((2, chans), F32),
        ),
        in_specs=[pl.BlockSpec(memory_space=pltpu.SMEM)] + [vmem] * (slabs + 2),
        out_specs=(vmem, vmem),
        scratch_shapes=[pltpu.VMEM((4 * slabs * chunk, LANES), F32)],
        compiler_params=pltpu.CompilerParams(vmem_limit_bytes=16 * 1024 * 1024),
        name="unpack",
    )(place, *near, beside, across)


def restored(parts, size_x, chans):
    slabs, micros, local_y, width, _ = parts.shape
    slab = lax.axis_index("gy")
    got = spread([parts[turn] for turn in range(slabs)])
    twice = jnp.stack((got[::-1] * 2)[: 2 * slabs - 1])
    whole = lax.dynamic_slice_in_dim(twice, slabs - 1 - slab, slabs, 0)
    whole = whole.reshape(slabs, micros, local_y, width, size_x, chans)
    whole = whole.transpose(1, 5, 4, 2, 0, 3)
    return whole.reshape(1, micros, chans, size_x, local_y, slabs * width)


def edge_piece(fields, owner, reach):
    slabs, columns = lax.axis_size("gy"), lax.axis_size("gz")
    local_z = fields.shape[3]
    width = local_z // slabs
    follower = (owner + 1) % slabs
    whole = 0.0
    for r in range(reach):
        low = fields[:, :, :, local_z - HALO + r * width :]
        low = jnp.pad(low, ((0, 0),) * 3 + ((0, r * width), (0, 0)))
        high = fields[:, :, :, : HALO - r * width]
        high = jnp.pad(high, ((0, 0),) * 3 + ((r * width, 0), (0, 0)))
        route = [(owner * columns + g, r * columns + g + 1) for g in range(columns - 1)]
        last = (slabs - 1 - r) * columns
        route += [(follower * columns + g, last + g - 1) for g in range(1, columns)]
        sent = jnp.where(lax.axis_index("gy") == owner, low, high)
        whole = whole + lax.ppermute(sent, ("gy", "gz"), route) if r else lax.ppermute(sent, ("gy", "gz"), route)
    return whole


def per_device(inflow, weights, biases, cotangent):
    micros, chans, size_x, local_y, local_z = inflow.shape
    slabs, columns = lax.axis_size("gy"), lax.axis_size("gz")
    rows_y = local_y * slabs
    width = local_z // slabs
    span = width + 2 * HALO
    reach = -(-HALO // width)
    depth = -(-span // 16) * 16
    chunk_y = max(n for n in range(1, rows_y + 1) if rows_y % n == 0 and n * depth <= 384)
    scale = 1.0 / math.sqrt(micros * size_x * rows_y * local_z * columns)
    section = lax.axis_index("section")
    slab, column = lax.axis_index("gy"), lax.axis_index("gz")
    swap = 2 * (column % 2) + column // 2 % 2

    own = packed(weights, biases)
    half = own.shape[0] // 2
    sent = jnp.where(column % 2 == 1, own[half:], own[:half])
    first = lax.ppermute(sent, "section", [(0, 1), (1, 0)])
    second = swapped(first, 1)

    fields = jnp.stack([inflow, cotangent]).transpose(0, 1, 4, 5, 3, 2)
    fields = fields.reshape(2, micros, local_y, local_z, size_x * chans)
    wide = jnp.pad(fields, ((0, 0),) * 3 + ((HALO, HALO), (0, 0)))
    edges = []
    if slabs > 8:
        up = [(i, i + 1) for i in range(columns - 1)]
        down = [(i + 1, i) for i in range(columns - 1)]
        before = lax.ppermute(fields[:, :, :, local_z - HALO :], "gz", up)
        after = lax.ppermute(fields[:, :, :, :HALO], "gz", down)
        wide = jnp.concatenate([before, fields, after], axis=3)
    else:
        for m in range(slabs):
            edges.append(edge_piece(fields, m, reach))

    def window(turn):
        return lax.dynamic_slice_in_dim(wide, (slab + turn) % slabs * width, span, axis=3)

    windows = spread([window(turn) for turn in range(slabs)])

    origin = column * local_z + slab * width - HALO
    place = jnp.stack([section, slab, swap, origin]).astype(jnp.int32)
    dims = (
        (micros, rows_y, depth, width, chunk_y, chans, local_z * columns, scale, slabs, reach)
    )
    padded = (rows_y + 2) * depth
    full = rows_y * depth
    vmem = pl.BlockSpec(memory_space=pltpu.VMEM)
    piece = jax.ShapeDtypeStruct((slabs, micros, local_y, width, LANES), F32)
    scratch = [
        pltpu.VMEM((4, 9 * LANES, 3 * LANES), BF16),
        pltpu.VMEM((4, 9 * LANES, 3 * LANES), BF16),
        pltpu.VMEM((4, micros, padded, 2 * LANES), BF16),
        pltpu.VMEM((2, micros, padded, 2 * LANES), BF16),
        pltpu.VMEM((4, micros, full, LANES), F32),
        pltpu.VMEM((4, micros, full, LANES), F32),
        pltpu.VMEM((micros, full, LANES), F32),
        pltpu.VMEM((3 * LANES + 8, 3 * LANES), F32),
    ]
    held = sum(math.prod(item.shape) * item.dtype.itemsize for item in scratch)
    held += 4 * (2 * 28 * chans * LANES + 6 * micros * full * LANES)
    front, back, sums = pl.pallas_call(
        functools.partial(slab_kernel, dims),
        out_shape=(piece, piece, jax.ShapeDtypeStruct((28, chans, LANES), F32)),
        in_specs=[pl.BlockSpec(memory_space=pltpu.SMEM)] + [vmem] * (3 + slabs + len(edges)),
        out_specs=(vmem, vmem, vmem),
        scratch_shapes=scratch,
        compiler_params=pltpu.CompilerParams(vmem_limit_bytes=held + 8 * 1024 * 1024),
        name="slab",
    )(place, own, first, second, *windows, *edges)

    weight_total, bias_total = summed_over_grid(sums.reshape(28 * chans, LANES), place, chans)
    section_out = restored(front, size_x, chans)
    section_grad = restored(back, size_x, chans)
    return (section_out, section_grad, weight_total, bias_total)


def solution(mesh):
    grid = P(None, None, None, "gy", "gz")
    section_grid = P("section", None, None, None, "gy", "gz")
    return jax.shard_map(
        per_device,
        mesh=mesh,
        in_specs=(grid, P("section", None, None, None), P("section", None), grid),
        out_specs=(section_grid, section_grid, P("section", None, None, None), P("section", None)),
        check_vma=False,
    )
```

time: 129 us -> 117 us (0.907)
  starting transfers between devices: 22.5 us -> 49.2 us
  blocking collectives: 22.8 us -> 0 us
  waiting for transfers between devices: 52.9 us -> 43.7 us
  local copies, waits for them, and re-layouts: 9.1 us -> 5.58 us
  other arithmetic: 4.15 us -> 0.81 us
    ppermute x3 -> x25, starting transfers between devices: 5.21 us -> 49.2 us  [the longest x15 24 us: turned(): lax.ppermute(block, 'gy', [(i, (i + distance) % count) for i in range(cou...]
    all_to_all x4 -> x0, waiting for transfers between devices: 30.8 us -> none  [the longest x2 17.2 us: summed_over_grid(): block = jnp.sum(lax.all_to_all(parts, axis, 0, 0), axis=0)]
    all_gather x2 -> x0, blocking collectives: 22.8 us -> none  [summed_over_grid(): block = lax.all_gather(block, axis, tiled=True)]
    ppermute x3 -> x25, waiting for transfers between devices: 22.1 us -> 43.7 us  [the longest x15 19.4 us: turned(): lax.ppermute(block, 'gy', [(i, (i + distance) % count) for i in range(cou...]
    all_to_all x4 -> x0, starting transfers between devices: 17.3 us -> none  [the longest x2 7.02 us: summed_over_grid(): block = jnp.sum(lax.all_to_all(parts, axis, 0, 0), axis=0)]
    another operation x4 -> x1, other arithmetic: 2.99 us -> 0.08 us  [per_device(): place = jnp.stack([section, slab, swap, origin]).astype(jnp.int32)]
    unnamed x12 -> x21, local copies, waits for them, and re-layouts: 3.63 us -> 1.89 us
    pallas_call x1 -> x2, Pallas kernels: 15.8 us -> 16.2 us  [the longest x1 14 us: per_device(): pl.pallas_call(functools.partial(slab_kernel, dims), out_shape=(piece, pi...]
  transfers between devices with their start and end apart: 7 -> 25, of which waited for: 5 -> 10; matrix products, arithmetic and copies ran while one was open for 5% -> 3% of each run, Pallas kernels for 0% -> 0%
where the time goes in v2:
time: 117 us
  starting transfers between devices  49.2 us (42%)
  waiting for transfers between devices  43.7 us (37%)
  Pallas kernels  16.2 us (14%)
  local copies, waits for them, and re-layouts  5.58 us (5%)
    ppermute x15, starting transfers between devices, turned(): lax.ppermute(block, 'gy', [(i, (i + distance) % count) for i in range(cou...  24 us
    ppermute x4, starting transfers between devices, edge_piece(): lax.ppermute(sent, ('gy', 'gz'), route)  19.8 us
    ppermute x15, waiting for transfers between devices, turned(): lax.ppermute(block, 'gy', [(i, (i + distance) % count) for i in range(cou...  19.4 us
    pallas_call x1, Pallas kernels, per_device(): pl.pallas_call(functools.partial(slab_kernel, dims), out_shape=(piece, pi...  14 us
    ppermute x5, waiting for transfers between devices, swapped(): return lax.ppermute(block, 'gz', [(i, i ^ bit) for i in range(count)])  13.3 us
    ppermute x1, waiting for transfers between devices, per_device(): first = lax.ppermute(sent, 'section', [(0, 1), (1, 0)])  10.2 us
    ppermute x1, starting transfers between devices, per_device(): first = lax.ppermute(sent, 'section', [(0, 1), (1, 0)])  3 us
    ppermute x5, starting transfers between devices, swapped(): return lax.ppermute(block, 'gz', [(i, i ^ bit) for i in range(count)])  2.45 us
  transfers between devices with their start and end apart: 25, of which 10 were waited for; matrix products, arithmetic and copies ran while one was open for 3% of the time, Pallas kernels for 0%

profile of v2, /device:TPU:0, one launch (start us, length us, event | category | flops | bytes accessed | tf_op | source)
XLA Modules:
  0.0 116.5 jit_solution(5098254486327726080)
XLA Ops:
  0.6 0.8 slice_bitcast_fusion.9
  1.4 1.6 %slice_bitcast_fusion.1 = (f32[27,64,64]{2,1,0:T(8,128)S(1)}, f32[27,64,64]{2,1,0:T(8,128)S(1)}) fusion(f32[2,27,64,64]{3,2,1,0:T(8,128)} %param.5), kind=kLoop, calls=%fused_computation.3 | loop fusion | bytes 1769472 | tf_op jit(solution)/shard_map/squeeze | solution.py:253
  3.0 0.1 maximum_bitcast_fusion
  3.1 0.3 select_maximum_fusion.own
  3.4 0.0 copy-start
  3.4 0.0 copy-start.1
  3.4 0.2 fusion
  3.6 3.0 %collective-permute-start = (f32[14,64,128]{2,1,0:T(8,128)S(1)}, f32[14,64,128]{2,1,0:T(8,128)S(1)}, u32[]{:S(2)}, u32[]{:S(2)}) collective-permute-start(f32[14,64,128]{2,1,0:T(8,128)S(1)} %fusion), channel_id=1, source_target_pairs={{0,16},{16,0},{1,17},{17,1},{2,18},{18,2},{3,19},{19,3},{4,20},{20... | collective-permute-start | bytes 1376264 | tf_op jit(solution)/shard_map/ppermute | solution.py:387
  6.7 0.1 copy_bitcast_fusion
  6.8 0.2 copy.11
  7.0 10.2 %collective-permute-done.first = f32[14,64,128]{2,1,0:T(8,128)S(1)} collective-permute-done((f32[14,64,128]{2,1,0:T(8,128)S(1)}, f32[14,64,128]{2,1,0:T(8,128)S(1)}, u32[]{:S(2)}, u32[]{:S(2)}) %collective-permute-start) | collective-permute-done | bytes 458784 | tf_op jit(solution)/shard_map/ppermute | solution.py:387
  17.2 0.0 collective-permute-start.1
  17.2 0.7 collective-permute-start.8
  17.9 0.1 pad_dynamic-slice_fusion
  18.0 5.2 %collective-permute-start.4 = (f32[2,2,2,48,128]{4,3,2,1,0:T(8,128)S(1)}, f32[2,2,2,48,128]{4,3,2,1,0:T(8,128)S(1)}, u32[]{:S(2)}, u32[]{:S(2)}) collective-permute-start(f32[2,2,2,48,128]{4,3,2,1,0:T(8,128)S(1)} %get-tuple-element.28), channel_id=1, source_target_pairs={{0,12},{4,0},{8,4},{12,8},{1,13},{5,1},{9,5},{13,9},{2,14},{6,2},{... | collective-permute-start | bytes 589832 | tf_op jit(solution)/shard_map/ppermute | solution.py:261
  23.2 0.0 collective-permute-start.2
  23.2 0.6 collective-permute-start.3
  23.9 0.0 collective-permute-done.8.rest_7_
  23.9 0.7 collective-permute-start.7
  24.5 0.0 collective-permute-done.7.rest_6_
  24.5 17.8 %collective-permute-start.5 = (f32[2,2,2,8,128]{4,3,2,1,0:T(8,128)S(1)}, f32[2,2,2,8,128]{4,3,2,1,0:T(8,128)S(1)}, u32[]{:S(2)}, u32[]{:S(2)}) collective-permute-start(f32[2,2,2,8,128]{4,3,2,1,0:T(8,128)S(1)} %get-tuple-element.26), channel_id=1, source_target_pairs={{0,1},{1,2},{2,3},{5,12},{6,13},{7,14},{16,17},{17,18},{18,19},{21... | collective-permute-start | bytes 98312 | tf_op jit(solution)/shard_map/ppermute | solution.py:366
  42.4 0.8 collective-permute-done.5.rest_4_
  43.2 0.7 collective-permute-start.6
  43.9 0.1 pad_add_fusion.place
  43.9 0.0 collective-permute-done.6.rest_5_
  43.9 0.0 collective-permute-done.4.rest_3_
  43.9 0.0 collective-permute-done.2.rest_1_
  43.9 0.0 collective-permute-done.3.rest_2_
  44.0 0.0 collective-permute-done.1.second
  44.0 14.0 %slab.1 = (f32[4,2,2,32,128]{4,3,2,1,0:T(8,128)S(1)}, f32[4,2,2,32,128]{4,3,2,1,0:T(8,128)S(1)}, f32[28,64,128]{2,1,0:T(8,128)S(1)}) custom-call(s32[4]{0:T(128)S(1)} %pad_add_fusion.place, f32[28,64,128]{2,1,0:T(8,128)S(1)} %select_maximum_fusion.own, f32[14,64,128]{2,1,0:T(8,128)S(1)} %collective-permute-done.first, ...), custom_call_target="tpu_custom_call" | custom-call | tf_op jit(solution)/shard_map/slab/pallas_call | solution.py:430
  58.0 0.1 fusion.4
  58.1 4.7 %collective-permute-start.12 = (f32[2,2,32,128]{3,2,1,0:T(8,128)S(1)}, f32[2,2,32,128]{3,2,1,0:T(8,128)S(1)}, u32[]{:S(2)}, u32[]{:S(2)}) collective-permute-start(f32[2,2,32,128]{3,2,1,0:T(8,128)S(1)} %get-tuple-element.34), channel_id=1, source_target_pairs={{0,12},{4,0},{8,4},{12,8},{1,13},{5,1},{9,5},{13,9},{2,14},{6,2},{... | collective-permute-start | bytes 196616 | tf_op jit(solution)/shard_map/ppermute | solution.py:261
  62.8 2.1 %collective-permute-start.11 = (f32[2,2,32,128]{3,2,1,0:T(8,128)S(1)}, f32[2,2,32,128]{3,2,1,0:T(8,128)S(1)}, u32[]{:S(2)}, u32[]{:S(2)}) collective-permute-start(f32[2,2,32,128]{3,2,1,0:T(8,128)S(1)} %get-tuple-element.35), channel_id=1, source_target_pairs={{0,4},{4,8},{8,12},{12,0},{1,5},{5,9},{9,13},{13,1},{2,6},{6,10},{... | collective-permute-start | bytes 196616 | tf_op jit(solution)/shard_map/ppermute | solution.py:261
  65.0 1.5 %collective-permute-start.10 = (f32[2,2,32,128]{3,2,1,0:T(8,128)S(1)}, f32[2,2,32,128]{3,2,1,0:T(8,128)S(1)}, u32[]{:S(2)}, u32[]{:S(2)}) collective-permute-start(f32[2,2,32,128]{3,2,1,0:T(8,128)S(1)} %get-tuple-element.36), channel_id=1, source_target_pairs={{0,8},{4,12},{8,0},{12,4},{1,9},{5,13},{9,1},{13,5},{2,10},{6,14},... | collective-permute-start | bytes 196616 | tf_op jit(solution)/shard_map/ppermute | solution.py:261
  66.5 2.8 %collective-permute-start.9 = (f32[2,2,32,128]{3,2,1,0:T(8,128)S(1)}, f32[2,2,32,128]{3,2,1,0:T(8,128)S(1)}, u32[]{:S(2)}, u32[]{:S(2)}) collective-permute-start(f32[2,2,32,128]{3,2,1,0:T(8,128)S(1)} %get-tuple-element.37), channel_id=1, source_target_pairs={{0,12},{4,0},{8,4},{12,8},{1,13},{5,1},{9,5},{13,9},{2,14},{6,2},{... | collective-permute-start | bytes 196616 | tf_op jit(solution)/shard_map/ppermute | solution.py:261
  69.4 0.6 collective-permute-start.13
  70.0 8.6 %collective-permute-done.13 = f32[2,2,32,128]{3,2,1,0:T(8,128)S(1)} collective-permute-done((f32[2,2,32,128]{3,2,1,0:T(8,128)S(1)}, f32[2,2,32,128]{3,2,1,0:T(8,128)S(1)}, u32[]{:S(2)}, u32[]{:S(2)}) %collective-permute-start.13) | collective-permute-done | bytes 65568 | tf_op jit(solution)/shard_map/ppermute | solution.py:261
  78.6 0.4 collective-permute-start.15
  79.0 0.0 collective-permute-done.9
  79.0 0.0 collective-permute-done.10
  79.1 1.3 %collective-permute-done.15 = f32[896,128]{1,0:T(8,128)S(1)} collective-permute-done((f32[896,128]{1,0:T(8,128)S(1)}, f32[896,128]{1,0:T(8,128)S(1)}, u32[]{:S(2)}, u32[]{:S(2)}) %collective-permute-start.15) | collective-permute-done | bytes 458784 | tf_op jit(solution)/shard_map/ppermute | solution.py:276
  80.5 1.1 collective-permute-start.16
  81.6 6.8 %collective-permute-done.16 = f32[448,128]{1,0:T(8,128)S(1)} collective-permute-done((f32[448,128]{1,0:T(8,128)S(1)}, f32[448,128]{1,0:T(8,128)S(1)}, u32[]{:S(2)}, u32[]{:S(2)}) %collective-permute-start.16) | collective-permute-done | bytes 229408 | tf_op jit(solution)/shard_map/ppermute | solution.py:276
  88.5 0.1 collective-permute-start.17
  88.6 3.8 %collective-permute-start.19 = (f32[112,128]{1,0:T(8,128)S(1)}, f32[112,128]{1,0:T(8,128)S(1)}, u32[]{:S(2)}, u32[]{:S(2)}) collective-permute-start(f32[112,128]{1,0:T(8,128)S(1)} %get-tuple-element.39), channel_id=1, source_target_pairs={{0,12},{4,0},{8,4},{12,8},{1,13},{5,1},{9,5},{13,9},{2,14},{6,2},{... | collective-permute-start | bytes 172040 | tf_op jit(solution)/shard_map/ppermute | solution.py:261
  92.4 0.0 collective-permute-start.18
  92.4 2.6 %collective-permute-done.17 = f32[112,128]{1,0:T(8,128)S(1)} collective-permute-done((f32[112,128]{1,0:T(8,128)S(1)}, f32[112,128]{1,0:T(8,128)S(1)}, u32[]{:S(2)}, u32[]{:S(2)}) %collective-permute-start.17) | collective-permute-done | bytes 57376 | tf_op jit(solution)/shard_map/ppermute | solution.py:261
  94.9 2.8 %collective-permute-done.18 = f32[112,128]{1,0:T(8,128)S(1)} collective-permute-done((f32[112,128]{1,0:T(8,128)S(1)}, f32[112,128]{1,0:T(8,128)S(1)}, u32[]{:S(2)}, u32[]{:S(2)}) %collective-permute-start.18) | collective-permute-done | bytes 57376 | tf_op jit(solution)/shard_map/ppermute | solution.py:261
  97.8 1.5 %collective-permute-start.22 = (f32[112,128]{1,0:T(8,128)S(1)}, f32[112,128]{1,0:T(8,128)S(1)}, u32[]{:S(2)}, u32[]{:S(2)}) collective-permute-start(f32[112,128]{1,0:T(8,128)S(1)} %get-tuple-element.19.rest_0_), channel_id=1, source_target_pairs={{0,12},{4,0},{8,4},{12,8},{1,13},{5,1},{9,5},{13,9},{2,14},{6,2},{... | collective-permute-start | bytes 172040 | tf_op jit(solution)/shard_map/ppermute | solution.py:261
  99.3 0.0 collective-permute-start.21
  99.3 1.0 collective-permute-start.20
  100.3 2.2 %collective-permute-done.22.rest_3_ = f32[112,128]{1,0:T(8,128)S(1)} collective-permute-done((f32[112,128]{1,0:T(8,128)S(1)}, f32[112,128]{1,0:T(8,128)S(1)}, u32[]{:S(2)}, u32[]{:S(2)}) %collective-permute-start.22) | collective-permute-done | bytes 57376 | tf_op jit(solution)/shard_map/ppermute | solution.py:261
  102.4 3.1 %collective-permute-done.21.rest_2_ = f32[112,128]{1,0:T(8,128)S(1)} collective-permute-done((f32[112,128]{1,0:T(8,128)S(1)}, f32[112,128]{1,0:T(8,128)S(1)}, u32[]{:S(2)}, u32[]{:S(2)}) %collective-permute-start.21) | collective-permute-done | bytes 57376 | tf_op jit(solution)/shard_map/ppermute | solution.py:261
  105.6 0.9 collective-permute-start.23
  106.5 5.2 %collective-permute-done.23.rest_4_ = f32[448,128]{1,0:T(8,128)S(1)} collective-permute-done((f32[448,128]{1,0:T(8,128)S(1)}, f32[448,128]{1,0:T(8,128)S(1)}, u32[]{:S(2)}, u32[]{:S(2)}) %collective-permute-start.23) | collective-permute-done | bytes 229408 | tf_op jit(solution)/shard_map/ppermute | solution.py:276
  111.7 0.1 collective-permute-start.24
  111.8 0.3 reshape.32
  112.2 0.1 copy.15
  112.2 0.9 copy.17
  113.1 0.3 reshape.30
  113.5 0.1 copy.14
  113.5 0.9 copy.16
  114.4 0.0 collective-permute-done.24.rest_5_
  114.4 2.1 %unpack.1 = (f32[2,27,64,64]{3,2,1,0:T(8,128)}, f32[2,64]{1,0:T(2,128)}) custom-call(s32[4]{0:T(128)S(1)} %pad_add_fusion.place, f32[112,128]{1,0:T(8,128)S(1)} %get-tuple-element.19.rest_0_, f32[112,128]{1,0:T(8,128)S(1)} %collective-permute-done.20.rest_1_, f32[112,128]{1,0:T(8,128)S(1)} %collective-permute-done.21.rest_2_, ...), custom_call_target="tpu_custom_call" | custom-call | tf_op jit(solution)/shard_map/unpack/pallas_call | solution.py:326
  (38 shorter events, 0.4 us)
Async XLA Ops:
  3.4 3.2 %copy-start = (f32[2,64,2,2,128]{4,3,2,1,0:T(2,128)S(1)}, f32[2,64,2,2,128]{4,3,2,1,0:T(2,128)}, u32[]{:S(2)}) copy-start(f32[2,64,2,2,128]{4,3,2,1,0:T(2,128)} %param.7) | copy-start | bytes 786436
  3.4 3.2 %copy-start.1 = (f32[2,64,2,2,128]{4,3,2,1,0:T(2,128)S(1)}, f32[2,64,2,2,128]{4,3,2,1,0:T(2,128)}, u32[]{:S(2)}) copy-start(f32[2,64,2,2,128]{4,3,2,1,0:T(2,128)} %param.4) | copy-start | bytes 786436
  3.6 13.5 %collective-permute-start = (f32[14,64,128]{2,1,0:T(8,128)S(1)}, f32[14,64,128]{2,1,0:T(8,128)S(1)}, u32[]{:S(2)}, u32[]{:S(2)}) collective-permute-start(f32[14,64,128]{2,1,0:T(8,128)S(1)} %fusion), channel_id=1, source_target_pairs={{0,16},{16,0},{1,17},{17,1},{2,18},{18,2},{3,19},{19,3},{4,20},{20... | collective-permute-start | bytes 1376264 | tf_op jit(solution)/shard_map/ppermute | solution.py:387
  17.2 26.8 %collective-permute-start.1 = (f32[14,64,128]{2,1,0:T(8,128)S(1)}, f32[14,64,128]{2,1,0:T(8,128)S(1)}, u32[]{:S(2)}, u32[]{:S(2)}) collective-permute-start(f32[14,64,128]{2,1,0:T(8,128)S(1)} %collective-permute-done.first), channel_id=1, source_target_pairs={{0,1},{1,0},{2,3},{3,2},{4,5},{5,4},{6,7},{7,6},{8,9},{9,8},{10,11... | collective-permute-start | bytes 1376264 | tf_op jit(solution)/shard_map/ppermute | solution.py:276
  17.2 6.7 %collective-permute-start.8 = (f32[2,2,2,8,128]{4,3,2,1,0:T(8,128)S(1)}, f32[2,2,2,8,128]{4,3,2,1,0:T(8,128)S(1)}, u32[]{:S(2)}, u32[]{:S(2)}) collective-permute-start(f32[2,2,2,8,128]{4,3,2,1,0:T(8,128)S(1)} %get-tuple-element.24), channel_id=1, source_target_pairs={{12,1},{13,2},{14,3},{1,12},{2,13},{3,14},{28,17},{29,18},{30,19},... | collective-permute-start | bytes 98312 | tf_op jit(solution)/shard_map/ppermute | solution.py:366
  18.0 25.9 %collective-permute-start.4 = (f32[2,2,2,48,128]{4,3,2,1,0:T(8,128)S(1)}, f32[2,2,2,48,128]{4,3,2,1,0:T(8,128)S(1)}, u32[]{:S(2)}, u32[]{:S(2)}) collective-permute-start(f32[2,2,2,48,128]{4,3,2,1,0:T(8,128)S(1)} %get-tuple-element.28), channel_id=1, source_target_pairs={{0,12},{4,0},{8,4},{12,8},{1,13},{5,1},{9,5},{13,9},{2,14},{6,2},{... | collective-permute-start | bytes 589832 | tf_op jit(solution)/shard_map/ppermute | solution.py:261
  23.2 20.7 %collective-permute-start.2 = (f32[2,2,2,48,128]{4,3,2,1,0:T(8,128)S(1)}, f32[2,2,2,48,128]{4,3,2,1,0:T(8,128)S(1)}, u32[]{:S(2)}, u32[]{:S(2)}) collective-permute-start(f32[2,2,2,48,128]{4,3,2,1,0:T(8,128)S(1)} %get-tuple-element.29), channel_id=1, source_target_pairs={{0,4},{4,8},{8,12},{12,0},{1,5},{5,9},{9,13},{13,1},{2,6},{6,10},{... | collective-permute-start | bytes 589832 | tf_op jit(solution)/shard_map/ppermute | solution.py:261
  23.2 20.7 %collective-permute-start.3 = (f32[2,2,2,48,128]{4,3,2,1,0:T(8,128)S(1)}, f32[2,2,2,48,128]{4,3,2,1,0:T(8,128)S(1)}, u32[]{:S(2)}, u32[]{:S(2)}) collective-permute-start(f32[2,2,2,48,128]{4,3,2,1,0:T(8,128)S(1)} %get-tuple-element.30), channel_id=1, source_target_pairs={{0,8},{4,12},{8,0},{12,4},{1,9},{5,13},{9,1},{13,5},{2,10},{6,14},... | collective-permute-start | bytes 589832 | tf_op jit(solution)/shard_map/ppermute | solution.py:261
  23.9 0.7 collective-permute-start.7
  24.5 18.7 %collective-permute-start.5 = (f32[2,2,2,8,128]{4,3,2,1,0:T(8,128)S(1)}, f32[2,2,2,8,128]{4,3,2,1,0:T(8,128)S(1)}, u32[]{:S(2)}, u32[]{:S(2)}) collective-permute-start(f32[2,2,2,8,128]{4,3,2,1,0:T(8,128)S(1)} %get-tuple-element.26), channel_id=1, source_target_pairs={{0,1},{1,2},{2,3},{5,12},{6,13},{7,14},{16,17},{17,18},{18,19},{21... | collective-permute-start | bytes 98312 | tf_op jit(solution)/shard_map/ppermute | solution.py:366
  43.2 0.7 collective-permute-start.6
  58.1 11.2 %collective-permute-start.12 = (f32[2,2,32,128]{3,2,1,0:T(8,128)S(1)}, f32[2,2,32,128]{3,2,1,0:T(8,128)S(1)}, u32[]{:S(2)}, u32[]{:S(2)}) collective-permute-start(f32[2,2,32,128]{3,2,1,0:T(8,128)S(1)} %get-tuple-element.34), channel_id=1, source_target_pairs={{0,12},{4,0},{8,4},{12,8},{1,13},{5,1},{9,5},{13,9},{2,14},{6,2},{... | collective-permute-start | bytes 196616 | tf_op jit(solution)/shard_map/ppermute | solution.py:261
  62.8 16.2 %collective-permute-start.11 = (f32[2,2,32,128]{3,2,1,0:T(8,128)S(1)}, f32[2,2,32,128]{3,2,1,0:T(8,128)S(1)}, u32[]{:S(2)}, u32[]{:S(2)}) collective-permute-start(f32[2,2,32,128]{3,2,1,0:T(8,128)S(1)} %get-tuple-element.35), channel_id=1, source_target_pairs={{0,4},{4,8},{8,12},{12,0},{1,5},{5,9},{9,13},{13,1},{2,6},{6,10},{... | collective-permute-start | bytes 196616 | tf_op jit(solution)/shard_map/ppermute | solution.py:261
  65.0 14.0 %collective-permute-start.10 = (f32[2,2,32,128]{3,2,1,0:T(8,128)S(1)}, f32[2,2,32,128]{3,2,1,0:T(8,128)S(1)}, u32[]{:S(2)}, u32[]{:S(2)}) collective-permute-start(f32[2,2,32,128]{3,2,1,0:T(8,128)S(1)} %get-tuple-element.36), channel_id=1, source_target_pairs={{0,8},{4,12},{8,0},{12,4},{1,9},{5,13},{9,1},{13,5},{2,10},{6,14},... | collective-permute-start | bytes 196616 | tf_op jit(solution)/shard_map/ppermute | solution.py:261
  66.5 12.5 %collective-permute-start.9 = (f32[2,2,32,128]{3,2,1,0:T(8,128)S(1)}, f32[2,2,32,128]{3,2,1,0:T(8,128)S(1)}, u32[]{:S(2)}, u32[]{:S(2)}) collective-permute-start(f32[2,2,32,128]{3,2,1,0:T(8,128)S(1)} %get-tuple-element.37), channel_id=1, source_target_pairs={{0,12},{4,0},{8,4},{12,8},{1,13},{5,1},{9,5},{13,9},{2,14},{6,2},{... | collective-permute-start | bytes 196616 | tf_op jit(solution)/shard_map/ppermute | solution.py:261
  69.4 9.6 %collective-permute-start.14 = (f32[2,2,32,128]{3,2,1,0:T(8,128)S(1)}, f32[2,2,32,128]{3,2,1,0:T(8,128)S(1)}, u32[]{:S(2)}, u32[]{:S(2)}) collective-permute-start(f32[2,2,32,128]{3,2,1,0:T(8,128)S(1)} %get-tuple-element.32), channel_id=1, source_target_pairs={{0,4},{4,8},{8,12},{12,0},{1,5},{5,9},{9,13},{13,1},{2,6},{6,10},{... | collective-permute-start | bytes 196616 | tf_op jit(solution)/shard_map/ppermute | solution.py:261
  69.4 9.2 %collective-permute-start.13 = (f32[2,2,32,128]{3,2,1,0:T(8,128)S(1)}, f32[2,2,32,128]{3,2,1,0:T(8,128)S(1)}, u32[]{:S(2)}, u32[]{:S(2)}) collective-permute-start(f32[2,2,32,128]{3,2,1,0:T(8,128)S(1)} %get-tuple-element.33), channel_id=1, source_target_pairs={{0,8},{4,12},{8,0},{12,4},{1,9},{5,13},{9,1},{13,5},{2,10},{6,14},... | collective-permute-start | bytes 196616 | tf_op jit(solution)/shard_map/ppermute | solution.py:261
  78.6 1.8 %collective-permute-start.15 = (f32[896,128]{1,0:T(8,128)S(1)}, f32[896,128]{1,0:T(8,128)S(1)}, u32[]{:S(2)}, u32[]{:S(2)}) collective-permute-start(f32[896,128]{1,0:T(8,128)S(1)} %bitcast.83), channel_id=1, source_target_pairs={{0,1},{1,0},{2,3},{3,2},{4,5},{5,4},{6,7},{7,6},{8,9},{9,8},{10,11... | collective-permute-start | bytes 1376264 | tf_op jit(solution)/shard_map/ppermute | solution.py:276
  80.5 7.9 %collective-permute-start.16 = (f32[448,128]{1,0:T(8,128)S(1)}, f32[448,128]{1,0:T(8,128)S(1)}, u32[]{:S(2)}, u32[]{:S(2)}) collective-permute-start(f32[448,128]{1,0:T(8,128)S(1)} %slice.98), channel_id=1, source_target_pairs={{0,2},{1,3},{2,0},{3,1},{4,6},{5,7},{6,4},{7,5},{8,10},{9,11},{10,... | collective-permute-start | bytes 688136 | tf_op jit(solution)/shard_map/ppermute | solution.py:276
  88.5 6.5 %collective-permute-start.17 = (f32[112,128]{1,0:T(8,128)S(1)}, f32[112,128]{1,0:T(8,128)S(1)}, u32[]{:S(2)}, u32[]{:S(2)}) collective-permute-start(f32[112,128]{1,0:T(8,128)S(1)} %get-tuple-element.38), channel_id=1, source_target_pairs={{0,4},{4,8},{8,12},{12,0},{1,5},{5,9},{9,13},{13,1},{2,6},{6,10},{... | collective-permute-start | bytes 172040 | tf_op jit(solution)/shard_map/ppermute | solution.py:261
  88.6 6.4 %collective-permute-start.19 = (f32[112,128]{1,0:T(8,128)S(1)}, f32[112,128]{1,0:T(8,128)S(1)}, u32[]{:S(2)}, u32[]{:S(2)}) collective-permute-start(f32[112,128]{1,0:T(8,128)S(1)} %get-tuple-element.39), channel_id=1, source_target_pairs={{0,12},{4,0},{8,4},{12,8},{1,13},{5,1},{9,5},{13,9},{2,14},{6,2},{... | collective-permute-start | bytes 172040 | tf_op jit(solution)/shard_map/ppermute | solution.py:261
  92.4 5.4 %collective-permute-start.18 = (f32[112,128]{1,0:T(8,128)S(1)}, f32[112,128]{1,0:T(8,128)S(1)}, u32[]{:S(2)}, u32[]{:S(2)}) collective-permute-start(f32[112,128]{1,0:T(8,128)S(1)} %get-tuple-element.40), channel_id=1, source_target_pairs={{0,8},{4,12},{8,0},{12,4},{1,9},{5,13},{9,1},{13,5},{2,10},{6,14},... | collective-permute-start | bytes 172040 | tf_op jit(solution)/shard_map/ppermute | solution.py:261
  97.8 4.6 %collective-permute-start.22 = (f32[112,128]{1,0:T(8,128)S(1)}, f32[112,128]{1,0:T(8,128)S(1)}, u32[]{:S(2)}, u32[]{:S(2)}) collective-permute-start(f32[112,128]{1,0:T(8,128)S(1)} %get-tuple-element.19.rest_0_), channel_id=1, source_target_pairs={{0,12},{4,0},{8,4},{12,8},{1,13},{5,1},{9,5},{13,9},{2,14},{6,2},{... | collective-permute-start | bytes 172040 | tf_op jit(solution)/shard_map/ppermute | solution.py:261
  99.3 6.3 %collective-permute-start.21 = (f32[112,128]{1,0:T(8,128)S(1)}, f32[112,128]{1,0:T(8,128)S(1)}, u32[]{:S(2)}, u32[]{:S(2)}) collective-permute-start(f32[112,128]{1,0:T(8,128)S(1)} %get-tuple-element.19.rest_0_), channel_id=1, source_target_pairs={{0,8},{4,12},{8,0},{12,4},{1,9},{5,13},{9,1},{13,5},{2,10},{6,14},... | collective-permute-start | bytes 172040 | tf_op jit(solution)/shard_map/ppermute | solution.py:261
  99.3 6.3 %collective-permute-start.20 = (f32[112,128]{1,0:T(8,128)S(1)}, f32[112,128]{1,0:T(8,128)S(1)}, u32[]{:S(2)}, u32[]{:S(2)}) collective-permute-start(f32[112,128]{1,0:T(8,128)S(1)} %get-tuple-element.19.rest_0_), channel_id=1, source_target_pairs={{0,4},{4,8},{8,12},{12,0},{1,5},{5,9},{9,13},{13,1},{2,6},{6,10},{... | collective-permute-start | bytes 172040 | tf_op jit(solution)/shard_map/ppermute | solution.py:261
  105.6 6.1 %collective-permute-start.23 = (f32[448,128]{1,0:T(8,128)S(1)}, f32[448,128]{1,0:T(8,128)S(1)}, u32[]{:S(2)}, u32[]{:S(2)}) collective-permute-start(f32[448,128]{1,0:T(8,128)S(1)} %pad_maximum_fusion.2), channel_id=1, source_target_pairs={{0,2},{1,3},{2,0},{3,1},{4,6},{5,7},{6,4},{7,5},{8,10},{9,11},{10,... | collective-permute-start | bytes 688136 | tf_op jit(solution)/shard_map/ppermute | solution.py:276
  111.7 2.7 %collective-permute-start.24 = (f32[896,128]{1,0:T(8,128)S(1)}, f32[896,128]{1,0:T(8,128)S(1)}, u32[]{:S(2)}, u32[]{:S(2)}) collective-permute-start(f32[896,128]{1,0:T(8,128)S(1)} %constant_dynamic-update-slice_fusion), channel_id=1, source_target_pairs={{0,1},{1,0},{2,3},{3,2},{4,5},{5,4},{6,7},{7,6},{8,9},{9,8},{10,11... | collective-permute-start | bytes 1376264 | tf_op jit(solution)/shard_map/ppermute | solution.py:276

commit v3 on v1

v3 whole, which is shorter than its diff:
```python
import functools
import math

import jax
import jax.numpy as jnp
from jax import lax
from jax.experimental import pallas as pl
from jax.experimental.pallas import tpu as pltpu
from jax.sharding import PartitionSpec as P

HALO = 8
LANES = 128
TAPS = 27
BLOCKS = 28
BF16 = jnp.bfloat16
F32 = jnp.float32
SMEM = pl.BlockSpec(memory_space=pltpu.SMEM)
VMEM = pl.BlockSpec(memory_space=pltpu.VMEM)


def call(kernel, name, outs, args, scratch=(), flops=0):
    arrays = [jax.ShapeDtypeStruct(shape, kind) for shape, kind in outs]
    size = sum(math.prod(item.shape) * item.dtype.itemsize for item in [*arrays, *args[1:], *scratch])
    return pl.pallas_call(
        kernel,
        out_shape=arrays,
        in_specs=[SMEM] + [VMEM] * (len(args) - 1),
        out_specs=[VMEM] * len(arrays),
        scratch_shapes=list(scratch),
        compiler_params=pltpu.CompilerParams(vmem_limit_bytes=size + 6 * 1024 * 1024),
        cost_estimate=pl.CostEstimate(flops=flops, bytes_accessed=size, transcendentals=0),
        name=name,
    )(*args)


def split_terms(values):
    high = values.astype(BF16)
    return high, (values - high.astype(F32)).astype(BF16)


def pack_kernel(place, weights, biases, own, sent):
    chans = weights.shape[2]
    half = sent.shape[0]
    for tap in range(TAPS):
        own[tap] = jnp.concatenate([weights[0, tap], weights[1, tap]], axis=1)
    own[TAPS] = jnp.zeros((chans, LANES), F32)
    own[TAPS, 0:1, :] = jnp.concatenate([biases[0:1, :], biases[1:2, :]], axis=1)
    start = place[2] // 2 * half

    def copy(index, carry):
        sent[index] = own[start + index]
        return carry

    lax.fori_loop(0, half, copy, 0)


def table_kernel(place, *refs):
    parts, (fwd, bwd, row) = refs[:-3], refs[-3:]
    swap = place[2]
    count = parts[0].shape[0]
    chans = parts[0].shape[1]

    def block_of(tap):
        if len(parts) == 1:
            return parts[0][tap]
        index = tap % count
        return jnp.where(swap // 2 == tap // count, parts[0][index], parts[1][index])

    for b in range(3):
        for c in range(3):
            taps = [block_of(9 * a + 3 * b + c) for a in range(3)]
            for layer in range(2):
                lanes = slice(layer * chans, (layer + 1) * chans)
                below, level, above = [tap[:, lanes] for tap in taps]
                top = jnp.concatenate([level, above], axis=1)
                low = jnp.concatenate([below, level], axis=1)
                block = jnp.concatenate([top, low], axis=0)
                for target, value, r, at in ((fwd, block.T, b, c), (bwd, block, 2 - b, 2 - c)):
                    hi, lo = split_terms(value)
                    at = slice(at * LANES, (at + 1) * LANES)
                    target[layer, 2 * r * LANES : (2 * r + 1) * LANES, at] = hi
                    target[layer, (2 * r + 1) * LANES : (2 * r + 2) * LANES, at] = hi
                    target[layer, (6 + r) * LANES : (7 + r) * LANES, at] = lo
    last = block_of(TAPS)[0:1, :]
    for layer in range(2):
        part = last[:, layer * chans : (layer + 1) * chans]
        row[layer] = jnp.broadcast_to(jnp.concatenate([part, part], axis=1), (8, LANES))


def cut_kernel(dims, place, *refs):
    micros, chans, size_x, local_y, local_z, slabs, width, span, edged, fields = dims
    sources, refs = refs[:fields], refs[fields:]
    outs, wide = refs[:-1], refs[-1]
    slab = place[1]
    step = size_x * local_y
    for field, source in enumerate(sources):
        windows = outs[field * slabs : (field + 1) * slabs]
        edges = outs[fields * slabs :]
        for micro in range(micros):
            for y in range(local_y):
                first = micro * chans * step + y
                parts = [
                    source[pl.ds(first + x * local_y, chans, stride=step), :] for x in range(size_x)
                ]
                wide[field, micro, y, HALO : HALO + local_z] = jnp.concatenate(parts, axis=0).T
                wide[field, micro, y, :HALO] = jnp.zeros((HALO, LANES), F32)
                wide[field, micro, y, HALO + local_z :] = jnp.zeros((HALO, LANES), F32)
                if edged:
                    for turn in range(slabs):
                        start = lax.rem(slab + turn, slabs) * width
                        if width % 8 == 0:
                            start = pl.multiple_of(start, 8)
                        windows[turn][micro, y] = wide[field, micro, y, pl.ds(start, span)]
                    low = wide[field, micro, y, local_z : local_z + HALO]
                    high = wide[field, micro, y, HALO : 2 * HALO]
                    for m in range(slabs):
                        edges[m][field, micro, y] = jnp.where(slab == m, low, high)
                else:
                    windows[0][micro, y] = wide[field, micro, y, HALO : HALO + local_z]


class Slab:
    def __init__(self, dims, place):
        self.micros, self.rows_y, self.depth, self.width, self.chunk_y, self.slabs, limit_z = dims
        self.section, self.slab, self.swap, origin = place[0], place[1], place[2], place[3]
        self.chunk = self.chunk_y * self.depth
        self.chunks = self.rows_y // self.chunk_y
        self.per_owner = self.rows_y // self.slabs
        zs = lax.broadcasted_iota(jnp.int32, (self.depth, LANES), 0)
        inside = (zs + origin >= 0) & (zs + origin < limit_z)
        self.in_grid = inside.astype(F32)[None]
        self.mine = ((zs >= HALO) & (zs < HALO + self.width)).astype(F32)[None]

    def over_chunks(self, body):
        if self.chunks == 1:
            body(0, 0)
        else:

            def step(part, carry):
                body(part, pl.multiple_of(part * self.chunk, 16))
                return carry

            lax.fori_loop(0, self.chunks, step, 0)

    def masked(self, values, mask):
        cut = values.reshape(-1, self.depth, LANES) * mask
        return cut.reshape(values.shape)

    def put_rows(self, target, lead, start, values):
        hi, lo = split_terms(values)
        at = pl.ds(start + self.depth, self.chunk)
        for micro in range(self.micros):
            rows = slice(micro * self.chunk, (micro + 1) * self.chunk)
            target[lead, micro, at, slice(0, LANES)] = hi[rows]
            target[lead, micro, at, slice(LANES, 2 * LANES)] = lo[rows]

    def pieces_of(self, source, lead, start):
        pieces = []
        for b in range(3):
            at = pl.ds(start + b * self.depth, self.chunk)
            parts = [source[lead, micro, at, :] for micro in range(self.micros)]
            pieces.append(jnp.concatenate(parts, axis=0))
        return pieces

    def conv(self, source, lead, start, table):
        pieces = self.pieces_of(source, lead, start)
        left = jnp.concatenate(pieces + [piece[:, :LANES] for piece in pieces], axis=1)
        out = jnp.dot(left, table[...], preferred_element_type=F32)
        before = pltpu.roll(out[:, :LANES], 1, 0)
        after = pltpu.roll(out[:, 2 * LANES :], out.shape[0] - 1, 0)
        return before + out[:, LANES : 2 * LANES] + after

    def by_owner(self, layer, own, other, body):
        mine = layer // 2 == self.section
        pl.when(mine)(lambda: body(own, layer % 2))
        pl.when(jnp.logical_not(mine))(lambda: body(other, layer % 2))

    def blank_edges(self, target):
        blank = jnp.zeros((self.depth, 2 * LANES), BF16)
        for lead in range(target.shape[0]):
            for micro in range(self.micros):
                for edge in (0, self.rows_y + 1):
                    target[lead, micro, edge * self.depth : (edge + 1) * self.depth, :] = blank

    def read(self, source, lead, start):
        at = pl.ds(start, self.chunk)
        return jnp.concatenate([source[lead, micro, at, :] for micro in range(self.micros)], axis=0)

    def write(self, target, lead, start, values):
        for micro in range(self.micros):
            rows = slice(micro * self.chunk, (micro + 1) * self.chunk)
            target[lead, micro, pl.ds(start, self.chunk), :] = values[rows]

    def emit(self, target, part, values):
        inner = values.reshape(self.micros, self.chunk_y, self.depth, LANES)
        for y in range(self.chunk_y):
            row = part * self.chunk_y + y
            to = lax.rem(row // self.per_owner + self.slabs - self.slab, self.slabs)
            for micro in range(self.micros):
                value = inner[micro, y, HALO : HALO + self.width, :]
                target[to, micro, row % self.per_owner] = value

    def fill(self, field, windows, edges, which):
        span = windows[0].shape[2]
        for micro in range(self.micros):
            for turn, window in enumerate(windows):
                owner = lax.rem(self.slab + self.slabs - turn, self.slabs)
                for y in range(self.per_owner):
                    value = window[micro, y]
                    if span < self.depth:
                        extra = jnp.zeros((self.depth - span, LANES), F32)
                        value = jnp.concatenate([value, extra], axis=0)
                    start = pl.multiple_of((owner * self.per_owner + y) * self.depth, 16)
                    field[0, micro, pl.ds(start, self.depth), :] = value
        if not edges:
            return
        left = self.slab == 0
        at = jnp.where(left, 0, HALO + self.width)

        @pl.when(left | (self.slab == self.slabs - 1))
        def _():
            for m, edge in enumerate(edges):
                owner = jnp.where(left, m, (m + 1) % self.slabs)
                for micro in range(self.micros):
                    for y in range(self.per_owner):
                        start = pl.multiple_of((owner * self.per_owner + y) * self.depth + at, 8)
                        field[0, micro, pl.ds(start, HALO), :] = edge[which, micro, y]


def forward_kernel(dims, place, own, own_row, other, other_row, *refs):
    slab = Slab(dims, place)
    refs, (acts, kept, front, field) = refs[:-4], refs[-4:]
    slab.blank_edges(acts)
    slab.fill(field, refs[: slab.slabs], refs[slab.slabs :], 0)
    slab.over_chunks(
        lambda part, start: slab.put_rows(acts, 0, start, slab.read(field, 0, start))
    )

    def layer_step(layer, carry):
        def run(tables, half):
            table, row = tables

            def body(part, start):
                pre = slab.conv(acts, layer, start, table.at[half]) + row[half][0:1, :]
                grown = 1.0 + jnp.exp(-pre)
                sigma = 1.0 / grown
                slab.write(kept, layer, start, sigma * (1.0 + pre * (1.0 - sigma)))
                out = slab.masked(pre / grown, slab.in_grid)
                pl.when(layer < 3)(lambda: slab.put_rows(acts, layer + 1, start, out))
                pl.when(layer == 2 * slab.section + 1)(lambda: slab.emit(front, part, out))

            slab.over_chunks(body)

        slab.by_owner(layer, (own, own_row), (other, other_row), run)
        return carry

    lax.fori_loop(0, 4, layer_step, 0)


def backward_kernel(dims, scale, place, own, other, acts, kept, *refs):
    slab = Slab(dims, place)
    refs, (back, sums, rim, slopes, field, acc) = refs[:-6], refs[-6:]
    slab.blank_edges(rim)
    slab.fill(field, refs[: slab.slabs], refs[slab.slabs :], 1)

    def take_gradient(layer, start, gradient):
        slope = slab.masked(gradient * slab.read(kept, layer, start), slab.in_grid)
        slab.write(slopes, layer, start, slab.masked(slope, slab.mine))
        slab.put_rows(rim, layer % 2, start, slope)

    slab.over_chunks(lambda part, start: take_gradient(3, start, slab.read(field, 0, start)))

    def layer_step(index, carry):
        layer = 3 - index

        def run(table, half):
            def body(part, start):
                gradient = slab.conv(rim, layer % 2, start, table.at[half])
                pl.when(layer > 0)(lambda: take_gradient(layer - 1, start, gradient))
                pl.when(layer == 2 * slab.section)(lambda: slab.emit(back, part, gradient))

            slab.over_chunks(body)

        slab.by_owner(layer, own, other, run)
        return carry

    lax.fori_loop(0, jnp.where(slab.section == 0, 4, 2), layer_step, 0)

    quarter = BLOCKS // 4
    chans = LANES // 2

    def spot(tap):
        return (tap // quarter ^ slab.swap) * quarter + tap % quarter

    sums[spot(TAPS)] = jnp.zeros((chans, LANES), F32)
    for slot in range(2):
        layer = 2 * slab.section + slot
        acc[...] = jnp.zeros(acc.shape, F32)

        def gather(part, start):
            slope = slab.read(slopes, layer, start)
            moved = [pltpu.roll(slope, slope.shape[0] - 1, 0), slope, pltpu.roll(slope, 1, 0)]
            terms = [split_terms(value) for value in moved]
            left_hi = jnp.concatenate([hi for hi, lo in terms], axis=1)
            left_lo = jnp.concatenate([lo for hi, lo in terms], axis=1)
            pieces = slab.pieces_of(acts, layer, start)
            full = jnp.concatenate(pieces, axis=1)
            high = jnp.concatenate([piece[:, :LANES] for piece in pieces], axis=1)
            over_rows = (((0,), (0,)), ((), ()))
            one = lax.dot_general(left_hi, full, over_rows, preferred_element_type=F32)
            two = lax.dot_general(left_lo, high, over_rows, preferred_element_type=F32)
            for b in range(3):
                at = slice(b * LANES, (b + 1) * LANES)
                acc[0 : 3 * LANES, at] += (
                    one[:, 2 * b * LANES : (2 * b + 1) * LANES]
                    + one[:, (2 * b + 1) * LANES : (2 * b + 2) * LANES]
                    + two[:, at]
                )
            acc[3 * LANES : 3 * LANES + 1, 0:LANES] += jnp.sum(slope, axis=0, keepdims=True)

        slab.over_chunks(gather)
        lanes = slice(slot * chans, (slot + 1) * chans)
        for b in range(3):
            for c in range(3):
                block = acc[c * LANES : (c + 1) * LANES, b * LANES : (b + 1) * LANES] * scale
                tap = 3 * b + c
                sums[spot(tap), :, lanes] = block[chans:, :chans]
                sums[spot(9 + tap), :, lanes] = block[:chans, :chans] + block[chans:, chans:]
                sums[spot(18 + tap), :, lanes] = block[:chans, chans:]
        row = acc[3 * LANES : 3 * LANES + 1, 0:LANES] * scale
        sums[spot(TAPS), 0:1, lanes] = row[:, :chans] + row[:, chans:]


def unpack_kernel(chunk, place, *refs):
    slab, swap = place[1], place[2]
    near, (beside, across, weight, bias, whole) = refs[:-5], refs[-5:]
    slabs = len(near)
    quarter = slabs * chunk
    chans = weight.shape[-1]

    def put(relative, turn, values):
        at = (relative ^ swap) * quarter + lax.rem(slab + slabs - turn, slabs) * chunk
        whole[pl.ds(pl.multiple_of(at, 8), chunk), :] = values

    for turn in range(slabs):
        first = turn * chunk
        put(0, turn, near[turn][...])
        put(1, turn, beside[first : first + chunk, :])
        for part in range(2):
            start = part * quarter + first
            put(2 + part, turn, across[start : start + chunk, :])
    for layer in range(2):
        lanes = slice(layer * chans, (layer + 1) * chans)
        for tap in range(BLOCKS):
            at = tap // 7 * quarter + tap % 7 * chans
            if tap < TAPS:
                weight[layer, tap] = whole[at : at + chans, lanes]
            else:
                bias[layer : layer + 1, :] = whole[at : at + 1, lanes]


def restore_kernel(dims, place, *refs):
    micros, chans, size_x, local_y, width = dims
    pieces, (target, whole) = refs[:-2], refs[-2:]
    slab = place[1]
    slabs = len(pieces)
    step = size_x * local_y
    for micro in range(micros):
        for y in range(local_y):
            for turn in range(slabs):
                start = lax.rem(slab + slabs - turn, slabs) * width
                if width % 8 == 0:
                    start = pl.multiple_of(start, 8)
                whole[pl.ds(start, width), :] = pieces[turn][micro, y]
            block = whole[...].T
            for x in range(size_x):
                first = micro * chans * step + x * local_y + y
                part = block[x * chans : (x + 1) * chans]
                target[pl.ds(first, chans, stride=step), :] = part


def turned(block, distance):
    count = lax.axis_size("gy")
    return lax.ppermute(block, "gy", [(i, (i + distance) % count) for i in range(count)])


def spread(blocks):
    slabs = len(blocks)
    if slabs <= 8:
        return [blocks[0]] + [turned(blocks[turn], turn) for turn in range(1, slabs)]
    slab = lax.axis_index("gy")
    got = lax.all_to_all(jnp.roll(jnp.stack(blocks), slab, axis=0), "gy", 0, 0)
    got = jnp.roll(got[::-1], slab + 1, axis=0)
    return [got[turn] for turn in range(slabs)]


def swapped(block, bit):
    count = lax.axis_size("gz")
    return lax.ppermute(block, "gz", [(i, i ^ bit) for i in range(count)])


def edge_route(owner):
    slabs, columns = lax.axis_size("gy"), lax.axis_size("gz")
    follower = (owner + 1) % slabs
    route = [(owner * columns + g, g + 1) for g in range(columns - 1)]
    last = (slabs - 1) * columns
    return route + [(follower * columns + g, last + g - 1) for g in range(1, columns)]


def windows_of(inflow, cotangent, place, slabs, width, span):
    micros, chans, size_x, local_y, local_z = inflow.shape
    rows = micros * chans * size_x * local_y
    edged = width >= HALO and slabs > 1
    dims = (micros, chans, size_x, local_y, local_z, slabs if edged else 1, width, span, edged, 2)
    outs = [((micros, local_y, span if edged else local_z, LANES), F32)] * (2 * dims[5])
    if edged:
        outs += [((2, micros, local_y, HALO, LANES), F32)] * slabs
    wide = pltpu.VMEM((2, micros, local_y, local_z + 2 * HALO, LANES), F32)
    fields = [inflow.reshape(rows, local_z), cotangent.reshape(rows, local_z)]
    got = call(functools.partial(cut_kernel, dims), "cut", outs, [place, *fields], [wide])
    if edged:
        edges = [
            lax.ppermute(edge, ("gy", "gz"), edge_route(m))
            for m, edge in enumerate(got[2 * slabs :])
        ]
        return spread(got[:slabs]), spread(got[slabs : 2 * slabs]), edges
    columns = lax.axis_size("gz")
    slab = lax.axis_index("gy")
    results = []
    for field in got:
        up = [(i, i + 1) for i in range(columns - 1)]
        down = [(i + 1, i) for i in range(columns - 1)]
        before = lax.ppermute(field[:, :, local_z - HALO :], "gz", up)
        after = lax.ppermute(field[:, :, :HALO], "gz", down)
        wide = jnp.concatenate([before, field, after], axis=2)
        cuts = [
            lax.dynamic_slice_in_dim(wide, (slab + turn) % slabs * width, span, axis=2)
            for turn in range(slabs)
        ]
        results.append(spread(cuts))
    return results[0], results[1], []


def summed_over_grid(block):
    slabs = lax.axis_size("gy")
    slab = lax.axis_index("gy")
    for bit in (1, 2):
        rows = block.shape[0] // 2
        block = block[:rows] + swapped(block[rows:], bit)
    chunk = -(-block.shape[0] // (8 * slabs)) * 8
    block = jnp.pad(block, ((0, slabs * chunk - block.shape[0]), (0, 0)))
    parts = block.reshape(slabs, chunk, LANES)
    sent = [
        lax.dynamic_index_in_dim(parts, (slab + turn) % slabs, 0, keepdims=False)
        for turn in range(slabs)
    ]
    return sum(spread(sent))


def restored(pieces, shape, place):
    micros, chans, size_x, local_y, local_z = shape
    width = pieces[0].shape[2]
    dims = (micros, chans, size_x, local_y, width)
    rows = micros * chans * size_x * local_y
    kernel = functools.partial(restore_kernel, dims)
    scratch = [pltpu.VMEM((local_z, LANES), F32)]
    (whole,) = call(kernel, "restore", [((rows, local_z), F32)], [place, *pieces], scratch)
    return whole.reshape(1, *shape)


def per_device(inflow, weights, biases, cotangent):
    micros, chans, size_x, local_y, local_z = inflow.shape
    slabs, columns = lax.axis_size("gy"), lax.axis_size("gz")
    rows_y = local_y * slabs
    width = local_z // slabs
    span = width + 2 * HALO
    depth = -(-span // 16) * 16
    chunk_y = max(n for n in range(1, rows_y + 1) if rows_y % n == 0 and n * depth <= 384)
    scale = 1.0 / math.sqrt(micros * size_x * rows_y * local_z * columns)
    slab, column = lax.axis_index("gy"), lax.axis_index("gz")
    swap = 2 * (column % 2) + column // 2 % 2
    origin = column * local_z + slab * width - HALO
    place = jnp.stack([lax.axis_index("section"), slab, swap, origin]).astype(jnp.int32)

    half = BLOCKS // 2
    packs = [((BLOCKS, chans, LANES), F32), ((half, chans, LANES), F32)]
    own, sent = call(pack_kernel, "pack", packs, [place, weights, biases])
    first = lax.ppermute(sent, "section", [(0, 1), (1, 0)])

    windows, pulls, edges = windows_of(inflow, cotangent, place, slabs, width, span)
    first, windows, edges = lax.optimization_barrier((first, windows, edges))
    second = swapped(first, 1)

    tables = [((2, 9 * LANES, 3 * LANES), BF16)] * 2 + [((2, 8, LANES), F32)]
    own_fwd, own_bwd, own_row = call(table_kernel, "own_table", tables, [place, own])
    far_fwd, far_bwd, far_row = call(table_kernel, "far_table", tables, [place, first, second])

    dims = (micros, rows_y, depth, width, chunk_y, slabs, local_z * columns)
    padded = (rows_y + 2) * depth
    full = rows_y * depth
    piece = ((slabs, micros, local_y, width, LANES), F32)
    work = 2 * micros * full * 9 * LANES * 3 * LANES
    acts, kept, front = call(
        functools.partial(forward_kernel, dims),
        "forward",
        [((4, micros, padded, 2 * LANES), BF16), ((4, micros, full, LANES), F32), piece],
        [place, own_fwd, own_row, far_fwd, far_row, *windows, *edges],
        [pltpu.VMEM((1, micros, full, LANES), F32)],
        4 * work,
    )
    outward = spread([front[turn] for turn in range(slabs)])
    back, sums = call(
        functools.partial(backward_kernel, dims, scale),
        "backward",
        [piece, ((BLOCKS, chans, LANES), F32)],
        [place, own_bwd, far_bwd, acts, kept, *pulls, *edges],
        [
            pltpu.VMEM((2, micros, padded, 2 * LANES), BF16),
            pltpu.VMEM((4, micros, full, LANES), F32),
            pltpu.VMEM((1, micros, full, LANES), F32),
            pltpu.VMEM((3 * LANES + 8, 3 * LANES), F32),
        ],
        6 * work,
    )

    mine = summed_over_grid(sums.reshape(BLOCKS * chans, LANES))
    near = spread([mine] * slabs)
    near, back = lax.optimization_barrier((near, back))
    quarter = jnp.concatenate(near, axis=0)
    beside = swapped(quarter, 2)
    inward = spread([back[turn] for turn in range(slabs)])
    across = swapped(jnp.concatenate([quarter, beside], axis=0), 1)
    section_out = restored(outward, inflow.shape, place)
    section_grad = restored(inward, inflow.shape, place)
    chunk = mine.shape[0]
    weight_total, bias_total = call(
        functools.partial(unpack_kernel, chunk),
        "unpack",
        [((2, TAPS, chans, chans), F32), ((2, chans), F32)],
        [place, *near, beside, across],
        [pltpu.VMEM((4 * slabs * chunk, LANES), F32)],
    )
    return (section_out, section_grad, weight_total, bias_total)


def solution(mesh):
    grid = P(None, None, None, "gy", "gz")
    section_grid = P("section", None, None, None, "gy", "gz")
    return jax.shard_map(
        per_device,
        mesh=mesh,
        in_specs=(grid, P("section", None, None, None), P("section", None), grid),
        out_specs=(section_grid, section_grid, P("section", None, None, None), P("section", None)),
        check_vma=False,
    )
```

time: 129 us -> 105 us (0.81)
  starting transfers between devices: 22.5 us -> 48.5 us
  waiting for transfers between devices: 52.9 us -> 29.5 us
  blocking collectives: 22.8 us -> 0 us
  Pallas kernels: 15.8 us -> 22.9 us
  local copies, waits for them, and re-layouts: 9.1 us -> 2.34 us
  other arithmetic: 4.15 us -> 0.19 us
    ppermute x3 -> x28, starting transfers between devices: 5.21 us -> 48.5 us  [the longest x18 28.1 us: turned(): lax.ppermute(block, 'gy', [(i, (i + distance) % count) for i in range(cou...]
    all_to_all x4 -> x0, waiting for transfers between devices: 30.8 us -> none  [the longest x2 17.2 us: summed_over_grid(): block = jnp.sum(lax.all_to_all(parts, axis, 0, 0), axis=0)]
    all_gather x2 -> x0, blocking collectives: 22.8 us -> none  [summed_over_grid(): block = lax.all_gather(block, axis, tiled=True)]
    all_to_all x4 -> x0, starting transfers between devices: 17.3 us -> none  [the longest x2 7.02 us: summed_over_grid(): block = jnp.sum(lax.all_to_all(parts, axis, 0, 0), axis=0)]
    ppermute x3 -> x28, waiting for transfers between devices: 22.1 us -> 29.5 us  [the longest x18 17.2 us: turned(): lax.ppermute(block, 'gy', [(i, (i + distance) % count) for i in range(cou...]
    pallas_call x1 -> x9, Pallas kernels: 15.8 us -> 22.9 us  [call(): pl.pallas_call(kernel, out_shape=arrays, in_specs=[SMEM] + [VMEM] * (len(...]
    another operation x5 -> x1, other arithmetic: 3.03 us -> 0.08 us  [per_device(): jnp.stack([lax.axis_index('section'), slab, swap, origin]).astype(jnp.int32)]
    another operation x3 -> x0, local copies, waits for them, and re-layouts: 2.04 us -> none  [the longest x1 1.08 us: per_device(): fields = jnp.stack([inflow, cotangent]).transpose(0, 1, 4, 5, 3, 2)]
  transfers between devices with their start and end apart: 7 -> 28, of which waited for: 5 -> 12; matrix products, arithmetic and copies ran while one was open for 5% -> 0% of each run, Pallas kernels for 0% -> 12%
where the time goes in v3:
time: 105 us; the launch traced here: 104 us
  starting transfers between devices  48.5 us (46%)
  waiting for transfers between devices  29.5 us (28%)
  Pallas kernels  22.9 us (22%)
  local copies, waits for them, and re-layouts  2.34 us (2%)
    ppermute x18, starting transfers between devices, turned(): lax.ppermute(block, 'gy', [(i, (i + distance) % count) for i in range(cou...  28.1 us
    pallas_call x9, Pallas kernels, call(): pl.pallas_call(kernel, out_shape=arrays, in_specs=[SMEM] + [VMEM] * (len(...  22.9 us
    ppermute x18, waiting for transfers between devices, turned(): lax.ppermute(block, 'gy', [(i, (i + distance) % count) for i in range(cou...  17.2 us
    ppermute x5, starting transfers between devices, swapped(): return lax.ppermute(block, 'gz', [(i, i ^ bit) for i in range(count)])  14 us
    ppermute x5, waiting for transfers between devices, swapped(): return lax.ppermute(block, 'gz', [(i, i ^ bit) for i in range(count)])  12.3 us
    ppermute x4, starting transfers between devices, windows_of(): lax.ppermute(edge, ('gy', 'gz'), edge_route(m))  3.44 us
    ppermute x1, starting transfers between devices, per_device(): first = lax.ppermute(sent, 'section', [(0, 1), (1, 0)])  3 us
    unnamed x12, local copies, waits for them, and re-layouts  2.19 us
  transfers between devices with their start and end apart: 28, of which 12 were waited for; matrix products, arithmetic and copies ran while one was open for 0% of the time, Pallas kernels for 12%

profile of v3, /device:TPU:0, one launch (start us, length us, event | category | flops | bytes accessed | tf_op | source)
XLA Modules:
  0.0 104.4 jit_solution(6243111775507670382)
XLA Ops:
  0.7 0.1 pad_add_fusion.place
  0.8 1.5 %copy-done = f32[2,27,64,64]{3,2,1,0:T(8,128)S(1)} copy-done((f32[2,27,64,64]{3,2,1,0:T(8,128)S(1)}, f32[2,27,64,64]{3,2,1,0:T(8,128)}, u32[]{:S(2)}) %copy-start) | copy-done | bytes 884760
  2.2 0.7 copy-done.3
  2.9 0.9 pack.1
  3.8 3.0 %collective-permute-start = (f32[14,64,128]{2,1,0:T(8,128)S(1)}, f32[14,64,128]{2,1,0:T(8,128)S(1)}, u32[]{:S(2)}, u32[]{:S(2)}) collective-permute-start(f32[14,64,128]{2,1,0:T(8,128)S(1)} %get-tuple-element.48), channel_id=1, source_target_pairs={{0,16},{16,0},{1,17},{17,1},{2,18},{18,2},{3,19},{19,3},{4,20},{20... | collective-permute-start | bytes 1376264 | tf_op jit(solution)/shard_map/ppermute | solution.py:488
  6.8 0.8 cut.1
  7.6 1.5 %collective-permute-start.4 = (f32[2,2,2,8,128]{4,3,2,1,0:T(8,128)S(1)}, f32[2,2,2,8,128]{4,3,2,1,0:T(8,128)S(1)}, u32[]{:S(2)}, u32[]{:S(2)}) collective-permute-start(f32[2,2,2,8,128]{4,3,2,1,0:T(8,128)S(1)} %get-tuple-element.53), channel_id=1, source_target_pairs={{0,1},{1,2},{2,3},{5,12},{6,13},{7,14},{16,17},{17,18},{18,19},{21... | collective-permute-start | bytes 98312 | tf_op jit(solution)/shard_map/ppermute | solution.py:423
  9.1 0.7 collective-permute-start.5
  9.8 5.0 %collective-permute-start.1 = (f32[2,2,48,128]{3,2,1,0:T(8,128)S(1)}, f32[2,2,48,128]{3,2,1,0:T(8,128)S(1)}, u32[]{:S(2)}, u32[]{:S(2)}) collective-permute-start(f32[2,2,48,128]{3,2,1,0:T(8,128)S(1)} %get-tuple-element.50), channel_id=1, source_target_pairs={{0,4},{4,8},{8,12},{12,0},{1,5},{5,9},{9,13},{13,1},{2,6},{6,10},{... | collective-permute-start | bytes 294920 | tf_op jit(solution)/shard_map/ppermute | solution.py:384
  14.8 0.0 collective-permute-start.2
  14.8 0.0 collective-permute-done.4.refs_4_
  14.8 2.6 %collective-permute-start.3 = (f32[2,2,48,128]{3,2,1,0:T(8,128)S(1)}, f32[2,2,48,128]{3,2,1,0:T(8,128)S(1)}, u32[]{:S(2)}, u32[]{:S(2)}) collective-permute-start(f32[2,2,48,128]{3,2,1,0:T(8,128)S(1)} %get-tuple-element.52), channel_id=1, source_target_pairs={{0,12},{4,0},{8,4},{12,8},{1,13},{5,1},{9,5},{13,9},{2,14},{6,2},{... | collective-permute-start | bytes 294920 | tf_op jit(solution)/shard_map/ppermute | solution.py:384
  17.4 0.7 collective-permute-start.6
  18.0 0.0 collective-permute-done.6.refs_6_
  18.1 0.7 collective-permute-start.7
  18.7 0.0 collective-permute-done.7.refs_7_
  18.8 3.9 %collective-permute-done.2.refs_2_ = f32[2,2,48,128]{3,2,1,0:T(8,128)S(1)} collective-permute-done((f32[2,2,48,128]{3,2,1,0:T(8,128)S(1)}, f32[2,2,48,128]{3,2,1,0:T(8,128)S(1)}, u32[]{:S(2)}, u32[]{:S(2)}) %collective-permute-start.2) | collective-permute-done | bytes 98336 | tf_op jit(solution)/shard_map/ppermute | solution.py:384
  22.7 0.0 collective-permute-done.3.refs_3_
  22.7 0.0 collective-permute-done.refs_0_
  22.7 9.4 %collective-permute-start.8 = (f32[14,64,128]{2,1,0:T(8,128)S(1)}, f32[14,64,128]{2,1,0:T(8,128)S(1)}, u32[]{:S(2)}, u32[]{:S(2)}) collective-permute-start(f32[14,64,128]{2,1,0:T(8,128)S(1)} %collective-permute-done.refs_0_), channel_id=1, source_target_pairs={{0,1},{1,0},{2,3},{3,2},{4,5},{5,4},{6,7},{7,6},{8,9},{9,8},{10,11... | collective-permute-start | bytes 1376264 | tf_op jit(solution)/shard_map/ppermute | solution.py:399
  32.1 0.0 collective-permute-start.12
  32.1 2.3 %collective-permute-start.13 = (f32[2,2,48,128]{3,2,1,0:T(8,128)S(1)}, f32[2,2,48,128]{3,2,1,0:T(8,128)S(1)}, u32[]{:S(2)}, u32[]{:S(2)}) collective-permute-start(f32[2,2,48,128]{3,2,1,0:T(8,128)S(1)} %get-tuple-element.75), channel_id=1, source_target_pairs={{0,8},{4,12},{8,0},{12,4},{1,9},{5,13},{9,1},{13,5},{2,10},{6,14},... | collective-permute-start | bytes 294920 | tf_op jit(solution)/shard_map/ppermute | solution.py:384
  34.4 1.5 %collective-permute-start.14 = (f32[2,2,48,128]{3,2,1,0:T(8,128)S(1)}, f32[2,2,48,128]{3,2,1,0:T(8,128)S(1)}, u32[]{:S(2)}, u32[]{:S(2)}) collective-permute-start(f32[2,2,48,128]{3,2,1,0:T(8,128)S(1)} %get-tuple-element.76), channel_id=1, source_target_pairs={{0,12},{4,0},{8,4},{12,8},{1,13},{5,1},{9,5},{13,9},{2,14},{6,2},{... | collective-permute-start | bytes 294920 | tf_op jit(solution)/shard_map/ppermute | solution.py:384
  36.0 1.2 %own_table.1 = (bf16[2,1152,384]{2,1,0:T(8,128)(2,1)S(1)}, bf16[2,1152,384]{2,1,0:T(8,128)(2,1)S(1)}, f32[2,8,128]{2,1,0:T(8,128)S(1)}) custom-call(s32[4]{0:T(128)S(1)} %pad_add_fusion.place, f32[28,64,128]{2,1,0:T(8,128)S(1)} %get-tuple-element.45.refs_0_), custom_call_target="tpu_custom_call" | custom-call | bytes 4464640 | tf_op jit(solution)/shard_map/own_table/pallas_call | solution.py:24
  37.2 0.0 collective-permute-done.8.refs_1_
  37.2 1.3 %far_table.1 = (bf16[2,1152,384]{2,1,0:T(8,128)(2,1)S(1)}, bf16[2,1152,384]{2,1,0:T(8,128)(2,1)S(1)}, f32[2,8,128]{2,1,0:T(8,128)S(1)}) custom-call(s32[4]{0:T(128)S(1)} %pad_add_fusion.place, f32[14,64,128]{2,1,0:T(8,128)S(1)} %collective-permute-done.refs_0_, f32[14,64,128]{2,1,0:T(8,128)S(1)} %collective-permute-done.8.refs_1_), custom_call_target="tpu_custom_call" | custom-call | bytes 4464640 | tf_op jit(solution)/shard_map/far_table/pallas_call | solution.py:24
  38.5 6.0 %forward.1 = (bf16[4,2,480,256]{3,2,1,0:T(8,128)(2,1)S(1)}, f32[4,2,384,128]{3,2,1,0:T(8,128)S(1)}, f32[4,2,2,32,128]{4,3,2,1,0:T(8,128)S(1)}) custom-call(s32[4]{0:T(128)S(1)} %pad_add_fusion.place, bf16[2,1152,384]{2,1,0:T(8,128)(2,1)S(1)} %get-tuple-element.46.own, f32[2,8,128]{2,1,0:T(8,128)S(1)} %get-tuple-element.47.own_row, ...), custom_call_target="tpu_custom_call" | custom-call | flops 2717908992 | bytes 8273920 | tf_op jit(solution)/shard_map/forward/pallas_call | solution.py:24
  44.6 0.0 collective-permute-done.12.refs_1_
  44.6 0.0 collective-permute-done.14.refs_3_
  44.6 7.6 %backward.1 = (f32[4,2,2,32,128]{4,3,2,1,0:T(8,128)S(1)}, f32[28,64,128]{2,1,0:T(8,128)S(1)}) custom-call(s32[4]{0:T(128)S(1)} %pad_add_fusion.place, bf16[2,1152,384]{2,1,0:T(8,128)(2,1)S(1)} %get-tuple-element.69.own, bf16[2,1152,384]{2,1,0:T(8,128)(2,1)S(1)} %get-tuple-element.70.other, bf16[4,2,480,256]{3,2,1,0:T(8,128)(2,1)S(1)} %get-tuple-element.71.acts, ...), custom_call_target="tpu_custom_call" | custom-call | flops 4076863488 | bytes 12333056 | tf_op jit(solution)/shard_map/backward/pallas_call | solution.py:24
  52.2 0.1 fusion.2
  52.3 0.1 collective-permute-start.15
  52.4 1.8 %collective-permute-done.15 = f32[896,128]{1,0:T(8,128)S(1)} collective-permute-done((f32[896,128]{1,0:T(8,128)S(1)}, f32[896,128]{1,0:T(8,128)S(1)}, u32[]{:S(2)}, u32[]{:S(2)}) %collective-permute-start.15) | collective-permute-done | bytes 458784 | tf_op jit(solution)/shard_map/ppermute | solution.py:399
  54.2 0.1 bitcast_add_fusion
  54.2 2.9 %collective-permute-start.16 = (f32[448,128]{1,0:T(8,128)S(1)}, f32[448,128]{1,0:T(8,128)S(1)}, u32[]{:S(2)}, u32[]{:S(2)}) collective-permute-start(f32[448,128]{1,0:T(8,128)S(1)} %slice.57), channel_id=1, source_target_pairs={{0,2},{1,3},{2,0},{3,1},{4,6},{5,7},{6,4},{7,5},{8,10},{9,11},{10,... | collective-permute-start | bytes 688136 | tf_op jit(solution)/shard_map/ppermute | solution.py:399
  57.2 5.9 %collective-permute-done.16 = f32[448,128]{1,0:T(8,128)S(1)} collective-permute-done((f32[448,128]{1,0:T(8,128)S(1)}, f32[448,128]{1,0:T(8,128)S(1)}, u32[]{:S(2)}, u32[]{:S(2)}) %collective-permute-start.16) | collective-permute-done | bytes 229408 | tf_op jit(solution)/shard_map/ppermute | solution.py:399
  63.1 0.6 collective-permute-start.17
  63.7 1.5 %collective-permute-start.18 = (f32[112,128]{1,0:T(8,128)S(1)}, f32[112,128]{1,0:T(8,128)S(1)}, u32[]{:S(2)}, u32[]{:S(2)}) collective-permute-start(f32[112,128]{1,0:T(8,128)S(1)} %get-tuple-element.98), channel_id=1, source_target_pairs={{0,8},{4,12},{8,0},{12,4},{1,9},{5,13},{9,1},{13,5},{2,10},{6,14},... | collective-permute-start | bytes 172040 | tf_op jit(solution)/shard_map/ppermute | solution.py:384
  65.3 2.8 %collective-permute-start.19 = (f32[112,128]{1,0:T(8,128)S(1)}, f32[112,128]{1,0:T(8,128)S(1)}, u32[]{:S(2)}, u32[]{:S(2)}) collective-permute-start(f32[112,128]{1,0:T(8,128)S(1)} %get-tuple-element.97), channel_id=1, source_target_pairs={{0,12},{4,0},{8,4},{12,8},{1,13},{5,1},{9,5},{13,9},{2,14},{6,2},{... | collective-permute-start | bytes 172040 | tf_op jit(solution)/shard_map/ppermute | solution.py:384
  68.1 1.6 %collective-permute-done.17 = f32[112,128]{1,0:T(8,128)S(1)} collective-permute-done((f32[112,128]{1,0:T(8,128)S(1)}, f32[112,128]{1,0:T(8,128)S(1)}, u32[]{:S(2)}, u32[]{:S(2)}) %collective-permute-start.17) | collective-permute-done | bytes 57376 | tf_op jit(solution)/shard_map/ppermute | solution.py:384
  69.7 1.4 %collective-permute-done.18 = f32[112,128]{1,0:T(8,128)S(1)} collective-permute-done((f32[112,128]{1,0:T(8,128)S(1)}, f32[112,128]{1,0:T(8,128)S(1)}, u32[]{:S(2)}, u32[]{:S(2)}) %collective-permute-start.18) | collective-permute-done | bytes 57376 | tf_op jit(solution)/shard_map/ppermute | solution.py:384
  71.1 1.3 %collective-permute-start.20 = (f32[112,128]{1,0:T(8,128)S(1)}, f32[112,128]{1,0:T(8,128)S(1)}, u32[]{:S(2)}, u32[]{:S(2)}) collective-permute-start(f32[112,128]{1,0:T(8,128)S(1)} %fusion.1.refs_0_), channel_id=1, source_target_pairs={{0,4},{4,8},{8,12},{12,0},{1,5},{5,9},{9,13},{13,1},{2,6},{6,10},{... | collective-permute-start | bytes 172040 | tf_op jit(solution)/shard_map/ppermute | solution.py:384
  72.4 2.4 %collective-permute-start.21 = (f32[112,128]{1,0:T(8,128)S(1)}, f32[112,128]{1,0:T(8,128)S(1)}, u32[]{:S(2)}, u32[]{:S(2)}) collective-permute-start(f32[112,128]{1,0:T(8,128)S(1)} %fusion.1.refs_0_), channel_id=1, source_target_pairs={{0,8},{4,12},{8,0},{12,4},{1,9},{5,13},{9,1},{13,5},{2,10},{6,14},... | collective-permute-start | bytes 172040 | tf_op jit(solution)/shard_map/ppermute | solution.py:384
  74.7 0.2 collective-permute-start.22
  75.0 2.7 %collective-permute-done.20.refs_1_ = f32[112,128]{1,0:T(8,128)S(1)} collective-permute-done((f32[112,128]{1,0:T(8,128)S(1)}, f32[112,128]{1,0:T(8,128)S(1)}, u32[]{:S(2)}, u32[]{:S(2)}) %collective-permute-start.20) | collective-permute-done | bytes 57376 | tf_op jit(solution)/shard_map/ppermute | solution.py:384
  77.6 1.0 collective-permute-done.21.refs_2_
  78.6 0.6 collective-permute-done.22.refs_3_
  79.2 1.5 %collective-permute-start.26 = (f32[448,128]{1,0:T(8,128)S(1)}, f32[448,128]{1,0:T(8,128)S(1)}, u32[]{:S(2)}, u32[]{:S(2)}) collective-permute-start(f32[448,128]{1,0:T(8,128)S(1)} %pad_maximum_fusion), channel_id=1, source_target_pairs={{0,2},{1,3},{2,0},{3,1},{4,6},{5,7},{6,4},{7,5},{8,10},{9,11},{10,... | collective-permute-start | bytes 688136 | tf_op jit(solution)/shard_map/ppermute | solution.py:399
  80.8 4.5 %collective-permute-done.26.refs_4_ = f32[448,128]{1,0:T(8,128)S(1)} collective-permute-done((f32[448,128]{1,0:T(8,128)S(1)}, f32[448,128]{1,0:T(8,128)S(1)}, u32[]{:S(2)}, u32[]{:S(2)}) %collective-permute-start.26) | collective-permute-done | bytes 229408 | tf_op jit(solution)/shard_map/ppermute | solution.py:399
  85.3 0.1 collective-permute-start.27
  85.4 0.7 collective-permute-start.10
  86.1 2.3 %collective-permute-start.11 = (f32[2,2,32,128]{3,2,1,0:T(8,128)S(1)}, f32[2,2,32,128]{3,2,1,0:T(8,128)S(1)}, u32[]{:S(2)}, u32[]{:S(2)}) collective-permute-start(f32[2,2,32,128]{3,2,1,0:T(8,128)S(1)} %get-tuple-element.92), channel_id=1, source_target_pairs={{0,12},{4,0},{8,4},{12,8},{1,13},{5,1},{9,5},{13,9},{2,14},{6,2},{... | collective-permute-start | bytes 196616 | tf_op jit(solution)/shard_map/ppermute | solution.py:384
  88.4 0.0 collective-permute-start.9
  88.5 1.8 %collective-permute-start.23 = (f32[2,2,32,128]{3,2,1,0:T(8,128)S(1)}, f32[2,2,32,128]{3,2,1,0:T(8,128)S(1)}, u32[]{:S(2)}, u32[]{:S(2)}) collective-permute-start(f32[2,2,32,128]{3,2,1,0:T(8,128)S(1)} %get-tuple-element.90), channel_id=1, source_target_pairs={{0,4},{4,8},{8,12},{12,0},{1,5},{5,9},{9,13},{13,1},{2,6},{6,10},{... | collective-permute-start | bytes 196616 | tf_op jit(solution)/shard_map/ppermute | solution.py:384
  90.3 2.0 %collective-permute-done.10.refs_2_ = f32[2,2,32,128]{3,2,1,0:T(8,128)S(1)} collective-permute-done((f32[2,2,32,128]{3,2,1,0:T(8,128)S(1)}, f32[2,2,32,128]{3,2,1,0:T(8,128)S(1)}, u32[]{:S(2)}, u32[]{:S(2)}) %collective-permute-start.10) | collective-permute-done | bytes 65568 | tf_op jit(solution)/shard_map/ppermute | solution.py:384
  92.3 0.6 collective-permute-start.24
  92.9 0.0 collective-permute-done.11.refs_3_
  92.9 2.4 %collective-permute-start.25 = (f32[2,2,32,128]{3,2,1,0:T(8,128)S(1)}, f32[2,2,32,128]{3,2,1,0:T(8,128)S(1)}, u32[]{:S(2)}, u32[]{:S(2)}) collective-permute-start(f32[2,2,32,128]{3,2,1,0:T(8,128)S(1)} %get-tuple-element.88), channel_id=1, source_target_pairs={{0,12},{4,0},{8,4},{12,8},{1,13},{5,1},{9,5},{13,9},{2,14},{6,2},{... | collective-permute-start | bytes 196616 | tf_op jit(solution)/shard_map/ppermute | solution.py:384
  95.3 1.4 %restore.2 = f32[512,128]{1,0:T(8,128)} custom-call(s32[4]{0:T(128)S(1)} %pad_add_fusion.place, f32[2,2,32,128]{3,2,1,0:T(8,128)S(1)} %get-tuple-element.95.refs_0_, f32[2,2,32,128]{3,2,1,0:T(8,128)S(1)} %collective-permute-done.9.refs_1_, f32[2,2,32,128]{3,2,1,0:T(8,128)S(1)} %collective-permute-done.10.refs_2_, ...), custom_call_target="tpu_custom_call" | custom-call | bytes 589824 | tf_op jit(solution)/shard_map/restore/pallas_call | solution.py:24
  96.8 2.5 %collective-permute-done.24.refs_2_ = f32[2,2,32,128]{3,2,1,0:T(8,128)S(1)} collective-permute-done((f32[2,2,32,128]{3,2,1,0:T(8,128)S(1)}, f32[2,2,32,128]{3,2,1,0:T(8,128)S(1)}, u32[]{:S(2)}, u32[]{:S(2)}) %collective-permute-start.24) | collective-permute-done | bytes 65568 | tf_op jit(solution)/shard_map/ppermute | solution.py:384
  99.3 1.5 %collective-permute-done.25.refs_3_ = f32[2,2,32,128]{3,2,1,0:T(8,128)S(1)} collective-permute-done((f32[2,2,32,128]{3,2,1,0:T(8,128)S(1)}, f32[2,2,32,128]{3,2,1,0:T(8,128)S(1)}, u32[]{:S(2)}, u32[]{:S(2)}) %collective-permute-start.25) | collective-permute-done | bytes 65568 | tf_op jit(solution)/shard_map/ppermute | solution.py:384
  100.8 1.4 %restore.3 = f32[512,128]{1,0:T(8,128)} custom-call(s32[4]{0:T(128)S(1)} %pad_add_fusion.place, f32[2,2,32,128]{3,2,1,0:T(8,128)S(1)} %get-tuple-element.91.refs_0_, f32[2,2,32,128]{3,2,1,0:T(8,128)S(1)} %collective-permute-done.23.refs_1_, f32[2,2,32,128]{3,2,1,0:T(8,128)S(1)} %collective-permute-done.24.refs_2_, ...), custom_call_target="tpu_custom_call" | custom-call | bytes 589824 | tf_op jit(solution)/shard_map/restore/pallas_call | solution.py:24
  102.2 0.0 collective-permute-done.27.refs_5_
  102.2 2.1 %unpack.1 = (f32[2,27,64,64]{3,2,1,0:T(8,128)}, f32[2,64]{1,0:T(2,128)}) custom-call(s32[4]{0:T(128)S(1)} %pad_add_fusion.place, f32[112,128]{1,0:T(8,128)S(1)} %fusion.1.refs_0_, f32[112,128]{1,0:T(8,128)S(1)} %collective-permute-done.20.refs_1_, f32[112,128]{1,0:T(8,128)S(1)} %collective-permute-done.21.refs_2_, ...), custom_call_target="tpu_custom_call" | custom-call | bytes 2720256 | tf_op jit(solution)/shard_map/unpack/pallas_call | solution.py:24
  (24 shorter events, 0.2 us)
Async XLA Ops:
  0.7 1.5 %copy-start = (f32[2,27,64,64]{3,2,1,0:T(8,128)S(1)}, f32[2,27,64,64]{3,2,1,0:T(8,128)}, u32[]{:S(2)}) copy-start(f32[2,27,64,64]{3,2,1,0:T(8,128)} %weights.1) | copy-start | bytes 2654212
  2.2 0.7 copy-start.3
  2.9 3.9 %copy-start.1 = (f32[2,64,2,2,128]{4,3,2,1,0:T(2,128)S(1)}, f32[2,64,2,2,128]{4,3,2,1,0:T(2,128)}, u32[]{:S(2)}) copy-start(f32[2,64,2,2,128]{4,3,2,1,0:T(2,128)} %param.4) | copy-start | bytes 786436
  2.9 3.9 %copy-start.2 = (f32[2,64,2,2,128]{4,3,2,1,0:T(2,128)S(1)}, f32[2,64,2,2,128]{4,3,2,1,0:T(2,128)}, u32[]{:S(2)}) copy-start(f32[2,64,2,2,128]{4,3,2,1,0:T(2,128)} %param.7) | copy-start | bytes 786436
  3.8 18.9 %collective-permute-start = (f32[14,64,128]{2,1,0:T(8,128)S(1)}, f32[14,64,128]{2,1,0:T(8,128)S(1)}, u32[]{:S(2)}, u32[]{:S(2)}) collective-permute-start(f32[14,64,128]{2,1,0:T(8,128)S(1)} %get-tuple-element.48), channel_id=1, source_target_pairs={{0,16},{16,0},{1,17},{17,1},{2,18},{18,2},{3,19},{19,3},{4,20},{20... | collective-permute-start | bytes 1376264 | tf_op jit(solution)/shard_map/ppermute | solution.py:488
  7.6 7.2 %collective-permute-start.4 = (f32[2,2,2,8,128]{4,3,2,1,0:T(8,128)S(1)}, f32[2,2,2,8,128]{4,3,2,1,0:T(8,128)S(1)}, u32[]{:S(2)}, u32[]{:S(2)}) collective-permute-start(f32[2,2,2,8,128]{4,3,2,1,0:T(8,128)S(1)} %get-tuple-element.53), channel_id=1, source_target_pairs={{0,1},{1,2},{2,3},{5,12},{6,13},{7,14},{16,17},{17,18},{18,19},{21... | collective-permute-start | bytes 98312 | tf_op jit(solution)/shard_map/ppermute | solution.py:423
  9.1 8.3 %collective-permute-start.5 = (f32[2,2,2,8,128]{4,3,2,1,0:T(8,128)S(1)}, f32[2,2,2,8,128]{4,3,2,1,0:T(8,128)S(1)}, u32[]{:S(2)}, u32[]{:S(2)}) collective-permute-start(f32[2,2,2,8,128]{4,3,2,1,0:T(8,128)S(1)} %get-tuple-element.54), channel_id=1, source_target_pairs={{4,1},{5,2},{6,3},{9,12},{10,13},{11,14},{20,17},{21,18},{22,19},{... | collective-permute-start | bytes 98312 | tf_op jit(solution)/shard_map/ppermute | solution.py:423
  9.8 9.0 %collective-permute-start.1 = (f32[2,2,48,128]{3,2,1,0:T(8,128)S(1)}, f32[2,2,48,128]{3,2,1,0:T(8,128)S(1)}, u32[]{:S(2)}, u32[]{:S(2)}) collective-permute-start(f32[2,2,48,128]{3,2,1,0:T(8,128)S(1)} %get-tuple-element.50), channel_id=1, source_target_pairs={{0,4},{4,8},{8,12},{12,0},{1,5},{5,9},{9,13},{13,1},{2,6},{6,10},{... | collective-permute-start | bytes 294920 | tf_op jit(solution)/shard_map/ppermute | solution.py:384
  14.8 7.9 %collective-permute-start.2 = (f32[2,2,48,128]{3,2,1,0:T(8,128)S(1)}, f32[2,2,48,128]{3,2,1,0:T(8,128)S(1)}, u32[]{:S(2)}, u32[]{:S(2)}) collective-permute-start(f32[2,2,48,128]{3,2,1,0:T(8,128)S(1)} %get-tuple-element.51), channel_id=1, source_target_pairs={{0,8},{4,12},{8,0},{12,4},{1,9},{5,13},{9,1},{13,5},{2,10},{6,14},... | collective-permute-start | bytes 294920 | tf_op jit(solution)/shard_map/ppermute | solution.py:384
  14.8 7.9 %collective-permute-start.3 = (f32[2,2,48,128]{3,2,1,0:T(8,128)S(1)}, f32[2,2,48,128]{3,2,1,0:T(8,128)S(1)}, u32[]{:S(2)}, u32[]{:S(2)}) collective-permute-start(f32[2,2,48,128]{3,2,1,0:T(8,128)S(1)} %get-tuple-element.52), channel_id=1, source_target_pairs={{0,12},{4,0},{8,4},{12,8},{1,13},{5,1},{9,5},{13,9},{2,14},{6,2},{... | collective-permute-start | bytes 294920 | tf_op jit(solution)/shard_map/ppermute | solution.py:384
  17.4 0.7 collective-permute-start.6
  18.1 0.7 collective-permute-start.7
  22.7 14.5 %collective-permute-start.8 = (f32[14,64,128]{2,1,0:T(8,128)S(1)}, f32[14,64,128]{2,1,0:T(8,128)S(1)}, u32[]{:S(2)}, u32[]{:S(2)}) collective-permute-start(f32[14,64,128]{2,1,0:T(8,128)S(1)} %collective-permute-done.refs_0_), channel_id=1, source_target_pairs={{0,1},{1,0},{2,3},{3,2},{4,5},{5,4},{6,7},{7,6},{8,9},{9,8},{10,11... | collective-permute-start | bytes 1376264 | tf_op jit(solution)/shard_map/ppermute | solution.py:399
  32.1 12.4 %collective-permute-start.12 = (f32[2,2,48,128]{3,2,1,0:T(8,128)S(1)}, f32[2,2,48,128]{3,2,1,0:T(8,128)S(1)}, u32[]{:S(2)}, u32[]{:S(2)}) collective-permute-start(f32[2,2,48,128]{3,2,1,0:T(8,128)S(1)} %get-tuple-element.74), channel_id=1, source_target_pairs={{0,4},{4,8},{8,12},{12,0},{1,5},{5,9},{9,13},{13,1},{2,6},{6,10},{... | collective-permute-start | bytes 294920 | tf_op jit(solution)/shard_map/ppermute | solution.py:384
  32.1 12.4 %collective-permute-start.13 = (f32[2,2,48,128]{3,2,1,0:T(8,128)S(1)}, f32[2,2,48,128]{3,2,1,0:T(8,128)S(1)}, u32[]{:S(2)}, u32[]{:S(2)}) collective-permute-start(f32[2,2,48,128]{3,2,1,0:T(8,128)S(1)} %get-tuple-element.75), channel_id=1, source_target_pairs={{0,8},{4,12},{8,0},{12,4},{1,9},{5,13},{9,1},{13,5},{2,10},{6,14},... | collective-permute-start | bytes 294920 | tf_op jit(solution)/shard_map/ppermute | solution.py:384
  34.4 10.2 %collective-permute-start.14 = (f32[2,2,48,128]{3,2,1,0:T(8,128)S(1)}, f32[2,2,48,128]{3,2,1,0:T(8,128)S(1)}, u32[]{:S(2)}, u32[]{:S(2)}) collective-permute-start(f32[2,2,48,128]{3,2,1,0:T(8,128)S(1)} %get-tuple-element.76), channel_id=1, source_target_pairs={{0,12},{4,0},{8,4},{12,8},{1,13},{5,1},{9,5},{13,9},{2,14},{6,2},{... | collective-permute-start | bytes 294920 | tf_op jit(solution)/shard_map/ppermute | solution.py:384
  52.3 1.9 %collective-permute-start.15 = (f32[896,128]{1,0:T(8,128)S(1)}, f32[896,128]{1,0:T(8,128)S(1)}, u32[]{:S(2)}, u32[]{:S(2)}) collective-permute-start(f32[896,128]{1,0:T(8,128)S(1)} %bitcast.44), channel_id=1, source_target_pairs={{0,1},{1,0},{2,3},{3,2},{4,5},{5,4},{6,7},{7,6},{8,9},{9,8},{10,11... | collective-permute-start | bytes 1376264 | tf_op jit(solution)/shard_map/ppermute | solution.py:399
  54.2 8.8 %collective-permute-start.16 = (f32[448,128]{1,0:T(8,128)S(1)}, f32[448,128]{1,0:T(8,128)S(1)}, u32[]{:S(2)}, u32[]{:S(2)}) collective-permute-start(f32[448,128]{1,0:T(8,128)S(1)} %slice.57), channel_id=1, source_target_pairs={{0,2},{1,3},{2,0},{3,1},{4,6},{5,7},{6,4},{7,5},{8,10},{9,11},{10,... | collective-permute-start | bytes 688136 | tf_op jit(solution)/shard_map/ppermute | solution.py:399
  63.1 6.6 %collective-permute-start.17 = (f32[112,128]{1,0:T(8,128)S(1)}, f32[112,128]{1,0:T(8,128)S(1)}, u32[]{:S(2)}, u32[]{:S(2)}) collective-permute-start(f32[112,128]{1,0:T(8,128)S(1)} %get-tuple-element.96), channel_id=1, source_target_pairs={{0,4},{4,8},{8,12},{12,0},{1,5},{5,9},{9,13},{13,1},{2,6},{6,10},{... | collective-permute-start | bytes 172040 | tf_op jit(solution)/shard_map/ppermute | solution.py:384
  63.7 7.3 %collective-permute-start.18 = (f32[112,128]{1,0:T(8,128)S(1)}, f32[112,128]{1,0:T(8,128)S(1)}, u32[]{:S(2)}, u32[]{:S(2)}) collective-permute-start(f32[112,128]{1,0:T(8,128)S(1)} %get-tuple-element.98), channel_id=1, source_target_pairs={{0,8},{4,12},{8,0},{12,4},{1,9},{5,13},{9,1},{13,5},{2,10},{6,14},... | collective-permute-start | bytes 172040 | tf_op jit(solution)/shard_map/ppermute | solution.py:384
  65.3 5.8 %collective-permute-start.19 = (f32[112,128]{1,0:T(8,128)S(1)}, f32[112,128]{1,0:T(8,128)S(1)}, u32[]{:S(2)}, u32[]{:S(2)}) collective-permute-start(f32[112,128]{1,0:T(8,128)S(1)} %get-tuple-element.97), channel_id=1, source_target_pairs={{0,12},{4,0},{8,4},{12,8},{1,13},{5,1},{9,5},{13,9},{2,14},{6,2},{... | collective-permute-start | bytes 172040 | tf_op jit(solution)/shard_map/ppermute | solution.py:384
  71.1 6.5 %collective-permute-start.20 = (f32[112,128]{1,0:T(8,128)S(1)}, f32[112,128]{1,0:T(8,128)S(1)}, u32[]{:S(2)}, u32[]{:S(2)}) collective-permute-start(f32[112,128]{1,0:T(8,128)S(1)} %fusion.1.refs_0_), channel_id=1, source_target_pairs={{0,4},{4,8},{8,12},{12,0},{1,5},{5,9},{9,13},{13,1},{2,6},{6,10},{... | collective-permute-start | bytes 172040 | tf_op jit(solution)/shard_map/ppermute | solution.py:384
  72.4 6.3 %collective-permute-start.21 = (f32[112,128]{1,0:T(8,128)S(1)}, f32[112,128]{1,0:T(8,128)S(1)}, u32[]{:S(2)}, u32[]{:S(2)}) collective-permute-start(f32[112,128]{1,0:T(8,128)S(1)} %fusion.1.refs_0_), channel_id=1, source_target_pairs={{0,8},{4,12},{8,0},{12,4},{1,9},{5,13},{9,1},{13,5},{2,10},{6,14},... | collective-permute-start | bytes 172040 | tf_op jit(solution)/shard_map/ppermute | solution.py:384
  74.7 4.5 %collective-permute-start.22 = (f32[112,128]{1,0:T(8,128)S(1)}, f32[112,128]{1,0:T(8,128)S(1)}, u32[]{:S(2)}, u32[]{:S(2)}) collective-permute-start(f32[112,128]{1,0:T(8,128)S(1)} %fusion.1.refs_0_), channel_id=1, source_target_pairs={{0,12},{4,0},{8,4},{12,8},{1,13},{5,1},{9,5},{13,9},{2,14},{6,2},{... | collective-permute-start | bytes 172040 | tf_op jit(solution)/shard_map/ppermute | solution.py:384
  79.2 6.1 %collective-permute-start.26 = (f32[448,128]{1,0:T(8,128)S(1)}, f32[448,128]{1,0:T(8,128)S(1)}, u32[]{:S(2)}, u32[]{:S(2)}) collective-permute-start(f32[448,128]{1,0:T(8,128)S(1)} %pad_maximum_fusion), channel_id=1, source_target_pairs={{0,2},{1,3},{2,0},{3,1},{4,6},{5,7},{6,4},{7,5},{8,10},{9,11},{10,... | collective-permute-start | bytes 688136 | tf_op jit(solution)/shard_map/ppermute | solution.py:399
  85.3 16.9 %collective-permute-start.27 = (f32[896,128]{1,0:T(8,128)S(1)}, f32[896,128]{1,0:T(8,128)S(1)}, u32[]{:S(2)}, u32[]{:S(2)}) collective-permute-start(f32[896,128]{1,0:T(8,128)S(1)} %constant_dynamic-update-slice_fusion), channel_id=1, source_target_pairs={{0,1},{1,0},{2,3},{3,2},{4,5},{5,4},{6,7},{7,6},{8,9},{9,8},{10,11... | collective-permute-start | bytes 1376264 | tf_op jit(solution)/shard_map/ppermute | solution.py:399
  85.4 6.9 %collective-permute-start.10 = (f32[2,2,32,128]{3,2,1,0:T(8,128)S(1)}, f32[2,2,32,128]{3,2,1,0:T(8,128)S(1)}, u32[]{:S(2)}, u32[]{:S(2)}) collective-permute-start(f32[2,2,32,128]{3,2,1,0:T(8,128)S(1)} %get-tuple-element.93), channel_id=1, source_target_pairs={{0,8},{4,12},{8,0},{12,4},{1,9},{5,13},{9,1},{13,5},{2,10},{6,14},... | collective-permute-start | bytes 196616 | tf_op jit(solution)/shard_map/ppermute | solution.py:384
  86.1 6.8 %collective-permute-start.11 = (f32[2,2,32,128]{3,2,1,0:T(8,128)S(1)}, f32[2,2,32,128]{3,2,1,0:T(8,128)S(1)}, u32[]{:S(2)}, u32[]{:S(2)}) collective-permute-start(f32[2,2,32,128]{3,2,1,0:T(8,128)S(1)} %get-tuple-element.92), channel_id=1, source_target_pairs={{0,12},{4,0},{8,4},{12,8},{1,13},{5,1},{9,5},{13,9},{2,14},{6,2},{... | collective-permute-start | bytes 196616 | tf_op jit(solution)/shard_map/ppermute | solution.py:384
  88.4 6.9 %collective-permute-start.9 = (f32[2,2,32,128]{3,2,1,0:T(8,128)S(1)}, f32[2,2,32,128]{3,2,1,0:T(8,128)S(1)}, u32[]{:S(2)}, u32[]{:S(2)}) collective-permute-start(f32[2,2,32,128]{3,2,1,0:T(8,128)S(1)} %get-tuple-element.94), channel_id=1, source_target_pairs={{0,4},{4,8},{8,12},{12,0},{1,5},{5,9},{9,13},{13,1},{2,6},{6,10},{... | collective-permute-start | bytes 196616 | tf_op jit(solution)/shard_map/ppermute | solution.py:384
  88.5 8.3 %collective-permute-start.23 = (f32[2,2,32,128]{3,2,1,0:T(8,128)S(1)}, f32[2,2,32,128]{3,2,1,0:T(8,128)S(1)}, u32[]{:S(2)}, u32[]{:S(2)}) collective-permute-start(f32[2,2,32,128]{3,2,1,0:T(8,128)S(1)} %get-tuple-element.90), channel_id=1, source_target_pairs={{0,4},{4,8},{8,12},{12,0},{1,5},{5,9},{9,13},{13,1},{2,6},{6,10},{... | collective-permute-start | bytes 196616 | tf_op jit(solution)/shard_map/ppermute | solution.py:384
  92.3 7.0 %collective-permute-start.24 = (f32[2,2,32,128]{3,2,1,0:T(8,128)S(1)}, f32[2,2,32,128]{3,2,1,0:T(8,128)S(1)}, u32[]{:S(2)}, u32[]{:S(2)}) collective-permute-start(f32[2,2,32,128]{3,2,1,0:T(8,128)S(1)} %get-tuple-element.89), channel_id=1, source_target_pairs={{0,8},{4,12},{8,0},{12,4},{1,9},{5,13},{9,1},{13,5},{2,10},{6,14},... | collective-permute-start | bytes 196616 | tf_op jit(solution)/shard_map/ppermute | solution.py:384
  92.9 7.9 %collective-permute-start.25 = (f32[2,2,32,128]{3,2,1,0:T(8,128)S(1)}, f32[2,2,32,128]{3,2,1,0:T(8,128)S(1)}, u32[]{:S(2)}, u32[]{:S(2)}) collective-permute-start(f32[2,2,32,128]{3,2,1,0:T(8,128)S(1)} %get-tuple-element.88), channel_id=1, source_target_pairs={{0,12},{4,0},{8,4},{12,8},{1,13},{5,1},{9,5},{13,9},{2,14},{6,2},{... | collective-permute-start | bytes 196616 | tf_op jit(solution)/shard_map/ppermute | solution.py:384

commit v4 on v3

--- a/solution.py
+++ b/solution.py
@@ -18,16 +18,19 @@
 VMEM = pl.BlockSpec(memory_space=pltpu.VMEM)
 
 
-def call(kernel, name, outs, args, scratch=(), flops=0):
+def call(kernel, name, outs, args, scratch=(), flops=0, specs=None):
     arrays = [jax.ShapeDtypeStruct(shape, kind) for shape, kind in outs]
-    size = sum(math.prod(item.shape) * item.dtype.itemsize for item in [*arrays, *args[1:], *scratch])
+    sized = [item for item in [*arrays, *args[1:], *scratch] if hasattr(item.dtype, "itemsize")]
+    size = sum(math.prod(item.shape) * item.dtype.itemsize for item in sized)
     return pl.pallas_call(
         kernel,
         out_shape=arrays,
-        in_specs=[SMEM] + [VMEM] * (len(args) - 1),
+        in_specs=[SMEM] + (specs or [VMEM] * (len(args) - 1)),
         out_specs=[VMEM] * len(arrays),
         scratch_shapes=list(scratch),
-        compiler_params=pltpu.CompilerParams(vmem_limit_bytes=size + 6 * 1024 * 1024),
+        compiler_params=pltpu.CompilerParams(
+            vmem_limit_bytes=56 * 1024 * 1024 if specs else size + 6 * 1024 * 1024
+        ),
         cost_estimate=pl.CostEstimate(flops=flops, bytes_accessed=size, transcendentals=0),
         name=name,
     )(*args)
@@ -38,13 +41,40 @@
     return high, (values - high.astype(F32)).astype(BF16)
 
 
-def pack_kernel(place, weights, biases, own, sent):
-    chans = weights.shape[2]
+def start_kernel(dims, place, weights, biases, inflow, cotangent, own, sent, rows, pair, inner, *refs):
+    micros, chans, size_x, local_y, local_z = dims
+    blocks, small, fields, sems = refs
+    copies = [
+        pltpu.make_async_copy(weights, blocks, sems.at[0]),
+        pltpu.make_async_copy(biases, small, sems.at[1]),
+        pltpu.make_async_copy(inflow, fields.at[0], sems.at[2]),
+        pltpu.make_async_copy(cotangent, fields.at[1], sems.at[3]),
+    ]
+    for copy in copies:
+        copy.start()
+    step = size_x * local_y
+    odd = place[4] % 2 == 1
+    for field in range(2):
+        copies[2 + field].wait()
+        for micro in range(micros):
+            for y in range(local_y):
+                first = micro * chans * step + y
+                parts = [
+                    fields[field, pl.ds(first + x * local_y, chans, stride=step), :]
+                    for x in range(size_x)
+                ]
+                turned_rows = jnp.concatenate(parts, axis=0).T
+                rows[field, micro, y] = turned_rows
+                low, high = turned_rows[:HALO], turned_rows[local_z - HALO :]
+                pair[field, micro, y] = jnp.where(odd, low, high)
+                inner[field, micro, y] = jnp.where(odd, high, low)
+    copies[0].wait()
+    copies[1].wait()
     half = sent.shape[0]
     for tap in range(TAPS):
-        own[tap] = jnp.concatenate([weights[0, tap], weights[1, tap]], axis=1)
+        own[tap] = jnp.concatenate([blocks[0, tap], blocks[1, tap]], axis=1)
     own[TAPS] = jnp.zeros((chans, LANES), F32)
-    own[TAPS, 0:1, :] = jnp.concatenate([biases[0:1, :], biases[1:2, :]], axis=1)
+    own[TAPS, 0:1, :] = jnp.concatenate([small[0:1, :], small[1:2, :]], axis=1)
     start = place[2] // 2 * half
 
     def copy(index, carry):
@@ -52,6 +82,28 @@
         return carry
 
     lax.fori_loop(0, half, copy, 0)
+
+
+def window_kernel(dims, place, rows, pair, inner, *refs):
+    slabs, width, span, columns = dims
+    outs, wide = refs[:-1], refs[-1]
+    slab, column = place[1], place[4]
+    odd = column % 2 == 1
+    _, micros, local_y, local_z, _ = rows.shape
+    for field in range(2):
+        for micro in range(micros):
+            for y in range(local_y):
+                one, two = pair[field, micro, y], inner[field, micro, y]
+                before = jnp.where(column > 0, jnp.where(odd, one, two), 0.0)
+                after = jnp.where(column < columns - 1, jnp.where(odd, two, one), 0.0)
+                wide[micro, y, :HALO] = before
+                wide[micro, y, HALO : HALO + local_z] = rows[field, micro, y]
+                wide[micro, y, HALO + local_z :] = after
+                for turn in range(slabs):
+                    start = (slab ^ turn) * width
+                    if width % 8 == 0:
+                        start = pl.multiple_of(start, 8)
+                    outs[field * slabs + turn][micro, y] = wide[micro, y, pl.ds(start, span)]
 
 
 def table_kernel(place, *refs):
@@ -195,16 +247,16 @@
         inner = values.reshape(self.micros, self.chunk_y, self.depth, LANES)
         for y in range(self.chunk_y):
             row = part * self.chunk_y + y
-            to = lax.rem(row // self.per_owner + self.slabs - self.slab, self.slabs)
+            to = (row // self.per_owner) ^ self.slab
             for micro in range(self.micros):
                 value = inner[micro, y, HALO : HALO + self.width, :]
                 target[to, micro, row % self.per_owner] = value
 
-    def fill(self, field, windows, edges, which):
+    def fill(self, field, windows):
         span = windows[0].shape[2]
         for micro in range(self.micros):
             for turn, window in enumerate(windows):
-                owner = lax.rem(self.slab + self.slabs - turn, self.slabs)
+                owner = self.slab ^ turn
                 for y in range(self.per_owner):
                     value = window[micro, y]
                     if span < self.depth:
@@ -212,26 +264,13 @@
                         value = jnp.concatenate([value, extra], axis=0)
                     start = pl.multiple_of((owner * self.per_owner + y) * self.depth, 16)
                     field[0, micro, pl.ds(start, self.depth), :] = value
-        if not edges:
-            return
-        left = self.slab == 0
-        at = jnp.where(left, 0, HALO + self.width)
-
-        @pl.when(left | (self.slab == self.slabs - 1))
-        def _():
-            for m, edge in enumerate(edges):
-                owner = jnp.where(left, m, (m + 1) % self.slabs)
-                for micro in range(self.micros):
-                    for y in range(self.per_owner):
-                        start = pl.multiple_of((owner * self.per_owner + y) * self.depth + at, 8)
-                        field[0, micro, pl.ds(start, HALO), :] = edge[which, micro, y]
 
 
 def forward_kernel(dims, place, own, own_row, other, other_row, *refs):
     slab = Slab(dims, place)
     refs, (acts, kept, front, field) = refs[:-4], refs[-4:]
     slab.blank_edges(acts)
-    slab.fill(field, refs[: slab.slabs], refs[slab.slabs :], 0)
+    slab.fill(field, refs)
     slab.over_chunks(
         lambda part, start: slab.put_rows(acts, 0, start, slab.read(field, 0, start))
     )
@@ -261,7 +300,7 @@
     slab = Slab(dims, place)
     refs, (back, sums, rim, slopes, field, acc) = refs[:-6], refs[-6:]
     slab.blank_edges(rim)
-    slab.fill(field, refs[: slab.slabs], refs[slab.slabs :], 1)
+    slab.fill(field, refs)
 
     def take_gradient(layer, start, gradient):
         slope = slab.masked(gradient * slab.read(kept, layer, start), slab.in_grid)
@@ -339,7 +378,7 @@
     chans = weight.shape[-1]
 
     def put(relative, turn, values):
-        at = (relative ^ swap) * quarter + lax.rem(slab + slabs - turn, slabs) * chunk
+        at = (relative ^ swap) * quarter + (slab ^ turn) * chunk
         whole[pl.ds(pl.multiple_of(at, 8), chunk), :] = values
 
     for turn in range(slabs):
@@ -368,7 +407,7 @@
     for micro in range(micros):
         for y in range(local_y):
             for turn in range(slabs):
-                start = lax.rem(slab + slabs - turn, slabs) * width
+                start = (slab ^ turn) * width
                 if width % 8 == 0:
                     start = pl.multiple_of(start, 8)
                 whole[pl.ds(start, width), :] = pieces[turn][micro, y]
@@ -379,66 +418,22 @@
                 target[pl.ds(first, chans, stride=step), :] = part
 
 
-def turned(block, distance):
-    count = lax.axis_size("gy")
-    return lax.ppermute(block, "gy", [(i, (i + distance) % count) for i in range(count)])
-
-
 def spread(blocks):
     slabs = len(blocks)
     if slabs <= 8:
-        return [blocks[0]] + [turned(blocks[turn], turn) for turn in range(1, slabs)]
-    slab = lax.axis_index("gy")
-    got = lax.all_to_all(jnp.roll(jnp.stack(blocks), slab, axis=0), "gy", 0, 0)
-    got = jnp.roll(got[::-1], slab + 1, axis=0)
+        got = [blocks[0]]
+        for turn in range(1, slabs):
+            route = [(i, i ^ turn) for i in range(slabs)]
+            got.append(lax.ppermute(blocks[turn], "gy", route))
+        return got
+    order = jnp.arange(slabs) ^ lax.axis_index("gy")
+    got = lax.all_to_all(jnp.stack(blocks)[order], "gy", 0, 0)[order]
     return [got[turn] for turn in range(slabs)]
 
 
 def swapped(block, bit):
     count = lax.axis_size("gz")
     return lax.ppermute(block, "gz", [(i, i ^ bit) for i in range(count)])
-
-
-def edge_route(owner):
-    slabs, columns = lax.axis_size("gy"), lax.axis_size("gz")
-    follower = (owner + 1) % slabs
-    route = [(owner * columns + g, g + 1) for g in range(columns - 1)]
-    last = (slabs - 1) * columns
-    return route + [(follower * columns + g, last + g - 1) for g in range(1, columns)]
-
-
-def windows_of(inflow, cotangent, place, slabs, width, span):
-    micros, chans, size_x, local_y, local_z = inflow.shape
-    rows = micros * chans * size_x * local_y
-    edged = width >= HALO and slabs > 1
-    dims = (micros, chans, size_x, local_y, local_z, slabs if edged else 1, width, span, edged, 2)
-    outs = [((micros, local_y, span if edged else local_z, LANES), F32)] * (2 * dims[5])
-    if edged:
-        outs += [((2, micros, local_y, HALO, LANES), F32)] * slabs
-    wide = pltpu.VMEM((2, micros, local_y, local_z + 2 * HALO, LANES), F32)
-    fields = [inflow.reshape(rows, local_z), cotangent.reshape(rows, local_z)]
-    got = call(functools.partial(cut_kernel, dims), "cut", outs, [place, *fields], [wide])
-    if edged:
-        edges = [
-            lax.ppermute(edge, ("gy", "gz"), edge_route(m))
-            for m, edge in enumerate(got[2 * slabs :])
-        ]
-        return spread(got[:slabs]), spread(got[slabs : 2 * slabs]), edges
-    columns = lax.axis_size("gz")
-    slab = lax.axis_index("gy")
-    results = []
-    for field in got:
-        up = [(i, i + 1) for i in range(columns - 1)]
-        down = [(i + 1, i) for i in range(columns - 1)]
-        before = lax.ppermute(field[:, :, local_z - HALO :], "gz", up)
-        after = lax.ppermute(field[:, :, :HALO], "gz", down)
-        wide = jnp.concatenate([before, field, after], axis=2)
-        cuts = [
-            lax.dynamic_slice_in_dim(wide, (slab + turn) % slabs * width, span, axis=2)
-            for turn in range(slabs)
-        ]
-        results.append(spread(cuts))
-    return results[0], results[1], []
 
 
 def summed_over_grid(block):
@@ -451,7 +446,7 @@
     block = jnp.pad(block, ((0, slabs * chunk - block.shape[0]), (0, 0)))
     parts = block.reshape(slabs, chunk, LANES)
     sent = [
-        lax.dynamic_index_in_dim(parts, (slab + turn) % slabs, 0, keepdims=False)
+        lax.dynamic_index_in_dim(parts, slab ^ turn, 0, keepdims=False)
         for turn in range(slabs)
     ]
     return sum(spread(sent))
@@ -480,15 +475,45 @@
     slab, column = lax.axis_index("gy"), lax.axis_index("gz")
     swap = 2 * (column % 2) + column // 2 % 2
     origin = column * local_z + slab * width - HALO
-    place = jnp.stack([lax.axis_index("section"), slab, swap, origin]).astype(jnp.int32)
+    place = [lax.axis_index("section"), slab, swap, origin, column]
+    place = jnp.stack(place).astype(jnp.int32)
 
     half = BLOCKS // 2
-    packs = [((BLOCKS, chans, LANES), F32), ((half, chans, LANES), F32)]
-    own, sent = call(pack_kernel, "pack", packs, [place, weights, biases])
+    rows = micros * chans * size_x * local_y
+    ends = ((2, micros, local_y, HALO, LANES), F32)
+    got = call(
+        functools.partial(start_kernel, inflow.shape),
+        "start",
+        [
+            ((BLOCKS, chans, LANES), F32),
+            ((half, chans, LANES), F32),
+            ((2, micros, local_y, local_z, LANES), F32),
+            ends,
+            ends,
+        ],
+        [place, weights, biases, inflow.reshape(rows, local_z), cotangent.reshape(rows, local_z)],
+        [
+            pltpu.VMEM(weights.shape, F32),
+            pltpu.VMEM(biases.shape, F32),
+            pltpu.VMEM((2, rows, local_z), F32),
+            pltpu.SemaphoreType.DMA((4,)),
+        ],
+        specs=[pl.BlockSpec(memory_space=pl.ANY)] * 4,
+    )
+    own, sent, fields, pair, inner = got
     first = lax.ppermute(sent, "section", [(0, 1), (1, 0)])
-
-    windows, pulls, edges = windows_of(inflow, cotangent, place, slabs, width, span)
-    first, windows, edges = lax.optimization_barrier((first, windows, edges))
+    pair = swapped(pair, 1)
+    route = [(i, i + 1) for i in range(1, columns - 1, 2)]
+    inner = lax.ppermute(inner, "gz", route + [(after, before) for before, after in route])
+    windows = call(
+        functools.partial(window_kernel, (slabs, width, span, columns)),
+        "windows",
+        [((micros, local_y, span, LANES), F32)] * (2 * slabs),
+        [place, fields, pair, inner],
+        [pltpu.VMEM((micros, local_y, local_z + 2 * HALO, LANES), F32)],
+    )
+    flows, pulls = spread(windows[:slabs]), spread(windows[slabs:])
+    first, flows = lax.optimization_barrier((first, flows))
     second = swapped(first, 1)
 
     tables = [((2, 9 * LANES, 3 * LANES), BF16)] * 2 + [((2, 8, LANES), F32)]
@@ -504,7 +529,7 @@
         functools.partial(forward_kernel, dims),
         "forward",
         [((4, micros, padded, 2 * LANES), BF16), ((4, micros, full, LANES), F32), piece],
-        [place, own_fwd, own_row, far_fwd, far_row, *windows, *edges],
+        [place, own_fwd, own_row, far_fwd, far_row, *flows],
         [pltpu.VMEM((1, micros, full, LANES), F32)],
         4 * work,
     )
@@ -513,7 +538,7 @@
         functools.partial(backward_kernel, dims, scale),
         "backward",
         [piece, ((BLOCKS, chans, LANES), F32)],
-        [place, own_bwd, far_bwd, acts, kept, *pulls, *edges],
+        [place, own_bwd, far_bwd, acts, kept, *pulls],
         [
             pltpu.VMEM((2, micros, padded, 2 * LANES), BF16),
             pltpu.VMEM((4, micros, full, LANES), F32),
@@ -523,12 +548,14 @@
         6 * work,
     )
 
+    sums, outward = lax.optimization_barrier((sums, outward))
     mine = summed_over_grid(sums.reshape(BLOCKS * chans, LANES))
     near = spread([mine] * slabs)
     near, back = lax.optimization_barrier((near, back))
     quarter = jnp.concatenate(near, axis=0)
     beside = swapped(quarter, 2)
     inward = spread([back[turn] for turn in range(slabs)])
+    beside, inward = lax.optimization_barrier((beside, inward))
     across = swapped(jnp.concatenate([quarter, beside], axis=0), 1)
     section_out = restored(outward, inflow.shape, place)
     section_grad = restored(inward, inflow.shape, place)

time: 105 us -> 94 us (0.90)
  starting transfers between devices: 48.5 us -> 36.6 us
  Pallas kernels: 22.9 us -> 25.9 us
  waiting for transfers between devices: 29.5 us -> 27.2 us
    ppermute x5 -> x6, starting transfers between devices: 14 us -> 6.22 us  [swapped(): return lax.ppermute(block, 'gz', [(i, i ^ bit) for i in range(count)])]
    ppermute x22 -> x19, starting transfers between devices: 31.5 us -> 27.4 us  [the longest x18 26.7 us: spread(): got.append(lax.ppermute(blocks[turn], 'gy', route))]
    ppermute x5 -> x6, waiting for transfers between devices: 12.3 us -> 8.47 us  [swapped(): return lax.ppermute(block, 'gz', [(i, i ^ bit) for i in range(count)])]
    pallas_call x9, Pallas kernels: 22.9 us -> 25.9 us  [call(): pl.pallas_call(kernel, out_shape=arrays, in_specs=[SMEM] + (specs or [VME...]
    ppermute x22 -> x19, waiting for transfers between devices: 17.2 us -> 18.7 us  [the longest x18 18.7 us: spread(): got.append(lax.ppermute(blocks[turn], 'gy', route))]
    unnamed x12 -> x10, local copies, waits for them, and re-layouts: 2.19 us -> 2.24 us
  transfers between devices with their start and end apart: 28 -> 26, of which waited for: 12 -> 12; matrix products, arithmetic and copies ran while one was open for 0% -> 0% of each run, Pallas kernels for 12% -> 21%
where the time goes in v4:
time: 94 us; the launch traced here: 93.7 us
  starting transfers between devices  36.6 us (39%)
  waiting for transfers between devices  27.2 us (29%)
  Pallas kernels  25.9 us (28%)
  local copies, waits for them, and re-layouts  3.08 us (3%)
    ppermute x18, starting transfers between devices, spread(): got.append(lax.ppermute(blocks[turn], 'gy', route))  26.7 us
    pallas_call x9, Pallas kernels, call(): pl.pallas_call(kernel, out_shape=arrays, in_specs=[SMEM] + (specs or [VME...  25.9 us
    ppermute x18, waiting for transfers between devices, spread(): got.append(lax.ppermute(blocks[turn], 'gy', route))  18.7 us
    ppermute x6, waiting for transfers between devices, swapped(): return lax.ppermute(block, 'gz', [(i, i ^ bit) for i in range(count)])  8.47 us
    ppermute x6, starting transfers between devices, swapped(): return lax.ppermute(block, 'gz', [(i, i ^ bit) for i in range(count)])  6.22 us
    ppermute x1, starting transfers between devices, per_device(): first = lax.ppermute(sent, 'section', [(0, 1), (1, 0)])  3 us
    unnamed x10, local copies, waits for them, and re-layouts  2.24 us
  transfers between devices with their start and end apart: 26, of which 12 were waited for; matrix products, arithmetic and copies ran while one was open for 0% of the time, Pallas kernels for 21%

profile of v4, /device:TPU:0, one launch (start us, length us, event | category | flops | bytes accessed | tf_op | source)
XLA Modules:
  0.0 93.7 jit_solution(5495623622392419327)
XLA Ops:
  0.7 0.7 stack.23.place
  1.4 4.2 %start.1 = (f32[28,64,128]{2,1,0:T(8,128)}, f32[14,64,128]{2,1,0:T(8,128)}, f32[2,2,2,128,128]{4,3,2,1,0:T(8,128)}, f32[2,2,2,8,128]{4,3,2,1,0:T(8,128)}, f32[2,2,2,8,128]{4,3,2,1,0:T(8,128)}) custom-call(s32[5]{0:T(128)} %stack.23.place, f32[2,27,64,64]{3,2,1,0:T(8,128)} %weights.1, f32[2,64]{1,0:T(2,128)} %biases.1, f32[512,128]{1,0:T(8,128)} %bitcast.44, ...), custom_call_target="tpu_custom_call" | custom-call | bytes 4785152 | tf_op jit(solution)/shard_map/start/pallas_call | solution.py:25
  5.5 3.0 %collective-permute-start = (f32[14,64,128]{2,1,0:T(8,128)}, f32[14,64,128]{2,1,0:T(8,128)S(1)}, u32[]{:S(2)}, u32[]{:S(2)}) collective-permute-start(f32[14,64,128]{2,1,0:T(8,128)} %get-tuple-element.52), channel_id=1, source_target_pairs={{0,16},{16,0},{1,17},{17,1},{2,18},{18,2},{3,19},{19,3},{4,20},{20... | collective-permute-start | bytes 1376264 | tf_op jit(solution)/shard_map/ppermute | solution.py:504
  8.5 0.0 collective-permute-start.1
  8.6 0.7 collective-permute-start.2
  9.2 0.8 collective-permute-done.1.pair
  10.0 0.0 collective-permute-done.2.inner
  10.0 1.0 %copy-done.1 = f32[2,2,2,128,128]{4,3,2,1,0:T(8,128)S(1)} copy-done((f32[2,2,2,128,128]{4,3,2,1,0:T(8,128)S(1)}, f32[2,2,2,128,128]{4,3,2,1,0:T(8,128)}, u32[]{:S(2)}) %copy-start.1) | copy-done | bytes 524312
  11.0 0.7 windows.1
  11.7 1.6 %collective-permute-start.3 = (f32[2,2,48,128]{3,2,1,0:T(8,128)S(1)}, f32[2,2,48,128]{3,2,1,0:T(8,128)S(1)}, u32[]{:S(2)}, u32[]{:S(2)}) collective-permute-start(f32[2,2,48,128]{3,2,1,0:T(8,128)S(1)} %get-tuple-element.57), channel_id=1, source_target_pairs={{0,4},{4,0},{8,12},{12,8},{1,5},{5,1},{9,13},{13,9},{2,6},{6,2},{1... | collective-permute-start | bytes 294920 | tf_op jit(solution)/shard_map/ppermute | solution.py:427
  13.3 2.6 %collective-permute-start.4 = (f32[2,2,48,128]{3,2,1,0:T(8,128)S(1)}, f32[2,2,48,128]{3,2,1,0:T(8,128)S(1)}, u32[]{:S(2)}, u32[]{:S(2)}) collective-permute-start(f32[2,2,48,128]{3,2,1,0:T(8,128)S(1)} %get-tuple-element.58), channel_id=1, source_target_pairs={{0,8},{4,12},{8,0},{12,4},{1,9},{5,13},{9,1},{13,5},{2,10},{6,14},... | collective-permute-start | bytes 294920 | tf_op jit(solution)/shard_map/ppermute | solution.py:427
  15.9 0.2 collective-permute-start.5
  16.1 0.2 collective-permute-done.3.refs_1_
  16.4 3.6 %collective-permute-done.4.refs_2_ = f32[2,2,48,128]{3,2,1,0:T(8,128)S(1)} collective-permute-done((f32[2,2,48,128]{3,2,1,0:T(8,128)S(1)}, f32[2,2,48,128]{3,2,1,0:T(8,128)S(1)}, u32[]{:S(2)}, u32[]{:S(2)}) %collective-permute-start.4) | collective-permute-done | bytes 98336 | tf_op jit(solution)/shard_map/ppermute | solution.py:427
  20.0 3.5 %collective-permute-done.5.refs_3_ = f32[2,2,48,128]{3,2,1,0:T(8,128)S(1)} collective-permute-done((f32[2,2,48,128]{3,2,1,0:T(8,128)S(1)}, f32[2,2,48,128]{3,2,1,0:T(8,128)S(1)}, u32[]{:S(2)}, u32[]{:S(2)}) %collective-permute-start.5) | collective-permute-done | bytes 98336 | tf_op jit(solution)/shard_map/ppermute | solution.py:427
  23.5 0.0 collective-permute-done.refs_0_
  23.5 2.0 %collective-permute-start.6 = (f32[14,64,128]{2,1,0:T(8,128)S(1)}, f32[14,64,128]{2,1,0:T(8,128)S(1)}, u32[]{:S(2)}, u32[]{:S(2)}) collective-permute-start(f32[14,64,128]{2,1,0:T(8,128)S(1)} %collective-permute-done.refs_0_), channel_id=1, source_target_pairs={{0,1},{1,0},{2,3},{3,2},{4,5},{5,4},{6,7},{7,6},{8,9},{9,8},{10,11... | collective-permute-start | bytes 1376264 | tf_op jit(solution)/shard_map/ppermute | solution.py:436
  25.5 1.2 %copy-done = f32[28,64,128]{2,1,0:T(8,128)S(1)} copy-done((f32[28,64,128]{2,1,0:T(8,128)S(1)}, f32[28,64,128]{2,1,0:T(8,128)}, u32[]{:S(2)}) %copy-start) | copy-done | bytes 917528
  26.7 1.2 %own_table.1 = (bf16[2,1152,384]{2,1,0:T(8,128)(2,1)S(1)}, bf16[2,1152,384]{2,1,0:T(8,128)(2,1)S(1)}, f32[2,8,128]{2,1,0:T(8,128)S(1)}) custom-call(s32[5]{0:T(128)S(1)} %copy-done.2, f32[28,64,128]{2,1,0:T(8,128)S(1)} %copy-done), custom_call_target="tpu_custom_call" | custom-call | bytes 4464640 | tf_op jit(solution)/shard_map/own_table/pallas_call | solution.py:25
  27.9 1.5 %collective-permute-start.7 = (f32[2,2,48,128]{3,2,1,0:T(8,128)S(1)}, f32[2,2,48,128]{3,2,1,0:T(8,128)S(1)}, u32[]{:S(2)}, u32[]{:S(2)}) collective-permute-start(f32[2,2,48,128]{3,2,1,0:T(8,128)S(1)} %get-tuple-element.73), channel_id=1, source_target_pairs={{0,4},{4,0},{8,12},{12,8},{1,5},{5,1},{9,13},{13,9},{2,6},{6,2},{1... | collective-permute-start | bytes 294920 | tf_op jit(solution)/shard_map/ppermute | solution.py:427
  29.4 1.1 %collective-permute-start.8 = (f32[2,2,48,128]{3,2,1,0:T(8,128)S(1)}, f32[2,2,48,128]{3,2,1,0:T(8,128)S(1)}, u32[]{:S(2)}, u32[]{:S(2)}) collective-permute-start(f32[2,2,48,128]{3,2,1,0:T(8,128)S(1)} %get-tuple-element.74), channel_id=1, source_target_pairs={{0,8},{4,12},{8,0},{12,4},{1,9},{5,13},{9,1},{13,5},{2,10},{6,14},... | collective-permute-start | bytes 294920 | tf_op jit(solution)/shard_map/ppermute | solution.py:427
  30.5 1.9 %collective-permute-start.9 = (f32[2,2,48,128]{3,2,1,0:T(8,128)S(1)}, f32[2,2,48,128]{3,2,1,0:T(8,128)S(1)}, u32[]{:S(2)}, u32[]{:S(2)}) collective-permute-start(f32[2,2,48,128]{3,2,1,0:T(8,128)S(1)} %get-tuple-element.75), channel_id=1, source_target_pairs={{0,12},{4,8},{8,4},{12,0},{1,13},{5,9},{9,5},{13,1},{2,14},{6,10},... | collective-permute-start | bytes 294920 | tf_op jit(solution)/shard_map/ppermute | solution.py:427
  32.4 0.0 collective-permute-done.6.refs_1_
  32.4 1.3 %far_table.1 = (bf16[2,1152,384]{2,1,0:T(8,128)(2,1)S(1)}, bf16[2,1152,384]{2,1,0:T(8,128)(2,1)S(1)}, f32[2,8,128]{2,1,0:T(8,128)S(1)}) custom-call(s32[5]{0:T(128)S(1)} %copy-done.2, f32[14,64,128]{2,1,0:T(8,128)S(1)} %collective-permute-done.refs_0_, f32[14,64,128]{2,1,0:T(8,128)S(1)} %collective-permute-done.6.refs_1_), custom_call_target="tpu_custom_call" | custom-call | bytes 4464640 | tf_op jit(solution)/shard_map/far_table/pallas_call | solution.py:25
  33.7 6.1 %forward.1 = (bf16[4,2,480,256]{3,2,1,0:T(8,128)(2,1)S(1)}, f32[4,2,384,128]{3,2,1,0:T(8,128)S(1)}, f32[4,2,2,32,128]{4,3,2,1,0:T(8,128)S(1)}) custom-call(s32[5]{0:T(128)S(1)} %copy-done.2, bf16[2,1152,384]{2,1,0:T(8,128)(2,1)S(1)} %get-tuple-element.62.own, f32[2,8,128]{2,1,0:T(8,128)S(1)} %get-tuple-element.63.own_row, ...), custom_call_target="tpu_custom_call" | custom-call | flops 2717908992 | bytes 8142848 | tf_op jit(solution)/shard_map/forward/pallas_call | solution.py:25
  39.8 0.6 collective-permute-start.10
  40.4 2.0 %collective-permute-start.11 = (f32[2,2,32,128]{3,2,1,0:T(8,128)S(1)}, f32[2,2,32,128]{3,2,1,0:T(8,128)S(1)}, u32[]{:S(2)}, u32[]{:S(2)}) collective-permute-start(f32[2,2,32,128]{3,2,1,0:T(8,128)S(1)} %get-tuple-element.103), channel_id=1, source_target_pairs={{0,8},{4,12},{8,0},{12,4},{1,9},{5,13},{9,1},{13,5},{2,10},{6,14},... | collective-permute-start | bytes 196616 | tf_op jit(solution)/shard_map/ppermute | solution.py:427
  42.4 0.0 collective-permute-done.7.refs_1_
  42.4 1.9 %collective-permute-start.12 = (f32[2,2,32,128]{3,2,1,0:T(8,128)S(1)}, f32[2,2,32,128]{3,2,1,0:T(8,128)S(1)}, u32[]{:S(2)}, u32[]{:S(2)}) collective-permute-start(f32[2,2,32,128]{3,2,1,0:T(8,128)S(1)} %get-tuple-element.102), channel_id=1, source_target_pairs={{0,12},{4,8},{8,4},{12,0},{1,13},{5,9},{9,5},{13,1},{2,14},{6,10},... | collective-permute-start | bytes 196616 | tf_op jit(solution)/shard_map/ppermute | solution.py:427
  44.2 0.0 collective-permute-done.8.refs_2_
  44.2 0.0 collective-permute-done.9.refs_3_
  44.2 7.6 %backward.1 = (f32[4,2,2,32,128]{4,3,2,1,0:T(8,128)S(1)}, f32[28,64,128]{2,1,0:T(8,128)S(1)}) custom-call(s32[5]{0:T(128)S(1)} %copy-done.2, bf16[2,1152,384]{2,1,0:T(8,128)(2,1)S(1)} %get-tuple-element.51.own, bf16[2,1152,384]{2,1,0:T(8,128)(2,1)S(1)} %get-tuple-element.61.other, bf16[4,2,480,256]{3,2,1,0:T(8,128)(2,1)S(1)} %get-tuple-element.70.acts, ...), custom_call_target="tpu_custom_call" | custom-call | flops 4076863488 | bytes 12201984 | tf_op jit(solution)/shard_map/backward/pallas_call | solution.py:25
  51.8 0.0 collective-permute-done.10.refs_1_
  51.8 0.0 collective-permute-done.11.refs_2_
  51.8 0.0 collective-permute-done.12.refs_3_
  51.8 0.1 fusion.2
  51.9 0.1 collective-permute-start.13
  52.0 1.8 %collective-permute-done.13 = f32[896,128]{1,0:T(8,128)S(1)} collective-permute-done((f32[896,128]{1,0:T(8,128)S(1)}, f32[896,128]{1,0:T(8,128)S(1)}, u32[]{:S(2)}, u32[]{:S(2)}) %collective-permute-start.13) | collective-permute-done | bytes 458784 | tf_op jit(solution)/shard_map/ppermute | solution.py:436
  53.8 0.1 bitcast_add_fusion
  53.9 2.4 %collective-permute-start.14 = (f32[448,128]{1,0:T(8,128)S(1)}, f32[448,128]{1,0:T(8,128)S(1)}, u32[]{:S(2)}, u32[]{:S(2)}) collective-permute-start(f32[448,128]{1,0:T(8,128)S(1)} %slice.57), channel_id=1, source_target_pairs={{0,2},{1,3},{2,0},{3,1},{4,6},{5,7},{6,4},{7,5},{8,10},{9,11},{10,... | collective-permute-start | bytes 688136 | tf_op jit(solution)/shard_map/ppermute | solution.py:436
  56.3 5.9 %collective-permute-done.14 = f32[448,128]{1,0:T(8,128)S(1)} collective-permute-done((f32[448,128]{1,0:T(8,128)S(1)}, f32[448,128]{1,0:T(8,128)S(1)}, u32[]{:S(2)}, u32[]{:S(2)}) %collective-permute-start.14) | collective-permute-done | bytes 229408 | tf_op jit(solution)/shard_map/ppermute | solution.py:436
  62.3 1.4 %collective-permute-start.17 = (f32[112,128]{1,0:T(8,128)S(1)}, f32[112,128]{1,0:T(8,128)S(1)}, u32[]{:S(2)}, u32[]{:S(2)}) collective-permute-start(f32[112,128]{1,0:T(8,128)S(1)} %get-tuple-element.107), channel_id=1, source_target_pairs={{0,12},{4,8},{8,4},{12,0},{1,13},{5,9},{9,5},{13,1},{2,14},{6,10},... | collective-permute-start | bytes 172040 | tf_op jit(solution)/shard_map/ppermute | solution.py:427
  63.7 0.0 collective-permute-start.16
  63.7 3.1 %collective-permute-start.15 = (f32[112,128]{1,0:T(8,128)S(1)}, f32[112,128]{1,0:T(8,128)S(1)}, u32[]{:S(2)}, u32[]{:S(2)}) collective-permute-start(f32[112,128]{1,0:T(8,128)S(1)} %get-tuple-element.106), channel_id=1, source_target_pairs={{0,4},{4,0},{8,12},{12,8},{1,5},{5,1},{9,13},{13,9},{2,6},{6,2},{1... | collective-permute-start | bytes 172040 | tf_op jit(solution)/shard_map/ppermute | solution.py:427
  66.7 2.2 %collective-permute-done.17 = f32[112,128]{1,0:T(8,128)S(1)} collective-permute-done((f32[112,128]{1,0:T(8,128)S(1)}, f32[112,128]{1,0:T(8,128)S(1)}, u32[]{:S(2)}, u32[]{:S(2)}) %collective-permute-start.17) | collective-permute-done | bytes 57376 | tf_op jit(solution)/shard_map/ppermute | solution.py:427
  68.9 1.0 %collective-permute-done.16 = f32[112,128]{1,0:T(8,128)S(1)} collective-permute-done((f32[112,128]{1,0:T(8,128)S(1)}, f32[112,128]{1,0:T(8,128)S(1)}, u32[]{:S(2)}, u32[]{:S(2)}) %collective-permute-start.16) | collective-permute-done | bytes 57376 | tf_op jit(solution)/shard_map/ppermute | solution.py:427
  69.9 0.0 collective-permute-done.15
  69.9 1.1 %collective-permute-start.18 = (f32[112,128]{1,0:T(8,128)S(1)}, f32[112,128]{1,0:T(8,128)S(1)}, u32[]{:S(2)}, u32[]{:S(2)}) collective-permute-start(f32[112,128]{1,0:T(8,128)S(1)} %fusion.1.refs_0_), channel_id=1, source_target_pairs={{0,4},{4,0},{8,12},{12,8},{1,5},{5,1},{9,13},{13,9},{2,6},{6,2},{1... | collective-permute-start | bytes 172040 | tf_op jit(solution)/shard_map/ppermute | solution.py:427
  71.0 1.1 %collective-permute-start.19 = (f32[112,128]{1,0:T(8,128)S(1)}, f32[112,128]{1,0:T(8,128)S(1)}, u32[]{:S(2)}, u32[]{:S(2)}) collective-permute-start(f32[112,128]{1,0:T(8,128)S(1)} %fusion.1.refs_0_), channel_id=1, source_target_pairs={{0,8},{4,12},{8,0},{12,4},{1,9},{5,13},{9,1},{13,5},{2,10},{6,14},... | collective-permute-start | bytes 172040 | tf_op jit(solution)/shard_map/ppermute | solution.py:427
  72.1 2.2 %collective-permute-start.20 = (f32[112,128]{1,0:T(8,128)S(1)}, f32[112,128]{1,0:T(8,128)S(1)}, u32[]{:S(2)}, u32[]{:S(2)}) collective-permute-start(f32[112,128]{1,0:T(8,128)S(1)} %fusion.1.refs_0_), channel_id=1, source_target_pairs={{0,12},{4,8},{8,4},{12,0},{1,13},{5,9},{9,5},{13,1},{2,14},{6,10},... | collective-permute-start | bytes 172040 | tf_op jit(solution)/shard_map/ppermute | solution.py:427
  74.4 0.0 collective-permute-done.18.refs_1_
  74.4 2.9 %collective-permute-done.19.refs_2_ = f32[112,128]{1,0:T(8,128)S(1)} collective-permute-done((f32[112,128]{1,0:T(8,128)S(1)}, f32[112,128]{1,0:T(8,128)S(1)}, u32[]{:S(2)}, u32[]{:S(2)}) %collective-permute-start.19) | collective-permute-done | bytes 57376 | tf_op jit(solution)/shard_map/ppermute | solution.py:427
  77.3 0.9 collective-permute-done.20.refs_3_
  78.2 1.6 %collective-permute-start.21 = (f32[448,128]{1,0:T(8,128)S(1)}, f32[448,128]{1,0:T(8,128)S(1)}, u32[]{:S(2)}, u32[]{:S(2)}) collective-permute-start(f32[448,128]{1,0:T(8,128)S(1)} %pad_maximum_fusion), channel_id=1, source_target_pairs={{0,2},{1,3},{2,0},{3,1},{4,6},{5,7},{6,4},{7,5},{8,10},{9,11},{10,... | collective-permute-start | bytes 688136 | tf_op jit(solution)/shard_map/ppermute | solution.py:436
  79.9 0.1 collective-permute-start.22
  80.0 2.7 %collective-permute-start.23 = (f32[2,2,32,128]{3,2,1,0:T(8,128)S(1)}, f32[2,2,32,128]{3,2,1,0:T(8,128)S(1)}, u32[]{:S(2)}, u32[]{:S(2)}) collective-permute-start(f32[2,2,32,128]{3,2,1,0:T(8,128)S(1)} %get-tuple-element.99), channel_id=1, source_target_pairs={{0,8},{4,12},{8,0},{12,4},{1,9},{5,13},{9,1},{13,5},{2,10},{6,14},... | collective-permute-start | bytes 196616 | tf_op jit(solution)/shard_map/ppermute | solution.py:427
  82.7 1.7 %collective-permute-start.24 = (f32[2,2,32,128]{3,2,1,0:T(8,128)S(1)}, f32[2,2,32,128]{3,2,1,0:T(8,128)S(1)}, u32[]{:S(2)}, u32[]{:S(2)}) collective-permute-start(f32[2,2,32,128]{3,2,1,0:T(8,128)S(1)} %get-tuple-element.98), channel_id=1, source_target_pairs={{0,12},{4,8},{8,4},{12,0},{1,13},{5,9},{9,5},{13,1},{2,14},{6,10},... | collective-permute-start | bytes 196616 | tf_op jit(solution)/shard_map/ppermute | solution.py:427
  84.4 1.3 %collective-permute-done.22.refs_1_ = f32[2,2,32,128]{3,2,1,0:T(8,128)S(1)} collective-permute-done((f32[2,2,32,128]{3,2,1,0:T(8,128)S(1)}, f32[2,2,32,128]{3,2,1,0:T(8,128)S(1)}, u32[]{:S(2)}, u32[]{:S(2)}) %collective-permute-start.22) | collective-permute-done | bytes 65568 | tf_op jit(solution)/shard_map/ppermute | solution.py:427
  85.6 3.1 %collective-permute-done.24.refs_3_ = f32[2,2,32,128]{3,2,1,0:T(8,128)S(1)} collective-permute-done((f32[2,2,32,128]{3,2,1,0:T(8,128)S(1)}, f32[2,2,32,128]{3,2,1,0:T(8,128)S(1)}, u32[]{:S(2)}, u32[]{:S(2)}) %collective-permute-start.24) | collective-permute-done | bytes 65568 | tf_op jit(solution)/shard_map/ppermute | solution.py:427
  88.8 0.1 collective-permute-start.25
  88.8 1.4 %restore.2 = f32[512,128]{1,0:T(8,128)} custom-call(s32[5]{0:T(128)S(1)} %copy-done.2, f32[2,2,32,128]{3,2,1,0:T(8,128)S(1)} %get-tuple-element.78.refs_0_, f32[2,2,32,128]{3,2,1,0:T(8,128)S(1)} %collective-permute-done.10.refs_1_, f32[2,2,32,128]{3,2,1,0:T(8,128)S(1)} %collective-permute-done.11.refs_2_, f32[2,2,32,128]{3,2,1,0:T(8,128)S(1)} %collective-permute-done.12.refs_3_), custom_call_target="tpu_custom_call" | custom-call | bytes 589824 | tf_op jit(solution)/shard_map/restore/pallas_call | solution.py:25
  90.2 1.4 %restore.3 = f32[512,128]{1,0:T(8,128)} custom-call(s32[5]{0:T(128)S(1)} %copy-done.2, f32[2,2,32,128]{3,2,1,0:T(8,128)S(1)} %get-tuple-element.89.refs_0_, f32[2,2,32,128]{3,2,1,0:T(8,128)S(1)} %collective-permute-done.22.refs_1_, f32[2,2,32,128]{3,2,1,0:T(8,128)S(1)} %collective-permute-done.23.refs_2_, f32[2,2,32,128]{3,2,1,0:T(8,128)S(1)} %collective-permute-done.24.refs_3_), custom_call_target="tpu_custom_call" | custom-call | bytes 589824 | tf_op jit(solution)/shard_map/restore/pallas_call | solution.py:25
  91.6 0.0 collective-permute-done.25.refs_5_
  91.6 2.1 %unpack.1 = (f32[2,27,64,64]{3,2,1,0:T(8,128)}, f32[2,64]{1,0:T(2,128)}) custom-call(s32[5]{0:T(128)S(1)} %copy-done.2, f32[112,128]{1,0:T(8,128)S(1)} %fusion.1.refs_0_, f32[112,128]{1,0:T(8,128)S(1)} %collective-permute-done.18.refs_1_, f32[112,128]{1,0:T(8,128)S(1)} %collective-permute-done.19.refs_2_, f32[112,128]{1,0:T(8,128)S(1)} %collective-permute-done.20.refs_3_, ...), custom_call_target="tpu_custom_call" | custom-call | bytes 2720256 | tf_op jit(solution)/shard_map/unpack/pallas_call | solution.py:25
  (18 shorter events, 0.2 us)
Async XLA Ops:
  1.4 8.6 %copy-start.2 = (s32[5]{0:T(128)S(1)}, s32[5]{0:T(128)}, u32[]{:S(2)}) copy-start(s32[5]{0:T(128)} %stack.23.place) | copy-start | bytes 64
  5.5 17.9 %collective-permute-start = (f32[14,64,128]{2,1,0:T(8,128)}, f32[14,64,128]{2,1,0:T(8,128)S(1)}, u32[]{:S(2)}, u32[]{:S(2)}) collective-permute-start(f32[14,64,128]{2,1,0:T(8,128)} %get-tuple-element.52), channel_id=1, source_target_pairs={{0,16},{16,0},{1,17},{17,1},{2,18},{18,2},{3,19},{19,3},{4,20},{20... | collective-permute-start | bytes 1376264 | tf_op jit(solution)/shard_map/ppermute | solution.py:504
  8.5 1.4 %collective-permute-start.1 = (f32[2,2,2,8,128]{4,3,2,1,0:T(8,128)}, f32[2,2,2,8,128]{4,3,2,1,0:T(8,128)S(1)}, u32[]{:S(2)}, u32[]{:S(2)}) collective-permute-start(f32[2,2,2,8,128]{4,3,2,1,0:T(8,128)} %get-tuple-element.54), channel_id=1, source_target_pairs={{0,1},{1,0},{2,3},{3,2},{4,5},{5,4},{6,7},{7,6},{8,9},{9,8},{10,11... | collective-permute-start | bytes 98312 | tf_op jit(solution)/shard_map/ppermute | solution.py:436
  8.6 1.4 %collective-permute-start.2 = (f32[2,2,2,8,128]{4,3,2,1,0:T(8,128)}, f32[2,2,2,8,128]{4,3,2,1,0:T(8,128)S(1)}, u32[]{:S(2)}, u32[]{:S(2)}) collective-permute-start(f32[2,2,2,8,128]{4,3,2,1,0:T(8,128)} %get-tuple-element.55), channel_id=1, source_target_pairs={{1,2},{2,1},{5,6},{6,5},{9,10},{10,9},{13,14},{14,13},{17,18},{18,... | collective-permute-start | bytes 98312 | tf_op jit(solution)/shard_map/ppermute | solution.py:507
  10.0 1.0 %copy-start.1 = (f32[2,2,2,128,128]{4,3,2,1,0:T(8,128)S(1)}, f32[2,2,2,128,128]{4,3,2,1,0:T(8,128)}, u32[]{:S(2)}) copy-start(f32[2,2,2,128,128]{4,3,2,1,0:T(8,128)} %get-tuple-element.53.rows) | copy-start | bytes 1572868
  11.7 4.7 %collective-permute-start.3 = (f32[2,2,48,128]{3,2,1,0:T(8,128)S(1)}, f32[2,2,48,128]{3,2,1,0:T(8,128)S(1)}, u32[]{:S(2)}, u32[]{:S(2)}) collective-permute-start(f32[2,2,48,128]{3,2,1,0:T(8,128)S(1)} %get-tuple-element.57), channel_id=1, source_target_pairs={{0,4},{4,0},{8,12},{12,8},{1,5},{5,1},{9,13},{13,9},{2,6},{6,2},{1... | collective-permute-start | bytes 294920 | tf_op jit(solution)/shard_map/ppermute | solution.py:427
  13.3 6.7 %collective-permute-start.4 = (f32[2,2,48,128]{3,2,1,0:T(8,128)S(1)}, f32[2,2,48,128]{3,2,1,0:T(8,128)S(1)}, u32[]{:S(2)}, u32[]{:S(2)}) collective-permute-start(f32[2,2,48,128]{3,2,1,0:T(8,128)S(1)} %get-tuple-element.58), channel_id=1, source_target_pairs={{0,8},{4,12},{8,0},{12,4},{1,9},{5,13},{9,1},{13,5},{2,10},{6,14},... | collective-permute-start | bytes 294920 | tf_op jit(solution)/shard_map/ppermute | solution.py:427
  15.9 7.6 %collective-permute-start.5 = (f32[2,2,48,128]{3,2,1,0:T(8,128)S(1)}, f32[2,2,48,128]{3,2,1,0:T(8,128)S(1)}, u32[]{:S(2)}, u32[]{:S(2)}) collective-permute-start(f32[2,2,48,128]{3,2,1,0:T(8,128)S(1)} %get-tuple-element.59), channel_id=1, source_target_pairs={{0,12},{4,8},{8,4},{12,0},{1,13},{5,9},{9,5},{13,1},{2,14},{6,10},... | collective-permute-start | bytes 294920 | tf_op jit(solution)/shard_map/ppermute | solution.py:427
  23.5 8.9 %collective-permute-start.6 = (f32[14,64,128]{2,1,0:T(8,128)S(1)}, f32[14,64,128]{2,1,0:T(8,128)S(1)}, u32[]{:S(2)}, u32[]{:S(2)}) collective-permute-start(f32[14,64,128]{2,1,0:T(8,128)S(1)} %collective-permute-done.refs_0_), channel_id=1, source_target_pairs={{0,1},{1,0},{2,3},{3,2},{4,5},{5,4},{6,7},{7,6},{8,9},{9,8},{10,11... | collective-permute-start | bytes 1376264 | tf_op jit(solution)/shard_map/ppermute | solution.py:436
  25.5 1.2 %copy-start = (f32[28,64,128]{2,1,0:T(8,128)S(1)}, f32[28,64,128]{2,1,0:T(8,128)}, u32[]{:S(2)}) copy-start(f32[28,64,128]{2,1,0:T(8,128)} %get-tuple-element.50.refs_0_) | copy-start | bytes 2752516
  27.9 14.4 %collective-permute-start.7 = (f32[2,2,48,128]{3,2,1,0:T(8,128)S(1)}, f32[2,2,48,128]{3,2,1,0:T(8,128)S(1)}, u32[]{:S(2)}, u32[]{:S(2)}) collective-permute-start(f32[2,2,48,128]{3,2,1,0:T(8,128)S(1)} %get-tuple-element.73), channel_id=1, source_target_pairs={{0,4},{4,0},{8,12},{12,8},{1,5},{5,1},{9,13},{13,9},{2,6},{6,2},{1... | collective-permute-start | bytes 294920 | tf_op jit(solution)/shard_map/ppermute | solution.py:427
  29.4 14.8 %collective-permute-start.8 = (f32[2,2,48,128]{3,2,1,0:T(8,128)S(1)}, f32[2,2,48,128]{3,2,1,0:T(8,128)S(1)}, u32[]{:S(2)}, u32[]{:S(2)}) collective-permute-start(f32[2,2,48,128]{3,2,1,0:T(8,128)S(1)} %get-tuple-element.74), channel_id=1, source_target_pairs={{0,8},{4,12},{8,0},{12,4},{1,9},{5,13},{9,1},{13,5},{2,10},{6,14},... | collective-permute-start | bytes 294920 | tf_op jit(solution)/shard_map/ppermute | solution.py:427
  30.5 13.7 %collective-permute-start.9 = (f32[2,2,48,128]{3,2,1,0:T(8,128)S(1)}, f32[2,2,48,128]{3,2,1,0:T(8,128)S(1)}, u32[]{:S(2)}, u32[]{:S(2)}) collective-permute-start(f32[2,2,48,128]{3,2,1,0:T(8,128)S(1)} %get-tuple-element.75), channel_id=1, source_target_pairs={{0,12},{4,8},{8,4},{12,0},{1,13},{5,9},{9,5},{13,1},{2,14},{6,10},... | collective-permute-start | bytes 294920 | tf_op jit(solution)/shard_map/ppermute | solution.py:427
  39.8 12.1 %collective-permute-start.10 = (f32[2,2,32,128]{3,2,1,0:T(8,128)S(1)}, f32[2,2,32,128]{3,2,1,0:T(8,128)S(1)}, u32[]{:S(2)}, u32[]{:S(2)}) collective-permute-start(f32[2,2,32,128]{3,2,1,0:T(8,128)S(1)} %get-tuple-element.104), channel_id=1, source_target_pairs={{0,4},{4,0},{8,12},{12,8},{1,5},{5,1},{9,13},{13,9},{2,6},{6,2},{1... | collective-permute-start | bytes 196616 | tf_op jit(solution)/shard_map/ppermute | solution.py:427
  40.4 11.4 %collective-permute-start.11 = (f32[2,2,32,128]{3,2,1,0:T(8,128)S(1)}, f32[2,2,32,128]{3,2,1,0:T(8,128)S(1)}, u32[]{:S(2)}, u32[]{:S(2)}) collective-permute-start(f32[2,2,32,128]{3,2,1,0:T(8,128)S(1)} %get-tuple-element.103), channel_id=1, source_target_pairs={{0,8},{4,12},{8,0},{12,4},{1,9},{5,13},{9,1},{13,5},{2,10},{6,14},... | collective-permute-start | bytes 196616 | tf_op jit(solution)/shard_map/ppermute | solution.py:427
  42.4 9.5 %collective-permute-start.12 = (f32[2,2,32,128]{3,2,1,0:T(8,128)S(1)}, f32[2,2,32,128]{3,2,1,0:T(8,128)S(1)}, u32[]{:S(2)}, u32[]{:S(2)}) collective-permute-start(f32[2,2,32,128]{3,2,1,0:T(8,128)S(1)} %get-tuple-element.102), channel_id=1, source_target_pairs={{0,12},{4,8},{8,4},{12,0},{1,13},{5,9},{9,5},{13,1},{2,14},{6,10},... | collective-permute-start | bytes 196616 | tf_op jit(solution)/shard_map/ppermute | solution.py:427
  51.9 1.9 %collective-permute-start.13 = (f32[896,128]{1,0:T(8,128)S(1)}, f32[896,128]{1,0:T(8,128)S(1)}, u32[]{:S(2)}, u32[]{:S(2)}) collective-permute-start(f32[896,128]{1,0:T(8,128)S(1)} %bitcast.43), channel_id=1, source_target_pairs={{0,1},{1,0},{2,3},{3,2},{4,5},{5,4},{6,7},{7,6},{8,9},{9,8},{10,11... | collective-permute-start | bytes 1376264 | tf_op jit(solution)/shard_map/ppermute | solution.py:436
  53.9 8.3 %collective-permute-start.14 = (f32[448,128]{1,0:T(8,128)S(1)}, f32[448,128]{1,0:T(8,128)S(1)}, u32[]{:S(2)}, u32[]{:S(2)}) collective-permute-start(f32[448,128]{1,0:T(8,128)S(1)} %slice.57), channel_id=1, source_target_pairs={{0,2},{1,3},{2,0},{3,1},{4,6},{5,7},{6,4},{7,5},{8,10},{9,11},{10,... | collective-permute-start | bytes 688136 | tf_op jit(solution)/shard_map/ppermute | solution.py:436
  62.3 6.6 %collective-permute-start.17 = (f32[112,128]{1,0:T(8,128)S(1)}, f32[112,128]{1,0:T(8,128)S(1)}, u32[]{:S(2)}, u32[]{:S(2)}) collective-permute-start(f32[112,128]{1,0:T(8,128)S(1)} %get-tuple-element.107), channel_id=1, source_target_pairs={{0,12},{4,8},{8,4},{12,0},{1,13},{5,9},{9,5},{13,1},{2,14},{6,10},... | collective-permute-start | bytes 172040 | tf_op jit(solution)/shard_map/ppermute | solution.py:427
  63.7 6.2 %collective-permute-start.16 = (f32[112,128]{1,0:T(8,128)S(1)}, f32[112,128]{1,0:T(8,128)S(1)}, u32[]{:S(2)}, u32[]{:S(2)}) collective-permute-start(f32[112,128]{1,0:T(8,128)S(1)} %get-tuple-element.108), channel_id=1, source_target_pairs={{0,8},{4,12},{8,0},{12,4},{1,9},{5,13},{9,1},{13,5},{2,10},{6,14},... | collective-permute-start | bytes 172040 | tf_op jit(solution)/shard_map/ppermute | solution.py:427
  63.7 6.2 %collective-permute-start.15 = (f32[112,128]{1,0:T(8,128)S(1)}, f32[112,128]{1,0:T(8,128)S(1)}, u32[]{:S(2)}, u32[]{:S(2)}) collective-permute-start(f32[112,128]{1,0:T(8,128)S(1)} %get-tuple-element.106), channel_id=1, source_target_pairs={{0,4},{4,0},{8,12},{12,8},{1,5},{5,1},{9,13},{13,9},{2,6},{6,2},{1... | collective-permute-start | bytes 172040 | tf_op jit(solution)/shard_map/ppermute | solution.py:427
  69.9 4.5 %collective-permute-start.18 = (f32[112,128]{1,0:T(8,128)S(1)}, f32[112,128]{1,0:T(8,128)S(1)}, u32[]{:S(2)}, u32[]{:S(2)}) collective-permute-start(f32[112,128]{1,0:T(8,128)S(1)} %fusion.1.refs_0_), channel_id=1, source_target_pairs={{0,4},{4,0},{8,12},{12,8},{1,5},{5,1},{9,13},{13,9},{2,6},{6,2},{1... | collective-permute-start | bytes 172040 | tf_op jit(solution)/shard_map/ppermute | solution.py:427
  71.0 6.3 %collective-permute-start.19 = (f32[112,128]{1,0:T(8,128)S(1)}, f32[112,128]{1,0:T(8,128)S(1)}, u32[]{:S(2)}, u32[]{:S(2)}) collective-permute-start(f32[112,128]{1,0:T(8,128)S(1)} %fusion.1.refs_0_), channel_id=1, source_target_pairs={{0,8},{4,12},{8,0},{12,4},{1,9},{5,13},{9,1},{13,5},{2,10},{6,14},... | collective-permute-start | bytes 172040 | tf_op jit(solution)/shard_map/ppermute | solution.py:427
  72.1 6.1 %collective-permute-start.20 = (f32[112,128]{1,0:T(8,128)S(1)}, f32[112,128]{1,0:T(8,128)S(1)}, u32[]{:S(2)}, u32[]{:S(2)}) collective-permute-start(f32[112,128]{1,0:T(8,128)S(1)} %fusion.1.refs_0_), channel_id=1, source_target_pairs={{0,12},{4,8},{8,4},{12,0},{1,13},{5,9},{9,5},{13,1},{2,14},{6,10},... | collective-permute-start | bytes 172040 | tf_op jit(solution)/shard_map/ppermute | solution.py:427
  78.2 10.5 %collective-permute-start.21 = (f32[448,128]{1,0:T(8,128)S(1)}, f32[448,128]{1,0:T(8,128)S(1)}, u32[]{:S(2)}, u32[]{:S(2)}) collective-permute-start(f32[448,128]{1,0:T(8,128)S(1)} %pad_maximum_fusion), channel_id=1, source_target_pairs={{0,2},{1,3},{2,0},{3,1},{4,6},{5,7},{6,4},{7,5},{8,10},{9,11},{10,... | collective-permute-start | bytes 688136 | tf_op jit(solution)/shard_map/ppermute | solution.py:436
  79.9 5.7 %collective-permute-start.22 = (f32[2,2,32,128]{3,2,1,0:T(8,128)S(1)}, f32[2,2,32,128]{3,2,1,0:T(8,128)S(1)}, u32[]{:S(2)}, u32[]{:S(2)}) collective-permute-start(f32[2,2,32,128]{3,2,1,0:T(8,128)S(1)} %get-tuple-element.100), channel_id=1, source_target_pairs={{0,4},{4,0},{8,12},{12,8},{1,5},{5,1},{9,13},{13,9},{2,6},{6,2},{1... | collective-permute-start | bytes 196616 | tf_op jit(solution)/shard_map/ppermute | solution.py:427
  80.0 5.7 %collective-permute-start.23 = (f32[2,2,32,128]{3,2,1,0:T(8,128)S(1)}, f32[2,2,32,128]{3,2,1,0:T(8,128)S(1)}, u32[]{:S(2)}, u32[]{:S(2)}) collective-permute-start(f32[2,2,32,128]{3,2,1,0:T(8,128)S(1)} %get-tuple-element.99), channel_id=1, source_target_pairs={{0,8},{4,12},{8,0},{12,4},{1,9},{5,13},{9,1},{13,5},{2,10},{6,14},... | collective-permute-start | bytes 196616 | tf_op jit(solution)/shard_map/ppermute | solution.py:427
  82.7 6.1 %collective-permute-start.24 = (f32[2,2,32,128]{3,2,1,0:T(8,128)S(1)}, f32[2,2,32,128]{3,2,1,0:T(8,128)S(1)}, u32[]{:S(2)}, u32[]{:S(2)}) collective-permute-start(f32[2,2,32,128]{3,2,1,0:T(8,128)S(1)} %get-tuple-element.98), channel_id=1, source_target_pairs={{0,12},{4,8},{8,4},{12,0},{1,13},{5,9},{9,5},{13,1},{2,14},{6,10},... | collective-permute-start | bytes 196616 | tf_op jit(solution)/shard_map/ppermute | solution.py:427
  88.8 2.9 %collective-permute-start.25 = (f32[896,128]{1,0:T(8,128)S(1)}, f32[896,128]{1,0:T(8,128)S(1)}, u32[]{:S(2)}, u32[]{:S(2)}) collective-permute-start(f32[896,128]{1,0:T(8,128)S(1)} %constant_dynamic-update-slice_fusion), channel_id=1, source_target_pairs={{0,1},{1,0},{2,3},{3,2},{4,5},{5,4},{6,7},{7,6},{8,9},{9,8},{10,11... | collective-permute-start | bytes 1376264 | tf_op jit(solution)/shard_map/ppermute | solution.py:436

commit v5 on v4

--- a/solution.py
+++ b/solution.py
@@ -14,26 +14,27 @@
 BLOCKS = 28
 BF16 = jnp.bfloat16
 F32 = jnp.float32
-SMEM = pl.BlockSpec(memory_space=pltpu.SMEM)
 VMEM = pl.BlockSpec(memory_space=pltpu.VMEM)
 
 
-def call(kernel, name, outs, args, scratch=(), flops=0, specs=None):
+def call(kernel, name, outs, args, scratch=(), flops=0):
     arrays = [jax.ShapeDtypeStruct(shape, kind) for shape, kind in outs]
-    sized = [item for item in [*arrays, *args[1:], *scratch] if hasattr(item.dtype, "itemsize")]
-    size = sum(math.prod(item.shape) * item.dtype.itemsize for item in sized)
+    size = sum(math.prod(item.shape) * item.dtype.itemsize for item in [*arrays, *args, *scratch])
     return pl.pallas_call(
         kernel,
         out_shape=arrays,
-        in_specs=[SMEM] + (specs or [VMEM] * (len(args) - 1)),
+        in_specs=[VMEM] * len(args),
         out_specs=[VMEM] * len(arrays),
         scratch_shapes=list(scratch),
-        compiler_params=pltpu.CompilerParams(
-            vmem_limit_bytes=56 * 1024 * 1024 if specs else size + 6 * 1024 * 1024
-        ),
-        cost_estimate=pl.CostEstimate(flops=flops, bytes_accessed=size, transcendentals=0),
+        compiler_params=pltpu.CompilerParams(vmem_limit_bytes=size + 6 * 1024 * 1024),
+        cost_estimate=pl.CostEstimate(flops=flops, bytes_accessed=1024, transcendentals=0),
         name=name,
     )(*args)
+
+
+def column_bits():
+    column = lax.axis_index("gz")
+    return 2 * (column % 2) + column // 2 % 2
 
 
 def split_terms(values):
@@ -41,53 +42,44 @@
     return high, (values - high.astype(F32)).astype(BF16)
 
 
-def start_kernel(dims, place, weights, biases, inflow, cotangent, own, sent, rows, pair, inner, *refs):
+def pack_kernel(weights, biases, own, sent):
+    chans = weights.shape[2]
+    half = sent.shape[0]
+    for tap in range(TAPS):
+        own[tap] = jnp.concatenate([weights[0, tap], weights[1, tap]], axis=1)
+    own[TAPS] = jnp.zeros((chans, LANES), F32)
+    own[TAPS, 0:1, :] = jnp.concatenate([biases[0:1, :], biases[1:2, :]], axis=1)
+    start = lax.axis_index("gz") % 2 * half
+
+    def copy(index, carry):
+        sent[index] = own[start + index]
+        return carry
+
+    lax.fori_loop(0, half, copy, 0)
+
+
+def turn_kernel(dims, inflow, cotangent, rows, pair, inner):
     micros, chans, size_x, local_y, local_z = dims
-    blocks, small, fields, sems = refs
-    copies = [
-        pltpu.make_async_copy(weights, blocks, sems.at[0]),
-        pltpu.make_async_copy(biases, small, sems.at[1]),
-        pltpu.make_async_copy(inflow, fields.at[0], sems.at[2]),
-        pltpu.make_async_copy(cotangent, fields.at[1], sems.at[3]),
-    ]
-    for copy in copies:
-        copy.start()
     step = size_x * local_y
-    odd = place[4] % 2 == 1
-    for field in range(2):
-        copies[2 + field].wait()
+    odd = lax.axis_index("gz") % 2 == 1
+    for field, source in enumerate((inflow, cotangent)):
         for micro in range(micros):
             for y in range(local_y):
                 first = micro * chans * step + y
                 parts = [
-                    fields[field, pl.ds(first + x * local_y, chans, stride=step), :]
-                    for x in range(size_x)
+                    source[pl.ds(first + x * local_y, chans, stride=step), :] for x in range(size_x)
                 ]
-                turned_rows = jnp.concatenate(parts, axis=0).T
-                rows[field, micro, y] = turned_rows
-                low, high = turned_rows[:HALO], turned_rows[local_z - HALO :]
+                turned = jnp.concatenate(parts, axis=0).T
+                rows[field, micro, y] = turned
+                low, high = turned[:HALO], turned[local_z - HALO :]
                 pair[field, micro, y] = jnp.where(odd, low, high)
                 inner[field, micro, y] = jnp.where(odd, high, low)
-    copies[0].wait()
-    copies[1].wait()
-    half = sent.shape[0]
-    for tap in range(TAPS):
-        own[tap] = jnp.concatenate([blocks[0, tap], blocks[1, tap]], axis=1)
-    own[TAPS] = jnp.zeros((chans, LANES), F32)
-    own[TAPS, 0:1, :] = jnp.concatenate([small[0:1, :], small[1:2, :]], axis=1)
-    start = place[2] // 2 * half
-
-    def copy(index, carry):
-        sent[index] = own[start + index]
-        return carry
-
-    lax.fori_loop(0, half, copy, 0)
-
-
-def window_kernel(dims, place, rows, pair, inner, *refs):
+
+
+def window_kernel(dims, rows, pair, inner, *refs):
     slabs, width, span, columns = dims
     outs, wide = refs[:-1], refs[-1]
-    slab, column = place[1], place[4]
+    slab, column = lax.axis_index("gy"), lax.axis_index("gz")
     odd = column % 2 == 1
     _, micros, local_y, local_z, _ = rows.shape
     for field in range(2):
@@ -106,9 +98,9 @@
                     outs[field * slabs + turn][micro, y] = wide[micro, y, pl.ds(start, span)]
 
 
-def table_kernel(place, *refs):
+def table_kernel(*refs):
     parts, (fwd, bwd, row) = refs[:-3], refs[-3:]
-    swap = place[2]
+    odd = lax.axis_index("gz") % 2
     count = parts[0].shape[0]
     chans = parts[0].shape[1]
 
@@ -116,7 +108,7 @@
         if len(parts) == 1:
             return parts[0][tap]
         index = tap % count
-        return jnp.where(swap // 2 == tap // count, parts[0][index], parts[1][index])
+        return jnp.where(odd == tap // count, parts[0][index], parts[1][index])
 
     for b in range(3):
         for c in range(3):
@@ -172,9 +164,10 @@
 
 
 class Slab:
-    def __init__(self, dims, place):
+    def __init__(self, dims):
         self.micros, self.rows_y, self.depth, self.width, self.chunk_y, self.slabs, limit_z = dims
-        self.section, self.slab, self.swap, origin = place[0], place[1], place[2], place[3]
+        self.section, self.slab = lax.axis_index("section"), lax.axis_index("gy")
+        origin = (lax.axis_index("gz") * self.slabs + self.slab) * self.width - HALO
         self.chunk = self.chunk_y * self.depth
         self.chunks = self.rows_y // self.chunk_y
         self.per_owner = self.rows_y // self.slabs
@@ -266,8 +259,8 @@
                     field[0, micro, pl.ds(start, self.depth), :] = value
 
 
-def forward_kernel(dims, place, own, own_row, other, other_row, *refs):
-    slab = Slab(dims, place)
+def forward_kernel(dims, own, own_row, other, other_row, *refs):
+    slab = Slab(dims)
     refs, (acts, kept, front, field) = refs[:-4], refs[-4:]
     slab.blank_edges(acts)
     slab.fill(field, refs)
@@ -281,10 +274,9 @@
 
             def body(part, start):
                 pre = slab.conv(acts, layer, start, table.at[half]) + row[half][0:1, :]
-                grown = 1.0 + jnp.exp(-pre)
-                sigma = 1.0 / grown
+                sigma = 1.0 / (1.0 + jnp.exp(-pre))
                 slab.write(kept, layer, start, sigma * (1.0 + pre * (1.0 - sigma)))
-                out = slab.masked(pre / grown, slab.in_grid)
+                out = slab.masked(pre * sigma, slab.in_grid)
                 pl.when(layer < 3)(lambda: slab.put_rows(acts, layer + 1, start, out))
                 pl.when(layer == 2 * slab.section + 1)(lambda: slab.emit(front, part, out))
 
@@ -296,8 +288,8 @@
     lax.fori_loop(0, 4, layer_step, 0)
 
 
-def backward_kernel(dims, scale, place, own, other, acts, kept, *refs):
-    slab = Slab(dims, place)
+def backward_kernel(dims, scale, own, other, acts, kept, *refs):
+    slab = Slab(dims)
     refs, (back, sums, rim, slopes, field, acc) = refs[:-6], refs[-6:]
     slab.blank_edges(rim)
     slab.fill(field, refs)
@@ -327,9 +319,10 @@
 
     quarter = BLOCKS // 4
     chans = LANES // 2
+    swap = column_bits()
 
     def spot(tap):
-        return (tap // quarter ^ slab.swap) * quarter + tap % quarter
+        return (tap // quarter ^ swap) * quarter + tap % quarter
 
     sums[spot(TAPS)] = jnp.zeros((chans, LANES), F32)
     for slot in range(2):
@@ -370,8 +363,8 @@
         sums[spot(TAPS), 0:1, lanes] = row[:, :chans] + row[:, chans:]
 
 
-def unpack_kernel(chunk, place, *refs):
-    slab, swap = place[1], place[2]
+def unpack_kernel(chunk, *refs):
+    slab, swap = lax.axis_index("gy"), column_bits()
     near, (beside, across, weight, bias, whole) = refs[:-5], refs[-5:]
     slabs = len(near)
     quarter = slabs * chunk
@@ -398,10 +391,10 @@
                 bias[layer : layer + 1, :] = whole[at : at + 1, lanes]
 
 
-def restore_kernel(dims, place, *refs):
+def restore_kernel(dims, *refs):
     micros, chans, size_x, local_y, width = dims
     pieces, (target, whole) = refs[:-2], refs[-2:]
-    slab = place[1]
+    slab = lax.axis_index("gy")
     slabs = len(pieces)
     step = size_x * local_y
     for micro in range(micros):
@@ -436,30 +429,19 @@
     return lax.ppermute(block, "gz", [(i, i ^ bit) for i in range(count)])
 
 
-def summed_over_grid(block):
-    slabs = lax.axis_size("gy")
-    slab = lax.axis_index("gy")
-    for bit in (1, 2):
-        rows = block.shape[0] // 2
-        block = block[:rows] + swapped(block[rows:], bit)
-    chunk = -(-block.shape[0] // (8 * slabs)) * 8
-    block = jnp.pad(block, ((0, slabs * chunk - block.shape[0]), (0, 0)))
-    parts = block.reshape(slabs, chunk, LANES)
-    sent = [
-        lax.dynamic_index_in_dim(parts, slab ^ turn, 0, keepdims=False)
-        for turn in range(slabs)
-    ]
-    return sum(spread(sent))
-
-
-def restored(pieces, shape, place):
+def halved(block, bit):
+    rows = block.shape[0] // 2
+    return block[:rows] + swapped(block[rows:], bit)
+
+
+def restored(pieces, shape):
     micros, chans, size_x, local_y, local_z = shape
     width = pieces[0].shape[2]
     dims = (micros, chans, size_x, local_y, width)
     rows = micros * chans * size_x * local_y
     kernel = functools.partial(restore_kernel, dims)
     scratch = [pltpu.VMEM((local_z, LANES), F32)]
-    (whole,) = call(kernel, "restore", [((rows, local_z), F32)], [place, *pieces], scratch)
+    (whole,) = call(kernel, "restore", [((rows, local_z), F32)], [*pieces], scratch)
     return whole.reshape(1, *shape)
 
 
@@ -472,44 +454,27 @@
     depth = -(-span // 16) * 16
     chunk_y = max(n for n in range(1, rows_y + 1) if rows_y % n == 0 and n * depth <= 384)
     scale = 1.0 / math.sqrt(micros * size_x * rows_y * local_z * columns)
-    slab, column = lax.axis_index("gy"), lax.axis_index("gz")
-    swap = 2 * (column % 2) + column // 2 % 2
-    origin = column * local_z + slab * width - HALO
-    place = [lax.axis_index("section"), slab, swap, origin, column]
-    place = jnp.stack(place).astype(jnp.int32)
-
     half = BLOCKS // 2
     rows = micros * chans * size_x * local_y
     ends = ((2, micros, local_y, HALO, LANES), F32)
-    got = call(
-        functools.partial(start_kernel, inflow.shape),
-        "start",
-        [
-            ((BLOCKS, chans, LANES), F32),
-            ((half, chans, LANES), F32),
-            ((2, micros, local_y, local_z, LANES), F32),
-            ends,
-            ends,
-        ],
-        [place, weights, biases, inflow.reshape(rows, local_z), cotangent.reshape(rows, local_z)],
-        [
-            pltpu.VMEM(weights.shape, F32),
-            pltpu.VMEM(biases.shape, F32),
-            pltpu.VMEM((2, rows, local_z), F32),
-            pltpu.SemaphoreType.DMA((4,)),
-        ],
-        specs=[pl.BlockSpec(memory_space=pl.ANY)] * 4,
-    )
-    own, sent, fields, pair, inner = got
-    first = lax.ppermute(sent, "section", [(0, 1), (1, 0)])
+    fields, pair, inner = call(
+        functools.partial(turn_kernel, inflow.shape),
+        "turn",
+        [((2, micros, local_y, local_z, LANES), F32), ends, ends],
+        [inflow.reshape(rows, local_z), cotangent.reshape(rows, local_z)],
+    )
     pair = swapped(pair, 1)
     route = [(i, i + 1) for i in range(1, columns - 1, 2)]
     inner = lax.ppermute(inner, "gz", route + [(after, before) for before, after in route])
+    packs = [((BLOCKS, chans, LANES), F32), ((half, chans, LANES), F32)]
+    weights, fields = lax.optimization_barrier((weights, fields))
+    own, sent = call(pack_kernel, "pack", packs, [weights, biases])
+    first = lax.ppermute(sent, "section", [(0, 1), (1, 0)])
     windows = call(
         functools.partial(window_kernel, (slabs, width, span, columns)),
         "windows",
         [((micros, local_y, span, LANES), F32)] * (2 * slabs),
-        [place, fields, pair, inner],
+        [fields, pair, inner],
         [pltpu.VMEM((micros, local_y, local_z + 2 * HALO, LANES), F32)],
     )
     flows, pulls = spread(windows[:slabs]), spread(windows[slabs:])
@@ -517,8 +482,8 @@
     second = swapped(first, 1)
 
     tables = [((2, 9 * LANES, 3 * LANES), BF16)] * 2 + [((2, 8, LANES), F32)]
-    own_fwd, own_bwd, own_row = call(table_kernel, "own_table", tables, [place, own])
-    far_fwd, far_bwd, far_row = call(table_kernel, "far_table", tables, [place, first, second])
+    own_fwd, own_bwd, own_row = call(table_kernel, "own_table", tables, [own])
+    far_fwd, far_bwd, far_row = call(table_kernel, "far_table", tables, [first, second])
 
     dims = (micros, rows_y, depth, width, chunk_y, slabs, local_z * columns)
     padded = (rows_y + 2) * depth
@@ -529,16 +494,14 @@
         functools.partial(forward_kernel, dims),
         "forward",
         [((4, micros, padded, 2 * LANES), BF16), ((4, micros, full, LANES), F32), piece],
-        [place, own_fwd, own_row, far_fwd, far_row, *flows],
+        [own_fwd, own_row, far_fwd, far_row, *flows],
         [pltpu.VMEM((1, micros, full, LANES), F32)],
-        4 * work,
-    )
-    outward = spread([front[turn] for turn in range(slabs)])
+    )
     back, sums = call(
         functools.partial(backward_kernel, dims, scale),
         "backward",
         [piece, ((BLOCKS, chans, LANES), F32)],
-        [place, own_bwd, far_bwd, acts, kept, *pulls],
+        [own_bwd, far_bwd, acts, kept, *pulls],
         [
             pltpu.VMEM((2, micros, padded, 2 * LANES), BF16),
             pltpu.VMEM((4, micros, full, LANES), F32),
@@ -548,25 +511,33 @@
         6 * work,
     )
 
-    sums, outward = lax.optimization_barrier((sums, outward))
-    mine = summed_over_grid(sums.reshape(BLOCKS * chans, LANES))
-    near = spread([mine] * slabs)
+    block = halved(sums.reshape(BLOCKS * chans, LANES), 1)
+    block, front = lax.optimization_barrier((block, front))
+    outward = spread([front[turn] for turn in range(slabs)])
+    block = halved(block, 2)
+    block, outward = lax.optimization_barrier((block, outward))
+    chunk = -(-block.shape[0] // (8 * slabs)) * 8
+    block = jnp.pad(block, ((0, slabs * chunk - block.shape[0]), (0, 0)))
+    parts = block.reshape(slabs, chunk, LANES)
+    slab = lax.axis_index("gy")
+    sent = [
+        lax.dynamic_index_in_dim(parts, slab ^ turn, 0, keepdims=False) for turn in range(slabs)
+    ]
+    near = spread([sum(spread(sent))] * slabs)
     near, back = lax.optimization_barrier((near, back))
     quarter = jnp.concatenate(near, axis=0)
     beside = swapped(quarter, 2)
     inward = spread([back[turn] for turn in range(slabs)])
-    beside, inward = lax.optimization_barrier((beside, inward))
     across = swapped(jnp.concatenate([quarter, beside], axis=0), 1)
-    section_out = restored(outward, inflow.shape, place)
-    section_grad = restored(inward, inflow.shape, place)
-    chunk = mine.shape[0]
+    section_out = restored(outward, inflow.shape)
     weight_total, bias_total = call(
         functools.partial(unpack_kernel, chunk),
         "unpack",
         [((2, TAPS, chans, chans), F32), ((2, chans), F32)],
-        [place, *near, beside, across],
+        [*near, beside, across],
         [pltpu.VMEM((4 * slabs * chunk, LANES), F32)],
     )
+    section_grad = restored(inward, inflow.shape)
     return (section_out, section_grad, weight_total, bias_total)
 
 

time: 94 us -> 90.5 us (0.963)
  Pallas kernels: 25.9 us -> 18.1 us
  waiting for transfers between devices: 27.2 us -> 32.2 us
  starting transfers between devices: 36.6 us -> 34.8 us
  local copies, waits for them, and re-layouts: 3.08 us -> 4.24 us
    pallas_call x9 -> x10, Pallas kernels: 25.9 us -> 18.1 us  [call(): pl.pallas_call(kernel, out_shape=arrays, in_specs=[VMEM] * len(args), out...]
    ppermute x18, waiting for transfers between devices: 18.7 us -> 22.9 us  [spread(): got.append(lax.ppermute(blocks[turn], 'gy', route))]
    unnamed x10 -> x12, local copies, waits for them, and re-layouts: 2.24 us -> 4.07 us
    ppermute x6, starting transfers between devices: 6.22 us -> 4.53 us  [swapped(): return lax.ppermute(block, 'gz', [(i, i ^ bit) for i in range(count)])]
  transfers between devices with their start and end apart: 26 -> 26, of which waited for: 12 -> 15; matrix products, arithmetic and copies ran while one was open for 0% -> 0% of each run, Pallas kernels for 21% -> 10%
where the time goes in v5:
time: 90.5 us; the launch traced here: 90.3 us
  starting transfers between devices  34.8 us (38%)
  waiting for transfers between devices  32.2 us (36%)
  Pallas kernels  18.1 us (20%)
  local copies, waits for them, and re-layouts  4.24 us (5%)
    ppermute x18, starting transfers between devices, spread(): got.append(lax.ppermute(blocks[turn], 'gy', route))  26.6 us
    ppermute x18, waiting for transfers between devices, spread(): got.append(lax.ppermute(blocks[turn], 'gy', route))  22.9 us
    pallas_call x10, Pallas kernels, call(): pl.pallas_call(kernel, out_shape=arrays, in_specs=[VMEM] * len(args), out...  18.1 us
    ppermute x6, waiting for transfers between devices, swapped(): return lax.ppermute(block, 'gz', [(i, i ^ bit) for i in range(count)])  9.33 us
    ppermute x6, starting transfers between devices, swapped(): return lax.ppermute(block, 'gz', [(i, i ^ bit) for i in range(count)])  4.53 us
    unnamed x12, local copies, waits for them, and re-layouts  4.07 us
    ppermute x1, starting transfers between devices, per_device(): first = lax.ppermute(sent, 'section', [(0, 1), (1, 0)])  3 us
  transfers between devices with their start and end apart: 26, of which 15 were waited for; matrix products, arithmetic and copies ran while one was open for 0% of the time, Pallas kernels for 10%

profile of v5, /device:TPU:0, one launch (start us, length us, event | category | flops | bytes accessed | tf_op | source)
XLA Modules:
  0.0 90.3 jit_solution(15925980502967418216)
XLA Ops:
  0.6 0.9 %copy-done.1 = f32[2,64,2,2,128]{4,3,2,1,0:T(2,128)S(1)} copy-done((f32[2,64,2,2,128]{4,3,2,1,0:T(2,128)S(1)}, f32[2,64,2,2,128]{4,3,2,1,0:T(2,128)}, u32[]{:S(2)}) %copy-start.1) | copy-done | bytes 262168
  1.6 0.9 %copy-done.2 = f32[2,64,2,2,128]{4,3,2,1,0:T(2,128)S(1)} copy-done((f32[2,64,2,2,128]{4,3,2,1,0:T(2,128)S(1)}, f32[2,64,2,2,128]{4,3,2,1,0:T(2,128)}, u32[]{:S(2)}) %copy-start.2) | copy-done | bytes 262168
  2.5 0.2 turn.1
  2.7 0.0 copy-start
  2.7 1.5 %copy-done = f32[2,27,64,64]{3,2,1,0:T(8,128)S(1)} copy-done((f32[2,27,64,64]{3,2,1,0:T(8,128)S(1)}, f32[2,27,64,64]{3,2,1,0:T(8,128)}, u32[]{:S(2)}) %copy-start) | copy-done | bytes 884760
  4.2 0.7 copy-done.3
  4.9 0.4 pack.1
  5.3 3.0 %collective-permute-start = (f32[14,64,128]{2,1,0:T(8,128)S(1)}, f32[14,64,128]{2,1,0:T(8,128)S(1)}, u32[]{:S(2)}, u32[]{:S(2)}) collective-permute-start(f32[14,64,128]{2,1,0:T(8,128)S(1)} %get-tuple-element.53), channel_id=1, source_target_pairs={{0,16},{16,0},{1,17},{17,1},{2,18},{18,2},{3,19},{19,3},{4,20},{20... | collective-permute-start | bytes 1376264 | tf_op jit(solution)/shard_map/ppermute | solution.py:472
  8.3 0.7 collective-permute-start.2
  8.9 0.5 collective-permute-done.1.pair
  9.5 0.1 windows.1
  9.6 1.6 %collective-permute-start.3 = (f32[2,2,48,128]{3,2,1,0:T(8,128)S(1)}, f32[2,2,48,128]{3,2,1,0:T(8,128)S(1)}, u32[]{:S(2)}, u32[]{:S(2)}) collective-permute-start(f32[2,2,48,128]{3,2,1,0:T(8,128)S(1)} %get-tuple-element.58), channel_id=1, source_target_pairs={{0,4},{4,0},{8,12},{12,8},{1,5},{5,1},{9,13},{13,9},{2,6},{6,2},{1... | collective-permute-start | bytes 294920 | tf_op jit(solution)/shard_map/ppermute | solution.py:420
  11.3 2.6 %collective-permute-start.4 = (f32[2,2,48,128]{3,2,1,0:T(8,128)S(1)}, f32[2,2,48,128]{3,2,1,0:T(8,128)S(1)}, u32[]{:S(2)}, u32[]{:S(2)}) collective-permute-start(f32[2,2,48,128]{3,2,1,0:T(8,128)S(1)} %get-tuple-element.59), channel_id=1, source_target_pairs={{0,8},{4,12},{8,0},{12,4},{1,9},{5,13},{9,1},{13,5},{2,10},{6,14},... | collective-permute-start | bytes 294920 | tf_op jit(solution)/shard_map/ppermute | solution.py:420
  13.9 0.2 collective-permute-start.5
  14.1 0.2 collective-permute-done.3.refs_1_
  14.3 3.6 %collective-permute-done.4.refs_2_ = f32[2,2,48,128]{3,2,1,0:T(8,128)S(1)} collective-permute-done((f32[2,2,48,128]{3,2,1,0:T(8,128)S(1)}, f32[2,2,48,128]{3,2,1,0:T(8,128)S(1)}, u32[]{:S(2)}, u32[]{:S(2)}) %collective-permute-start.4) | collective-permute-done | bytes 98336 | tf_op jit(solution)/shard_map/ppermute | solution.py:420
  17.9 3.5 %collective-permute-done.5.refs_3_ = f32[2,2,48,128]{3,2,1,0:T(8,128)S(1)} collective-permute-done((f32[2,2,48,128]{3,2,1,0:T(8,128)S(1)}, f32[2,2,48,128]{3,2,1,0:T(8,128)S(1)}, u32[]{:S(2)}, u32[]{:S(2)}) %collective-permute-start.5) | collective-permute-done | bytes 98336 | tf_op jit(solution)/shard_map/ppermute | solution.py:420
  21.4 0.0 collective-permute-done.refs_0_
  21.4 2.0 %collective-permute-start.6 = (f32[14,64,128]{2,1,0:T(8,128)S(1)}, f32[14,64,128]{2,1,0:T(8,128)S(1)}, u32[]{:S(2)}, u32[]{:S(2)}) collective-permute-start(f32[14,64,128]{2,1,0:T(8,128)S(1)} %collective-permute-done.refs_0_), channel_id=1, source_target_pairs={{0,1},{1,0},{2,3},{3,2},{4,5},{5,4},{6,7},{7,6},{8,9},{9,8},{10,11... | collective-permute-start | bytes 1376264 | tf_op jit(solution)/shard_map/ppermute | solution.py:429
  23.5 1.5 %collective-permute-start.7 = (f32[2,2,48,128]{3,2,1,0:T(8,128)S(1)}, f32[2,2,48,128]{3,2,1,0:T(8,128)S(1)}, u32[]{:S(2)}, u32[]{:S(2)}) collective-permute-start(f32[2,2,48,128]{3,2,1,0:T(8,128)S(1)} %get-tuple-element.74), channel_id=1, source_target_pairs={{0,4},{4,0},{8,12},{12,8},{1,5},{5,1},{9,13},{13,9},{2,6},{6,2},{1... | collective-permute-start | bytes 294920 | tf_op jit(solution)/shard_map/ppermute | solution.py:420
  24.9 1.1 %collective-permute-start.8 = (f32[2,2,48,128]{3,2,1,0:T(8,128)S(1)}, f32[2,2,48,128]{3,2,1,0:T(8,128)S(1)}, u32[]{:S(2)}, u32[]{:S(2)}) collective-permute-start(f32[2,2,48,128]{3,2,1,0:T(8,128)S(1)} %get-tuple-element.75), channel_id=1, source_target_pairs={{0,8},{4,12},{8,0},{12,4},{1,9},{5,13},{9,1},{13,5},{2,10},{6,14},... | collective-permute-start | bytes 294920 | tf_op jit(solution)/shard_map/ppermute | solution.py:420
  26.0 1.9 %collective-permute-start.9 = (f32[2,2,48,128]{3,2,1,0:T(8,128)S(1)}, f32[2,2,48,128]{3,2,1,0:T(8,128)S(1)}, u32[]{:S(2)}, u32[]{:S(2)}) collective-permute-start(f32[2,2,48,128]{3,2,1,0:T(8,128)S(1)} %get-tuple-element.76), channel_id=1, source_target_pairs={{0,12},{4,8},{8,4},{12,0},{1,13},{5,9},{9,5},{13,1},{2,14},{6,10},... | collective-permute-start | bytes 294920 | tf_op jit(solution)/shard_map/ppermute | solution.py:420
  27.8 0.7 own_table.1
  28.5 0.0 collective-permute-done.6.refs_1_
  28.5 0.7 far_table.1
  29.3 5.5 %forward.1 = (bf16[4,2,480,256]{3,2,1,0:T(8,128)(2,1)S(1)}, f32[4,2,384,128]{3,2,1,0:T(8,128)S(1)}, f32[4,2,2,32,128]{4,3,2,1,0:T(8,128)S(1)}) custom-call(bf16[2,1152,384]{2,1,0:T(8,128)(2,1)S(1)} %get-tuple-element.63.own, f32[2,8,128]{2,1,0:T(8,128)S(1)} %get-tuple-element.64.own_row, bf16[2,1152,384]{2,1,0:T(8,128)(2,1)S(1)} %get-tuple-element.65.other, ...), custom_call_target="tpu_custom_call" | custom-call | bytes 1024 | tf_op jit(solution)/shard_map/forward/pallas_call | solution.py:23
  34.8 0.0 collective-permute-done.7.refs_1_
  34.8 0.6 collective-permute-done.8.refs_2_
  35.4 0.0 collective-permute-done.9.refs_3_
  35.4 7.1 %backward.1 = (f32[4,2,2,32,128]{4,3,2,1,0:T(8,128)S(1)}, f32[28,64,128]{2,1,0:T(8,128)S(1)}) custom-call(bf16[2,1152,384]{2,1,0:T(8,128)(2,1)S(1)} %get-tuple-element.52.own, bf16[2,1152,384]{2,1,0:T(8,128)(2,1)S(1)} %get-tuple-element.62.other, bf16[4,2,480,256]{3,2,1,0:T(8,128)(2,1)S(1)} %get-tuple-element.71.acts, ...), custom_call_target="tpu_custom_call" | custom-call | flops 4076863488 | bytes 1024 | tf_op jit(solution)/shard_map/backward/pallas_call | solution.py:23
  42.5 0.1 fusion.2
  42.6 0.1 collective-permute-start.10
  42.7 1.8 %collective-permute-done.10 = f32[896,128]{1,0:T(8,128)S(1)} collective-permute-done((f32[896,128]{1,0:T(8,128)S(1)}, f32[896,128]{1,0:T(8,128)S(1)}, u32[]{:S(2)}, u32[]{:S(2)}) %collective-permute-start.10) | collective-permute-done | bytes 458784 | tf_op jit(solution)/shard_map/ppermute | solution.py:429
  44.6 1.9 %collective-permute-start.11 = (f32[448,128]{1,0:T(8,128)S(1)}, f32[448,128]{1,0:T(8,128)S(1)}, u32[]{:S(2)}, u32[]{:S(2)}) collective-permute-start(f32[448,128]{1,0:T(8,128)S(1)} %slice.47), channel_id=1, source_target_pairs={{0,2},{1,3},{2,0},{3,1},{4,6},{5,7},{6,4},{7,5},{8,10},{9,11},{10,... | collective-permute-start | bytes 688136 | tf_op jit(solution)/shard_map/ppermute | solution.py:429
  46.5 1.7 %collective-permute-start.12 = (f32[2,2,32,128]{3,2,1,0:T(8,128)S(1)}, f32[2,2,32,128]{3,2,1,0:T(8,128)S(1)}, u32[]{:S(2)}, u32[]{:S(2)}) collective-permute-start(f32[2,2,32,128]{3,2,1,0:T(8,128)S(1)} %get-tuple-element.102), channel_id=1, source_target_pairs={{0,4},{4,0},{8,12},{12,8},{1,5},{5,1},{9,13},{13,9},{2,6},{6,2},{1... | collective-permute-start | bytes 196616 | tf_op jit(solution)/shard_map/ppermute | solution.py:420
  48.2 1.0 %collective-permute-start.13 = (f32[2,2,32,128]{3,2,1,0:T(8,128)S(1)}, f32[2,2,32,128]{3,2,1,0:T(8,128)S(1)}, u32[]{:S(2)}, u32[]{:S(2)}) collective-permute-start(f32[2,2,32,128]{3,2,1,0:T(8,128)S(1)} %get-tuple-element.101), channel_id=1, source_target_pairs={{0,8},{4,12},{8,0},{12,4},{1,9},{5,13},{9,1},{13,5},{2,10},{6,14},... | collective-permute-start | bytes 196616 | tf_op jit(solution)/shard_map/ppermute | solution.py:420
  49.2 1.8 %collective-permute-start.14 = (f32[2,2,32,128]{3,2,1,0:T(8,128)S(1)}, f32[2,2,32,128]{3,2,1,0:T(8,128)S(1)}, u32[]{:S(2)}, u32[]{:S(2)}) collective-permute-start(f32[2,2,32,128]{3,2,1,0:T(8,128)S(1)} %get-tuple-element.100), channel_id=1, source_target_pairs={{0,12},{4,8},{8,4},{12,0},{1,13},{5,9},{9,5},{13,1},{2,14},{6,10},... | collective-permute-start | bytes 196616 | tf_op jit(solution)/shard_map/ppermute | solution.py:420
  51.0 1.4 %collective-permute-done.11 = f32[448,128]{1,0:T(8,128)S(1)} collective-permute-done((f32[448,128]{1,0:T(8,128)S(1)}, f32[448,128]{1,0:T(8,128)S(1)}, u32[]{:S(2)}, u32[]{:S(2)}) %collective-permute-start.11) | collective-permute-done | bytes 229408 | tf_op jit(solution)/shard_map/ppermute | solution.py:429
  52.4 0.0 collective-permute-done.12.refs_1_
  52.4 3.8 %collective-permute-done.13.refs_2_ = f32[2,2,32,128]{3,2,1,0:T(8,128)S(1)} collective-permute-done((f32[2,2,32,128]{3,2,1,0:T(8,128)S(1)}, f32[2,2,32,128]{3,2,1,0:T(8,128)S(1)}, u32[]{:S(2)}, u32[]{:S(2)}) %collective-permute-start.13) | collective-permute-done | bytes 65568 | tf_op jit(solution)/shard_map/ppermute | solution.py:420
  56.2 2.3 %collective-permute-start.17 = (f32[112,128]{1,0:T(8,128)S(1)}, f32[112,128]{1,0:T(8,128)S(1)}, u32[]{:S(2)}, u32[]{:S(2)}) collective-permute-start(f32[112,128]{1,0:T(8,128)S(1)} %get-tuple-element.105), channel_id=1, source_target_pairs={{0,12},{4,8},{8,4},{12,0},{1,13},{5,9},{9,5},{13,1},{2,14},{6,10},... | collective-permute-start | bytes 172040 | tf_op jit(solution)/shard_map/ppermute | solution.py:420
  58.5 0.5 collective-permute-start.16
  59.0 1.7 %collective-permute-start.15 = (f32[112,128]{1,0:T(8,128)S(1)}, f32[112,128]{1,0:T(8,128)S(1)}, u32[]{:S(2)}, u32[]{:S(2)}) collective-permute-start(f32[112,128]{1,0:T(8,128)S(1)} %get-tuple-element.104), channel_id=1, source_target_pairs={{0,4},{4,0},{8,12},{12,8},{1,5},{5,1},{9,13},{13,9},{2,6},{6,2},{1... | collective-permute-start | bytes 172040 | tf_op jit(solution)/shard_map/ppermute | solution.py:420
  60.7 1.7 %collective-permute-done.17 = f32[112,128]{1,0:T(8,128)S(1)} collective-permute-done((f32[112,128]{1,0:T(8,128)S(1)}, f32[112,128]{1,0:T(8,128)S(1)}, u32[]{:S(2)}, u32[]{:S(2)}) %collective-permute-start.17) | collective-permute-done | bytes 57376 | tf_op jit(solution)/shard_map/ppermute | solution.py:420
  62.4 1.6 %collective-permute-done.16 = f32[112,128]{1,0:T(8,128)S(1)} collective-permute-done((f32[112,128]{1,0:T(8,128)S(1)}, f32[112,128]{1,0:T(8,128)S(1)}, u32[]{:S(2)}, u32[]{:S(2)}) %collective-permute-start.16) | collective-permute-done | bytes 57376 | tf_op jit(solution)/shard_map/ppermute | solution.py:420
  64.0 0.0 collective-permute-done.15
  64.0 1.3 %collective-permute-start.18 = (f32[112,128]{1,0:T(8,128)S(1)}, f32[112,128]{1,0:T(8,128)S(1)}, u32[]{:S(2)}, u32[]{:S(2)}) collective-permute-start(f32[112,128]{1,0:T(8,128)S(1)} %fusion.1.refs_0_), channel_id=1, source_target_pairs={{0,4},{4,0},{8,12},{12,8},{1,5},{5,1},{9,13},{13,9},{2,6},{6,2},{1... | collective-permute-start | bytes 172040 | tf_op jit(solution)/shard_map/ppermute | solution.py:420
  65.4 1.5 %collective-permute-start.19 = (f32[112,128]{1,0:T(8,128)S(1)}, f32[112,128]{1,0:T(8,128)S(1)}, u32[]{:S(2)}, u32[]{:S(2)}) collective-permute-start(f32[112,128]{1,0:T(8,128)S(1)} %fusion.1.refs_0_), channel_id=1, source_target_pairs={{0,8},{4,12},{8,0},{12,4},{1,9},{5,13},{9,1},{13,5},{2,10},{6,14},... | collective-permute-start | bytes 172040 | tf_op jit(solution)/shard_map/ppermute | solution.py:420
  66.9 1.6 %collective-permute-start.20 = (f32[112,128]{1,0:T(8,128)S(1)}, f32[112,128]{1,0:T(8,128)S(1)}, u32[]{:S(2)}, u32[]{:S(2)}) collective-permute-start(f32[112,128]{1,0:T(8,128)S(1)} %fusion.1.refs_0_), channel_id=1, source_target_pairs={{0,12},{4,8},{8,4},{12,0},{1,13},{5,9},{9,5},{13,1},{2,14},{6,10},... | collective-permute-start | bytes 172040 | tf_op jit(solution)/shard_map/ppermute | solution.py:420
  68.5 0.0 collective-permute-done.18.refs_1_
  68.5 2.5 %collective-permute-done.19.refs_2_ = f32[112,128]{1,0:T(8,128)S(1)} collective-permute-done((f32[112,128]{1,0:T(8,128)S(1)}, f32[112,128]{1,0:T(8,128)S(1)}, u32[]{:S(2)}, u32[]{:S(2)}) %collective-permute-start.19) | collective-permute-done | bytes 57376 | tf_op jit(solution)/shard_map/ppermute | solution.py:420
  71.0 1.8 %collective-permute-done.20.refs_3_ = f32[112,128]{1,0:T(8,128)S(1)} collective-permute-done((f32[112,128]{1,0:T(8,128)S(1)}, f32[112,128]{1,0:T(8,128)S(1)}, u32[]{:S(2)}, u32[]{:S(2)}) %collective-permute-start.20) | collective-permute-done | bytes 57376 | tf_op jit(solution)/shard_map/ppermute | solution.py:420
  72.9 0.5 collective-permute-start.24
  73.4 5.6 %collective-permute-done.24.refs_4_ = f32[448,128]{1,0:T(8,128)S(1)} collective-permute-done((f32[448,128]{1,0:T(8,128)S(1)}, f32[448,128]{1,0:T(8,128)S(1)}, u32[]{:S(2)}, u32[]{:S(2)}) %collective-permute-start.24) | collective-permute-done | bytes 229408 | tf_op jit(solution)/shard_map/ppermute | solution.py:429
  79.0 0.1 collective-permute-start.25
  79.1 0.1 collective-permute-start.21
  79.1 2.2 %collective-permute-start.22 = (f32[2,2,32,128]{3,2,1,0:T(8,128)S(1)}, f32[2,2,32,128]{3,2,1,0:T(8,128)S(1)}, u32[]{:S(2)}, u32[]{:S(2)}) collective-permute-start(f32[2,2,32,128]{3,2,1,0:T(8,128)S(1)} %get-tuple-element.97), channel_id=1, source_target_pairs={{0,8},{4,12},{8,0},{12,4},{1,9},{5,13},{9,1},{13,5},{2,10},{6,14},... | collective-permute-start | bytes 196616 | tf_op jit(solution)/shard_map/ppermute | solution.py:420
  81.3 2.2 %collective-permute-start.23 = (f32[2,2,32,128]{3,2,1,0:T(8,128)S(1)}, f32[2,2,32,128]{3,2,1,0:T(8,128)S(1)}, u32[]{:S(2)}, u32[]{:S(2)}) collective-permute-start(f32[2,2,32,128]{3,2,1,0:T(8,128)S(1)} %get-tuple-element.96), channel_id=1, source_target_pairs={{0,12},{4,8},{8,4},{12,0},{1,13},{5,9},{9,5},{13,1},{2,14},{6,10},... | collective-permute-start | bytes 196616 | tf_op jit(solution)/shard_map/ppermute | solution.py:420
  83.5 0.9 restore.2
  84.4 0.3 collective-permute-done.21.refs_1_
  84.7 3.2 %collective-permute-done.22.refs_2_ = f32[2,2,32,128]{3,2,1,0:T(8,128)S(1)} collective-permute-done((f32[2,2,32,128]{3,2,1,0:T(8,128)S(1)}, f32[2,2,32,128]{3,2,1,0:T(8,128)S(1)}, u32[]{:S(2)}, u32[]{:S(2)}) %collective-permute-start.22) | collective-permute-done | bytes 65568 | tf_op jit(solution)/shard_map/ppermute | solution.py:420
  87.9 0.9 restore.3
  88.7 0.0 collective-permute-done.25.refs_5_
  88.7 1.6 %unpack.1 = (f32[2,27,64,64]{3,2,1,0:T(8,128)}, f32[2,64]{1,0:T(2,128)}) custom-call(f32[112,128]{1,0:T(8,128)S(1)} %fusion.1.refs_0_, f32[112,128]{1,0:T(8,128)S(1)} %collective-permute-done.18.refs_1_, f32[112,128]{1,0:T(8,128)S(1)} %collective-permute-done.19.refs_2_, f32[112,128]{1,0:T(8,128)S(1)} %collective-permute-done.20.refs_3_, ...), custom_call_target="tpu_custom_call" | custom-call | bytes 1024 | tf_op jit(solution)/shard_map/unpack/pallas_call | solution.py:23
  (20 shorter events, 0.2 us)
Async XLA Ops:
  0.6 1.0 %copy-start.1 = (f32[2,64,2,2,128]{4,3,2,1,0:T(2,128)S(1)}, f32[2,64,2,2,128]{4,3,2,1,0:T(2,128)}, u32[]{:S(2)}) copy-start(f32[2,64,2,2,128]{4,3,2,1,0:T(2,128)} %param.4) | copy-start | bytes 786436
  1.6 0.9 %copy-start.2 = (f32[2,64,2,2,128]{4,3,2,1,0:T(2,128)S(1)}, f32[2,64,2,2,128]{4,3,2,1,0:T(2,128)}, u32[]{:S(2)}) copy-start(f32[2,64,2,2,128]{4,3,2,1,0:T(2,128)} %param.7) | copy-start | bytes 786436
  2.7 1.5 %copy-start = (f32[2,27,64,64]{3,2,1,0:T(8,128)S(1)}, f32[2,27,64,64]{3,2,1,0:T(8,128)}, u32[]{:S(2)}) copy-start(f32[2,27,64,64]{3,2,1,0:T(8,128)} %weights) | copy-start | bytes 2654212
  4.2 0.7 copy-start.3
  5.3 16.2 %collective-permute-start = (f32[14,64,128]{2,1,0:T(8,128)S(1)}, f32[14,64,128]{2,1,0:T(8,128)S(1)}, u32[]{:S(2)}, u32[]{:S(2)}) collective-permute-start(f32[14,64,128]{2,1,0:T(8,128)S(1)} %get-tuple-element.53), channel_id=1, source_target_pairs={{0,16},{16,0},{1,17},{17,1},{2,18},{18,2},{3,19},{19,3},{4,20},{20... | collective-permute-start | bytes 1376264 | tf_op jit(solution)/shard_map/ppermute | solution.py:472
  8.3 1.2 %collective-permute-start.1 = (f32[2,2,2,8,128]{4,3,2,1,0:T(8,128)S(1)}, f32[2,2,2,8,128]{4,3,2,1,0:T(8,128)S(1)}, u32[]{:S(2)}, u32[]{:S(2)}) collective-permute-start(f32[2,2,2,8,128]{4,3,2,1,0:T(8,128)S(1)} %get-tuple-element.55), channel_id=1, source_target_pairs={{0,1},{1,0},{2,3},{3,2},{4,5},{5,4},{6,7},{7,6},{8,9},{9,8},{10,11... | collective-permute-start | bytes 98312 | tf_op jit(solution)/shard_map/ppermute | solution.py:429
  8.3 1.2 %collective-permute-start.2 = (f32[2,2,2,8,128]{4,3,2,1,0:T(8,128)S(1)}, f32[2,2,2,8,128]{4,3,2,1,0:T(8,128)S(1)}, u32[]{:S(2)}, u32[]{:S(2)}) collective-permute-start(f32[2,2,2,8,128]{4,3,2,1,0:T(8,128)S(1)} %get-tuple-element.56), channel_id=1, source_target_pairs={{1,2},{2,1},{5,6},{6,5},{9,10},{10,9},{13,14},{14,13},{17,18},{18,... | collective-permute-start | bytes 98312 | tf_op jit(solution)/shard_map/ppermute | solution.py:468
  9.6 4.7 %collective-permute-start.3 = (f32[2,2,48,128]{3,2,1,0:T(8,128)S(1)}, f32[2,2,48,128]{3,2,1,0:T(8,128)S(1)}, u32[]{:S(2)}, u32[]{:S(2)}) collective-permute-start(f32[2,2,48,128]{3,2,1,0:T(8,128)S(1)} %get-tuple-element.58), channel_id=1, source_target_pairs={{0,4},{4,0},{8,12},{12,8},{1,5},{5,1},{9,13},{13,9},{2,6},{6,2},{1... | collective-permute-start | bytes 294920 | tf_op jit(solution)/shard_map/ppermute | solution.py:420
  11.3 6.7 %collective-permute-start.4 = (f32[2,2,48,128]{3,2,1,0:T(8,128)S(1)}, f32[2,2,48,128]{3,2,1,0:T(8,128)S(1)}, u32[]{:S(2)}, u32[]{:S(2)}) collective-permute-start(f32[2,2,48,128]{3,2,1,0:T(8,128)S(1)} %get-tuple-element.59), channel_id=1, source_target_pairs={{0,8},{4,12},{8,0},{12,4},{1,9},{5,13},{9,1},{13,5},{2,10},{6,14},... | collective-permute-start | bytes 294920 | tf_op jit(solution)/shard_map/ppermute | solution.py:420
  13.9 7.6 %collective-permute-start.5 = (f32[2,2,48,128]{3,2,1,0:T(8,128)S(1)}, f32[2,2,48,128]{3,2,1,0:T(8,128)S(1)}, u32[]{:S(2)}, u32[]{:S(2)}) collective-permute-start(f32[2,2,48,128]{3,2,1,0:T(8,128)S(1)} %get-tuple-element.60), channel_id=1, source_target_pairs={{0,12},{4,8},{8,4},{12,0},{1,13},{5,9},{9,5},{13,1},{2,14},{6,10},... | collective-permute-start | bytes 294920 | tf_op jit(solution)/shard_map/ppermute | solution.py:420
  21.4 7.1 %collective-permute-start.6 = (f32[14,64,128]{2,1,0:T(8,128)S(1)}, f32[14,64,128]{2,1,0:T(8,128)S(1)}, u32[]{:S(2)}, u32[]{:S(2)}) collective-permute-start(f32[14,64,128]{2,1,0:T(8,128)S(1)} %collective-permute-done.refs_0_), channel_id=1, source_target_pairs={{0,1},{1,0},{2,3},{3,2},{4,5},{5,4},{6,7},{7,6},{8,9},{9,8},{10,11... | collective-permute-start | bytes 1376264 | tf_op jit(solution)/shard_map/ppermute | solution.py:429
  23.5 11.4 %collective-permute-start.7 = (f32[2,2,48,128]{3,2,1,0:T(8,128)S(1)}, f32[2,2,48,128]{3,2,1,0:T(8,128)S(1)}, u32[]{:S(2)}, u32[]{:S(2)}) collective-permute-start(f32[2,2,48,128]{3,2,1,0:T(8,128)S(1)} %get-tuple-element.74), channel_id=1, source_target_pairs={{0,4},{4,0},{8,12},{12,8},{1,5},{5,1},{9,13},{13,9},{2,6},{6,2},{1... | collective-permute-start | bytes 294920 | tf_op jit(solution)/shard_map/ppermute | solution.py:420
  24.9 10.5 %collective-permute-start.8 = (f32[2,2,48,128]{3,2,1,0:T(8,128)S(1)}, f32[2,2,48,128]{3,2,1,0:T(8,128)S(1)}, u32[]{:S(2)}, u32[]{:S(2)}) collective-permute-start(f32[2,2,48,128]{3,2,1,0:T(8,128)S(1)} %get-tuple-element.75), channel_id=1, source_target_pairs={{0,8},{4,12},{8,0},{12,4},{1,9},{5,13},{9,1},{13,5},{2,10},{6,14},... | collective-permute-start | bytes 294920 | tf_op jit(solution)/shard_map/ppermute | solution.py:420
  26.0 9.4 %collective-permute-start.9 = (f32[2,2,48,128]{3,2,1,0:T(8,128)S(1)}, f32[2,2,48,128]{3,2,1,0:T(8,128)S(1)}, u32[]{:S(2)}, u32[]{:S(2)}) collective-permute-start(f32[2,2,48,128]{3,2,1,0:T(8,128)S(1)} %get-tuple-element.76), channel_id=1, source_target_pairs={{0,12},{4,8},{8,4},{12,0},{1,13},{5,9},{9,5},{13,1},{2,14},{6,10},... | collective-permute-start | bytes 294920 | tf_op jit(solution)/shard_map/ppermute | solution.py:420
  42.6 1.9 %collective-permute-start.10 = (f32[896,128]{1,0:T(8,128)S(1)}, f32[896,128]{1,0:T(8,128)S(1)}, u32[]{:S(2)}, u32[]{:S(2)}) collective-permute-start(f32[896,128]{1,0:T(8,128)S(1)} %bitcast.40), channel_id=1, source_target_pairs={{0,1},{1,0},{2,3},{3,2},{4,5},{5,4},{6,7},{7,6},{8,9},{9,8},{10,11... | collective-permute-start | bytes 1376264 | tf_op jit(solution)/shard_map/ppermute | solution.py:429
  44.6 7.8 %collective-permute-start.11 = (f32[448,128]{1,0:T(8,128)S(1)}, f32[448,128]{1,0:T(8,128)S(1)}, u32[]{:S(2)}, u32[]{:S(2)}) collective-permute-start(f32[448,128]{1,0:T(8,128)S(1)} %slice.47), channel_id=1, source_target_pairs={{0,2},{1,3},{2,0},{3,1},{4,6},{5,7},{6,4},{7,5},{8,10},{9,11},{10,... | collective-permute-start | bytes 688136 | tf_op jit(solution)/shard_map/ppermute | solution.py:429
  46.5 5.9 %collective-permute-start.12 = (f32[2,2,32,128]{3,2,1,0:T(8,128)S(1)}, f32[2,2,32,128]{3,2,1,0:T(8,128)S(1)}, u32[]{:S(2)}, u32[]{:S(2)}) collective-permute-start(f32[2,2,32,128]{3,2,1,0:T(8,128)S(1)} %get-tuple-element.102), channel_id=1, source_target_pairs={{0,4},{4,0},{8,12},{12,8},{1,5},{5,1},{9,13},{13,9},{2,6},{6,2},{1... | collective-permute-start | bytes 196616 | tf_op jit(solution)/shard_map/ppermute | solution.py:420
  48.2 8.0 %collective-permute-start.13 = (f32[2,2,32,128]{3,2,1,0:T(8,128)S(1)}, f32[2,2,32,128]{3,2,1,0:T(8,128)S(1)}, u32[]{:S(2)}, u32[]{:S(2)}) collective-permute-start(f32[2,2,32,128]{3,2,1,0:T(8,128)S(1)} %get-tuple-element.101), channel_id=1, source_target_pairs={{0,8},{4,12},{8,0},{12,4},{1,9},{5,13},{9,1},{13,5},{2,10},{6,14},... | collective-permute-start | bytes 196616 | tf_op jit(solution)/shard_map/ppermute | solution.py:420
  49.2 7.0 %collective-permute-start.14 = (f32[2,2,32,128]{3,2,1,0:T(8,128)S(1)}, f32[2,2,32,128]{3,2,1,0:T(8,128)S(1)}, u32[]{:S(2)}, u32[]{:S(2)}) collective-permute-start(f32[2,2,32,128]{3,2,1,0:T(8,128)S(1)} %get-tuple-element.100), channel_id=1, source_target_pairs={{0,12},{4,8},{8,4},{12,0},{1,13},{5,9},{9,5},{13,1},{2,14},{6,10},... | collective-permute-start | bytes 196616 | tf_op jit(solution)/shard_map/ppermute | solution.py:420
  56.2 6.2 %collective-permute-start.17 = (f32[112,128]{1,0:T(8,128)S(1)}, f32[112,128]{1,0:T(8,128)S(1)}, u32[]{:S(2)}, u32[]{:S(2)}) collective-permute-start(f32[112,128]{1,0:T(8,128)S(1)} %get-tuple-element.105), channel_id=1, source_target_pairs={{0,12},{4,8},{8,4},{12,0},{1,13},{5,9},{9,5},{13,1},{2,14},{6,10},... | collective-permute-start | bytes 172040 | tf_op jit(solution)/shard_map/ppermute | solution.py:420
  58.5 5.5 %collective-permute-start.16 = (f32[112,128]{1,0:T(8,128)S(1)}, f32[112,128]{1,0:T(8,128)S(1)}, u32[]{:S(2)}, u32[]{:S(2)}) collective-permute-start(f32[112,128]{1,0:T(8,128)S(1)} %get-tuple-element.106), channel_id=1, source_target_pairs={{0,8},{4,12},{8,0},{12,4},{1,9},{5,13},{9,1},{13,5},{2,10},{6,14},... | collective-permute-start | bytes 172040 | tf_op jit(solution)/shard_map/ppermute | solution.py:420
  59.0 5.0 %collective-permute-start.15 = (f32[112,128]{1,0:T(8,128)S(1)}, f32[112,128]{1,0:T(8,128)S(1)}, u32[]{:S(2)}, u32[]{:S(2)}) collective-permute-start(f32[112,128]{1,0:T(8,128)S(1)} %get-tuple-element.104), channel_id=1, source_target_pairs={{0,4},{4,0},{8,12},{12,8},{1,5},{5,1},{9,13},{13,9},{2,6},{6,2},{1... | collective-permute-start | bytes 172040 | tf_op jit(solution)/shard_map/ppermute | solution.py:420
  64.0 4.5 %collective-permute-start.18 = (f32[112,128]{1,0:T(8,128)S(1)}, f32[112,128]{1,0:T(8,128)S(1)}, u32[]{:S(2)}, u32[]{:S(2)}) collective-permute-start(f32[112,128]{1,0:T(8,128)S(1)} %fusion.1.refs_0_), channel_id=1, source_target_pairs={{0,4},{4,0},{8,12},{12,8},{1,5},{5,1},{9,13},{13,9},{2,6},{6,2},{1... | collective-permute-start | bytes 172040 | tf_op jit(solution)/shard_map/ppermute | solution.py:420
  65.4 5.7 %collective-permute-start.19 = (f32[112,128]{1,0:T(8,128)S(1)}, f32[112,128]{1,0:T(8,128)S(1)}, u32[]{:S(2)}, u32[]{:S(2)}) collective-permute-start(f32[112,128]{1,0:T(8,128)S(1)} %fusion.1.refs_0_), channel_id=1, source_target_pairs={{0,8},{4,12},{8,0},{12,4},{1,9},{5,13},{9,1},{13,5},{2,10},{6,14},... | collective-permute-start | bytes 172040 | tf_op jit(solution)/shard_map/ppermute | solution.py:420
  66.9 6.0 %collective-permute-start.20 = (f32[112,128]{1,0:T(8,128)S(1)}, f32[112,128]{1,0:T(8,128)S(1)}, u32[]{:S(2)}, u32[]{:S(2)}) collective-permute-start(f32[112,128]{1,0:T(8,128)S(1)} %fusion.1.refs_0_), channel_id=1, source_target_pairs={{0,12},{4,8},{8,4},{12,0},{1,13},{5,9},{9,5},{13,1},{2,14},{6,10},... | collective-permute-start | bytes 172040 | tf_op jit(solution)/shard_map/ppermute | solution.py:420
  72.9 6.1 %collective-permute-start.24 = (f32[448,128]{1,0:T(8,128)S(1)}, f32[448,128]{1,0:T(8,128)S(1)}, u32[]{:S(2)}, u32[]{:S(2)}) collective-permute-start(f32[448,128]{1,0:T(8,128)S(1)} %pad_maximum_fusion), channel_id=1, source_target_pairs={{0,2},{1,3},{2,0},{3,1},{4,6},{5,7},{6,4},{7,5},{8,10},{9,11},{10,... | collective-permute-start | bytes 688136 | tf_op jit(solution)/shard_map/ppermute | solution.py:429
  79.0 9.8 %collective-permute-start.25 = (f32[896,128]{1,0:T(8,128)S(1)}, f32[896,128]{1,0:T(8,128)S(1)}, u32[]{:S(2)}, u32[]{:S(2)}) collective-permute-start(f32[896,128]{1,0:T(8,128)S(1)} %constant_dynamic-update-slice_fusion), channel_id=1, source_target_pairs={{0,1},{1,0},{2,3},{3,2},{4,5},{5,4},{6,7},{7,6},{8,9},{9,8},{10,11... | collective-permute-start | bytes 1376264 | tf_op jit(solution)/shard_map/ppermute | solution.py:429
  79.1 5.6 %collective-permute-start.21 = (f32[2,2,32,128]{3,2,1,0:T(8,128)S(1)}, f32[2,2,32,128]{3,2,1,0:T(8,128)S(1)}, u32[]{:S(2)}, u32[]{:S(2)}) collective-permute-start(f32[2,2,32,128]{3,2,1,0:T(8,128)S(1)} %get-tuple-element.98), channel_id=1, source_target_pairs={{0,4},{4,0},{8,12},{12,8},{1,5},{5,1},{9,13},{13,9},{2,6},{6,2},{1... | collective-permute-start | bytes 196616 | tf_op jit(solution)/shard_map/ppermute | solution.py:420
  79.1 8.7 %collective-permute-start.22 = (f32[2,2,32,128]{3,2,1,0:T(8,128)S(1)}, f32[2,2,32,128]{3,2,1,0:T(8,128)S(1)}, u32[]{:S(2)}, u32[]{:S(2)}) collective-permute-start(f32[2,2,32,128]{3,2,1,0:T(8,128)S(1)} %get-tuple-element.97), channel_id=1, source_target_pairs={{0,8},{4,12},{8,0},{12,4},{1,9},{5,13},{9,1},{13,5},{2,10},{6,14},... | collective-permute-start | bytes 196616 | tf_op jit(solution)/shard_map/ppermute | solution.py:420
  81.3 6.5 %collective-permute-start.23 = (f32[2,2,32,128]{3,2,1,0:T(8,128)S(1)}, f32[2,2,32,128]{3,2,1,0:T(8,128)S(1)}, u32[]{:S(2)}, u32[]{:S(2)}) collective-permute-start(f32[2,2,32,128]{3,2,1,0:T(8,128)S(1)} %get-tuple-element.96), channel_id=1, source_target_pairs={{0,12},{4,8},{8,4},{12,0},{1,13},{5,9},{9,5},{13,1},{2,14},{6,10},... | collective-permute-start | bytes 196616 | tf_op jit(solution)/shard_map/ppermute | solution.py:420

commit v6 on v5

v6 whole, which is shorter than its diff:
```python
import functools
import math

import jax
import jax.numpy as jnp
from jax import lax
from jax.experimental import pallas as pl
from jax.experimental.pallas import tpu as pltpu
from jax.sharding import PartitionSpec as P

HALO = 8
HALOS = (8, 4)
LANES = 128
TAPS = 27
BLOCKS = 28
BF16 = jnp.bfloat16
F32 = jnp.float32
VMEM = pl.BlockSpec(memory_space=pltpu.VMEM)


def call(kernel, name, outs, args, scratch=(), flops=0):
    arrays = [jax.ShapeDtypeStruct(shape, kind) for shape, kind in outs]
    size = sum(math.prod(item.shape) * item.dtype.itemsize for item in [*arrays, *args, *scratch])
    return pl.pallas_call(
        kernel,
        out_shape=arrays,
        in_specs=[VMEM] * len(args),
        out_specs=[VMEM] * len(arrays),
        scratch_shapes=list(scratch),
        compiler_params=pltpu.CompilerParams(vmem_limit_bytes=size + 6 * 1024 * 1024),
        cost_estimate=pl.CostEstimate(flops=flops, bytes_accessed=1024, transcendentals=0),
        name=name,
    )(*args)


def column_bits():
    column = lax.axis_index("gz")
    return 2 * (column % 2) + column // 2 % 2


def split_terms(values):
    high = values.astype(BF16)
    return high, (values - high.astype(F32)).astype(BF16)


def pack_kernel(weights, biases, own):
    chans = weights.shape[2]
    for tap in range(TAPS):
        own[tap] = jnp.concatenate([weights[0, tap], weights[1, tap]], axis=1)
    own[TAPS] = jnp.zeros((chans, LANES), F32)
    own[TAPS, 0:1, :] = jnp.concatenate([biases[0:1, :], biases[1:2, :]], axis=1)


def turn_kernel(dims, inflow, cotangent, rows, pair, inner):
    micros, chans, size_x, local_y, local_z = dims
    step = size_x * local_y
    odd = lax.axis_index("gz") % 2 == 1
    for field, source in enumerate((inflow, cotangent)):
        for micro in range(micros):
            for y in range(local_y):
                first = micro * chans * step + y
                parts = [
                    source[pl.ds(first + x * local_y, chans, stride=step), :] for x in range(size_x)
                ]
                turned = jnp.concatenate(parts, axis=0).T
                rows[field, micro, y] = turned
                low, high = turned[:HALO], turned[local_z - HALO :]
                pair[field, micro, y] = jnp.where(odd, low, high)
                inner[field, micro, y] = jnp.where(odd, high, low)


def window_kernel(dims, rows, pair, inner, *refs):
    slabs, width, columns = dims
    outs, wide = refs[:-1], refs[-1]
    slab, column = lax.axis_index("gy"), lax.axis_index("gz")
    odd = column % 2 == 1
    _, micros, local_y, local_z, _ = rows.shape
    for field, halo in enumerate(HALOS):
        at = slice(0, width + 2 * halo) if field == 0 else slice(width + 2 * HALO, None)
        for micro in range(micros):
            for y in range(local_y):
                one, two = pair[field, micro, y], inner[field, micro, y]
                before = jnp.where(column > 0, jnp.where(odd, one, two), 0.0)
                after = jnp.where(column < columns - 1, jnp.where(odd, two, one), 0.0)
                wide[field, micro, y, :HALO] = before
                wide[field, micro, y, HALO : HALO + local_z] = rows[field, micro, y]
                wide[field, micro, y, HALO + local_z :] = after
                for turn in range(slabs):
                    start = (slab ^ turn) * width + HALO - halo
                    if width % 8 == 0 and halo % 8 == 0:
                        start = pl.multiple_of(start, 8)
                    outs[turn][micro, y, at] = wide[field, micro, y, pl.ds(start, width + 2 * halo)]


def table_kernel(source, fwd, bwd, row):
    chans = source.shape[1]
    for b in range(3):
        for c in range(3):
            taps = [source[9 * a + 3 * b + c] for a in range(3)]
            for layer in range(2):
                lanes = slice(layer * chans, (layer + 1) * chans)
                below, level, above = [tap[:, lanes] for tap in taps]
                top = jnp.concatenate([level, above], axis=1)
                low = jnp.concatenate([below, level], axis=1)
                block = jnp.concatenate([top, low], axis=0)
                for target, value, r, at in ((fwd, block.T, b, c), (bwd, block, 2 - b, 2 - c)):
                    hi, lo = split_terms(value)
                    at = slice(at * LANES, (at + 1) * LANES)
                    target[layer, 2 * r * LANES : (2 * r + 1) * LANES, at] = hi
                    target[layer, (2 * r + 1) * LANES : (2 * r + 2) * LANES, at] = hi
                    target[layer, (6 + r) * LANES : (7 + r) * LANES, at] = lo
    last = source[TAPS, 0:1, :]
    for layer in range(2):
        part = last[:, layer * chans : (layer + 1) * chans]
        row[layer] = jnp.broadcast_to(jnp.concatenate([part, part], axis=1), (8, LANES))


def cut_kernel(dims, place, *refs):
    micros, chans, size_x, local_y, local_z, slabs, width, span, edged, fields = dims
    sources, refs = refs[:fields], refs[fields:]
    outs, wide = refs[:-1], refs[-1]
    slab = place[1]
    step = size_x * local_y
    for field, source in enumerate(sources):
        windows = outs[field * slabs : (field + 1) * slabs]
        edges = outs[fields * slabs :]
        for micro in range(micros):
            for y in range(local_y):
                first = micro * chans * step + y
                parts = [
                    source[pl.ds(first + x * local_y, chans, stride=step), :] for x in range(size_x)
                ]
                wide[field, micro, y, HALO : HALO + local_z] = jnp.concatenate(parts, axis=0).T
                wide[field, micro, y, :HALO] = jnp.zeros((HALO, LANES), F32)
                wide[field, micro, y, HALO + local_z :] = jnp.zeros((HALO, LANES), F32)
                if edged:
                    for turn in range(slabs):
                        start = lax.rem(slab + turn, slabs) * width
                        if width % 8 == 0:
                            start = pl.multiple_of(start, 8)
                        windows[turn][micro, y] = wide[field, micro, y, pl.ds(start, span)]
                    low = wide[field, micro, y, local_z : local_z + HALO]
                    high = wide[field, micro, y, HALO : 2 * HALO]
                    for m in range(slabs):
                        edges[m][field, micro, y] = jnp.where(slab == m, low, high)
                else:
                    windows[0][micro, y] = wide[field, micro, y, HALO : HALO + local_z]


class Slab:
    def __init__(self, dims):
        self.micros, self.rows_y, self.depth, self.width, self.chunk_y, self.slabs, limit_z = dims
        self.section, self.slab = lax.axis_index("section"), lax.axis_index("gy")
        origin = (lax.axis_index("gz") * self.slabs + self.slab) * self.width - HALO
        self.chunk = self.chunk_y * self.depth
        self.chunks = self.rows_y // self.chunk_y
        self.per_owner = self.rows_y // self.slabs
        zs = lax.broadcasted_iota(jnp.int32, (self.depth, LANES), 0)
        inside = (zs + origin >= 0) & (zs + origin < limit_z)
        self.in_grid = inside.astype(F32)[None]
        self.mine = ((zs >= HALO) & (zs < HALO + self.width)).astype(F32)[None]

    def over_chunks(self, body):
        if self.chunks == 1:
            body(0)
        else:

            def step(part, carry):
                body(pl.multiple_of(part * self.chunk, 16))
                return carry

            lax.fori_loop(0, self.chunks, step, 0)

    def masked(self, values, mask):
        return (values.reshape(-1, self.depth, LANES) * mask).reshape(values.shape)

    def put_rows(self, target, lead, micro, start, values):
        hi, lo = split_terms(values)
        at = pl.ds(start + self.depth, self.chunk)
        target[lead, micro, at, slice(0, LANES)] = hi
        target[lead, micro, at, slice(LANES, 2 * LANES)] = lo

    def pieces_of(self, source, lead, micro, start):
        return [
            source[lead, micro, pl.ds(start + b * self.depth, self.chunk), :] for b in range(3)
        ]

    def conv(self, source, lead, start, table):
        lefts = []
        for micro in range(self.micros):
            pieces = self.pieces_of(source, lead, micro, start)
            lefts.append(jnp.concatenate(pieces + [piece[:, :LANES] for piece in pieces], axis=1))
        results = []
        for left in lefts:
            out = jnp.dot(left, table[...], preferred_element_type=F32)
            before = pltpu.roll(out[:, :LANES], 1, 0)
            after = pltpu.roll(out[:, 2 * LANES :], out.shape[0] - 1, 0)
            results.append(before + out[:, LANES : 2 * LANES] + after)
        return results

    def by_owner(self, layer, own, other, body):
        mine = layer // 2 == self.section
        pl.when(mine)(lambda: body(own, layer % 2))
        pl.when(jnp.logical_not(mine))(lambda: body(other, layer % 2))

    def blank_edges(self, target):
        blank = jnp.zeros((self.depth, 2 * LANES), BF16)
        for lead in range(target.shape[0]):
            for micro in range(self.micros):
                for edge in (0, self.rows_y + 1):
                    target[lead, micro, edge * self.depth : (edge + 1) * self.depth, :] = blank

    def fill(self, field, windows, which):
        halo = HALOS[which]
        span = self.width + 2 * halo
        at = 0 if which == 0 else self.width + 2 * HALO
        extra = [HALO - halo, self.depth - span - (HALO - halo)]
        for micro in range(self.micros):
            for turn, window in enumerate(windows):
                owner = self.slab ^ turn
                for y in range(self.per_owner):
                    blanks = [jnp.zeros((rows, LANES), F32) for rows in extra]
                    parts = [blanks[0], window[micro, y, at : at + span], blanks[1]]
                    parts = [part for part in parts if part.shape[0]]
                    start = pl.multiple_of((owner * self.per_owner + y) * self.depth, 16)
                    value = jnp.concatenate(parts, axis=0) if len(parts) > 1 else parts[0]
                    field[micro, pl.ds(start, self.depth), :] = value

    def cut_out(self, targets, slot, source):
        for turn, target in enumerate(targets):
            owner = self.slab ^ turn
            for micro in range(self.micros):
                for y in range(self.per_owner):
                    start = (owner * self.per_owner + y) * self.depth + HALO
                    rows = pl.ds(pl.multiple_of(start, 8), self.width)
                    target[slot, micro, y] = source[micro, rows, :]


def forward_kernel(dims, own, own_row, other, other_row, *refs):
    slab = Slab(dims)
    windows, (acts, kept, front, field) = refs[:-4], refs[-4:]
    slab.blank_edges(acts)
    slab.fill(field, windows, 0)

    def take_in(start):
        for micro in range(slab.micros):
            slab.put_rows(acts, 0, micro, start, field[micro, pl.ds(start, slab.chunk), :])

    slab.over_chunks(take_in)

    def layer_step(layer, carry):
        def run(tables, half):
            table, row = tables

            def body(start):
                at = pl.ds(start, slab.chunk)
                sums = slab.conv(acts, layer, start, table.at[half])
                outs = []
                for micro, total in enumerate(sums):
                    pre = total + row[half][0:1, :]
                    sigma = 1.0 / (1.0 + jnp.exp(-pre))
                    kept[layer, micro, at, :] = sigma * (1.0 + pre * (1.0 - sigma))
                    out = slab.masked(pre * sigma, slab.in_grid)
                    slab.put_rows(acts, layer + 1, micro, start, out)
                    outs.append(out)

                @pl.when(layer == 2 * slab.section + 1)
                def _():
                    for micro, out in enumerate(outs):
                        front[micro, at, :] = out

            slab.over_chunks(body)

        slab.by_owner(layer, (own, own_row), (other, other_row), run)
        return carry

    lax.fori_loop(0, 4, layer_step, 0)


def backward_kernel(dims, scale, own, other, acts, kept, front, *refs):
    slab = Slab(dims)
    windows, refs = refs[: slab.slabs], refs[slab.slabs :]
    outs, (sums, rim, slopes, field, acc) = refs[: slab.slabs], refs[slab.slabs :]
    slab.blank_edges(rim)
    slab.cut_out(outs, 0, front)
    slab.fill(field, windows, 1)

    def take_gradient(layer, micro, start, gradient):
        at = pl.ds(start, slab.chunk)
        slope = slab.masked(gradient * kept[layer, micro, at, :], slab.in_grid)
        slopes[layer, micro, at, :] = slab.masked(slope, slab.mine)
        slab.put_rows(rim, layer % 2, micro, start, slope)

    def take_cotangent(start):
        for micro in range(slab.micros):
            take_gradient(3, micro, start, field[micro, pl.ds(start, slab.chunk), :])

    slab.over_chunks(take_cotangent)

    def layer_step(index, carry):
        layer = 3 - index

        def run(table, half):
            def body(start):
                gradients = slab.conv(rim, layer % 2, start, table.at[half])
                last = layer == 2 * slab.section

                @pl.when(last)
                def _():
                    for micro, gradient in enumerate(gradients):
                        field[micro, pl.ds(start, slab.chunk), :] = gradient

                @pl.when(jnp.logical_not(last))
                def _():
                    for micro, gradient in enumerate(gradients):
                        take_gradient(layer - 1, micro, start, gradient)

            slab.over_chunks(body)

        slab.by_owner(layer, own, other, run)
        return carry

    lax.fori_loop(0, jnp.where(slab.section == 0, 4, 2), layer_step, 0)
    slab.cut_out(outs, 1, field)

    quarter = BLOCKS // 4
    chans = LANES // 2
    swap = column_bits()

    def spot(tap):
        return (tap // quarter ^ swap) * quarter + tap % quarter

    def products(layer, start):
        at = pl.ds(start, slab.chunk)
        slope = jnp.concatenate([slopes[layer, micro, at, :] for micro in range(slab.micros)])
        moved = [pltpu.roll(slope, slope.shape[0] - 1, 0), slope, pltpu.roll(slope, 1, 0)]
        terms = [split_terms(value) for value in moved]
        left_hi = jnp.concatenate([hi for hi, lo in terms], axis=1)
        left_lo = jnp.concatenate([lo for hi, lo in terms], axis=1)
        pieces = [slab.pieces_of(acts, layer, micro, start) for micro in range(slab.micros)]
        pieces = [jnp.concatenate(parts, axis=0) for parts in zip(*pieces)]
        full = jnp.concatenate(pieces, axis=1)
        high = jnp.concatenate([piece[:, :LANES] for piece in pieces], axis=1)
        over_rows = (((0,), (0,)), ((), ()))
        one = lax.dot_general(left_hi, full, over_rows, preferred_element_type=F32)
        two = lax.dot_general(left_lo, high, over_rows, preferred_element_type=F32)
        total = []
        for b in range(3):
            hi = one[:, 2 * b * LANES : (2 * b + 1) * LANES]
            lo = one[:, (2 * b + 1) * LANES : (2 * b + 2) * LANES]
            total.append(hi + lo + two[:, b * LANES : (b + 1) * LANES])
        return total, jnp.sum(slope, axis=0, keepdims=True)

    sums[spot(TAPS)] = jnp.zeros((chans, LANES), F32)
    for slot in range(2):
        layer = 2 * slab.section + slot
        if slab.chunks == 1:
            total, row = products(layer, 0)
        else:
            acc[...] = jnp.zeros(acc.shape, F32)

            def gather(start):
                total, row = products(layer, start)
                for b in range(3):
                    acc[0 : 3 * LANES, b * LANES : (b + 1) * LANES] += total[b]
                acc[3 * LANES : 3 * LANES + 1, 0:LANES] += row

            slab.over_chunks(gather)
            total = [acc[0 : 3 * LANES, b * LANES : (b + 1) * LANES] for b in range(3)]
            row = acc[3 * LANES : 3 * LANES + 1, 0:LANES]
        lanes = slice(slot * chans, (slot + 1) * chans)
        for b in range(3):
            for c in range(3):
                block = total[b][c * LANES : (c + 1) * LANES] * scale
                tap = 3 * b + c
                sums[spot(tap), :, lanes] = block[chans:, :chans]
                sums[spot(9 + tap), :, lanes] = block[:chans, :chans] + block[chans:, chans:]
                sums[spot(18 + tap), :, lanes] = block[:chans, chans:]
        row = row * scale
        sums[spot(TAPS), 0:1, lanes] = row[:, :chans] + row[:, chans:]


def unpack_kernel(kept, theirs, beside, across, weight, bias, whole):
    half = kept.shape[0]
    chans = weight.shape[-1]
    odd, swap = lax.axis_index("gy") % 2, column_bits()
    parts = [(kept, 0), (theirs, 0), (beside, 0), (beside, half)]
    parts += [(across, half * i) for i in range(4)]
    for index, (source, first) in enumerate(parts):
        at = ((index // 2 ^ swap) * 2 + (index % 2 ^ odd)) * half
        whole[pl.ds(pl.multiple_of(at, 8), half), :] = source[first : first + half, :]
    for layer in range(2):
        lanes = slice(layer * chans, (layer + 1) * chans)
        for tap in range(TAPS):
            weight[layer, tap] = whole[tap * chans : (tap + 1) * chans, lanes]
        bias[layer : layer + 1, :] = whole[TAPS * chans : TAPS * chans + 1, lanes]


def restore_kernel(dims, *refs):
    micros, chans, size_x, local_y, width = dims
    pieces, (*targets, whole) = refs[:-3], refs[-3:]
    slab = lax.axis_index("gy")
    step = size_x * local_y
    for slot, target in enumerate(targets):
        for micro in range(micros):
            for y in range(local_y):
                for turn, piece in enumerate(pieces):
                    start = (slab ^ turn) * width
                    if width % 8 == 0:
                        start = pl.multiple_of(start, 8)
                    whole[slot, micro, y, pl.ds(start, width), :] = piece[slot, micro, y]
                block = whole[slot, micro, y].T
                for x in range(size_x):
                    first = micro * chans * step + x * local_y + y
                    part = block[x * chans : (x + 1) * chans]
                    target[pl.ds(first, chans, stride=step), :] = part


def spread(blocks):
    slabs = len(blocks)
    if slabs <= 8:
        got = [blocks[0]]
        for turn in range(1, slabs):
            route = [(i, i ^ turn) for i in range(slabs)]
            got.append(lax.ppermute(blocks[turn], "gy", route))
        return got
    order = jnp.arange(slabs) ^ lax.axis_index("gy")
    got = lax.all_to_all(jnp.stack(blocks)[order], "gy", 0, 0)[order]
    return [got[turn] for turn in range(slabs)]


def swapped(block, bit, axis="gz"):
    return lax.ppermute(block, axis, [(i, i ^ bit) for i in range(lax.axis_size(axis))])


def halved(block, bit):
    rows = block.shape[0] // 2
    return block[:rows] + swapped(block[rows:], bit)


def per_device(inflow, weights, biases, cotangent):
    micros, chans, size_x, local_y, local_z = inflow.shape
    slabs, columns = lax.axis_size("gy"), lax.axis_size("gz")
    rows_y = local_y * slabs
    width = local_z // slabs
    span = width + 2 * HALO
    depth = -(-span // 16) * 16
    chunk_y = max(n for n in range(1, rows_y + 1) if rows_y % n == 0 and n * depth <= 384)
    scale = 1.0 / math.sqrt(micros * size_x * rows_y * local_z * columns)
    rows = micros * chans * size_x * local_y
    ends = ((2, micros, local_y, HALO, LANES), F32)
    (own,) = call(pack_kernel, "pack", [((BLOCKS, chans, LANES), F32)], [weights, biases])
    fields, pair, inner = call(
        functools.partial(turn_kernel, inflow.shape),
        "turn",
        [((2, micros, local_y, local_z, LANES), F32), ends, ends],
        [inflow.reshape(rows, local_z), cotangent.reshape(rows, local_z)],
    )
    far = lax.ppermute(own, "section", [(0, 1), (1, 0)])
    pair = swapped(pair, 1)
    route = [(i, i + 1) for i in range(1, columns - 1, 2)]
    inner = lax.ppermute(inner, "gz", route + [(after, before) for before, after in route])
    reach = sum(width + 2 * halo for halo in HALOS)
    windows = call(
        functools.partial(window_kernel, (slabs, width, columns)),
        "windows",
        [((micros, local_y, reach, LANES), F32)] * slabs,
        [fields, pair, inner],
        [pltpu.VMEM((2, micros, local_y, local_z + 2 * HALO, LANES), F32)],
    )
    windows = spread(windows)
    far, windows = lax.optimization_barrier((far, windows))

    tables = [((2, 9 * LANES, 3 * LANES), BF16)] * 2 + [((2, 8, LANES), F32)]
    own_fwd, own_bwd, own_row = call(table_kernel, "own_table", tables, [own])
    far_fwd, far_bwd, far_row = call(table_kernel, "far_table", tables, [far])

    dims = (micros, rows_y, depth, width, chunk_y, slabs, local_z * columns)
    padded = (rows_y + 2) * depth
    full = rows_y * depth
    acts, kept, front = call(
        functools.partial(forward_kernel, dims),
        "forward",
        [
            ((5, micros, padded, 2 * LANES), BF16),
            ((4, micros, full, LANES), F32),
            ((micros, full, LANES), F32),
        ],
        [own_fwd, own_row, far_fwd, far_row, *windows],
        [pltpu.VMEM((micros, full, LANES), F32)],
    )
    *outs, sums = call(
        functools.partial(backward_kernel, dims, scale),
        "backward",
        [((2, micros, local_y, width, LANES), F32)] * slabs + [((BLOCKS, chans, LANES), F32)],
        [own_bwd, far_bwd, acts, kept, front, *windows],
        [
            pltpu.VMEM((2, micros, padded, 2 * LANES), BF16),
            pltpu.VMEM((4, micros, full, LANES), F32),
            pltpu.VMEM((micros, full, LANES), F32),
            pltpu.VMEM((3 * LANES + 8, 3 * LANES), F32),
        ],
    )

    block = halved(sums.reshape(BLOCKS * chans, LANES), 1)
    block, outs = lax.optimization_barrier((block, outs))
    outs = spread(outs)
    block = halved(block, 2)
    block, outs = lax.optimization_barrier((block, outs))
    half = block.shape[0] // 2
    odd = lax.axis_index("gy") % 2 == 1
    kept_half = jnp.where(odd, block[half:], block[:half])
    kept_half = kept_half + swapped(jnp.where(odd, block[:half], block[half:]), 1, "gy")
    bit = 2
    while bit < slabs:
        kept_half = kept_half + swapped(kept_half, bit, "gy")
        bit *= 2
    theirs = swapped(kept_half, 1, "gy")
    quarter = jnp.concatenate([kept_half, theirs], axis=0)
    beside = swapped(quarter, 2)
    across = swapped(jnp.concatenate([quarter, beside], axis=0), 1)
    section_out, section_grad = call(
        functools.partial(restore_kernel, (micros, chans, size_x, local_y, width)),
        "restore",
        [((rows, local_z), F32)] * 2,
        outs,
        [pltpu.VMEM((2, micros, local_y, local_z, LANES), F32)],
    )
    weight_total, bias_total = call(
        unpack_kernel,
        "unpack",
        [((2, TAPS, chans, chans), F32), ((2, chans), F32)],
        [kept_half, theirs, beside, across],
        [pltpu.VMEM((BLOCKS * chans, LANES), F32)],
    )
    shape = (1, *inflow.shape)
    return (section_out.reshape(shape), section_grad.reshape(shape), weight_total, bias_total)


def solution(mesh):
    grid = P(None, None, None, "gy", "gz")
    section_grid = P("section", None, None, None, "gy", "gz")
    return jax.shard_map(
        per_device,
        mesh=mesh,
        in_specs=(grid, P("section", None, None, None), P("section", None), grid),
        out_specs=(section_grid, section_grid, P("section", None, None, None), P("section", None)),
        check_vma=False,
    )
```

time: 90.5 us -> 84.5 us (0.934)
  starting transfers between devices: 34.8 us -> 22.7 us
  waiting for transfers between devices: 32.2 us -> 41.5 us
  local copies, waits for them, and re-layouts: 4.24 us -> 2.23 us
  Pallas kernels: 18.1 us -> 17 us
    ppermute x18 -> x6, starting transfers between devices: 26.6 us -> 9.06 us  [spread(): got.append(lax.ppermute(blocks[turn], 'gy', route))]
    ppermute x7 -> x9, waiting for transfers between devices: 9.33 us -> 24.4 us  [the longest x8 19.1 us: swapped(): lax.ppermute(block, axis, [(i, i ^ bit) for i in range(lax.axis_size(axis...]
    ppermute x18 -> x6, waiting for transfers between devices: 22.9 us -> 17.1 us  [spread(): got.append(lax.ppermute(blocks[turn], 'gy', route))]
    ppermute x7 -> x9, starting transfers between devices: 7.54 us -> 13 us  [the longest x8 9.95 us: swapped(): lax.ppermute(block, axis, [(i, i ^ bit) for i in range(lax.axis_size(axis...]
    unnamed x12 -> x8, local copies, waits for them, and re-layouts: 4.07 us -> 2.16 us
    pallas_call x10 -> x9, Pallas kernels: 18.1 us -> 17 us  [call(): pl.pallas_call(kernel, out_shape=arrays, in_specs=[VMEM] * len(args), out...]
  transfers between devices with their start and end apart: 26 -> 16, of which waited for: 15 -> 14; matrix products, arithmetic and copies ran while one was open for 0% -> 0% of each run, Pallas kernels for 10% -> 2%
where the time goes in v6:
time: 84.5 us; the launch traced here: 84.4 us
  waiting for transfers between devices  41.5 us (49%)
  starting transfers between devices  22.7 us (27%)
  Pallas kernels  17 us (20%)
  local copies, waits for them, and re-layouts  2.23 us (3%)
    ppermute x8, waiting for transfers between devices, swapped(): lax.ppermute(block, axis, [(i, i ^ bit) for i in range(lax.axis_size(axis...  19.1 us
    ppermute x6, waiting for transfers between devices, spread(): got.append(lax.ppermute(blocks[turn], 'gy', route))  17.1 us
    pallas_call x9, Pallas kernels, call(): pl.pallas_call(kernel, out_shape=arrays, in_specs=[VMEM] * len(args), out...  17 us
    ppermute x8, starting transfers between devices, swapped(): lax.ppermute(block, axis, [(i, i ^ bit) for i in range(lax.axis_size(axis...  9.95 us
    ppermute x6, starting transfers between devices, spread(): got.append(lax.ppermute(blocks[turn], 'gy', route))  9.06 us
    ppermute x1, waiting for transfers between devices, per_device(): far = lax.ppermute(own, 'section', [(0, 1), (1, 0)])  5.28 us
    ppermute x1, starting transfers between devices, per_device(): far = lax.ppermute(own, 'section', [(0, 1), (1, 0)])  3 us
    unnamed x8, local copies, waits for them, and re-layouts  2.16 us
  transfers between devices with their start and end apart: 16, of which 14 were waited for; matrix products, arithmetic and copies ran while one was open for 0% of the time, Pallas kernels for 2%

profile of v6, /device:TPU:0, one launch (start us, length us, event | category | flops | bytes accessed | tf_op | source)
XLA Modules:
  0.0 84.4 jit_solution(4552668441450436656)
XLA Ops:
  0.6 0.0 copy-start
  0.6 1.5 %copy-done = f32[2,27,64,64]{3,2,1,0:T(8,128)S(1)} copy-done((f32[2,27,64,64]{3,2,1,0:T(8,128)S(1)}, f32[2,27,64,64]{3,2,1,0:T(8,128)}, u32[]{:S(2)}) %copy-start) | copy-done | bytes 884760
  2.1 0.0 copy-start.3
  2.1 0.7 copy-done.3
  2.8 0.0 copy-start.1
  2.8 0.0 copy-start.2
  2.8 0.3 pack.1.source
  3.1 3.0 %collective-permute-start = (f32[28,64,128]{2,1,0:T(8,128)S(1)}, f32[28,64,128]{2,1,0:T(8,128)S(1)}, u32[]{:S(2)}, u32[]{:S(2)}) collective-permute-start(f32[28,64,128]{2,1,0:T(8,128)S(1)} %pack.1.source), channel_id=1, source_target_pairs={{0,16},{16,0},{1,17},{17,1},{2,18},{18,2},{3,19},{19,3},{4,20},{20... | collective-permute-start | bytes 2752520 | tf_op jit(solution)/shard_map/ppermute | solution.py:459
  6.1 0.0 copy-done.1
  6.1 0.0 copy-done.2
  6.1 0.2 turn.1
  6.3 0.1 collective-permute-start.1
  6.4 0.7 collective-permute-start.2
  7.0 0.5 collective-permute-done.1.pair
  7.6 0.0 collective-permute-done.2.inner
  7.6 0.1 windows.1
  7.7 1.6 %collective-permute-start.3 = (f32[2,2,88,128]{3,2,1,0:T(8,128)S(1)}, f32[2,2,88,128]{3,2,1,0:T(8,128)S(1)}, u32[]{:S(2)}, u32[]{:S(2)}) collective-permute-start(f32[2,2,88,128]{3,2,1,0:T(8,128)S(1)} %get-tuple-element.49), channel_id=1, source_target_pairs={{0,4},{4,0},{8,12},{12,8},{1,5},{5,1},{9,13},{13,9},{2,6},{6,2},{1... | collective-permute-start | bytes 540680 | tf_op jit(solution)/shard_map/ppermute | solution.py:425
  9.3 2.6 %collective-permute-start.4 = (f32[2,2,88,128]{3,2,1,0:T(8,128)S(1)}, f32[2,2,88,128]{3,2,1,0:T(8,128)S(1)}, u32[]{:S(2)}, u32[]{:S(2)}) collective-permute-start(f32[2,2,88,128]{3,2,1,0:T(8,128)S(1)} %get-tuple-element.50), channel_id=1, source_target_pairs={{0,8},{4,12},{8,0},{12,4},{1,9},{5,13},{9,1},{13,5},{2,10},{6,14},... | collective-permute-start | bytes 540680 | tf_op jit(solution)/shard_map/ppermute | solution.py:425
  11.9 0.2 collective-permute-start.5
  12.1 0.7 own_table.1
  12.8 0.4 collective-permute-done.3.refs_1_
  13.3 5.3 %collective-permute-done.4.refs_2_ = f32[2,2,88,128]{3,2,1,0:T(8,128)S(1)} collective-permute-done((f32[2,2,88,128]{3,2,1,0:T(8,128)S(1)}, f32[2,2,88,128]{3,2,1,0:T(8,128)S(1)}, u32[]{:S(2)}, u32[]{:S(2)}) %collective-permute-start.4) | collective-permute-done | bytes 180256 | tf_op jit(solution)/shard_map/ppermute | solution.py:425
  18.6 2.6 %collective-permute-done.5.refs_3_ = f32[2,2,88,128]{3,2,1,0:T(8,128)S(1)} collective-permute-done((f32[2,2,88,128]{3,2,1,0:T(8,128)S(1)}, f32[2,2,88,128]{3,2,1,0:T(8,128)S(1)}, u32[]{:S(2)}, u32[]{:S(2)}) %collective-permute-start.5) | collective-permute-done | bytes 180256 | tf_op jit(solution)/shard_map/ppermute | solution.py:425
  21.2 5.3 %collective-permute-done.source = f32[28,64,128]{2,1,0:T(8,128)S(1)} collective-permute-done((f32[28,64,128]{2,1,0:T(8,128)S(1)}, f32[28,64,128]{2,1,0:T(8,128)S(1)}, u32[]{:S(2)}, u32[]{:S(2)}) %collective-permute-start) | collective-permute-done | bytes 917536 | tf_op jit(solution)/shard_map/ppermute | solution.py:459
  26.4 0.7 far_table.1
  27.1 5.3 %forward.1 = (bf16[5,2,480,256]{3,2,1,0:T(8,128)(2,1)S(1)}, f32[4,2,384,128]{3,2,1,0:T(8,128)S(1)}, f32[2,384,128]{2,1,0:T(8,128)S(1)}) custom-call(bf16[2,1152,384]{2,1,0:T(8,128)(2,1)S(1)} %get-tuple-element.54.own, f32[2,8,128]{2,1,0:T(8,128)S(1)} %get-tuple-element.55.own_row, bf16[2,1152,384]{2,1,0:T(8,128)(2,1)S(1)} %get-tuple-element.56.other, ...), custom_call_target="tpu_custom_call" | custom-call | bytes 1024 | tf_op jit(solution)/shard_map/forward/pallas_call | solution.py:24
  32.4 7.2 %backward.1 = (f32[2,2,2,32,128]{4,3,2,1,0:T(8,128)S(1)}, f32[2,2,2,32,128]{4,3,2,1,0:T(8,128)S(1)}, f32[2,2,2,32,128]{4,3,2,1,0:T(8,128)S(1)}, f32[2,2,2,32,128]{4,3,2,1,0:T(8,128)S(1)}, f32[28,64,128]{2,1,0:T(8,128)S(1)}) custom-call(bf16[2,1152,384]{2,1,0:T(8,128)(2,1)S(1)} %get-tuple-element.44.own, bf16[2,1152,384]{2,1,0:T(8,128)(2,1)S(1)} %get-tuple-element.53.other, ...), custom_call_target="tpu_custom_call" | custom-call | bytes 1024 | tf_op jit(solution)/shard_map/backward/pallas_call | solution.py:24
  39.6 0.1 fusion
  39.7 0.5 collective-permute-start.6
  40.2 1.4 %collective-permute-done.6 = f32[896,128]{1,0:T(8,128)S(1)} collective-permute-done((f32[896,128]{1,0:T(8,128)S(1)}, f32[896,128]{1,0:T(8,128)S(1)}, u32[]{:S(2)}, u32[]{:S(2)}) %collective-permute-start.6) | collective-permute-done | bytes 458784 | tf_op jit(solution)/shard_map/ppermute | solution.py:433
  41.7 0.1 bitcast_add_fusion
  41.7 1.8 %collective-permute-start.7 = (f32[448,128]{1,0:T(8,128)S(1)}, f32[448,128]{1,0:T(8,128)S(1)}, u32[]{:S(2)}, u32[]{:S(2)}) collective-permute-start(f32[448,128]{1,0:T(8,128)S(1)} %slice.31), channel_id=1, source_target_pairs={{0,2},{1,3},{2,0},{3,1},{4,6},{5,7},{6,4},{7,5},{8,10},{9,11},{10,... | collective-permute-start | bytes 688136 | tf_op jit(solution)/shard_map/ppermute | solution.py:433
  43.5 2.1 %collective-permute-start.8 = (f32[2,2,2,32,128]{4,3,2,1,0:T(8,128)S(1)}, f32[2,2,2,32,128]{4,3,2,1,0:T(8,128)S(1)}, u32[]{:S(2)}, u32[]{:S(2)}) collective-permute-start(f32[2,2,2,32,128]{4,3,2,1,0:T(8,128)S(1)} %get-tuple-element.72), channel_id=1, source_target_pairs={{0,4},{4,0},{8,12},{12,8},{1,5},{5,1},{9,13},{13,9},{2,6},{6,2},{1... | collective-permute-start | bytes 393224 | tf_op jit(solution)/shard_map/ppermute | solution.py:425
  45.6 2.1 %collective-permute-start.9 = (f32[2,2,2,32,128]{4,3,2,1,0:T(8,128)S(1)}, f32[2,2,2,32,128]{4,3,2,1,0:T(8,128)S(1)}, u32[]{:S(2)}, u32[]{:S(2)}) collective-permute-start(f32[2,2,2,32,128]{4,3,2,1,0:T(8,128)S(1)} %get-tuple-element.73), channel_id=1, source_target_pairs={{0,8},{4,12},{8,0},{12,4},{1,9},{5,13},{9,1},{13,5},{2,10},{6,14},... | collective-permute-start | bytes 393224 | tf_op jit(solution)/shard_map/ppermute | solution.py:425
  47.7 0.4 collective-permute-start.10
  48.1 1.6 %collective-permute-done.7 = f32[448,128]{1,0:T(8,128)S(1)} collective-permute-done((f32[448,128]{1,0:T(8,128)S(1)}, f32[448,128]{1,0:T(8,128)S(1)}, u32[]{:S(2)}, u32[]{:S(2)}) %collective-permute-start.7) | collective-permute-done | bytes 229408 | tf_op jit(solution)/shard_map/ppermute | solution.py:433
  49.7 1.0 %collective-permute-done.8.refs_1_ = f32[2,2,2,32,128]{4,3,2,1,0:T(8,128)S(1)} collective-permute-done((f32[2,2,2,32,128]{4,3,2,1,0:T(8,128)S(1)}, f32[2,2,2,32,128]{4,3,2,1,0:T(8,128)S(1)}, u32[]{:S(2)}, u32[]{:S(2)}) %collective-permute-start.8) | collective-permute-done | bytes 131104 | tf_op jit(solution)/shard_map/ppermute | solution.py:425
  50.7 7.8 %collective-permute-done.9.refs_2_ = f32[2,2,2,32,128]{4,3,2,1,0:T(8,128)S(1)} collective-permute-done((f32[2,2,2,32,128]{4,3,2,1,0:T(8,128)S(1)}, f32[2,2,2,32,128]{4,3,2,1,0:T(8,128)S(1)}, u32[]{:S(2)}, u32[]{:S(2)}) %collective-permute-start.9) | collective-permute-done | bytes 131104 | tf_op jit(solution)/shard_map/ppermute | solution.py:425
  58.5 0.0 collective-permute-done.10.refs_3_
  58.6 2.0 %collective-permute-start.11 = (f32[224,128]{1,0:T(8,128)S(1)}, f32[224,128]{1,0:T(8,128)S(1)}, u32[]{:S(2)}, u32[]{:S(2)}) collective-permute-start(f32[224,128]{1,0:T(8,128)S(1)} %slice_select_fusion), channel_id=1, source_target_pairs={{0,4},{4,0},{8,12},{12,8},{1,5},{5,1},{9,13},{13,9},{2,6},{6,2},{1... | collective-permute-start | bytes 344072 | tf_op jit(solution)/shard_map/ppermute | solution.py:433
  60.6 2.8 %collective-permute-done.11 = f32[224,128]{1,0:T(8,128)S(1)} collective-permute-done((f32[224,128]{1,0:T(8,128)S(1)}, f32[224,128]{1,0:T(8,128)S(1)}, u32[]{:S(2)}, u32[]{:S(2)}) %collective-permute-start.11) | collective-permute-done | bytes 114720 | tf_op jit(solution)/shard_map/ppermute | solution.py:433
  63.4 3.2 %collective-permute-start.12 = (f32[224,128]{1,0:T(8,128)S(1)}, f32[224,128]{1,0:T(8,128)S(1)}, u32[]{:S(2)}, u32[]{:S(2)}) collective-permute-start(f32[224,128]{1,0:T(8,128)S(1)} %select_add_fusion), channel_id=1, source_target_pairs={{0,8},{4,12},{8,0},{12,4},{1,9},{5,13},{9,1},{13,5},{2,10},{6,14},... | collective-permute-start | bytes 344072 | tf_op jit(solution)/shard_map/ppermute | solution.py:433
  66.6 3.2 %collective-permute-done.12 = f32[224,128]{1,0:T(8,128)S(1)} collective-permute-done((f32[224,128]{1,0:T(8,128)S(1)}, f32[224,128]{1,0:T(8,128)S(1)}, u32[]{:S(2)}, u32[]{:S(2)}) %collective-permute-start.12) | collective-permute-done | bytes 114720 | tf_op jit(solution)/shard_map/ppermute | solution.py:433
  69.9 1.4 %collective-permute-start.13 = (f32[224,128]{1,0:T(8,128)S(1)}, f32[224,128]{1,0:T(8,128)S(1)}, u32[]{:S(2)}, u32[]{:S(2)}) collective-permute-start(f32[224,128]{1,0:T(8,128)S(1)} %add.20.kept), channel_id=1, source_target_pairs={{0,4},{4,0},{8,12},{12,8},{1,5},{5,1},{9,13},{13,9},{2,6},{6,2},{1... | collective-permute-start | bytes 344072 | tf_op jit(solution)/shard_map/ppermute | solution.py:433
  71.3 3.5 %collective-permute-done.13.theirs = f32[224,128]{1,0:T(8,128)S(1)} collective-permute-done((f32[224,128]{1,0:T(8,128)S(1)}, f32[224,128]{1,0:T(8,128)S(1)}, u32[]{:S(2)}, u32[]{:S(2)}) %collective-permute-start.13) | collective-permute-done | bytes 114720 | tf_op jit(solution)/shard_map/ppermute | solution.py:433
  74.8 0.9 %collective-permute-start.14 = (f32[448,128]{1,0:T(8,128)S(1)}, f32[448,128]{1,0:T(8,128)S(1)}, u32[]{:S(2)}, u32[]{:S(2)}) collective-permute-start(f32[448,128]{1,0:T(8,128)S(1)} %pad_maximum_fusion.1), channel_id=1, source_target_pairs={{0,2},{1,3},{2,0},{3,1},{4,6},{5,7},{6,4},{7,5},{8,10},{9,11},{10,... | collective-permute-start | bytes 688136 | tf_op jit(solution)/shard_map/ppermute | solution.py:433
  75.7 5.2 %collective-permute-done.14.beside = f32[448,128]{1,0:T(8,128)S(1)} collective-permute-done((f32[448,128]{1,0:T(8,128)S(1)}, f32[448,128]{1,0:T(8,128)S(1)}, u32[]{:S(2)}, u32[]{:S(2)}) %collective-permute-start.14) | collective-permute-done | bytes 229408 | tf_op jit(solution)/shard_map/ppermute | solution.py:433
  80.9 0.1 collective-permute-start.15
  81.0 1.0 %restore.1 = (f32[512,128]{1,0:T(8,128)}, f32[512,128]{1,0:T(8,128)}) custom-call(f32[2,2,2,32,128]{4,3,2,1,0:T(8,128)S(1)} %get-tuple-element.75.refs_0_, f32[2,2,2,32,128]{4,3,2,1,0:T(8,128)S(1)} %collective-permute-done.8.refs_1_, f32[2,2,2,32,128]{4,3,2,1,0:T(8,128)S(1)} %collective-permute-done.9.refs_2_, ...), custom_call_target="tpu_custom_call" | custom-call | bytes 1024 | tf_op jit(solution)/shard_map/restore/pallas_call | solution.py:24
  81.9 0.8 collective-permute-done.15.across
  82.8 1.6 %unpack.1 = (f32[2,27,64,64]{3,2,1,0:T(8,128)}, f32[2,64]{1,0:T(2,128)}) custom-call(f32[224,128]{1,0:T(8,128)S(1)} %add.20.kept, f32[224,128]{1,0:T(8,128)S(1)} %collective-permute-done.13.theirs, f32[448,128]{1,0:T(8,128)S(1)} %collective-permute-done.14.beside, f32[896,128]{1,0:T(8,128)S(1)} %collective-permute-done.15.across), custom_call_target="tpu_custom_call" | custom-call | bytes 1024 | tf_op jit(solution)/shard_map/unpack/pallas_call | solution.py:24
  (7 shorter events, 0.1 us)
Async XLA Ops:
  0.6 1.5 %copy-start = (f32[2,27,64,64]{3,2,1,0:T(8,128)S(1)}, f32[2,27,64,64]{3,2,1,0:T(8,128)}, u32[]{:S(2)}) copy-start(f32[2,27,64,64]{3,2,1,0:T(8,128)} %weights.1) | copy-start | bytes 2654212
  2.1 0.7 copy-start.3
  2.8 3.3 %copy-start.1 = (f32[2,64,2,2,128]{4,3,2,1,0:T(2,128)S(1)}, f32[2,64,2,2,128]{4,3,2,1,0:T(2,128)}, u32[]{:S(2)}) copy-start(f32[2,64,2,2,128]{4,3,2,1,0:T(2,128)} %param.4) | copy-start | bytes 786436
  2.8 3.3 %copy-start.2 = (f32[2,64,2,2,128]{4,3,2,1,0:T(2,128)S(1)}, f32[2,64,2,2,128]{4,3,2,1,0:T(2,128)}, u32[]{:S(2)}) copy-start(f32[2,64,2,2,128]{4,3,2,1,0:T(2,128)} %param.7) | copy-start | bytes 786436
  3.1 23.4 %collective-permute-start = (f32[28,64,128]{2,1,0:T(8,128)S(1)}, f32[28,64,128]{2,1,0:T(8,128)S(1)}, u32[]{:S(2)}, u32[]{:S(2)}) collective-permute-start(f32[28,64,128]{2,1,0:T(8,128)S(1)} %pack.1.source), channel_id=1, source_target_pairs={{0,16},{16,0},{1,17},{17,1},{2,18},{18,2},{3,19},{19,3},{4,20},{20... | collective-permute-start | bytes 2752520 | tf_op jit(solution)/shard_map/ppermute | solution.py:459
  6.3 1.3 %collective-permute-start.1 = (f32[2,2,2,8,128]{4,3,2,1,0:T(8,128)S(1)}, f32[2,2,2,8,128]{4,3,2,1,0:T(8,128)S(1)}, u32[]{:S(2)}, u32[]{:S(2)}) collective-permute-start(f32[2,2,2,8,128]{4,3,2,1,0:T(8,128)S(1)} %get-tuple-element.46), channel_id=1, source_target_pairs={{0,1},{1,0},{2,3},{3,2},{4,5},{5,4},{6,7},{7,6},{8,9},{9,8},{10,11... | collective-permute-start | bytes 98312 | tf_op jit(solution)/shard_map/ppermute | solution.py:433
  6.4 1.2 %collective-permute-start.2 = (f32[2,2,2,8,128]{4,3,2,1,0:T(8,128)S(1)}, f32[2,2,2,8,128]{4,3,2,1,0:T(8,128)S(1)}, u32[]{:S(2)}, u32[]{:S(2)}) collective-permute-start(f32[2,2,2,8,128]{4,3,2,1,0:T(8,128)S(1)} %get-tuple-element.47), channel_id=1, source_target_pairs={{1,2},{2,1},{5,6},{6,5},{9,10},{10,9},{13,14},{14,13},{17,18},{18,... | collective-permute-start | bytes 98312 | tf_op jit(solution)/shard_map/ppermute | solution.py:462
  7.7 5.6 %collective-permute-start.3 = (f32[2,2,88,128]{3,2,1,0:T(8,128)S(1)}, f32[2,2,88,128]{3,2,1,0:T(8,128)S(1)}, u32[]{:S(2)}, u32[]{:S(2)}) collective-permute-start(f32[2,2,88,128]{3,2,1,0:T(8,128)S(1)} %get-tuple-element.49), channel_id=1, source_target_pairs={{0,4},{4,0},{8,12},{12,8},{1,5},{5,1},{9,13},{13,9},{2,6},{6,2},{1... | collective-permute-start | bytes 540680 | tf_op jit(solution)/shard_map/ppermute | solution.py:425
  9.3 9.2 %collective-permute-start.4 = (f32[2,2,88,128]{3,2,1,0:T(8,128)S(1)}, f32[2,2,88,128]{3,2,1,0:T(8,128)S(1)}, u32[]{:S(2)}, u32[]{:S(2)}) collective-permute-start(f32[2,2,88,128]{3,2,1,0:T(8,128)S(1)} %get-tuple-element.50), channel_id=1, source_target_pairs={{0,8},{4,12},{8,0},{12,4},{1,9},{5,13},{9,1},{13,5},{2,10},{6,14},... | collective-permute-start | bytes 540680 | tf_op jit(solution)/shard_map/ppermute | solution.py:425
  11.9 9.2 %collective-permute-start.5 = (f32[2,2,88,128]{3,2,1,0:T(8,128)S(1)}, f32[2,2,88,128]{3,2,1,0:T(8,128)S(1)}, u32[]{:S(2)}, u32[]{:S(2)}) collective-permute-start(f32[2,2,88,128]{3,2,1,0:T(8,128)S(1)} %get-tuple-element.51), channel_id=1, source_target_pairs={{0,12},{4,8},{8,4},{12,0},{1,13},{5,9},{9,5},{13,1},{2,14},{6,10},... | collective-permute-start | bytes 540680 | tf_op jit(solution)/shard_map/ppermute | solution.py:425
  39.7 2.0 %collective-permute-start.6 = (f32[896,128]{1,0:T(8,128)S(1)}, f32[896,128]{1,0:T(8,128)S(1)}, u32[]{:S(2)}, u32[]{:S(2)}) collective-permute-start(f32[896,128]{1,0:T(8,128)S(1)} %bitcast.9), channel_id=1, source_target_pairs={{0,1},{1,0},{2,3},{3,2},{4,5},{5,4},{6,7},{7,6},{8,9},{9,8},{10,11... | collective-permute-start | bytes 1376264 | tf_op jit(solution)/shard_map/ppermute | solution.py:433
  41.7 7.9 %collective-permute-start.7 = (f32[448,128]{1,0:T(8,128)S(1)}, f32[448,128]{1,0:T(8,128)S(1)}, u32[]{:S(2)}, u32[]{:S(2)}) collective-permute-start(f32[448,128]{1,0:T(8,128)S(1)} %slice.31), channel_id=1, source_target_pairs={{0,2},{1,3},{2,0},{3,1},{4,6},{5,7},{6,4},{7,5},{8,10},{9,11},{10,... | collective-permute-start | bytes 688136 | tf_op jit(solution)/shard_map/ppermute | solution.py:433
  43.5 7.2 %collective-permute-start.8 = (f32[2,2,2,32,128]{4,3,2,1,0:T(8,128)S(1)}, f32[2,2,2,32,128]{4,3,2,1,0:T(8,128)S(1)}, u32[]{:S(2)}, u32[]{:S(2)}) collective-permute-start(f32[2,2,2,32,128]{4,3,2,1,0:T(8,128)S(1)} %get-tuple-element.72), channel_id=1, source_target_pairs={{0,4},{4,0},{8,12},{12,8},{1,5},{5,1},{9,13},{13,9},{2,6},{6,2},{1... | collective-permute-start | bytes 393224 | tf_op jit(solution)/shard_map/ppermute | solution.py:425
  45.6 12.9 %collective-permute-start.9 = (f32[2,2,2,32,128]{4,3,2,1,0:T(8,128)S(1)}, f32[2,2,2,32,128]{4,3,2,1,0:T(8,128)S(1)}, u32[]{:S(2)}, u32[]{:S(2)}) collective-permute-start(f32[2,2,2,32,128]{4,3,2,1,0:T(8,128)S(1)} %get-tuple-element.73), channel_id=1, source_target_pairs={{0,8},{4,12},{8,0},{12,4},{1,9},{5,13},{9,1},{13,5},{2,10},{6,14},... | collective-permute-start | bytes 393224 | tf_op jit(solution)/shard_map/ppermute | solution.py:425
  47.7 10.9 %collective-permute-start.10 = (f32[2,2,2,32,128]{4,3,2,1,0:T(8,128)S(1)}, f32[2,2,2,32,128]{4,3,2,1,0:T(8,128)S(1)}, u32[]{:S(2)}, u32[]{:S(2)}) collective-permute-start(f32[2,2,2,32,128]{4,3,2,1,0:T(8,128)S(1)} %get-tuple-element.74), channel_id=1, source_target_pairs={{0,12},{4,8},{8,4},{12,0},{1,13},{5,9},{9,5},{13,1},{2,14},{6,10},... | collective-permute-start | bytes 393224 | tf_op jit(solution)/shard_map/ppermute | solution.py:425
  58.6 4.9 %collective-permute-start.11 = (f32[224,128]{1,0:T(8,128)S(1)}, f32[224,128]{1,0:T(8,128)S(1)}, u32[]{:S(2)}, u32[]{:S(2)}) collective-permute-start(f32[224,128]{1,0:T(8,128)S(1)} %slice_select_fusion), channel_id=1, source_target_pairs={{0,4},{4,0},{8,12},{12,8},{1,5},{5,1},{9,13},{13,9},{2,6},{6,2},{1... | collective-permute-start | bytes 344072 | tf_op jit(solution)/shard_map/ppermute | solution.py:433
  63.4 6.4 %collective-permute-start.12 = (f32[224,128]{1,0:T(8,128)S(1)}, f32[224,128]{1,0:T(8,128)S(1)}, u32[]{:S(2)}, u32[]{:S(2)}) collective-permute-start(f32[224,128]{1,0:T(8,128)S(1)} %select_add_fusion), channel_id=1, source_target_pairs={{0,8},{4,12},{8,0},{12,4},{1,9},{5,13},{9,1},{13,5},{2,10},{6,14},... | collective-permute-start | bytes 344072 | tf_op jit(solution)/shard_map/ppermute | solution.py:433
  69.9 4.9 %collective-permute-start.13 = (f32[224,128]{1,0:T(8,128)S(1)}, f32[224,128]{1,0:T(8,128)S(1)}, u32[]{:S(2)}, u32[]{:S(2)}) collective-permute-start(f32[224,128]{1,0:T(8,128)S(1)} %add.20.kept), channel_id=1, source_target_pairs={{0,4},{4,0},{8,12},{12,8},{1,5},{5,1},{9,13},{13,9},{2,6},{6,2},{1... | collective-permute-start | bytes 344072 | tf_op jit(solution)/shard_map/ppermute | solution.py:433
  74.8 6.1 %collective-permute-start.14 = (f32[448,128]{1,0:T(8,128)S(1)}, f32[448,128]{1,0:T(8,128)S(1)}, u32[]{:S(2)}, u32[]{:S(2)}) collective-permute-start(f32[448,128]{1,0:T(8,128)S(1)} %pad_maximum_fusion.1), channel_id=1, source_target_pairs={{0,2},{1,3},{2,0},{3,1},{4,6},{5,7},{6,4},{7,5},{8,10},{9,11},{10,... | collective-permute-start | bytes 688136 | tf_op jit(solution)/shard_map/ppermute | solution.py:433
  80.9 1.9 %collective-permute-start.15 = (f32[896,128]{1,0:T(8,128)S(1)}, f32[896,128]{1,0:T(8,128)S(1)}, u32[]{:S(2)}, u32[]{:S(2)}) collective-permute-start(f32[896,128]{1,0:T(8,128)S(1)} %pad_maximum_fusion), channel_id=1, source_target_pairs={{0,1},{1,0},{2,3},{3,2},{4,5},{5,4},{6,7},{7,6},{8,9},{9,8},{10,11... | collective-permute-start | bytes 1376264 | tf_op jit(solution)/shard_map/ppermute | solution.py:433

commit v7 on v6

--- a/solution.py
+++ b/solution.py
@@ -43,12 +43,16 @@
     return high, (values - high.astype(F32)).astype(BF16)
 
 
-def pack_kernel(weights, biases, own):
+def pack_kernel(weights, biases, own, sent):
     chans = weights.shape[2]
     for tap in range(TAPS):
         own[tap] = jnp.concatenate([weights[0, tap], weights[1, tap]], axis=1)
     own[TAPS] = jnp.zeros((chans, LANES), F32)
     own[TAPS, 0:1, :] = jnp.concatenate([biases[0:1, :], biases[1:2, :]], axis=1)
+    half = sent.shape[0]
+    start = lax.axis_index("gz") % 2 * half
+    for index in range(half):
+        sent[index] = own[start + index]
 
 
 def turn_kernel(dims, inflow, cotangent, rows, pair, inner):
@@ -92,11 +96,20 @@
                     outs[turn][micro, y, at] = wide[field, micro, y, pl.ds(start, width + 2 * halo)]
 
 
-def table_kernel(source, fwd, bwd, row):
-    chans = source.shape[1]
+def table_kernel(*refs):
+    parts, (fwd, bwd, row) = refs[:-3], refs[-3:]
+    odd = lax.axis_index("gz") % 2
+    count, chans, _ = parts[0].shape
+
+    def block_of(tap):
+        if len(parts) == 1:
+            return parts[0][tap]
+        index = tap % count
+        return jnp.where(odd == tap // count, parts[0][index], parts[1][index])
+
     for b in range(3):
         for c in range(3):
-            taps = [source[9 * a + 3 * b + c] for a in range(3)]
+            taps = [block_of(9 * a + 3 * b + c) for a in range(3)]
             for layer in range(2):
                 lanes = slice(layer * chans, (layer + 1) * chans)
                 below, level, above = [tap[:, lanes] for tap in taps]
@@ -109,7 +122,7 @@
                     target[layer, 2 * r * LANES : (2 * r + 1) * LANES, at] = hi
                     target[layer, (2 * r + 1) * LANES : (2 * r + 2) * LANES, at] = hi
                     target[layer, (6 + r) * LANES : (7 + r) * LANES, at] = lo
-    last = source[TAPS, 0:1, :]
+    last = block_of(TAPS)[0:1, :]
     for layer in range(2):
         part = last[:, layer * chans : (layer + 1) * chans]
         row[layer] = jnp.broadcast_to(jnp.concatenate([part, part], axis=1), (8, LANES))
@@ -380,15 +393,15 @@
         sums[spot(TAPS), 0:1, lanes] = row[:, :chans] + row[:, chans:]
 
 
-def unpack_kernel(kept, theirs, beside, across, weight, bias, whole):
-    half = kept.shape[0]
+def unpack_kernel(near, core, weight, bias, whole):
+    part = near.shape[0] // 4
     chans = weight.shape[-1]
     odd, swap = lax.axis_index("gy") % 2, column_bits()
-    parts = [(kept, 0), (theirs, 0), (beside, 0), (beside, half)]
-    parts += [(across, half * i) for i in range(4)]
-    for index, (source, first) in enumerate(parts):
-        at = ((index // 2 ^ swap) * 2 + (index % 2 ^ odd)) * half
-        whole[pl.ds(pl.multiple_of(at, 8), half), :] = source[first : first + half, :]
+    for index in range(8):
+        source = near if index < 4 else core
+        first = index % 4 * part
+        at = ((index // 2 ^ swap) * 2 + (index % 2 ^ odd)) * part
+        whole[pl.ds(pl.multiple_of(at, 8), part), :] = source[first : first + part, :]
     for layer in range(2):
         lanes = slice(layer * chans, (layer + 1) * chans)
         for tap in range(TAPS):
@@ -433,9 +446,14 @@
     return lax.ppermute(block, axis, [(i, i ^ bit) for i in range(lax.axis_size(axis))])
 
 
-def halved(block, bit):
-    rows = block.shape[0] // 2
-    return block[:rows] + swapped(block[rows:], bit)
+def around(above, beside, across):
+    slabs, columns = lax.axis_size("gy"), lax.axis_size("gz")
+    route = [
+        (i * columns + g, (i ^ 1) * columns + (g ^ 2)) for i in range(slabs) for g in range(columns)
+    ]
+    beside = swapped(beside, 2)
+    across = lax.ppermute(across, ("gy", "gz"), route)
+    return [swapped(above, 1, "gy"), beside, across]
 
 
 def per_device(inflow, weights, biases, cotangent):
@@ -449,14 +467,15 @@
     scale = 1.0 / math.sqrt(micros * size_x * rows_y * local_z * columns)
     rows = micros * chans * size_x * local_y
     ends = ((2, micros, local_y, HALO, LANES), F32)
-    (own,) = call(pack_kernel, "pack", [((BLOCKS, chans, LANES), F32)], [weights, biases])
+    packs = [((BLOCKS, chans, LANES), F32), ((BLOCKS // 2, chans, LANES), F32)]
+    own, sent = call(pack_kernel, "pack", packs, [weights, biases])
     fields, pair, inner = call(
         functools.partial(turn_kernel, inflow.shape),
         "turn",
         [((2, micros, local_y, local_z, LANES), F32), ends, ends],
         [inflow.reshape(rows, local_z), cotangent.reshape(rows, local_z)],
     )
-    far = lax.ppermute(own, "section", [(0, 1), (1, 0)])
+    near_half = lax.ppermute(sent, "section", [(0, 1), (1, 0)])
     pair = swapped(pair, 1)
     route = [(i, i + 1) for i in range(1, columns - 1, 2)]
     inner = lax.ppermute(inner, "gz", route + [(after, before) for before, after in route])
@@ -469,11 +488,12 @@
         [pltpu.VMEM((2, micros, local_y, local_z + 2 * HALO, LANES), F32)],
     )
     windows = spread(windows)
-    far, windows = lax.optimization_barrier((far, windows))
+    near_half, windows = lax.optimization_barrier((near_half, windows))
+    far_half = swapped(near_half, 1)
 
     tables = [((2, 9 * LANES, 3 * LANES), BF16)] * 2 + [((2, 8, LANES), F32)]
     own_fwd, own_bwd, own_row = call(table_kernel, "own_table", tables, [own])
-    far_fwd, far_bwd, far_row = call(table_kernel, "far_table", tables, [far])
+    far_fwd, far_bwd, far_row = call(table_kernel, "far_table", tables, [near_half, far_half])
 
     dims = (micros, rows_y, depth, width, chunk_y, slabs, local_z * columns)
     padded = (rows_y + 2) * depth
@@ -502,23 +522,26 @@
         ],
     )
 
-    block = halved(sums.reshape(BLOCKS * chans, LANES), 1)
+    block = sums.reshape(BLOCKS * chans, LANES)
+    half = block.shape[0] // 2
+    block = block[:half] + swapped(block[half:], 1)
     block, outs = lax.optimization_barrier((block, outs))
     outs = spread(outs)
-    block = halved(block, 2)
-    block, outs = lax.optimization_barrier((block, outs))
-    half = block.shape[0] // 2
+    part = half // 4
     odd = lax.axis_index("gy") % 2 == 1
-    kept_half = jnp.where(odd, block[half:], block[:half])
-    kept_half = kept_half + swapped(jnp.where(odd, block[:half], block[half:]), 1, "gy")
+    lows, highs = [block[i * part : (i + 1) * part] for i in (0, 2)], [
+        block[i * part : (i + 1) * part] for i in (1, 3)
+    ]
+    mine, beside = [jnp.where(odd, high, low) for low, high in zip(lows, highs)]
+    above, across = [jnp.where(odd, low, high) for low, high in zip(lows, highs)]
+    kept = mine + sum(around(above, beside, across))
+    kept, outs = lax.optimization_barrier((kept, outs))
     bit = 2
     while bit < slabs:
-        kept_half = kept_half + swapped(kept_half, bit, "gy")
+        kept = kept + swapped(kept, bit, "gy")
         bit *= 2
-    theirs = swapped(kept_half, 1, "gy")
-    quarter = jnp.concatenate([kept_half, theirs], axis=0)
-    beside = swapped(quarter, 2)
-    across = swapped(jnp.concatenate([quarter, beside], axis=0), 1)
+    near = jnp.concatenate([kept, *around(kept, kept, kept)], axis=0)
+    core = swapped(near, 1)
     section_out, section_grad = call(
         functools.partial(restore_kernel, (micros, chans, size_x, local_y, width)),
         "restore",
@@ -530,7 +553,7 @@
         unpack_kernel,
         "unpack",
         [((2, TAPS, chans, chans), F32), ((2, chans), F32)],
-        [kept_half, theirs, beside, across],
+        [near, core],
         [pltpu.VMEM((BLOCKS * chans, LANES), F32)],
     )
     shape = (1, *inflow.shape)

time: 84.5 us -> 81.6 us (0.966)
  waiting for transfers between devices: 41.5 us -> 31.5 us
  starting transfers between devices: 22.7 us -> 29.7 us
    ppermute x8 -> x9, waiting for transfers between devices: 19.1 us -> 10.8 us  [swapped(): lax.ppermute(block, axis, [(i, i ^ bit) for i in range(lax.axis_size(axis...]
    ppermute x1 -> x3, starting transfers between devices: 3 us -> 6.37 us  [the longest x2 3.37 us: around(): across = lax.ppermute(across, ('gy', 'gz'), route)]
    ppermute x8 -> x9, starting transfers between devices: 9.95 us -> 13 us  [swapped(): lax.ppermute(block, axis, [(i, i ^ bit) for i in range(lax.axis_size(axis...]
    ppermute x1 -> x3, waiting for transfers between devices: 5.28 us -> 2.54 us  [the longest x2 2.54 us: around(): across = lax.ppermute(across, ('gy', 'gz'), route)]
    ppermute x6, waiting for transfers between devices: 17.1 us -> 18.2 us  [spread(): got.append(lax.ppermute(blocks[turn], 'gy', route))]
  transfers between devices with their start and end apart: 16 -> 19, of which waited for: 14 -> 15; matrix products, arithmetic and copies ran while one was open for 0% -> 0% of each run, Pallas kernels for 2% -> 2%
where the time goes in v7:
time: 81.6 us; the launch traced here: 81.5 us
  waiting for transfers between devices  31.5 us (39%)
  starting transfers between devices  29.7 us (36%)
  Pallas kernels  17.1 us (21%)
  local copies, waits for them, and re-layouts  2.24 us (3%)
    ppermute x6, waiting for transfers between devices, spread(): got.append(lax.ppermute(blocks[turn], 'gy', route))  18.2 us
    pallas_call x9, Pallas kernels, call(): pl.pallas_call(kernel, out_shape=arrays, in_specs=[VMEM] * len(args), out...  17.1 us
    ppermute x9, starting transfers between devices, swapped(): lax.ppermute(block, axis, [(i, i ^ bit) for i in range(lax.axis_size(axis...  13 us
    ppermute x9, waiting for transfers between devices, swapped(): lax.ppermute(block, axis, [(i, i ^ bit) for i in range(lax.axis_size(axis...  10.8 us
    ppermute x6, starting transfers between devices, spread(): got.append(lax.ppermute(blocks[turn], 'gy', route))  9.67 us
    ppermute x2, starting transfers between devices, around(): across = lax.ppermute(across, ('gy', 'gz'), route)  3.37 us
    ppermute x1, starting transfers between devices, per_device(): near_half = lax.ppermute(sent, 'section', [(0, 1), (1, 0)])  3 us
    ppermute x2, waiting for transfers between devices, around(): across = lax.ppermute(across, ('gy', 'gz'), route)  2.54 us
  transfers between devices with their start and end apart: 19, of which 15 were waited for; matrix products, arithmetic and copies ran while one was open for 0% of the time, Pallas kernels for 2%

profile of v7, /device:TPU:0, one launch (start us, length us, event | category | flops | bytes accessed | tf_op | source)
XLA Modules:
  0.0 81.5 jit_solution(13821081713241211473)
XLA Ops:
  0.6 0.0 copy-start
  0.6 1.5 %copy-done = f32[2,27,64,64]{3,2,1,0:T(8,128)S(1)} copy-done((f32[2,27,64,64]{3,2,1,0:T(8,128)S(1)}, f32[2,27,64,64]{3,2,1,0:T(8,128)}, u32[]{:S(2)}) %copy-start) | copy-done | bytes 884760
  2.1 0.0 copy-start.3
  2.1 0.7 copy-done.3
  2.8 0.0 copy-start.1
  2.8 0.0 copy-start.2
  2.8 0.3 pack.1
  3.1 3.0 %collective-permute-start = (f32[14,64,128]{2,1,0:T(8,128)S(1)}, f32[14,64,128]{2,1,0:T(8,128)S(1)}, u32[]{:S(2)}, u32[]{:S(2)}) collective-permute-start(f32[14,64,128]{2,1,0:T(8,128)S(1)} %get-tuple-element.48), channel_id=1, source_target_pairs={{0,16},{16,0},{1,17},{17,1},{2,18},{18,2},{3,19},{19,3},{4,20},{20... | collective-permute-start | bytes 1376264 | tf_op jit(solution)/shard_map/ppermute | solution.py:478
  6.1 0.0 copy-done.1
  6.1 0.0 copy-done.2
  6.1 0.2 turn.1
  6.3 0.1 collective-permute-start.1
  6.4 0.7 collective-permute-start.2
  7.1 0.5 collective-permute-done.1.pair
  7.6 0.0 collective-permute-done.2.inner
  7.6 0.1 windows.1
  7.7 1.6 %collective-permute-start.3 = (f32[2,2,88,128]{3,2,1,0:T(8,128)S(1)}, f32[2,2,88,128]{3,2,1,0:T(8,128)S(1)}, u32[]{:S(2)}, u32[]{:S(2)}) collective-permute-start(f32[2,2,88,128]{3,2,1,0:T(8,128)S(1)} %get-tuple-element.53), channel_id=1, source_target_pairs={{0,4},{4,0},{8,12},{12,8},{1,5},{5,1},{9,13},{13,9},{2,6},{6,2},{1... | collective-permute-start | bytes 540680 | tf_op jit(solution)/shard_map/ppermute | solution.py:438
  9.4 2.6 %collective-permute-start.4 = (f32[2,2,88,128]{3,2,1,0:T(8,128)S(1)}, f32[2,2,88,128]{3,2,1,0:T(8,128)S(1)}, u32[]{:S(2)}, u32[]{:S(2)}) collective-permute-start(f32[2,2,88,128]{3,2,1,0:T(8,128)S(1)} %get-tuple-element.54), channel_id=1, source_target_pairs={{0,8},{4,12},{8,0},{12,4},{1,9},{5,13},{9,1},{13,5},{2,10},{6,14},... | collective-permute-start | bytes 540680 | tf_op jit(solution)/shard_map/ppermute | solution.py:438
  12.0 0.2 collective-permute-start.5
  12.2 1.1 %collective-permute-done.3.refs_1_ = f32[2,2,88,128]{3,2,1,0:T(8,128)S(1)} collective-permute-done((f32[2,2,88,128]{3,2,1,0:T(8,128)S(1)}, f32[2,2,88,128]{3,2,1,0:T(8,128)S(1)}, u32[]{:S(2)}, u32[]{:S(2)}) %collective-permute-start.3) | collective-permute-done | bytes 180256 | tf_op jit(solution)/shard_map/ppermute | solution.py:438
  13.3 5.3 %collective-permute-done.4.refs_2_ = f32[2,2,88,128]{3,2,1,0:T(8,128)S(1)} collective-permute-done((f32[2,2,88,128]{3,2,1,0:T(8,128)S(1)}, f32[2,2,88,128]{3,2,1,0:T(8,128)S(1)}, u32[]{:S(2)}, u32[]{:S(2)}) %collective-permute-start.4) | collective-permute-done | bytes 180256 | tf_op jit(solution)/shard_map/ppermute | solution.py:438
  18.6 2.6 %collective-permute-done.5.refs_3_ = f32[2,2,88,128]{3,2,1,0:T(8,128)S(1)} collective-permute-done((f32[2,2,88,128]{3,2,1,0:T(8,128)S(1)}, f32[2,2,88,128]{3,2,1,0:T(8,128)S(1)}, u32[]{:S(2)}, u32[]{:S(2)}) %collective-permute-start.5) | collective-permute-done | bytes 180256 | tf_op jit(solution)/shard_map/ppermute | solution.py:438
  21.2 0.0 collective-permute-done.refs_0_
  21.2 5.7 %collective-permute-start.6 = (f32[14,64,128]{2,1,0:T(8,128)S(1)}, f32[14,64,128]{2,1,0:T(8,128)S(1)}, u32[]{:S(2)}, u32[]{:S(2)}) collective-permute-start(f32[14,64,128]{2,1,0:T(8,128)S(1)} %collective-permute-done.refs_0_), channel_id=1, source_target_pairs={{0,1},{1,0},{2,3},{3,2},{4,5},{5,4},{6,7},{7,6},{8,9},{9,8},{10,11... | collective-permute-start | bytes 1376264 | tf_op jit(solution)/shard_map/ppermute | solution.py:446
  26.9 0.7 own_table.1
  27.6 0.7 collective-permute-done.6.refs_1_
  28.4 0.7 far_table.1
  29.1 5.3 %forward.1 = (bf16[5,2,480,256]{3,2,1,0:T(8,128)(2,1)S(1)}, f32[4,2,384,128]{3,2,1,0:T(8,128)S(1)}, f32[2,384,128]{2,1,0:T(8,128)S(1)}) custom-call(bf16[2,1152,384]{2,1,0:T(8,128)(2,1)S(1)} %get-tuple-element.58.own, f32[2,8,128]{2,1,0:T(8,128)S(1)} %get-tuple-element.59.own_row, bf16[2,1152,384]{2,1,0:T(8,128)(2,1)S(1)} %get-tuple-element.60.other, ...), custom_call_target="tpu_custom_call" | custom-call | bytes 1024 | tf_op jit(solution)/shard_map/forward/pallas_call | solution.py:24
  34.4 7.2 %backward.1 = (f32[2,2,2,32,128]{4,3,2,1,0:T(8,128)S(1)}, f32[2,2,2,32,128]{4,3,2,1,0:T(8,128)S(1)}, f32[2,2,2,32,128]{4,3,2,1,0:T(8,128)S(1)}, f32[2,2,2,32,128]{4,3,2,1,0:T(8,128)S(1)}, f32[28,64,128]{2,1,0:T(8,128)S(1)}) custom-call(bf16[2,1152,384]{2,1,0:T(8,128)(2,1)S(1)} %get-tuple-element.47.own, bf16[2,1152,384]{2,1,0:T(8,128)(2,1)S(1)} %get-tuple-element.57.other, ...), custom_call_target="tpu_custom_call" | custom-call | bytes 1024 | tf_op jit(solution)/shard_map/backward/pallas_call | solution.py:24
  41.6 0.1 fusion
  41.7 0.4 collective-permute-start.7
  42.2 1.4 %collective-permute-done.7 = f32[896,128]{1,0:T(8,128)S(1)} collective-permute-done((f32[896,128]{1,0:T(8,128)S(1)}, f32[896,128]{1,0:T(8,128)S(1)}, u32[]{:S(2)}, u32[]{:S(2)}) %collective-permute-start.7) | collective-permute-done | bytes 458784 | tf_op jit(solution)/shard_map/ppermute | solution.py:446
  43.7 3.3 %collective-permute-start.10 = (f32[224,128]{1,0:T(8,128)S(1)}, f32[224,128]{1,0:T(8,128)S(1)}, u32[]{:S(2)}, u32[]{:S(2)}) collective-permute-start(f32[224,128]{1,0:T(8,128)S(1)} %get-tuple-element.91), channel_id=1, source_target_pairs={{0,6},{1,7},{2,4},{3,5},{4,2},{5,3},{6,0},{7,1},{8,14},{9,15},{10,... | collective-permute-start | bytes 344072 | tf_op jit(solution)/shard_map/ppermute | solution.py:455
  47.0 0.0 collective-permute-start.8
  47.0 1.0 %collective-permute-start.9 = (f32[224,128]{1,0:T(8,128)S(1)}, f32[224,128]{1,0:T(8,128)S(1)}, u32[]{:S(2)}, u32[]{:S(2)}) collective-permute-start(f32[224,128]{1,0:T(8,128)S(1)} %get-tuple-element.90), channel_id=1, source_target_pairs={{0,2},{1,3},{2,0},{3,1},{4,6},{5,7},{6,4},{7,5},{8,10},{9,11},{10,... | collective-permute-start | bytes 344072 | tf_op jit(solution)/shard_map/ppermute | solution.py:446
  48.0 2.0 %collective-permute-start.11 = (f32[2,2,2,32,128]{4,3,2,1,0:T(8,128)S(1)}, f32[2,2,2,32,128]{4,3,2,1,0:T(8,128)S(1)}, u32[]{:S(2)}, u32[]{:S(2)}) collective-permute-start(f32[2,2,2,32,128]{4,3,2,1,0:T(8,128)S(1)} %get-tuple-element.76), channel_id=1, source_target_pairs={{0,4},{4,0},{8,12},{12,8},{1,5},{5,1},{9,13},{13,9},{2,6},{6,2},{1... | collective-permute-start | bytes 393224 | tf_op jit(solution)/shard_map/ppermute | solution.py:438
  50.0 1.1 %collective-permute-start.12 = (f32[2,2,2,32,128]{4,3,2,1,0:T(8,128)S(1)}, f32[2,2,2,32,128]{4,3,2,1,0:T(8,128)S(1)}, u32[]{:S(2)}, u32[]{:S(2)}) collective-permute-start(f32[2,2,2,32,128]{4,3,2,1,0:T(8,128)S(1)} %get-tuple-element.77), channel_id=1, source_target_pairs={{0,8},{4,12},{8,0},{12,4},{1,9},{5,13},{9,1},{13,5},{2,10},{6,14},... | collective-permute-start | bytes 393224 | tf_op jit(solution)/shard_map/ppermute | solution.py:438
  51.1 0.0 collective-permute-done.10
  51.1 2.1 %collective-permute-start.13 = (f32[2,2,2,32,128]{4,3,2,1,0:T(8,128)S(1)}, f32[2,2,2,32,128]{4,3,2,1,0:T(8,128)S(1)}, u32[]{:S(2)}, u32[]{:S(2)}) collective-permute-start(f32[2,2,2,32,128]{4,3,2,1,0:T(8,128)S(1)} %get-tuple-element.78), channel_id=1, source_target_pairs={{0,12},{4,8},{8,4},{12,0},{1,13},{5,9},{9,5},{13,1},{2,14},{6,10},... | collective-permute-start | bytes 393224 | tf_op jit(solution)/shard_map/ppermute | solution.py:438
  53.2 1.3 %collective-permute-done.8 = f32[224,128]{1,0:T(8,128)S(1)} collective-permute-done((f32[224,128]{1,0:T(8,128)S(1)}, f32[224,128]{1,0:T(8,128)S(1)}, u32[]{:S(2)}, u32[]{:S(2)}) %collective-permute-start.8) | collective-permute-done | bytes 114720 | tf_op jit(solution)/shard_map/ppermute | solution.py:446
  54.5 0.0 collective-permute-done.9
  54.5 3.8 %collective-permute-done.11.refs_1_ = f32[2,2,2,32,128]{4,3,2,1,0:T(8,128)S(1)} collective-permute-done((f32[2,2,2,32,128]{4,3,2,1,0:T(8,128)S(1)}, f32[2,2,2,32,128]{4,3,2,1,0:T(8,128)S(1)}, u32[]{:S(2)}, u32[]{:S(2)}) %collective-permute-start.11) | collective-permute-done | bytes 131104 | tf_op jit(solution)/shard_map/ppermute | solution.py:438
  58.3 0.3 collective-permute-done.12.refs_2_
  58.6 5.0 %collective-permute-done.13.refs_3_ = f32[2,2,2,32,128]{4,3,2,1,0:T(8,128)S(1)} collective-permute-done((f32[2,2,2,32,128]{4,3,2,1,0:T(8,128)S(1)}, f32[2,2,2,32,128]{4,3,2,1,0:T(8,128)S(1)}, u32[]{:S(2)}, u32[]{:S(2)}) %collective-permute-start.13) | collective-permute-done | bytes 131104 | tf_op jit(solution)/shard_map/ppermute | solution.py:438
  63.7 2.2 %collective-permute-start.14 = (f32[224,128]{1,0:T(8,128)S(1)}, f32[224,128]{1,0:T(8,128)S(1)}, u32[]{:S(2)}, u32[]{:S(2)}) collective-permute-start(f32[224,128]{1,0:T(8,128)S(1)} %add_add_fusion), channel_id=1, source_target_pairs={{0,8},{4,12},{8,0},{12,4},{1,9},{5,13},{9,1},{13,5},{2,10},{6,14},... | collective-permute-start | bytes 344072 | tf_op jit(solution)/shard_map/ppermute | solution.py:446
  65.9 4.7 %collective-permute-done.14 = f32[224,128]{1,0:T(8,128)S(1)} collective-permute-done((f32[224,128]{1,0:T(8,128)S(1)}, f32[224,128]{1,0:T(8,128)S(1)}, u32[]{:S(2)}, u32[]{:S(2)}) %collective-permute-start.14) | collective-permute-done | bytes 114720 | tf_op jit(solution)/shard_map/ppermute | solution.py:446
  70.6 0.1 collective-permute-start.17
  70.7 1.5 %collective-permute-start.16 = (f32[224,128]{1,0:T(8,128)S(1)}, f32[224,128]{1,0:T(8,128)S(1)}, u32[]{:S(2)}, u32[]{:S(2)}) collective-permute-start(f32[224,128]{1,0:T(8,128)S(1)} %add.24), channel_id=1, source_target_pairs={{0,2},{1,3},{2,0},{3,1},{4,6},{5,7},{6,4},{7,5},{8,10},{9,11},{10,... | collective-permute-start | bytes 344072 | tf_op jit(solution)/shard_map/ppermute | solution.py:446
  72.2 2.0 %collective-permute-start.15 = (f32[224,128]{1,0:T(8,128)S(1)}, f32[224,128]{1,0:T(8,128)S(1)}, u32[]{:S(2)}, u32[]{:S(2)}) collective-permute-start(f32[224,128]{1,0:T(8,128)S(1)} %add.24), channel_id=1, source_target_pairs={{0,4},{4,0},{8,12},{12,8},{1,5},{5,1},{9,13},{13,9},{2,6},{6,2},{1... | collective-permute-start | bytes 344072 | tf_op jit(solution)/shard_map/ppermute | solution.py:446
  74.2 2.5 %collective-permute-done.17 = f32[224,128]{1,0:T(8,128)S(1)} collective-permute-done((f32[224,128]{1,0:T(8,128)S(1)}, f32[224,128]{1,0:T(8,128)S(1)}, u32[]{:S(2)}, u32[]{:S(2)}) %collective-permute-start.17) | collective-permute-done | bytes 114720 | tf_op jit(solution)/shard_map/ppermute | solution.py:455
  76.7 0.1 collective-permute-done.16
  76.8 1.2 %collective-permute-done.15 = f32[224,128]{1,0:T(8,128)S(1)} collective-permute-done((f32[224,128]{1,0:T(8,128)S(1)}, f32[224,128]{1,0:T(8,128)S(1)}, u32[]{:S(2)}, u32[]{:S(2)}) %collective-permute-start.15) | collective-permute-done | bytes 114720 | tf_op jit(solution)/shard_map/ppermute | solution.py:446
  78.0 0.1 collective-permute-start.18
  78.1 1.0 %restore.1 = (f32[512,128]{1,0:T(8,128)}, f32[512,128]{1,0:T(8,128)}) custom-call(f32[2,2,2,32,128]{4,3,2,1,0:T(8,128)S(1)} %get-tuple-element.79.refs_0_, f32[2,2,2,32,128]{4,3,2,1,0:T(8,128)S(1)} %collective-permute-done.11.refs_1_, f32[2,2,2,32,128]{4,3,2,1,0:T(8,128)S(1)} %collective-permute-done.12.refs_2_, ...), custom_call_target="tpu_custom_call" | custom-call | bytes 1024 | tf_op jit(solution)/shard_map/restore/pallas_call | solution.py:24
  79.0 0.8 %collective-permute-done.18.core = f32[896,128]{1,0:T(8,128)S(1)} collective-permute-done((f32[896,128]{1,0:T(8,128)S(1)}, f32[896,128]{1,0:T(8,128)S(1)}, u32[]{:S(2)}, u32[]{:S(2)}) %collective-permute-start.18) | collective-permute-done | bytes 458784 | tf_op jit(solution)/shard_map/ppermute | solution.py:446
  79.9 1.6 %unpack.1 = (f32[2,27,64,64]{3,2,1,0:T(8,128)}, f32[2,64]{1,0:T(2,128)}) custom-call(f32[896,128]{1,0:T(8,128)S(1)} %pad_maximum_fusion.near, f32[896,128]{1,0:T(8,128)S(1)} %collective-permute-done.18.core), custom_call_target="tpu_custom_call" | custom-call | bytes 1024 | tf_op jit(solution)/shard_map/unpack/pallas_call | solution.py:24
  (5 shorter events, 0.2 us)
Async XLA Ops:
  0.6 1.5 %copy-start = (f32[2,27,64,64]{3,2,1,0:T(8,128)S(1)}, f32[2,27,64,64]{3,2,1,0:T(8,128)}, u32[]{:S(2)}) copy-start(f32[2,27,64,64]{3,2,1,0:T(8,128)} %weights.1) | copy-start | bytes 2654212
  2.1 0.7 copy-start.3
  2.8 3.4 %copy-start.1 = (f32[2,64,2,2,128]{4,3,2,1,0:T(2,128)S(1)}, f32[2,64,2,2,128]{4,3,2,1,0:T(2,128)}, u32[]{:S(2)}) copy-start(f32[2,64,2,2,128]{4,3,2,1,0:T(2,128)} %param.4) | copy-start | bytes 786436
  2.8 3.4 %copy-start.2 = (f32[2,64,2,2,128]{4,3,2,1,0:T(2,128)S(1)}, f32[2,64,2,2,128]{4,3,2,1,0:T(2,128)}, u32[]{:S(2)}) copy-start(f32[2,64,2,2,128]{4,3,2,1,0:T(2,128)} %param.7) | copy-start | bytes 786436
  3.1 18.1 %collective-permute-start = (f32[14,64,128]{2,1,0:T(8,128)S(1)}, f32[14,64,128]{2,1,0:T(8,128)S(1)}, u32[]{:S(2)}, u32[]{:S(2)}) collective-permute-start(f32[14,64,128]{2,1,0:T(8,128)S(1)} %get-tuple-element.48), channel_id=1, source_target_pairs={{0,16},{16,0},{1,17},{17,1},{2,18},{18,2},{3,19},{19,3},{4,20},{20... | collective-permute-start | bytes 1376264 | tf_op jit(solution)/shard_map/ppermute | solution.py:478
  6.3 1.3 %collective-permute-start.1 = (f32[2,2,2,8,128]{4,3,2,1,0:T(8,128)S(1)}, f32[2,2,2,8,128]{4,3,2,1,0:T(8,128)S(1)}, u32[]{:S(2)}, u32[]{:S(2)}) collective-permute-start(f32[2,2,2,8,128]{4,3,2,1,0:T(8,128)S(1)} %get-tuple-element.50), channel_id=1, source_target_pairs={{0,1},{1,0},{2,3},{3,2},{4,5},{5,4},{6,7},{7,6},{8,9},{9,8},{10,11... | collective-permute-start | bytes 98312 | tf_op jit(solution)/shard_map/ppermute | solution.py:446
  6.4 1.2 %collective-permute-start.2 = (f32[2,2,2,8,128]{4,3,2,1,0:T(8,128)S(1)}, f32[2,2,2,8,128]{4,3,2,1,0:T(8,128)S(1)}, u32[]{:S(2)}, u32[]{:S(2)}) collective-permute-start(f32[2,2,2,8,128]{4,3,2,1,0:T(8,128)S(1)} %get-tuple-element.51), channel_id=1, source_target_pairs={{1,2},{2,1},{5,6},{6,5},{9,10},{10,9},{13,14},{14,13},{17,18},{18,... | collective-permute-start | bytes 98312 | tf_op jit(solution)/shard_map/ppermute | solution.py:481
  7.7 5.6 %collective-permute-start.3 = (f32[2,2,88,128]{3,2,1,0:T(8,128)S(1)}, f32[2,2,88,128]{3,2,1,0:T(8,128)S(1)}, u32[]{:S(2)}, u32[]{:S(2)}) collective-permute-start(f32[2,2,88,128]{3,2,1,0:T(8,128)S(1)} %get-tuple-element.53), channel_id=1, source_target_pairs={{0,4},{4,0},{8,12},{12,8},{1,5},{5,1},{9,13},{13,9},{2,6},{6,2},{1... | collective-permute-start | bytes 540680 | tf_op jit(solution)/shard_map/ppermute | solution.py:438
  9.4 9.2 %collective-permute-start.4 = (f32[2,2,88,128]{3,2,1,0:T(8,128)S(1)}, f32[2,2,88,128]{3,2,1,0:T(8,128)S(1)}, u32[]{:S(2)}, u32[]{:S(2)}) collective-permute-start(f32[2,2,88,128]{3,2,1,0:T(8,128)S(1)} %get-tuple-element.54), channel_id=1, source_target_pairs={{0,8},{4,12},{8,0},{12,4},{1,9},{5,13},{9,1},{13,5},{2,10},{6,14},... | collective-permute-start | bytes 540680 | tf_op jit(solution)/shard_map/ppermute | solution.py:438
  12.0 9.2 %collective-permute-start.5 = (f32[2,2,88,128]{3,2,1,0:T(8,128)S(1)}, f32[2,2,88,128]{3,2,1,0:T(8,128)S(1)}, u32[]{:S(2)}, u32[]{:S(2)}) collective-permute-start(f32[2,2,88,128]{3,2,1,0:T(8,128)S(1)} %get-tuple-element.55), channel_id=1, source_target_pairs={{0,12},{4,8},{8,4},{12,0},{1,13},{5,9},{9,5},{13,1},{2,14},{6,10},... | collective-permute-start | bytes 540680 | tf_op jit(solution)/shard_map/ppermute | solution.py:438
  21.2 7.2 %collective-permute-start.6 = (f32[14,64,128]{2,1,0:T(8,128)S(1)}, f32[14,64,128]{2,1,0:T(8,128)S(1)}, u32[]{:S(2)}, u32[]{:S(2)}) collective-permute-start(f32[14,64,128]{2,1,0:T(8,128)S(1)} %collective-permute-done.refs_0_), channel_id=1, source_target_pairs={{0,1},{1,0},{2,3},{3,2},{4,5},{5,4},{6,7},{7,6},{8,9},{9,8},{10,11... | collective-permute-start | bytes 1376264 | tf_op jit(solution)/shard_map/ppermute | solution.py:446
  41.7 1.9 %collective-permute-start.7 = (f32[896,128]{1,0:T(8,128)S(1)}, f32[896,128]{1,0:T(8,128)S(1)}, u32[]{:S(2)}, u32[]{:S(2)}) collective-permute-start(f32[896,128]{1,0:T(8,128)S(1)} %bitcast.9), channel_id=1, source_target_pairs={{0,1},{1,0},{2,3},{3,2},{4,5},{5,4},{6,7},{7,6},{8,9},{9,8},{10,11... | collective-permute-start | bytes 1376264 | tf_op jit(solution)/shard_map/ppermute | solution.py:446
  43.7 7.4 %collective-permute-start.10 = (f32[224,128]{1,0:T(8,128)S(1)}, f32[224,128]{1,0:T(8,128)S(1)}, u32[]{:S(2)}, u32[]{:S(2)}) collective-permute-start(f32[224,128]{1,0:T(8,128)S(1)} %get-tuple-element.91), channel_id=1, source_target_pairs={{0,6},{1,7},{2,4},{3,5},{4,2},{5,3},{6,0},{7,1},{8,14},{9,15},{10,... | collective-permute-start | bytes 344072 | tf_op jit(solution)/shard_map/ppermute | solution.py:455
  47.0 7.5 %collective-permute-start.8 = (f32[224,128]{1,0:T(8,128)S(1)}, f32[224,128]{1,0:T(8,128)S(1)}, u32[]{:S(2)}, u32[]{:S(2)}) collective-permute-start(f32[224,128]{1,0:T(8,128)S(1)} %get-tuple-element.92), channel_id=1, source_target_pairs={{0,4},{4,0},{8,12},{12,8},{1,5},{5,1},{9,13},{13,9},{2,6},{6,2},{1... | collective-permute-start | bytes 344072 | tf_op jit(solution)/shard_map/ppermute | solution.py:446
  47.0 7.5 %collective-permute-start.9 = (f32[224,128]{1,0:T(8,128)S(1)}, f32[224,128]{1,0:T(8,128)S(1)}, u32[]{:S(2)}, u32[]{:S(2)}) collective-permute-start(f32[224,128]{1,0:T(8,128)S(1)} %get-tuple-element.90), channel_id=1, source_target_pairs={{0,2},{1,3},{2,0},{3,1},{4,6},{5,7},{6,4},{7,5},{8,10},{9,11},{10,... | collective-permute-start | bytes 344072 | tf_op jit(solution)/shard_map/ppermute | solution.py:446
  48.0 10.3 %collective-permute-start.11 = (f32[2,2,2,32,128]{4,3,2,1,0:T(8,128)S(1)}, f32[2,2,2,32,128]{4,3,2,1,0:T(8,128)S(1)}, u32[]{:S(2)}, u32[]{:S(2)}) collective-permute-start(f32[2,2,2,32,128]{4,3,2,1,0:T(8,128)S(1)} %get-tuple-element.76), channel_id=1, source_target_pairs={{0,4},{4,0},{8,12},{12,8},{1,5},{5,1},{9,13},{13,9},{2,6},{6,2},{1... | collective-permute-start | bytes 393224 | tf_op jit(solution)/shard_map/ppermute | solution.py:438
  50.0 8.6 %collective-permute-start.12 = (f32[2,2,2,32,128]{4,3,2,1,0:T(8,128)S(1)}, f32[2,2,2,32,128]{4,3,2,1,0:T(8,128)S(1)}, u32[]{:S(2)}, u32[]{:S(2)}) collective-permute-start(f32[2,2,2,32,128]{4,3,2,1,0:T(8,128)S(1)} %get-tuple-element.77), channel_id=1, source_target_pairs={{0,8},{4,12},{8,0},{12,4},{1,9},{5,13},{9,1},{13,5},{2,10},{6,14},... | collective-permute-start | bytes 393224 | tf_op jit(solution)/shard_map/ppermute | solution.py:438
  51.1 12.6 %collective-permute-start.13 = (f32[2,2,2,32,128]{4,3,2,1,0:T(8,128)S(1)}, f32[2,2,2,32,128]{4,3,2,1,0:T(8,128)S(1)}, u32[]{:S(2)}, u32[]{:S(2)}) collective-permute-start(f32[2,2,2,32,128]{4,3,2,1,0:T(8,128)S(1)} %get-tuple-element.78), channel_id=1, source_target_pairs={{0,12},{4,8},{8,4},{12,0},{1,13},{5,9},{9,5},{13,1},{2,14},{6,10},... | collective-permute-start | bytes 393224 | tf_op jit(solution)/shard_map/ppermute | solution.py:438
  63.7 6.9 %collective-permute-start.14 = (f32[224,128]{1,0:T(8,128)S(1)}, f32[224,128]{1,0:T(8,128)S(1)}, u32[]{:S(2)}, u32[]{:S(2)}) collective-permute-start(f32[224,128]{1,0:T(8,128)S(1)} %add_add_fusion), channel_id=1, source_target_pairs={{0,8},{4,12},{8,0},{12,4},{1,9},{5,13},{9,1},{13,5},{2,10},{6,14},... | collective-permute-start | bytes 344072 | tf_op jit(solution)/shard_map/ppermute | solution.py:446
  70.6 6.1 %collective-permute-start.17 = (f32[224,128]{1,0:T(8,128)S(1)}, f32[224,128]{1,0:T(8,128)S(1)}, u32[]{:S(2)}, u32[]{:S(2)}) collective-permute-start(f32[224,128]{1,0:T(8,128)S(1)} %add.24), channel_id=1, source_target_pairs={{0,6},{1,7},{2,4},{3,5},{4,2},{5,3},{6,0},{7,1},{8,14},{9,15},{10,... | collective-permute-start | bytes 344072 | tf_op jit(solution)/shard_map/ppermute | solution.py:455
  70.7 6.1 %collective-permute-start.16 = (f32[224,128]{1,0:T(8,128)S(1)}, f32[224,128]{1,0:T(8,128)S(1)}, u32[]{:S(2)}, u32[]{:S(2)}) collective-permute-start(f32[224,128]{1,0:T(8,128)S(1)} %add.24), channel_id=1, source_target_pairs={{0,2},{1,3},{2,0},{3,1},{4,6},{5,7},{6,4},{7,5},{8,10},{9,11},{10,... | collective-permute-start | bytes 344072 | tf_op jit(solution)/shard_map/ppermute | solution.py:446
  72.2 5.8 %collective-permute-start.15 = (f32[224,128]{1,0:T(8,128)S(1)}, f32[224,128]{1,0:T(8,128)S(1)}, u32[]{:S(2)}, u32[]{:S(2)}) collective-permute-start(f32[224,128]{1,0:T(8,128)S(1)} %add.24), channel_id=1, source_target_pairs={{0,4},{4,0},{8,12},{12,8},{1,5},{5,1},{9,13},{13,9},{2,6},{6,2},{1... | collective-permute-start | bytes 344072 | tf_op jit(solution)/shard_map/ppermute | solution.py:446
  78.0 1.9 %collective-permute-start.18 = (f32[896,128]{1,0:T(8,128)S(1)}, f32[896,128]{1,0:T(8,128)S(1)}, u32[]{:S(2)}, u32[]{:S(2)}) collective-permute-start(f32[896,128]{1,0:T(8,128)S(1)} %pad_maximum_fusion.near), channel_id=1, source_target_pairs={{0,1},{1,0},{2,3},{3,2},{4,5},{5,4},{6,7},{7,6},{8,9},{9,8},{10,11... | collective-permute-start | bytes 1376264 | tf_op jit(solution)/shard_map/ppermute | solution.py:446

commit v8 on v7

--- a/solution.py
+++ b/solution.py
@@ -55,22 +55,59 @@
         sent[index] = own[start + index]
 
 
+def turned_rows(dims, source, micro, y):
+    _, chans, size_x, local_y, _ = dims
+    step = size_x * local_y
+    first = micro * chans * step + y
+    parts = [source[pl.ds(first + x * local_y, chans, stride=step), :] for x in range(size_x)]
+    return jnp.concatenate(parts, axis=0).T
+
+
 def turn_kernel(dims, inflow, cotangent, rows, pair, inner):
-    micros, chans, size_x, local_y, local_z = dims
-    step = size_x * local_y
+    micros, _, _, local_y, local_z = dims
     odd = lax.axis_index("gz") % 2 == 1
     for field, source in enumerate((inflow, cotangent)):
         for micro in range(micros):
             for y in range(local_y):
-                first = micro * chans * step + y
-                parts = [
-                    source[pl.ds(first + x * local_y, chans, stride=step), :] for x in range(size_x)
-                ]
-                turned = jnp.concatenate(parts, axis=0).T
+                turned = turned_rows(dims, source, micro, y)
                 rows[field, micro, y] = turned
                 low, high = turned[:HALO], turned[local_z - HALO :]
                 pair[field, micro, y] = jnp.where(odd, low, high)
                 inner[field, micro, y] = jnp.where(odd, high, low)
+
+
+def cut_kernel(dims, slabs, width, inflow, cotangent, *refs):
+    micros, _, _, local_y, local_z = dims
+    outs, wide = refs[:-1], refs[-1]
+    slab = lax.axis_index("gy")
+    for field, (source, halo) in enumerate(zip((inflow, cotangent), HALOS)):
+        at = slice(0, width + 2 * halo) if field == 0 else slice(width + 2 * HALO, None)
+        for micro in range(micros):
+            for y in range(local_y):
+                wide[field, micro, y, :HALO] = jnp.zeros((HALO, LANES), F32)
+                wide[field, micro, y, HALO + local_z :] = jnp.zeros((HALO, LANES), F32)
+                turned = turned_rows(dims, source, micro, y)
+                wide[field, micro, y, HALO : HALO + local_z] = turned
+                for turn in range(slabs):
+                    start = (slab ^ turn) * width + HALO - halo
+                    if width % 8 == 0 and halo % 8 == 0:
+                        start = pl.multiple_of(start, 8)
+                    outs[turn][micro, y, at] = wide[field, micro, y, pl.ds(start, width + 2 * halo)]
+
+
+def edge_kernel(width, *refs):
+    windows, edge = refs[:-1], refs[-1]
+    slab = lax.axis_index("gy")
+    micros, local_y = windows[0].shape[:2]
+    for field, halo in enumerate(HALOS):
+        base = halo if field == 0 else width + 2 * HALO + halo
+        for turn, window in enumerate(windows):
+            owner = slab ^ turn
+            for micro in range(micros):
+                for y in range(local_y):
+                    low = window[micro, y, base : base + HALO]
+                    high = window[micro, y, base + width - HALO : base + width]
+                    edge[field, micro, owner * local_y + y] = jnp.where(slab == 0, low, high)
 
 
 def window_kernel(dims, rows, pair, inner, *refs):
@@ -128,38 +165,6 @@
         row[layer] = jnp.broadcast_to(jnp.concatenate([part, part], axis=1), (8, LANES))
 
 
-def cut_kernel(dims, place, *refs):
-    micros, chans, size_x, local_y, local_z, slabs, width, span, edged, fields = dims
-    sources, refs = refs[:fields], refs[fields:]
-    outs, wide = refs[:-1], refs[-1]
-    slab = place[1]
-    step = size_x * local_y
-    for field, source in enumerate(sources):
-        windows = outs[field * slabs : (field + 1) * slabs]
-        edges = outs[fields * slabs :]
-        for micro in range(micros):
-            for y in range(local_y):
-                first = micro * chans * step + y
-                parts = [
-                    source[pl.ds(first + x * local_y, chans, stride=step), :] for x in range(size_x)
-                ]
-                wide[field, micro, y, HALO : HALO + local_z] = jnp.concatenate(parts, axis=0).T
-                wide[field, micro, y, :HALO] = jnp.zeros((HALO, LANES), F32)
-                wide[field, micro, y, HALO + local_z :] = jnp.zeros((HALO, LANES), F32)
-                if edged:
-                    for turn in range(slabs):
-                        start = lax.rem(slab + turn, slabs) * width
-                        if width % 8 == 0:
-                            start = pl.multiple_of(start, 8)
-                        windows[turn][micro, y] = wide[field, micro, y, pl.ds(start, span)]
-                    low = wide[field, micro, y, local_z : local_z + HALO]
-                    high = wide[field, micro, y, HALO : 2 * HALO]
-                    for m in range(slabs):
-                        edges[m][field, micro, y] = jnp.where(slab == m, low, high)
-                else:
-                    windows[0][micro, y] = wide[field, micro, y, HALO : HALO + local_z]
-
-
 class Slab:
     def __init__(self, dims):
         self.micros, self.rows_y, self.depth, self.width, self.chunk_y, self.slabs, limit_z = dims
@@ -223,7 +228,7 @@
                 for edge in (0, self.rows_y + 1):
                     target[lead, micro, edge * self.depth : (edge + 1) * self.depth, :] = blank
 
-    def fill(self, field, windows, which):
+    def fill(self, field, windows, which, edge):
         halo = HALOS[which]
         span = self.width + 2 * halo
         at = 0 if which == 0 else self.width + 2 * HALO
@@ -238,22 +243,36 @@
                     start = pl.multiple_of((owner * self.per_owner + y) * self.depth, 16)
                     value = jnp.concatenate(parts, axis=0) if len(parts) > 1 else parts[0]
                     field[micro, pl.ds(start, self.depth), :] = value
-
-    def cut_out(self, targets, slot, source):
+        if edge is None:
+            return
+        for side, rows, at in (
+            (0, slice(HALO - halo, HALO), HALO - halo),
+            (self.slabs - 1, slice(0, halo), HALO + self.width),
+        ):
+
+            @pl.when(self.slab == side)
+            def _():
+                for micro in range(self.micros):
+                    for y in range(self.rows_y):
+                        start = y * self.depth + at
+                        field[micro, start : start + halo, :] = edge[which, micro, y, rows]
+
+    def cut_out(self, targets, source):
         for turn, target in enumerate(targets):
             owner = self.slab ^ turn
             for micro in range(self.micros):
                 for y in range(self.per_owner):
                     start = (owner * self.per_owner + y) * self.depth + HALO
                     rows = pl.ds(pl.multiple_of(start, 8), self.width)
-                    target[slot, micro, y] = source[micro, rows, :]
-
-
-def forward_kernel(dims, own, own_row, other, other_row, *refs):
+                    target[micro, y] = source[micro, rows, :]
+
+
+def forward_kernel(dims, edged, own, own_row, other, other_row, *refs):
     slab = Slab(dims)
-    windows, (acts, kept, front, field) = refs[:-4], refs[-4:]
+    windows, (*edge, acts, kept) = refs[: slab.slabs], refs[slab.slabs : slab.slabs + edged + 2]
+    outs, (whole, field) = refs[slab.slabs + edged + 2 : -2], refs[-2:]
     slab.blank_edges(acts)
-    slab.fill(field, windows, 0)
+    slab.fill(field, windows, 0, edge[0] if edged else None)
 
     def take_in(start):
         for micro in range(slab.micros):
@@ -268,19 +287,19 @@
             def body(start):
                 at = pl.ds(start, slab.chunk)
                 sums = slab.conv(acts, layer, start, table.at[half])
-                outs = []
+                values = []
                 for micro, total in enumerate(sums):
                     pre = total + row[half][0:1, :]
                     sigma = 1.0 / (1.0 + jnp.exp(-pre))
                     kept[layer, micro, at, :] = sigma * (1.0 + pre * (1.0 - sigma))
                     out = slab.masked(pre * sigma, slab.in_grid)
                     slab.put_rows(acts, layer + 1, micro, start, out)
-                    outs.append(out)
+                    values.append(out)
 
                 @pl.when(layer == 2 * slab.section + 1)
                 def _():
-                    for micro, out in enumerate(outs):
-                        front[micro, at, :] = out
+                    for micro, value in enumerate(values):
+                        whole[micro, at, :] = value
 
             slab.over_chunks(body)
 
@@ -288,15 +307,16 @@
         return carry
 
     lax.fori_loop(0, 4, layer_step, 0)
-
-
-def backward_kernel(dims, scale, own, other, acts, kept, front, *refs):
+    slab.cut_out(outs, whole)
+
+
+def backward_kernel(dims, edged, scale, own, other, acts, kept, *refs):
     slab = Slab(dims)
     windows, refs = refs[: slab.slabs], refs[slab.slabs :]
+    edge, refs = refs[:edged], refs[edged:]
     outs, (sums, rim, slopes, field, acc) = refs[: slab.slabs], refs[slab.slabs :]
     slab.blank_edges(rim)
-    slab.cut_out(outs, 0, front)
-    slab.fill(field, windows, 1)
+    slab.fill(field, windows, 1, edge[0] if edged else None)
 
     def take_gradient(layer, micro, start, gradient):
         at = pl.ds(start, slab.chunk)
@@ -334,7 +354,7 @@
         return carry
 
     lax.fori_loop(0, jnp.where(slab.section == 0, 4, 2), layer_step, 0)
-    slab.cut_out(outs, 1, field)
+    slab.cut_out(outs, field)
 
     quarter = BLOCKS // 4
     chans = LANES // 2
@@ -414,14 +434,16 @@
     pieces, (*targets, whole) = refs[:-3], refs[-3:]
     slab = lax.axis_index("gy")
     step = size_x * local_y
+    slabs = len(pieces) // 2
     for slot, target in enumerate(targets):
         for micro in range(micros):
             for y in range(local_y):
-                for turn, piece in enumerate(pieces):
+                for turn in range(slabs):
                     start = (slab ^ turn) * width
                     if width % 8 == 0:
                         start = pl.multiple_of(start, 8)
-                    whole[slot, micro, y, pl.ds(start, width), :] = piece[slot, micro, y]
+                    rows = pl.ds(start, width)
+                    whole[slot, micro, y, rows, :] = pieces[slot * slabs + turn][micro, y]
                 block = whole[slot, micro, y].T
                 for x in range(size_x):
                     first = micro * chans * step + x * local_y + y
@@ -466,67 +488,81 @@
     chunk_y = max(n for n in range(1, rows_y + 1) if rows_y % n == 0 and n * depth <= 384)
     scale = 1.0 / math.sqrt(micros * size_x * rows_y * local_z * columns)
     rows = micros * chans * size_x * local_y
-    ends = ((2, micros, local_y, HALO, LANES), F32)
+    blocks = [inflow.reshape(rows, local_z), cotangent.reshape(rows, local_z)]
     packs = [((BLOCKS, chans, LANES), F32), ((BLOCKS // 2, chans, LANES), F32)]
     own, sent = call(pack_kernel, "pack", packs, [weights, biases])
-    fields, pair, inner = call(
-        functools.partial(turn_kernel, inflow.shape),
-        "turn",
-        [((2, micros, local_y, local_z, LANES), F32), ends, ends],
-        [inflow.reshape(rows, local_z), cotangent.reshape(rows, local_z)],
-    )
     near_half = lax.ppermute(sent, "section", [(0, 1), (1, 0)])
-    pair = swapped(pair, 1)
-    route = [(i, i + 1) for i in range(1, columns - 1, 2)]
-    inner = lax.ppermute(inner, "gz", route + [(after, before) for before, after in route])
     reach = sum(width + 2 * halo for halo in HALOS)
-    windows = call(
-        functools.partial(window_kernel, (slabs, width, columns)),
-        "windows",
-        [((micros, local_y, reach, LANES), F32)] * slabs,
-        [fields, pair, inner],
-        [pltpu.VMEM((2, micros, local_y, local_z + 2 * HALO, LANES), F32)],
-    )
+    cuts = [((micros, local_y, reach, LANES), F32)] * slabs
+    wide = pltpu.VMEM((2, micros, local_y, local_z + 2 * HALO, LANES), F32)
+    edged = width >= HALO and slabs > 1
+    if edged:
+        kernel = functools.partial(cut_kernel, inflow.shape, slabs, width)
+        windows = call(kernel, "cut", cuts, blocks, [wide])
+    else:
+        ends = ((2, micros, local_y, HALO, LANES), F32)
+        kernel = functools.partial(turn_kernel, inflow.shape)
+        whole = ((2, micros, local_y, local_z, LANES), F32)
+        fields, pair, inner = call(kernel, "turn", [whole, ends, ends], blocks)
+        pair = swapped(pair, 1)
+        route = [(i, i + 1) for i in range(1, columns - 1, 2)]
+        inner = lax.ppermute(inner, "gz", route + [(after, before) for before, after in route])
+        kernel = functools.partial(window_kernel, (slabs, width, columns))
+        windows = call(kernel, "windows", cuts, [fields, pair, inner], [wide])
     windows = spread(windows)
-    near_half, windows = lax.optimization_barrier((near_half, windows))
-    far_half = swapped(near_half, 1)
 
     tables = [((2, 9 * LANES, 3 * LANES), BF16)] * 2 + [((2, 8, LANES), F32)]
     own_fwd, own_bwd, own_row = call(table_kernel, "own_table", tables, [own])
+    near_half, windows, own_row = lax.optimization_barrier((near_half, windows, own_row))
+    edges = []
+    if edged:
+        edge = ((2, micros, rows_y, HALO, LANES), F32)
+        edges = call(functools.partial(edge_kernel, width), "edge", [edge], windows)
+        last = (slabs - 1) * columns
+        route = [(g, last + g - 1) for g in range(1, columns)]
+        route += [(after, before) for before, after in route]
+        edges = [lax.ppermute(edges[0], ("gy", "gz"), route)]
+    far_half = swapped(near_half, 1)
     far_fwd, far_bwd, far_row = call(table_kernel, "far_table", tables, [near_half, far_half])
 
     dims = (micros, rows_y, depth, width, chunk_y, slabs, local_z * columns)
     padded = (rows_y + 2) * depth
     full = rows_y * depth
-    acts, kept, front = call(
-        functools.partial(forward_kernel, dims),
+    piece = ((micros, local_y, width, LANES), F32)
+    acts, kept, *fronts = call(
+        functools.partial(forward_kernel, dims, edged),
         "forward",
-        [
-            ((5, micros, padded, 2 * LANES), BF16),
-            ((4, micros, full, LANES), F32),
-            ((micros, full, LANES), F32),
-        ],
-        [own_fwd, own_row, far_fwd, far_row, *windows],
-        [pltpu.VMEM((micros, full, LANES), F32)],
+        [((5, micros, padded, 2 * LANES), BF16), ((4, micros, full, LANES), F32)] + [piece] * slabs,
+        [own_fwd, own_row, far_fwd, far_row, *windows, *edges],
+        [pltpu.VMEM((micros, full, LANES), F32)] * 2,
     )
-    *outs, sums = call(
-        functools.partial(backward_kernel, dims, scale),
+    if slabs == 4:
+        passed = swapped(jnp.stack(fronts[2:]), 2, "gy")
+    *backs, sums = call(
+        functools.partial(backward_kernel, dims, edged, scale),
         "backward",
-        [((2, micros, local_y, width, LANES), F32)] * slabs + [((BLOCKS, chans, LANES), F32)],
-        [own_bwd, far_bwd, acts, kept, front, *windows],
+        [piece] * slabs + [((BLOCKS, chans, LANES), F32)],
+        [own_bwd, far_bwd, acts, kept, *windows, *edges],
         [
             pltpu.VMEM((2, micros, padded, 2 * LANES), BF16),
             pltpu.VMEM((4, micros, full, LANES), F32),
             pltpu.VMEM((micros, full, LANES), F32),
             pltpu.VMEM((3 * LANES + 8, 3 * LANES), F32),
         ],
+        12 * micros * full * 9 * LANES * 3 * LANES,
     )
+    if slabs == 4:
+        sums, passed = lax.optimization_barrier((sums, passed))
 
     block = sums.reshape(BLOCKS * chans, LANES)
     half = block.shape[0] // 2
     block = block[:half] + swapped(block[half:], 1)
-    block, outs = lax.optimization_barrier((block, outs))
-    outs = spread(outs)
+    block, fronts, backs = lax.optimization_barrier((block, fronts, backs))
+    if slabs == 4:
+        near = swapped(jnp.stack([fronts[1], passed[1], backs[1]]), 1, "gy")
+        outs = [near, swapped(backs[2], 2, "gy"), swapped(backs[3], 3, "gy")]
+    else:
+        outs = spread([jnp.stack(pair) for pair in zip(fronts, backs)])
     part = half // 4
     odd = lax.axis_index("gy") % 2 == 1
     lows, highs = [block[i * part : (i + 1) * part] for i in (0, 2)], [
@@ -540,6 +576,10 @@
     while bit < slabs:
         kept = kept + swapped(kept, bit, "gy")
         bit *= 2
+    if slabs == 4:
+        outs = [fronts[0], outs[0][0], passed[0], outs[0][1], backs[0], outs[0][2], *outs[1:]]
+    else:
+        outs = [out[slot] for slot in range(2) for out in outs]
     near = jnp.concatenate([kept, *around(kept, kept, kept)], axis=0)
     core = swapped(near, 1)
     section_out, section_grad = call(

time: 81.6 us -> 85.2 us (1.044)
  waiting for transfers between devices: 31.5 us -> 35.7 us
    ppermute x9 -> x12, waiting for transfers between devices: 10.8 us -> 19.6 us  [swapped(): lax.ppermute(block, axis, [(i, i ^ bit) for i in range(lax.axis_size(axis...]
    ppermute x6 -> x3, waiting for transfers between devices: 18.2 us -> 12.6 us  [spread(): got.append(lax.ppermute(blocks[turn], 'gy', route))]
    ppermute x6 -> x3, starting transfers between devices: 9.67 us -> 4.45 us  [spread(): got.append(lax.ppermute(blocks[turn], 'gy', route))]
    ppermute x9 -> x12, starting transfers between devices: 13 us -> 17.6 us  [swapped(): lax.ppermute(block, axis, [(i, i ^ bit) for i in range(lax.axis_size(axis...]
    ppermute x2, waiting for transfers between devices: 2.54 us -> 3.39 us  [around(): across = lax.ppermute(across, ('gy', 'gz'), route)]
  transfers between devices with their start and end apart: 19 -> 19, of which waited for: 15 -> 11; matrix products, arithmetic and copies ran while one was open for 0% -> 0% of each run, Pallas kernels for 2% -> 12%
where the time goes in v8:
time: 85.2 us; the launch traced here: 85 us
  waiting for transfers between devices  35.7 us (42%)
  starting transfers between devices  29.1 us (34%)
  Pallas kernels  17 us (20%)
  local copies, waits for them, and re-layouts  2.27 us (3%)
    ppermute x12, waiting for transfers between devices, swapped(): lax.ppermute(block, axis, [(i, i ^ bit) for i in range(lax.axis_size(axis...  19.6 us
    ppermute x12, starting transfers between devices, swapped(): lax.ppermute(block, axis, [(i, i ^ bit) for i in range(lax.axis_size(axis...  17.6 us
    pallas_call x9, Pallas kernels, call(): pl.pallas_call(kernel, out_shape=arrays, in_specs=[VMEM] * len(args), out...  17 us
    ppermute x3, waiting for transfers between devices, spread(): got.append(lax.ppermute(blocks[turn], 'gy', route))  12.6 us
    ppermute x3, starting transfers between devices, spread(): got.append(lax.ppermute(blocks[turn], 'gy', route))  4.45 us
    ppermute x2, starting transfers between devices, around(): across = lax.ppermute(across, ('gy', 'gz'), route)  3.45 us
    ppermute x2, waiting for transfers between devices, around(): across = lax.ppermute(across, ('gy', 'gz'), route)  3.39 us
    ppermute x1, starting transfers between devices, per_device(): near_half = lax.ppermute(sent, 'section', [(0, 1), (1, 0)])  3 us
  transfers between devices with their start and end apart: 19, of which 11 were waited for; matrix products, arithmetic and copies ran while one was open for 0% of the time, Pallas kernels for 12%

profile of v8, /device:TPU:0, one launch (start us, length us, event | category | flops | bytes accessed | tf_op | source)
XLA Modules:
  0.0 85.0 jit_solution(17308291822514086779)
XLA Ops:
  0.6 0.0 copy-start
  0.6 1.5 %copy-done = f32[2,27,64,64]{3,2,1,0:T(8,128)S(1)} copy-done((f32[2,27,64,64]{3,2,1,0:T(8,128)S(1)}, f32[2,27,64,64]{3,2,1,0:T(8,128)}, u32[]{:S(2)}) %copy-start) | copy-done | bytes 884760
  2.1 0.0 copy-start.3
  2.1 0.7 copy-done.3
  2.8 0.0 copy-start.1
  2.8 0.0 copy-start.2
  2.8 0.3 pack.1
  3.1 3.0 %collective-permute-start = (f32[14,64,128]{2,1,0:T(8,128)S(1)}, f32[14,64,128]{2,1,0:T(8,128)S(1)}, u32[]{:S(2)}, u32[]{:S(2)}) collective-permute-start(f32[14,64,128]{2,1,0:T(8,128)S(1)} %get-tuple-element.52), channel_id=1, source_target_pairs={{0,16},{16,0},{1,17},{17,1},{2,18},{18,2},{3,19},{19,3},{4,20},{20... | collective-permute-start | bytes 1376264 | tf_op jit(solution)/shard_map/ppermute | solution.py:494
  6.1 0.0 copy-done.1
  6.1 0.0 copy-done.2
  6.1 0.2 cut.1
  6.4 1.6 %collective-permute-start.1 = (f32[2,2,88,128]{3,2,1,0:T(8,128)S(1)}, f32[2,2,88,128]{3,2,1,0:T(8,128)S(1)}, u32[]{:S(2)}, u32[]{:S(2)}) collective-permute-start(f32[2,2,88,128]{3,2,1,0:T(8,128)S(1)} %get-tuple-element.54), channel_id=1, source_target_pairs={{0,4},{4,0},{8,12},{12,8},{1,5},{5,1},{9,13},{13,9},{2,6},{6,2},{1... | collective-permute-start | bytes 540680 | tf_op jit(solution)/shard_map/ppermute | solution.py:460
  8.0 2.6 %collective-permute-start.2 = (f32[2,2,88,128]{3,2,1,0:T(8,128)S(1)}, f32[2,2,88,128]{3,2,1,0:T(8,128)S(1)}, u32[]{:S(2)}, u32[]{:S(2)}) collective-permute-start(f32[2,2,88,128]{3,2,1,0:T(8,128)S(1)} %get-tuple-element.55), channel_id=1, source_target_pairs={{0,8},{4,12},{8,0},{12,4},{1,9},{5,13},{9,1},{13,5},{2,10},{6,14},... | collective-permute-start | bytes 540680 | tf_op jit(solution)/shard_map/ppermute | solution.py:460
  10.6 0.2 collective-permute-start.3
  10.8 0.7 own_table.1
  11.5 3.7 %collective-permute-done.1.refs_1_ = f32[2,2,88,128]{3,2,1,0:T(8,128)S(1)} collective-permute-done((f32[2,2,88,128]{3,2,1,0:T(8,128)S(1)}, f32[2,2,88,128]{3,2,1,0:T(8,128)S(1)}, u32[]{:S(2)}, u32[]{:S(2)}) %collective-permute-start.1) | collective-permute-done | bytes 180256 | tf_op jit(solution)/shard_map/ppermute | solution.py:460
  15.2 8.9 %collective-permute-done.2.refs_2_ = f32[2,2,88,128]{3,2,1,0:T(8,128)S(1)} collective-permute-done((f32[2,2,88,128]{3,2,1,0:T(8,128)S(1)}, f32[2,2,88,128]{3,2,1,0:T(8,128)S(1)}, u32[]{:S(2)}, u32[]{:S(2)}) %collective-permute-start.2) | collective-permute-done | bytes 180256 | tf_op jit(solution)/shard_map/ppermute | solution.py:460
  24.2 0.0 collective-permute-done.3.refs_3_
  24.2 0.0 collective-permute-done.refs_0_
  24.2 0.0 collective-permute-start.4
  24.2 0.7 collective-permute-start.5
  24.9 1.1 %collective-permute-done.4.refs_1_ = f32[14,64,128]{2,1,0:T(8,128)S(1)} collective-permute-done((f32[14,64,128]{2,1,0:T(8,128)S(1)}, f32[14,64,128]{2,1,0:T(8,128)S(1)}, u32[]{:S(2)}, u32[]{:S(2)}) %collective-permute-start.4) | collective-permute-done | bytes 458784 | tf_op jit(solution)/shard_map/ppermute | solution.py:468
  26.0 0.8 far_table.1
  26.7 0.0 collective-permute-done.5.refs_4_
  26.7 5.3 %forward.1 = (bf16[5,2,480,256]{3,2,1,0:T(8,128)(2,1)S(1)}, f32[4,2,384,128]{3,2,1,0:T(8,128)S(1)}, f32[2,2,32,128]{3,2,1,0:T(8,128)S(1)}, f32[2,2,32,128]{3,2,1...) custom-call(bf16[2,1152,384]{2,1,0:T(8,128)(2,1)S(1)} %get-tuple-element.60.own, ...), custom_call_target="tpu_custom_call" | custom-call | bytes 1024 | tf_op jit(solution)/shard_map/forward/pallas_call | solution.py:24
  32.1 3.8 %collective-permute-start.6 = (f32[2,2,2,32,128]{4,3,2,1,0:T(8,128)S(1)}, f32[2,2,2,32,128]{4,3,2,1,0:T(8,128)S(1)}, u32[]{:S(2)}, u32[]{:S(2)}) collective-permute-start(f32[2,2,2,32,128]{4,3,2,1,0:T(8,128)S(1)} %pad_maximum_fusion.2), channel_id=1, source_target_pairs={{0,8},{4,12},{8,0},{12,4},{1,9},{5,13},{9,1},{13,5},{2,10},{6,14},... | collective-permute-start | bytes 393224 | tf_op jit(solution)/shard_map/ppermute | solution.py:468
  35.9 7.1 %backward.1 = (f32[2,2,32,128]{3,2,1,0:T(8,128)S(1)}, f32[2,2,32,128]{3,2,1,0:T(8,128)S(1)}, f32[2,2,32,128]{3,2,1,0:T(8,128)S(1)}, f32[2,2,32,128]{3,2,1,0:T(8,128)S(1)}, f32[28,64,128]{2,1,0:T(8,128)S(1)}) custom-call(bf16[2,1152,384]{2,1,0:T(8,128)(2,1)S(1)} %get-tuple-element.51.own, bf16[2,1152,384]{2,1,0:T(8,128)(2,1)S(1)} %get-tuple-element.59.other, ...), custom_call_target="tpu_custom_call" | custom-call | flops 4076863488 | bytes 1024 | tf_op jit(solution)/shard_map/backward/pallas_call | solution.py:24
  43.0 0.0 collective-permute-done.6
  43.0 0.1 fusion
  43.1 3.5 %collective-permute-start.7 = (f32[896,128]{1,0:T(8,128)S(1)}, f32[896,128]{1,0:T(8,128)S(1)}, u32[]{:S(2)}, u32[]{:S(2)}) collective-permute-start(f32[896,128]{1,0:T(8,128)S(1)} %bitcast.25), channel_id=1, source_target_pairs={{0,1},{1,0},{2,3},{3,2},{4,5},{5,4},{6,7},{7,6},{8,9},{9,8},{10,11... | collective-permute-start | bytes 1376264 | tf_op jit(solution)/shard_map/ppermute | solution.py:468
  46.6 1.4 %collective-permute-done.7 = f32[896,128]{1,0:T(8,128)S(1)} collective-permute-done((f32[896,128]{1,0:T(8,128)S(1)}, f32[896,128]{1,0:T(8,128)S(1)}, u32[]{:S(2)}, u32[]{:S(2)}) %collective-permute-start.7) | collective-permute-done | bytes 458784 | tf_op jit(solution)/shard_map/ppermute | solution.py:468
  48.1 3.4 %collective-permute-start.10 = (f32[224,128]{1,0:T(8,128)S(1)}, f32[224,128]{1,0:T(8,128)S(1)}, u32[]{:S(2)}, u32[]{:S(2)}) collective-permute-start(f32[224,128]{1,0:T(8,128)S(1)} %get-tuple-element.99), channel_id=1, source_target_pairs={{0,6},{1,7},{2,4},{3,5},{4,2},{5,3},{6,0},{7,1},{8,14},{9,15},{10,... | collective-permute-start | bytes 344072 | tf_op jit(solution)/shard_map/ppermute | solution.py:477
  51.5 0.5 collective-permute-start.8
  52.0 0.8 collective-permute-start.9
  52.7 2.1 %collective-permute-start.11 = (f32[3,2,2,32,128]{4,3,2,1,0:T(8,128)S(1)}, f32[3,2,2,32,128]{4,3,2,1,0:T(8,128)S(1)}, u32[]{:S(2)}, u32[]{:S(2)}) collective-permute-start(f32[3,2,2,32,128]{4,3,2,1,0:T(8,128)S(1)} %pad_maximum_fusion.1), channel_id=1, source_target_pairs={{0,4},{4,0},{8,12},{12,8},{1,5},{5,1},{9,13},{13,9},{2,6},{6,2},{1... | collective-permute-start | bytes 589832 | tf_op jit(solution)/shard_map/ppermute | solution.py:468
  54.8 0.8 collective-permute-start.12
  55.6 0.0 collective-permute-done.10
  55.6 2.6 %collective-permute-start.13 = (f32[2,2,32,128]{3,2,1,0:T(8,128)S(1)}, f32[2,2,32,128]{3,2,1,0:T(8,128)S(1)}, u32[]{:S(2)}, u32[]{:S(2)}) collective-permute-start(f32[2,2,32,128]{3,2,1,0:T(8,128)S(1)} %get-tuple-element.86), channel_id=1, source_target_pairs={{0,12},{4,8},{8,4},{12,0},{1,13},{5,9},{9,5},{13,1},{2,14},{6,10},... | collective-permute-start | bytes 196616 | tf_op jit(solution)/shard_map/ppermute | solution.py:468
  58.2 0.9 %collective-permute-done.8 = f32[224,128]{1,0:T(8,128)S(1)} collective-permute-done((f32[224,128]{1,0:T(8,128)S(1)}, f32[224,128]{1,0:T(8,128)S(1)}, u32[]{:S(2)}, u32[]{:S(2)}) %collective-permute-start.8) | collective-permute-done | bytes 114720 | tf_op jit(solution)/shard_map/ppermute | solution.py:468
  59.1 0.0 collective-permute-done.9
  59.1 3.9 %collective-permute-done.12.refs_6_ = f32[2,2,32,128]{3,2,1,0:T(8,128)S(1)} collective-permute-done((f32[2,2,32,128]{3,2,1,0:T(8,128)S(1)}, f32[2,2,32,128]{3,2,1,0:T(8,128)S(1)}, u32[]{:S(2)}, u32[]{:S(2)}) %collective-permute-start.12) | collective-permute-done | bytes 65568 | tf_op jit(solution)/shard_map/ppermute | solution.py:468
  63.0 3.9 %collective-permute-done.13.refs_7_ = f32[2,2,32,128]{3,2,1,0:T(8,128)S(1)} collective-permute-done((f32[2,2,32,128]{3,2,1,0:T(8,128)S(1)}, f32[2,2,32,128]{3,2,1,0:T(8,128)S(1)}, u32[]{:S(2)}, u32[]{:S(2)}) %collective-permute-start.13) | collective-permute-done | bytes 65568 | tf_op jit(solution)/shard_map/ppermute | solution.py:468
  67.0 0.0 collective-permute-done.11
  67.0 0.0 collective-permute-start.14
  67.0 6.2 %collective-permute-done.14 = f32[224,128]{1,0:T(8,128)S(1)} collective-permute-done((f32[224,128]{1,0:T(8,128)S(1)}, f32[224,128]{1,0:T(8,128)S(1)}, u32[]{:S(2)}, u32[]{:S(2)}) %collective-permute-start.14) | collective-permute-done | bytes 114720 | tf_op jit(solution)/shard_map/ppermute | solution.py:468
  73.2 0.1 collective-permute-start.17
  73.3 1.5 %collective-permute-start.16 = (f32[224,128]{1,0:T(8,128)S(1)}, f32[224,128]{1,0:T(8,128)S(1)}, u32[]{:S(2)}, u32[]{:S(2)}) collective-permute-start(f32[224,128]{1,0:T(8,128)S(1)} %add.24), channel_id=1, source_target_pairs={{0,2},{1,3},{2,0},{3,1},{4,6},{5,7},{6,4},{7,5},{8,10},{9,11},{10,... | collective-permute-start | bytes 344072 | tf_op jit(solution)/shard_map/ppermute | solution.py:468
  74.8 2.0 %collective-permute-start.15 = (f32[224,128]{1,0:T(8,128)S(1)}, f32[224,128]{1,0:T(8,128)S(1)}, u32[]{:S(2)}, u32[]{:S(2)}) collective-permute-start(f32[224,128]{1,0:T(8,128)S(1)} %add.24), channel_id=1, source_target_pairs={{0,4},{4,0},{8,12},{12,8},{1,5},{5,1},{9,13},{13,9},{2,6},{6,2},{1... | collective-permute-start | bytes 344072 | tf_op jit(solution)/shard_map/ppermute | solution.py:468
  76.8 3.4 %collective-permute-done.17 = f32[224,128]{1,0:T(8,128)S(1)} collective-permute-done((f32[224,128]{1,0:T(8,128)S(1)}, f32[224,128]{1,0:T(8,128)S(1)}, u32[]{:S(2)}, u32[]{:S(2)}) %collective-permute-start.17) | collective-permute-done | bytes 114720 | tf_op jit(solution)/shard_map/ppermute | solution.py:477
  80.1 0.0 collective-permute-done.16
  80.1 1.4 %collective-permute-done.15 = f32[224,128]{1,0:T(8,128)S(1)} collective-permute-done((f32[224,128]{1,0:T(8,128)S(1)}, f32[224,128]{1,0:T(8,128)S(1)}, u32[]{:S(2)}, u32[]{:S(2)}) %collective-permute-start.15) | collective-permute-done | bytes 114720 | tf_op jit(solution)/shard_map/ppermute | solution.py:468
  81.6 0.1 collective-permute-start.18
  81.7 1.0 %restore.1 = (f32[512,128]{1,0:T(8,128)}, f32[512,128]{1,0:T(8,128)}) custom-call(f32[2,2,32,128]{3,2,1,0:T(8,128)S(1)} %get-tuple-element.80.refs_0_, f32[2,2,32,128]{3,2,1,0:T(8,128)S(1)} %get-tuple-element.103.refs_1_, f32[2,2,32,128]{3,2,1,0:T(8,128)S(1)} %get-tuple-element.104.refs_2_, f32[2,2,32,128]{3,2,1,0:T(8,128)S(1)} %get-tuple-element.102.refs_3_, ...), custom_call_target="tpu_custom_call" | custom-call | bytes 1024 | tf_op jit(solution)/shard_map/restore/pallas_call | solution.py:24
  82.6 0.8 collective-permute-done.18.core
  83.5 1.6 %unpack.1 = (f32[2,27,64,64]{3,2,1,0:T(8,128)}, f32[2,64]{1,0:T(2,128)}) custom-call(f32[896,128]{1,0:T(8,128)S(1)} %pad_maximum_fusion.near, f32[896,128]{1,0:T(8,128)S(1)} %collective-permute-done.18.core), custom_call_target="tpu_custom_call" | custom-call | bytes 1024 | tf_op jit(solution)/shard_map/unpack/pallas_call | solution.py:24
  (10 shorter events, 0.2 us)
Async XLA Ops:
  0.6 1.5 %copy-start = (f32[2,27,64,64]{3,2,1,0:T(8,128)S(1)}, f32[2,27,64,64]{3,2,1,0:T(8,128)}, u32[]{:S(2)}) copy-start(f32[2,27,64,64]{3,2,1,0:T(8,128)} %weights.1) | copy-start | bytes 2654212
  2.1 0.7 copy-start.3
  2.8 3.4 %copy-start.1 = (f32[2,64,2,2,128]{4,3,2,1,0:T(2,128)S(1)}, f32[2,64,2,2,128]{4,3,2,1,0:T(2,128)}, u32[]{:S(2)}) copy-start(f32[2,64,2,2,128]{4,3,2,1,0:T(2,128)} %param.4) | copy-start | bytes 786436
  2.8 3.4 %copy-start.2 = (f32[2,64,2,2,128]{4,3,2,1,0:T(2,128)S(1)}, f32[2,64,2,2,128]{4,3,2,1,0:T(2,128)}, u32[]{:S(2)}) copy-start(f32[2,64,2,2,128]{4,3,2,1,0:T(2,128)} %param.7) | copy-start | bytes 786436
  3.1 21.0 %collective-permute-start = (f32[14,64,128]{2,1,0:T(8,128)S(1)}, f32[14,64,128]{2,1,0:T(8,128)S(1)}, u32[]{:S(2)}, u32[]{:S(2)}) collective-permute-start(f32[14,64,128]{2,1,0:T(8,128)S(1)} %get-tuple-element.52), channel_id=1, source_target_pairs={{0,16},{16,0},{1,17},{17,1},{2,18},{18,2},{3,19},{19,3},{4,20},{20... | collective-permute-start | bytes 1376264 | tf_op jit(solution)/shard_map/ppermute | solution.py:494
  6.4 8.9 %collective-permute-start.1 = (f32[2,2,88,128]{3,2,1,0:T(8,128)S(1)}, f32[2,2,88,128]{3,2,1,0:T(8,128)S(1)}, u32[]{:S(2)}, u32[]{:S(2)}) collective-permute-start(f32[2,2,88,128]{3,2,1,0:T(8,128)S(1)} %get-tuple-element.54), channel_id=1, source_target_pairs={{0,4},{4,0},{8,12},{12,8},{1,5},{5,1},{9,13},{13,9},{2,6},{6,2},{1... | collective-permute-start | bytes 540680 | tf_op jit(solution)/shard_map/ppermute | solution.py:460
  8.0 16.1 %collective-permute-start.2 = (f32[2,2,88,128]{3,2,1,0:T(8,128)S(1)}, f32[2,2,88,128]{3,2,1,0:T(8,128)S(1)}, u32[]{:S(2)}, u32[]{:S(2)}) collective-permute-start(f32[2,2,88,128]{3,2,1,0:T(8,128)S(1)} %get-tuple-element.55), channel_id=1, source_target_pairs={{0,8},{4,12},{8,0},{12,4},{1,9},{5,13},{9,1},{13,5},{2,10},{6,14},... | collective-permute-start | bytes 540680 | tf_op jit(solution)/shard_map/ppermute | solution.py:460
  10.6 13.5 %collective-permute-start.3 = (f32[2,2,88,128]{3,2,1,0:T(8,128)S(1)}, f32[2,2,88,128]{3,2,1,0:T(8,128)S(1)}, u32[]{:S(2)}, u32[]{:S(2)}) collective-permute-start(f32[2,2,88,128]{3,2,1,0:T(8,128)S(1)} %get-tuple-element.56), channel_id=1, source_target_pairs={{0,12},{4,8},{8,4},{12,0},{1,13},{5,9},{9,5},{13,1},{2,14},{6,10},... | collective-permute-start | bytes 540680 | tf_op jit(solution)/shard_map/ppermute | solution.py:460
  24.2 1.8 %collective-permute-start.4 = (f32[14,64,128]{2,1,0:T(8,128)S(1)}, f32[14,64,128]{2,1,0:T(8,128)S(1)}, u32[]{:S(2)}, u32[]{:S(2)}) collective-permute-start(f32[14,64,128]{2,1,0:T(8,128)S(1)} %collective-permute-done.refs_0_), channel_id=1, source_target_pairs={{0,1},{1,0},{2,3},{3,2},{4,5},{5,4},{6,7},{7,6},{8,9},{9,8},{10,11... | collective-permute-start | bytes 1376264 | tf_op jit(solution)/shard_map/ppermute | solution.py:468
  24.2 2.5 %collective-permute-start.5 = (f32[2,2,8,8,128]{4,3,2,1,0:T(8,128)S(1)}, f32[2,2,8,8,128]{4,3,2,1,0:T(8,128)S(1)}, u32[]{:S(2)}, u32[]{:S(2)}) collective-permute-start(f32[2,2,8,8,128]{4,3,2,1,0:T(8,128)S(1)} %edge.1), channel_id=1, source_target_pairs={{1,12},{2,13},{3,14},{12,1},{13,2},{14,3},{17,28},{18,29},{19,30},... | collective-permute-start | bytes 393224 | tf_op jit(solution)/shard_map/ppermute | solution.py:524
  32.1 10.9 %collective-permute-start.6 = (f32[2,2,2,32,128]{4,3,2,1,0:T(8,128)S(1)}, f32[2,2,2,32,128]{4,3,2,1,0:T(8,128)S(1)}, u32[]{:S(2)}, u32[]{:S(2)}) collective-permute-start(f32[2,2,2,32,128]{4,3,2,1,0:T(8,128)S(1)} %pad_maximum_fusion.2), channel_id=1, source_target_pairs={{0,8},{4,12},{8,0},{12,4},{1,9},{5,13},{9,1},{13,5},{2,10},{6,14},... | collective-permute-start | bytes 393224 | tf_op jit(solution)/shard_map/ppermute | solution.py:468
  43.1 4.9 %collective-permute-start.7 = (f32[896,128]{1,0:T(8,128)S(1)}, f32[896,128]{1,0:T(8,128)S(1)}, u32[]{:S(2)}, u32[]{:S(2)}) collective-permute-start(f32[896,128]{1,0:T(8,128)S(1)} %bitcast.25), channel_id=1, source_target_pairs={{0,1},{1,0},{2,3},{3,2},{4,5},{5,4},{6,7},{7,6},{8,9},{9,8},{10,11... | collective-permute-start | bytes 1376264 | tf_op jit(solution)/shard_map/ppermute | solution.py:468
  48.1 7.5 %collective-permute-start.10 = (f32[224,128]{1,0:T(8,128)S(1)}, f32[224,128]{1,0:T(8,128)S(1)}, u32[]{:S(2)}, u32[]{:S(2)}) collective-permute-start(f32[224,128]{1,0:T(8,128)S(1)} %get-tuple-element.99), channel_id=1, source_target_pairs={{0,6},{1,7},{2,4},{3,5},{4,2},{5,3},{6,0},{7,1},{8,14},{9,15},{10,... | collective-permute-start | bytes 344072 | tf_op jit(solution)/shard_map/ppermute | solution.py:477
  51.5 7.6 %collective-permute-start.8 = (f32[224,128]{1,0:T(8,128)S(1)}, f32[224,128]{1,0:T(8,128)S(1)}, u32[]{:S(2)}, u32[]{:S(2)}) collective-permute-start(f32[224,128]{1,0:T(8,128)S(1)} %get-tuple-element.100), channel_id=1, source_target_pairs={{0,4},{4,0},{8,12},{12,8},{1,5},{5,1},{9,13},{13,9},{2,6},{6,2},{1... | collective-permute-start | bytes 344072 | tf_op jit(solution)/shard_map/ppermute | solution.py:468
  52.0 7.1 %collective-permute-start.9 = (f32[224,128]{1,0:T(8,128)S(1)}, f32[224,128]{1,0:T(8,128)S(1)}, u32[]{:S(2)}, u32[]{:S(2)}) collective-permute-start(f32[224,128]{1,0:T(8,128)S(1)} %get-tuple-element.98), channel_id=1, source_target_pairs={{0,2},{1,3},{2,0},{3,1},{4,6},{5,7},{6,4},{7,5},{8,10},{9,11},{10,... | collective-permute-start | bytes 344072 | tf_op jit(solution)/shard_map/ppermute | solution.py:468
  52.7 14.2 %collective-permute-start.11 = (f32[3,2,2,32,128]{4,3,2,1,0:T(8,128)S(1)}, f32[3,2,2,32,128]{4,3,2,1,0:T(8,128)S(1)}, u32[]{:S(2)}, u32[]{:S(2)}) collective-permute-start(f32[3,2,2,32,128]{4,3,2,1,0:T(8,128)S(1)} %pad_maximum_fusion.1), channel_id=1, source_target_pairs={{0,4},{4,0},{8,12},{12,8},{1,5},{5,1},{9,13},{13,9},{2,6},{6,2},{1... | collective-permute-start | bytes 589832 | tf_op jit(solution)/shard_map/ppermute | solution.py:468
  54.8 8.2 %collective-permute-start.12 = (f32[2,2,32,128]{3,2,1,0:T(8,128)S(1)}, f32[2,2,32,128]{3,2,1,0:T(8,128)S(1)}, u32[]{:S(2)}, u32[]{:S(2)}) collective-permute-start(f32[2,2,32,128]{3,2,1,0:T(8,128)S(1)} %get-tuple-element.85), channel_id=1, source_target_pairs={{0,8},{4,12},{8,0},{12,4},{1,9},{5,13},{9,1},{13,5},{2,10},{6,14},... | collective-permute-start | bytes 196616 | tf_op jit(solution)/shard_map/ppermute | solution.py:468
  55.6 11.3 %collective-permute-start.13 = (f32[2,2,32,128]{3,2,1,0:T(8,128)S(1)}, f32[2,2,32,128]{3,2,1,0:T(8,128)S(1)}, u32[]{:S(2)}, u32[]{:S(2)}) collective-permute-start(f32[2,2,32,128]{3,2,1,0:T(8,128)S(1)} %get-tuple-element.86), channel_id=1, source_target_pairs={{0,12},{4,8},{8,4},{12,0},{1,13},{5,9},{9,5},{13,1},{2,14},{6,10},... | collective-permute-start | bytes 196616 | tf_op jit(solution)/shard_map/ppermute | solution.py:468
  67.0 6.2 %collective-permute-start.14 = (f32[224,128]{1,0:T(8,128)S(1)}, f32[224,128]{1,0:T(8,128)S(1)}, u32[]{:S(2)}, u32[]{:S(2)}) collective-permute-start(f32[224,128]{1,0:T(8,128)S(1)} %add_add_fusion), channel_id=1, source_target_pairs={{0,8},{4,12},{8,0},{12,4},{1,9},{5,13},{9,1},{13,5},{2,10},{6,14},... | collective-permute-start | bytes 344072 | tf_op jit(solution)/shard_map/ppermute | solution.py:468
  73.2 6.9 %collective-permute-start.17 = (f32[224,128]{1,0:T(8,128)S(1)}, f32[224,128]{1,0:T(8,128)S(1)}, u32[]{:S(2)}, u32[]{:S(2)}) collective-permute-start(f32[224,128]{1,0:T(8,128)S(1)} %add.24), channel_id=1, source_target_pairs={{0,6},{1,7},{2,4},{3,5},{4,2},{5,3},{6,0},{7,1},{8,14},{9,15},{10,... | collective-permute-start | bytes 344072 | tf_op jit(solution)/shard_map/ppermute | solution.py:477
  73.3 6.9 %collective-permute-start.16 = (f32[224,128]{1,0:T(8,128)S(1)}, f32[224,128]{1,0:T(8,128)S(1)}, u32[]{:S(2)}, u32[]{:S(2)}) collective-permute-start(f32[224,128]{1,0:T(8,128)S(1)} %add.24), channel_id=1, source_target_pairs={{0,2},{1,3},{2,0},{3,1},{4,6},{5,7},{6,4},{7,5},{8,10},{9,11},{10,... | collective-permute-start | bytes 344072 | tf_op jit(solution)/shard_map/ppermute | solution.py:468
  74.8 6.8 %collective-permute-start.15 = (f32[224,128]{1,0:T(8,128)S(1)}, f32[224,128]{1,0:T(8,128)S(1)}, u32[]{:S(2)}, u32[]{:S(2)}) collective-permute-start(f32[224,128]{1,0:T(8,128)S(1)} %add.24), channel_id=1, source_target_pairs={{0,4},{4,0},{8,12},{12,8},{1,5},{5,1},{9,13},{13,9},{2,6},{6,2},{1... | collective-permute-start | bytes 344072 | tf_op jit(solution)/shard_map/ppermute | solution.py:468
  81.6 1.9 %collective-permute-start.18 = (f32[896,128]{1,0:T(8,128)S(1)}, f32[896,128]{1,0:T(8,128)S(1)}, u32[]{:S(2)}, u32[]{:S(2)}) collective-permute-start(f32[896,128]{1,0:T(8,128)S(1)} %pad_maximum_fusion.near), channel_id=1, source_target_pairs={{0,1},{1,0},{2,3},{3,2},{4,5},{5,4},{6,7},{7,6},{8,9},{9,8},{10,11... | collective-permute-start | bytes 1376264 | tf_op jit(solution)/shard_map/ppermute | solution.py:468

commit v9 on v8

--- a/solution.py
+++ b/solution.py
@@ -74,40 +74,6 @@
                 low, high = turned[:HALO], turned[local_z - HALO :]
                 pair[field, micro, y] = jnp.where(odd, low, high)
                 inner[field, micro, y] = jnp.where(odd, high, low)
-
-
-def cut_kernel(dims, slabs, width, inflow, cotangent, *refs):
-    micros, _, _, local_y, local_z = dims
-    outs, wide = refs[:-1], refs[-1]
-    slab = lax.axis_index("gy")
-    for field, (source, halo) in enumerate(zip((inflow, cotangent), HALOS)):
-        at = slice(0, width + 2 * halo) if field == 0 else slice(width + 2 * HALO, None)
-        for micro in range(micros):
-            for y in range(local_y):
-                wide[field, micro, y, :HALO] = jnp.zeros((HALO, LANES), F32)
-                wide[field, micro, y, HALO + local_z :] = jnp.zeros((HALO, LANES), F32)
-                turned = turned_rows(dims, source, micro, y)
-                wide[field, micro, y, HALO : HALO + local_z] = turned
-                for turn in range(slabs):
-                    start = (slab ^ turn) * width + HALO - halo
-                    if width % 8 == 0 and halo % 8 == 0:
-                        start = pl.multiple_of(start, 8)
-                    outs[turn][micro, y, at] = wide[field, micro, y, pl.ds(start, width + 2 * halo)]
-
-
-def edge_kernel(width, *refs):
-    windows, edge = refs[:-1], refs[-1]
-    slab = lax.axis_index("gy")
-    micros, local_y = windows[0].shape[:2]
-    for field, halo in enumerate(HALOS):
-        base = halo if field == 0 else width + 2 * HALO + halo
-        for turn, window in enumerate(windows):
-            owner = slab ^ turn
-            for micro in range(micros):
-                for y in range(local_y):
-                    low = window[micro, y, base : base + HALO]
-                    high = window[micro, y, base + width - HALO : base + width]
-                    edge[field, micro, owner * local_y + y] = jnp.where(slab == 0, low, high)
 
 
 def window_kernel(dims, rows, pair, inner, *refs):
@@ -228,7 +194,7 @@
                 for edge in (0, self.rows_y + 1):
                     target[lead, micro, edge * self.depth : (edge + 1) * self.depth, :] = blank
 
-    def fill(self, field, windows, which, edge):
+    def fill(self, field, windows, which):
         halo = HALOS[which]
         span = self.width + 2 * halo
         at = 0 if which == 0 else self.width + 2 * HALO
@@ -243,19 +209,6 @@
                     start = pl.multiple_of((owner * self.per_owner + y) * self.depth, 16)
                     value = jnp.concatenate(parts, axis=0) if len(parts) > 1 else parts[0]
                     field[micro, pl.ds(start, self.depth), :] = value
-        if edge is None:
-            return
-        for side, rows, at in (
-            (0, slice(HALO - halo, HALO), HALO - halo),
-            (self.slabs - 1, slice(0, halo), HALO + self.width),
-        ):
-
-            @pl.when(self.slab == side)
-            def _():
-                for micro in range(self.micros):
-                    for y in range(self.rows_y):
-                        start = y * self.depth + at
-                        field[micro, start : start + halo, :] = edge[which, micro, y, rows]
 
     def cut_out(self, targets, source):
         for turn, target in enumerate(targets):
@@ -267,12 +220,12 @@
                     target[micro, y] = source[micro, rows, :]
 
 
-def forward_kernel(dims, edged, own, own_row, other, other_row, *refs):
+def forward_kernel(dims, own, own_row, other, other_row, *refs):
     slab = Slab(dims)
-    windows, (*edge, acts, kept) = refs[: slab.slabs], refs[slab.slabs : slab.slabs + edged + 2]
-    outs, (whole, field) = refs[slab.slabs + edged + 2 : -2], refs[-2:]
+    windows, (acts, kept) = refs[: slab.slabs], refs[slab.slabs : slab.slabs + 2]
+    outs, (whole, field) = refs[slab.slabs + 2 : -2], refs[-2:]
     slab.blank_edges(acts)
-    slab.fill(field, windows, 0, edge[0] if edged else None)
+    slab.fill(field, windows, 0)
 
     def take_in(start):
         for micro in range(slab.micros):
@@ -310,13 +263,12 @@
     slab.cut_out(outs, whole)
 
 
-def backward_kernel(dims, edged, scale, own, other, acts, kept, *refs):
+def backward_kernel(dims, scale, own, other, acts, kept, *refs):
     slab = Slab(dims)
     windows, refs = refs[: slab.slabs], refs[slab.slabs :]
-    edge, refs = refs[:edged], refs[edged:]
     outs, (sums, rim, slopes, field, acc) = refs[: slab.slabs], refs[slab.slabs :]
     slab.blank_edges(rim)
-    slab.fill(field, windows, 1, edge[0] if edged else None)
+    slab.fill(field, windows, 1)
 
     def take_gradient(layer, micro, start, gradient):
         at = pl.ds(start, slab.chunk)
@@ -489,39 +441,32 @@
     scale = 1.0 / math.sqrt(micros * size_x * rows_y * local_z * columns)
     rows = micros * chans * size_x * local_y
     blocks = [inflow.reshape(rows, local_z), cotangent.reshape(rows, local_z)]
+    ends = ((2, micros, local_y, HALO, LANES), F32)
+    fields, pair, inner = call(
+        functools.partial(turn_kernel, inflow.shape),
+        "turn",
+        [((2, micros, local_y, local_z, LANES), F32), ends, ends],
+        blocks,
+    )
     packs = [((BLOCKS, chans, LANES), F32), ((BLOCKS // 2, chans, LANES), F32)]
     own, sent = call(pack_kernel, "pack", packs, [weights, biases])
+    pair = swapped(pair, 1)
+    route = [(i, i + 1) for i in range(1, columns - 1, 2)]
+    inner = lax.ppermute(inner, "gz", route + [(after, before) for before, after in route])
+    windows = call(
+        functools.partial(window_kernel, (slabs, width, columns)),
+        "windows",
+        [((micros, local_y, sum(width + 2 * halo for halo in HALOS), LANES), F32)] * slabs,
+        [fields, pair, inner],
+        [pltpu.VMEM((2, micros, local_y, local_z + 2 * HALO, LANES), F32)],
+    )
+    sent, windows = lax.optimization_barrier((sent, windows))
     near_half = lax.ppermute(sent, "section", [(0, 1), (1, 0)])
-    reach = sum(width + 2 * halo for halo in HALOS)
-    cuts = [((micros, local_y, reach, LANES), F32)] * slabs
-    wide = pltpu.VMEM((2, micros, local_y, local_z + 2 * HALO, LANES), F32)
-    edged = width >= HALO and slabs > 1
-    if edged:
-        kernel = functools.partial(cut_kernel, inflow.shape, slabs, width)
-        windows = call(kernel, "cut", cuts, blocks, [wide])
-    else:
-        ends = ((2, micros, local_y, HALO, LANES), F32)
-        kernel = functools.partial(turn_kernel, inflow.shape)
-        whole = ((2, micros, local_y, local_z, LANES), F32)
-        fields, pair, inner = call(kernel, "turn", [whole, ends, ends], blocks)
-        pair = swapped(pair, 1)
-        route = [(i, i + 1) for i in range(1, columns - 1, 2)]
-        inner = lax.ppermute(inner, "gz", route + [(after, before) for before, after in route])
-        kernel = functools.partial(window_kernel, (slabs, width, columns))
-        windows = call(kernel, "windows", cuts, [fields, pair, inner], [wide])
     windows = spread(windows)
 
     tables = [((2, 9 * LANES, 3 * LANES), BF16)] * 2 + [((2, 8, LANES), F32)]
     own_fwd, own_bwd, own_row = call(table_kernel, "own_table", tables, [own])
     near_half, windows, own_row = lax.optimization_barrier((near_half, windows, own_row))
-    edges = []
-    if edged:
-        edge = ((2, micros, rows_y, HALO, LANES), F32)
-        edges = call(functools.partial(edge_kernel, width), "edge", [edge], windows)
-        last = (slabs - 1) * columns
-        route = [(g, last + g - 1) for g in range(1, columns)]
-        route += [(after, before) for before, after in route]
-        edges = [lax.ppermute(edges[0], ("gy", "gz"), route)]
     far_half = swapped(near_half, 1)
     far_fwd, far_bwd, far_row = call(table_kernel, "far_table", tables, [near_half, far_half])
 
@@ -530,19 +475,19 @@
     full = rows_y * depth
     piece = ((micros, local_y, width, LANES), F32)
     acts, kept, *fronts = call(
-        functools.partial(forward_kernel, dims, edged),
+        functools.partial(forward_kernel, dims),
         "forward",
         [((5, micros, padded, 2 * LANES), BF16), ((4, micros, full, LANES), F32)] + [piece] * slabs,
-        [own_fwd, own_row, far_fwd, far_row, *windows, *edges],
+        [own_fwd, own_row, far_fwd, far_row, *windows],
         [pltpu.VMEM((micros, full, LANES), F32)] * 2,
     )
     if slabs == 4:
         passed = swapped(jnp.stack(fronts[2:]), 2, "gy")
     *backs, sums = call(
-        functools.partial(backward_kernel, dims, edged, scale),
+        functools.partial(backward_kernel, dims, scale),
         "backward",
         [piece] * slabs + [((BLOCKS, chans, LANES), F32)],
-        [own_bwd, far_bwd, acts, kept, *windows, *edges],
+        [own_bwd, far_bwd, acts, kept, *windows],
         [
             pltpu.VMEM((2, micros, padded, 2 * LANES), BF16),
             pltpu.VMEM((4, micros, full, LANES), F32),
@@ -564,14 +509,11 @@
     else:
         outs = spread([jnp.stack(pair) for pair in zip(fronts, backs)])
     part = half // 4
+    block = block[: 2 * part] + swapped(block[2 * part :], 2)
+    block, outs = lax.optimization_barrier((block, outs))
     odd = lax.axis_index("gy") % 2 == 1
-    lows, highs = [block[i * part : (i + 1) * part] for i in (0, 2)], [
-        block[i * part : (i + 1) * part] for i in (1, 3)
-    ]
-    mine, beside = [jnp.where(odd, high, low) for low, high in zip(lows, highs)]
-    above, across = [jnp.where(odd, low, high) for low, high in zip(lows, highs)]
-    kept = mine + sum(around(above, beside, across))
-    kept, outs = lax.optimization_barrier((kept, outs))
+    kept = jnp.where(odd, block[part:], block[:part])
+    kept = kept + swapped(jnp.where(odd, block[:part], block[part:]), 1, "gy")
     bit = 2
     while bit < slabs:
         kept = kept + swapped(kept, bit, "gy")

time: 85.2 us -> 81.2 us (0.953)
  starting transfers between devices: 29.1 us -> 25.7 us
  waiting for transfers between devices: 35.7 us -> 33 us
  local copies, waits for them, and re-layouts: 2.27 us -> 4.17 us
    ppermute x2 -> x1, starting transfers between devices: 3.45 us -> 0.07 us  [around(): across = lax.ppermute(across, ('gy', 'gz'), route)]
    ppermute x3, waiting for transfers between devices: 12.6 us -> 10.5 us  [spread(): got.append(lax.ppermute(blocks[turn], 'gy', route))]
    unnamed x8, local copies, waits for them, and re-layouts: 2.16 us -> 4.04 us
    ppermute x2 -> x1, waiting for transfers between devices: 3.39 us -> 2.31 us  [around(): across = lax.ppermute(across, ('gy', 'gz'), route)]
    ppermute x12 -> x13, waiting for transfers between devices: 19.6 us -> 20.3 us  [swapped(): lax.ppermute(block, axis, [(i, i ^ bit) for i in range(lax.axis_size(axis...]
    ppermute x12 -> x13, starting transfers between devices: 17.6 us -> 18 us  [swapped(): lax.ppermute(block, axis, [(i, i ^ bit) for i in range(lax.axis_size(axis...]
  transfers between devices with their start and end apart: 19 -> 19, of which waited for: 11 -> 14; matrix products, arithmetic and copies ran while one was open for 0% -> 0% of each run, Pallas kernels for 12% -> 11%
where the time goes in v9:
time: 81.2 us; the launch traced here: 81 us
  waiting for transfers between devices  33 us (41%)
  starting transfers between devices  25.7 us (32%)
  Pallas kernels  17.1 us (21%)
  local copies, waits for them, and re-layouts  4.17 us (5%)
  between operations  0.82 us (1%)
    ppermute x13, waiting for transfers between devices, swapped(): lax.ppermute(block, axis, [(i, i ^ bit) for i in range(lax.axis_size(axis...  20.3 us
    ppermute x13, starting transfers between devices, swapped(): lax.ppermute(block, axis, [(i, i ^ bit) for i in range(lax.axis_size(axis...  18 us
    pallas_call x9, Pallas kernels, call(): pl.pallas_call(kernel, out_shape=arrays, in_specs=[VMEM] * len(args), out...  17.1 us
    ppermute x3, waiting for transfers between devices, spread(): got.append(lax.ppermute(blocks[turn], 'gy', route))  10.5 us
    ppermute x3, starting transfers between devices, spread(): got.append(lax.ppermute(blocks[turn], 'gy', route))  4.39 us
    unnamed x8, local copies, waits for them, and re-layouts  4.04 us
    ppermute x1, starting transfers between devices, per_device(): near_half = lax.ppermute(sent, 'section', [(0, 1), (1, 0)])  2.58 us
    ppermute x1, waiting for transfers between devices, around(): across = lax.ppermute(across, ('gy', 'gz'), route)  2.31 us
  transfers between devices with their start and end apart: 19, of which 14 were waited for; matrix products, arithmetic and copies ran while one was open for 0% of the time, Pallas kernels for 11%

profile of v9, /device:TPU:0, one launch (start us, length us, event | category | flops | bytes accessed | tf_op | source)
XLA Modules:
  0.0 81.0 jit_solution(17275237972716567556)
XLA Ops:
  0.6 0.0 copy-start.1
  0.6 0.9 %copy-done.1 = f32[2,64,2,2,128]{4,3,2,1,0:T(2,128)S(1)} copy-done((f32[2,64,2,2,128]{4,3,2,1,0:T(2,128)S(1)}, f32[2,64,2,2,128]{4,3,2,1,0:T(2,128)}, u32[]{:S(2)}) %copy-start.1) | copy-done | bytes 262168
  1.6 0.0 copy-start.2
  1.6 0.9 %copy-done.2 = f32[2,64,2,2,128]{4,3,2,1,0:T(2,128)S(1)} copy-done((f32[2,64,2,2,128]{4,3,2,1,0:T(2,128)S(1)}, f32[2,64,2,2,128]{4,3,2,1,0:T(2,128)}, u32[]{:S(2)}) %copy-start.2) | copy-done | bytes 262168
  2.5 0.2 turn.1
  2.7 0.5 collective-permute-start
  3.2 0.7 collective-permute-start.1
  3.9 0.0 copy-start
  3.9 1.5 %copy-done = f32[2,27,64,64]{3,2,1,0:T(8,128)S(1)} copy-done((f32[2,27,64,64]{3,2,1,0:T(8,128)S(1)}, f32[2,27,64,64]{3,2,1,0:T(8,128)}, u32[]{:S(2)}) %copy-start) | copy-done | bytes 884760
  5.4 0.0 copy-start.3
  5.4 0.7 copy-done.3
  6.1 0.3 pack.1
  6.4 0.0 collective-permute-done.pair
  6.4 0.0 collective-permute-done.1.inner
  6.4 0.1 windows.1
  6.6 2.6 %collective-permute-start.2 = (f32[14,64,128]{2,1,0:T(8,128)S(1)}, f32[14,64,128]{2,1,0:T(8,128)S(1)}, u32[]{:S(2)}, u32[]{:S(2)}) collective-permute-start(f32[14,64,128]{2,1,0:T(8,128)S(1)} %get-tuple-element.68), channel_id=1, source_target_pairs={{0,16},{16,0},{1,17},{17,1},{2,18},{18,2},{3,19},{19,3},{4,20},{20... | collective-permute-start | bytes 1376264 | tf_op jit(solution)/shard_map/ppermute | solution.py:464
  9.1 1.6 %collective-permute-start.3 = (f32[2,2,88,128]{3,2,1,0:T(8,128)S(1)}, f32[2,2,88,128]{3,2,1,0:T(8,128)S(1)}, u32[]{:S(2)}, u32[]{:S(2)}) collective-permute-start(f32[2,2,88,128]{3,2,1,0:T(8,128)S(1)} %get-tuple-element.70), channel_id=1, source_target_pairs={{0,4},{4,0},{8,12},{12,8},{1,5},{5,1},{9,13},{13,9},{2,6},{6,2},{1... | collective-permute-start | bytes 540680 | tf_op jit(solution)/shard_map/ppermute | solution.py:412
  10.7 2.6 %collective-permute-start.4 = (f32[2,2,88,128]{3,2,1,0:T(8,128)S(1)}, f32[2,2,88,128]{3,2,1,0:T(8,128)S(1)}, u32[]{:S(2)}, u32[]{:S(2)}) collective-permute-start(f32[2,2,88,128]{3,2,1,0:T(8,128)S(1)} %get-tuple-element.71), channel_id=1, source_target_pairs={{0,8},{4,12},{8,0},{12,4},{1,9},{5,13},{9,1},{13,5},{2,10},{6,14},... | collective-permute-start | bytes 540680 | tf_op jit(solution)/shard_map/ppermute | solution.py:412
  13.3 0.2 collective-permute-start.5
  13.5 0.7 own_table.1
  14.2 0.6 collective-permute-done.3.refs_1_
  14.8 3.7 %collective-permute-done.4.refs_2_ = f32[2,2,88,128]{3,2,1,0:T(8,128)S(1)} collective-permute-done((f32[2,2,88,128]{3,2,1,0:T(8,128)S(1)}, f32[2,2,88,128]{3,2,1,0:T(8,128)S(1)}, u32[]{:S(2)}, u32[]{:S(2)}) %collective-permute-start.4) | collective-permute-done | bytes 180256 | tf_op jit(solution)/shard_map/ppermute | solution.py:412
  18.5 6.2 %collective-permute-done.5.refs_3_ = f32[2,2,88,128]{3,2,1,0:T(8,128)S(1)} collective-permute-done((f32[2,2,88,128]{3,2,1,0:T(8,128)S(1)}, f32[2,2,88,128]{3,2,1,0:T(8,128)S(1)}, u32[]{:S(2)}, u32[]{:S(2)}) %collective-permute-start.5) | collective-permute-done | bytes 180256 | tf_op jit(solution)/shard_map/ppermute | solution.py:412
  24.7 0.0 collective-permute-done.2.refs_0_
  24.7 3.3 %collective-permute-start.6 = (f32[14,64,128]{2,1,0:T(8,128)S(1)}, f32[14,64,128]{2,1,0:T(8,128)S(1)}, u32[]{:S(2)}, u32[]{:S(2)}) collective-permute-start(f32[14,64,128]{2,1,0:T(8,128)S(1)} %collective-permute-done.2.refs_0_), channel_id=1, source_target_pairs={{0,1},{1,0},{2,3},{3,2},{4,5},{5,4},{6,7},{7,6},{8,9},{9,8},{10,11... | collective-permute-start | bytes 1376264 | tf_op jit(solution)/shard_map/ppermute | solution.py:420
  28.0 1.4 %collective-permute-done.6.refs_1_ = f32[14,64,128]{2,1,0:T(8,128)S(1)} collective-permute-done((f32[14,64,128]{2,1,0:T(8,128)S(1)}, f32[14,64,128]{2,1,0:T(8,128)S(1)}, u32[]{:S(2)}, u32[]{:S(2)}) %collective-permute-start.6) | collective-permute-done | bytes 458784 | tf_op jit(solution)/shard_map/ppermute | solution.py:420
  29.5 0.7 far_table.1
  30.2 5.3 %forward.1 = (bf16[5,2,480,256]{3,2,1,0:T(8,128)(2,1)S(1)}, f32[4,2,384,128]{3,2,1,0:T(8,128)S(1)}, f32[2,2,32,128]{3,2,1,0:T(8,128)S(1)}, f32[2,2,32,128]{3,2,1...) custom-call(bf16[2,1152,384]{2,1,0:T(8,128)(2,1)S(1)} %get-tuple-element.76.own, ...), custom_call_target="tpu_custom_call" | custom-call | bytes 1024 | tf_op jit(solution)/shard_map/forward/pallas_call | solution.py:24
  35.6 4.1 %collective-permute-start.7 = (f32[2,2,2,32,128]{4,3,2,1,0:T(8,128)S(1)}, f32[2,2,2,32,128]{4,3,2,1,0:T(8,128)S(1)}, u32[]{:S(2)}, u32[]{:S(2)}) collective-permute-start(f32[2,2,2,32,128]{4,3,2,1,0:T(8,128)S(1)} %pad_maximum_fusion.2), channel_id=1, source_target_pairs={{0,8},{4,12},{8,0},{12,4},{1,9},{5,13},{9,1},{13,5},{2,10},{6,14},... | collective-permute-start | bytes 393224 | tf_op jit(solution)/shard_map/ppermute | solution.py:420
  39.7 7.1 %backward.1 = (f32[2,2,32,128]{3,2,1,0:T(8,128)S(1)}, f32[2,2,32,128]{3,2,1,0:T(8,128)S(1)}, f32[2,2,32,128]{3,2,1,0:T(8,128)S(1)}, f32[2,2,32,128]{3,2,1,0:T(8,128)S(1)}, f32[28,64,128]{2,1,0:T(8,128)S(1)}) custom-call(bf16[2,1152,384]{2,1,0:T(8,128)(2,1)S(1)} %get-tuple-element.59.own, bf16[2,1152,384]{2,1,0:T(8,128)(2,1)S(1)} %get-tuple-element.75.other, ...), custom_call_target="tpu_custom_call" | custom-call | flops 4076863488 | bytes 1024 | tf_op jit(solution)/shard_map/backward/pallas_call | solution.py:24
  46.8 0.0 collective-permute-done.7
  46.9 0.1 fusion
  46.9 0.1 collective-permute-start.8
  47.1 1.7 %collective-permute-done.8 = f32[896,128]{1,0:T(8,128)S(1)} collective-permute-done((f32[896,128]{1,0:T(8,128)S(1)}, f32[896,128]{1,0:T(8,128)S(1)}, u32[]{:S(2)}, u32[]{:S(2)}) %collective-permute-start.8) | collective-permute-done | bytes 458784 | tf_op jit(solution)/shard_map/ppermute | solution.py:420
  48.9 1.1 %collective-permute-start.9 = (f32[448,128]{1,0:T(8,128)S(1)}, f32[448,128]{1,0:T(8,128)S(1)}, u32[]{:S(2)}, u32[]{:S(2)}) collective-permute-start(f32[448,128]{1,0:T(8,128)S(1)} %slice.46), channel_id=1, source_target_pairs={{0,2},{1,3},{2,0},{3,1},{4,6},{5,7},{6,4},{7,5},{8,10},{9,11},{10,... | collective-permute-start | bytes 688136 | tf_op jit(solution)/shard_map/ppermute | solution.py:420
  50.1 0.1 collective-permute-start.10
  50.1 1.8 %collective-permute-start.11 = (f32[2,2,32,128]{3,2,1,0:T(8,128)S(1)}, f32[2,2,32,128]{3,2,1,0:T(8,128)S(1)}, u32[]{:S(2)}, u32[]{:S(2)}) collective-permute-start(f32[2,2,32,128]{3,2,1,0:T(8,128)S(1)} %get-tuple-element.101), channel_id=1, source_target_pairs={{0,8},{4,12},{8,0},{12,4},{1,9},{5,13},{9,1},{13,5},{2,10},{6,14},... | collective-permute-start | bytes 196616 | tf_op jit(solution)/shard_map/ppermute | solution.py:420
  52.0 2.5 %collective-permute-start.12 = (f32[2,2,32,128]{3,2,1,0:T(8,128)S(1)}, f32[2,2,32,128]{3,2,1,0:T(8,128)S(1)}, u32[]{:S(2)}, u32[]{:S(2)}) collective-permute-start(f32[2,2,32,128]{3,2,1,0:T(8,128)S(1)} %get-tuple-element.102), channel_id=1, source_target_pairs={{0,12},{4,8},{8,4},{12,0},{1,13},{5,9},{9,5},{13,1},{2,14},{6,10},... | collective-permute-start | bytes 196616 | tf_op jit(solution)/shard_map/ppermute | solution.py:420
  54.5 2.1 %collective-permute-done.9 = f32[448,128]{1,0:T(8,128)S(1)} collective-permute-done((f32[448,128]{1,0:T(8,128)S(1)}, f32[448,128]{1,0:T(8,128)S(1)}, u32[]{:S(2)}, u32[]{:S(2)}) %collective-permute-start.9) | collective-permute-done | bytes 229408 | tf_op jit(solution)/shard_map/ppermute | solution.py:420
  56.6 0.0 collective-permute-done.11.refs_6_
  56.7 2.6 %collective-permute-done.12.refs_7_ = f32[2,2,32,128]{3,2,1,0:T(8,128)S(1)} collective-permute-done((f32[2,2,32,128]{3,2,1,0:T(8,128)S(1)}, f32[2,2,32,128]{3,2,1,0:T(8,128)S(1)}, u32[]{:S(2)}, u32[]{:S(2)}) %collective-permute-start.12) | collective-permute-done | bytes 65568 | tf_op jit(solution)/shard_map/ppermute | solution.py:420
  59.3 0.3 collective-permute-done.10
  59.6 0.1 collective-permute-start.13
  59.7 4.8 %collective-permute-done.13 = f32[224,128]{1,0:T(8,128)S(1)} collective-permute-done((f32[224,128]{1,0:T(8,128)S(1)}, f32[224,128]{1,0:T(8,128)S(1)}, u32[]{:S(2)}, u32[]{:S(2)}) %collective-permute-start.13) | collective-permute-done | bytes 114720 | tf_op jit(solution)/shard_map/ppermute | solution.py:420
  64.5 0.7 collective-permute-start.14
  65.2 5.7 %collective-permute-done.14 = f32[224,128]{1,0:T(8,128)S(1)} collective-permute-done((f32[224,128]{1,0:T(8,128)S(1)}, f32[224,128]{1,0:T(8,128)S(1)}, u32[]{:S(2)}, u32[]{:S(2)}) %collective-permute-start.14) | collective-permute-done | bytes 114720 | tf_op jit(solution)/shard_map/ppermute | solution.py:420
  70.9 0.1 collective-permute-start.17
  71.0 1.0 %collective-permute-start.16 = (f32[224,128]{1,0:T(8,128)S(1)}, f32[224,128]{1,0:T(8,128)S(1)}, u32[]{:S(2)}, u32[]{:S(2)}) collective-permute-start(f32[224,128]{1,0:T(8,128)S(1)} %add.20), channel_id=1, source_target_pairs={{0,2},{1,3},{2,0},{3,1},{4,6},{5,7},{6,4},{7,5},{8,10},{9,11},{10,... | collective-permute-start | bytes 344072 | tf_op jit(solution)/shard_map/ppermute | solution.py:420
  72.1 2.4 %collective-permute-start.15 = (f32[224,128]{1,0:T(8,128)S(1)}, f32[224,128]{1,0:T(8,128)S(1)}, u32[]{:S(2)}, u32[]{:S(2)}) collective-permute-start(f32[224,128]{1,0:T(8,128)S(1)} %add.20), channel_id=1, source_target_pairs={{0,4},{4,0},{8,12},{12,8},{1,5},{5,1},{9,13},{13,9},{2,6},{6,2},{1... | collective-permute-start | bytes 344072 | tf_op jit(solution)/shard_map/ppermute | solution.py:420
  74.5 2.3 %collective-permute-done.17 = f32[224,128]{1,0:T(8,128)S(1)} collective-permute-done((f32[224,128]{1,0:T(8,128)S(1)}, f32[224,128]{1,0:T(8,128)S(1)}, u32[]{:S(2)}, u32[]{:S(2)}) %collective-permute-start.17) | collective-permute-done | bytes 114720 | tf_op jit(solution)/shard_map/ppermute | solution.py:429
  76.8 0.3 collective-permute-done.16
  77.1 0.4 collective-permute-done.15
  77.5 0.1 collective-permute-start.18
  77.6 1.0 %restore.1 = (f32[512,128]{1,0:T(8,128)}, f32[512,128]{1,0:T(8,128)}) custom-call(f32[2,2,32,128]{3,2,1,0:T(8,128)S(1)} %get-tuple-element.96.refs_0_, f32[2,2,32,128]{3,2,1,0:T(8,128)S(1)} %get-tuple-element.116.refs_1_, f32[2,2,32,128]{3,2,1,0:T(8,128)S(1)} %get-tuple-element.117.refs_2_, f32[2,2,32,128]{3,2,1,0:T(8,128)S(1)} %get-tuple-element.115.refs_3_, ...), custom_call_target="tpu_custom_call" | custom-call | bytes 1024 | tf_op jit(solution)/shard_map/restore/pallas_call | solution.py:24
  78.6 0.8 %collective-permute-done.18.core = f32[896,128]{1,0:T(8,128)S(1)} collective-permute-done((f32[896,128]{1,0:T(8,128)S(1)}, f32[896,128]{1,0:T(8,128)S(1)}, u32[]{:S(2)}, u32[]{:S(2)}) %collective-permute-start.18) | collective-permute-done | bytes 458784 | tf_op jit(solution)/shard_map/ppermute | solution.py:420
  79.4 1.6 %unpack.1 = (f32[2,27,64,64]{3,2,1,0:T(8,128)}, f32[2,64]{1,0:T(2,128)}) custom-call(f32[896,128]{1,0:T(8,128)S(1)} %pad_maximum_fusion.near, f32[896,128]{1,0:T(8,128)S(1)} %collective-permute-done.18.core), custom_call_target="tpu_custom_call" | custom-call | bytes 1024 | tf_op jit(solution)/shard_map/unpack/pallas_call | solution.py:24
  (11 shorter events, 0.2 us)
Async XLA Ops:
  0.6 1.0 %copy-start.1 = (f32[2,64,2,2,128]{4,3,2,1,0:T(2,128)S(1)}, f32[2,64,2,2,128]{4,3,2,1,0:T(2,128)}, u32[]{:S(2)}) copy-start(f32[2,64,2,2,128]{4,3,2,1,0:T(2,128)} %param.4) | copy-start | bytes 786436
  1.6 0.9 %copy-start.2 = (f32[2,64,2,2,128]{4,3,2,1,0:T(2,128)S(1)}, f32[2,64,2,2,128]{4,3,2,1,0:T(2,128)}, u32[]{:S(2)}) copy-start(f32[2,64,2,2,128]{4,3,2,1,0:T(2,128)} %param.7) | copy-start | bytes 786436
  2.7 3.7 %collective-permute-start = (f32[2,2,2,8,128]{4,3,2,1,0:T(8,128)S(1)}, f32[2,2,2,8,128]{4,3,2,1,0:T(8,128)S(1)}, u32[]{:S(2)}, u32[]{:S(2)}) collective-permute-start(f32[2,2,2,8,128]{4,3,2,1,0:T(8,128)S(1)} %get-tuple-element.62), channel_id=1, source_target_pairs={{0,1},{1,0},{2,3},{3,2},{4,5},{5,4},{6,7},{7,6},{8,9},{9,8},{10,11... | collective-permute-start | bytes 98312 | tf_op jit(solution)/shard_map/ppermute | solution.py:420
  3.2 3.2 %collective-permute-start.1 = (f32[2,2,2,8,128]{4,3,2,1,0:T(8,128)S(1)}, f32[2,2,2,8,128]{4,3,2,1,0:T(8,128)S(1)}, u32[]{:S(2)}, u32[]{:S(2)}) collective-permute-start(f32[2,2,2,8,128]{4,3,2,1,0:T(8,128)S(1)} %get-tuple-element.63), channel_id=1, source_target_pairs={{1,2},{2,1},{5,6},{6,5},{9,10},{10,9},{13,14},{14,13},{17,18},{18,... | collective-permute-start | bytes 98312 | tf_op jit(solution)/shard_map/ppermute | solution.py:455
  3.9 1.5 %copy-start = (f32[2,27,64,64]{3,2,1,0:T(8,128)S(1)}, f32[2,27,64,64]{3,2,1,0:T(8,128)}, u32[]{:S(2)}) copy-start(f32[2,27,64,64]{3,2,1,0:T(8,128)} %weights.1) | copy-start | bytes 2654212
  5.4 0.7 copy-start.3
  6.6 18.1 %collective-permute-start.2 = (f32[14,64,128]{2,1,0:T(8,128)S(1)}, f32[14,64,128]{2,1,0:T(8,128)S(1)}, u32[]{:S(2)}, u32[]{:S(2)}) collective-permute-start(f32[14,64,128]{2,1,0:T(8,128)S(1)} %get-tuple-element.68), channel_id=1, source_target_pairs={{0,16},{16,0},{1,17},{17,1},{2,18},{18,2},{3,19},{19,3},{4,20},{20... | collective-permute-start | bytes 1376264 | tf_op jit(solution)/shard_map/ppermute | solution.py:464
  9.1 5.7 %collective-permute-start.3 = (f32[2,2,88,128]{3,2,1,0:T(8,128)S(1)}, f32[2,2,88,128]{3,2,1,0:T(8,128)S(1)}, u32[]{:S(2)}, u32[]{:S(2)}) collective-permute-start(f32[2,2,88,128]{3,2,1,0:T(8,128)S(1)} %get-tuple-element.70), channel_id=1, source_target_pairs={{0,4},{4,0},{8,12},{12,8},{1,5},{5,1},{9,13},{13,9},{2,6},{6,2},{1... | collective-permute-start | bytes 540680 | tf_op jit(solution)/shard_map/ppermute | solution.py:412
  10.7 7.8 %collective-permute-start.4 = (f32[2,2,88,128]{3,2,1,0:T(8,128)S(1)}, f32[2,2,88,128]{3,2,1,0:T(8,128)S(1)}, u32[]{:S(2)}, u32[]{:S(2)}) collective-permute-start(f32[2,2,88,128]{3,2,1,0:T(8,128)S(1)} %get-tuple-element.71), channel_id=1, source_target_pairs={{0,8},{4,12},{8,0},{12,4},{1,9},{5,13},{9,1},{13,5},{2,10},{6,14},... | collective-permute-start | bytes 540680 | tf_op jit(solution)/shard_map/ppermute | solution.py:412
  13.3 11.4 %collective-permute-start.5 = (f32[2,2,88,128]{3,2,1,0:T(8,128)S(1)}, f32[2,2,88,128]{3,2,1,0:T(8,128)S(1)}, u32[]{:S(2)}, u32[]{:S(2)}) collective-permute-start(f32[2,2,88,128]{3,2,1,0:T(8,128)S(1)} %get-tuple-element.72), channel_id=1, source_target_pairs={{0,12},{4,8},{8,4},{12,0},{1,13},{5,9},{9,5},{13,1},{2,14},{6,10},... | collective-permute-start | bytes 540680 | tf_op jit(solution)/shard_map/ppermute | solution.py:412
  24.7 4.8 %collective-permute-start.6 = (f32[14,64,128]{2,1,0:T(8,128)S(1)}, f32[14,64,128]{2,1,0:T(8,128)S(1)}, u32[]{:S(2)}, u32[]{:S(2)}) collective-permute-start(f32[14,64,128]{2,1,0:T(8,128)S(1)} %collective-permute-done.2.refs_0_), channel_id=1, source_target_pairs={{0,1},{1,0},{2,3},{3,2},{4,5},{5,4},{6,7},{7,6},{8,9},{9,8},{10,11... | collective-permute-start | bytes 1376264 | tf_op jit(solution)/shard_map/ppermute | solution.py:420
  35.6 11.3 %collective-permute-start.7 = (f32[2,2,2,32,128]{4,3,2,1,0:T(8,128)S(1)}, f32[2,2,2,32,128]{4,3,2,1,0:T(8,128)S(1)}, u32[]{:S(2)}, u32[]{:S(2)}) collective-permute-start(f32[2,2,2,32,128]{4,3,2,1,0:T(8,128)S(1)} %pad_maximum_fusion.2), channel_id=1, source_target_pairs={{0,8},{4,12},{8,0},{12,4},{1,9},{5,13},{9,1},{13,5},{2,10},{6,14},... | collective-permute-start | bytes 393224 | tf_op jit(solution)/shard_map/ppermute | solution.py:420
  46.9 1.9 %collective-permute-start.8 = (f32[896,128]{1,0:T(8,128)S(1)}, f32[896,128]{1,0:T(8,128)S(1)}, u32[]{:S(2)}, u32[]{:S(2)}) collective-permute-start(f32[896,128]{1,0:T(8,128)S(1)} %bitcast.25), channel_id=1, source_target_pairs={{0,1},{1,0},{2,3},{3,2},{4,5},{5,4},{6,7},{7,6},{8,9},{9,8},{10,11... | collective-permute-start | bytes 1376264 | tf_op jit(solution)/shard_map/ppermute | solution.py:420
  48.9 7.7 %collective-permute-start.9 = (f32[448,128]{1,0:T(8,128)S(1)}, f32[448,128]{1,0:T(8,128)S(1)}, u32[]{:S(2)}, u32[]{:S(2)}) collective-permute-start(f32[448,128]{1,0:T(8,128)S(1)} %slice.46), channel_id=1, source_target_pairs={{0,2},{1,3},{2,0},{3,1},{4,6},{5,7},{6,4},{7,5},{8,10},{9,11},{10,... | collective-permute-start | bytes 688136 | tf_op jit(solution)/shard_map/ppermute | solution.py:420
  50.1 9.5 %collective-permute-start.10 = (f32[3,2,2,32,128]{4,3,2,1,0:T(8,128)S(1)}, f32[3,2,2,32,128]{4,3,2,1,0:T(8,128)S(1)}, u32[]{:S(2)}, u32[]{:S(2)}) collective-permute-start(f32[3,2,2,32,128]{4,3,2,1,0:T(8,128)S(1)} %pad_maximum_fusion.1), channel_id=1, source_target_pairs={{0,4},{4,0},{8,12},{12,8},{1,5},{5,1},{9,13},{13,9},{2,6},{6,2},{1... | collective-permute-start | bytes 589832 | tf_op jit(solution)/shard_map/ppermute | solution.py:420
  50.1 6.6 %collective-permute-start.11 = (f32[2,2,32,128]{3,2,1,0:T(8,128)S(1)}, f32[2,2,32,128]{3,2,1,0:T(8,128)S(1)}, u32[]{:S(2)}, u32[]{:S(2)}) collective-permute-start(f32[2,2,32,128]{3,2,1,0:T(8,128)S(1)} %get-tuple-element.101), channel_id=1, source_target_pairs={{0,8},{4,12},{8,0},{12,4},{1,9},{5,13},{9,1},{13,5},{2,10},{6,14},... | collective-permute-start | bytes 196616 | tf_op jit(solution)/shard_map/ppermute | solution.py:420
  52.0 7.3 %collective-permute-start.12 = (f32[2,2,32,128]{3,2,1,0:T(8,128)S(1)}, f32[2,2,32,128]{3,2,1,0:T(8,128)S(1)}, u32[]{:S(2)}, u32[]{:S(2)}) collective-permute-start(f32[2,2,32,128]{3,2,1,0:T(8,128)S(1)} %get-tuple-element.102), channel_id=1, source_target_pairs={{0,12},{4,8},{8,4},{12,0},{1,13},{5,9},{9,5},{13,1},{2,14},{6,10},... | collective-permute-start | bytes 196616 | tf_op jit(solution)/shard_map/ppermute | solution.py:420
  59.6 4.9 %collective-permute-start.13 = (f32[224,128]{1,0:T(8,128)S(1)}, f32[224,128]{1,0:T(8,128)S(1)}, u32[]{:S(2)}, u32[]{:S(2)}) collective-permute-start(f32[224,128]{1,0:T(8,128)S(1)} %slice_select_fusion), channel_id=1, source_target_pairs={{0,4},{4,0},{8,12},{12,8},{1,5},{5,1},{9,13},{13,9},{2,6},{6,2},{1... | collective-permute-start | bytes 344072 | tf_op jit(solution)/shard_map/ppermute | solution.py:420
  64.5 6.4 %collective-permute-start.14 = (f32[224,128]{1,0:T(8,128)S(1)}, f32[224,128]{1,0:T(8,128)S(1)}, u32[]{:S(2)}, u32[]{:S(2)}) collective-permute-start(f32[224,128]{1,0:T(8,128)S(1)} %select_add_fusion), channel_id=1, source_target_pairs={{0,8},{4,12},{8,0},{12,4},{1,9},{5,13},{9,1},{13,5},{2,10},{6,14},... | collective-permute-start | bytes 344072 | tf_op jit(solution)/shard_map/ppermute | solution.py:420
  70.9 5.9 %collective-permute-start.17 = (f32[224,128]{1,0:T(8,128)S(1)}, f32[224,128]{1,0:T(8,128)S(1)}, u32[]{:S(2)}, u32[]{:S(2)}) collective-permute-start(f32[224,128]{1,0:T(8,128)S(1)} %add.20), channel_id=1, source_target_pairs={{0,6},{1,7},{2,4},{3,5},{4,2},{5,3},{6,0},{7,1},{8,14},{9,15},{10,... | collective-permute-start | bytes 344072 | tf_op jit(solution)/shard_map/ppermute | solution.py:429
  71.0 6.1 %collective-permute-start.16 = (f32[224,128]{1,0:T(8,128)S(1)}, f32[224,128]{1,0:T(8,128)S(1)}, u32[]{:S(2)}, u32[]{:S(2)}) collective-permute-start(f32[224,128]{1,0:T(8,128)S(1)} %add.20), channel_id=1, source_target_pairs={{0,2},{1,3},{2,0},{3,1},{4,6},{5,7},{6,4},{7,5},{8,10},{9,11},{10,... | collective-permute-start | bytes 344072 | tf_op jit(solution)/shard_map/ppermute | solution.py:420
  72.1 5.4 %collective-permute-start.15 = (f32[224,128]{1,0:T(8,128)S(1)}, f32[224,128]{1,0:T(8,128)S(1)}, u32[]{:S(2)}, u32[]{:S(2)}) collective-permute-start(f32[224,128]{1,0:T(8,128)S(1)} %add.20), channel_id=1, source_target_pairs={{0,4},{4,0},{8,12},{12,8},{1,5},{5,1},{9,13},{13,9},{2,6},{6,2},{1... | collective-permute-start | bytes 344072 | tf_op jit(solution)/shard_map/ppermute | solution.py:420
  77.5 1.9 %collective-permute-start.18 = (f32[896,128]{1,0:T(8,128)S(1)}, f32[896,128]{1,0:T(8,128)S(1)}, u32[]{:S(2)}, u32[]{:S(2)}) collective-permute-start(f32[896,128]{1,0:T(8,128)S(1)} %pad_maximum_fusion.near), channel_id=1, source_target_pairs={{0,1},{1,0},{2,3},{3,2},{4,5},{5,4},{6,7},{7,6},{8,9},{9,8},{10,11... | collective-permute-start | bytes 1376264 | tf_op jit(solution)/shard_map/ppermute | solution.py:420

commit v10 on v9

--- a/solution.py
+++ b/solution.py
@@ -80,23 +80,25 @@
     slabs, width, columns = dims
     outs, wide = refs[:-1], refs[-1]
     slab, column = lax.axis_index("gy"), lax.axis_index("gz")
+    section = lax.axis_index("section")
     odd = column % 2 == 1
     _, micros, local_y, local_z, _ = rows.shape
     for field, halo in enumerate(HALOS):
         at = slice(0, width + 2 * halo) if field == 0 else slice(width + 2 * HALO, None)
-        for micro in range(micros):
-            for y in range(local_y):
+        for y in range(local_y):
+            for micro in range(micros):
                 one, two = pair[field, micro, y], inner[field, micro, y]
                 before = jnp.where(column > 0, jnp.where(odd, one, two), 0.0)
                 after = jnp.where(column < columns - 1, jnp.where(odd, two, one), 0.0)
                 wide[field, micro, y, :HALO] = before
                 wide[field, micro, y, HALO : HALO + local_z] = rows[field, micro, y]
                 wide[field, micro, y, HALO + local_z :] = after
-                for turn in range(slabs):
-                    start = (slab ^ turn) * width + HALO - halo
-                    if width % 8 == 0 and halo % 8 == 0:
-                        start = pl.multiple_of(start, 8)
-                    outs[turn][micro, y, at] = wide[field, micro, y, pl.ds(start, width + 2 * halo)]
+            for turn, out in enumerate(outs):
+                start = (slab ^ turn % slabs) * width + HALO - halo
+                if width % 8 == 0 and halo % 8 == 0:
+                    start = pl.multiple_of(start, 8)
+                micro = section if turn < slabs else 1 - section
+                out[y, at] = wide[field, micro, y, pl.ds(start, width + 2 * halo)]
 
 
 def table_kernel(*refs):
@@ -199,16 +201,16 @@
         span = self.width + 2 * halo
         at = 0 if which == 0 else self.width + 2 * HALO
         extra = [HALO - halo, self.depth - span - (HALO - halo)]
-        for micro in range(self.micros):
-            for turn, window in enumerate(windows):
-                owner = self.slab ^ turn
-                for y in range(self.per_owner):
-                    blanks = [jnp.zeros((rows, LANES), F32) for rows in extra]
-                    parts = [blanks[0], window[micro, y, at : at + span], blanks[1]]
-                    parts = [part for part in parts if part.shape[0]]
-                    start = pl.multiple_of((owner * self.per_owner + y) * self.depth, 16)
-                    value = jnp.concatenate(parts, axis=0) if len(parts) > 1 else parts[0]
-                    field[micro, pl.ds(start, self.depth), :] = value
+        for index, window in enumerate(windows):
+            owner = self.slab ^ index % self.slabs
+            micro = self.section if index < self.slabs else 1 - self.section
+            for y in range(self.per_owner):
+                blanks = [jnp.zeros((rows, LANES), F32) for rows in extra]
+                parts = [blanks[0], window[y, at : at + span], blanks[1]]
+                parts = [part for part in parts if part.shape[0]]
+                start = pl.multiple_of((owner * self.per_owner + y) * self.depth, 16)
+                value = jnp.concatenate(parts, axis=0) if len(parts) > 1 else parts[0]
+                field[micro, pl.ds(start, self.depth), :] = value
 
     def cut_out(self, targets, source):
         for turn, target in enumerate(targets):
@@ -222,8 +224,11 @@
 
 def forward_kernel(dims, own, own_row, other, other_row, *refs):
     slab = Slab(dims)
-    windows, (acts, kept) = refs[: slab.slabs], refs[slab.slabs : slab.slabs + 2]
-    outs, (whole, field) = refs[slab.slabs + 2 : -2], refs[-2:]
+    windows, (acts, kept, *outs), (whole, field) = (
+        refs[: 2 * slab.slabs],
+        refs[2 * slab.slabs : -2],
+        refs[-2:],
+    )
     slab.blank_edges(acts)
     slab.fill(field, windows, 0)
 
@@ -265,7 +270,7 @@
 
 def backward_kernel(dims, scale, own, other, acts, kept, *refs):
     slab = Slab(dims)
-    windows, refs = refs[: slab.slabs], refs[slab.slabs :]
+    windows, refs = refs[: 2 * slab.slabs], refs[2 * slab.slabs :]
     outs, (sums, rim, slopes, field, acc) = refs[: slab.slabs], refs[slab.slabs :]
     slab.blank_edges(rim)
     slab.fill(field, windows, 1)
@@ -420,6 +425,10 @@
     return lax.ppermute(block, axis, [(i, i ^ bit) for i in range(lax.axis_size(axis))])
 
 
+def crossed(block):
+    return lax.ppermute(block, "section", [(0, 1), (1, 0)])
+
+
 def around(above, beside, across):
     slabs, columns = lax.axis_size("gy"), lax.axis_size("gz")
     route = [
@@ -432,6 +441,7 @@
 
 def per_device(inflow, weights, biases, cotangent):
     micros, chans, size_x, local_y, local_z = inflow.shape
+    assert micros == lax.axis_size("section") == 2
     slabs, columns = lax.axis_size("gy"), lax.axis_size("gz")
     rows_y = local_y * slabs
     width = local_z // slabs
@@ -456,17 +466,23 @@
     windows = call(
         functools.partial(window_kernel, (slabs, width, columns)),
         "windows",
-        [((micros, local_y, sum(width + 2 * halo for halo in HALOS), LANES), F32)] * slabs,
+        [((local_y, sum(width + 2 * halo for halo in HALOS), LANES), F32)] * (slabs + 1),
         [fields, pair, inner],
         [pltpu.VMEM((2, micros, local_y, local_z + 2 * HALO, LANES), F32)],
     )
     sent, windows = lax.optimization_barrier((sent, windows))
-    near_half = lax.ppermute(sent, "section", [(0, 1), (1, 0)])
-    windows = spread(windows)
+    near_half = crossed(sent)
+    *mine, home = windows
+    mine = spread(mine)
 
     tables = [((2, 9 * LANES, 3 * LANES), BF16)] * 2 + [((2, 8, LANES), F32)]
     own_fwd, own_bwd, own_row = call(table_kernel, "own_table", tables, [own])
-    near_half, windows, own_row = lax.optimization_barrier((near_half, windows, own_row))
+    if slabs <= 8:
+        theirs = [home] + [crossed(window) for window in mine[1:]]
+    else:
+        theirs = list(crossed(jnp.stack(mine)))
+    windows = mine + theirs
+    near_half, mine, own_row = lax.optimization_barrier((near_half, mine, own_row))
     far_half = swapped(near_half, 1)
     far_fwd, far_bwd, far_row = call(table_kernel, "far_table", tables, [near_half, far_half])
 

time: 81.2 us -> 80.3 us (0.989)
  waiting for transfers between devices: 33 us -> 31.7 us
    ppermute x3, waiting for transfers between devices: 10.5 us -> 5.44 us  [spread(): got.append(lax.ppermute(blocks[turn], 'gy', route))]
    ppermute x1 -> x4, waiting for transfers between devices: 0.01 us -> 4.8 us  [crossed(): return lax.ppermute(block, 'section', [(0, 1), (1, 0)])]
    ppermute x1 -> x4, starting transfers between devices: 2.58 us -> 5.49 us  [crossed(): return lax.ppermute(block, 'section', [(0, 1), (1, 0)])]
    ppermute x13, starting transfers between devices: 18 us -> 15.6 us  [swapped(): lax.ppermute(block, axis, [(i, i ^ bit) for i in range(lax.axis_size(axis...]
    ppermute x13, waiting for transfers between devices: 20.3 us -> 19.1 us  [swapped(): lax.ppermute(block, axis, [(i, i ^ bit) for i in range(lax.axis_size(axis...]
  transfers between devices with their start and end apart: 19 -> 22, of which waited for: 14 -> 15; matrix products, arithmetic and copies ran while one was open for 0% -> 0% of each run, Pallas kernels for 11% -> 12%
where the time goes in v10:
time: 80.3 us; the launch traced here: 80.1 us
  waiting for transfers between devices  31.7 us (39%)
  starting transfers between devices  26.2 us (33%)
  Pallas kernels  17.1 us (21%)
  local copies, waits for them, and re-layouts  4.17 us (5%)
  between operations  0.84 us (1%)
    ppermute x13, waiting for transfers between devices, swapped(): lax.ppermute(block, axis, [(i, i ^ bit) for i in range(lax.axis_size(axis...  19.1 us
    pallas_call x9, Pallas kernels, call(): pl.pallas_call(kernel, out_shape=arrays, in_specs=[VMEM] * len(args), out...  17.1 us
    ppermute x13, starting transfers between devices, swapped(): lax.ppermute(block, axis, [(i, i ^ bit) for i in range(lax.axis_size(axis...  15.6 us
    ppermute x4, starting transfers between devices, crossed(): return lax.ppermute(block, 'section', [(0, 1), (1, 0)])  5.49 us
    ppermute x3, waiting for transfers between devices, spread(): got.append(lax.ppermute(blocks[turn], 'gy', route))  5.44 us
    ppermute x4, waiting for transfers between devices, crossed(): return lax.ppermute(block, 'section', [(0, 1), (1, 0)])  4.8 us
    ppermute x3, starting transfers between devices, spread(): got.append(lax.ppermute(blocks[turn], 'gy', route))  4.39 us
    unnamed x8, local copies, waits for them, and re-layouts  4.04 us
  transfers between devices with their start and end apart: 22, of which 15 were waited for; matrix products, arithmetic and copies ran while one was open for 0% of the time, Pallas kernels for 12%

profile of v10, /device:TPU:0, one launch (start us, length us, event | category | flops | bytes accessed | tf_op | source)
XLA Modules:
  0.0 80.1 jit_solution(18000451726174058860)
XLA Ops:
  0.6 0.0 copy-start.1
  0.6 0.9 %copy-done.1 = f32[2,64,2,2,128]{4,3,2,1,0:T(2,128)S(1)} copy-done((f32[2,64,2,2,128]{4,3,2,1,0:T(2,128)S(1)}, f32[2,64,2,2,128]{4,3,2,1,0:T(2,128)}, u32[]{:S(2)}) %copy-start.1) | copy-done | bytes 262168
  1.6 0.0 copy-start.2
  1.6 0.9 %copy-done.2 = f32[2,64,2,2,128]{4,3,2,1,0:T(2,128)S(1)} copy-done((f32[2,64,2,2,128]{4,3,2,1,0:T(2,128)S(1)}, f32[2,64,2,2,128]{4,3,2,1,0:T(2,128)}, u32[]{:S(2)}) %copy-start.2) | copy-done | bytes 262168
  2.5 0.2 turn.1
  2.7 0.5 collective-permute-start
  3.2 0.7 collective-permute-start.1
  3.9 0.0 copy-start
  3.9 1.5 %copy-done = f32[2,27,64,64]{3,2,1,0:T(8,128)S(1)} copy-done((f32[2,27,64,64]{3,2,1,0:T(8,128)S(1)}, f32[2,27,64,64]{3,2,1,0:T(8,128)}, u32[]{:S(2)}) %copy-start) | copy-done | bytes 884760
  5.4 0.0 copy-start.3
  5.4 0.7 copy-done.3
  6.1 0.3 pack.1
  6.4 0.0 collective-permute-done.pair
  6.4 0.0 collective-permute-done.1.inner
  6.4 0.1 windows.1
  6.5 2.6 %collective-permute-start.2 = (f32[14,64,128]{2,1,0:T(8,128)S(1)}, f32[14,64,128]{2,1,0:T(8,128)S(1)}, u32[]{:S(2)}, u32[]{:S(2)}) collective-permute-start(f32[14,64,128]{2,1,0:T(8,128)S(1)} %get-tuple-element.67), channel_id=1, source_target_pairs={{0,16},{16,0},{1,17},{17,1},{2,18},{18,2},{3,19},{19,3},{4,20},{20... | collective-permute-start | bytes 1376264 | tf_op jit(solution)/shard_map/ppermute | solution.py:429
  9.1 1.6 %collective-permute-start.3 = (f32[2,88,128]{2,1,0:T(8,128)S(1)}, f32[2,88,128]{2,1,0:T(8,128)S(1)}, u32[]{:S(2)}, u32[]{:S(2)}) collective-permute-start(f32[2,88,128]{2,1,0:T(8,128)S(1)} %get-tuple-element.69), channel_id=1, source_target_pairs={{0,4},{4,0},{8,12},{12,8},{1,5},{5,1},{9,13},{13,9},{2,6},{6,2},{1... | collective-permute-start | bytes 270344 | tf_op jit(solution)/shard_map/ppermute | solution.py:417
  10.7 2.6 %collective-permute-start.4 = (f32[2,88,128]{2,1,0:T(8,128)S(1)}, f32[2,88,128]{2,1,0:T(8,128)S(1)}, u32[]{:S(2)}, u32[]{:S(2)}) collective-permute-start(f32[2,88,128]{2,1,0:T(8,128)S(1)} %get-tuple-element.70), channel_id=1, source_target_pairs={{0,8},{4,12},{8,0},{12,4},{1,9},{5,13},{9,1},{13,5},{2,10},{6,14},... | collective-permute-start | bytes 270344 | tf_op jit(solution)/shard_map/ppermute | solution.py:417
  13.3 0.2 collective-permute-start.5
  13.5 0.7 own_table.1
  14.2 0.0 collective-permute-done.3.refs_1_
  14.2 3.2 %collective-permute-done.4.refs_2_ = f32[2,88,128]{2,1,0:T(8,128)S(1)} collective-permute-done((f32[2,88,128]{2,1,0:T(8,128)S(1)}, f32[2,88,128]{2,1,0:T(8,128)S(1)}, u32[]{:S(2)}, u32[]{:S(2)}) %collective-permute-start.4) | collective-permute-done | bytes 90144 | tf_op jit(solution)/shard_map/ppermute | solution.py:417
  17.4 2.3 %collective-permute-done.5.refs_3_ = f32[2,88,128]{2,1,0:T(8,128)S(1)} collective-permute-done((f32[2,88,128]{2,1,0:T(8,128)S(1)}, f32[2,88,128]{2,1,0:T(8,128)S(1)}, u32[]{:S(2)}, u32[]{:S(2)}) %collective-permute-start.5) | collective-permute-done | bytes 90144 | tf_op jit(solution)/shard_map/ppermute | solution.py:417
  19.6 0.0 collective-permute-done.2.refs_0_
  19.6 1.8 %collective-permute-start.6 = (f32[14,64,128]{2,1,0:T(8,128)S(1)}, f32[14,64,128]{2,1,0:T(8,128)S(1)}, u32[]{:S(2)}, u32[]{:S(2)}) collective-permute-start(f32[14,64,128]{2,1,0:T(8,128)S(1)} %collective-permute-done.2.refs_0_), channel_id=1, source_target_pairs={{0,1},{1,0},{2,3},{3,2},{4,5},{5,4},{6,7},{7,6},{8,9},{9,8},{10,11... | collective-permute-start | bytes 1376264 | tf_op jit(solution)/shard_map/ppermute | solution.py:425
  21.4 0.9 %collective-permute-start.7 = (f32[2,88,128]{2,1,0:T(8,128)S(1)}, f32[2,88,128]{2,1,0:T(8,128)S(1)}, u32[]{:S(2)}, u32[]{:S(2)}) collective-permute-start(f32[2,88,128]{2,1,0:T(8,128)S(1)} %collective-permute-done.3.refs_1_), channel_id=1, source_target_pairs={{0,16},{16,0},{1,17},{17,1},{2,18},{18,2},{3,19},{19,3},{4,20},{20... | collective-permute-start | bytes 270344 | tf_op jit(solution)/shard_map/ppermute | solution.py:429
  22.3 1.1 %collective-permute-start.8 = (f32[2,88,128]{2,1,0:T(8,128)S(1)}, f32[2,88,128]{2,1,0:T(8,128)S(1)}, u32[]{:S(2)}, u32[]{:S(2)}) collective-permute-start(f32[2,88,128]{2,1,0:T(8,128)S(1)} %collective-permute-done.4.refs_2_), channel_id=1, source_target_pairs={{0,16},{16,0},{1,17},{17,1},{2,18},{18,2},{3,19},{19,3},{4,20},{20... | collective-permute-start | bytes 270344 | tf_op jit(solution)/shard_map/ppermute | solution.py:429
  23.5 0.9 %collective-permute-start.9 = (f32[2,88,128]{2,1,0:T(8,128)S(1)}, f32[2,88,128]{2,1,0:T(8,128)S(1)}, u32[]{:S(2)}, u32[]{:S(2)}) collective-permute-start(f32[2,88,128]{2,1,0:T(8,128)S(1)} %collective-permute-done.5.refs_3_), channel_id=1, source_target_pairs={{0,16},{16,0},{1,17},{17,1},{2,18},{18,2},{3,19},{19,3},{4,20},{20... | collective-permute-start | bytes 270344 | tf_op jit(solution)/shard_map/ppermute | solution.py:429
  24.3 0.0 collective-permute-done.6.refs_1_
  24.3 0.7 far_table.1
  25.1 1.8 %collective-permute-done.7.refs_5_ = f32[2,88,128]{2,1,0:T(8,128)S(1)} collective-permute-done((f32[2,88,128]{2,1,0:T(8,128)S(1)}, f32[2,88,128]{2,1,0:T(8,128)S(1)}, u32[]{:S(2)}, u32[]{:S(2)}) %collective-permute-start.7) | collective-permute-done | bytes 90144 | tf_op jit(solution)/shard_map/ppermute | solution.py:429
  26.9 1.9 %collective-permute-done.8.refs_6_ = f32[2,88,128]{2,1,0:T(8,128)S(1)} collective-permute-done((f32[2,88,128]{2,1,0:T(8,128)S(1)}, f32[2,88,128]{2,1,0:T(8,128)S(1)}, u32[]{:S(2)}, u32[]{:S(2)}) %collective-permute-start.8) | collective-permute-done | bytes 90144 | tf_op jit(solution)/shard_map/ppermute | solution.py:429
  28.8 1.1 %collective-permute-done.9.refs_7_ = f32[2,88,128]{2,1,0:T(8,128)S(1)} collective-permute-done((f32[2,88,128]{2,1,0:T(8,128)S(1)}, f32[2,88,128]{2,1,0:T(8,128)S(1)}, u32[]{:S(2)}, u32[]{:S(2)}) %collective-permute-start.9) | collective-permute-done | bytes 90144 | tf_op jit(solution)/shard_map/ppermute | solution.py:429
  29.9 5.3 %forward.1 = (bf16[5,2,480,256]{3,2,1,0:T(8,128)(2,1)S(1)}, f32[4,2,384,128]{3,2,1,0:T(8,128)S(1)}, f32[2,2,32,128]{3,2,1,0:T(8,128)S(1)}, f32[2,2,32,128]{3,2,1...) custom-call(bf16[2,1152,384]{2,1,0:T(8,128)(2,1)S(1)} %get-tuple-element.75.own, ...), custom_call_target="tpu_custom_call" | custom-call | bytes 1024 | tf_op jit(solution)/shard_map/forward/pallas_call | solution.py:24
  35.3 2.8 %collective-permute-start.10 = (f32[2,2,2,32,128]{4,3,2,1,0:T(8,128)S(1)}, f32[2,2,2,32,128]{4,3,2,1,0:T(8,128)S(1)}, u32[]{:S(2)}, u32[]{:S(2)}) collective-permute-start(f32[2,2,2,32,128]{4,3,2,1,0:T(8,128)S(1)} %pad_maximum_fusion.2), channel_id=1, source_target_pairs={{0,8},{4,12},{8,0},{12,4},{1,9},{5,13},{9,1},{13,5},{2,10},{6,14},... | collective-permute-start | bytes 393224 | tf_op jit(solution)/shard_map/ppermute | solution.py:425
  38.1 7.1 %backward.1 = (f32[2,2,32,128]{3,2,1,0:T(8,128)S(1)}, f32[2,2,32,128]{3,2,1,0:T(8,128)S(1)}, f32[2,2,32,128]{3,2,1,0:T(8,128)S(1)}, f32[2,2,32,128]{3,2,1,0:T(8,128)S(1)}, f32[28,64,128]{2,1,0:T(8,128)S(1)}) custom-call(bf16[2,1152,384]{2,1,0:T(8,128)(2,1)S(1)} %get-tuple-element.57.own, bf16[2,1152,384]{2,1,0:T(8,128)(2,1)S(1)} %get-tuple-element.74.other, ...), custom_call_target="tpu_custom_call" | custom-call | flops 4076863488 | bytes 1024 | tf_op jit(solution)/shard_map/backward/pallas_call | solution.py:24
  45.2 0.0 collective-permute-done.10
  45.2 0.1 fusion
  45.3 0.1 collective-permute-start.11
  45.4 1.8 %collective-permute-done.11 = f32[896,128]{1,0:T(8,128)S(1)} collective-permute-done((f32[896,128]{1,0:T(8,128)S(1)}, f32[896,128]{1,0:T(8,128)S(1)}, u32[]{:S(2)}, u32[]{:S(2)}) %collective-permute-start.11) | collective-permute-done | bytes 458784 | tf_op jit(solution)/shard_map/ppermute | solution.py:425
  47.3 1.3 %collective-permute-start.12 = (f32[448,128]{1,0:T(8,128)S(1)}, f32[448,128]{1,0:T(8,128)S(1)}, u32[]{:S(2)}, u32[]{:S(2)}) collective-permute-start(f32[448,128]{1,0:T(8,128)S(1)} %slice.46), channel_id=1, source_target_pairs={{0,2},{1,3},{2,0},{3,1},{4,6},{5,7},{6,4},{7,5},{8,10},{9,11},{10,... | collective-permute-start | bytes 688136 | tf_op jit(solution)/shard_map/ppermute | solution.py:425
  48.6 1.3 %collective-permute-start.13 = (f32[3,2,2,32,128]{4,3,2,1,0:T(8,128)S(1)}, f32[3,2,2,32,128]{4,3,2,1,0:T(8,128)S(1)}, u32[]{:S(2)}, u32[]{:S(2)}) collective-permute-start(f32[3,2,2,32,128]{4,3,2,1,0:T(8,128)S(1)} %pad_maximum_fusion.1), channel_id=1, source_target_pairs={{0,4},{4,0},{8,12},{12,8},{1,5},{5,1},{9,13},{13,9},{2,6},{6,2},{1... | collective-permute-start | bytes 589832 | tf_op jit(solution)/shard_map/ppermute | solution.py:425
  49.9 1.7 %collective-permute-start.14 = (f32[2,2,32,128]{3,2,1,0:T(8,128)S(1)}, f32[2,2,32,128]{3,2,1,0:T(8,128)S(1)}, u32[]{:S(2)}, u32[]{:S(2)}) collective-permute-start(f32[2,2,32,128]{3,2,1,0:T(8,128)S(1)} %get-tuple-element.97), channel_id=1, source_target_pairs={{0,8},{4,12},{8,0},{12,4},{1,9},{5,13},{9,1},{13,5},{2,10},{6,14},... | collective-permute-start | bytes 196616 | tf_op jit(solution)/shard_map/ppermute | solution.py:425
  51.6 1.4 %collective-permute-start.15 = (f32[2,2,32,128]{3,2,1,0:T(8,128)S(1)}, f32[2,2,32,128]{3,2,1,0:T(8,128)S(1)}, u32[]{:S(2)}, u32[]{:S(2)}) collective-permute-start(f32[2,2,32,128]{3,2,1,0:T(8,128)S(1)} %get-tuple-element.98), channel_id=1, source_target_pairs={{0,12},{4,8},{8,4},{12,0},{1,13},{5,9},{9,5},{13,1},{2,14},{6,10},... | collective-permute-start | bytes 196616 | tf_op jit(solution)/shard_map/ppermute | solution.py:425
  53.0 2.0 %collective-permute-done.12 = f32[448,128]{1,0:T(8,128)S(1)} collective-permute-done((f32[448,128]{1,0:T(8,128)S(1)}, f32[448,128]{1,0:T(8,128)S(1)}, u32[]{:S(2)}, u32[]{:S(2)}) %collective-permute-start.12) | collective-permute-done | bytes 229408 | tf_op jit(solution)/shard_map/ppermute | solution.py:425
  55.0 1.2 %collective-permute-done.14.refs_6_ = f32[2,2,32,128]{3,2,1,0:T(8,128)S(1)} collective-permute-done((f32[2,2,32,128]{3,2,1,0:T(8,128)S(1)}, f32[2,2,32,128]{3,2,1,0:T(8,128)S(1)}, u32[]{:S(2)}, u32[]{:S(2)}) %collective-permute-start.14) | collective-permute-done | bytes 65568 | tf_op jit(solution)/shard_map/ppermute | solution.py:425
  56.2 2.6 %collective-permute-done.15.refs_7_ = f32[2,2,32,128]{3,2,1,0:T(8,128)S(1)} collective-permute-done((f32[2,2,32,128]{3,2,1,0:T(8,128)S(1)}, f32[2,2,32,128]{3,2,1,0:T(8,128)S(1)}, u32[]{:S(2)}, u32[]{:S(2)}) %collective-permute-start.15) | collective-permute-done | bytes 65568 | tf_op jit(solution)/shard_map/ppermute | solution.py:425
  58.8 0.0 collective-permute-done.13
  58.8 0.1 collective-permute-start.16
  58.9 4.8 %collective-permute-done.16 = f32[224,128]{1,0:T(8,128)S(1)} collective-permute-done((f32[224,128]{1,0:T(8,128)S(1)}, f32[224,128]{1,0:T(8,128)S(1)}, u32[]{:S(2)}, u32[]{:S(2)}) %collective-permute-start.16) | collective-permute-done | bytes 114720 | tf_op jit(solution)/shard_map/ppermute | solution.py:425
  63.7 1.0 %collective-permute-start.17 = (f32[224,128]{1,0:T(8,128)S(1)}, f32[224,128]{1,0:T(8,128)S(1)}, u32[]{:S(2)}, u32[]{:S(2)}) collective-permute-start(f32[224,128]{1,0:T(8,128)S(1)} %select_add_fusion), channel_id=1, source_target_pairs={{0,8},{4,12},{8,0},{12,4},{1,9},{5,13},{9,1},{13,5},{2,10},{6,14},... | collective-permute-start | bytes 344072 | tf_op jit(solution)/shard_map/ppermute | solution.py:425
  64.7 5.5 %collective-permute-done.17 = f32[224,128]{1,0:T(8,128)S(1)} collective-permute-done((f32[224,128]{1,0:T(8,128)S(1)}, f32[224,128]{1,0:T(8,128)S(1)}, u32[]{:S(2)}, u32[]{:S(2)}) %collective-permute-start.17) | collective-permute-done | bytes 114720 | tf_op jit(solution)/shard_map/ppermute | solution.py:425
  70.3 0.1 collective-permute-start.20
  70.3 0.9 %collective-permute-start.19 = (f32[224,128]{1,0:T(8,128)S(1)}, f32[224,128]{1,0:T(8,128)S(1)}, u32[]{:S(2)}, u32[]{:S(2)}) collective-permute-start(f32[224,128]{1,0:T(8,128)S(1)} %add.20), channel_id=1, source_target_pairs={{0,2},{1,3},{2,0},{3,1},{4,6},{5,7},{6,4},{7,5},{8,10},{9,11},{10,... | collective-permute-start | bytes 344072 | tf_op jit(solution)/shard_map/ppermute | solution.py:425
  71.3 2.5 %collective-permute-start.18 = (f32[224,128]{1,0:T(8,128)S(1)}, f32[224,128]{1,0:T(8,128)S(1)}, u32[]{:S(2)}, u32[]{:S(2)}) collective-permute-start(f32[224,128]{1,0:T(8,128)S(1)} %add.20), channel_id=1, source_target_pairs={{0,4},{4,0},{8,12},{12,8},{1,5},{5,1},{9,13},{13,9},{2,6},{6,2},{1... | collective-permute-start | bytes 344072 | tf_op jit(solution)/shard_map/ppermute | solution.py:425
  73.8 2.3 %collective-permute-done.20 = f32[224,128]{1,0:T(8,128)S(1)} collective-permute-done((f32[224,128]{1,0:T(8,128)S(1)}, f32[224,128]{1,0:T(8,128)S(1)}, u32[]{:S(2)}, u32[]{:S(2)}) %collective-permute-start.20) | collective-permute-done | bytes 114720 | tf_op jit(solution)/shard_map/ppermute | solution.py:438
  76.1 0.3 collective-permute-done.19
  76.4 0.2 collective-permute-done.18
  76.6 0.1 collective-permute-start.21
  76.7 1.0 %restore.1 = (f32[512,128]{1,0:T(8,128)}, f32[512,128]{1,0:T(8,128)}) custom-call(f32[2,2,32,128]{3,2,1,0:T(8,128)S(1)} %get-tuple-element.92.refs_0_, f32[2,2,32,128]{3,2,1,0:T(8,128)S(1)} %get-tuple-element.112.refs_1_, f32[2,2,32,128]{3,2,1,0:T(8,128)S(1)} %get-tuple-element.113.refs_2_, f32[2,2,32,128]{3,2,1,0:T(8,128)S(1)} %get-tuple-element.111.refs_3_, ...), custom_call_target="tpu_custom_call" | custom-call | bytes 1024 | tf_op jit(solution)/shard_map/restore/pallas_call | solution.py:24
  77.7 0.8 %collective-permute-done.21.core = f32[896,128]{1,0:T(8,128)S(1)} collective-permute-done((f32[896,128]{1,0:T(8,128)S(1)}, f32[896,128]{1,0:T(8,128)S(1)}, u32[]{:S(2)}, u32[]{:S(2)}) %collective-permute-start.21) | collective-permute-done | bytes 458784 | tf_op jit(solution)/shard_map/ppermute | solution.py:425
  78.5 1.6 %unpack.1 = (f32[2,27,64,64]{3,2,1,0:T(8,128)}, f32[2,64]{1,0:T(2,128)}) custom-call(f32[896,128]{1,0:T(8,128)S(1)} %pad_maximum_fusion.near, f32[896,128]{1,0:T(8,128)S(1)} %collective-permute-done.21.core), custom_call_target="tpu_custom_call" | custom-call | bytes 1024 | tf_op jit(solution)/shard_map/unpack/pallas_call | solution.py:24
  (11 shorter events, 0.2 us)
Async XLA Ops:
  0.6 1.0 %copy-start.1 = (f32[2,64,2,2,128]{4,3,2,1,0:T(2,128)S(1)}, f32[2,64,2,2,128]{4,3,2,1,0:T(2,128)}, u32[]{:S(2)}) copy-start(f32[2,64,2,2,128]{4,3,2,1,0:T(2,128)} %param.4) | copy-start | bytes 786436
  1.6 0.9 %copy-start.2 = (f32[2,64,2,2,128]{4,3,2,1,0:T(2,128)S(1)}, f32[2,64,2,2,128]{4,3,2,1,0:T(2,128)}, u32[]{:S(2)}) copy-start(f32[2,64,2,2,128]{4,3,2,1,0:T(2,128)} %param.7) | copy-start | bytes 786436
  2.7 3.7 %collective-permute-start = (f32[2,2,2,8,128]{4,3,2,1,0:T(8,128)S(1)}, f32[2,2,2,8,128]{4,3,2,1,0:T(8,128)S(1)}, u32[]{:S(2)}, u32[]{:S(2)}) collective-permute-start(f32[2,2,2,8,128]{4,3,2,1,0:T(8,128)S(1)} %get-tuple-element.60), channel_id=1, source_target_pairs={{0,1},{1,0},{2,3},{3,2},{4,5},{5,4},{6,7},{7,6},{8,9},{9,8},{10,11... | collective-permute-start | bytes 98312 | tf_op jit(solution)/shard_map/ppermute | solution.py:425
  3.2 3.2 %collective-permute-start.1 = (f32[2,2,2,8,128]{4,3,2,1,0:T(8,128)S(1)}, f32[2,2,2,8,128]{4,3,2,1,0:T(8,128)S(1)}, u32[]{:S(2)}, u32[]{:S(2)}) collective-permute-start(f32[2,2,2,8,128]{4,3,2,1,0:T(8,128)S(1)} %get-tuple-element.61), channel_id=1, source_target_pairs={{1,2},{2,1},{5,6},{6,5},{9,10},{10,9},{13,14},{14,13},{17,18},{18,... | collective-permute-start | bytes 98312 | tf_op jit(solution)/shard_map/ppermute | solution.py:465
  3.9 1.5 %copy-start = (f32[2,27,64,64]{3,2,1,0:T(8,128)S(1)}, f32[2,27,64,64]{3,2,1,0:T(8,128)}, u32[]{:S(2)}) copy-start(f32[2,27,64,64]{3,2,1,0:T(8,128)} %weights.1) | copy-start | bytes 2654212
  5.4 0.7 copy-start.3
  6.5 13.1 %collective-permute-start.2 = (f32[14,64,128]{2,1,0:T(8,128)S(1)}, f32[14,64,128]{2,1,0:T(8,128)S(1)}, u32[]{:S(2)}, u32[]{:S(2)}) collective-permute-start(f32[14,64,128]{2,1,0:T(8,128)S(1)} %get-tuple-element.67), channel_id=1, source_target_pairs={{0,16},{16,0},{1,17},{17,1},{2,18},{18,2},{3,19},{19,3},{4,20},{20... | collective-permute-start | bytes 1376264 | tf_op jit(solution)/shard_map/ppermute | solution.py:429
  9.1 5.1 %collective-permute-start.3 = (f32[2,88,128]{2,1,0:T(8,128)S(1)}, f32[2,88,128]{2,1,0:T(8,128)S(1)}, u32[]{:S(2)}, u32[]{:S(2)}) collective-permute-start(f32[2,88,128]{2,1,0:T(8,128)S(1)} %get-tuple-element.69), channel_id=1, source_target_pairs={{0,4},{4,0},{8,12},{12,8},{1,5},{5,1},{9,13},{13,9},{2,6},{6,2},{1... | collective-permute-start | bytes 270344 | tf_op jit(solution)/shard_map/ppermute | solution.py:417
  10.7 6.7 %collective-permute-start.4 = (f32[2,88,128]{2,1,0:T(8,128)S(1)}, f32[2,88,128]{2,1,0:T(8,128)S(1)}, u32[]{:S(2)}, u32[]{:S(2)}) collective-permute-start(f32[2,88,128]{2,1,0:T(8,128)S(1)} %get-tuple-element.70), channel_id=1, source_target_pairs={{0,8},{4,12},{8,0},{12,4},{1,9},{5,13},{9,1},{13,5},{2,10},{6,14},... | collective-permute-start | bytes 270344 | tf_op jit(solution)/shard_map/ppermute | solution.py:417
  13.3 6.3 %collective-permute-start.5 = (f32[2,88,128]{2,1,0:T(8,128)S(1)}, f32[2,88,128]{2,1,0:T(8,128)S(1)}, u32[]{:S(2)}, u32[]{:S(2)}) collective-permute-start(f32[2,88,128]{2,1,0:T(8,128)S(1)} %get-tuple-element.71), channel_id=1, source_target_pairs={{0,12},{4,8},{8,4},{12,0},{1,13},{5,9},{9,5},{13,1},{2,14},{6,10},... | collective-permute-start | bytes 270344 | tf_op jit(solution)/shard_map/ppermute | solution.py:417
  19.6 4.7 %collective-permute-start.6 = (f32[14,64,128]{2,1,0:T(8,128)S(1)}, f32[14,64,128]{2,1,0:T(8,128)S(1)}, u32[]{:S(2)}, u32[]{:S(2)}) collective-permute-start(f32[14,64,128]{2,1,0:T(8,128)S(1)} %collective-permute-done.2.refs_0_), channel_id=1, source_target_pairs={{0,1},{1,0},{2,3},{3,2},{4,5},{5,4},{6,7},{7,6},{8,9},{9,8},{10,11... | collective-permute-start | bytes 1376264 | tf_op jit(solution)/shard_map/ppermute | solution.py:425
  21.4 5.5 %collective-permute-start.7 = (f32[2,88,128]{2,1,0:T(8,128)S(1)}, f32[2,88,128]{2,1,0:T(8,128)S(1)}, u32[]{:S(2)}, u32[]{:S(2)}) collective-permute-start(f32[2,88,128]{2,1,0:T(8,128)S(1)} %collective-permute-done.3.refs_1_), channel_id=1, source_target_pairs={{0,16},{16,0},{1,17},{17,1},{2,18},{18,2},{3,19},{19,3},{4,20},{20... | collective-permute-start | bytes 270344 | tf_op jit(solution)/shard_map/ppermute | solution.py:429
  22.3 6.5 %collective-permute-start.8 = (f32[2,88,128]{2,1,0:T(8,128)S(1)}, f32[2,88,128]{2,1,0:T(8,128)S(1)}, u32[]{:S(2)}, u32[]{:S(2)}) collective-permute-start(f32[2,88,128]{2,1,0:T(8,128)S(1)} %collective-permute-done.4.refs_2_), channel_id=1, source_target_pairs={{0,16},{16,0},{1,17},{17,1},{2,18},{18,2},{3,19},{19,3},{4,20},{20... | collective-permute-start | bytes 270344 | tf_op jit(solution)/shard_map/ppermute | solution.py:429
  23.5 6.4 %collective-permute-start.9 = (f32[2,88,128]{2,1,0:T(8,128)S(1)}, f32[2,88,128]{2,1,0:T(8,128)S(1)}, u32[]{:S(2)}, u32[]{:S(2)}) collective-permute-start(f32[2,88,128]{2,1,0:T(8,128)S(1)} %collective-permute-done.5.refs_3_), channel_id=1, source_target_pairs={{0,16},{16,0},{1,17},{17,1},{2,18},{18,2},{3,19},{19,3},{4,20},{20... | collective-permute-start | bytes 270344 | tf_op jit(solution)/shard_map/ppermute | solution.py:429
  35.3 10.0 %collective-permute-start.10 = (f32[2,2,2,32,128]{4,3,2,1,0:T(8,128)S(1)}, f32[2,2,2,32,128]{4,3,2,1,0:T(8,128)S(1)}, u32[]{:S(2)}, u32[]{:S(2)}) collective-permute-start(f32[2,2,2,32,128]{4,3,2,1,0:T(8,128)S(1)} %pad_maximum_fusion.2), channel_id=1, source_target_pairs={{0,8},{4,12},{8,0},{12,4},{1,9},{5,13},{9,1},{13,5},{2,10},{6,14},... | collective-permute-start | bytes 393224 | tf_op jit(solution)/shard_map/ppermute | solution.py:425
  45.3 1.9 %collective-permute-start.11 = (f32[896,128]{1,0:T(8,128)S(1)}, f32[896,128]{1,0:T(8,128)S(1)}, u32[]{:S(2)}, u32[]{:S(2)}) collective-permute-start(f32[896,128]{1,0:T(8,128)S(1)} %bitcast.25), channel_id=1, source_target_pairs={{0,1},{1,0},{2,3},{3,2},{4,5},{5,4},{6,7},{7,6},{8,9},{9,8},{10,11... | collective-permute-start | bytes 1376264 | tf_op jit(solution)/shard_map/ppermute | solution.py:425
  47.3 7.7 %collective-permute-start.12 = (f32[448,128]{1,0:T(8,128)S(1)}, f32[448,128]{1,0:T(8,128)S(1)}, u32[]{:S(2)}, u32[]{:S(2)}) collective-permute-start(f32[448,128]{1,0:T(8,128)S(1)} %slice.46), channel_id=1, source_target_pairs={{0,2},{1,3},{2,0},{3,1},{4,6},{5,7},{6,4},{7,5},{8,10},{9,11},{10,... | collective-permute-start | bytes 688136 | tf_op jit(solution)/shard_map/ppermute | solution.py:425
  48.6 10.2 %collective-permute-start.13 = (f32[3,2,2,32,128]{4,3,2,1,0:T(8,128)S(1)}, f32[3,2,2,32,128]{4,3,2,1,0:T(8,128)S(1)}, u32[]{:S(2)}, u32[]{:S(2)}) collective-permute-start(f32[3,2,2,32,128]{4,3,2,1,0:T(8,128)S(1)} %pad_maximum_fusion.1), channel_id=1, source_target_pairs={{0,4},{4,0},{8,12},{12,8},{1,5},{5,1},{9,13},{13,9},{2,6},{6,2},{1... | collective-permute-start | bytes 589832 | tf_op jit(solution)/shard_map/ppermute | solution.py:425
  49.9 6.3 %collective-permute-start.14 = (f32[2,2,32,128]{3,2,1,0:T(8,128)S(1)}, f32[2,2,32,128]{3,2,1,0:T(8,128)S(1)}, u32[]{:S(2)}, u32[]{:S(2)}) collective-permute-start(f32[2,2,32,128]{3,2,1,0:T(8,128)S(1)} %get-tuple-element.97), channel_id=1, source_target_pairs={{0,8},{4,12},{8,0},{12,4},{1,9},{5,13},{9,1},{13,5},{2,10},{6,14},... | collective-permute-start | bytes 196616 | tf_op jit(solution)/shard_map/ppermute | solution.py:425
  51.6 7.2 %collective-permute-start.15 = (f32[2,2,32,128]{3,2,1,0:T(8,128)S(1)}, f32[2,2,32,128]{3,2,1,0:T(8,128)S(1)}, u32[]{:S(2)}, u32[]{:S(2)}) collective-permute-start(f32[2,2,32,128]{3,2,1,0:T(8,128)S(1)} %get-tuple-element.98), channel_id=1, source_target_pairs={{0,12},{4,8},{8,4},{12,0},{1,13},{5,9},{9,5},{13,1},{2,14},{6,10},... | collective-permute-start | bytes 196616 | tf_op jit(solution)/shard_map/ppermute | solution.py:425
  58.8 4.9 %collective-permute-start.16 = (f32[224,128]{1,0:T(8,128)S(1)}, f32[224,128]{1,0:T(8,128)S(1)}, u32[]{:S(2)}, u32[]{:S(2)}) collective-permute-start(f32[224,128]{1,0:T(8,128)S(1)} %slice_select_fusion), channel_id=1, source_target_pairs={{0,4},{4,0},{8,12},{12,8},{1,5},{5,1},{9,13},{13,9},{2,6},{6,2},{1... | collective-permute-start | bytes 344072 | tf_op jit(solution)/shard_map/ppermute | solution.py:425
  63.7 6.5 %collective-permute-start.17 = (f32[224,128]{1,0:T(8,128)S(1)}, f32[224,128]{1,0:T(8,128)S(1)}, u32[]{:S(2)}, u32[]{:S(2)}) collective-permute-start(f32[224,128]{1,0:T(8,128)S(1)} %select_add_fusion), channel_id=1, source_target_pairs={{0,8},{4,12},{8,0},{12,4},{1,9},{5,13},{9,1},{13,5},{2,10},{6,14},... | collective-permute-start | bytes 344072 | tf_op jit(solution)/shard_map/ppermute | solution.py:425
  70.3 5.9 %collective-permute-start.20 = (f32[224,128]{1,0:T(8,128)S(1)}, f32[224,128]{1,0:T(8,128)S(1)}, u32[]{:S(2)}, u32[]{:S(2)}) collective-permute-start(f32[224,128]{1,0:T(8,128)S(1)} %add.20), channel_id=1, source_target_pairs={{0,6},{1,7},{2,4},{3,5},{4,2},{5,3},{6,0},{7,1},{8,14},{9,15},{10,... | collective-permute-start | bytes 344072 | tf_op jit(solution)/shard_map/ppermute | solution.py:438
  70.3 6.1 %collective-permute-start.19 = (f32[224,128]{1,0:T(8,128)S(1)}, f32[224,128]{1,0:T(8,128)S(1)}, u32[]{:S(2)}, u32[]{:S(2)}) collective-permute-start(f32[224,128]{1,0:T(8,128)S(1)} %add.20), channel_id=1, source_target_pairs={{0,2},{1,3},{2,0},{3,1},{4,6},{5,7},{6,4},{7,5},{8,10},{9,11},{10,... | collective-permute-start | bytes 344072 | tf_op jit(solution)/shard_map/ppermute | solution.py:425
  71.3 5.3 %collective-permute-start.18 = (f32[224,128]{1,0:T(8,128)S(1)}, f32[224,128]{1,0:T(8,128)S(1)}, u32[]{:S(2)}, u32[]{:S(2)}) collective-permute-start(f32[224,128]{1,0:T(8,128)S(1)} %add.20), channel_id=1, source_target_pairs={{0,4},{4,0},{8,12},{12,8},{1,5},{5,1},{9,13},{13,9},{2,6},{6,2},{1... | collective-permute-start | bytes 344072 | tf_op jit(solution)/shard_map/ppermute | solution.py:425
  76.6 1.9 %collective-permute-start.21 = (f32[896,128]{1,0:T(8,128)S(1)}, f32[896,128]{1,0:T(8,128)S(1)}, u32[]{:S(2)}, u32[]{:S(2)}) collective-permute-start(f32[896,128]{1,0:T(8,128)S(1)} %pad_maximum_fusion.near), channel_id=1, source_target_pairs={{0,1},{1,0},{2,3},{3,2},{4,5},{5,4},{6,7},{7,6},{8,9},{9,8},{10,11... | collective-permute-start | bytes 1376264 | tf_op jit(solution)/shard_map/ppermute | solution.py:425

commit v11 on v10

--- a/solution.py
+++ b/solution.py
@@ -116,17 +116,23 @@
         for c in range(3):
             taps = [block_of(9 * a + 3 * b + c) for a in range(3)]
             for layer in range(2):
-                lanes = slice(layer * chans, (layer + 1) * chans)
-                below, level, above = [tap[:, lanes] for tap in taps]
+                own_lanes = slice(layer * chans, (layer + 1) * chans)
+                below, level, above = [tap[:, own_lanes] for tap in taps]
                 top = jnp.concatenate([level, above], axis=1)
                 low = jnp.concatenate([below, level], axis=1)
                 block = jnp.concatenate([top, low], axis=0)
                 for target, value, r, at in ((fwd, block.T, b, c), (bwd, block, 2 - b, 2 - c)):
                     hi, lo = split_terms(value)
-                    at = slice(at * LANES, (at + 1) * LANES)
-                    target[layer, 2 * r * LANES : (2 * r + 1) * LANES, at] = hi
-                    target[layer, (2 * r + 1) * LANES : (2 * r + 2) * LANES, at] = hi
-                    target[layer, (6 + r) * LANES : (7 + r) * LANES, at] = lo
+                    if at == 1:
+                        for row_at in (9 + 2 * r, 10 + 2 * r):
+                            rows = slice(row_at * LANES, (row_at + 1) * LANES)
+                            target[layer, rows, 0:LANES] = hi
+                            target[layer, rows, LANES : 2 * LANES] = lo
+                    else:
+                        lanes = slice(at // 2 * LANES, (at // 2 + 1) * LANES)
+                        for row_at, term in ((2 * r, hi), (2 * r + 1, hi), (6 + r, lo)):
+                            rows = slice(row_at * LANES, (row_at + 1) * LANES)
+                            target[layer, rows, lanes] = term
     last = block_of(TAPS)[0:1, :]
     for layer in range(2):
         part = last[:, layer * chans : (layer + 1) * chans]
@@ -178,10 +184,15 @@
             lefts.append(jnp.concatenate(pieces + [piece[:, :LANES] for piece in pieces], axis=1))
         results = []
         for left in lefts:
-            out = jnp.dot(left, table[...], preferred_element_type=F32)
-            before = pltpu.roll(out[:, :LANES], 1, 0)
-            after = pltpu.roll(out[:, 2 * LANES :], out.shape[0] - 1, 0)
-            results.append(before + out[:, LANES : 2 * LANES] + after)
+            outer = jnp.dot(left, table[0 : 9 * LANES, :], preferred_element_type=F32)
+            middle = jnp.dot(
+                left[:, 0 : 6 * LANES],
+                table[9 * LANES : 15 * LANES, :],
+                preferred_element_type=F32,
+            )
+            before = pltpu.roll(outer[:, :LANES], 1, 0)
+            after = pltpu.roll(outer[:, LANES:], outer.shape[0] - 1, 0)
+            results.append(before + (middle[:, :LANES] + middle[:, LANES:]) + after)
         return results
 
     def by_owner(self, layer, own, other, body):
@@ -475,14 +486,15 @@
     *mine, home = windows
     mine = spread(mine)
 
-    tables = [((2, 9 * LANES, 3 * LANES), BF16)] * 2 + [((2, 8, LANES), F32)]
+    tables = [((2, 15 * LANES, 2 * LANES), BF16)] * 2 + [((2, 8, LANES), F32)]
     own_fwd, own_bwd, own_row = call(table_kernel, "own_table", tables, [own])
     if slabs <= 8:
         theirs = [home] + [crossed(window) for window in mine[1:]]
     else:
         theirs = list(crossed(jnp.stack(mine)))
     windows = mine + theirs
-    near_half, mine, own_row = lax.optimization_barrier((near_half, mine, own_row))
+    gate = [*theirs[1:3], *mine[3:]]
+    near_half, own_row, *_ = lax.optimization_barrier((near_half, own_row, *gate))
     far_half = swapped(near_half, 1)
     far_fwd, far_bwd, far_row = call(table_kernel, "far_table", tables, [near_half, far_half])
 

time: 80.3 us -> 79.9 us (level)
  waiting for transfers between devices: 31.7 us -> 33.6 us
  Pallas kernels: 17.1 us -> 15.7 us
  starting transfers between devices: 26.2 us -> 25.2 us
    ppermute x13, waiting for transfers between devices: 19.1 us -> 21 us  [swapped(): lax.ppermute(block, axis, [(i, i ^ bit) for i in range(lax.axis_size(axis...]
    pallas_call x9, Pallas kernels: 17.1 us -> 15.7 us  [call(): pl.pallas_call(kernel, out_shape=arrays, in_specs=[VMEM] * len(args), out...]
    ppermute x4, starting transfers between devices: 5.49 us -> 4.67 us  [crossed(): return lax.ppermute(block, 'section', [(0, 1), (1, 0)])]
    ppermute x4, waiting for transfers between devices: 4.8 us -> 5.62 us  [crossed(): return lax.ppermute(block, 'section', [(0, 1), (1, 0)])]
  transfers between devices with their start and end apart: 22 -> 22, of which waited for: 15 -> 17; matrix products, arithmetic and copies ran while one was open for 0% -> 0% of each run, Pallas kernels for 12% -> 12%
where the time goes in v11:
time: 79.9 us; the launch traced here: 79.7 us
  waiting for transfers between devices  33.6 us (42%)
  starting transfers between devices  25.2 us (32%)
  Pallas kernels  15.7 us (20%)
  local copies, waits for them, and re-layouts  4.17 us (5%)
  between operations  0.84 us (1%)
    ppermute x13, waiting for transfers between devices, swapped(): lax.ppermute(block, axis, [(i, i ^ bit) for i in range(lax.axis_size(axis...  21 us
    pallas_call x9, Pallas kernels, call(): pl.pallas_call(kernel, out_shape=arrays, in_specs=[VMEM] * len(args), out...  15.7 us
    ppermute x13, starting transfers between devices, swapped(): lax.ppermute(block, axis, [(i, i ^ bit) for i in range(lax.axis_size(axis...  15.4 us
    ppermute x4, waiting for transfers between devices, crossed(): return lax.ppermute(block, 'section', [(0, 1), (1, 0)])  5.62 us
    ppermute x3, waiting for transfers between devices, spread(): got.append(lax.ppermute(blocks[turn], 'gy', route))  4.7 us
    ppermute x4, starting transfers between devices, crossed(): return lax.ppermute(block, 'section', [(0, 1), (1, 0)])  4.67 us
    ppermute x3, starting transfers between devices, spread(): got.append(lax.ppermute(blocks[turn], 'gy', route))  4.39 us
    unnamed x8, local copies, waits for them, and re-layouts  4.04 us
  transfers between devices with their start and end apart: 22, of which 17 were waited for; matrix products, arithmetic and copies ran while one was open for 0% of the time, Pallas kernels for 12%

profile of v11, /device:TPU:0, one launch (start us, length us, event | category | flops | bytes accessed | tf_op | source)
XLA Modules:
  0.0 79.7 jit_solution(1643941358759883862)
XLA Ops:
  0.6 0.0 copy-start.1
  0.6 0.9 %copy-done.1 = f32[2,64,2,2,128]{4,3,2,1,0:T(2,128)S(1)} copy-done((f32[2,64,2,2,128]{4,3,2,1,0:T(2,128)S(1)}, f32[2,64,2,2,128]{4,3,2,1,0:T(2,128)}, u32[]{:S(2)}) %copy-start.1) | copy-done | bytes 262168
  1.6 0.0 copy-start.2
  1.6 0.9 %copy-done.2 = f32[2,64,2,2,128]{4,3,2,1,0:T(2,128)S(1)} copy-done((f32[2,64,2,2,128]{4,3,2,1,0:T(2,128)S(1)}, f32[2,64,2,2,128]{4,3,2,1,0:T(2,128)}, u32[]{:S(2)}) %copy-start.2) | copy-done | bytes 262168
  2.5 0.2 turn.1
  2.7 0.5 collective-permute-start
  3.2 0.7 collective-permute-start.1
  3.9 0.0 copy-start
  3.9 1.5 %copy-done = f32[2,27,64,64]{3,2,1,0:T(8,128)S(1)} copy-done((f32[2,27,64,64]{3,2,1,0:T(8,128)S(1)}, f32[2,27,64,64]{3,2,1,0:T(8,128)}, u32[]{:S(2)}) %copy-start) | copy-done | bytes 884760
  5.4 0.0 copy-start.3
  5.4 0.7 copy-done.3
  6.1 0.3 pack.1
  6.4 0.0 collective-permute-done.pair
  6.4 0.0 collective-permute-done.1.inner
  6.4 0.1 windows.1
  6.5 2.6 %collective-permute-start.2 = (f32[14,64,128]{2,1,0:T(8,128)S(1)}, f32[14,64,128]{2,1,0:T(8,128)S(1)}, u32[]{:S(2)}, u32[]{:S(2)}) collective-permute-start(f32[14,64,128]{2,1,0:T(8,128)S(1)} %get-tuple-element.67), channel_id=1, source_target_pairs={{0,16},{16,0},{1,17},{17,1},{2,18},{18,2},{3,19},{19,3},{4,20},{20... | collective-permute-start | bytes 1376264 | tf_op jit(solution)/shard_map/ppermute | solution.py:440
  9.1 1.6 %collective-permute-start.3 = (f32[2,88,128]{2,1,0:T(8,128)S(1)}, f32[2,88,128]{2,1,0:T(8,128)S(1)}, u32[]{:S(2)}, u32[]{:S(2)}) collective-permute-start(f32[2,88,128]{2,1,0:T(8,128)S(1)} %get-tuple-element.69), channel_id=1, source_target_pairs={{0,4},{4,0},{8,12},{12,8},{1,5},{5,1},{9,13},{13,9},{2,6},{6,2},{1... | collective-permute-start | bytes 270344 | tf_op jit(solution)/shard_map/ppermute | solution.py:428
  10.7 2.6 %collective-permute-start.5 = (f32[2,88,128]{2,1,0:T(8,128)S(1)}, f32[2,88,128]{2,1,0:T(8,128)S(1)}, u32[]{:S(2)}, u32[]{:S(2)}) collective-permute-start(f32[2,88,128]{2,1,0:T(8,128)S(1)} %get-tuple-element.70), channel_id=1, source_target_pairs={{0,8},{4,12},{8,0},{12,4},{1,9},{5,13},{9,1},{13,5},{2,10},{6,14},... | collective-permute-start | bytes 270344 | tf_op jit(solution)/shard_map/ppermute | solution.py:428
  13.3 0.2 collective-permute-start.7
  13.5 0.1 collective-permute-done.3.refs_1_
  13.6 0.2 collective-permute-start.4
  13.8 3.6 %collective-permute-done.5.refs_2_ = f32[2,88,128]{2,1,0:T(8,128)S(1)} collective-permute-done((f32[2,88,128]{2,1,0:T(8,128)S(1)}, f32[2,88,128]{2,1,0:T(8,128)S(1)}, u32[]{:S(2)}, u32[]{:S(2)}) %collective-permute-start.5) | collective-permute-done | bytes 90144 | tf_op jit(solution)/shard_map/ppermute | solution.py:428
  17.4 0.5 collective-permute-start.6
  17.9 0.7 own_table.1
  18.6 1.0 %collective-permute-done.7.refs_3_ = f32[2,88,128]{2,1,0:T(8,128)S(1)} collective-permute-done((f32[2,88,128]{2,1,0:T(8,128)S(1)}, f32[2,88,128]{2,1,0:T(8,128)S(1)}, u32[]{:S(2)}, u32[]{:S(2)}) %collective-permute-start.7) | collective-permute-done | bytes 90144 | tf_op jit(solution)/shard_map/ppermute | solution.py:428
  19.6 0.3 collective-permute-done.4.refs_5_
  19.9 3.0 %collective-permute-done.6.refs_6_ = f32[2,88,128]{2,1,0:T(8,128)S(1)} collective-permute-done((f32[2,88,128]{2,1,0:T(8,128)S(1)}, f32[2,88,128]{2,1,0:T(8,128)S(1)}, u32[]{:S(2)}, u32[]{:S(2)}) %collective-permute-start.6) | collective-permute-done | bytes 90144 | tf_op jit(solution)/shard_map/ppermute | solution.py:440
  22.9 0.0 collective-permute-done.2.refs_0_
  22.9 1.9 %collective-permute-start.8 = (f32[14,64,128]{2,1,0:T(8,128)S(1)}, f32[14,64,128]{2,1,0:T(8,128)S(1)}, u32[]{:S(2)}, u32[]{:S(2)}) collective-permute-start(f32[14,64,128]{2,1,0:T(8,128)S(1)} %collective-permute-done.2.refs_0_), channel_id=1, source_target_pairs={{0,1},{1,0},{2,3},{3,2},{4,5},{5,4},{6,7},{7,6},{8,9},{9,8},{10,11... | collective-permute-start | bytes 1376264 | tf_op jit(solution)/shard_map/ppermute | solution.py:436
  24.8 1.4 %collective-permute-start.9 = (f32[2,88,128]{2,1,0:T(8,128)S(1)}, f32[2,88,128]{2,1,0:T(8,128)S(1)}, u32[]{:S(2)}, u32[]{:S(2)}) collective-permute-start(f32[2,88,128]{2,1,0:T(8,128)S(1)} %collective-permute-done.7.refs_3_), channel_id=1, source_target_pairs={{0,16},{16,0},{1,17},{17,1},{2,18},{18,2},{3,19},{19,3},{4,20},{20... | collective-permute-start | bytes 270344 | tf_op jit(solution)/shard_map/ppermute | solution.py:440
  26.2 0.1 collective-permute-done.8.refs_1_
  26.3 0.8 far_table.1
  27.0 2.3 %collective-permute-done.9.refs_7_ = f32[2,88,128]{2,1,0:T(8,128)S(1)} collective-permute-done((f32[2,88,128]{2,1,0:T(8,128)S(1)}, f32[2,88,128]{2,1,0:T(8,128)S(1)}, u32[]{:S(2)}, u32[]{:S(2)}) %collective-permute-start.9) | collective-permute-done | bytes 90144 | tf_op jit(solution)/shard_map/ppermute | solution.py:440
  29.3 4.5 %forward.1 = (bf16[5,2,480,256]{3,2,1,0:T(8,128)(2,1)S(1)}, f32[4,2,384,128]{3,2,1,0:T(8,128)S(1)}, f32[2,2,32,128]{3,2,1,0:T(8,128)S(1)}, f32[2,2,32,128]{3,2,1...) custom-call(bf16[2,1920,256]{2,1,0:T(8,128)(2,1)S(1)} %get-tuple-element.74.own, ...), custom_call_target="tpu_custom_call" | custom-call | bytes 1024 | tf_op jit(solution)/shard_map/forward/pallas_call | solution.py:24
  33.9 2.5 %collective-permute-start.10 = (f32[2,2,2,32,128]{4,3,2,1,0:T(8,128)S(1)}, f32[2,2,2,32,128]{4,3,2,1,0:T(8,128)S(1)}, u32[]{:S(2)}, u32[]{:S(2)}) collective-permute-start(f32[2,2,2,32,128]{4,3,2,1,0:T(8,128)S(1)} %pad_maximum_fusion.2), channel_id=1, source_target_pairs={{0,8},{4,12},{8,0},{12,4},{1,9},{5,13},{9,1},{13,5},{2,10},{6,14},... | collective-permute-start | bytes 393224 | tf_op jit(solution)/shard_map/ppermute | solution.py:436
  36.4 6.5 %backward.1 = (f32[2,2,32,128]{3,2,1,0:T(8,128)S(1)}, f32[2,2,32,128]{3,2,1,0:T(8,128)S(1)}, f32[2,2,32,128]{3,2,1,0:T(8,128)S(1)}, f32[2,2,32,128]{3,2,1,0:T(8,128)S(1)}, f32[28,64,128]{2,1,0:T(8,128)S(1)}) custom-call(bf16[2,1920,256]{2,1,0:T(8,128)(2,1)S(1)} %get-tuple-element.57.own, bf16[2,1920,256]{2,1,0:T(8,128)(2,1)S(1)} %get-tuple-element.73.other, ...), custom_call_target="tpu_custom_call" | custom-call | flops 4076863488 | bytes 1024 | tf_op jit(solution)/shard_map/backward/pallas_call | solution.py:24
  42.9 0.0 collective-permute-done.10
  42.9 0.1 fusion
  43.0 0.1 collective-permute-start.11
  43.1 1.8 %collective-permute-done.11 = f32[896,128]{1,0:T(8,128)S(1)} collective-permute-done((f32[896,128]{1,0:T(8,128)S(1)}, f32[896,128]{1,0:T(8,128)S(1)}, u32[]{:S(2)}, u32[]{:S(2)}) %collective-permute-start.11) | collective-permute-done | bytes 458784 | tf_op jit(solution)/shard_map/ppermute | solution.py:436
  45.0 1.8 %collective-permute-start.12 = (f32[448,128]{1,0:T(8,128)S(1)}, f32[448,128]{1,0:T(8,128)S(1)}, u32[]{:S(2)}, u32[]{:S(2)}) collective-permute-start(f32[448,128]{1,0:T(8,128)S(1)} %slice.46), channel_id=1, source_target_pairs={{0,2},{1,3},{2,0},{3,1},{4,6},{5,7},{6,4},{7,5},{8,10},{9,11},{10,... | collective-permute-start | bytes 688136 | tf_op jit(solution)/shard_map/ppermute | solution.py:436
  46.9 1.6 %collective-permute-start.13 = (f32[3,2,2,32,128]{4,3,2,1,0:T(8,128)S(1)}, f32[3,2,2,32,128]{4,3,2,1,0:T(8,128)S(1)}, u32[]{:S(2)}, u32[]{:S(2)}) collective-permute-start(f32[3,2,2,32,128]{4,3,2,1,0:T(8,128)S(1)} %pad_maximum_fusion.1), channel_id=1, source_target_pairs={{0,4},{4,0},{8,12},{12,8},{1,5},{5,1},{9,13},{13,9},{2,6},{6,2},{1... | collective-permute-start | bytes 589832 | tf_op jit(solution)/shard_map/ppermute | solution.py:436
  48.5 2.2 %collective-permute-start.14 = (f32[2,2,32,128]{3,2,1,0:T(8,128)S(1)}, f32[2,2,32,128]{3,2,1,0:T(8,128)S(1)}, u32[]{:S(2)}, u32[]{:S(2)}) collective-permute-start(f32[2,2,32,128]{3,2,1,0:T(8,128)S(1)} %get-tuple-element.97), channel_id=1, source_target_pairs={{0,8},{4,12},{8,0},{12,4},{1,9},{5,13},{9,1},{13,5},{2,10},{6,14},... | collective-permute-start | bytes 196616 | tf_op jit(solution)/shard_map/ppermute | solution.py:436
  50.7 0.6 collective-permute-start.15
  51.3 1.4 %collective-permute-done.12 = f32[448,128]{1,0:T(8,128)S(1)} collective-permute-done((f32[448,128]{1,0:T(8,128)S(1)}, f32[448,128]{1,0:T(8,128)S(1)}, u32[]{:S(2)}, u32[]{:S(2)}) %collective-permute-start.12) | collective-permute-done | bytes 229408 | tf_op jit(solution)/shard_map/ppermute | solution.py:436
  52.8 2.0 %collective-permute-done.14.refs_6_ = f32[2,2,32,128]{3,2,1,0:T(8,128)S(1)} collective-permute-done((f32[2,2,32,128]{3,2,1,0:T(8,128)S(1)}, f32[2,2,32,128]{3,2,1,0:T(8,128)S(1)}, u32[]{:S(2)}, u32[]{:S(2)}) %collective-permute-start.14) | collective-permute-done | bytes 65568 | tf_op jit(solution)/shard_map/ppermute | solution.py:436
  54.8 3.1 %collective-permute-done.15.refs_7_ = f32[2,2,32,128]{3,2,1,0:T(8,128)S(1)} collective-permute-done((f32[2,2,32,128]{3,2,1,0:T(8,128)S(1)}, f32[2,2,32,128]{3,2,1,0:T(8,128)S(1)}, u32[]{:S(2)}, u32[]{:S(2)}) %collective-permute-start.15) | collective-permute-done | bytes 65568 | tf_op jit(solution)/shard_map/ppermute | solution.py:436
  57.9 0.0 collective-permute-done.13
  57.9 0.1 collective-permute-start.16
  58.0 4.8 %collective-permute-done.16 = f32[224,128]{1,0:T(8,128)S(1)} collective-permute-done((f32[224,128]{1,0:T(8,128)S(1)}, f32[224,128]{1,0:T(8,128)S(1)}, u32[]{:S(2)}, u32[]{:S(2)}) %collective-permute-start.16) | collective-permute-done | bytes 114720 | tf_op jit(solution)/shard_map/ppermute | solution.py:436
  62.8 0.5 collective-permute-start.17
  63.3 5.9 %collective-permute-done.17 = f32[224,128]{1,0:T(8,128)S(1)} collective-permute-done((f32[224,128]{1,0:T(8,128)S(1)}, f32[224,128]{1,0:T(8,128)S(1)}, u32[]{:S(2)}, u32[]{:S(2)}) %collective-permute-start.17) | collective-permute-done | bytes 114720 | tf_op jit(solution)/shard_map/ppermute | solution.py:436
  69.2 0.1 collective-permute-start.20
  69.3 0.9 %collective-permute-start.19 = (f32[224,128]{1,0:T(8,128)S(1)}, f32[224,128]{1,0:T(8,128)S(1)}, u32[]{:S(2)}, u32[]{:S(2)}) collective-permute-start(f32[224,128]{1,0:T(8,128)S(1)} %add.20), channel_id=1, source_target_pairs={{0,2},{1,3},{2,0},{3,1},{4,6},{5,7},{6,4},{7,5},{8,10},{9,11},{10,... | collective-permute-start | bytes 344072 | tf_op jit(solution)/shard_map/ppermute | solution.py:436
  70.2 2.6 %collective-permute-start.18 = (f32[224,128]{1,0:T(8,128)S(1)}, f32[224,128]{1,0:T(8,128)S(1)}, u32[]{:S(2)}, u32[]{:S(2)}) collective-permute-start(f32[224,128]{1,0:T(8,128)S(1)} %add.20), channel_id=1, source_target_pairs={{0,4},{4,0},{8,12},{12,8},{1,5},{5,1},{9,13},{13,9},{2,6},{6,2},{1... | collective-permute-start | bytes 344072 | tf_op jit(solution)/shard_map/ppermute | solution.py:436
  72.8 2.3 %collective-permute-done.20 = f32[224,128]{1,0:T(8,128)S(1)} collective-permute-done((f32[224,128]{1,0:T(8,128)S(1)}, f32[224,128]{1,0:T(8,128)S(1)}, u32[]{:S(2)}, u32[]{:S(2)}) %collective-permute-start.20) | collective-permute-done | bytes 114720 | tf_op jit(solution)/shard_map/ppermute | solution.py:449
  75.1 0.3 collective-permute-done.19
  75.4 0.8 collective-permute-done.18
  76.2 0.1 collective-permute-start.21
  76.3 1.0 %restore.1 = (f32[512,128]{1,0:T(8,128)}, f32[512,128]{1,0:T(8,128)}) custom-call(f32[2,2,32,128]{3,2,1,0:T(8,128)S(1)} %get-tuple-element.92.refs_0_, f32[2,2,32,128]{3,2,1,0:T(8,128)S(1)} %get-tuple-element.112.refs_1_, f32[2,2,32,128]{3,2,1,0:T(8,128)S(1)} %get-tuple-element.113.refs_2_, f32[2,2,32,128]{3,2,1,0:T(8,128)S(1)} %get-tuple-element.111.refs_3_, ...), custom_call_target="tpu_custom_call" | custom-call | bytes 1024 | tf_op jit(solution)/shard_map/restore/pallas_call | solution.py:24
  77.3 0.8 %collective-permute-done.21.core = f32[896,128]{1,0:T(8,128)S(1)} collective-permute-done((f32[896,128]{1,0:T(8,128)S(1)}, f32[896,128]{1,0:T(8,128)S(1)}, u32[]{:S(2)}, u32[]{:S(2)}) %collective-permute-start.21) | collective-permute-done | bytes 458784 | tf_op jit(solution)/shard_map/ppermute | solution.py:436
  78.1 1.6 %unpack.1 = (f32[2,27,64,64]{3,2,1,0:T(8,128)}, f32[2,64]{1,0:T(2,128)}) custom-call(f32[896,128]{1,0:T(8,128)S(1)} %pad_maximum_fusion.near, f32[896,128]{1,0:T(8,128)S(1)} %collective-permute-done.21.core), custom_call_target="tpu_custom_call" | custom-call | bytes 1024 | tf_op jit(solution)/shard_map/unpack/pallas_call | solution.py:24
  (11 shorter events, 0.2 us)
Async XLA Ops:
  0.6 1.0 %copy-start.1 = (f32[2,64,2,2,128]{4,3,2,1,0:T(2,128)S(1)}, f32[2,64,2,2,128]{4,3,2,1,0:T(2,128)}, u32[]{:S(2)}) copy-start(f32[2,64,2,2,128]{4,3,2,1,0:T(2,128)} %param.4) | copy-start | bytes 786436
  1.6 0.9 %copy-start.2 = (f32[2,64,2,2,128]{4,3,2,1,0:T(2,128)S(1)}, f32[2,64,2,2,128]{4,3,2,1,0:T(2,128)}, u32[]{:S(2)}) copy-start(f32[2,64,2,2,128]{4,3,2,1,0:T(2,128)} %param.7) | copy-start | bytes 786436
  2.7 3.7 %collective-permute-start = (f32[2,2,2,8,128]{4,3,2,1,0:T(8,128)S(1)}, f32[2,2,2,8,128]{4,3,2,1,0:T(8,128)S(1)}, u32[]{:S(2)}, u32[]{:S(2)}) collective-permute-start(f32[2,2,2,8,128]{4,3,2,1,0:T(8,128)S(1)} %get-tuple-element.60), channel_id=1, source_target_pairs={{0,1},{1,0},{2,3},{3,2},{4,5},{5,4},{6,7},{7,6},{8,9},{9,8},{10,11... | collective-permute-start | bytes 98312 | tf_op jit(solution)/shard_map/ppermute | solution.py:436
  3.2 3.2 %collective-permute-start.1 = (f32[2,2,2,8,128]{4,3,2,1,0:T(8,128)S(1)}, f32[2,2,2,8,128]{4,3,2,1,0:T(8,128)S(1)}, u32[]{:S(2)}, u32[]{:S(2)}) collective-permute-start(f32[2,2,2,8,128]{4,3,2,1,0:T(8,128)S(1)} %get-tuple-element.61), channel_id=1, source_target_pairs={{1,2},{2,1},{5,6},{6,5},{9,10},{10,9},{13,14},{14,13},{17,18},{18,... | collective-permute-start | bytes 98312 | tf_op jit(solution)/shard_map/ppermute | solution.py:476
  3.9 1.5 %copy-start = (f32[2,27,64,64]{3,2,1,0:T(8,128)S(1)}, f32[2,27,64,64]{3,2,1,0:T(8,128)}, u32[]{:S(2)}) copy-start(f32[2,27,64,64]{3,2,1,0:T(8,128)} %weights.1) | copy-start | bytes 2654212
  5.4 0.7 copy-start.3
  6.5 16.4 %collective-permute-start.2 = (f32[14,64,128]{2,1,0:T(8,128)S(1)}, f32[14,64,128]{2,1,0:T(8,128)S(1)}, u32[]{:S(2)}, u32[]{:S(2)}) collective-permute-start(f32[14,64,128]{2,1,0:T(8,128)S(1)} %get-tuple-element.67), channel_id=1, source_target_pairs={{0,16},{16,0},{1,17},{17,1},{2,18},{18,2},{3,19},{19,3},{4,20},{20... | collective-permute-start | bytes 1376264 | tf_op jit(solution)/shard_map/ppermute | solution.py:440
  9.1 4.5 %collective-permute-start.3 = (f32[2,88,128]{2,1,0:T(8,128)S(1)}, f32[2,88,128]{2,1,0:T(8,128)S(1)}, u32[]{:S(2)}, u32[]{:S(2)}) collective-permute-start(f32[2,88,128]{2,1,0:T(8,128)S(1)} %get-tuple-element.69), channel_id=1, source_target_pairs={{0,4},{4,0},{8,12},{12,8},{1,5},{5,1},{9,13},{13,9},{2,6},{6,2},{1... | collective-permute-start | bytes 270344 | tf_op jit(solution)/shard_map/ppermute | solution.py:428
  10.7 6.7 %collective-permute-start.5 = (f32[2,88,128]{2,1,0:T(8,128)S(1)}, f32[2,88,128]{2,1,0:T(8,128)S(1)}, u32[]{:S(2)}, u32[]{:S(2)}) collective-permute-start(f32[2,88,128]{2,1,0:T(8,128)S(1)} %get-tuple-element.70), channel_id=1, source_target_pairs={{0,8},{4,12},{8,0},{12,4},{1,9},{5,13},{9,1},{13,5},{2,10},{6,14},... | collective-permute-start | bytes 270344 | tf_op jit(solution)/shard_map/ppermute | solution.py:428
  13.3 6.3 %collective-permute-start.7 = (f32[2,88,128]{2,1,0:T(8,128)S(1)}, f32[2,88,128]{2,1,0:T(8,128)S(1)}, u32[]{:S(2)}, u32[]{:S(2)}) collective-permute-start(f32[2,88,128]{2,1,0:T(8,128)S(1)} %get-tuple-element.71), channel_id=1, source_target_pairs={{0,12},{4,8},{8,4},{12,0},{1,13},{5,9},{9,5},{13,1},{2,14},{6,10},... | collective-permute-start | bytes 270344 | tf_op jit(solution)/shard_map/ppermute | solution.py:428
  13.6 6.3 %collective-permute-start.4 = (f32[2,88,128]{2,1,0:T(8,128)S(1)}, f32[2,88,128]{2,1,0:T(8,128)S(1)}, u32[]{:S(2)}, u32[]{:S(2)}) collective-permute-start(f32[2,88,128]{2,1,0:T(8,128)S(1)} %collective-permute-done.3.refs_1_), channel_id=1, source_target_pairs={{0,16},{16,0},{1,17},{17,1},{2,18},{18,2},{3,19},{19,3},{4,20},{20... | collective-permute-start | bytes 270344 | tf_op jit(solution)/shard_map/ppermute | solution.py:440
  17.4 5.6 %collective-permute-start.6 = (f32[2,88,128]{2,1,0:T(8,128)S(1)}, f32[2,88,128]{2,1,0:T(8,128)S(1)}, u32[]{:S(2)}, u32[]{:S(2)}) collective-permute-start(f32[2,88,128]{2,1,0:T(8,128)S(1)} %collective-permute-done.5.refs_2_), channel_id=1, source_target_pairs={{0,16},{16,0},{1,17},{17,1},{2,18},{18,2},{3,19},{19,3},{4,20},{20... | collective-permute-start | bytes 270344 | tf_op jit(solution)/shard_map/ppermute | solution.py:440
  22.9 3.3 %collective-permute-start.8 = (f32[14,64,128]{2,1,0:T(8,128)S(1)}, f32[14,64,128]{2,1,0:T(8,128)S(1)}, u32[]{:S(2)}, u32[]{:S(2)}) collective-permute-start(f32[14,64,128]{2,1,0:T(8,128)S(1)} %collective-permute-done.2.refs_0_), channel_id=1, source_target_pairs={{0,1},{1,0},{2,3},{3,2},{4,5},{5,4},{6,7},{7,6},{8,9},{9,8},{10,11... | collective-permute-start | bytes 1376264 | tf_op jit(solution)/shard_map/ppermute | solution.py:436
  24.8 4.5 %collective-permute-start.9 = (f32[2,88,128]{2,1,0:T(8,128)S(1)}, f32[2,88,128]{2,1,0:T(8,128)S(1)}, u32[]{:S(2)}, u32[]{:S(2)}) collective-permute-start(f32[2,88,128]{2,1,0:T(8,128)S(1)} %collective-permute-done.7.refs_3_), channel_id=1, source_target_pairs={{0,16},{16,0},{1,17},{17,1},{2,18},{18,2},{3,19},{19,3},{4,20},{20... | collective-permute-start | bytes 270344 | tf_op jit(solution)/shard_map/ppermute | solution.py:440
  33.9 9.1 %collective-permute-start.10 = (f32[2,2,2,32,128]{4,3,2,1,0:T(8,128)S(1)}, f32[2,2,2,32,128]{4,3,2,1,0:T(8,128)S(1)}, u32[]{:S(2)}, u32[]{:S(2)}) collective-permute-start(f32[2,2,2,32,128]{4,3,2,1,0:T(8,128)S(1)} %pad_maximum_fusion.2), channel_id=1, source_target_pairs={{0,8},{4,12},{8,0},{12,4},{1,9},{5,13},{9,1},{13,5},{2,10},{6,14},... | collective-permute-start | bytes 393224 | tf_op jit(solution)/shard_map/ppermute | solution.py:436
  43.0 1.9 %collective-permute-start.11 = (f32[896,128]{1,0:T(8,128)S(1)}, f32[896,128]{1,0:T(8,128)S(1)}, u32[]{:S(2)}, u32[]{:S(2)}) collective-permute-start(f32[896,128]{1,0:T(8,128)S(1)} %bitcast.25), channel_id=1, source_target_pairs={{0,1},{1,0},{2,3},{3,2},{4,5},{5,4},{6,7},{7,6},{8,9},{9,8},{10,11... | collective-permute-start | bytes 1376264 | tf_op jit(solution)/shard_map/ppermute | solution.py:436
  45.0 7.7 %collective-permute-start.12 = (f32[448,128]{1,0:T(8,128)S(1)}, f32[448,128]{1,0:T(8,128)S(1)}, u32[]{:S(2)}, u32[]{:S(2)}) collective-permute-start(f32[448,128]{1,0:T(8,128)S(1)} %slice.46), channel_id=1, source_target_pairs={{0,2},{1,3},{2,0},{3,1},{4,6},{5,7},{6,4},{7,5},{8,10},{9,11},{10,... | collective-permute-start | bytes 688136 | tf_op jit(solution)/shard_map/ppermute | solution.py:436
  46.9 11.0 %collective-permute-start.13 = (f32[3,2,2,32,128]{4,3,2,1,0:T(8,128)S(1)}, f32[3,2,2,32,128]{4,3,2,1,0:T(8,128)S(1)}, u32[]{:S(2)}, u32[]{:S(2)}) collective-permute-start(f32[3,2,2,32,128]{4,3,2,1,0:T(8,128)S(1)} %pad_maximum_fusion.1), channel_id=1, source_target_pairs={{0,4},{4,0},{8,12},{12,8},{1,5},{5,1},{9,13},{13,9},{2,6},{6,2},{1... | collective-permute-start | bytes 589832 | tf_op jit(solution)/shard_map/ppermute | solution.py:436
  48.5 6.3 %collective-permute-start.14 = (f32[2,2,32,128]{3,2,1,0:T(8,128)S(1)}, f32[2,2,32,128]{3,2,1,0:T(8,128)S(1)}, u32[]{:S(2)}, u32[]{:S(2)}) collective-permute-start(f32[2,2,32,128]{3,2,1,0:T(8,128)S(1)} %get-tuple-element.97), channel_id=1, source_target_pairs={{0,8},{4,12},{8,0},{12,4},{1,9},{5,13},{9,1},{13,5},{2,10},{6,14},... | collective-permute-start | bytes 196616 | tf_op jit(solution)/shard_map/ppermute | solution.py:436
  50.7 7.2 %collective-permute-start.15 = (f32[2,2,32,128]{3,2,1,0:T(8,128)S(1)}, f32[2,2,32,128]{3,2,1,0:T(8,128)S(1)}, u32[]{:S(2)}, u32[]{:S(2)}) collective-permute-start(f32[2,2,32,128]{3,2,1,0:T(8,128)S(1)} %get-tuple-element.98), channel_id=1, source_target_pairs={{0,12},{4,8},{8,4},{12,0},{1,13},{5,9},{9,5},{13,1},{2,14},{6,10},... | collective-permute-start | bytes 196616 | tf_op jit(solution)/shard_map/ppermute | solution.py:436
  57.9 4.9 %collective-permute-start.16 = (f32[224,128]{1,0:T(8,128)S(1)}, f32[224,128]{1,0:T(8,128)S(1)}, u32[]{:S(2)}, u32[]{:S(2)}) collective-permute-start(f32[224,128]{1,0:T(8,128)S(1)} %slice_select_fusion), channel_id=1, source_target_pairs={{0,4},{4,0},{8,12},{12,8},{1,5},{5,1},{9,13},{13,9},{2,6},{6,2},{1... | collective-permute-start | bytes 344072 | tf_op jit(solution)/shard_map/ppermute | solution.py:436
  62.8 6.4 %collective-permute-start.17 = (f32[224,128]{1,0:T(8,128)S(1)}, f32[224,128]{1,0:T(8,128)S(1)}, u32[]{:S(2)}, u32[]{:S(2)}) collective-permute-start(f32[224,128]{1,0:T(8,128)S(1)} %select_add_fusion), channel_id=1, source_target_pairs={{0,8},{4,12},{8,0},{12,4},{1,9},{5,13},{9,1},{13,5},{2,10},{6,14},... | collective-permute-start | bytes 344072 | tf_op jit(solution)/shard_map/ppermute | solution.py:436
  69.2 5.9 %collective-permute-start.20 = (f32[224,128]{1,0:T(8,128)S(1)}, f32[224,128]{1,0:T(8,128)S(1)}, u32[]{:S(2)}, u32[]{:S(2)}) collective-permute-start(f32[224,128]{1,0:T(8,128)S(1)} %add.20), channel_id=1, source_target_pairs={{0,6},{1,7},{2,4},{3,5},{4,2},{5,3},{6,0},{7,1},{8,14},{9,15},{10,... | collective-permute-start | bytes 344072 | tf_op jit(solution)/shard_map/ppermute | solution.py:449
  69.3 6.1 %collective-permute-start.19 = (f32[224,128]{1,0:T(8,128)S(1)}, f32[224,128]{1,0:T(8,128)S(1)}, u32[]{:S(2)}, u32[]{:S(2)}) collective-permute-start(f32[224,128]{1,0:T(8,128)S(1)} %add.20), channel_id=1, source_target_pairs={{0,2},{1,3},{2,0},{3,1},{4,6},{5,7},{6,4},{7,5},{8,10},{9,11},{10,... | collective-permute-start | bytes 344072 | tf_op jit(solution)/shard_map/ppermute | solution.py:436
  70.2 6.0 %collective-permute-start.18 = (f32[224,128]{1,0:T(8,128)S(1)}, f32[224,128]{1,0:T(8,128)S(1)}, u32[]{:S(2)}, u32[]{:S(2)}) collective-permute-start(f32[224,128]{1,0:T(8,128)S(1)} %add.20), channel_id=1, source_target_pairs={{0,4},{4,0},{8,12},{12,8},{1,5},{5,1},{9,13},{13,9},{2,6},{6,2},{1... | collective-permute-start | bytes 344072 | tf_op jit(solution)/shard_map/ppermute | solution.py:436
  76.2 1.9 %collective-permute-start.21 = (f32[896,128]{1,0:T(8,128)S(1)}, f32[896,128]{1,0:T(8,128)S(1)}, u32[]{:S(2)}, u32[]{:S(2)}) collective-permute-start(f32[896,128]{1,0:T(8,128)S(1)} %pad_maximum_fusion.near), channel_id=1, source_target_pairs={{0,1},{1,0},{2,3},{3,2},{4,5},{5,4},{6,7},{7,6},{8,9},{9,8},{10,11... | collective-permute-start | bytes 1376264 | tf_op jit(solution)/shard_map/ppermute | solution.py:436

commit v12 on v11

--- a/solution.py
+++ b/solution.py
@@ -493,7 +493,7 @@
     else:
         theirs = list(crossed(jnp.stack(mine)))
     windows = mine + theirs
-    gate = [*theirs[1:3], *mine[3:]]
+    gate = [theirs[1], *mine[2:]]
     near_half, own_row, *_ = lax.optimization_barrier((near_half, own_row, *gate))
     far_half = swapped(near_half, 1)
     far_fwd, far_bwd, far_row = call(table_kernel, "far_table", tables, [near_half, far_half])
@@ -510,7 +510,7 @@
         [pltpu.VMEM((micros, full, LANES), F32)] * 2,
     )
     if slabs == 4:
-        passed = swapped(jnp.stack(fronts[2:]), 2, "gy")
+        passed = swapped(fronts[3], 2, "gy")
     *backs, sums = call(
         functools.partial(backward_kernel, dims, scale),
         "backward",
@@ -532,8 +532,10 @@
     block = block[:half] + swapped(block[half:], 1)
     block, fronts, backs = lax.optimization_barrier((block, fronts, backs))
     if slabs == 4:
-        near = swapped(jnp.stack([fronts[1], passed[1], backs[1]]), 1, "gy")
-        outs = [near, swapped(backs[2], 2, "gy"), swapped(backs[3], 3, "gy")]
+        outs = [
+            swapped(jnp.stack([fronts[1], passed, backs[1]]), 1, "gy"),
+            swapped(backs[3], 3, "gy"),
+        ]
     else:
         outs = spread([jnp.stack(pair) for pair in zip(fronts, backs)])
     part = half // 4
@@ -547,10 +549,15 @@
         kept = kept + swapped(kept, bit, "gy")
         bit *= 2
     if slabs == 4:
-        outs = [fronts[0], outs[0][0], passed[0], outs[0][1], backs[0], outs[0][2], *outs[1:]]
+        kept, far = lax.optimization_barrier((kept, [fronts[2], backs[2]]))
+        far = swapped(jnp.stack(far), 2, "gy")
+    near = jnp.concatenate([kept, *around(kept, kept, kept)], axis=0)
+    if slabs == 4:
+        near, far = lax.optimization_barrier((near, far))
+        (first, relayed, back), last = outs
+        outs = [fronts[0], first, far[0], relayed, backs[0], back, far[1], last]
     else:
         outs = [out[slot] for slot in range(2) for out in outs]
-    near = jnp.concatenate([kept, *around(kept, kept, kept)], axis=0)
     core = swapped(near, 1)
     section_out, section_grad = call(
         functools.partial(restore_kernel, (micros, chans, size_x, local_y, width)),

time: 79.9 us -> 81.5 us (1.020)
  starting transfers between devices: 25.2 us -> 27.2 us
    ppermute x13, waiting for transfers between devices: 21 us -> 22.9 us  [swapped(): lax.ppermute(block, axis, [(i, i ^ bit) for i in range(lax.axis_size(axis...]
    ppermute x13, starting transfers between devices: 15.4 us -> 17.3 us  [swapped(): lax.ppermute(block, axis, [(i, i ^ bit) for i in range(lax.axis_size(axis...]
    ppermute x1, waiting for transfers between devices: 2.31 us -> 0.88 us  [around(): across = lax.ppermute(across, ('gy', 'gz'), route)]
    ppermute x4, waiting for transfers between devices: 5.62 us -> 4.21 us  [crossed(): return lax.ppermute(block, 'section', [(0, 1), (1, 0)])]
  transfers between devices with their start and end apart: 22 -> 22, of which waited for: 17 -> 17; matrix products, arithmetic and copies ran while one was open for 0% -> 0% of each run, Pallas kernels for 12% -> 11%
where the time goes in v12:
time: 81.5 us; the launch traced here: 81.3 us
  waiting for transfers between devices  33.2 us (41%)
  starting transfers between devices  27.2 us (33%)
  Pallas kernels  15.7 us (19%)
  local copies, waits for them, and re-layouts  4.15 us (5%)
    ppermute x13, waiting for transfers between devices, swapped(): lax.ppermute(block, axis, [(i, i ^ bit) for i in range(lax.axis_size(axis...  22.9 us
    ppermute x13, starting transfers between devices, swapped(): lax.ppermute(block, axis, [(i, i ^ bit) for i in range(lax.axis_size(axis...  17.3 us
    pallas_call x9, Pallas kernels, call(): pl.pallas_call(kernel, out_shape=arrays, in_specs=[VMEM] * len(args), out...  15.7 us
    ppermute x3, waiting for transfers between devices, spread(): got.append(lax.ppermute(blocks[turn], 'gy', route))  5.24 us
    ppermute x4, starting transfers between devices, crossed(): return lax.ppermute(block, 'section', [(0, 1), (1, 0)])  4.81 us
    ppermute x3, starting transfers between devices, spread(): got.append(lax.ppermute(blocks[turn], 'gy', route))  4.39 us
    ppermute x4, waiting for transfers between devices, crossed(): return lax.ppermute(block, 'section', [(0, 1), (1, 0)])  4.21 us
    unnamed x8, local copies, waits for them, and re-layouts  4.04 us
  transfers between devices with their start and end apart: 22, of which 17 were waited for; matrix products, arithmetic and copies ran while one was open for 0% of the time, Pallas kernels for 11%

profile of v12, /device:TPU:0, one launch (start us, length us, event | category | flops | bytes accessed | tf_op | source)
XLA Modules:
  0.0 81.3 jit_solution(7611513537334070764)
XLA Ops:
  0.6 0.0 copy-start.1
  0.6 0.9 %copy-done.1 = f32[2,64,2,2,128]{4,3,2,1,0:T(2,128)S(1)} copy-done((f32[2,64,2,2,128]{4,3,2,1,0:T(2,128)S(1)}, f32[2,64,2,2,128]{4,3,2,1,0:T(2,128)}, u32[]{:S(2)}) %copy-start.1) | copy-done | bytes 262168
  1.6 0.0 copy-start.2
  1.6 0.9 %copy-done.2 = f32[2,64,2,2,128]{4,3,2,1,0:T(2,128)S(1)} copy-done((f32[2,64,2,2,128]{4,3,2,1,0:T(2,128)S(1)}, f32[2,64,2,2,128]{4,3,2,1,0:T(2,128)}, u32[]{:S(2)}) %copy-start.2) | copy-done | bytes 262168
  2.5 0.2 turn.1
  2.7 0.5 collective-permute-start
  3.2 0.7 collective-permute-start.1
  3.9 0.0 copy-start
  3.9 1.5 %copy-done = f32[2,27,64,64]{3,2,1,0:T(8,128)S(1)} copy-done((f32[2,27,64,64]{3,2,1,0:T(8,128)S(1)}, f32[2,27,64,64]{3,2,1,0:T(8,128)}, u32[]{:S(2)}) %copy-start) | copy-done | bytes 884760
  5.4 0.0 copy-start.3
  5.4 0.7 copy-done.3
  6.1 0.3 pack.1
  6.4 0.0 collective-permute-done.pair
  6.4 0.0 collective-permute-done.1.inner
  6.4 0.1 windows.1
  6.5 2.6 %collective-permute-start.2 = (f32[14,64,128]{2,1,0:T(8,128)S(1)}, f32[14,64,128]{2,1,0:T(8,128)S(1)}, u32[]{:S(2)}, u32[]{:S(2)}) collective-permute-start(f32[14,64,128]{2,1,0:T(8,128)S(1)} %get-tuple-element.72), channel_id=1, source_target_pairs={{0,16},{16,0},{1,17},{17,1},{2,18},{18,2},{3,19},{19,3},{4,20},{20... | collective-permute-start | bytes 1376264 | tf_op jit(solution)/shard_map/ppermute | solution.py:440
  9.1 1.6 %collective-permute-start.3 = (f32[2,88,128]{2,1,0:T(8,128)S(1)}, f32[2,88,128]{2,1,0:T(8,128)S(1)}, u32[]{:S(2)}, u32[]{:S(2)}) collective-permute-start(f32[2,88,128]{2,1,0:T(8,128)S(1)} %get-tuple-element.74), channel_id=1, source_target_pairs={{0,4},{4,0},{8,12},{12,8},{1,5},{5,1},{9,13},{13,9},{2,6},{6,2},{1... | collective-permute-start | bytes 270344 | tf_op jit(solution)/shard_map/ppermute | solution.py:428
  10.7 2.6 %collective-permute-start.5 = (f32[2,88,128]{2,1,0:T(8,128)S(1)}, f32[2,88,128]{2,1,0:T(8,128)S(1)}, u32[]{:S(2)}, u32[]{:S(2)}) collective-permute-start(f32[2,88,128]{2,1,0:T(8,128)S(1)} %get-tuple-element.75), channel_id=1, source_target_pairs={{0,8},{4,12},{8,0},{12,4},{1,9},{5,13},{9,1},{13,5},{2,10},{6,14},... | collective-permute-start | bytes 270344 | tf_op jit(solution)/shard_map/ppermute | solution.py:428
  13.3 0.2 collective-permute-start.6
  13.5 0.1 collective-permute-done.3.refs_1_
  13.6 0.2 collective-permute-start.4
  13.8 0.7 own_table.1
  14.5 2.8 %collective-permute-done.5.refs_2_ = f32[2,88,128]{2,1,0:T(8,128)S(1)} collective-permute-done((f32[2,88,128]{2,1,0:T(8,128)S(1)}, f32[2,88,128]{2,1,0:T(8,128)S(1)}, u32[]{:S(2)}, u32[]{:S(2)}) %collective-permute-start.5) | collective-permute-done | bytes 90144 | tf_op jit(solution)/shard_map/ppermute | solution.py:428
  17.4 2.3 %collective-permute-done.6.refs_3_ = f32[2,88,128]{2,1,0:T(8,128)S(1)} collective-permute-done((f32[2,88,128]{2,1,0:T(8,128)S(1)}, f32[2,88,128]{2,1,0:T(8,128)S(1)}, u32[]{:S(2)}, u32[]{:S(2)}) %collective-permute-start.6) | collective-permute-done | bytes 90144 | tf_op jit(solution)/shard_map/ppermute | solution.py:428
  19.6 0.3 collective-permute-done.4.refs_5_
  19.9 0.0 collective-permute-done.2.refs_0_
  19.9 2.3 %collective-permute-start.7 = (f32[14,64,128]{2,1,0:T(8,128)S(1)}, f32[14,64,128]{2,1,0:T(8,128)S(1)}, u32[]{:S(2)}, u32[]{:S(2)}) collective-permute-start(f32[14,64,128]{2,1,0:T(8,128)S(1)} %collective-permute-done.2.refs_0_), channel_id=1, source_target_pairs={{0,1},{1,0},{2,3},{3,2},{4,5},{5,4},{6,7},{7,6},{8,9},{9,8},{10,11... | collective-permute-start | bytes 1376264 | tf_op jit(solution)/shard_map/ppermute | solution.py:436
  22.2 2.0 %collective-permute-start.8 = (f32[2,88,128]{2,1,0:T(8,128)S(1)}, f32[2,88,128]{2,1,0:T(8,128)S(1)}, u32[]{:S(2)}, u32[]{:S(2)}) collective-permute-start(f32[2,88,128]{2,1,0:T(8,128)S(1)} %collective-permute-done.5.refs_2_), channel_id=1, source_target_pairs={{0,16},{16,0},{1,17},{17,1},{2,18},{18,2},{3,19},{19,3},{4,20},{20... | collective-permute-start | bytes 270344 | tf_op jit(solution)/shard_map/ppermute | solution.py:440
  24.3 0.0 collective-permute-start.9
  24.3 0.0 collective-permute-done.7.refs_1_
  24.3 0.8 far_table.1
  25.1 2.5 %collective-permute-done.8.refs_6_ = f32[2,88,128]{2,1,0:T(8,128)S(1)} collective-permute-done((f32[2,88,128]{2,1,0:T(8,128)S(1)}, f32[2,88,128]{2,1,0:T(8,128)S(1)}, u32[]{:S(2)}, u32[]{:S(2)}) %collective-permute-start.8) | collective-permute-done | bytes 90144 | tf_op jit(solution)/shard_map/ppermute | solution.py:440
  27.5 1.4 %collective-permute-done.9.refs_7_ = f32[2,88,128]{2,1,0:T(8,128)S(1)} collective-permute-done((f32[2,88,128]{2,1,0:T(8,128)S(1)}, f32[2,88,128]{2,1,0:T(8,128)S(1)}, u32[]{:S(2)}, u32[]{:S(2)}) %collective-permute-start.9) | collective-permute-done | bytes 90144 | tf_op jit(solution)/shard_map/ppermute | solution.py:440
  29.0 4.5 %forward.1 = (bf16[5,2,480,256]{3,2,1,0:T(8,128)(2,1)S(1)}, f32[4,2,384,128]{3,2,1,0:T(8,128)S(1)}, f32[2,2,32,128]{3,2,1,0:T(8,128)S(1)}, f32[2,2,32,128]{3,2,1...) custom-call(bf16[2,1920,256]{2,1,0:T(8,128)(2,1)S(1)} %get-tuple-element.79.own, ...), custom_call_target="tpu_custom_call" | custom-call | bytes 1024 | tf_op jit(solution)/shard_map/forward/pallas_call | solution.py:24
  33.5 2.9 %collective-permute-start.10 = (f32[2,2,32,128]{3,2,1,0:T(8,128)S(1)}, f32[2,2,32,128]{3,2,1,0:T(8,128)S(1)}, u32[]{:S(2)}, u32[]{:S(2)}) collective-permute-start(f32[2,2,32,128]{3,2,1,0:T(8,128)S(1)} %get-tuple-element.88), channel_id=1, source_target_pairs={{0,8},{4,12},{8,0},{12,4},{1,9},{5,13},{9,1},{13,5},{2,10},{6,14},... | collective-permute-start | bytes 196616 | tf_op jit(solution)/shard_map/ppermute | solution.py:436
  36.4 6.6 %backward.1 = (f32[2,2,32,128]{3,2,1,0:T(8,128)S(1)}, f32[2,2,32,128]{3,2,1,0:T(8,128)S(1)}, f32[2,2,32,128]{3,2,1,0:T(8,128)S(1)}, f32[2,2,32,128]{3,2,1,0:T(8,128)S(1)}, f32[28,64,128]{2,1,0:T(8,128)S(1)}) custom-call(bf16[2,1920,256]{2,1,0:T(8,128)(2,1)S(1)} %get-tuple-element.62.own, bf16[2,1920,256]{2,1,0:T(8,128)(2,1)S(1)} %get-tuple-element.78.other, ...), custom_call_target="tpu_custom_call" | custom-call | flops 4076863488 | bytes 1024 | tf_op jit(solution)/shard_map/backward/pallas_call | solution.py:24
  43.0 0.0 collective-permute-done.10
  43.0 0.1 fusion
  43.0 0.1 collective-permute-start.11
  43.1 1.8 %collective-permute-done.11 = f32[896,128]{1,0:T(8,128)S(1)} collective-permute-done((f32[896,128]{1,0:T(8,128)S(1)}, f32[896,128]{1,0:T(8,128)S(1)}, u32[]{:S(2)}, u32[]{:S(2)}) %collective-permute-start.11) | collective-permute-done | bytes 458784 | tf_op jit(solution)/shard_map/ppermute | solution.py:436
  44.9 0.1 bitcast_add_fusion
  45.0 1.8 %collective-permute-start.12 = (f32[448,128]{1,0:T(8,128)S(1)}, f32[448,128]{1,0:T(8,128)S(1)}, u32[]{:S(2)}, u32[]{:S(2)}) collective-permute-start(f32[448,128]{1,0:T(8,128)S(1)} %slice.37), channel_id=1, source_target_pairs={{0,2},{1,3},{2,0},{3,1},{4,6},{5,7},{6,4},{7,5},{8,10},{9,11},{10,... | collective-permute-start | bytes 688136 | tf_op jit(solution)/shard_map/ppermute | solution.py:436
  46.9 1.6 %collective-permute-start.13 = (f32[3,2,2,32,128]{4,3,2,1,0:T(8,128)S(1)}, f32[3,2,2,32,128]{4,3,2,1,0:T(8,128)S(1)}, u32[]{:S(2)}, u32[]{:S(2)}) collective-permute-start(f32[3,2,2,32,128]{4,3,2,1,0:T(8,128)S(1)} %pad_maximum_fusion.1), channel_id=1, source_target_pairs={{0,4},{4,0},{8,12},{12,8},{1,5},{5,1},{9,13},{13,9},{2,6},{6,2},{1... | collective-permute-start | bytes 589832 | tf_op jit(solution)/shard_map/ppermute | solution.py:436
  48.5 0.2 collective-permute-start.14
  48.7 4.0 %collective-permute-done.12 = f32[448,128]{1,0:T(8,128)S(1)} collective-permute-done((f32[448,128]{1,0:T(8,128)S(1)}, f32[448,128]{1,0:T(8,128)S(1)}, u32[]{:S(2)}, u32[]{:S(2)}) %collective-permute-start.12) | collective-permute-done | bytes 229408 | tf_op jit(solution)/shard_map/ppermute | solution.py:436
  52.8 2.1 %collective-permute-done.14.refs_7_ = f32[2,2,32,128]{3,2,1,0:T(8,128)S(1)} collective-permute-done((f32[2,2,32,128]{3,2,1,0:T(8,128)S(1)}, f32[2,2,32,128]{3,2,1,0:T(8,128)S(1)}, u32[]{:S(2)}, u32[]{:S(2)}) %collective-permute-start.14) | collective-permute-done | bytes 65568 | tf_op jit(solution)/shard_map/ppermute | solution.py:436
  54.9 0.1 collective-permute-done.13
  55.0 0.9 %collective-permute-start.15 = (f32[224,128]{1,0:T(8,128)S(1)}, f32[224,128]{1,0:T(8,128)S(1)}, u32[]{:S(2)}, u32[]{:S(2)}) collective-permute-start(f32[224,128]{1,0:T(8,128)S(1)} %slice_select_fusion), channel_id=1, source_target_pairs={{0,4},{4,0},{8,12},{12,8},{1,5},{5,1},{9,13},{13,9},{2,6},{6,2},{1... | collective-permute-start | bytes 344072 | tf_op jit(solution)/shard_map/ppermute | solution.py:436
  55.9 3.9 %collective-permute-done.15 = f32[224,128]{1,0:T(8,128)S(1)} collective-permute-done((f32[224,128]{1,0:T(8,128)S(1)}, f32[224,128]{1,0:T(8,128)S(1)}, u32[]{:S(2)}, u32[]{:S(2)}) %collective-permute-start.15) | collective-permute-done | bytes 114720 | tf_op jit(solution)/shard_map/ppermute | solution.py:436
  59.9 2.0 %collective-permute-start.16 = (f32[224,128]{1,0:T(8,128)S(1)}, f32[224,128]{1,0:T(8,128)S(1)}, u32[]{:S(2)}, u32[]{:S(2)}) collective-permute-start(f32[224,128]{1,0:T(8,128)S(1)} %select_add_fusion), channel_id=1, source_target_pairs={{0,8},{4,12},{8,0},{12,4},{1,9},{5,13},{9,1},{13,5},{2,10},{6,14},... | collective-permute-start | bytes 344072 | tf_op jit(solution)/shard_map/ppermute | solution.py:436
  61.9 5.1 %collective-permute-done.16 = f32[224,128]{1,0:T(8,128)S(1)} collective-permute-done((f32[224,128]{1,0:T(8,128)S(1)}, f32[224,128]{1,0:T(8,128)S(1)}, u32[]{:S(2)}, u32[]{:S(2)}) %collective-permute-start.16) | collective-permute-done | bytes 114720 | tf_op jit(solution)/shard_map/ppermute | solution.py:436
  67.0 0.1 collective-permute-start.19
  67.1 1.4 %collective-permute-start.18 = (f32[224,128]{1,0:T(8,128)S(1)}, f32[224,128]{1,0:T(8,128)S(1)}, u32[]{:S(2)}, u32[]{:S(2)}) collective-permute-start(f32[224,128]{1,0:T(8,128)S(1)} %add.20), channel_id=1, source_target_pairs={{0,2},{1,3},{2,0},{3,1},{4,6},{5,7},{6,4},{7,5},{8,10},{9,11},{10,... | collective-permute-start | bytes 344072 | tf_op jit(solution)/shard_map/ppermute | solution.py:436
  68.4 2.1 %collective-permute-start.17 = (f32[224,128]{1,0:T(8,128)S(1)}, f32[224,128]{1,0:T(8,128)S(1)}, u32[]{:S(2)}, u32[]{:S(2)}) collective-permute-start(f32[224,128]{1,0:T(8,128)S(1)} %add.20), channel_id=1, source_target_pairs={{0,4},{4,0},{8,12},{12,8},{1,5},{5,1},{9,13},{13,9},{2,6},{6,2},{1... | collective-permute-start | bytes 344072 | tf_op jit(solution)/shard_map/ppermute | solution.py:436
  70.6 1.4 %collective-permute-start.20 = (f32[2,2,2,32,128]{4,3,2,1,0:T(8,128)S(1)}, f32[2,2,2,32,128]{4,3,2,1,0:T(8,128)S(1)}, u32[]{:S(2)}, u32[]{:S(2)}) collective-permute-start(f32[2,2,2,32,128]{4,3,2,1,0:T(8,128)S(1)} %pad_maximum_fusion.2), channel_id=1, source_target_pairs={{0,8},{4,12},{8,0},{12,4},{1,9},{5,13},{9,1},{13,5},{2,10},{6,14},... | collective-permute-start | bytes 393224 | tf_op jit(solution)/shard_map/ppermute | solution.py:436
  72.0 0.9 %collective-permute-done.19 = f32[224,128]{1,0:T(8,128)S(1)} collective-permute-done((f32[224,128]{1,0:T(8,128)S(1)}, f32[224,128]{1,0:T(8,128)S(1)}, u32[]{:S(2)}, u32[]{:S(2)}) %collective-permute-start.19) | collective-permute-done | bytes 114720 | tf_op jit(solution)/shard_map/ppermute | solution.py:449
  72.9 0.3 collective-permute-done.18
  73.2 0.4 collective-permute-done.17
  73.6 4.3 %collective-permute-done.20 = f32[2,2,2,32,128]{4,3,2,1,0:T(8,128)S(1)} collective-permute-done((f32[2,2,2,32,128]{4,3,2,1,0:T(8,128)S(1)}, f32[2,2,2,32,128]{4,3,2,1,0:T(8,128)S(1)}, u32[]{:S(2)}, u32[]{:S(2)}) %collective-permute-start.20) | collective-permute-done | bytes 131104 | tf_op jit(solution)/shard_map/ppermute | solution.py:436
  77.9 0.0 collective-permute-start.21
  77.9 1.0 %restore.1 = (f32[512,128]{1,0:T(8,128)}, f32[512,128]{1,0:T(8,128)}) custom-call(f32[2,2,32,128]{3,2,1,0:T(8,128)S(1)} %get-tuple-element.97.refs_0_, f32[2,2,32,128]{3,2,1,0:T(8,128)S(1)} %get-tuple-element.122.refs_1_, f32[2,2,32,128]{3,2,1,0:T(8,128)S(1)} %get-tuple-element.124.refs_2_, f32[2,2,32,128]{3,2,1,0:T(8,128)S(1)} %get-tuple-element.121.refs_3_, ...), custom_call_target="tpu_custom_call" | custom-call | bytes 1024 | tf_op jit(solution)/shard_map/restore/pallas_call | solution.py:24
  78.9 0.8 collective-permute-done.21.core
  79.7 1.6 %unpack.1 = (f32[2,27,64,64]{3,2,1,0:T(8,128)}, f32[2,64]{1,0:T(2,128)}) custom-call(f32[896,128]{1,0:T(8,128)S(1)} %pad_maximum_fusion.near, f32[896,128]{1,0:T(8,128)S(1)} %collective-permute-done.21.core), custom_call_target="tpu_custom_call" | custom-call | bytes 1024 | tf_op jit(solution)/shard_map/unpack/pallas_call | solution.py:24
  (10 shorter events, 0.2 us)
Async XLA Ops:
  0.6 1.0 %copy-start.1 = (f32[2,64,2,2,128]{4,3,2,1,0:T(2,128)S(1)}, f32[2,64,2,2,128]{4,3,2,1,0:T(2,128)}, u32[]{:S(2)}) copy-start(f32[2,64,2,2,128]{4,3,2,1,0:T(2,128)} %param.4) | copy-start | bytes 786436
  1.6 0.9 %copy-start.2 = (f32[2,64,2,2,128]{4,3,2,1,0:T(2,128)S(1)}, f32[2,64,2,2,128]{4,3,2,1,0:T(2,128)}, u32[]{:S(2)}) copy-start(f32[2,64,2,2,128]{4,3,2,1,0:T(2,128)} %param.7) | copy-start | bytes 786436
  2.7 3.7 %collective-permute-start = (f32[2,2,2,8,128]{4,3,2,1,0:T(8,128)S(1)}, f32[2,2,2,8,128]{4,3,2,1,0:T(8,128)S(1)}, u32[]{:S(2)}, u32[]{:S(2)}) collective-permute-start(f32[2,2,2,8,128]{4,3,2,1,0:T(8,128)S(1)} %get-tuple-element.65), channel_id=1, source_target_pairs={{0,1},{1,0},{2,3},{3,2},{4,5},{5,4},{6,7},{7,6},{8,9},{9,8},{10,11... | collective-permute-start | bytes 98312 | tf_op jit(solution)/shard_map/ppermute | solution.py:436
  3.2 3.2 %collective-permute-start.1 = (f32[2,2,2,8,128]{4,3,2,1,0:T(8,128)S(1)}, f32[2,2,2,8,128]{4,3,2,1,0:T(8,128)S(1)}, u32[]{:S(2)}, u32[]{:S(2)}) collective-permute-start(f32[2,2,2,8,128]{4,3,2,1,0:T(8,128)S(1)} %get-tuple-element.66), channel_id=1, source_target_pairs={{1,2},{2,1},{5,6},{6,5},{9,10},{10,9},{13,14},{14,13},{17,18},{18,... | collective-permute-start | bytes 98312 | tf_op jit(solution)/shard_map/ppermute | solution.py:476
  3.9 1.5 %copy-start = (f32[2,27,64,64]{3,2,1,0:T(8,128)S(1)}, f32[2,27,64,64]{3,2,1,0:T(8,128)}, u32[]{:S(2)}) copy-start(f32[2,27,64,64]{3,2,1,0:T(8,128)} %weights.1) | copy-start | bytes 2654212
  5.4 0.7 copy-start.3
  6.5 13.4 %collective-permute-start.2 = (f32[14,64,128]{2,1,0:T(8,128)S(1)}, f32[14,64,128]{2,1,0:T(8,128)S(1)}, u32[]{:S(2)}, u32[]{:S(2)}) collective-permute-start(f32[14,64,128]{2,1,0:T(8,128)S(1)} %get-tuple-element.72), channel_id=1, source_target_pairs={{0,16},{16,0},{1,17},{17,1},{2,18},{18,2},{3,19},{19,3},{4,20},{20... | collective-permute-start | bytes 1376264 | tf_op jit(solution)/shard_map/ppermute | solution.py:440
  9.1 4.5 %collective-permute-start.3 = (f32[2,88,128]{2,1,0:T(8,128)S(1)}, f32[2,88,128]{2,1,0:T(8,128)S(1)}, u32[]{:S(2)}, u32[]{:S(2)}) collective-permute-start(f32[2,88,128]{2,1,0:T(8,128)S(1)} %get-tuple-element.74), channel_id=1, source_target_pairs={{0,4},{4,0},{8,12},{12,8},{1,5},{5,1},{9,13},{13,9},{2,6},{6,2},{1... | collective-permute-start | bytes 270344 | tf_op jit(solution)/shard_map/ppermute | solution.py:428
  10.7 6.7 %collective-permute-start.5 = (f32[2,88,128]{2,1,0:T(8,128)S(1)}, f32[2,88,128]{2,1,0:T(8,128)S(1)}, u32[]{:S(2)}, u32[]{:S(2)}) collective-permute-start(f32[2,88,128]{2,1,0:T(8,128)S(1)} %get-tuple-element.75), channel_id=1, source_target_pairs={{0,8},{4,12},{8,0},{12,4},{1,9},{5,13},{9,1},{13,5},{2,10},{6,14},... | collective-permute-start | bytes 270344 | tf_op jit(solution)/shard_map/ppermute | solution.py:428
  13.3 6.3 %collective-permute-start.6 = (f32[2,88,128]{2,1,0:T(8,128)S(1)}, f32[2,88,128]{2,1,0:T(8,128)S(1)}, u32[]{:S(2)}, u32[]{:S(2)}) collective-permute-start(f32[2,88,128]{2,1,0:T(8,128)S(1)} %get-tuple-element.76), channel_id=1, source_target_pairs={{0,12},{4,8},{8,4},{12,0},{1,13},{5,9},{9,5},{13,1},{2,14},{6,10},... | collective-permute-start | bytes 270344 | tf_op jit(solution)/shard_map/ppermute | solution.py:428
  13.6 6.3 %collective-permute-start.4 = (f32[2,88,128]{2,1,0:T(8,128)S(1)}, f32[2,88,128]{2,1,0:T(8,128)S(1)}, u32[]{:S(2)}, u32[]{:S(2)}) collective-permute-start(f32[2,88,128]{2,1,0:T(8,128)S(1)} %collective-permute-done.3.refs_1_), channel_id=1, source_target_pairs={{0,16},{16,0},{1,17},{17,1},{2,18},{18,2},{3,19},{19,3},{4,20},{20... | collective-permute-start | bytes 270344 | tf_op jit(solution)/shard_map/ppermute | solution.py:440
  19.9 4.4 %collective-permute-start.7 = (f32[14,64,128]{2,1,0:T(8,128)S(1)}, f32[14,64,128]{2,1,0:T(8,128)S(1)}, u32[]{:S(2)}, u32[]{:S(2)}) collective-permute-start(f32[14,64,128]{2,1,0:T(8,128)S(1)} %collective-permute-done.2.refs_0_), channel_id=1, source_target_pairs={{0,1},{1,0},{2,3},{3,2},{4,5},{5,4},{6,7},{7,6},{8,9},{9,8},{10,11... | collective-permute-start | bytes 1376264 | tf_op jit(solution)/shard_map/ppermute | solution.py:436
  22.2 5.3 %collective-permute-start.8 = (f32[2,88,128]{2,1,0:T(8,128)S(1)}, f32[2,88,128]{2,1,0:T(8,128)S(1)}, u32[]{:S(2)}, u32[]{:S(2)}) collective-permute-start(f32[2,88,128]{2,1,0:T(8,128)S(1)} %collective-permute-done.5.refs_2_), channel_id=1, source_target_pairs={{0,16},{16,0},{1,17},{17,1},{2,18},{18,2},{3,19},{19,3},{4,20},{20... | collective-permute-start | bytes 270344 | tf_op jit(solution)/shard_map/ppermute | solution.py:440
  24.3 4.7 %collective-permute-start.9 = (f32[2,88,128]{2,1,0:T(8,128)S(1)}, f32[2,88,128]{2,1,0:T(8,128)S(1)}, u32[]{:S(2)}, u32[]{:S(2)}) collective-permute-start(f32[2,88,128]{2,1,0:T(8,128)S(1)} %collective-permute-done.6.refs_3_), channel_id=1, source_target_pairs={{0,16},{16,0},{1,17},{17,1},{2,18},{18,2},{3,19},{19,3},{4,20},{20... | collective-permute-start | bytes 270344 | tf_op jit(solution)/shard_map/ppermute | solution.py:440
  33.5 9.5 %collective-permute-start.10 = (f32[2,2,32,128]{3,2,1,0:T(8,128)S(1)}, f32[2,2,32,128]{3,2,1,0:T(8,128)S(1)}, u32[]{:S(2)}, u32[]{:S(2)}) collective-permute-start(f32[2,2,32,128]{3,2,1,0:T(8,128)S(1)} %get-tuple-element.88), channel_id=1, source_target_pairs={{0,8},{4,12},{8,0},{12,4},{1,9},{5,13},{9,1},{13,5},{2,10},{6,14},... | collective-permute-start | bytes 196616 | tf_op jit(solution)/shard_map/ppermute | solution.py:436
  43.0 1.9 %collective-permute-start.11 = (f32[896,128]{1,0:T(8,128)S(1)}, f32[896,128]{1,0:T(8,128)S(1)}, u32[]{:S(2)}, u32[]{:S(2)}) collective-permute-start(f32[896,128]{1,0:T(8,128)S(1)} %bitcast.28), channel_id=1, source_target_pairs={{0,1},{1,0},{2,3},{3,2},{4,5},{5,4},{6,7},{7,6},{8,9},{9,8},{10,11... | collective-permute-start | bytes 1376264 | tf_op jit(solution)/shard_map/ppermute | solution.py:436
  45.0 7.7 %collective-permute-start.12 = (f32[448,128]{1,0:T(8,128)S(1)}, f32[448,128]{1,0:T(8,128)S(1)}, u32[]{:S(2)}, u32[]{:S(2)}) collective-permute-start(f32[448,128]{1,0:T(8,128)S(1)} %slice.37), channel_id=1, source_target_pairs={{0,2},{1,3},{2,0},{3,1},{4,6},{5,7},{6,4},{7,5},{8,10},{9,11},{10,... | collective-permute-start | bytes 688136 | tf_op jit(solution)/shard_map/ppermute | solution.py:436
  46.9 8.1 %collective-permute-start.13 = (f32[3,2,2,32,128]{4,3,2,1,0:T(8,128)S(1)}, f32[3,2,2,32,128]{4,3,2,1,0:T(8,128)S(1)}, u32[]{:S(2)}, u32[]{:S(2)}) collective-permute-start(f32[3,2,2,32,128]{4,3,2,1,0:T(8,128)S(1)} %pad_maximum_fusion.1), channel_id=1, source_target_pairs={{0,4},{4,0},{8,12},{12,8},{1,5},{5,1},{9,13},{13,9},{2,6},{6,2},{1... | collective-permute-start | bytes 589832 | tf_op jit(solution)/shard_map/ppermute | solution.py:436
  48.5 6.4 %collective-permute-start.14 = (f32[2,2,32,128]{3,2,1,0:T(8,128)S(1)}, f32[2,2,32,128]{3,2,1,0:T(8,128)S(1)}, u32[]{:S(2)}, u32[]{:S(2)}) collective-permute-start(f32[2,2,32,128]{3,2,1,0:T(8,128)S(1)} %get-tuple-element.102), channel_id=1, source_target_pairs={{0,12},{4,8},{8,4},{12,0},{1,13},{5,9},{9,5},{13,1},{2,14},{6,10},... | collective-permute-start | bytes 196616 | tf_op jit(solution)/shard_map/ppermute | solution.py:436
  55.0 4.9 %collective-permute-start.15 = (f32[224,128]{1,0:T(8,128)S(1)}, f32[224,128]{1,0:T(8,128)S(1)}, u32[]{:S(2)}, u32[]{:S(2)}) collective-permute-start(f32[224,128]{1,0:T(8,128)S(1)} %slice_select_fusion), channel_id=1, source_target_pairs={{0,4},{4,0},{8,12},{12,8},{1,5},{5,1},{9,13},{13,9},{2,6},{6,2},{1... | collective-permute-start | bytes 344072 | tf_op jit(solution)/shard_map/ppermute | solution.py:436
  59.9 7.1 %collective-permute-start.16 = (f32[224,128]{1,0:T(8,128)S(1)}, f32[224,128]{1,0:T(8,128)S(1)}, u32[]{:S(2)}, u32[]{:S(2)}) collective-permute-start(f32[224,128]{1,0:T(8,128)S(1)} %select_add_fusion), channel_id=1, source_target_pairs={{0,8},{4,12},{8,0},{12,4},{1,9},{5,13},{9,1},{13,5},{2,10},{6,14},... | collective-permute-start | bytes 344072 | tf_op jit(solution)/shard_map/ppermute | solution.py:436
  67.0 5.9 %collective-permute-start.19 = (f32[224,128]{1,0:T(8,128)S(1)}, f32[224,128]{1,0:T(8,128)S(1)}, u32[]{:S(2)}, u32[]{:S(2)}) collective-permute-start(f32[224,128]{1,0:T(8,128)S(1)} %add.20), channel_id=1, source_target_pairs={{0,6},{1,7},{2,4},{3,5},{4,2},{5,3},{6,0},{7,1},{8,14},{9,15},{10,... | collective-permute-start | bytes 344072 | tf_op jit(solution)/shard_map/ppermute | solution.py:449
  67.1 6.1 %collective-permute-start.18 = (f32[224,128]{1,0:T(8,128)S(1)}, f32[224,128]{1,0:T(8,128)S(1)}, u32[]{:S(2)}, u32[]{:S(2)}) collective-permute-start(f32[224,128]{1,0:T(8,128)S(1)} %add.20), channel_id=1, source_target_pairs={{0,2},{1,3},{2,0},{3,1},{4,6},{5,7},{6,4},{7,5},{8,10},{9,11},{10,... | collective-permute-start | bytes 344072 | tf_op jit(solution)/shard_map/ppermute | solution.py:436
  68.4 5.1 %collective-permute-start.17 = (f32[224,128]{1,0:T(8,128)S(1)}, f32[224,128]{1,0:T(8,128)S(1)}, u32[]{:S(2)}, u32[]{:S(2)}) collective-permute-start(f32[224,128]{1,0:T(8,128)S(1)} %add.20), channel_id=1, source_target_pairs={{0,4},{4,0},{8,12},{12,8},{1,5},{5,1},{9,13},{13,9},{2,6},{6,2},{1... | collective-permute-start | bytes 344072 | tf_op jit(solution)/shard_map/ppermute | solution.py:436
  70.6 7.3 %collective-permute-start.20 = (f32[2,2,2,32,128]{4,3,2,1,0:T(8,128)S(1)}, f32[2,2,2,32,128]{4,3,2,1,0:T(8,128)S(1)}, u32[]{:S(2)}, u32[]{:S(2)}) collective-permute-start(f32[2,2,2,32,128]{4,3,2,1,0:T(8,128)S(1)} %pad_maximum_fusion.2), channel_id=1, source_target_pairs={{0,8},{4,12},{8,0},{12,4},{1,9},{5,13},{9,1},{13,5},{2,10},{6,14},... | collective-permute-start | bytes 393224 | tf_op jit(solution)/shard_map/ppermute | solution.py:436
  77.9 1.8 %collective-permute-start.21 = (f32[896,128]{1,0:T(8,128)S(1)}, f32[896,128]{1,0:T(8,128)S(1)}, u32[]{:S(2)}, u32[]{:S(2)}) collective-permute-start(f32[896,128]{1,0:T(8,128)S(1)} %pad_maximum_fusion.near), channel_id=1, source_target_pairs={{0,1},{1,0},{2,3},{3,2},{4,5},{5,4},{6,7},{7,6},{8,9},{9,8},{10,11... | collective-permute-start | bytes 1376264 | tf_op jit(solution)/shard_map/ppermute | solution.py:436

commit v13 on v11

--- a/solution.py
+++ b/solution.py
@@ -381,15 +381,17 @@
         sums[spot(TAPS), 0:1, lanes] = row[:, :chans] + row[:, chans:]
 
 
-def unpack_kernel(near, core, weight, bias, whole):
-    part = near.shape[0] // 4
+def unpack_kernel(*refs):
+    sources, (weight, bias, whole) = refs[:-3], refs[-3:]
+    part = sources[0].shape[0] // 4
     chans = weight.shape[-1]
     odd, swap = lax.axis_index("gy") % 2, column_bits()
-    for index in range(8):
-        source = near if index < 4 else core
-        first = index % 4 * part
-        at = ((index // 2 ^ swap) * 2 + (index % 2 ^ odd)) * part
-        whole[pl.ds(pl.multiple_of(at, 8), part), :] = source[first : first + part, :]
+    for number, source in enumerate(sources):
+        for index in range(4):
+            quarter = number // 2 * 2 + index // 2
+            at = (((quarter ^ swap) * 2 + (index % 2 ^ odd)) * 2 + number % 2) * part
+            rows = source[index * part : (index + 1) * part, :]
+            whole[pl.ds(pl.multiple_of(at, 8), part), :] = rows
     for layer in range(2):
         lanes = slice(layer * chans, (layer + 1) * chans)
         for tap in range(TAPS):
@@ -493,7 +495,7 @@
     else:
         theirs = list(crossed(jnp.stack(mine)))
     windows = mine + theirs
-    gate = [*theirs[1:3], *mine[3:]]
+    gate = [theirs[1], *mine[2:]]
     near_half, own_row, *_ = lax.optimization_barrier((near_half, own_row, *gate))
     far_half = swapped(near_half, 1)
     far_fwd, far_bwd, far_row = call(table_kernel, "far_table", tables, [near_half, far_half])
@@ -527,31 +529,35 @@
     if slabs == 4:
         sums, passed = lax.optimization_barrier((sums, passed))
 
-    block = sums.reshape(BLOCKS * chans, LANES)
-    half = block.shape[0] // 2
-    block = block[:half] + swapped(block[half:], 1)
-    block, fronts, backs = lax.optimization_barrier((block, fronts, backs))
+    part = BLOCKS * chans // 16
+    blocks = sums.reshape(8, 2, part, LANES)
+    odd = lax.axis_index("gy") % 2 == 1
+    streams = []
+    for stream in range(2):
+        block = blocks[:, stream].reshape(8 * part, LANES)
+        streams.append(block[: 4 * part] + swapped(block[4 * part :], 1))
+    streams[0], fronts, backs = lax.optimization_barrier((streams[0], fronts, backs))
     if slabs == 4:
         near = swapped(jnp.stack([fronts[1], passed[1], backs[1]]), 1, "gy")
         outs = [near, swapped(backs[2], 2, "gy"), swapped(backs[3], 3, "gy")]
     else:
         outs = spread([jnp.stack(pair) for pair in zip(fronts, backs)])
-    part = half // 4
-    block = block[: 2 * part] + swapped(block[2 * part :], 2)
-    block, outs = lax.optimization_barrier((block, outs))
-    odd = lax.axis_index("gy") % 2 == 1
-    kept = jnp.where(odd, block[part:], block[:part])
-    kept = kept + swapped(jnp.where(odd, block[:part], block[part:]), 1, "gy")
-    bit = 2
-    while bit < slabs:
-        kept = kept + swapped(kept, bit, "gy")
-        bit *= 2
+    streams = [block[: 2 * part] + swapped(block[2 * part :], 2) for block in streams]
+    streams[1], outs = lax.optimization_barrier((streams[1], outs))
+    sums = []
+    for block in streams:
+        kept = jnp.where(odd, block[part:], block[:part])
+        kept = kept + swapped(jnp.where(odd, block[:part], block[part:]), 1, "gy")
+        bit = 2
+        while bit < slabs:
+            kept = kept + swapped(kept, bit, "gy")
+            bit *= 2
+        sums.append(jnp.concatenate([kept, *around(kept, kept, kept)], axis=0))
+    sums += [swapped(block, 1) for block in sums]
     if slabs == 4:
         outs = [fronts[0], outs[0][0], passed[0], outs[0][1], backs[0], outs[0][2], *outs[1:]]
     else:
         outs = [out[slot] for slot in range(2) for out in outs]
-    near = jnp.concatenate([kept, *around(kept, kept, kept)], axis=0)
-    core = swapped(near, 1)
     section_out, section_grad = call(
         functools.partial(restore_kernel, (micros, chans, size_x, local_y, width)),
         "restore",
@@ -563,7 +569,7 @@
         unpack_kernel,
         "unpack",
         [((2, TAPS, chans, chans), F32), ((2, chans), F32)],
-        [near, core],
+        sums,
         [pltpu.VMEM((BLOCKS * chans, LANES), F32)],
     )
     shape = (1, *inflow.shape)

time: 79.9 us -> 78.6 us (0.984)
  waiting for transfers between devices: 33.6 us -> 22.2 us
  starting transfers between devices: 25.2 us -> 35.2 us
    ppermute x13 -> x20, waiting for transfers between devices: 21 us -> 11.3 us  [swapped(): lax.ppermute(block, axis, [(i, i ^ bit) for i in range(lax.axis_size(axis...]
    ppermute x13 -> x20, starting transfers between devices: 15.4 us -> 21.8 us  [swapped(): lax.ppermute(block, axis, [(i, i ^ bit) for i in range(lax.axis_size(axis...]
    ppermute x1 -> x2, starting transfers between devices: 0.07 us -> 3.58 us  [around(): across = lax.ppermute(across, ('gy', 'gz'), route)]
    ppermute x4, waiting for transfers between devices: 5.62 us -> 4.22 us  [crossed(): return lax.ppermute(block, 'section', [(0, 1), (1, 0)])]
    ppermute x1 -> x2, waiting for transfers between devices: 2.31 us -> 1.48 us  [around(): across = lax.ppermute(across, ('gy', 'gz'), route)]
  transfers between devices with their start and end apart: 22 -> 30, of which waited for: 17 -> 17; matrix products, arithmetic and copies ran while one was open for 0% -> 0% of each run, Pallas kernels for 12% -> 12%
where the time goes in v13:
time: 78.6 us; the launch traced here: 78.4 us
  starting transfers between devices  35.2 us (45%)
  waiting for transfers between devices  22.2 us (28%)
  Pallas kernels  15.7 us (20%)
  local copies, waits for them, and re-layouts  4.15 us (5%)
  between operations  0.88 us (1%)
    ppermute x20, starting transfers between devices, swapped(): lax.ppermute(block, axis, [(i, i ^ bit) for i in range(lax.axis_size(axis...  21.8 us
    pallas_call x9, Pallas kernels, call(): pl.pallas_call(kernel, out_shape=arrays, in_specs=[VMEM] * len(args), out...  15.7 us
    ppermute x20, waiting for transfers between devices, swapped(): lax.ppermute(block, axis, [(i, i ^ bit) for i in range(lax.axis_size(axis...  11.3 us
    ppermute x3, waiting for transfers between devices, spread(): got.append(lax.ppermute(blocks[turn], 'gy', route))  5.24 us
    ppermute x4, starting transfers between devices, crossed(): return lax.ppermute(block, 'section', [(0, 1), (1, 0)])  4.81 us
    ppermute x3, starting transfers between devices, spread(): got.append(lax.ppermute(blocks[turn], 'gy', route))  4.39 us
    ppermute x4, waiting for transfers between devices, crossed(): return lax.ppermute(block, 'section', [(0, 1), (1, 0)])  4.22 us
    unnamed x8, local copies, waits for them, and re-layouts  4.04 us
  transfers between devices with their start and end apart: 30, of which 17 were waited for; matrix products, arithmetic and copies ran while one was open for 0% of the time, Pallas kernels for 12%

profile of v13, /device:TPU:0, one launch (start us, length us, event | category | flops | bytes accessed | tf_op | source)
XLA Modules:
  0.0 78.4 jit_solution(6172261531095615593)
XLA Ops:
  0.6 0.9 %copy-done.1 = f32[2,64,2,2,128]{4,3,2,1,0:T(2,128)S(1)} copy-done((f32[2,64,2,2,128]{4,3,2,1,0:T(2,128)S(1)}, f32[2,64,2,2,128]{4,3,2,1,0:T(2,128)}, u32[]{:S(2)}) %copy-start.1) | copy-done | bytes 262168
  1.6 0.9 %copy-done.2 = f32[2,64,2,2,128]{4,3,2,1,0:T(2,128)S(1)} copy-done((f32[2,64,2,2,128]{4,3,2,1,0:T(2,128)S(1)}, f32[2,64,2,2,128]{4,3,2,1,0:T(2,128)}, u32[]{:S(2)}) %copy-start.2) | copy-done | bytes 262168
  2.5 0.2 turn.1
  2.7 0.5 collective-permute-start
  3.2 0.7 collective-permute-start.1
  3.9 0.0 copy-start
  3.9 1.5 %copy-done = f32[2,27,64,64]{3,2,1,0:T(8,128)S(1)} copy-done((f32[2,27,64,64]{3,2,1,0:T(8,128)S(1)}, f32[2,27,64,64]{3,2,1,0:T(8,128)}, u32[]{:S(2)}) %copy-start) | copy-done | bytes 884760
  5.4 0.7 copy-done.3
  6.1 0.3 pack.1
  6.4 0.0 collective-permute-done.pair
  6.4 0.1 windows.1
  6.5 2.6 %collective-permute-start.2 = (f32[14,64,128]{2,1,0:T(8,128)S(1)}, f32[14,64,128]{2,1,0:T(8,128)S(1)}, u32[]{:S(2)}, u32[]{:S(2)}) collective-permute-start(f32[14,64,128]{2,1,0:T(8,128)S(1)} %get-tuple-element.67), channel_id=1, source_target_pairs={{0,16},{16,0},{1,17},{17,1},{2,18},{18,2},{3,19},{19,3},{4,20},{20... | collective-permute-start | bytes 1376264 | tf_op jit(solution)/shard_map/ppermute | solution.py:442
  9.1 1.6 %collective-permute-start.3 = (f32[2,88,128]{2,1,0:T(8,128)S(1)}, f32[2,88,128]{2,1,0:T(8,128)S(1)}, u32[]{:S(2)}, u32[]{:S(2)}) collective-permute-start(f32[2,88,128]{2,1,0:T(8,128)S(1)} %get-tuple-element.69), channel_id=1, source_target_pairs={{0,4},{4,0},{8,12},{12,8},{1,5},{5,1},{9,13},{13,9},{2,6},{6,2},{1... | collective-permute-start | bytes 270344 | tf_op jit(solution)/shard_map/ppermute | solution.py:430
  10.7 2.6 %collective-permute-start.5 = (f32[2,88,128]{2,1,0:T(8,128)S(1)}, f32[2,88,128]{2,1,0:T(8,128)S(1)}, u32[]{:S(2)}, u32[]{:S(2)}) collective-permute-start(f32[2,88,128]{2,1,0:T(8,128)S(1)} %get-tuple-element.70), channel_id=1, source_target_pairs={{0,8},{4,12},{8,0},{12,4},{1,9},{5,13},{9,1},{13,5},{2,10},{6,14},... | collective-permute-start | bytes 270344 | tf_op jit(solution)/shard_map/ppermute | solution.py:430
  13.3 0.2 collective-permute-start.6
  13.5 0.1 collective-permute-done.3.refs_1_
  13.6 0.2 collective-permute-start.4
  13.8 0.7 own_table.1
  14.5 2.8 %collective-permute-done.5.refs_2_ = f32[2,88,128]{2,1,0:T(8,128)S(1)} collective-permute-done((f32[2,88,128]{2,1,0:T(8,128)S(1)}, f32[2,88,128]{2,1,0:T(8,128)S(1)}, u32[]{:S(2)}, u32[]{:S(2)}) %collective-permute-start.5) | collective-permute-done | bytes 90144 | tf_op jit(solution)/shard_map/ppermute | solution.py:430
  17.4 2.3 %collective-permute-done.6.refs_3_ = f32[2,88,128]{2,1,0:T(8,128)S(1)} collective-permute-done((f32[2,88,128]{2,1,0:T(8,128)S(1)}, f32[2,88,128]{2,1,0:T(8,128)S(1)}, u32[]{:S(2)}, u32[]{:S(2)}) %collective-permute-start.6) | collective-permute-done | bytes 90144 | tf_op jit(solution)/shard_map/ppermute | solution.py:430
  19.6 0.3 collective-permute-done.4.refs_5_
  19.9 0.0 collective-permute-done.2.refs_0_
  19.9 2.3 %collective-permute-start.7 = (f32[14,64,128]{2,1,0:T(8,128)S(1)}, f32[14,64,128]{2,1,0:T(8,128)S(1)}, u32[]{:S(2)}, u32[]{:S(2)}) collective-permute-start(f32[14,64,128]{2,1,0:T(8,128)S(1)} %collective-permute-done.2.refs_0_), channel_id=1, source_target_pairs={{0,1},{1,0},{2,3},{3,2},{4,5},{5,4},{6,7},{7,6},{8,9},{9,8},{10,11... | collective-permute-start | bytes 1376264 | tf_op jit(solution)/shard_map/ppermute | solution.py:438
  22.2 2.0 %collective-permute-start.8 = (f32[2,88,128]{2,1,0:T(8,128)S(1)}, f32[2,88,128]{2,1,0:T(8,128)S(1)}, u32[]{:S(2)}, u32[]{:S(2)}) collective-permute-start(f32[2,88,128]{2,1,0:T(8,128)S(1)} %collective-permute-done.5.refs_2_), channel_id=1, source_target_pairs={{0,16},{16,0},{1,17},{17,1},{2,18},{18,2},{3,19},{19,3},{4,20},{20... | collective-permute-start | bytes 270344 | tf_op jit(solution)/shard_map/ppermute | solution.py:442
  24.3 0.0 collective-permute-start.9
  24.3 0.8 far_table.1
  25.1 2.5 %collective-permute-done.8.refs_6_ = f32[2,88,128]{2,1,0:T(8,128)S(1)} collective-permute-done((f32[2,88,128]{2,1,0:T(8,128)S(1)}, f32[2,88,128]{2,1,0:T(8,128)S(1)}, u32[]{:S(2)}, u32[]{:S(2)}) %collective-permute-start.8) | collective-permute-done | bytes 90144 | tf_op jit(solution)/shard_map/ppermute | solution.py:442
  27.5 1.4 %collective-permute-done.9.refs_7_ = f32[2,88,128]{2,1,0:T(8,128)S(1)} collective-permute-done((f32[2,88,128]{2,1,0:T(8,128)S(1)}, f32[2,88,128]{2,1,0:T(8,128)S(1)}, u32[]{:S(2)}, u32[]{:S(2)}) %collective-permute-start.9) | collective-permute-done | bytes 90144 | tf_op jit(solution)/shard_map/ppermute | solution.py:442
  29.0 4.5 %forward.1 = (bf16[5,2,480,256]{3,2,1,0:T(8,128)(2,1)S(1)}, f32[4,2,384,128]{3,2,1,0:T(8,128)S(1)}, f32[2,2,32,128]{3,2,1,0:T(8,128)S(1)}, f32[2,2,32,128]{3,2,1...) custom-call(bf16[2,1920,256]{2,1,0:T(8,128)(2,1)S(1)} %get-tuple-element.74.own, ...), custom_call_target="tpu_custom_call" | custom-call | bytes 1024 | tf_op jit(solution)/shard_map/forward/pallas_call | solution.py:24
  33.5 2.9 %collective-permute-start.10 = (f32[2,2,2,32,128]{4,3,2,1,0:T(8,128)S(1)}, f32[2,2,2,32,128]{4,3,2,1,0:T(8,128)S(1)}, u32[]{:S(2)}, u32[]{:S(2)}) collective-permute-start(f32[2,2,2,32,128]{4,3,2,1,0:T(8,128)S(1)} %pad_maximum_fusion.3), channel_id=1, source_target_pairs={{0,8},{4,12},{8,0},{12,4},{1,9},{5,13},{9,1},{13,5},{2,10},{6,14},... | collective-permute-start | bytes 393224 | tf_op jit(solution)/shard_map/ppermute | solution.py:438
  36.4 6.5 %backward.1 = (f32[2,2,32,128]{3,2,1,0:T(8,128)S(1)}, f32[2,2,32,128]{3,2,1,0:T(8,128)S(1)}, f32[2,2,32,128]{3,2,1,0:T(8,128)S(1)}, f32[2,2,32,128]{3,2,1,0:T(8,128)S(1)}, f32[28,64,128]{2,1,0:T(8,128)S(1)}) custom-call(bf16[2,1920,256]{2,1,0:T(8,128)(2,1)S(1)} %get-tuple-element.57.own, bf16[2,1920,256]{2,1,0:T(8,128)(2,1)S(1)} %get-tuple-element.73.other, ...), custom_call_target="tpu_custom_call" | custom-call | flops 4076863488 | bytes 1024 | tf_op jit(solution)/shard_map/backward/pallas_call | solution.py:24
  42.9 0.1 fusion
  43.0 0.1 collective-permute-start.11
  43.1 0.5 collective-permute-start.12
  43.6 1.0 %collective-permute-done.11 = f32[448,128]{1,0:T(8,128)S(1)} collective-permute-done((f32[448,128]{1,0:T(8,128)S(1)}, f32[448,128]{1,0:T(8,128)S(1)}, u32[]{:S(2)}, u32[]{:S(2)}) %collective-permute-start.11) | collective-permute-done | bytes 229408 | tf_op jit(solution)/shard_map/ppermute | solution.py:438
  44.6 0.3 collective-permute-done.12
  45.0 1.8 %collective-permute-start.13 = (f32[224,128]{1,0:T(8,128)S(1)}, f32[224,128]{1,0:T(8,128)S(1)}, u32[]{:S(2)}, u32[]{:S(2)}) collective-permute-start(f32[224,128]{1,0:T(8,128)S(1)} %slice.99), channel_id=1, source_target_pairs={{0,2},{1,3},{2,0},{3,1},{4,6},{5,7},{6,4},{7,5},{8,10},{9,11},{10,... | collective-permute-start | bytes 344072 | tf_op jit(solution)/shard_map/ppermute | solution.py:438
  46.8 0.3 collective-permute-start.17
  47.1 1.6 %collective-permute-start.14 = (f32[3,2,2,32,128]{4,3,2,1,0:T(8,128)S(1)}, f32[3,2,2,32,128]{4,3,2,1,0:T(8,128)S(1)}, u32[]{:S(2)}, u32[]{:S(2)}) collective-permute-start(f32[3,2,2,32,128]{4,3,2,1,0:T(8,128)S(1)} %pad_maximum_fusion.2), channel_id=1, source_target_pairs={{0,4},{4,0},{8,12},{12,8},{1,5},{5,1},{9,13},{13,9},{2,6},{6,2},{1... | collective-permute-start | bytes 589832 | tf_op jit(solution)/shard_map/ppermute | solution.py:438
  48.8 1.9 %collective-permute-start.15 = (f32[2,2,32,128]{3,2,1,0:T(8,128)S(1)}, f32[2,2,32,128]{3,2,1,0:T(8,128)S(1)}, u32[]{:S(2)}, u32[]{:S(2)}) collective-permute-start(f32[2,2,32,128]{3,2,1,0:T(8,128)S(1)} %get-tuple-element.96), channel_id=1, source_target_pairs={{0,8},{4,12},{8,0},{12,4},{1,9},{5,13},{9,1},{13,5},{2,10},{6,14},... | collective-permute-start | bytes 196616 | tf_op jit(solution)/shard_map/ppermute | solution.py:438
  50.7 0.9 %collective-permute-start.16 = (f32[2,2,32,128]{3,2,1,0:T(8,128)S(1)}, f32[2,2,32,128]{3,2,1,0:T(8,128)S(1)}, u32[]{:S(2)}, u32[]{:S(2)}) collective-permute-start(f32[2,2,32,128]{3,2,1,0:T(8,128)S(1)} %get-tuple-element.97), channel_id=1, source_target_pairs={{0,12},{4,8},{8,4},{12,0},{1,13},{5,9},{9,5},{13,1},{2,14},{6,10},... | collective-permute-start | bytes 196616 | tf_op jit(solution)/shard_map/ppermute | solution.py:438
  51.6 1.1 %collective-permute-done.17 = f32[224,128]{1,0:T(8,128)S(1)} collective-permute-done((f32[224,128]{1,0:T(8,128)S(1)}, f32[224,128]{1,0:T(8,128)S(1)}, u32[]{:S(2)}, u32[]{:S(2)}) %collective-permute-start.17) | collective-permute-done | bytes 114720 | tf_op jit(solution)/shard_map/ppermute | solution.py:438
  52.8 1.6 %collective-permute-start.18 = (f32[112,128]{1,0:T(8,128)S(1)}, f32[112,128]{1,0:T(8,128)S(1)}, u32[]{:S(2)}, u32[]{:S(2)}) collective-permute-start(f32[112,128]{1,0:T(8,128)S(1)} %slice_select_fusion), channel_id=1, source_target_pairs={{0,4},{4,0},{8,12},{12,8},{1,5},{5,1},{9,13},{13,9},{2,6},{6,2},{1... | collective-permute-start | bytes 172040 | tf_op jit(solution)/shard_map/ppermute | solution.py:438
  54.4 1.1 %collective-permute-done.15.refs_6_ = f32[2,2,32,128]{3,2,1,0:T(8,128)S(1)} collective-permute-done((f32[2,2,32,128]{3,2,1,0:T(8,128)S(1)}, f32[2,2,32,128]{3,2,1,0:T(8,128)S(1)}, u32[]{:S(2)}, u32[]{:S(2)}) %collective-permute-start.15) | collective-permute-done | bytes 65568 | tf_op jit(solution)/shard_map/ppermute | solution.py:438
  55.5 3.0 %collective-permute-done.16.refs_7_ = f32[2,2,32,128]{3,2,1,0:T(8,128)S(1)} collective-permute-done((f32[2,2,32,128]{3,2,1,0:T(8,128)S(1)}, f32[2,2,32,128]{3,2,1,0:T(8,128)S(1)}, u32[]{:S(2)}, u32[]{:S(2)}) %collective-permute-start.16) | collective-permute-done | bytes 65568 | tf_op jit(solution)/shard_map/ppermute | solution.py:438
  58.6 0.1 collective-permute-start.23
  58.7 2.6 %collective-permute-start.19 = (f32[112,128]{1,0:T(8,128)S(1)}, f32[112,128]{1,0:T(8,128)S(1)}, u32[]{:S(2)}, u32[]{:S(2)}) collective-permute-start(f32[112,128]{1,0:T(8,128)S(1)} %select_add_fusion.1), channel_id=1, source_target_pairs={{0,8},{4,12},{8,0},{12,4},{1,9},{5,13},{9,1},{13,5},{2,10},{6,14},... | collective-permute-start | bytes 172040 | tf_op jit(solution)/shard_map/ppermute | solution.py:438
  61.3 1.5 %collective-permute-done.23 = f32[112,128]{1,0:T(8,128)S(1)} collective-permute-done((f32[112,128]{1,0:T(8,128)S(1)}, f32[112,128]{1,0:T(8,128)S(1)}, u32[]{:S(2)}, u32[]{:S(2)}) %collective-permute-start.23) | collective-permute-done | bytes 57376 | tf_op jit(solution)/shard_map/ppermute | solution.py:438
  62.8 0.9 %collective-permute-start.24 = (f32[112,128]{1,0:T(8,128)S(1)}, f32[112,128]{1,0:T(8,128)S(1)}, u32[]{:S(2)}, u32[]{:S(2)}) collective-permute-start(f32[112,128]{1,0:T(8,128)S(1)} %select_add_fusion), channel_id=1, source_target_pairs={{0,8},{4,12},{8,0},{12,4},{1,9},{5,13},{9,1},{13,5},{2,10},{6,14},... | collective-permute-start | bytes 172040 | tf_op jit(solution)/shard_map/ppermute | solution.py:438
  63.7 1.6 %collective-permute-done.19 = f32[112,128]{1,0:T(8,128)S(1)} collective-permute-done((f32[112,128]{1,0:T(8,128)S(1)}, f32[112,128]{1,0:T(8,128)S(1)}, u32[]{:S(2)}, u32[]{:S(2)}) %collective-permute-start.19) | collective-permute-done | bytes 57376 | tf_op jit(solution)/shard_map/ppermute | solution.py:438
  65.4 1.8 %collective-permute-start.22 = (f32[112,128]{1,0:T(8,128)S(1)}, f32[112,128]{1,0:T(8,128)S(1)}, u32[]{:S(2)}, u32[]{:S(2)}) collective-permute-start(f32[112,128]{1,0:T(8,128)S(1)} %add.34), channel_id=1, source_target_pairs={{0,6},{1,7},{2,4},{3,5},{4,2},{5,3},{6,0},{7,1},{8,14},{9,15},{10,... | collective-permute-start | bytes 172040 | tf_op jit(solution)/shard_map/ppermute | solution.py:451
  67.2 0.3 collective-permute-start.21
  67.5 1.5 %collective-permute-start.20 = (f32[112,128]{1,0:T(8,128)S(1)}, f32[112,128]{1,0:T(8,128)S(1)}, u32[]{:S(2)}, u32[]{:S(2)}) collective-permute-start(f32[112,128]{1,0:T(8,128)S(1)} %add.34), channel_id=1, source_target_pairs={{0,4},{4,0},{8,12},{12,8},{1,5},{5,1},{9,13},{13,9},{2,6},{6,2},{1... | collective-permute-start | bytes 172040 | tf_op jit(solution)/shard_map/ppermute | solution.py:438
  68.9 1.8 %collective-permute-start.27 = (f32[112,128]{1,0:T(8,128)S(1)}, f32[112,128]{1,0:T(8,128)S(1)}, u32[]{:S(2)}, u32[]{:S(2)}) collective-permute-start(f32[112,128]{1,0:T(8,128)S(1)} %add.36), channel_id=1, source_target_pairs={{0,6},{1,7},{2,4},{3,5},{4,2},{5,3},{6,0},{7,1},{8,14},{9,15},{10,... | collective-permute-start | bytes 172040 | tf_op jit(solution)/shard_map/ppermute | solution.py:451
  70.7 0.3 collective-permute-start.26
  71.0 1.5 %collective-permute-start.25 = (f32[112,128]{1,0:T(8,128)S(1)}, f32[112,128]{1,0:T(8,128)S(1)}, u32[]{:S(2)}, u32[]{:S(2)}) collective-permute-start(f32[112,128]{1,0:T(8,128)S(1)} %add.36), channel_id=1, source_target_pairs={{0,4},{4,0},{8,12},{12,8},{1,5},{5,1},{9,13},{13,9},{2,6},{6,2},{1... | collective-permute-start | bytes 172040 | tf_op jit(solution)/shard_map/ppermute | solution.py:438
  72.5 0.1 collective-permute-start.28
  72.6 1.5 %collective-permute-done.27 = f32[112,128]{1,0:T(8,128)S(1)} collective-permute-done((f32[112,128]{1,0:T(8,128)S(1)}, f32[112,128]{1,0:T(8,128)S(1)}, u32[]{:S(2)}, u32[]{:S(2)}) %collective-permute-start.27) | collective-permute-done | bytes 57376 | tf_op jit(solution)/shard_map/ppermute | solution.py:451
  74.1 0.8 %collective-permute-done.26 = f32[112,128]{1,0:T(8,128)S(1)} collective-permute-done((f32[112,128]{1,0:T(8,128)S(1)}, f32[112,128]{1,0:T(8,128)S(1)}, u32[]{:S(2)}, u32[]{:S(2)}) %collective-permute-start.26) | collective-permute-done | bytes 57376 | tf_op jit(solution)/shard_map/ppermute | solution.py:438
  74.9 0.3 collective-permute-done.25
  75.2 0.1 collective-permute-start.29
  75.3 1.0 %restore.1 = (f32[512,128]{1,0:T(8,128)}, f32[512,128]{1,0:T(8,128)}) custom-call(f32[2,2,32,128]{3,2,1,0:T(8,128)S(1)} %get-tuple-element.92.refs_0_, f32[2,2,32,128]{3,2,1,0:T(8,128)S(1)} %get-tuple-element.114.refs_1_, f32[2,2,32,128]{3,2,1,0:T(8,128)S(1)} %get-tuple-element.115.refs_2_, f32[2,2,32,128]{3,2,1,0:T(8,128)S(1)} %get-tuple-element.113.refs_3_, ...), custom_call_target="tpu_custom_call" | custom-call | bytes 1024 | tf_op jit(solution)/shard_map/restore/pallas_call | solution.py:24
  76.3 0.5 collective-permute-done.29.refs_3_
  76.8 1.6 %unpack.1 = (f32[2,27,64,64]{3,2,1,0:T(8,128)}, f32[2,64]{1,0:T(2,128)}) custom-call(f32[448,128]{1,0:T(8,128)S(1)} %pad_maximum_fusion.refs_0_, f32[448,128]{1,0:T(8,128)S(1)} %pad_maximum_fusion.1.refs_1_, f32[448,128]{1,0:T(8,128)S(1)} %collective-permute-done.28.refs_2_, f32[448,128]{1,0:T(8,128)S(1)} %collective-permute-done.29.refs_3_), custom_call_target="tpu_custom_call" | custom-call | bytes 1024 | tf_op jit(solution)/shard_map/unpack/pallas_call | solution.py:24
  (32 shorter events, 0.3 us)
Async XLA Ops:
  0.6 1.0 %copy-start.1 = (f32[2,64,2,2,128]{4,3,2,1,0:T(2,128)S(1)}, f32[2,64,2,2,128]{4,3,2,1,0:T(2,128)}, u32[]{:S(2)}) copy-start(f32[2,64,2,2,128]{4,3,2,1,0:T(2,128)} %param.4) | copy-start | bytes 786436
  1.6 0.9 %copy-start.2 = (f32[2,64,2,2,128]{4,3,2,1,0:T(2,128)S(1)}, f32[2,64,2,2,128]{4,3,2,1,0:T(2,128)}, u32[]{:S(2)}) copy-start(f32[2,64,2,2,128]{4,3,2,1,0:T(2,128)} %param.7) | copy-start | bytes 786436
  2.7 3.7 %collective-permute-start = (f32[2,2,2,8,128]{4,3,2,1,0:T(8,128)S(1)}, f32[2,2,2,8,128]{4,3,2,1,0:T(8,128)S(1)}, u32[]{:S(2)}, u32[]{:S(2)}) collective-permute-start(f32[2,2,2,8,128]{4,3,2,1,0:T(8,128)S(1)} %get-tuple-element.60), channel_id=1, source_target_pairs={{0,1},{1,0},{2,3},{3,2},{4,5},{5,4},{6,7},{7,6},{8,9},{9,8},{10,11... | collective-permute-start | bytes 98312 | tf_op jit(solution)/shard_map/ppermute | solution.py:438
  3.2 3.2 %collective-permute-start.1 = (f32[2,2,2,8,128]{4,3,2,1,0:T(8,128)S(1)}, f32[2,2,2,8,128]{4,3,2,1,0:T(8,128)S(1)}, u32[]{:S(2)}, u32[]{:S(2)}) collective-permute-start(f32[2,2,2,8,128]{4,3,2,1,0:T(8,128)S(1)} %get-tuple-element.61), channel_id=1, source_target_pairs={{1,2},{2,1},{5,6},{6,5},{9,10},{10,9},{13,14},{14,13},{17,18},{18,... | collective-permute-start | bytes 98312 | tf_op jit(solution)/shard_map/ppermute | solution.py:478
  3.9 1.5 %copy-start = (f32[2,27,64,64]{3,2,1,0:T(8,128)S(1)}, f32[2,27,64,64]{3,2,1,0:T(8,128)}, u32[]{:S(2)}) copy-start(f32[2,27,64,64]{3,2,1,0:T(8,128)} %weights.1) | copy-start | bytes 2654212
  5.4 0.7 copy-start.3
  6.5 13.4 %collective-permute-start.2 = (f32[14,64,128]{2,1,0:T(8,128)S(1)}, f32[14,64,128]{2,1,0:T(8,128)S(1)}, u32[]{:S(2)}, u32[]{:S(2)}) collective-permute-start(f32[14,64,128]{2,1,0:T(8,128)S(1)} %get-tuple-element.67), channel_id=1, source_target_pairs={{0,16},{16,0},{1,17},{17,1},{2,18},{18,2},{3,19},{19,3},{4,20},{20... | collective-permute-start | bytes 1376264 | tf_op jit(solution)/shard_map/ppermute | solution.py:442
  9.1 4.5 %collective-permute-start.3 = (f32[2,88,128]{2,1,0:T(8,128)S(1)}, f32[2,88,128]{2,1,0:T(8,128)S(1)}, u32[]{:S(2)}, u32[]{:S(2)}) collective-permute-start(f32[2,88,128]{2,1,0:T(8,128)S(1)} %get-tuple-element.69), channel_id=1, source_target_pairs={{0,4},{4,0},{8,12},{12,8},{1,5},{5,1},{9,13},{13,9},{2,6},{6,2},{1... | collective-permute-start | bytes 270344 | tf_op jit(solution)/shard_map/ppermute | solution.py:430
  10.7 6.7 %collective-permute-start.5 = (f32[2,88,128]{2,1,0:T(8,128)S(1)}, f32[2,88,128]{2,1,0:T(8,128)S(1)}, u32[]{:S(2)}, u32[]{:S(2)}) collective-permute-start(f32[2,88,128]{2,1,0:T(8,128)S(1)} %get-tuple-element.70), channel_id=1, source_target_pairs={{0,8},{4,12},{8,0},{12,4},{1,9},{5,13},{9,1},{13,5},{2,10},{6,14},... | collective-permute-start | bytes 270344 | tf_op jit(solution)/shard_map/ppermute | solution.py:430
  13.3 6.3 %collective-permute-start.6 = (f32[2,88,128]{2,1,0:T(8,128)S(1)}, f32[2,88,128]{2,1,0:T(8,128)S(1)}, u32[]{:S(2)}, u32[]{:S(2)}) collective-permute-start(f32[2,88,128]{2,1,0:T(8,128)S(1)} %get-tuple-element.71), channel_id=1, source_target_pairs={{0,12},{4,8},{8,4},{12,0},{1,13},{5,9},{9,5},{13,1},{2,14},{6,10},... | collective-permute-start | bytes 270344 | tf_op jit(solution)/shard_map/ppermute | solution.py:430
  13.6 6.3 %collective-permute-start.4 = (f32[2,88,128]{2,1,0:T(8,128)S(1)}, f32[2,88,128]{2,1,0:T(8,128)S(1)}, u32[]{:S(2)}, u32[]{:S(2)}) collective-permute-start(f32[2,88,128]{2,1,0:T(8,128)S(1)} %collective-permute-done.3.refs_1_), channel_id=1, source_target_pairs={{0,16},{16,0},{1,17},{17,1},{2,18},{18,2},{3,19},{19,3},{4,20},{20... | collective-permute-start | bytes 270344 | tf_op jit(solution)/shard_map/ppermute | solution.py:442
  19.9 4.4 %collective-permute-start.7 = (f32[14,64,128]{2,1,0:T(8,128)S(1)}, f32[14,64,128]{2,1,0:T(8,128)S(1)}, u32[]{:S(2)}, u32[]{:S(2)}) collective-permute-start(f32[14,64,128]{2,1,0:T(8,128)S(1)} %collective-permute-done.2.refs_0_), channel_id=1, source_target_pairs={{0,1},{1,0},{2,3},{3,2},{4,5},{5,4},{6,7},{7,6},{8,9},{9,8},{10,11... | collective-permute-start | bytes 1376264 | tf_op jit(solution)/shard_map/ppermute | solution.py:438
  22.2 5.3 %collective-permute-start.8 = (f32[2,88,128]{2,1,0:T(8,128)S(1)}, f32[2,88,128]{2,1,0:T(8,128)S(1)}, u32[]{:S(2)}, u32[]{:S(2)}) collective-permute-start(f32[2,88,128]{2,1,0:T(8,128)S(1)} %collective-permute-done.5.refs_2_), channel_id=1, source_target_pairs={{0,16},{16,0},{1,17},{17,1},{2,18},{18,2},{3,19},{19,3},{4,20},{20... | collective-permute-start | bytes 270344 | tf_op jit(solution)/shard_map/ppermute | solution.py:442
  24.3 4.7 %collective-permute-start.9 = (f32[2,88,128]{2,1,0:T(8,128)S(1)}, f32[2,88,128]{2,1,0:T(8,128)S(1)}, u32[]{:S(2)}, u32[]{:S(2)}) collective-permute-start(f32[2,88,128]{2,1,0:T(8,128)S(1)} %collective-permute-done.6.refs_3_), channel_id=1, source_target_pairs={{0,16},{16,0},{1,17},{17,1},{2,18},{18,2},{3,19},{19,3},{4,20},{20... | collective-permute-start | bytes 270344 | tf_op jit(solution)/shard_map/ppermute | solution.py:442
  33.5 9.4 %collective-permute-start.10 = (f32[2,2,2,32,128]{4,3,2,1,0:T(8,128)S(1)}, f32[2,2,2,32,128]{4,3,2,1,0:T(8,128)S(1)}, u32[]{:S(2)}, u32[]{:S(2)}) collective-permute-start(f32[2,2,2,32,128]{4,3,2,1,0:T(8,128)S(1)} %pad_maximum_fusion.3), channel_id=1, source_target_pairs={{0,8},{4,12},{8,0},{12,4},{1,9},{5,13},{9,1},{13,5},{2,10},{6,14},... | collective-permute-start | bytes 393224 | tf_op jit(solution)/shard_map/ppermute | solution.py:438
  43.0 1.6 %collective-permute-start.11 = (f32[448,128]{1,0:T(8,128)S(1)}, f32[448,128]{1,0:T(8,128)S(1)}, u32[]{:S(2)}, u32[]{:S(2)}) collective-permute-start(f32[448,128]{1,0:T(8,128)S(1)} %bitcast.39), channel_id=1, source_target_pairs={{0,1},{1,0},{2,3},{3,2},{4,5},{5,4},{6,7},{7,6},{8,9},{9,8},{10,11... | collective-permute-start | bytes 688136 | tf_op jit(solution)/shard_map/ppermute | solution.py:438
  43.1 1.8 %collective-permute-start.12 = (f32[448,128]{1,0:T(8,128)S(1)}, f32[448,128]{1,0:T(8,128)S(1)}, u32[]{:S(2)}, u32[]{:S(2)}) collective-permute-start(f32[448,128]{1,0:T(8,128)S(1)} %bitcast.38), channel_id=1, source_target_pairs={{0,1},{1,0},{2,3},{3,2},{4,5},{5,4},{6,7},{7,6},{8,9},{9,8},{10,11... | collective-permute-start | bytes 688136 | tf_op jit(solution)/shard_map/ppermute | solution.py:438
  45.0 9.5 %collective-permute-start.13 = (f32[224,128]{1,0:T(8,128)S(1)}, f32[224,128]{1,0:T(8,128)S(1)}, u32[]{:S(2)}, u32[]{:S(2)}) collective-permute-start(f32[224,128]{1,0:T(8,128)S(1)} %slice.99), channel_id=1, source_target_pairs={{0,2},{1,3},{2,0},{3,1},{4,6},{5,7},{6,4},{7,5},{8,10},{9,11},{10,... | collective-permute-start | bytes 344072 | tf_op jit(solution)/shard_map/ppermute | solution.py:438
  46.8 5.9 %collective-permute-start.17 = (f32[224,128]{1,0:T(8,128)S(1)}, f32[224,128]{1,0:T(8,128)S(1)}, u32[]{:S(2)}, u32[]{:S(2)}) collective-permute-start(f32[224,128]{1,0:T(8,128)S(1)} %slice.89), channel_id=1, source_target_pairs={{0,2},{1,3},{2,0},{3,1},{4,6},{5,7},{6,4},{7,5},{8,10},{9,11},{10,... | collective-permute-start | bytes 344072 | tf_op jit(solution)/shard_map/ppermute | solution.py:438
  47.1 11.4 %collective-permute-start.14 = (f32[3,2,2,32,128]{4,3,2,1,0:T(8,128)S(1)}, f32[3,2,2,32,128]{4,3,2,1,0:T(8,128)S(1)}, u32[]{:S(2)}, u32[]{:S(2)}) collective-permute-start(f32[3,2,2,32,128]{4,3,2,1,0:T(8,128)S(1)} %pad_maximum_fusion.2), channel_id=1, source_target_pairs={{0,4},{4,0},{8,12},{12,8},{1,5},{5,1},{9,13},{13,9},{2,6},{6,2},{1... | collective-permute-start | bytes 589832 | tf_op jit(solution)/shard_map/ppermute | solution.py:438
  48.8 6.7 %collective-permute-start.15 = (f32[2,2,32,128]{3,2,1,0:T(8,128)S(1)}, f32[2,2,32,128]{3,2,1,0:T(8,128)S(1)}, u32[]{:S(2)}, u32[]{:S(2)}) collective-permute-start(f32[2,2,32,128]{3,2,1,0:T(8,128)S(1)} %get-tuple-element.96), channel_id=1, source_target_pairs={{0,8},{4,12},{8,0},{12,4},{1,9},{5,13},{9,1},{13,5},{2,10},{6,14},... | collective-permute-start | bytes 196616 | tf_op jit(solution)/shard_map/ppermute | solution.py:438
  50.7 7.8 %collective-permute-start.16 = (f32[2,2,32,128]{3,2,1,0:T(8,128)S(1)}, f32[2,2,32,128]{3,2,1,0:T(8,128)S(1)}, u32[]{:S(2)}, u32[]{:S(2)}) collective-permute-start(f32[2,2,32,128]{3,2,1,0:T(8,128)S(1)} %get-tuple-element.97), channel_id=1, source_target_pairs={{0,12},{4,8},{8,4},{12,0},{1,13},{5,9},{9,5},{13,1},{2,14},{6,10},... | collective-permute-start | bytes 196616 | tf_op jit(solution)/shard_map/ppermute | solution.py:438
  52.8 5.9 %collective-permute-start.18 = (f32[112,128]{1,0:T(8,128)S(1)}, f32[112,128]{1,0:T(8,128)S(1)}, u32[]{:S(2)}, u32[]{:S(2)}) collective-permute-start(f32[112,128]{1,0:T(8,128)S(1)} %slice_select_fusion), channel_id=1, source_target_pairs={{0,4},{4,0},{8,12},{12,8},{1,5},{5,1},{9,13},{13,9},{2,6},{6,2},{1... | collective-permute-start | bytes 172040 | tf_op jit(solution)/shard_map/ppermute | solution.py:438
  58.6 4.2 %collective-permute-start.23 = (f32[112,128]{1,0:T(8,128)S(1)}, f32[112,128]{1,0:T(8,128)S(1)}, u32[]{:S(2)}, u32[]{:S(2)}) collective-permute-start(f32[112,128]{1,0:T(8,128)S(1)} %slice_select_fusion.1), channel_id=1, source_target_pairs={{0,4},{4,0},{8,12},{12,8},{1,5},{5,1},{9,13},{13,9},{2,6},{6,2},{1... | collective-permute-start | bytes 172040 | tf_op jit(solution)/shard_map/ppermute | solution.py:438
  58.7 6.7 %collective-permute-start.19 = (f32[112,128]{1,0:T(8,128)S(1)}, f32[112,128]{1,0:T(8,128)S(1)}, u32[]{:S(2)}, u32[]{:S(2)}) collective-permute-start(f32[112,128]{1,0:T(8,128)S(1)} %select_add_fusion.1), channel_id=1, source_target_pairs={{0,8},{4,12},{8,0},{12,4},{1,9},{5,13},{9,1},{13,5},{2,10},{6,14},... | collective-permute-start | bytes 172040 | tf_op jit(solution)/shard_map/ppermute | solution.py:438
  62.8 6.1 %collective-permute-start.24 = (f32[112,128]{1,0:T(8,128)S(1)}, f32[112,128]{1,0:T(8,128)S(1)}, u32[]{:S(2)}, u32[]{:S(2)}) collective-permute-start(f32[112,128]{1,0:T(8,128)S(1)} %select_add_fusion), channel_id=1, source_target_pairs={{0,8},{4,12},{8,0},{12,4},{1,9},{5,13},{9,1},{13,5},{2,10},{6,14},... | collective-permute-start | bytes 172040 | tf_op jit(solution)/shard_map/ppermute | solution.py:438
  65.4 5.7 %collective-permute-start.22 = (f32[112,128]{1,0:T(8,128)S(1)}, f32[112,128]{1,0:T(8,128)S(1)}, u32[]{:S(2)}, u32[]{:S(2)}) collective-permute-start(f32[112,128]{1,0:T(8,128)S(1)} %add.34), channel_id=1, source_target_pairs={{0,6},{1,7},{2,4},{3,5},{4,2},{5,3},{6,0},{7,1},{8,14},{9,15},{10,... | collective-permute-start | bytes 172040 | tf_op jit(solution)/shard_map/ppermute | solution.py:451
  67.2 5.3 %collective-permute-start.21 = (f32[112,128]{1,0:T(8,128)S(1)}, f32[112,128]{1,0:T(8,128)S(1)}, u32[]{:S(2)}, u32[]{:S(2)}) collective-permute-start(f32[112,128]{1,0:T(8,128)S(1)} %add.34), channel_id=1, source_target_pairs={{0,2},{1,3},{2,0},{3,1},{4,6},{5,7},{6,4},{7,5},{8,10},{9,11},{10,... | collective-permute-start | bytes 172040 | tf_op jit(solution)/shard_map/ppermute | solution.py:438
  67.5 5.0 %collective-permute-start.20 = (f32[112,128]{1,0:T(8,128)S(1)}, f32[112,128]{1,0:T(8,128)S(1)}, u32[]{:S(2)}, u32[]{:S(2)}) collective-permute-start(f32[112,128]{1,0:T(8,128)S(1)} %add.34), channel_id=1, source_target_pairs={{0,4},{4,0},{8,12},{12,8},{1,5},{5,1},{9,13},{13,9},{2,6},{6,2},{1... | collective-permute-start | bytes 172040 | tf_op jit(solution)/shard_map/ppermute | solution.py:438
  68.9 5.1 %collective-permute-start.27 = (f32[112,128]{1,0:T(8,128)S(1)}, f32[112,128]{1,0:T(8,128)S(1)}, u32[]{:S(2)}, u32[]{:S(2)}) collective-permute-start(f32[112,128]{1,0:T(8,128)S(1)} %add.36), channel_id=1, source_target_pairs={{0,6},{1,7},{2,4},{3,5},{4,2},{5,3},{6,0},{7,1},{8,14},{9,15},{10,... | collective-permute-start | bytes 172040 | tf_op jit(solution)/shard_map/ppermute | solution.py:451
  70.7 4.2 %collective-permute-start.26 = (f32[112,128]{1,0:T(8,128)S(1)}, f32[112,128]{1,0:T(8,128)S(1)}, u32[]{:S(2)}, u32[]{:S(2)}) collective-permute-start(f32[112,128]{1,0:T(8,128)S(1)} %add.36), channel_id=1, source_target_pairs={{0,2},{1,3},{2,0},{3,1},{4,6},{5,7},{6,4},{7,5},{8,10},{9,11},{10,... | collective-permute-start | bytes 172040 | tf_op jit(solution)/shard_map/ppermute | solution.py:438
  71.0 4.2 %collective-permute-start.25 = (f32[112,128]{1,0:T(8,128)S(1)}, f32[112,128]{1,0:T(8,128)S(1)}, u32[]{:S(2)}, u32[]{:S(2)}) collective-permute-start(f32[112,128]{1,0:T(8,128)S(1)} %add.36), channel_id=1, source_target_pairs={{0,4},{4,0},{8,12},{12,8},{1,5},{5,1},{9,13},{13,9},{2,6},{6,2},{1... | collective-permute-start | bytes 172040 | tf_op jit(solution)/shard_map/ppermute | solution.py:438
  72.5 3.8 %collective-permute-start.28 = (f32[448,128]{1,0:T(8,128)S(1)}, f32[448,128]{1,0:T(8,128)S(1)}, u32[]{:S(2)}, u32[]{:S(2)}) collective-permute-start(f32[448,128]{1,0:T(8,128)S(1)} %pad_maximum_fusion.refs_0_), channel_id=1, source_target_pairs={{0,1},{1,0},{2,3},{3,2},{4,5},{5,4},{6,7},{7,6},{8,9},{9,8},{10,11... | collective-permute-start | bytes 688136 | tf_op jit(solution)/shard_map/ppermute | solution.py:438
  75.2 1.6 %collective-permute-start.29 = (f32[448,128]{1,0:T(8,128)S(1)}, f32[448,128]{1,0:T(8,128)S(1)}, u32[]{:S(2)}, u32[]{:S(2)}) collective-permute-start(f32[448,128]{1,0:T(8,128)S(1)} %pad_maximum_fusion.1.refs_1_), channel_id=1, source_target_pairs={{0,1},{1,0},{2,3},{3,2},{4,5},{5,4},{6,7},{7,6},{8,9},{9,8},{10,11... | collective-permute-start | bytes 688136 | tf_op jit(solution)/shard_map/ppermute | solution.py:438

commit v14 on v13

--- a/solution.py
+++ b/solution.py
@@ -512,7 +512,7 @@
         [pltpu.VMEM((micros, full, LANES), F32)] * 2,
     )
     if slabs == 4:
-        passed = swapped(jnp.stack(fronts[2:]), 2, "gy")
+        passed = swapped(fronts[3], 2, "gy")
     *backs, sums = call(
         functools.partial(backward_kernel, dims, scale),
         "backward",
@@ -538,8 +538,9 @@
         streams.append(block[: 4 * part] + swapped(block[4 * part :], 1))
     streams[0], fronts, backs = lax.optimization_barrier((streams[0], fronts, backs))
     if slabs == 4:
-        near = swapped(jnp.stack([fronts[1], passed[1], backs[1]]), 1, "gy")
-        outs = [near, swapped(backs[2], 2, "gy"), swapped(backs[3], 3, "gy")]
+        near = swapped(jnp.stack([fronts[1], passed, backs[1]]), 1, "gy")
+        far = swapped(jnp.stack([fronts[2], backs[2]]), 2, "gy")
+        outs = [near, far, swapped(backs[3], 3, "gy")]
     else:
         outs = spread([jnp.stack(pair) for pair in zip(fronts, backs)])
     streams = [block[: 2 * part] + swapped(block[2 * part :], 2) for block in streams]
@@ -555,7 +556,8 @@
         sums.append(jnp.concatenate([kept, *around(kept, kept, kept)], axis=0))
     sums += [swapped(block, 1) for block in sums]
     if slabs == 4:
-        outs = [fronts[0], outs[0][0], passed[0], outs[0][1], backs[0], outs[0][2], *outs[1:]]
+        near, far, last = outs
+        outs = [fronts[0], near[0], far[0], near[1], backs[0], near[2], far[1], last]
     else:
         outs = [out[slot] for slot in range(2) for out in outs]
     section_out, section_grad = call(

time: 78.6 us -> 80.7 us (1.027)
  waiting for transfers between devices: 22.2 us -> 24.9 us
    ppermute x20, waiting for transfers between devices: 11.3 us -> 14 us  [swapped(): lax.ppermute(block, axis, [(i, i ^ bit) for i in range(lax.axis_size(axis...]
    ppermute x2, starting transfers between devices: 3.58 us -> 1.95 us  [around(): across = lax.ppermute(across, ('gy', 'gz'), route)]
    ppermute x20, starting transfers between devices: 21.8 us -> 22.8 us  [swapped(): lax.ppermute(block, axis, [(i, i ^ bit) for i in range(lax.axis_size(axis...]
where the time goes in v14:
time: 80.7 us; the launch traced here: 80.4 us
  starting transfers between devices  34.6 us (43%)
  waiting for transfers between devices  24.9 us (31%)
  Pallas kernels  15.7 us (19%)
  local copies, waits for them, and re-layouts  4.15 us (5%)
  between operations  0.86 us (1%)
    ppermute x20, starting transfers between devices, swapped(): lax.ppermute(block, axis, [(i, i ^ bit) for i in range(lax.axis_size(axis...  22.8 us
    pallas_call x9, Pallas kernels, call(): pl.pallas_call(kernel, out_shape=arrays, in_specs=[VMEM] * len(args), out...  15.7 us
    ppermute x20, waiting for transfers between devices, swapped(): lax.ppermute(block, axis, [(i, i ^ bit) for i in range(lax.axis_size(axis...  14 us
    ppermute x3, waiting for transfers between devices, spread(): got.append(lax.ppermute(blocks[turn], 'gy', route))  5.24 us
    ppermute x4, starting transfers between devices, crossed(): return lax.ppermute(block, 'section', [(0, 1), (1, 0)])  4.81 us
    ppermute x3, starting transfers between devices, spread(): got.append(lax.ppermute(blocks[turn], 'gy', route))  4.39 us
    ppermute x4, waiting for transfers between devices, crossed(): return lax.ppermute(block, 'section', [(0, 1), (1, 0)])  4.21 us
    unnamed x8, local copies, waits for them, and re-layouts  4.04 us
  transfers between devices with their start and end apart: 30, of which 17 were waited for; matrix products, arithmetic and copies ran while one was open for 0% of the time, Pallas kernels for 12%

profile of v14, /device:TPU:0, one launch (start us, length us, event | category | flops | bytes accessed | tf_op | source)
XLA Modules:
  0.0 80.4 jit_solution(14539530943065603618)
XLA Ops:
  0.6 0.9 %copy-done.1 = f32[2,64,2,2,128]{4,3,2,1,0:T(2,128)S(1)} copy-done((f32[2,64,2,2,128]{4,3,2,1,0:T(2,128)S(1)}, f32[2,64,2,2,128]{4,3,2,1,0:T(2,128)}, u32[]{:S(2)}) %copy-start.1) | copy-done | bytes 262168
  1.6 0.9 %copy-done.2 = f32[2,64,2,2,128]{4,3,2,1,0:T(2,128)S(1)} copy-done((f32[2,64,2,2,128]{4,3,2,1,0:T(2,128)S(1)}, f32[2,64,2,2,128]{4,3,2,1,0:T(2,128)}, u32[]{:S(2)}) %copy-start.2) | copy-done | bytes 262168
  2.5 0.2 turn.1
  2.7 0.5 collective-permute-start
  3.2 0.7 collective-permute-start.1
  3.9 0.0 copy-start
  3.9 1.5 %copy-done = f32[2,27,64,64]{3,2,1,0:T(8,128)S(1)} copy-done((f32[2,27,64,64]{3,2,1,0:T(8,128)S(1)}, f32[2,27,64,64]{3,2,1,0:T(8,128)}, u32[]{:S(2)}) %copy-start) | copy-done | bytes 884760
  5.4 0.7 copy-done.3
  6.1 0.3 pack.1
  6.4 0.0 collective-permute-done.pair
  6.4 0.0 collective-permute-done.1.inner
  6.4 0.1 windows.1
  6.5 2.6 %collective-permute-start.2 = (f32[14,64,128]{2,1,0:T(8,128)S(1)}, f32[14,64,128]{2,1,0:T(8,128)S(1)}, u32[]{:S(2)}, u32[]{:S(2)}) collective-permute-start(f32[14,64,128]{2,1,0:T(8,128)S(1)} %get-tuple-element.68), channel_id=1, source_target_pairs={{0,16},{16,0},{1,17},{17,1},{2,18},{18,2},{3,19},{19,3},{4,20},{20... | collective-permute-start | bytes 1376264 | tf_op jit(solution)/shard_map/ppermute | solution.py:442
  9.1 1.6 %collective-permute-start.3 = (f32[2,88,128]{2,1,0:T(8,128)S(1)}, f32[2,88,128]{2,1,0:T(8,128)S(1)}, u32[]{:S(2)}, u32[]{:S(2)}) collective-permute-start(f32[2,88,128]{2,1,0:T(8,128)S(1)} %get-tuple-element.70), channel_id=1, source_target_pairs={{0,4},{4,0},{8,12},{12,8},{1,5},{5,1},{9,13},{13,9},{2,6},{6,2},{1... | collective-permute-start | bytes 270344 | tf_op jit(solution)/shard_map/ppermute | solution.py:430
  10.7 2.6 %collective-permute-start.5 = (f32[2,88,128]{2,1,0:T(8,128)S(1)}, f32[2,88,128]{2,1,0:T(8,128)S(1)}, u32[]{:S(2)}, u32[]{:S(2)}) collective-permute-start(f32[2,88,128]{2,1,0:T(8,128)S(1)} %get-tuple-element.71), channel_id=1, source_target_pairs={{0,8},{4,12},{8,0},{12,4},{1,9},{5,13},{9,1},{13,5},{2,10},{6,14},... | collective-permute-start | bytes 270344 | tf_op jit(solution)/shard_map/ppermute | solution.py:430
  13.3 0.2 collective-permute-start.6
  13.5 0.1 collective-permute-done.3.refs_1_
  13.6 0.2 collective-permute-start.4
  13.8 0.7 own_table.1
  14.5 2.8 %collective-permute-done.5.refs_2_ = f32[2,88,128]{2,1,0:T(8,128)S(1)} collective-permute-done((f32[2,88,128]{2,1,0:T(8,128)S(1)}, f32[2,88,128]{2,1,0:T(8,128)S(1)}, u32[]{:S(2)}, u32[]{:S(2)}) %collective-permute-start.5) | collective-permute-done | bytes 90144 | tf_op jit(solution)/shard_map/ppermute | solution.py:430
  17.4 2.3 %collective-permute-done.6.refs_3_ = f32[2,88,128]{2,1,0:T(8,128)S(1)} collective-permute-done((f32[2,88,128]{2,1,0:T(8,128)S(1)}, f32[2,88,128]{2,1,0:T(8,128)S(1)}, u32[]{:S(2)}, u32[]{:S(2)}) %collective-permute-start.6) | collective-permute-done | bytes 90144 | tf_op jit(solution)/shard_map/ppermute | solution.py:430
  19.6 0.3 collective-permute-done.4.refs_5_
  19.9 2.3 %collective-permute-start.7 = (f32[14,64,128]{2,1,0:T(8,128)S(1)}, f32[14,64,128]{2,1,0:T(8,128)S(1)}, u32[]{:S(2)}, u32[]{:S(2)}) collective-permute-start(f32[14,64,128]{2,1,0:T(8,128)S(1)} %collective-permute-done.2.refs_0_), channel_id=1, source_target_pairs={{0,1},{1,0},{2,3},{3,2},{4,5},{5,4},{6,7},{7,6},{8,9},{9,8},{10,11... | collective-permute-start | bytes 1376264 | tf_op jit(solution)/shard_map/ppermute | solution.py:438
  22.2 2.0 %collective-permute-start.8 = (f32[2,88,128]{2,1,0:T(8,128)S(1)}, f32[2,88,128]{2,1,0:T(8,128)S(1)}, u32[]{:S(2)}, u32[]{:S(2)}) collective-permute-start(f32[2,88,128]{2,1,0:T(8,128)S(1)} %collective-permute-done.5.refs_2_), channel_id=1, source_target_pairs={{0,16},{16,0},{1,17},{17,1},{2,18},{18,2},{3,19},{19,3},{4,20},{20... | collective-permute-start | bytes 270344 | tf_op jit(solution)/shard_map/ppermute | solution.py:442
  24.3 0.0 collective-permute-start.9
  24.3 0.8 far_table.1
  25.1 2.5 %collective-permute-done.8.refs_6_ = f32[2,88,128]{2,1,0:T(8,128)S(1)} collective-permute-done((f32[2,88,128]{2,1,0:T(8,128)S(1)}, f32[2,88,128]{2,1,0:T(8,128)S(1)}, u32[]{:S(2)}, u32[]{:S(2)}) %collective-permute-start.8) | collective-permute-done | bytes 90144 | tf_op jit(solution)/shard_map/ppermute | solution.py:442
  27.5 1.4 %collective-permute-done.9.refs_7_ = f32[2,88,128]{2,1,0:T(8,128)S(1)} collective-permute-done((f32[2,88,128]{2,1,0:T(8,128)S(1)}, f32[2,88,128]{2,1,0:T(8,128)S(1)}, u32[]{:S(2)}, u32[]{:S(2)}) %collective-permute-start.9) | collective-permute-done | bytes 90144 | tf_op jit(solution)/shard_map/ppermute | solution.py:442
  29.0 4.5 %forward.1 = (bf16[5,2,480,256]{3,2,1,0:T(8,128)(2,1)S(1)}, f32[4,2,384,128]{3,2,1,0:T(8,128)S(1)}, f32[2,2,32,128]{3,2,1,0:T(8,128)S(1)}, f32[2,2,32,128]{3,2,1...) custom-call(bf16[2,1920,256]{2,1,0:T(8,128)(2,1)S(1)} %get-tuple-element.75.own, ...), custom_call_target="tpu_custom_call" | custom-call | bytes 1024 | tf_op jit(solution)/shard_map/forward/pallas_call | solution.py:24
  33.5 2.9 %collective-permute-start.10 = (f32[2,2,32,128]{3,2,1,0:T(8,128)S(1)}, f32[2,2,32,128]{3,2,1,0:T(8,128)S(1)}, u32[]{:S(2)}, u32[]{:S(2)}) collective-permute-start(f32[2,2,32,128]{3,2,1,0:T(8,128)S(1)} %get-tuple-element.84), channel_id=1, source_target_pairs={{0,8},{4,12},{8,0},{12,4},{1,9},{5,13},{9,1},{13,5},{2,10},{6,14},... | collective-permute-start | bytes 196616 | tf_op jit(solution)/shard_map/ppermute | solution.py:438
  36.4 6.6 %backward.1 = (f32[2,2,32,128]{3,2,1,0:T(8,128)S(1)}, f32[2,2,32,128]{3,2,1,0:T(8,128)S(1)}, f32[2,2,32,128]{3,2,1,0:T(8,128)S(1)}, f32[2,2,32,128]{3,2,1,0:T(8,128)S(1)}, f32[28,64,128]{2,1,0:T(8,128)S(1)}) custom-call(bf16[2,1920,256]{2,1,0:T(8,128)(2,1)S(1)} %get-tuple-element.58.own, bf16[2,1920,256]{2,1,0:T(8,128)(2,1)S(1)} %get-tuple-element.74.other, ...), custom_call_target="tpu_custom_call" | custom-call | flops 4076863488 | bytes 1024 | tf_op jit(solution)/shard_map/backward/pallas_call | solution.py:24
  43.0 0.1 fusion
  43.0 0.1 collective-permute-start.11
  43.1 0.5 collective-permute-start.12
  43.6 1.0 %collective-permute-done.11 = f32[448,128]{1,0:T(8,128)S(1)} collective-permute-done((f32[448,128]{1,0:T(8,128)S(1)}, f32[448,128]{1,0:T(8,128)S(1)}, u32[]{:S(2)}, u32[]{:S(2)}) %collective-permute-start.11) | collective-permute-done | bytes 229408 | tf_op jit(solution)/shard_map/ppermute | solution.py:438
  44.6 0.3 collective-permute-done.12
  45.0 1.8 %collective-permute-start.13 = (f32[224,128]{1,0:T(8,128)S(1)}, f32[224,128]{1,0:T(8,128)S(1)}, u32[]{:S(2)}, u32[]{:S(2)}) collective-permute-start(f32[224,128]{1,0:T(8,128)S(1)} %slice.99), channel_id=1, source_target_pairs={{0,2},{1,3},{2,0},{3,1},{4,6},{5,7},{6,4},{7,5},{8,10},{9,11},{10,... | collective-permute-start | bytes 344072 | tf_op jit(solution)/shard_map/ppermute | solution.py:438
  46.8 1.6 %collective-permute-start.14 = (f32[3,2,2,32,128]{4,3,2,1,0:T(8,128)S(1)}, f32[3,2,2,32,128]{4,3,2,1,0:T(8,128)S(1)}, u32[]{:S(2)}, u32[]{:S(2)}) collective-permute-start(f32[3,2,2,32,128]{4,3,2,1,0:T(8,128)S(1)} %pad_maximum_fusion.2), channel_id=1, source_target_pairs={{0,4},{4,0},{8,12},{12,8},{1,5},{5,1},{9,13},{13,9},{2,6},{6,2},{1... | collective-permute-start | bytes 589832 | tf_op jit(solution)/shard_map/ppermute | solution.py:438
  48.5 0.3 collective-permute-start.17
  48.8 0.4 collective-permute-start.15
  49.2 2.5 %collective-permute-start.16 = (f32[2,2,32,128]{3,2,1,0:T(8,128)S(1)}, f32[2,2,32,128]{3,2,1,0:T(8,128)S(1)}, u32[]{:S(2)}, u32[]{:S(2)}) collective-permute-start(f32[2,2,32,128]{3,2,1,0:T(8,128)S(1)} %get-tuple-element.99), channel_id=1, source_target_pairs={{0,12},{4,8},{8,4},{12,0},{1,13},{5,9},{9,5},{13,1},{2,14},{6,10},... | collective-permute-start | bytes 196616 | tf_op jit(solution)/shard_map/ppermute | solution.py:438
  51.7 1.6 %collective-permute-done.17 = f32[224,128]{1,0:T(8,128)S(1)} collective-permute-done((f32[224,128]{1,0:T(8,128)S(1)}, f32[224,128]{1,0:T(8,128)S(1)}, u32[]{:S(2)}, u32[]{:S(2)}) %collective-permute-start.17) | collective-permute-done | bytes 114720 | tf_op jit(solution)/shard_map/ppermute | solution.py:438
  53.4 1.1 %collective-permute-start.18 = (f32[112,128]{1,0:T(8,128)S(1)}, f32[112,128]{1,0:T(8,128)S(1)}, u32[]{:S(2)}, u32[]{:S(2)}) collective-permute-start(f32[112,128]{1,0:T(8,128)S(1)} %slice_select_fusion), channel_id=1, source_target_pairs={{0,4},{4,0},{8,12},{12,8},{1,5},{5,1},{9,13},{13,9},{2,6},{6,2},{1... | collective-permute-start | bytes 172040 | tf_op jit(solution)/shard_map/ppermute | solution.py:438
  54.5 3.8 %collective-permute-done.16.refs_7_ = f32[2,2,32,128]{3,2,1,0:T(8,128)S(1)} collective-permute-done((f32[2,2,32,128]{3,2,1,0:T(8,128)S(1)}, f32[2,2,32,128]{3,2,1,0:T(8,128)S(1)}, u32[]{:S(2)}, u32[]{:S(2)}) %collective-permute-start.16) | collective-permute-done | bytes 65568 | tf_op jit(solution)/shard_map/ppermute | solution.py:438
  58.3 1.2 %collective-permute-done.15 = f32[2,2,2,32,128]{4,3,2,1,0:T(8,128)S(1)} collective-permute-done((f32[2,2,2,32,128]{4,3,2,1,0:T(8,128)S(1)}, f32[2,2,2,32,128]{4,3,2,1,0:T(8,128)S(1)}, u32[]{:S(2)}, u32[]{:S(2)}) %collective-permute-start.15) | collective-permute-done | bytes 131104 | tf_op jit(solution)/shard_map/ppermute | solution.py:438
  59.5 1.3 %collective-permute-start.23 = (f32[112,128]{1,0:T(8,128)S(1)}, f32[112,128]{1,0:T(8,128)S(1)}, u32[]{:S(2)}, u32[]{:S(2)}) collective-permute-start(f32[112,128]{1,0:T(8,128)S(1)} %slice_select_fusion.1), channel_id=1, source_target_pairs={{0,4},{4,0},{8,12},{12,8},{1,5},{5,1},{9,13},{13,9},{2,6},{6,2},{1... | collective-permute-start | bytes 172040 | tf_op jit(solution)/shard_map/ppermute | solution.py:438
  60.8 1.7 %collective-permute-start.19 = (f32[112,128]{1,0:T(8,128)S(1)}, f32[112,128]{1,0:T(8,128)S(1)}, u32[]{:S(2)}, u32[]{:S(2)}) collective-permute-start(f32[112,128]{1,0:T(8,128)S(1)} %select_add_fusion.1), channel_id=1, source_target_pairs={{0,8},{4,12},{8,0},{12,4},{1,9},{5,13},{9,1},{13,5},{2,10},{6,14},... | collective-permute-start | bytes 172040 | tf_op jit(solution)/shard_map/ppermute | solution.py:438
  62.5 1.8 %collective-permute-done.23 = f32[112,128]{1,0:T(8,128)S(1)} collective-permute-done((f32[112,128]{1,0:T(8,128)S(1)}, f32[112,128]{1,0:T(8,128)S(1)}, u32[]{:S(2)}, u32[]{:S(2)}) %collective-permute-start.23) | collective-permute-done | bytes 57376 | tf_op jit(solution)/shard_map/ppermute | solution.py:438
  64.3 0.3 collective-permute-start.24
  64.7 2.5 %collective-permute-done.19 = f32[112,128]{1,0:T(8,128)S(1)} collective-permute-done((f32[112,128]{1,0:T(8,128)S(1)}, f32[112,128]{1,0:T(8,128)S(1)}, u32[]{:S(2)}, u32[]{:S(2)}) %collective-permute-start.19) | collective-permute-done | bytes 57376 | tf_op jit(solution)/shard_map/ppermute | solution.py:438
  67.2 0.4 collective-permute-start.22
  67.7 1.9 %collective-permute-start.21 = (f32[112,128]{1,0:T(8,128)S(1)}, f32[112,128]{1,0:T(8,128)S(1)}, u32[]{:S(2)}, u32[]{:S(2)}) collective-permute-start(f32[112,128]{1,0:T(8,128)S(1)} %add.34), channel_id=1, source_target_pairs={{0,2},{1,3},{2,0},{3,1},{4,6},{5,7},{6,4},{7,5},{8,10},{9,11},{10,... | collective-permute-start | bytes 172040 | tf_op jit(solution)/shard_map/ppermute | solution.py:438
  69.5 1.4 %collective-permute-start.20 = (f32[112,128]{1,0:T(8,128)S(1)}, f32[112,128]{1,0:T(8,128)S(1)}, u32[]{:S(2)}, u32[]{:S(2)}) collective-permute-start(f32[112,128]{1,0:T(8,128)S(1)} %add.34), channel_id=1, source_target_pairs={{0,4},{4,0},{8,12},{12,8},{1,5},{5,1},{9,13},{13,9},{2,6},{6,2},{1... | collective-permute-start | bytes 172040 | tf_op jit(solution)/shard_map/ppermute | solution.py:438
  70.9 1.5 %collective-permute-start.27 = (f32[112,128]{1,0:T(8,128)S(1)}, f32[112,128]{1,0:T(8,128)S(1)}, u32[]{:S(2)}, u32[]{:S(2)}) collective-permute-start(f32[112,128]{1,0:T(8,128)S(1)} %add.36), channel_id=1, source_target_pairs={{0,6},{1,7},{2,4},{3,5},{4,2},{5,3},{6,0},{7,1},{8,14},{9,15},{10,... | collective-permute-start | bytes 172040 | tf_op jit(solution)/shard_map/ppermute | solution.py:451
  72.4 0.6 collective-permute-start.26
  73.1 1.4 %collective-permute-start.25 = (f32[112,128]{1,0:T(8,128)S(1)}, f32[112,128]{1,0:T(8,128)S(1)}, u32[]{:S(2)}, u32[]{:S(2)}) collective-permute-start(f32[112,128]{1,0:T(8,128)S(1)} %add.36), channel_id=1, source_target_pairs={{0,4},{4,0},{8,12},{12,8},{1,5},{5,1},{9,13},{13,9},{2,6},{6,2},{1... | collective-permute-start | bytes 172040 | tf_op jit(solution)/shard_map/ppermute | solution.py:438
  74.5 0.1 collective-permute-start.28
  74.6 1.5 %collective-permute-done.27 = f32[112,128]{1,0:T(8,128)S(1)} collective-permute-done((f32[112,128]{1,0:T(8,128)S(1)}, f32[112,128]{1,0:T(8,128)S(1)}, u32[]{:S(2)}, u32[]{:S(2)}) %collective-permute-start.27) | collective-permute-done | bytes 57376 | tf_op jit(solution)/shard_map/ppermute | solution.py:451
  76.1 0.6 collective-permute-done.26
  76.7 0.6 collective-permute-done.25
  77.3 0.1 collective-permute-start.29
  77.4 1.0 %restore.1 = (f32[512,128]{1,0:T(8,128)}, f32[512,128]{1,0:T(8,128)}) custom-call(f32[2,2,32,128]{3,2,1,0:T(8,128)S(1)} %get-tuple-element.93.refs_0_, f32[2,2,32,128]{3,2,1,0:T(8,128)S(1)} %get-tuple-element.119.refs_1_, f32[2,2,32,128]{3,2,1,0:T(8,128)S(1)} %get-tuple-element.118.refs_2_, f32[2,2,32,128]{3,2,1,0:T(8,128)S(1)} %get-tuple-element.120.refs_3_, ...), custom_call_target="tpu_custom_call" | custom-call | bytes 1024 | tf_op jit(solution)/shard_map/restore/pallas_call | solution.py:24
  78.4 0.5 collective-permute-done.29.refs_3_
  78.8 1.6 %unpack.1 = (f32[2,27,64,64]{3,2,1,0:T(8,128)}, f32[2,64]{1,0:T(2,128)}) custom-call(f32[448,128]{1,0:T(8,128)S(1)} %pad_maximum_fusion.refs_0_, f32[448,128]{1,0:T(8,128)S(1)} %pad_maximum_fusion.1.refs_1_, f32[448,128]{1,0:T(8,128)S(1)} %collective-permute-done.28.refs_2_, f32[448,128]{1,0:T(8,128)S(1)} %collective-permute-done.29.refs_3_), custom_call_target="tpu_custom_call" | custom-call | bytes 1024 | tf_op jit(solution)/shard_map/unpack/pallas_call | solution.py:24
  (31 shorter events, 0.3 us)
Async XLA Ops:
  0.6 1.0 %copy-start.1 = (f32[2,64,2,2,128]{4,3,2,1,0:T(2,128)S(1)}, f32[2,64,2,2,128]{4,3,2,1,0:T(2,128)}, u32[]{:S(2)}) copy-start(f32[2,64,2,2,128]{4,3,2,1,0:T(2,128)} %param.4) | copy-start | bytes 786436
  1.6 0.9 %copy-start.2 = (f32[2,64,2,2,128]{4,3,2,1,0:T(2,128)S(1)}, f32[2,64,2,2,128]{4,3,2,1,0:T(2,128)}, u32[]{:S(2)}) copy-start(f32[2,64,2,2,128]{4,3,2,1,0:T(2,128)} %param.7) | copy-start | bytes 786436
  2.7 3.7 %collective-permute-start = (f32[2,2,2,8,128]{4,3,2,1,0:T(8,128)S(1)}, f32[2,2,2,8,128]{4,3,2,1,0:T(8,128)S(1)}, u32[]{:S(2)}, u32[]{:S(2)}) collective-permute-start(f32[2,2,2,8,128]{4,3,2,1,0:T(8,128)S(1)} %get-tuple-element.61), channel_id=1, source_target_pairs={{0,1},{1,0},{2,3},{3,2},{4,5},{5,4},{6,7},{7,6},{8,9},{9,8},{10,11... | collective-permute-start | bytes 98312 | tf_op jit(solution)/shard_map/ppermute | solution.py:438
  3.2 3.2 %collective-permute-start.1 = (f32[2,2,2,8,128]{4,3,2,1,0:T(8,128)S(1)}, f32[2,2,2,8,128]{4,3,2,1,0:T(8,128)S(1)}, u32[]{:S(2)}, u32[]{:S(2)}) collective-permute-start(f32[2,2,2,8,128]{4,3,2,1,0:T(8,128)S(1)} %get-tuple-element.62), channel_id=1, source_target_pairs={{1,2},{2,1},{5,6},{6,5},{9,10},{10,9},{13,14},{14,13},{17,18},{18,... | collective-permute-start | bytes 98312 | tf_op jit(solution)/shard_map/ppermute | solution.py:478
  3.9 1.5 %copy-start = (f32[2,27,64,64]{3,2,1,0:T(8,128)S(1)}, f32[2,27,64,64]{3,2,1,0:T(8,128)}, u32[]{:S(2)}) copy-start(f32[2,27,64,64]{3,2,1,0:T(8,128)} %weights.1) | copy-start | bytes 2654212
  5.4 0.7 copy-start.3
  6.5 13.4 %collective-permute-start.2 = (f32[14,64,128]{2,1,0:T(8,128)S(1)}, f32[14,64,128]{2,1,0:T(8,128)S(1)}, u32[]{:S(2)}, u32[]{:S(2)}) collective-permute-start(f32[14,64,128]{2,1,0:T(8,128)S(1)} %get-tuple-element.68), channel_id=1, source_target_pairs={{0,16},{16,0},{1,17},{17,1},{2,18},{18,2},{3,19},{19,3},{4,20},{20... | collective-permute-start | bytes 1376264 | tf_op jit(solution)/shard_map/ppermute | solution.py:442
  9.1 4.5 %collective-permute-start.3 = (f32[2,88,128]{2,1,0:T(8,128)S(1)}, f32[2,88,128]{2,1,0:T(8,128)S(1)}, u32[]{:S(2)}, u32[]{:S(2)}) collective-permute-start(f32[2,88,128]{2,1,0:T(8,128)S(1)} %get-tuple-element.70), channel_id=1, source_target_pairs={{0,4},{4,0},{8,12},{12,8},{1,5},{5,1},{9,13},{13,9},{2,6},{6,2},{1... | collective-permute-start | bytes 270344 | tf_op jit(solution)/shard_map/ppermute | solution.py:430
  10.7 6.7 %collective-permute-start.5 = (f32[2,88,128]{2,1,0:T(8,128)S(1)}, f32[2,88,128]{2,1,0:T(8,128)S(1)}, u32[]{:S(2)}, u32[]{:S(2)}) collective-permute-start(f32[2,88,128]{2,1,0:T(8,128)S(1)} %get-tuple-element.71), channel_id=1, source_target_pairs={{0,8},{4,12},{8,0},{12,4},{1,9},{5,13},{9,1},{13,5},{2,10},{6,14},... | collective-permute-start | bytes 270344 | tf_op jit(solution)/shard_map/ppermute | solution.py:430
  13.3 6.3 %collective-permute-start.6 = (f32[2,88,128]{2,1,0:T(8,128)S(1)}, f32[2,88,128]{2,1,0:T(8,128)S(1)}, u32[]{:S(2)}, u32[]{:S(2)}) collective-permute-start(f32[2,88,128]{2,1,0:T(8,128)S(1)} %get-tuple-element.72), channel_id=1, source_target_pairs={{0,12},{4,8},{8,4},{12,0},{1,13},{5,9},{9,5},{13,1},{2,14},{6,10},... | collective-permute-start | bytes 270344 | tf_op jit(solution)/shard_map/ppermute | solution.py:430
  13.6 6.3 %collective-permute-start.4 = (f32[2,88,128]{2,1,0:T(8,128)S(1)}, f32[2,88,128]{2,1,0:T(8,128)S(1)}, u32[]{:S(2)}, u32[]{:S(2)}) collective-permute-start(f32[2,88,128]{2,1,0:T(8,128)S(1)} %collective-permute-done.3.refs_1_), channel_id=1, source_target_pairs={{0,16},{16,0},{1,17},{17,1},{2,18},{18,2},{3,19},{19,3},{4,20},{20... | collective-permute-start | bytes 270344 | tf_op jit(solution)/shard_map/ppermute | solution.py:442
  19.9 4.4 %collective-permute-start.7 = (f32[14,64,128]{2,1,0:T(8,128)S(1)}, f32[14,64,128]{2,1,0:T(8,128)S(1)}, u32[]{:S(2)}, u32[]{:S(2)}) collective-permute-start(f32[14,64,128]{2,1,0:T(8,128)S(1)} %collective-permute-done.2.refs_0_), channel_id=1, source_target_pairs={{0,1},{1,0},{2,3},{3,2},{4,5},{5,4},{6,7},{7,6},{8,9},{9,8},{10,11... | collective-permute-start | bytes 1376264 | tf_op jit(solution)/shard_map/ppermute | solution.py:438
  22.2 5.3 %collective-permute-start.8 = (f32[2,88,128]{2,1,0:T(8,128)S(1)}, f32[2,88,128]{2,1,0:T(8,128)S(1)}, u32[]{:S(2)}, u32[]{:S(2)}) collective-permute-start(f32[2,88,128]{2,1,0:T(8,128)S(1)} %collective-permute-done.5.refs_2_), channel_id=1, source_target_pairs={{0,16},{16,0},{1,17},{17,1},{2,18},{18,2},{3,19},{19,3},{4,20},{20... | collective-permute-start | bytes 270344 | tf_op jit(solution)/shard_map/ppermute | solution.py:442
  24.3 4.7 %collective-permute-start.9 = (f32[2,88,128]{2,1,0:T(8,128)S(1)}, f32[2,88,128]{2,1,0:T(8,128)S(1)}, u32[]{:S(2)}, u32[]{:S(2)}) collective-permute-start(f32[2,88,128]{2,1,0:T(8,128)S(1)} %collective-permute-done.6.refs_3_), channel_id=1, source_target_pairs={{0,16},{16,0},{1,17},{17,1},{2,18},{18,2},{3,19},{19,3},{4,20},{20... | collective-permute-start | bytes 270344 | tf_op jit(solution)/shard_map/ppermute | solution.py:442
  33.5 9.5 %collective-permute-start.10 = (f32[2,2,32,128]{3,2,1,0:T(8,128)S(1)}, f32[2,2,32,128]{3,2,1,0:T(8,128)S(1)}, u32[]{:S(2)}, u32[]{:S(2)}) collective-permute-start(f32[2,2,32,128]{3,2,1,0:T(8,128)S(1)} %get-tuple-element.84), channel_id=1, source_target_pairs={{0,8},{4,12},{8,0},{12,4},{1,9},{5,13},{9,1},{13,5},{2,10},{6,14},... | collective-permute-start | bytes 196616 | tf_op jit(solution)/shard_map/ppermute | solution.py:438
  43.0 1.6 %collective-permute-start.11 = (f32[448,128]{1,0:T(8,128)S(1)}, f32[448,128]{1,0:T(8,128)S(1)}, u32[]{:S(2)}, u32[]{:S(2)}) collective-permute-start(f32[448,128]{1,0:T(8,128)S(1)} %bitcast.42), channel_id=1, source_target_pairs={{0,1},{1,0},{2,3},{3,2},{4,5},{5,4},{6,7},{7,6},{8,9},{9,8},{10,11... | collective-permute-start | bytes 688136 | tf_op jit(solution)/shard_map/ppermute | solution.py:438
  43.1 1.8 %collective-permute-start.12 = (f32[448,128]{1,0:T(8,128)S(1)}, f32[448,128]{1,0:T(8,128)S(1)}, u32[]{:S(2)}, u32[]{:S(2)}) collective-permute-start(f32[448,128]{1,0:T(8,128)S(1)} %bitcast.41), channel_id=1, source_target_pairs={{0,1},{1,0},{2,3},{3,2},{4,5},{5,4},{6,7},{7,6},{8,9},{9,8},{10,11... | collective-permute-start | bytes 688136 | tf_op jit(solution)/shard_map/ppermute | solution.py:438
  45.0 9.5 %collective-permute-start.13 = (f32[224,128]{1,0:T(8,128)S(1)}, f32[224,128]{1,0:T(8,128)S(1)}, u32[]{:S(2)}, u32[]{:S(2)}) collective-permute-start(f32[224,128]{1,0:T(8,128)S(1)} %slice.99), channel_id=1, source_target_pairs={{0,2},{1,3},{2,0},{3,1},{4,6},{5,7},{6,4},{7,5},{8,10},{9,11},{10,... | collective-permute-start | bytes 344072 | tf_op jit(solution)/shard_map/ppermute | solution.py:438
  46.8 12.7 %collective-permute-start.14 = (f32[3,2,2,32,128]{4,3,2,1,0:T(8,128)S(1)}, f32[3,2,2,32,128]{4,3,2,1,0:T(8,128)S(1)}, u32[]{:S(2)}, u32[]{:S(2)}) collective-permute-start(f32[3,2,2,32,128]{4,3,2,1,0:T(8,128)S(1)} %pad_maximum_fusion.2), channel_id=1, source_target_pairs={{0,4},{4,0},{8,12},{12,8},{1,5},{5,1},{9,13},{13,9},{2,6},{6,2},{1... | collective-permute-start | bytes 589832 | tf_op jit(solution)/shard_map/ppermute | solution.py:438
  48.5 4.9 %collective-permute-start.17 = (f32[224,128]{1,0:T(8,128)S(1)}, f32[224,128]{1,0:T(8,128)S(1)}, u32[]{:S(2)}, u32[]{:S(2)}) collective-permute-start(f32[224,128]{1,0:T(8,128)S(1)} %slice.89), channel_id=1, source_target_pairs={{0,2},{1,3},{2,0},{3,1},{4,6},{5,7},{6,4},{7,5},{8,10},{9,11},{10,... | collective-permute-start | bytes 344072 | tf_op jit(solution)/shard_map/ppermute | solution.py:438
  48.8 10.7 %collective-permute-start.15 = (f32[2,2,2,32,128]{4,3,2,1,0:T(8,128)S(1)}, f32[2,2,2,32,128]{4,3,2,1,0:T(8,128)S(1)}, u32[]{:S(2)}, u32[]{:S(2)}) collective-permute-start(f32[2,2,2,32,128]{4,3,2,1,0:T(8,128)S(1)} %pad_maximum_fusion.3), channel_id=1, source_target_pairs={{0,8},{4,12},{8,0},{12,4},{1,9},{5,13},{9,1},{13,5},{2,10},{6,14},... | collective-permute-start | bytes 393224 | tf_op jit(solution)/shard_map/ppermute | solution.py:438
  49.2 9.1 %collective-permute-start.16 = (f32[2,2,32,128]{3,2,1,0:T(8,128)S(1)}, f32[2,2,32,128]{3,2,1,0:T(8,128)S(1)}, u32[]{:S(2)}, u32[]{:S(2)}) collective-permute-start(f32[2,2,32,128]{3,2,1,0:T(8,128)S(1)} %get-tuple-element.99), channel_id=1, source_target_pairs={{0,12},{4,8},{8,4},{12,0},{1,13},{5,9},{9,5},{13,1},{2,14},{6,10},... | collective-permute-start | bytes 196616 | tf_op jit(solution)/shard_map/ppermute | solution.py:438
  53.4 7.5 %collective-permute-start.18 = (f32[112,128]{1,0:T(8,128)S(1)}, f32[112,128]{1,0:T(8,128)S(1)}, u32[]{:S(2)}, u32[]{:S(2)}) collective-permute-start(f32[112,128]{1,0:T(8,128)S(1)} %slice_select_fusion), channel_id=1, source_target_pairs={{0,4},{4,0},{8,12},{12,8},{1,5},{5,1},{9,13},{13,9},{2,6},{6,2},{1... | collective-permute-start | bytes 172040 | tf_op jit(solution)/shard_map/ppermute | solution.py:438
  59.5 4.8 %collective-permute-start.23 = (f32[112,128]{1,0:T(8,128)S(1)}, f32[112,128]{1,0:T(8,128)S(1)}, u32[]{:S(2)}, u32[]{:S(2)}) collective-permute-start(f32[112,128]{1,0:T(8,128)S(1)} %slice_select_fusion.1), channel_id=1, source_target_pairs={{0,4},{4,0},{8,12},{12,8},{1,5},{5,1},{9,13},{13,9},{2,6},{6,2},{1... | collective-permute-start | bytes 172040 | tf_op jit(solution)/shard_map/ppermute | solution.py:438
  60.8 6.4 %collective-permute-start.19 = (f32[112,128]{1,0:T(8,128)S(1)}, f32[112,128]{1,0:T(8,128)S(1)}, u32[]{:S(2)}, u32[]{:S(2)}) collective-permute-start(f32[112,128]{1,0:T(8,128)S(1)} %select_add_fusion.1), channel_id=1, source_target_pairs={{0,8},{4,12},{8,0},{12,4},{1,9},{5,13},{9,1},{13,5},{2,10},{6,14},... | collective-permute-start | bytes 172040 | tf_op jit(solution)/shard_map/ppermute | solution.py:438
  64.3 6.6 %collective-permute-start.24 = (f32[112,128]{1,0:T(8,128)S(1)}, f32[112,128]{1,0:T(8,128)S(1)}, u32[]{:S(2)}, u32[]{:S(2)}) collective-permute-start(f32[112,128]{1,0:T(8,128)S(1)} %select_add_fusion), channel_id=1, source_target_pairs={{0,8},{4,12},{8,0},{12,4},{1,9},{5,13},{9,1},{13,5},{2,10},{6,14},... | collective-permute-start | bytes 172040 | tf_op jit(solution)/shard_map/ppermute | solution.py:438
  67.2 5.9 %collective-permute-start.22 = (f32[112,128]{1,0:T(8,128)S(1)}, f32[112,128]{1,0:T(8,128)S(1)}, u32[]{:S(2)}, u32[]{:S(2)}) collective-permute-start(f32[112,128]{1,0:T(8,128)S(1)} %add.34), channel_id=1, source_target_pairs={{0,6},{1,7},{2,4},{3,5},{4,2},{5,3},{6,0},{7,1},{8,14},{9,15},{10,... | collective-permute-start | bytes 172040 | tf_op jit(solution)/shard_map/ppermute | solution.py:451
  67.7 6.8 %collective-permute-start.21 = (f32[112,128]{1,0:T(8,128)S(1)}, f32[112,128]{1,0:T(8,128)S(1)}, u32[]{:S(2)}, u32[]{:S(2)}) collective-permute-start(f32[112,128]{1,0:T(8,128)S(1)} %add.34), channel_id=1, source_target_pairs={{0,2},{1,3},{2,0},{3,1},{4,6},{5,7},{6,4},{7,5},{8,10},{9,11},{10,... | collective-permute-start | bytes 172040 | tf_op jit(solution)/shard_map/ppermute | solution.py:438
  69.5 5.0 %collective-permute-start.20 = (f32[112,128]{1,0:T(8,128)S(1)}, f32[112,128]{1,0:T(8,128)S(1)}, u32[]{:S(2)}, u32[]{:S(2)}) collective-permute-start(f32[112,128]{1,0:T(8,128)S(1)} %add.34), channel_id=1, source_target_pairs={{0,4},{4,0},{8,12},{12,8},{1,5},{5,1},{9,13},{13,9},{2,6},{6,2},{1... | collective-permute-start | bytes 172040 | tf_op jit(solution)/shard_map/ppermute | solution.py:438
  70.9 5.1 %collective-permute-start.27 = (f32[112,128]{1,0:T(8,128)S(1)}, f32[112,128]{1,0:T(8,128)S(1)}, u32[]{:S(2)}, u32[]{:S(2)}) collective-permute-start(f32[112,128]{1,0:T(8,128)S(1)} %add.36), channel_id=1, source_target_pairs={{0,6},{1,7},{2,4},{3,5},{4,2},{5,3},{6,0},{7,1},{8,14},{9,15},{10,... | collective-permute-start | bytes 172040 | tf_op jit(solution)/shard_map/ppermute | solution.py:451
  72.4 4.2 %collective-permute-start.26 = (f32[112,128]{1,0:T(8,128)S(1)}, f32[112,128]{1,0:T(8,128)S(1)}, u32[]{:S(2)}, u32[]{:S(2)}) collective-permute-start(f32[112,128]{1,0:T(8,128)S(1)} %add.36), channel_id=1, source_target_pairs={{0,2},{1,3},{2,0},{3,1},{4,6},{5,7},{6,4},{7,5},{8,10},{9,11},{10,... | collective-permute-start | bytes 172040 | tf_op jit(solution)/shard_map/ppermute | solution.py:438
  73.1 4.2 %collective-permute-start.25 = (f32[112,128]{1,0:T(8,128)S(1)}, f32[112,128]{1,0:T(8,128)S(1)}, u32[]{:S(2)}, u32[]{:S(2)}) collective-permute-start(f32[112,128]{1,0:T(8,128)S(1)} %add.36), channel_id=1, source_target_pairs={{0,4},{4,0},{8,12},{12,8},{1,5},{5,1},{9,13},{13,9},{2,6},{6,2},{1... | collective-permute-start | bytes 172040 | tf_op jit(solution)/shard_map/ppermute | solution.py:438
  74.5 3.9 %collective-permute-start.28 = (f32[448,128]{1,0:T(8,128)S(1)}, f32[448,128]{1,0:T(8,128)S(1)}, u32[]{:S(2)}, u32[]{:S(2)}) collective-permute-start(f32[448,128]{1,0:T(8,128)S(1)} %pad_maximum_fusion.refs_0_), channel_id=1, source_target_pairs={{0,1},{1,0},{2,3},{3,2},{4,5},{5,4},{6,7},{7,6},{8,9},{9,8},{10,11... | collective-permute-start | bytes 688136 | tf_op jit(solution)/shard_map/ppermute | solution.py:438
  77.3 1.6 %collective-permute-start.29 = (f32[448,128]{1,0:T(8,128)S(1)}, f32[448,128]{1,0:T(8,128)S(1)}, u32[]{:S(2)}, u32[]{:S(2)}) collective-permute-start(f32[448,128]{1,0:T(8,128)S(1)} %pad_maximum_fusion.1.refs_1_), channel_id=1, source_target_pairs={{0,1},{1,0},{2,3},{3,2},{4,5},{5,4},{6,7},{7,6},{8,9},{9,8},{10,11... | collective-permute-start | bytes 688136 | tf_op jit(solution)/shard_map/ppermute | solution.py:438

commit v15 on v13

--- a/solution.py
+++ b/solution.py
@@ -207,17 +207,19 @@
                 for edge in (0, self.rows_y + 1):
                     target[lead, micro, edge * self.depth : (edge + 1) * self.depth, :] = blank
 
-    def fill(self, field, windows, which):
+    def fill(self, field, windows, home, theirs, which):
         halo = HALOS[which]
         span = self.width + 2 * halo
         at = 0 if which == 0 else self.width + 2 * HALO
         extra = [HALO - halo, self.depth - span - (HALO - halo)]
-        for index, window in enumerate(windows):
-            owner = self.slab ^ index % self.slabs
-            micro = self.section if index < self.slabs else 1 - self.section
+        pieces = [(self.section, turn, window, at) for turn, window in enumerate(windows)]
+        pieces.append((1 - self.section, 0, home, at))
+        pieces += [(1 - self.section, turn + 1, window, 0) for turn, window in enumerate(theirs)]
+        for micro, turn, window, first in pieces:
+            owner = self.slab ^ turn
             for y in range(self.per_owner):
                 blanks = [jnp.zeros((rows, LANES), F32) for rows in extra]
-                parts = [blanks[0], window[y, at : at + span], blanks[1]]
+                parts = [blanks[0], window[y, first : first + span], blanks[1]]
                 parts = [part for part in parts if part.shape[0]]
                 start = pl.multiple_of((owner * self.per_owner + y) * self.depth, 16)
                 value = jnp.concatenate(parts, axis=0) if len(parts) > 1 else parts[0]
@@ -235,13 +237,11 @@
 
 def forward_kernel(dims, own, own_row, other, other_row, *refs):
     slab = Slab(dims)
-    windows, (acts, kept, *outs), (whole, field) = (
-        refs[: 2 * slab.slabs],
-        refs[2 * slab.slabs : -2],
-        refs[-2:],
-    )
+    count = slab.slabs
+    windows, home, theirs = refs[:count], refs[count], refs[count + 1 : 2 * count]
+    (acts, kept, *outs), (whole, field) = refs[2 * count : -2], refs[-2:]
     slab.blank_edges(acts)
-    slab.fill(field, windows, 0)
+    slab.fill(field, windows, home, theirs, 0)
 
     def take_in(start):
         for micro in range(slab.micros):
@@ -281,10 +281,11 @@
 
 def backward_kernel(dims, scale, own, other, acts, kept, *refs):
     slab = Slab(dims)
-    windows, refs = refs[: 2 * slab.slabs], refs[2 * slab.slabs :]
+    (*windows, home, other_cells), refs = refs[: slab.slabs + 2], refs[slab.slabs + 2 :]
+    theirs = [other_cells.at[turn] for turn in range(slab.slabs - 1)]
     outs, (sums, rim, slopes, field, acc) = refs[: slab.slabs], refs[slab.slabs :]
     slab.blank_edges(rim)
-    slab.fill(field, windows, 1)
+    slab.fill(field, windows, home, theirs, 1)
 
     def take_gradient(layer, micro, start, gradient):
         at = pl.ds(start, slab.chunk)
@@ -490,12 +491,13 @@
 
     tables = [((2, 15 * LANES, 2 * LANES), BF16)] * 2 + [((2, 8, LANES), F32)]
     own_fwd, own_bwd, own_row = call(table_kernel, "own_table", tables, [own])
+    ahead = [window[:, : width + 2 * HALOS[0]] for window in mine[1:]]
     if slabs <= 8:
-        theirs = [home] + [crossed(window) for window in mine[1:]]
+        ahead = [crossed(window) for window in ahead]
     else:
-        theirs = list(crossed(jnp.stack(mine)))
-    windows = mine + theirs
-    gate = [theirs[1], *mine[2:]]
+        ahead = list(crossed(jnp.stack(ahead)))
+    after = crossed(jnp.stack([window[:, width + 2 * HALOS[0] :] for window in mine[1:]]))
+    gate = [ahead[0], *mine[2:]]
     near_half, own_row, *_ = lax.optimization_barrier((near_half, own_row, *gate))
     far_half = swapped(near_half, 1)
     far_fwd, far_bwd, far_row = call(table_kernel, "far_table", tables, [near_half, far_half])
@@ -508,7 +510,7 @@
         functools.partial(forward_kernel, dims),
         "forward",
         [((5, micros, padded, 2 * LANES), BF16), ((4, micros, full, LANES), F32)] + [piece] * slabs,
-        [own_fwd, own_row, far_fwd, far_row, *windows],
+        [own_fwd, own_row, far_fwd, far_row, *mine, home, *ahead],
         [pltpu.VMEM((micros, full, LANES), F32)] * 2,
     )
     if slabs == 4:
@@ -517,7 +519,7 @@
         functools.partial(backward_kernel, dims, scale),
         "backward",
         [piece] * slabs + [((BLOCKS, chans, LANES), F32)],
-        [own_bwd, far_bwd, acts, kept, *windows],
+        [own_bwd, far_bwd, acts, kept, *mine, home, after],
         [
             pltpu.VMEM((2, micros, padded, 2 * LANES), BF16),
             pltpu.VMEM((4, micros, full, LANES), F32),

time: 78.6 us -> 75 us (0.954)
  waiting for transfers between devices: 22.2 us -> 18.6 us
    ppermute x4 -> x5, waiting for transfers between devices: 4.22 us -> 0.01 us  [crossed(): return lax.ppermute(block, 'section', [(0, 1), (1, 0)])]
    ppermute x20, waiting for transfers between devices: 11.3 us -> 12.6 us  [swapped(): lax.ppermute(block, axis, [(i, i ^ bit) for i in range(lax.axis_size(axis...]
    ppermute x4 -> x5, starting transfers between devices: 4.81 us -> 5.53 us  [crossed(): return lax.ppermute(block, 'section', [(0, 1), (1, 0)])]
  transfers between devices with their start and end apart: 30 -> 31, of which waited for: 17 -> 14; matrix products, arithmetic and copies ran while one was open for 0% -> 0% of each run, Pallas kernels for 12% -> 18%
where the time goes in v15:
time: 75 us; the launch traced here: 74.8 us
  starting transfers between devices  35.2 us (47%)
  waiting for transfers between devices  18.6 us (25%)
  Pallas kernels  15.7 us (21%)
  local copies, waits for them, and re-layouts  4.17 us (6%)
  between operations  0.91 us (1%)
    ppermute x20, starting transfers between devices, swapped(): lax.ppermute(block, axis, [(i, i ^ bit) for i in range(lax.axis_size(axis...  21.3 us
    pallas_call x9, Pallas kernels, call(): pl.pallas_call(kernel, out_shape=arrays, in_specs=[VMEM] * len(args), out...  15.7 us
    ppermute x20, waiting for transfers between devices, swapped(): lax.ppermute(block, axis, [(i, i ^ bit) for i in range(lax.axis_size(axis...  12.6 us
    ppermute x5, starting transfers between devices, crossed(): return lax.ppermute(block, 'section', [(0, 1), (1, 0)])  5.53 us
    ppermute x3, waiting for transfers between devices, spread(): got.append(lax.ppermute(blocks[turn], 'gy', route))  4.47 us
    ppermute x3, starting transfers between devices, spread(): got.append(lax.ppermute(blocks[turn], 'gy', route))  4.39 us
    unnamed x8, local copies, waits for them, and re-layouts  4.04 us
    ppermute x2, starting transfers between devices, around(): across = lax.ppermute(across, ('gy', 'gz'), route)  3.32 us
  transfers between devices with their start and end apart: 31, of which 14 were waited for; matrix products, arithmetic and copies ran while one was open for 0% of the time, Pallas kernels for 18%

profile of v15, /device:TPU:0, one launch (start us, length us, event | category | flops | bytes accessed | tf_op | source)
XLA Modules:
  0.0 74.8 jit_solution(239630909774783997)
XLA Ops:
  0.6 0.9 %copy-done.1 = f32[2,64,2,2,128]{4,3,2,1,0:T(2,128)S(1)} copy-done((f32[2,64,2,2,128]{4,3,2,1,0:T(2,128)S(1)}, f32[2,64,2,2,128]{4,3,2,1,0:T(2,128)}, u32[]{:S(2)}) %copy-start.1) | copy-done | bytes 262168
  1.6 0.9 %copy-done.2 = f32[2,64,2,2,128]{4,3,2,1,0:T(2,128)S(1)} copy-done((f32[2,64,2,2,128]{4,3,2,1,0:T(2,128)S(1)}, f32[2,64,2,2,128]{4,3,2,1,0:T(2,128)}, u32[]{:S(2)}) %copy-start.2) | copy-done | bytes 262168
  2.5 0.2 turn.1
  2.7 0.5 collective-permute-start
  3.2 0.7 collective-permute-start.1
  3.9 0.0 copy-start
  3.9 1.5 %copy-done = f32[2,27,64,64]{3,2,1,0:T(8,128)S(1)} copy-done((f32[2,27,64,64]{3,2,1,0:T(8,128)S(1)}, f32[2,27,64,64]{3,2,1,0:T(8,128)}, u32[]{:S(2)}) %copy-start) | copy-done | bytes 884760
  5.4 0.7 copy-done.3
  6.1 0.3 pack.1
  6.4 0.0 collective-permute-done.pair
  6.4 0.1 windows.1
  6.5 2.6 %collective-permute-start.2 = (f32[14,64,128]{2,1,0:T(8,128)S(1)}, f32[14,64,128]{2,1,0:T(8,128)S(1)}, u32[]{:S(2)}, u32[]{:S(2)}) collective-permute-start(f32[14,64,128]{2,1,0:T(8,128)S(1)} %get-tuple-element.67), channel_id=1, source_target_pairs={{0,16},{16,0},{1,17},{17,1},{2,18},{18,2},{3,19},{19,3},{4,20},{20... | collective-permute-start | bytes 1376264 | tf_op jit(solution)/shard_map/ppermute | solution.py:443
  9.1 1.6 %collective-permute-start.3 = (f32[2,88,128]{2,1,0:T(8,128)S(1)}, f32[2,88,128]{2,1,0:T(8,128)S(1)}, u32[]{:S(2)}, u32[]{:S(2)}) collective-permute-start(f32[2,88,128]{2,1,0:T(8,128)S(1)} %get-tuple-element.69), channel_id=1, source_target_pairs={{0,4},{4,0},{8,12},{12,8},{1,5},{5,1},{9,13},{13,9},{2,6},{6,2},{1... | collective-permute-start | bytes 270344 | tf_op jit(solution)/shard_map/ppermute | solution.py:431
  10.7 2.6 %collective-permute-start.5 = (f32[2,88,128]{2,1,0:T(8,128)S(1)}, f32[2,88,128]{2,1,0:T(8,128)S(1)}, u32[]{:S(2)}, u32[]{:S(2)}) collective-permute-start(f32[2,88,128]{2,1,0:T(8,128)S(1)} %get-tuple-element.70), channel_id=1, source_target_pairs={{0,8},{4,12},{8,0},{12,4},{1,9},{5,13},{9,1},{13,5},{2,10},{6,14},... | collective-permute-start | bytes 270344 | tf_op jit(solution)/shard_map/ppermute | solution.py:431
  13.3 0.2 collective-permute-start.6
  13.5 0.7 own_table.1
  14.2 0.4 collective-permute-start.4
  14.6 2.8 %collective-permute-done.5.refs_2_ = f32[2,88,128]{2,1,0:T(8,128)S(1)} collective-permute-done((f32[2,88,128]{2,1,0:T(8,128)S(1)}, f32[2,88,128]{2,1,0:T(8,128)S(1)}, u32[]{:S(2)}, u32[]{:S(2)}) %collective-permute-start.5) | collective-permute-done | bytes 90144 | tf_op jit(solution)/shard_map/ppermute | solution.py:431
  17.4 0.5 collective-permute-start.8
  17.9 1.7 %collective-permute-done.6.refs_3_ = f32[2,88,128]{2,1,0:T(8,128)S(1)} collective-permute-done((f32[2,88,128]{2,1,0:T(8,128)S(1)}, f32[2,88,128]{2,1,0:T(8,128)S(1)}, u32[]{:S(2)}, u32[]{:S(2)}) %collective-permute-start.6) | collective-permute-done | bytes 90144 | tf_op jit(solution)/shard_map/ppermute | solution.py:431
  19.6 0.5 collective-permute-start.9
  20.2 0.0 collective-permute-done.4.refs_5_
  20.2 0.0 collective-permute-done.2.refs_0_
  20.2 2.9 %collective-permute-start.7 = (f32[14,64,128]{2,1,0:T(8,128)S(1)}, f32[14,64,128]{2,1,0:T(8,128)S(1)}, u32[]{:S(2)}, u32[]{:S(2)}) collective-permute-start(f32[14,64,128]{2,1,0:T(8,128)S(1)} %collective-permute-done.2.refs_0_), channel_id=1, source_target_pairs={{0,1},{1,0},{2,3},{3,2},{4,5},{5,4},{6,7},{7,6},{8,9},{9,8},{10,11... | collective-permute-start | bytes 1376264 | tf_op jit(solution)/shard_map/ppermute | solution.py:439
  23.1 1.5 %collective-permute-start.10 = (f32[3,2,40,128]{3,2,1,0:T(8,128)S(1)}, f32[3,2,40,128]{3,2,1,0:T(8,128)S(1)}, u32[]{:S(2)}, u32[]{:S(2)}) collective-permute-start(f32[3,2,40,128]{3,2,1,0:T(8,128)S(1)} %pad_maximum_fusion.4), channel_id=1, source_target_pairs={{0,16},{16,0},{1,17},{17,1},{2,18},{18,2},{3,19},{19,3},{4,20},{20... | collective-permute-start | bytes 368648 | tf_op jit(solution)/shard_map/ppermute | solution.py:443
  24.6 0.0 collective-permute-done.7.refs_1_
  24.6 0.8 %far_table.1 = (bf16[2,1920,256]{2,1,0:T(8,128)(2,1)S(1)}, bf16[2,1920,256]{2,1,0:T(8,128)(2,1)S(1)}, f32[2,8,128]{2,1,0:T(8,128)S(1)}) custom-call(f32[14,64,128]{2,1,0:T(8,128)S(1)} %collective-permute-done.2.refs_0_, f32[14,64,128]{2,1,0:T(8,128)S(1)} %collective-permute-done.7.refs_1_), custom_call_target="tpu_custom_call" | custom-call | bytes 1024 | tf_op jit(solution)/shard_map/far_table/pallas_call | solution.py:24
  25.4 4.5 %forward.1 = (bf16[5,2,480,256]{3,2,1,0:T(8,128)(2,1)S(1)}, f32[4,2,384,128]{3,2,1,0:T(8,128)S(1)}, f32[2,2,32,128]{3,2,1,0:T(8,128)S(1)}, f32[2,2,32,128]{3,2,1...) custom-call(bf16[2,1920,256]{2,1,0:T(8,128)(2,1)S(1)} %get-tuple-element.74.own, ...), custom_call_target="tpu_custom_call" | custom-call | bytes 1024 | tf_op jit(solution)/shard_map/forward/pallas_call | solution.py:24
  29.9 2.6 %collective-permute-start.11 = (f32[2,2,2,32,128]{4,3,2,1,0:T(8,128)S(1)}, f32[2,2,2,32,128]{4,3,2,1,0:T(8,128)S(1)}, u32[]{:S(2)}, u32[]{:S(2)}) collective-permute-start(f32[2,2,2,32,128]{4,3,2,1,0:T(8,128)S(1)} %pad_maximum_fusion.3), channel_id=1, source_target_pairs={{0,8},{4,12},{8,0},{12,4},{1,9},{5,13},{9,1},{13,5},{2,10},{6,14},... | collective-permute-start | bytes 393224 | tf_op jit(solution)/shard_map/ppermute | solution.py:439
  32.5 6.5 %backward.1 = (f32[2,2,32,128]{3,2,1,0:T(8,128)S(1)}, f32[2,2,32,128]{3,2,1,0:T(8,128)S(1)}, f32[2,2,32,128]{3,2,1,0:T(8,128)S(1)}, f32[2,2,32,128]{3,2,1,0:T(8,128)S(1)}, f32[28,64,128]{2,1,0:T(8,128)S(1)}) custom-call(bf16[2,1920,256]{2,1,0:T(8,128)(2,1)S(1)} %get-tuple-element.57.own, bf16[2,1920,256]{2,1,0:T(8,128)(2,1)S(1)} %get-tuple-element.73.other, ...), custom_call_target="tpu_custom_call" | custom-call | flops 4076863488 | bytes 1024 | tf_op jit(solution)/shard_map/backward/pallas_call | solution.py:24
  39.0 0.4 collective-permute-done.11
  39.4 0.1 fusion
  39.4 0.1 collective-permute-start.12
  39.5 0.5 collective-permute-start.13
  40.0 1.0 %collective-permute-done.12 = f32[448,128]{1,0:T(8,128)S(1)} collective-permute-done((f32[448,128]{1,0:T(8,128)S(1)}, f32[448,128]{1,0:T(8,128)S(1)}, u32[]{:S(2)}, u32[]{:S(2)}) %collective-permute-start.12) | collective-permute-done | bytes 229408 | tf_op jit(solution)/shard_map/ppermute | solution.py:439
  41.0 0.3 collective-permute-done.13
  41.4 1.3 %collective-permute-start.14 = (f32[224,128]{1,0:T(8,128)S(1)}, f32[224,128]{1,0:T(8,128)S(1)}, u32[]{:S(2)}, u32[]{:S(2)}) collective-permute-start(f32[224,128]{1,0:T(8,128)S(1)} %slice.129), channel_id=1, source_target_pairs={{0,2},{1,3},{2,0},{3,1},{4,6},{5,7},{6,4},{7,5},{8,10},{9,11},{10,... | collective-permute-start | bytes 344072 | tf_op jit(solution)/shard_map/ppermute | solution.py:439
  42.7 0.9 %collective-permute-start.18 = (f32[224,128]{1,0:T(8,128)S(1)}, f32[224,128]{1,0:T(8,128)S(1)}, u32[]{:S(2)}, u32[]{:S(2)}) collective-permute-start(f32[224,128]{1,0:T(8,128)S(1)} %slice.113), channel_id=1, source_target_pairs={{0,2},{1,3},{2,0},{3,1},{4,6},{5,7},{6,4},{7,5},{8,10},{9,11},{10,... | collective-permute-start | bytes 344072 | tf_op jit(solution)/shard_map/ppermute | solution.py:439
  43.5 1.3 %collective-permute-start.15 = (f32[3,2,2,32,128]{4,3,2,1,0:T(8,128)S(1)}, f32[3,2,2,32,128]{4,3,2,1,0:T(8,128)S(1)}, u32[]{:S(2)}, u32[]{:S(2)}) collective-permute-start(f32[3,2,2,32,128]{4,3,2,1,0:T(8,128)S(1)} %pad_maximum_fusion.2), channel_id=1, source_target_pairs={{0,4},{4,0},{8,12},{12,8},{1,5},{5,1},{9,13},{13,9},{2,6},{6,2},{1... | collective-permute-start | bytes 589832 | tf_op jit(solution)/shard_map/ppermute | solution.py:439
  44.9 2.5 %collective-permute-start.16 = (f32[2,2,32,128]{3,2,1,0:T(8,128)S(1)}, f32[2,2,32,128]{3,2,1,0:T(8,128)S(1)}, u32[]{:S(2)}, u32[]{:S(2)}) collective-permute-start(f32[2,2,32,128]{3,2,1,0:T(8,128)S(1)} %get-tuple-element.96), channel_id=1, source_target_pairs={{0,8},{4,12},{8,0},{12,4},{1,9},{5,13},{9,1},{13,5},{2,10},{6,14},... | collective-permute-start | bytes 196616 | tf_op jit(solution)/shard_map/ppermute | solution.py:439
  47.4 0.6 collective-permute-start.17
  48.0 1.1 %collective-permute-done.18 = f32[224,128]{1,0:T(8,128)S(1)} collective-permute-done((f32[224,128]{1,0:T(8,128)S(1)}, f32[224,128]{1,0:T(8,128)S(1)}, u32[]{:S(2)}, u32[]{:S(2)}) %collective-permute-start.18) | collective-permute-done | bytes 114720 | tf_op jit(solution)/shard_map/ppermute | solution.py:439
  49.1 1.3 %collective-permute-start.19 = (f32[112,128]{1,0:T(8,128)S(1)}, f32[112,128]{1,0:T(8,128)S(1)}, u32[]{:S(2)}, u32[]{:S(2)}) collective-permute-start(f32[112,128]{1,0:T(8,128)S(1)} %slice_select_fusion), channel_id=1, source_target_pairs={{0,4},{4,0},{8,12},{12,8},{1,5},{5,1},{9,13},{13,9},{2,6},{6,2},{1... | collective-permute-start | bytes 172040 | tf_op jit(solution)/shard_map/ppermute | solution.py:439
  50.5 1.1 %collective-permute-done.16.refs_6_ = f32[2,2,32,128]{3,2,1,0:T(8,128)S(1)} collective-permute-done((f32[2,2,32,128]{3,2,1,0:T(8,128)S(1)}, f32[2,2,32,128]{3,2,1,0:T(8,128)S(1)}, u32[]{:S(2)}, u32[]{:S(2)}) %collective-permute-start.16) | collective-permute-done | bytes 65568 | tf_op jit(solution)/shard_map/ppermute | solution.py:439
  51.6 3.4 %collective-permute-done.17.refs_7_ = f32[2,2,32,128]{3,2,1,0:T(8,128)S(1)} collective-permute-done((f32[2,2,32,128]{3,2,1,0:T(8,128)S(1)}, f32[2,2,32,128]{3,2,1,0:T(8,128)S(1)}, u32[]{:S(2)}, u32[]{:S(2)}) %collective-permute-start.17) | collective-permute-done | bytes 65568 | tf_op jit(solution)/shard_map/ppermute | solution.py:439
  55.0 0.1 collective-permute-start.24
  55.1 2.3 %collective-permute-start.20 = (f32[112,128]{1,0:T(8,128)S(1)}, f32[112,128]{1,0:T(8,128)S(1)}, u32[]{:S(2)}, u32[]{:S(2)}) collective-permute-start(f32[112,128]{1,0:T(8,128)S(1)} %select_add_fusion.1), channel_id=1, source_target_pairs={{0,8},{4,12},{8,0},{12,4},{1,9},{5,13},{9,1},{13,5},{2,10},{6,14},... | collective-permute-start | bytes 172040 | tf_op jit(solution)/shard_map/ppermute | solution.py:439
  57.4 1.8 %collective-permute-done.24 = f32[112,128]{1,0:T(8,128)S(1)} collective-permute-done((f32[112,128]{1,0:T(8,128)S(1)}, f32[112,128]{1,0:T(8,128)S(1)}, u32[]{:S(2)}, u32[]{:S(2)}) %collective-permute-start.24) | collective-permute-done | bytes 57376 | tf_op jit(solution)/shard_map/ppermute | solution.py:439
  59.2 0.6 collective-permute-start.25
  59.8 2.1 %collective-permute-done.20 = f32[112,128]{1,0:T(8,128)S(1)} collective-permute-done((f32[112,128]{1,0:T(8,128)S(1)}, f32[112,128]{1,0:T(8,128)S(1)}, u32[]{:S(2)}, u32[]{:S(2)}) %collective-permute-start.20) | collective-permute-done | bytes 57376 | tf_op jit(solution)/shard_map/ppermute | solution.py:439
  61.9 1.7 %collective-permute-start.23 = (f32[112,128]{1,0:T(8,128)S(1)}, f32[112,128]{1,0:T(8,128)S(1)}, u32[]{:S(2)}, u32[]{:S(2)}) collective-permute-start(f32[112,128]{1,0:T(8,128)S(1)} %add.34), channel_id=1, source_target_pairs={{0,6},{1,7},{2,4},{3,5},{4,2},{5,3},{6,0},{7,1},{8,14},{9,15},{10,... | collective-permute-start | bytes 172040 | tf_op jit(solution)/shard_map/ppermute | solution.py:452
  63.6 0.2 collective-permute-start.22
  63.9 1.6 %collective-permute-start.21 = (f32[112,128]{1,0:T(8,128)S(1)}, f32[112,128]{1,0:T(8,128)S(1)}, u32[]{:S(2)}, u32[]{:S(2)}) collective-permute-start(f32[112,128]{1,0:T(8,128)S(1)} %add.34), channel_id=1, source_target_pairs={{0,4},{4,0},{8,12},{12,8},{1,5},{5,1},{9,13},{13,9},{2,6},{6,2},{1... | collective-permute-start | bytes 172040 | tf_op jit(solution)/shard_map/ppermute | solution.py:439
  65.5 1.7 %collective-permute-start.28 = (f32[112,128]{1,0:T(8,128)S(1)}, f32[112,128]{1,0:T(8,128)S(1)}, u32[]{:S(2)}, u32[]{:S(2)}) collective-permute-start(f32[112,128]{1,0:T(8,128)S(1)} %add.36), channel_id=1, source_target_pairs={{0,6},{1,7},{2,4},{3,5},{4,2},{5,3},{6,0},{7,1},{8,14},{9,15},{10,... | collective-permute-start | bytes 172040 | tf_op jit(solution)/shard_map/ppermute | solution.py:452
  67.2 0.3 collective-permute-start.27
  67.4 1.6 %collective-permute-start.26 = (f32[112,128]{1,0:T(8,128)S(1)}, f32[112,128]{1,0:T(8,128)S(1)}, u32[]{:S(2)}, u32[]{:S(2)}) collective-permute-start(f32[112,128]{1,0:T(8,128)S(1)} %add.36), channel_id=1, source_target_pairs={{0,4},{4,0},{8,12},{12,8},{1,5},{5,1},{9,13},{13,9},{2,6},{6,2},{1... | collective-permute-start | bytes 172040 | tf_op jit(solution)/shard_map/ppermute | solution.py:439
  69.1 0.1 collective-permute-start.29
  69.2 1.5 %collective-permute-done.28 = f32[112,128]{1,0:T(8,128)S(1)} collective-permute-done((f32[112,128]{1,0:T(8,128)S(1)}, f32[112,128]{1,0:T(8,128)S(1)}, u32[]{:S(2)}, u32[]{:S(2)}) %collective-permute-start.28) | collective-permute-done | bytes 57376 | tf_op jit(solution)/shard_map/ppermute | solution.py:452
  70.7 0.7 collective-permute-done.27
  71.4 0.3 collective-permute-done.26
  71.6 0.1 collective-permute-start.30
  71.7 1.0 %restore.1 = (f32[512,128]{1,0:T(8,128)}, f32[512,128]{1,0:T(8,128)}) custom-call(f32[2,2,32,128]{3,2,1,0:T(8,128)S(1)} %get-tuple-element.92.refs_0_, f32[2,2,32,128]{3,2,1,0:T(8,128)S(1)} %get-tuple-element.114.refs_1_, f32[2,2,32,128]{3,2,1,0:T(8,128)S(1)} %get-tuple-element.115.refs_2_, f32[2,2,32,128]{3,2,1,0:T(8,128)S(1)} %get-tuple-element.113.refs_3_, ...), custom_call_target="tpu_custom_call" | custom-call | bytes 1024 | tf_op jit(solution)/shard_map/restore/pallas_call | solution.py:24
  72.7 0.5 collective-permute-done.30.refs_3_
  73.2 1.6 %unpack.1 = (f32[2,27,64,64]{3,2,1,0:T(8,128)}, f32[2,64]{1,0:T(2,128)}) custom-call(f32[448,128]{1,0:T(8,128)S(1)} %pad_maximum_fusion.refs_0_, f32[448,128]{1,0:T(8,128)S(1)} %pad_maximum_fusion.1.refs_1_, f32[448,128]{1,0:T(8,128)S(1)} %collective-permute-done.29.refs_2_, f32[448,128]{1,0:T(8,128)S(1)} %collective-permute-done.30.refs_3_), custom_call_target="tpu_custom_call" | custom-call | bytes 1024 | tf_op jit(solution)/shard_map/unpack/pallas_call | solution.py:24
  (41 shorter events, 0.3 us)
Async XLA Ops:
  0.6 1.0 %copy-start.1 = (f32[2,64,2,2,128]{4,3,2,1,0:T(2,128)S(1)}, f32[2,64,2,2,128]{4,3,2,1,0:T(2,128)}, u32[]{:S(2)}) copy-start(f32[2,64,2,2,128]{4,3,2,1,0:T(2,128)} %param.4) | copy-start | bytes 786436
  1.6 0.9 %copy-start.2 = (f32[2,64,2,2,128]{4,3,2,1,0:T(2,128)S(1)}, f32[2,64,2,2,128]{4,3,2,1,0:T(2,128)}, u32[]{:S(2)}) copy-start(f32[2,64,2,2,128]{4,3,2,1,0:T(2,128)} %param.7) | copy-start | bytes 786436
  2.7 3.7 %collective-permute-start = (f32[2,2,2,8,128]{4,3,2,1,0:T(8,128)S(1)}, f32[2,2,2,8,128]{4,3,2,1,0:T(8,128)S(1)}, u32[]{:S(2)}, u32[]{:S(2)}) collective-permute-start(f32[2,2,2,8,128]{4,3,2,1,0:T(8,128)S(1)} %get-tuple-element.60), channel_id=1, source_target_pairs={{0,1},{1,0},{2,3},{3,2},{4,5},{5,4},{6,7},{7,6},{8,9},{9,8},{10,11... | collective-permute-start | bytes 98312 | tf_op jit(solution)/shard_map/ppermute | solution.py:439
  3.2 3.2 %collective-permute-start.1 = (f32[2,2,2,8,128]{4,3,2,1,0:T(8,128)S(1)}, f32[2,2,2,8,128]{4,3,2,1,0:T(8,128)S(1)}, u32[]{:S(2)}, u32[]{:S(2)}) collective-permute-start(f32[2,2,2,8,128]{4,3,2,1,0:T(8,128)S(1)} %get-tuple-element.61), channel_id=1, source_target_pairs={{1,2},{2,1},{5,6},{6,5},{9,10},{10,9},{13,14},{14,13},{17,18},{18,... | collective-permute-start | bytes 98312 | tf_op jit(solution)/shard_map/ppermute | solution.py:479
  3.9 1.5 %copy-start = (f32[2,27,64,64]{3,2,1,0:T(8,128)S(1)}, f32[2,27,64,64]{3,2,1,0:T(8,128)}, u32[]{:S(2)}) copy-start(f32[2,27,64,64]{3,2,1,0:T(8,128)} %weights.1) | copy-start | bytes 2654212
  5.4 0.7 copy-start.3
  6.5 13.6 %collective-permute-start.2 = (f32[14,64,128]{2,1,0:T(8,128)S(1)}, f32[14,64,128]{2,1,0:T(8,128)S(1)}, u32[]{:S(2)}, u32[]{:S(2)}) collective-permute-start(f32[14,64,128]{2,1,0:T(8,128)S(1)} %get-tuple-element.67), channel_id=1, source_target_pairs={{0,16},{16,0},{1,17},{17,1},{2,18},{18,2},{3,19},{19,3},{4,20},{20... | collective-permute-start | bytes 1376264 | tf_op jit(solution)/shard_map/ppermute | solution.py:443
  9.1 5.1 %collective-permute-start.3 = (f32[2,88,128]{2,1,0:T(8,128)S(1)}, f32[2,88,128]{2,1,0:T(8,128)S(1)}, u32[]{:S(2)}, u32[]{:S(2)}) collective-permute-start(f32[2,88,128]{2,1,0:T(8,128)S(1)} %get-tuple-element.69), channel_id=1, source_target_pairs={{0,4},{4,0},{8,12},{12,8},{1,5},{5,1},{9,13},{13,9},{2,6},{6,2},{1... | collective-permute-start | bytes 270344 | tf_op jit(solution)/shard_map/ppermute | solution.py:431
  10.7 6.7 %collective-permute-start.5 = (f32[2,88,128]{2,1,0:T(8,128)S(1)}, f32[2,88,128]{2,1,0:T(8,128)S(1)}, u32[]{:S(2)}, u32[]{:S(2)}) collective-permute-start(f32[2,88,128]{2,1,0:T(8,128)S(1)} %get-tuple-element.70), channel_id=1, source_target_pairs={{0,8},{4,12},{8,0},{12,4},{1,9},{5,13},{9,1},{13,5},{2,10},{6,14},... | collective-permute-start | bytes 270344 | tf_op jit(solution)/shard_map/ppermute | solution.py:431
  13.3 6.3 %collective-permute-start.6 = (f32[2,88,128]{2,1,0:T(8,128)S(1)}, f32[2,88,128]{2,1,0:T(8,128)S(1)}, u32[]{:S(2)}, u32[]{:S(2)}) collective-permute-start(f32[2,88,128]{2,1,0:T(8,128)S(1)} %get-tuple-element.71), channel_id=1, source_target_pairs={{0,12},{4,8},{8,4},{12,0},{1,13},{5,9},{9,5},{13,1},{2,14},{6,10},... | collective-permute-start | bytes 270344 | tf_op jit(solution)/shard_map/ppermute | solution.py:431
  14.2 5.9 %collective-permute-start.4 = (f32[2,48,128]{2,1,0:T(8,128)S(1)}, f32[2,48,128]{2,1,0:T(8,128)S(1)}, u32[]{:S(2)}, u32[]{:S(2)}) collective-permute-start(f32[2,48,128]{2,1,0:T(8,128)S(1)} %slice.118), channel_id=1, source_target_pairs={{0,16},{16,0},{1,17},{17,1},{2,18},{18,2},{3,19},{19,3},{4,20},{20... | collective-permute-start | bytes 147464 | tf_op jit(solution)/shard_map/ppermute | solution.py:443
  17.4 8.0 %collective-permute-start.8 = (f32[2,48,128]{2,1,0:T(8,128)S(1)}, f32[2,48,128]{2,1,0:T(8,128)S(1)}, u32[]{:S(2)}, u32[]{:S(2)}) collective-permute-start(f32[2,48,128]{2,1,0:T(8,128)S(1)} %slice.119), channel_id=1, source_target_pairs={{0,16},{16,0},{1,17},{17,1},{2,18},{18,2},{3,19},{19,3},{4,20},{20... | collective-permute-start | bytes 147464 | tf_op jit(solution)/shard_map/ppermute | solution.py:443
  19.6 5.7 %collective-permute-start.9 = (f32[2,48,128]{2,1,0:T(8,128)S(1)}, f32[2,48,128]{2,1,0:T(8,128)S(1)}, u32[]{:S(2)}, u32[]{:S(2)}) collective-permute-start(f32[2,48,128]{2,1,0:T(8,128)S(1)} %slice.120), channel_id=1, source_target_pairs={{0,16},{16,0},{1,17},{17,1},{2,18},{18,2},{3,19},{19,3},{4,20},{20... | collective-permute-start | bytes 147464 | tf_op jit(solution)/shard_map/ppermute | solution.py:443
  20.2 4.4 %collective-permute-start.7 = (f32[14,64,128]{2,1,0:T(8,128)S(1)}, f32[14,64,128]{2,1,0:T(8,128)S(1)}, u32[]{:S(2)}, u32[]{:S(2)}) collective-permute-start(f32[14,64,128]{2,1,0:T(8,128)S(1)} %collective-permute-done.2.refs_0_), channel_id=1, source_target_pairs={{0,1},{1,0},{2,3},{3,2},{4,5},{5,4},{6,7},{7,6},{8,9},{9,8},{10,11... | collective-permute-start | bytes 1376264 | tf_op jit(solution)/shard_map/ppermute | solution.py:439
  23.1 9.4 %collective-permute-start.10 = (f32[3,2,40,128]{3,2,1,0:T(8,128)S(1)}, f32[3,2,40,128]{3,2,1,0:T(8,128)S(1)}, u32[]{:S(2)}, u32[]{:S(2)}) collective-permute-start(f32[3,2,40,128]{3,2,1,0:T(8,128)S(1)} %pad_maximum_fusion.4), channel_id=1, source_target_pairs={{0,16},{16,0},{1,17},{17,1},{2,18},{18,2},{3,19},{19,3},{4,20},{20... | collective-permute-start | bytes 368648 | tf_op jit(solution)/shard_map/ppermute | solution.py:443
  29.9 9.4 %collective-permute-start.11 = (f32[2,2,2,32,128]{4,3,2,1,0:T(8,128)S(1)}, f32[2,2,2,32,128]{4,3,2,1,0:T(8,128)S(1)}, u32[]{:S(2)}, u32[]{:S(2)}) collective-permute-start(f32[2,2,2,32,128]{4,3,2,1,0:T(8,128)S(1)} %pad_maximum_fusion.3), channel_id=1, source_target_pairs={{0,8},{4,12},{8,0},{12,4},{1,9},{5,13},{9,1},{13,5},{2,10},{6,14},... | collective-permute-start | bytes 393224 | tf_op jit(solution)/shard_map/ppermute | solution.py:439
  39.4 1.6 %collective-permute-start.12 = (f32[448,128]{1,0:T(8,128)S(1)}, f32[448,128]{1,0:T(8,128)S(1)}, u32[]{:S(2)}, u32[]{:S(2)}) collective-permute-start(f32[448,128]{1,0:T(8,128)S(1)} %bitcast.45), channel_id=1, source_target_pairs={{0,1},{1,0},{2,3},{3,2},{4,5},{5,4},{6,7},{7,6},{8,9},{9,8},{10,11... | collective-permute-start | bytes 688136 | tf_op jit(solution)/shard_map/ppermute | solution.py:439
  39.5 1.8 %collective-permute-start.13 = (f32[448,128]{1,0:T(8,128)S(1)}, f32[448,128]{1,0:T(8,128)S(1)}, u32[]{:S(2)}, u32[]{:S(2)}) collective-permute-start(f32[448,128]{1,0:T(8,128)S(1)} %bitcast.44), channel_id=1, source_target_pairs={{0,1},{1,0},{2,3},{3,2},{4,5},{5,4},{6,7},{7,6},{8,9},{9,8},{10,11... | collective-permute-start | bytes 688136 | tf_op jit(solution)/shard_map/ppermute | solution.py:439
  41.4 9.1 %collective-permute-start.14 = (f32[224,128]{1,0:T(8,128)S(1)}, f32[224,128]{1,0:T(8,128)S(1)}, u32[]{:S(2)}, u32[]{:S(2)}) collective-permute-start(f32[224,128]{1,0:T(8,128)S(1)} %slice.129), channel_id=1, source_target_pairs={{0,2},{1,3},{2,0},{3,1},{4,6},{5,7},{6,4},{7,5},{8,10},{9,11},{10,... | collective-permute-start | bytes 344072 | tf_op jit(solution)/shard_map/ppermute | solution.py:439
  42.7 6.5 %collective-permute-start.18 = (f32[224,128]{1,0:T(8,128)S(1)}, f32[224,128]{1,0:T(8,128)S(1)}, u32[]{:S(2)}, u32[]{:S(2)}) collective-permute-start(f32[224,128]{1,0:T(8,128)S(1)} %slice.113), channel_id=1, source_target_pairs={{0,2},{1,3},{2,0},{3,1},{4,6},{5,7},{6,4},{7,5},{8,10},{9,11},{10,... | collective-permute-start | bytes 344072 | tf_op jit(solution)/shard_map/ppermute | solution.py:439
  43.5 11.4 %collective-permute-start.15 = (f32[3,2,2,32,128]{4,3,2,1,0:T(8,128)S(1)}, f32[3,2,2,32,128]{4,3,2,1,0:T(8,128)S(1)}, u32[]{:S(2)}, u32[]{:S(2)}) collective-permute-start(f32[3,2,2,32,128]{4,3,2,1,0:T(8,128)S(1)} %pad_maximum_fusion.2), channel_id=1, source_target_pairs={{0,4},{4,0},{8,12},{12,8},{1,5},{5,1},{9,13},{13,9},{2,6},{6,2},{1... | collective-permute-start | bytes 589832 | tf_op jit(solution)/shard_map/ppermute | solution.py:439
  44.9 6.7 %collective-permute-start.16 = (f32[2,2,32,128]{3,2,1,0:T(8,128)S(1)}, f32[2,2,32,128]{3,2,1,0:T(8,128)S(1)}, u32[]{:S(2)}, u32[]{:S(2)}) collective-permute-start(f32[2,2,32,128]{3,2,1,0:T(8,128)S(1)} %get-tuple-element.96), channel_id=1, source_target_pairs={{0,8},{4,12},{8,0},{12,4},{1,9},{5,13},{9,1},{13,5},{2,10},{6,14},... | collective-permute-start | bytes 196616 | tf_op jit(solution)/shard_map/ppermute | solution.py:439
  47.4 7.5 %collective-permute-start.17 = (f32[2,2,32,128]{3,2,1,0:T(8,128)S(1)}, f32[2,2,32,128]{3,2,1,0:T(8,128)S(1)}, u32[]{:S(2)}, u32[]{:S(2)}) collective-permute-start(f32[2,2,32,128]{3,2,1,0:T(8,128)S(1)} %get-tuple-element.97), channel_id=1, source_target_pairs={{0,12},{4,8},{8,4},{12,0},{1,13},{5,9},{9,5},{13,1},{2,14},{6,10},... | collective-permute-start | bytes 196616 | tf_op jit(solution)/shard_map/ppermute | solution.py:439
  49.1 5.9 %collective-permute-start.19 = (f32[112,128]{1,0:T(8,128)S(1)}, f32[112,128]{1,0:T(8,128)S(1)}, u32[]{:S(2)}, u32[]{:S(2)}) collective-permute-start(f32[112,128]{1,0:T(8,128)S(1)} %slice_select_fusion), channel_id=1, source_target_pairs={{0,4},{4,0},{8,12},{12,8},{1,5},{5,1},{9,13},{13,9},{2,6},{6,2},{1... | collective-permute-start | bytes 172040 | tf_op jit(solution)/shard_map/ppermute | solution.py:439
  55.0 4.2 %collective-permute-start.24 = (f32[112,128]{1,0:T(8,128)S(1)}, f32[112,128]{1,0:T(8,128)S(1)}, u32[]{:S(2)}, u32[]{:S(2)}) collective-permute-start(f32[112,128]{1,0:T(8,128)S(1)} %slice_select_fusion.1), channel_id=1, source_target_pairs={{0,4},{4,0},{8,12},{12,8},{1,5},{5,1},{9,13},{13,9},{2,6},{6,2},{1... | collective-permute-start | bytes 172040 | tf_op jit(solution)/shard_map/ppermute | solution.py:439
  55.1 6.9 %collective-permute-start.20 = (f32[112,128]{1,0:T(8,128)S(1)}, f32[112,128]{1,0:T(8,128)S(1)}, u32[]{:S(2)}, u32[]{:S(2)}) collective-permute-start(f32[112,128]{1,0:T(8,128)S(1)} %select_add_fusion.1), channel_id=1, source_target_pairs={{0,8},{4,12},{8,0},{12,4},{1,9},{5,13},{9,1},{13,5},{2,10},{6,14},... | collective-permute-start | bytes 172040 | tf_op jit(solution)/shard_map/ppermute | solution.py:439
  59.2 6.3 %collective-permute-start.25 = (f32[112,128]{1,0:T(8,128)S(1)}, f32[112,128]{1,0:T(8,128)S(1)}, u32[]{:S(2)}, u32[]{:S(2)}) collective-permute-start(f32[112,128]{1,0:T(8,128)S(1)} %select_add_fusion), channel_id=1, source_target_pairs={{0,8},{4,12},{8,0},{12,4},{1,9},{5,13},{9,1},{13,5},{2,10},{6,14},... | collective-permute-start | bytes 172040 | tf_op jit(solution)/shard_map/ppermute | solution.py:439
  61.9 5.5 %collective-permute-start.23 = (f32[112,128]{1,0:T(8,128)S(1)}, f32[112,128]{1,0:T(8,128)S(1)}, u32[]{:S(2)}, u32[]{:S(2)}) collective-permute-start(f32[112,128]{1,0:T(8,128)S(1)} %add.34), channel_id=1, source_target_pairs={{0,6},{1,7},{2,4},{3,5},{4,2},{5,3},{6,0},{7,1},{8,14},{9,15},{10,... | collective-permute-start | bytes 172040 | tf_op jit(solution)/shard_map/ppermute | solution.py:452
  63.6 5.5 %collective-permute-start.22 = (f32[112,128]{1,0:T(8,128)S(1)}, f32[112,128]{1,0:T(8,128)S(1)}, u32[]{:S(2)}, u32[]{:S(2)}) collective-permute-start(f32[112,128]{1,0:T(8,128)S(1)} %add.34), channel_id=1, source_target_pairs={{0,2},{1,3},{2,0},{3,1},{4,6},{5,7},{6,4},{7,5},{8,10},{9,11},{10,... | collective-permute-start | bytes 172040 | tf_op jit(solution)/shard_map/ppermute | solution.py:439
  63.9 5.2 %collective-permute-start.21 = (f32[112,128]{1,0:T(8,128)S(1)}, f32[112,128]{1,0:T(8,128)S(1)}, u32[]{:S(2)}, u32[]{:S(2)}) collective-permute-start(f32[112,128]{1,0:T(8,128)S(1)} %add.34), channel_id=1, source_target_pairs={{0,4},{4,0},{8,12},{12,8},{1,5},{5,1},{9,13},{13,9},{2,6},{6,2},{1... | collective-permute-start | bytes 172040 | tf_op jit(solution)/shard_map/ppermute | solution.py:439
  65.5 5.1 %collective-permute-start.28 = (f32[112,128]{1,0:T(8,128)S(1)}, f32[112,128]{1,0:T(8,128)S(1)}, u32[]{:S(2)}, u32[]{:S(2)}) collective-permute-start(f32[112,128]{1,0:T(8,128)S(1)} %add.36), channel_id=1, source_target_pairs={{0,6},{1,7},{2,4},{3,5},{4,2},{5,3},{6,0},{7,1},{8,14},{9,15},{10,... | collective-permute-start | bytes 172040 | tf_op jit(solution)/shard_map/ppermute | solution.py:452
  67.2 4.2 %collective-permute-start.27 = (f32[112,128]{1,0:T(8,128)S(1)}, f32[112,128]{1,0:T(8,128)S(1)}, u32[]{:S(2)}, u32[]{:S(2)}) collective-permute-start(f32[112,128]{1,0:T(8,128)S(1)} %add.36), channel_id=1, source_target_pairs={{0,2},{1,3},{2,0},{3,1},{4,6},{5,7},{6,4},{7,5},{8,10},{9,11},{10,... | collective-permute-start | bytes 172040 | tf_op jit(solution)/shard_map/ppermute | solution.py:439
  67.4 4.2 %collective-permute-start.26 = (f32[112,128]{1,0:T(8,128)S(1)}, f32[112,128]{1,0:T(8,128)S(1)}, u32[]{:S(2)}, u32[]{:S(2)}) collective-permute-start(f32[112,128]{1,0:T(8,128)S(1)} %add.36), channel_id=1, source_target_pairs={{0,4},{4,0},{8,12},{12,8},{1,5},{5,1},{9,13},{13,9},{2,6},{6,2},{1... | collective-permute-start | bytes 172040 | tf_op jit(solution)/shard_map/ppermute | solution.py:439
  69.1 3.6 %collective-permute-start.29 = (f32[448,128]{1,0:T(8,128)S(1)}, f32[448,128]{1,0:T(8,128)S(1)}, u32[]{:S(2)}, u32[]{:S(2)}) collective-permute-start(f32[448,128]{1,0:T(8,128)S(1)} %pad_maximum_fusion.refs_0_), channel_id=1, source_target_pairs={{0,1},{1,0},{2,3},{3,2},{4,5},{5,4},{6,7},{7,6},{8,9},{9,8},{10,11... | collective-permute-start | bytes 688136 | tf_op jit(solution)/shard_map/ppermute | solution.py:439
  71.6 1.6 %collective-permute-start.30 = (f32[448,128]{1,0:T(8,128)S(1)}, f32[448,128]{1,0:T(8,128)S(1)}, u32[]{:S(2)}, u32[]{:S(2)}) collective-permute-start(f32[448,128]{1,0:T(8,128)S(1)} %pad_maximum_fusion.1.refs_1_), channel_id=1, source_target_pairs={{0,1},{1,0},{2,3},{3,2},{4,5},{5,4},{6,7},{7,6},{8,9},{9,8},{10,11... | collective-permute-start | bytes 688136 | tf_op jit(solution)/shard_map/ppermute | solution.py:439

commit v16 on v15

--- a/solution.py
+++ b/solution.py
@@ -53,27 +53,6 @@
     start = lax.axis_index("gz") % 2 * half
     for index in range(half):
         sent[index] = own[start + index]
-
-
-def turned_rows(dims, source, micro, y):
-    _, chans, size_x, local_y, _ = dims
-    step = size_x * local_y
-    first = micro * chans * step + y
-    parts = [source[pl.ds(first + x * local_y, chans, stride=step), :] for x in range(size_x)]
-    return jnp.concatenate(parts, axis=0).T
-
-
-def turn_kernel(dims, inflow, cotangent, rows, pair, inner):
-    micros, _, _, local_y, local_z = dims
-    odd = lax.axis_index("gz") % 2 == 1
-    for field, source in enumerate((inflow, cotangent)):
-        for micro in range(micros):
-            for y in range(local_y):
-                turned = turned_rows(dims, source, micro, y)
-                rows[field, micro, y] = turned
-                low, high = turned[:HALO], turned[local_z - HALO :]
-                pair[field, micro, y] = jnp.where(odd, low, high)
-                inner[field, micro, y] = jnp.where(odd, high, low)
 
 
 def window_kernel(dims, rows, pair, inner, *refs):
@@ -464,14 +443,12 @@
     chunk_y = max(n for n in range(1, rows_y + 1) if rows_y % n == 0 and n * depth <= 384)
     scale = 1.0 / math.sqrt(micros * size_x * rows_y * local_z * columns)
     rows = micros * chans * size_x * local_y
-    blocks = [inflow.reshape(rows, local_z), cotangent.reshape(rows, local_z)]
-    ends = ((2, micros, local_y, HALO, LANES), F32)
-    fields, pair, inner = call(
-        functools.partial(turn_kernel, inflow.shape),
-        "turn",
-        [((2, micros, local_y, local_z, LANES), F32), ends, ends],
-        blocks,
-    )
+    fields = jnp.stack([inflow, cotangent]).transpose(0, 1, 4, 5, 3, 2)
+    fields = fields.reshape(2, micros, local_y, local_z, size_x * chans)
+    low, high = fields[:, :, :, :HALO], fields[:, :, :, local_z - HALO :]
+    odd = lax.axis_index("gz") % 2 == 1
+    pair = jnp.where(odd, low, high)
+    inner = jnp.where(odd, high, low)
     packs = [((BLOCKS, chans, LANES), F32), ((BLOCKS // 2, chans, LANES), F32)]
     own, sent = call(pack_kernel, "pack", packs, [weights, biases])
     pair = swapped(pair, 1)

time: 75 us -> 73.1 us (0.975)
  local copies, waits for them, and re-layouts: 4.17 us -> 1.54 us
  waiting for transfers between devices: 18.6 us -> 20.8 us
  starting transfers between devices: 35.2 us -> 33.9 us
    unnamed x8 -> x4, local copies, waits for them, and re-layouts: 4.04 us -> 0.01 us
    ppermute x20, starting transfers between devices: 21.3 us -> 19.3 us  [swapped(): lax.ppermute(block, axis, [(i, i ^ bit) for i in range(lax.axis_size(axis...]
    another operation x0 -> x1, local copies, waits for them, and re-layouts: none -> 1.21 us  [per_device(): fields = jnp.stack([inflow, cotangent]).transpose(0, 1, 4, 5, 3, 2)]
    ppermute x20, waiting for transfers between devices: 12.6 us -> 13.7 us  [swapped(): lax.ppermute(block, axis, [(i, i ^ bit) for i in range(lax.axis_size(axis...]
    ppermute x3, waiting for transfers between devices: 4.47 us -> 5.34 us  [spread(): got.append(lax.ppermute(blocks[turn], 'gy', route))]
    pallas_call x9 -> x8, Pallas kernels: 15.7 us -> 15.5 us  [call(): pl.pallas_call(kernel, out_shape=arrays, in_specs=[VMEM] * len(args), out...]
  transfers between devices with their start and end apart: 31 -> 31, of which waited for: 14 -> 15; matrix products, arithmetic and copies ran while one was open for 0% -> 0% of each run, Pallas kernels for 18% -> 19%
where the time goes in v16:
time: 73.1 us; the launch traced here: 72.9 us
  starting transfers between devices  33.9 us (46%)
  waiting for transfers between devices  20.8 us (28%)
  Pallas kernels  15.5 us (21%)
  local copies, waits for them, and re-layouts  1.54 us (2%)
  between operations  0.97 us (1%)
    ppermute x20, starting transfers between devices, swapped(): lax.ppermute(block, axis, [(i, i ^ bit) for i in range(lax.axis_size(axis...  19.3 us
    pallas_call x8, Pallas kernels, call(): pl.pallas_call(kernel, out_shape=arrays, in_specs=[VMEM] * len(args), out...  15.5 us
    ppermute x20, waiting for transfers between devices, swapped(): lax.ppermute(block, axis, [(i, i ^ bit) for i in range(lax.axis_size(axis...  13.7 us
    ppermute x5, starting transfers between devices, crossed(): return lax.ppermute(block, 'section', [(0, 1), (1, 0)])  5.71 us
    ppermute x3, waiting for transfers between devices, spread(): got.append(lax.ppermute(blocks[turn], 'gy', route))  5.34 us
    ppermute x3, starting transfers between devices, spread(): got.append(lax.ppermute(blocks[turn], 'gy', route))  4.39 us
    ppermute x2, starting transfers between devices, around(): across = lax.ppermute(across, ('gy', 'gz'), route)  3.82 us
    ppermute x2, waiting for transfers between devices, around(): across = lax.ppermute(across, ('gy', 'gz'), route)  1.73 us
  transfers between devices with their start and end apart: 31, of which 15 were waited for; matrix products, arithmetic and copies ran while one was open for 0% of the time, Pallas kernels for 19%

profile of v16, /device:TPU:0, one launch (start us, length us, event | category | flops | bytes accessed | tf_op | source)
XLA Modules:
  0.0 72.9 jit_solution(17390123943165238308)
XLA Ops:
  0.7 1.2 %copy_bitcast_fusion = (f32[1,2,64,2,2,128]{5,2,3,4,1,0:T(8,128)S(1)}, f32[1,2,64,2,2,128]{5,2,3,4,1,0:T(8,128)S(1)}) fusion(f32[2,64,2,2,128]{4,3,2,1,0:T(2,128)} %param.7, f32[2,64,2,2,128]{4,3,2,1,0:T(2,128)} %param.4), kind=kLoop, calls=%fused_computation.1 | loop fusion | bytes 1048576 | tf_op jit(solution)/shard_map/stack | solution.py:446
  1.9 0.2 copy.17.rows
  2.2 0.5 collective-permute-start
  2.7 0.7 collective-permute-start.1
  3.4 0.3 pack.1
  3.7 0.0 collective-permute-done.pair
  3.7 0.0 collective-permute-done.1.inner
  3.7 0.1 windows.1
  3.8 2.7 %collective-permute-start.2 = (f32[14,64,128]{2,1,0:T(8,128)S(1)}, f32[14,64,128]{2,1,0:T(8,128)S(1)}, u32[]{:S(2)}, u32[]{:S(2)}) collective-permute-start(f32[14,64,128]{2,1,0:T(8,128)S(1)} %get-tuple-element.61), channel_id=1, source_target_pairs={{0,16},{16,0},{1,17},{17,1},{2,18},{18,2},{3,19},{19,3},{4,20},{20... | collective-permute-start | bytes 1376264 | tf_op jit(solution)/shard_map/ppermute | solution.py:422
  6.5 1.6 %collective-permute-start.3 = (f32[2,88,128]{2,1,0:T(8,128)S(1)}, f32[2,88,128]{2,1,0:T(8,128)S(1)}, u32[]{:S(2)}, u32[]{:S(2)}) collective-permute-start(f32[2,88,128]{2,1,0:T(8,128)S(1)} %get-tuple-element.63), channel_id=1, source_target_pairs={{0,4},{4,0},{8,12},{12,8},{1,5},{5,1},{9,13},{13,9},{2,6},{6,2},{1... | collective-permute-start | bytes 270344 | tf_op jit(solution)/shard_map/ppermute | solution.py:410
  8.1 2.6 %collective-permute-start.5 = (f32[2,88,128]{2,1,0:T(8,128)S(1)}, f32[2,88,128]{2,1,0:T(8,128)S(1)}, u32[]{:S(2)}, u32[]{:S(2)}) collective-permute-start(f32[2,88,128]{2,1,0:T(8,128)S(1)} %get-tuple-element.64), channel_id=1, source_target_pairs={{0,8},{4,12},{8,0},{12,4},{1,9},{5,13},{9,1},{13,5},{2,10},{6,14},... | collective-permute-start | bytes 270344 | tf_op jit(solution)/shard_map/ppermute | solution.py:410
  10.7 0.2 collective-permute-start.6
  10.9 0.7 own_table.1
  11.6 0.0 collective-permute-done.3.refs_1_
  11.7 0.4 collective-permute-start.4
  12.0 2.6 %collective-permute-done.5.refs_2_ = f32[2,88,128]{2,1,0:T(8,128)S(1)} collective-permute-done((f32[2,88,128]{2,1,0:T(8,128)S(1)}, f32[2,88,128]{2,1,0:T(8,128)S(1)}, u32[]{:S(2)}, u32[]{:S(2)}) %collective-permute-start.5) | collective-permute-done | bytes 90144 | tf_op jit(solution)/shard_map/ppermute | solution.py:410
  14.6 0.5 collective-permute-start.8
  15.1 2.8 %collective-permute-done.6.refs_3_ = f32[2,88,128]{2,1,0:T(8,128)S(1)} collective-permute-done((f32[2,88,128]{2,1,0:T(8,128)S(1)}, f32[2,88,128]{2,1,0:T(8,128)S(1)}, u32[]{:S(2)}, u32[]{:S(2)}) %collective-permute-start.6) | collective-permute-done | bytes 90144 | tf_op jit(solution)/shard_map/ppermute | solution.py:410
  17.9 0.5 collective-permute-start.9
  18.4 0.0 collective-permute-done.2.refs_0_
  18.5 1.8 %collective-permute-start.7 = (f32[14,64,128]{2,1,0:T(8,128)S(1)}, f32[14,64,128]{2,1,0:T(8,128)S(1)}, u32[]{:S(2)}, u32[]{:S(2)}) collective-permute-start(f32[14,64,128]{2,1,0:T(8,128)S(1)} %collective-permute-done.2.refs_0_), channel_id=1, source_target_pairs={{0,1},{1,0},{2,3},{3,2},{4,5},{5,4},{6,7},{7,6},{8,9},{9,8},{10,11... | collective-permute-start | bytes 1376264 | tf_op jit(solution)/shard_map/ppermute | solution.py:418
  20.3 1.6 %collective-permute-start.10 = (f32[3,2,40,128]{3,2,1,0:T(8,128)S(1)}, f32[3,2,40,128]{3,2,1,0:T(8,128)S(1)}, u32[]{:S(2)}, u32[]{:S(2)}) collective-permute-start(f32[3,2,40,128]{3,2,1,0:T(8,128)S(1)} %pad_maximum_fusion.5), channel_id=1, source_target_pairs={{0,16},{16,0},{1,17},{17,1},{2,18},{18,2},{3,19},{19,3},{4,20},{20... | collective-permute-start | bytes 368648 | tf_op jit(solution)/shard_map/ppermute | solution.py:422
  21.9 0.0 collective-permute-done.7.refs_1_
  21.9 0.8 %far_table.1 = (bf16[2,1920,256]{2,1,0:T(8,128)(2,1)S(1)}, bf16[2,1920,256]{2,1,0:T(8,128)(2,1)S(1)}, f32[2,8,128]{2,1,0:T(8,128)S(1)}) custom-call(f32[14,64,128]{2,1,0:T(8,128)S(1)} %collective-permute-done.2.refs_0_, f32[14,64,128]{2,1,0:T(8,128)S(1)} %collective-permute-done.7.refs_1_), custom_call_target="tpu_custom_call" | custom-call | bytes 1024 | tf_op jit(solution)/shard_map/far_table/pallas_call | solution.py:24
  22.7 4.5 %forward.1 = (bf16[5,2,480,256]{3,2,1,0:T(8,128)(2,1)S(1)}, f32[4,2,384,128]{3,2,1,0:T(8,128)S(1)}, f32[2,2,32,128]{3,2,1,0:T(8,128)S(1)}, f32[2,2,32,128]{3,2,1...) custom-call(bf16[2,1920,256]{2,1,0:T(8,128)(2,1)S(1)} %get-tuple-element.68.own, ...), custom_call_target="tpu_custom_call" | custom-call | bytes 1024 | tf_op jit(solution)/shard_map/forward/pallas_call | solution.py:24
  27.2 2.7 %collective-permute-start.11 = (f32[2,2,2,32,128]{4,3,2,1,0:T(8,128)S(1)}, f32[2,2,2,32,128]{4,3,2,1,0:T(8,128)S(1)}, u32[]{:S(2)}, u32[]{:S(2)}) collective-permute-start(f32[2,2,2,32,128]{4,3,2,1,0:T(8,128)S(1)} %pad_maximum_fusion.4), channel_id=1, source_target_pairs={{0,8},{4,12},{8,0},{12,4},{1,9},{5,13},{9,1},{13,5},{2,10},{6,14},... | collective-permute-start | bytes 393224 | tf_op jit(solution)/shard_map/ppermute | solution.py:418
  29.9 0.0 collective-permute-done.10.refs_5_
  29.9 6.5 %backward.1 = (f32[2,2,32,128]{3,2,1,0:T(8,128)S(1)}, f32[2,2,32,128]{3,2,1,0:T(8,128)S(1)}, f32[2,2,32,128]{3,2,1,0:T(8,128)S(1)}, f32[2,2,32,128]{3,2,1,0:T(8,128)S(1)}, f32[28,64,128]{2,1,0:T(8,128)S(1)}) custom-call(bf16[2,1920,256]{2,1,0:T(8,128)(2,1)S(1)} %get-tuple-element.54.own, bf16[2,1920,256]{2,1,0:T(8,128)(2,1)S(1)} %get-tuple-element.67.other, ...), custom_call_target="tpu_custom_call" | custom-call | flops 4076863488 | bytes 1024 | tf_op jit(solution)/shard_map/backward/pallas_call | solution.py:24
  36.5 0.2 collective-permute-done.11
  36.7 0.1 fusion
  36.7 0.1 collective-permute-start.12
  36.8 0.5 collective-permute-start.13
  37.3 1.0 %collective-permute-done.12 = f32[448,128]{1,0:T(8,128)S(1)} collective-permute-done((f32[448,128]{1,0:T(8,128)S(1)}, f32[448,128]{1,0:T(8,128)S(1)}, u32[]{:S(2)}, u32[]{:S(2)}) %collective-permute-start.12) | collective-permute-done | bytes 229408 | tf_op jit(solution)/shard_map/ppermute | solution.py:418
  38.3 0.3 collective-permute-done.13
  38.7 2.5 %collective-permute-start.14 = (f32[224,128]{1,0:T(8,128)S(1)}, f32[224,128]{1,0:T(8,128)S(1)}, u32[]{:S(2)}, u32[]{:S(2)}) collective-permute-start(f32[224,128]{1,0:T(8,128)S(1)} %slice.139), channel_id=1, source_target_pairs={{0,2},{1,3},{2,0},{3,1},{4,6},{5,7},{6,4},{7,5},{8,10},{9,11},{10,... | collective-permute-start | bytes 344072 | tf_op jit(solution)/shard_map/ppermute | solution.py:418
  41.2 0.1 collective-permute-start.18
  41.3 1.1 %collective-permute-start.15 = (f32[3,2,2,32,128]{4,3,2,1,0:T(8,128)S(1)}, f32[3,2,2,32,128]{4,3,2,1,0:T(8,128)S(1)}, u32[]{:S(2)}, u32[]{:S(2)}) collective-permute-start(f32[3,2,2,32,128]{4,3,2,1,0:T(8,128)S(1)} %pad_maximum_fusion.3), channel_id=1, source_target_pairs={{0,4},{4,0},{8,12},{12,8},{1,5},{5,1},{9,13},{13,9},{2,6},{6,2},{1... | collective-permute-start | bytes 589832 | tf_op jit(solution)/shard_map/ppermute | solution.py:418
  42.3 2.7 %collective-permute-start.16 = (f32[2,2,32,128]{3,2,1,0:T(8,128)S(1)}, f32[2,2,32,128]{3,2,1,0:T(8,128)S(1)}, u32[]{:S(2)}, u32[]{:S(2)}) collective-permute-start(f32[2,2,32,128]{3,2,1,0:T(8,128)S(1)} %get-tuple-element.90), channel_id=1, source_target_pairs={{0,8},{4,12},{8,0},{12,4},{1,9},{5,13},{9,1},{13,5},{2,10},{6,14},... | collective-permute-start | bytes 196616 | tf_op jit(solution)/shard_map/ppermute | solution.py:418
  45.0 0.7 collective-permute-start.17
  45.7 1.4 %collective-permute-done.18 = f32[224,128]{1,0:T(8,128)S(1)} collective-permute-done((f32[224,128]{1,0:T(8,128)S(1)}, f32[224,128]{1,0:T(8,128)S(1)}, u32[]{:S(2)}, u32[]{:S(2)}) %collective-permute-start.18) | collective-permute-done | bytes 114720 | tf_op jit(solution)/shard_map/ppermute | solution.py:418
  47.1 0.8 %collective-permute-start.19 = (f32[112,128]{1,0:T(8,128)S(1)}, f32[112,128]{1,0:T(8,128)S(1)}, u32[]{:S(2)}, u32[]{:S(2)}) collective-permute-start(f32[112,128]{1,0:T(8,128)S(1)} %slice_select_fusion), channel_id=1, source_target_pairs={{0,4},{4,0},{8,12},{12,8},{1,5},{5,1},{9,13},{13,9},{2,6},{6,2},{1... | collective-permute-start | bytes 172040 | tf_op jit(solution)/shard_map/ppermute | solution.py:418
  47.9 1.1 %collective-permute-done.16.refs_6_ = f32[2,2,32,128]{3,2,1,0:T(8,128)S(1)} collective-permute-done((f32[2,2,32,128]{3,2,1,0:T(8,128)S(1)}, f32[2,2,32,128]{3,2,1,0:T(8,128)S(1)}, u32[]{:S(2)}, u32[]{:S(2)}) %collective-permute-start.16) | collective-permute-done | bytes 65568 | tf_op jit(solution)/shard_map/ppermute | solution.py:418
  49.0 3.8 %collective-permute-done.17.refs_7_ = f32[2,2,32,128]{3,2,1,0:T(8,128)S(1)} collective-permute-done((f32[2,2,32,128]{3,2,1,0:T(8,128)S(1)}, f32[2,2,32,128]{3,2,1,0:T(8,128)S(1)}, u32[]{:S(2)}, u32[]{:S(2)}) %collective-permute-start.17) | collective-permute-done | bytes 65568 | tf_op jit(solution)/shard_map/ppermute | solution.py:418
  52.9 0.1 collective-permute-start.24
  52.9 0.0 collective-permute-done.19
  53.0 2.1 %collective-permute-start.20 = (f32[112,128]{1,0:T(8,128)S(1)}, f32[112,128]{1,0:T(8,128)S(1)}, u32[]{:S(2)}, u32[]{:S(2)}) collective-permute-start(f32[112,128]{1,0:T(8,128)S(1)} %select_add_fusion.1), channel_id=1, source_target_pairs={{0,8},{4,12},{8,0},{12,4},{1,9},{5,13},{9,1},{13,5},{2,10},{6,14},... | collective-permute-start | bytes 172040 | tf_op jit(solution)/shard_map/ppermute | solution.py:418
  55.0 2.1 %collective-permute-done.24 = f32[112,128]{1,0:T(8,128)S(1)} collective-permute-done((f32[112,128]{1,0:T(8,128)S(1)}, f32[112,128]{1,0:T(8,128)S(1)}, u32[]{:S(2)}, u32[]{:S(2)}) %collective-permute-start.24) | collective-permute-done | bytes 57376 | tf_op jit(solution)/shard_map/ppermute | solution.py:418
  57.1 0.6 collective-permute-start.25
  57.7 2.1 %collective-permute-done.20 = f32[112,128]{1,0:T(8,128)S(1)} collective-permute-done((f32[112,128]{1,0:T(8,128)S(1)}, f32[112,128]{1,0:T(8,128)S(1)}, u32[]{:S(2)}, u32[]{:S(2)}) %collective-permute-start.20) | collective-permute-done | bytes 57376 | tf_op jit(solution)/shard_map/ppermute | solution.py:418
  59.8 1.9 %collective-permute-start.23 = (f32[112,128]{1,0:T(8,128)S(1)}, f32[112,128]{1,0:T(8,128)S(1)}, u32[]{:S(2)}, u32[]{:S(2)}) collective-permute-start(f32[112,128]{1,0:T(8,128)S(1)} %add.38), channel_id=1, source_target_pairs={{0,6},{1,7},{2,4},{3,5},{4,2},{5,3},{6,0},{7,1},{8,14},{9,15},{10,... | collective-permute-start | bytes 172040 | tf_op jit(solution)/shard_map/ppermute | solution.py:431
  61.7 0.0 collective-permute-start.22
  61.7 1.6 %collective-permute-start.21 = (f32[112,128]{1,0:T(8,128)S(1)}, f32[112,128]{1,0:T(8,128)S(1)}, u32[]{:S(2)}, u32[]{:S(2)}) collective-permute-start(f32[112,128]{1,0:T(8,128)S(1)} %add.38), channel_id=1, source_target_pairs={{0,4},{4,0},{8,12},{12,8},{1,5},{5,1},{9,13},{13,9},{2,6},{6,2},{1... | collective-permute-start | bytes 172040 | tf_op jit(solution)/shard_map/ppermute | solution.py:418
  63.4 1.9 %collective-permute-start.28 = (f32[112,128]{1,0:T(8,128)S(1)}, f32[112,128]{1,0:T(8,128)S(1)}, u32[]{:S(2)}, u32[]{:S(2)}) collective-permute-start(f32[112,128]{1,0:T(8,128)S(1)} %add.40), channel_id=1, source_target_pairs={{0,6},{1,7},{2,4},{3,5},{4,2},{5,3},{6,0},{7,1},{8,14},{9,15},{10,... | collective-permute-start | bytes 172040 | tf_op jit(solution)/shard_map/ppermute | solution.py:431
  65.3 0.0 collective-permute-start.27
  65.3 0.3 collective-permute-done.23
  65.6 1.4 %collective-permute-start.26 = (f32[112,128]{1,0:T(8,128)S(1)}, f32[112,128]{1,0:T(8,128)S(1)}, u32[]{:S(2)}, u32[]{:S(2)}) collective-permute-start(f32[112,128]{1,0:T(8,128)S(1)} %add.40), channel_id=1, source_target_pairs={{0,4},{4,0},{8,12},{12,8},{1,5},{5,1},{9,13},{13,9},{2,6},{6,2},{1... | collective-permute-start | bytes 172040 | tf_op jit(solution)/shard_map/ppermute | solution.py:418
  67.0 0.1 collective-permute-start.29
  67.1 1.5 %collective-permute-done.28 = f32[112,128]{1,0:T(8,128)S(1)} collective-permute-done((f32[112,128]{1,0:T(8,128)S(1)}, f32[112,128]{1,0:T(8,128)S(1)}, u32[]{:S(2)}, u32[]{:S(2)}) %collective-permute-start.28) | collective-permute-done | bytes 57376 | tf_op jit(solution)/shard_map/ppermute | solution.py:431
  68.5 0.9 %collective-permute-done.27 = f32[112,128]{1,0:T(8,128)S(1)} collective-permute-done((f32[112,128]{1,0:T(8,128)S(1)}, f32[112,128]{1,0:T(8,128)S(1)}, u32[]{:S(2)}, u32[]{:S(2)}) %collective-permute-start.27) | collective-permute-done | bytes 57376 | tf_op jit(solution)/shard_map/ppermute | solution.py:418
  69.5 0.3 collective-permute-done.26
  69.8 0.1 collective-permute-start.30
  69.9 1.0 %restore.1 = (f32[512,128]{1,0:T(8,128)}, f32[512,128]{1,0:T(8,128)}) custom-call(f32[2,2,32,128]{3,2,1,0:T(8,128)S(1)} %get-tuple-element.86.refs_0_, f32[2,2,32,128]{3,2,1,0:T(8,128)S(1)} %get-tuple-element.110.refs_1_, f32[2,2,32,128]{3,2,1,0:T(8,128)S(1)} %get-tuple-element.111.refs_2_, f32[2,2,32,128]{3,2,1,0:T(8,128)S(1)} %get-tuple-element.109.refs_3_, ...), custom_call_target="tpu_custom_call" | custom-call | bytes 1024 | tf_op jit(solution)/shard_map/restore/pallas_call | solution.py:24
  70.8 0.5 collective-permute-done.30.refs_3_
  71.3 1.6 %unpack.1 = (f32[2,27,64,64]{3,2,1,0:T(8,128)}, f32[2,64]{1,0:T(2,128)}) custom-call(f32[448,128]{1,0:T(8,128)S(1)} %pad_maximum_fusion.1.refs_0_, f32[448,128]{1,0:T(8,128)S(1)} %pad_maximum_fusion.2.refs_1_, f32[448,128]{1,0:T(8,128)S(1)} %collective-permute-done.29.refs_2_, f32[448,128]{1,0:T(8,128)S(1)} %collective-permute-done.30.refs_3_), custom_call_target="tpu_custom_call" | custom-call | bytes 1024 | tf_op jit(solution)/shard_map/unpack/pallas_call | solution.py:24
  (40 shorter events, 0.4 us)
Async XLA Ops:
  0.6 2.7 %copy-start = (f32[2,27,64,64]{3,2,1,0:T(8,128)S(1)}, f32[2,27,64,64]{3,2,1,0:T(8,128)}, u32[]{:S(2)}) copy-start(f32[2,27,64,64]{3,2,1,0:T(8,128)} %weights.1) | copy-start | bytes 2654212
  0.6 2.7 %copy-start.1 = (f32[2,64]{1,0:T(2,128)S(1)}, f32[2,64]{1,0:T(2,128)}, u32[]{:S(2)}) copy-start(f32[2,64]{1,0:T(2,128)} %biases.1) | copy-start | bytes 1540
  2.2 1.5 %collective-permute-start = (f32[2,2,2,8,128]{4,3,2,1,0:T(8,128)S(1)}, f32[2,2,2,8,128]{4,3,2,1,0:T(8,128)S(1)}, u32[]{:S(2)}, u32[]{:S(2)}) collective-permute-start(f32[2,2,2,8,128]{4,3,2,1,0:T(8,128)S(1)} %get-tuple-element.107), channel_id=1, source_target_pairs={{0,1},{1,0},{2,3},{3,2},{4,5},{5,4},{6,7},{7,6},{8,9},{9,8},{10,11... | collective-permute-start | bytes 98312 | tf_op jit(solution)/shard_map/ppermute | solution.py:418
  2.7 1.0 %collective-permute-start.1 = (f32[2,2,2,8,128]{4,3,2,1,0:T(8,128)S(1)}, f32[2,2,2,8,128]{4,3,2,1,0:T(8,128)S(1)}, u32[]{:S(2)}, u32[]{:S(2)}) collective-permute-start(f32[2,2,2,8,128]{4,3,2,1,0:T(8,128)S(1)} %get-tuple-element.106), channel_id=1, source_target_pairs={{1,2},{2,1},{5,6},{6,5},{9,10},{10,9},{13,14},{14,13},{17,18},{18,... | collective-permute-start | bytes 98312 | tf_op jit(solution)/shard_map/ppermute | solution.py:456
  3.8 14.6 %collective-permute-start.2 = (f32[14,64,128]{2,1,0:T(8,128)S(1)}, f32[14,64,128]{2,1,0:T(8,128)S(1)}, u32[]{:S(2)}, u32[]{:S(2)}) collective-permute-start(f32[14,64,128]{2,1,0:T(8,128)S(1)} %get-tuple-element.61), channel_id=1, source_target_pairs={{0,16},{16,0},{1,17},{17,1},{2,18},{18,2},{3,19},{19,3},{4,20},{20... | collective-permute-start | bytes 1376264 | tf_op jit(solution)/shard_map/ppermute | solution.py:422
  6.5 5.1 %collective-permute-start.3 = (f32[2,88,128]{2,1,0:T(8,128)S(1)}, f32[2,88,128]{2,1,0:T(8,128)S(1)}, u32[]{:S(2)}, u32[]{:S(2)}) collective-permute-start(f32[2,88,128]{2,1,0:T(8,128)S(1)} %get-tuple-element.63), channel_id=1, source_target_pairs={{0,4},{4,0},{8,12},{12,8},{1,5},{5,1},{9,13},{13,9},{2,6},{6,2},{1... | collective-permute-start | bytes 270344 | tf_op jit(solution)/shard_map/ppermute | solution.py:410
  8.1 6.5 %collective-permute-start.5 = (f32[2,88,128]{2,1,0:T(8,128)S(1)}, f32[2,88,128]{2,1,0:T(8,128)S(1)}, u32[]{:S(2)}, u32[]{:S(2)}) collective-permute-start(f32[2,88,128]{2,1,0:T(8,128)S(1)} %get-tuple-element.64), channel_id=1, source_target_pairs={{0,8},{4,12},{8,0},{12,4},{1,9},{5,13},{9,1},{13,5},{2,10},{6,14},... | collective-permute-start | bytes 270344 | tf_op jit(solution)/shard_map/ppermute | solution.py:410
  10.7 7.2 %collective-permute-start.6 = (f32[2,88,128]{2,1,0:T(8,128)S(1)}, f32[2,88,128]{2,1,0:T(8,128)S(1)}, u32[]{:S(2)}, u32[]{:S(2)}) collective-permute-start(f32[2,88,128]{2,1,0:T(8,128)S(1)} %get-tuple-element.65), channel_id=1, source_target_pairs={{0,12},{4,8},{8,4},{12,0},{1,13},{5,9},{9,5},{13,1},{2,14},{6,10},... | collective-permute-start | bytes 270344 | tf_op jit(solution)/shard_map/ppermute | solution.py:410
  11.7 6.8 %collective-permute-start.4 = (f32[2,48,128]{2,1,0:T(8,128)S(1)}, f32[2,48,128]{2,1,0:T(8,128)S(1)}, u32[]{:S(2)}, u32[]{:S(2)}) collective-permute-start(f32[2,48,128]{2,1,0:T(8,128)S(1)} %slice.128), channel_id=1, source_target_pairs={{0,16},{16,0},{1,17},{17,1},{2,18},{18,2},{3,19},{19,3},{4,20},{20... | collective-permute-start | bytes 147464 | tf_op jit(solution)/shard_map/ppermute | solution.py:422
  14.6 8.0 %collective-permute-start.8 = (f32[2,48,128]{2,1,0:T(8,128)S(1)}, f32[2,48,128]{2,1,0:T(8,128)S(1)}, u32[]{:S(2)}, u32[]{:S(2)}) collective-permute-start(f32[2,48,128]{2,1,0:T(8,128)S(1)} %slice.129), channel_id=1, source_target_pairs={{0,16},{16,0},{1,17},{17,1},{2,18},{18,2},{3,19},{19,3},{4,20},{20... | collective-permute-start | bytes 147464 | tf_op jit(solution)/shard_map/ppermute | solution.py:422
  17.9 4.8 %collective-permute-start.9 = (f32[2,48,128]{2,1,0:T(8,128)S(1)}, f32[2,48,128]{2,1,0:T(8,128)S(1)}, u32[]{:S(2)}, u32[]{:S(2)}) collective-permute-start(f32[2,48,128]{2,1,0:T(8,128)S(1)} %slice.130), channel_id=1, source_target_pairs={{0,16},{16,0},{1,17},{17,1},{2,18},{18,2},{3,19},{19,3},{4,20},{20... | collective-permute-start | bytes 147464 | tf_op jit(solution)/shard_map/ppermute | solution.py:422
  18.5 3.4 %collective-permute-start.7 = (f32[14,64,128]{2,1,0:T(8,128)S(1)}, f32[14,64,128]{2,1,0:T(8,128)S(1)}, u32[]{:S(2)}, u32[]{:S(2)}) collective-permute-start(f32[14,64,128]{2,1,0:T(8,128)S(1)} %collective-permute-done.2.refs_0_), channel_id=1, source_target_pairs={{0,1},{1,0},{2,3},{3,2},{4,5},{5,4},{6,7},{7,6},{8,9},{9,8},{10,11... | collective-permute-start | bytes 1376264 | tf_op jit(solution)/shard_map/ppermute | solution.py:418
  20.3 9.6 %collective-permute-start.10 = (f32[3,2,40,128]{3,2,1,0:T(8,128)S(1)}, f32[3,2,40,128]{3,2,1,0:T(8,128)S(1)}, u32[]{:S(2)}, u32[]{:S(2)}) collective-permute-start(f32[3,2,40,128]{3,2,1,0:T(8,128)S(1)} %pad_maximum_fusion.5), channel_id=1, source_target_pairs={{0,16},{16,0},{1,17},{17,1},{2,18},{18,2},{3,19},{19,3},{4,20},{20... | collective-permute-start | bytes 368648 | tf_op jit(solution)/shard_map/ppermute | solution.py:422
  27.2 9.5 %collective-permute-start.11 = (f32[2,2,2,32,128]{4,3,2,1,0:T(8,128)S(1)}, f32[2,2,2,32,128]{4,3,2,1,0:T(8,128)S(1)}, u32[]{:S(2)}, u32[]{:S(2)}) collective-permute-start(f32[2,2,2,32,128]{4,3,2,1,0:T(8,128)S(1)} %pad_maximum_fusion.4), channel_id=1, source_target_pairs={{0,8},{4,12},{8,0},{12,4},{1,9},{5,13},{9,1},{13,5},{2,10},{6,14},... | collective-permute-start | bytes 393224 | tf_op jit(solution)/shard_map/ppermute | solution.py:418
  36.7 1.6 %collective-permute-start.12 = (f32[448,128]{1,0:T(8,128)S(1)}, f32[448,128]{1,0:T(8,128)S(1)}, u32[]{:S(2)}, u32[]{:S(2)}) collective-permute-start(f32[448,128]{1,0:T(8,128)S(1)} %bitcast.49), channel_id=1, source_target_pairs={{0,1},{1,0},{2,3},{3,2},{4,5},{5,4},{6,7},{7,6},{8,9},{9,8},{10,11... | collective-permute-start | bytes 688136 | tf_op jit(solution)/shard_map/ppermute | solution.py:418
  36.8 1.8 %collective-permute-start.13 = (f32[448,128]{1,0:T(8,128)S(1)}, f32[448,128]{1,0:T(8,128)S(1)}, u32[]{:S(2)}, u32[]{:S(2)}) collective-permute-start(f32[448,128]{1,0:T(8,128)S(1)} %bitcast.48), channel_id=1, source_target_pairs={{0,1},{1,0},{2,3},{3,2},{4,5},{5,4},{6,7},{7,6},{8,9},{9,8},{10,11... | collective-permute-start | bytes 688136 | tf_op jit(solution)/shard_map/ppermute | solution.py:418
  38.7 9.2 %collective-permute-start.14 = (f32[224,128]{1,0:T(8,128)S(1)}, f32[224,128]{1,0:T(8,128)S(1)}, u32[]{:S(2)}, u32[]{:S(2)}) collective-permute-start(f32[224,128]{1,0:T(8,128)S(1)} %slice.139), channel_id=1, source_target_pairs={{0,2},{1,3},{2,0},{3,1},{4,6},{5,7},{6,4},{7,5},{8,10},{9,11},{10,... | collective-permute-start | bytes 344072 | tf_op jit(solution)/shard_map/ppermute | solution.py:418
  41.2 5.9 %collective-permute-start.18 = (f32[224,128]{1,0:T(8,128)S(1)}, f32[224,128]{1,0:T(8,128)S(1)}, u32[]{:S(2)}, u32[]{:S(2)}) collective-permute-start(f32[224,128]{1,0:T(8,128)S(1)} %slice.121), channel_id=1, source_target_pairs={{0,2},{1,3},{2,0},{3,1},{4,6},{5,7},{6,4},{7,5},{8,10},{9,11},{10,... | collective-permute-start | bytes 344072 | tf_op jit(solution)/shard_map/ppermute | solution.py:418
  41.3 11.6 %collective-permute-start.15 = (f32[3,2,2,32,128]{4,3,2,1,0:T(8,128)S(1)}, f32[3,2,2,32,128]{4,3,2,1,0:T(8,128)S(1)}, u32[]{:S(2)}, u32[]{:S(2)}) collective-permute-start(f32[3,2,2,32,128]{4,3,2,1,0:T(8,128)S(1)} %pad_maximum_fusion.3), channel_id=1, source_target_pairs={{0,4},{4,0},{8,12},{12,8},{1,5},{5,1},{9,13},{13,9},{2,6},{6,2},{1... | collective-permute-start | bytes 589832 | tf_op jit(solution)/shard_map/ppermute | solution.py:418
  42.3 6.7 %collective-permute-start.16 = (f32[2,2,32,128]{3,2,1,0:T(8,128)S(1)}, f32[2,2,32,128]{3,2,1,0:T(8,128)S(1)}, u32[]{:S(2)}, u32[]{:S(2)}) collective-permute-start(f32[2,2,32,128]{3,2,1,0:T(8,128)S(1)} %get-tuple-element.90), channel_id=1, source_target_pairs={{0,8},{4,12},{8,0},{12,4},{1,9},{5,13},{9,1},{13,5},{2,10},{6,14},... | collective-permute-start | bytes 196616 | tf_op jit(solution)/shard_map/ppermute | solution.py:418
  45.0 7.8 %collective-permute-start.17 = (f32[2,2,32,128]{3,2,1,0:T(8,128)S(1)}, f32[2,2,32,128]{3,2,1,0:T(8,128)S(1)}, u32[]{:S(2)}, u32[]{:S(2)}) collective-permute-start(f32[2,2,32,128]{3,2,1,0:T(8,128)S(1)} %get-tuple-element.91), channel_id=1, source_target_pairs={{0,12},{4,8},{8,4},{12,0},{1,13},{5,9},{9,5},{13,1},{2,14},{6,10},... | collective-permute-start | bytes 196616 | tf_op jit(solution)/shard_map/ppermute | solution.py:418
  47.1 5.8 %collective-permute-start.19 = (f32[112,128]{1,0:T(8,128)S(1)}, f32[112,128]{1,0:T(8,128)S(1)}, u32[]{:S(2)}, u32[]{:S(2)}) collective-permute-start(f32[112,128]{1,0:T(8,128)S(1)} %slice_select_fusion), channel_id=1, source_target_pairs={{0,4},{4,0},{8,12},{12,8},{1,5},{5,1},{9,13},{13,9},{2,6},{6,2},{1... | collective-permute-start | bytes 172040 | tf_op jit(solution)/shard_map/ppermute | solution.py:418
  52.9 4.2 %collective-permute-start.24 = (f32[112,128]{1,0:T(8,128)S(1)}, f32[112,128]{1,0:T(8,128)S(1)}, u32[]{:S(2)}, u32[]{:S(2)}) collective-permute-start(f32[112,128]{1,0:T(8,128)S(1)} %slice_select_fusion.1), channel_id=1, source_target_pairs={{0,4},{4,0},{8,12},{12,8},{1,5},{5,1},{9,13},{13,9},{2,6},{6,2},{1... | collective-permute-start | bytes 172040 | tf_op jit(solution)/shard_map/ppermute | solution.py:418
  53.0 6.9 %collective-permute-start.20 = (f32[112,128]{1,0:T(8,128)S(1)}, f32[112,128]{1,0:T(8,128)S(1)}, u32[]{:S(2)}, u32[]{:S(2)}) collective-permute-start(f32[112,128]{1,0:T(8,128)S(1)} %select_add_fusion.1), channel_id=1, source_target_pairs={{0,8},{4,12},{8,0},{12,4},{1,9},{5,13},{9,1},{13,5},{2,10},{6,14},... | collective-permute-start | bytes 172040 | tf_op jit(solution)/shard_map/ppermute | solution.py:418
  57.1 6.3 %collective-permute-start.25 = (f32[112,128]{1,0:T(8,128)S(1)}, f32[112,128]{1,0:T(8,128)S(1)}, u32[]{:S(2)}, u32[]{:S(2)}) collective-permute-start(f32[112,128]{1,0:T(8,128)S(1)} %select_add_fusion), channel_id=1, source_target_pairs={{0,8},{4,12},{8,0},{12,4},{1,9},{5,13},{9,1},{13,5},{2,10},{6,14},... | collective-permute-start | bytes 172040 | tf_op jit(solution)/shard_map/ppermute | solution.py:418
  59.8 5.7 %collective-permute-start.23 = (f32[112,128]{1,0:T(8,128)S(1)}, f32[112,128]{1,0:T(8,128)S(1)}, u32[]{:S(2)}, u32[]{:S(2)}) collective-permute-start(f32[112,128]{1,0:T(8,128)S(1)} %add.38), channel_id=1, source_target_pairs={{0,6},{1,7},{2,4},{3,5},{4,2},{5,3},{6,0},{7,1},{8,14},{9,15},{10,... | collective-permute-start | bytes 172040 | tf_op jit(solution)/shard_map/ppermute | solution.py:431
  61.7 5.2 %collective-permute-start.22 = (f32[112,128]{1,0:T(8,128)S(1)}, f32[112,128]{1,0:T(8,128)S(1)}, u32[]{:S(2)}, u32[]{:S(2)}) collective-permute-start(f32[112,128]{1,0:T(8,128)S(1)} %add.38), channel_id=1, source_target_pairs={{0,2},{1,3},{2,0},{3,1},{4,6},{5,7},{6,4},{7,5},{8,10},{9,11},{10,... | collective-permute-start | bytes 172040 | tf_op jit(solution)/shard_map/ppermute | solution.py:418
  61.7 5.2 %collective-permute-start.21 = (f32[112,128]{1,0:T(8,128)S(1)}, f32[112,128]{1,0:T(8,128)S(1)}, u32[]{:S(2)}, u32[]{:S(2)}) collective-permute-start(f32[112,128]{1,0:T(8,128)S(1)} %add.38), channel_id=1, source_target_pairs={{0,4},{4,0},{8,12},{12,8},{1,5},{5,1},{9,13},{13,9},{2,6},{6,2},{1... | collective-permute-start | bytes 172040 | tf_op jit(solution)/shard_map/ppermute | solution.py:418
  63.4 5.1 %collective-permute-start.28 = (f32[112,128]{1,0:T(8,128)S(1)}, f32[112,128]{1,0:T(8,128)S(1)}, u32[]{:S(2)}, u32[]{:S(2)}) collective-permute-start(f32[112,128]{1,0:T(8,128)S(1)} %add.40), channel_id=1, source_target_pairs={{0,6},{1,7},{2,4},{3,5},{4,2},{5,3},{6,0},{7,1},{8,14},{9,15},{10,... | collective-permute-start | bytes 172040 | tf_op jit(solution)/shard_map/ppermute | solution.py:431
  65.3 4.2 %collective-permute-start.27 = (f32[112,128]{1,0:T(8,128)S(1)}, f32[112,128]{1,0:T(8,128)S(1)}, u32[]{:S(2)}, u32[]{:S(2)}) collective-permute-start(f32[112,128]{1,0:T(8,128)S(1)} %add.40), channel_id=1, source_target_pairs={{0,2},{1,3},{2,0},{3,1},{4,6},{5,7},{6,4},{7,5},{8,10},{9,11},{10,... | collective-permute-start | bytes 172040 | tf_op jit(solution)/shard_map/ppermute | solution.py:418
  65.6 4.2 %collective-permute-start.26 = (f32[112,128]{1,0:T(8,128)S(1)}, f32[112,128]{1,0:T(8,128)S(1)}, u32[]{:S(2)}, u32[]{:S(2)}) collective-permute-start(f32[112,128]{1,0:T(8,128)S(1)} %add.40), channel_id=1, source_target_pairs={{0,4},{4,0},{8,12},{12,8},{1,5},{5,1},{9,13},{13,9},{2,6},{6,2},{1... | collective-permute-start | bytes 172040 | tf_op jit(solution)/shard_map/ppermute | solution.py:418
  67.0 3.9 %collective-permute-start.29 = (f32[448,128]{1,0:T(8,128)S(1)}, f32[448,128]{1,0:T(8,128)S(1)}, u32[]{:S(2)}, u32[]{:S(2)}) collective-permute-start(f32[448,128]{1,0:T(8,128)S(1)} %pad_maximum_fusion.1.refs_0_), channel_id=1, source_target_pairs={{0,1},{1,0},{2,3},{3,2},{4,5},{5,4},{6,7},{7,6},{8,9},{9,8},{10,11... | collective-permute-start | bytes 688136 | tf_op jit(solution)/shard_map/ppermute | solution.py:418
  69.8 1.6 %collective-permute-start.30 = (f32[448,128]{1,0:T(8,128)S(1)}, f32[448,128]{1,0:T(8,128)S(1)}, u32[]{:S(2)}, u32[]{:S(2)}) collective-permute-start(f32[448,128]{1,0:T(8,128)S(1)} %pad_maximum_fusion.2.refs_1_), channel_id=1, source_target_pairs={{0,1},{1,0},{2,3},{3,2},{4,5},{5,4},{6,7},{7,6},{8,9},{9,8},{10,11... | collective-permute-start | bytes 688136 | tf_op jit(solution)/shard_map/ppermute | solution.py:418

commit v17 on v16

--- a/solution.py
+++ b/solution.py
@@ -522,11 +522,12 @@
     else:
         outs = spread([jnp.stack(pair) for pair in zip(fronts, backs)])
     streams = [block[: 2 * part] + swapped(block[2 * part :], 2) for block in streams]
-    streams[1], outs = lax.optimization_barrier((streams[1], outs))
     sums = []
     for block in streams:
         kept = jnp.where(odd, block[part:], block[:part])
         kept = kept + swapped(jnp.where(odd, block[:part], block[part:]), 1, "gy")
+        if sums:
+            kept, outs = lax.optimization_barrier((kept, outs))
         bit = 2
         while bit < slabs:
             kept = kept + swapped(kept, bit, "gy")

time: 73.1 us -> 71.7 us (0.981)
  waiting for transfers between devices: 20.8 us -> 17.2 us
  starting transfers between devices: 33.9 us -> 36.1 us
    ppermute x20, starting transfers between devices: 19.3 us -> 23.5 us  [swapped(): lax.ppermute(block, axis, [(i, i ^ bit) for i in range(lax.axis_size(axis...]
    ppermute x20, waiting for transfers between devices: 13.7 us -> 10.2 us  [swapped(): lax.ppermute(block, axis, [(i, i ^ bit) for i in range(lax.axis_size(axis...]
    ppermute x2, starting transfers between devices: 3.82 us -> 1.86 us  [around(): across = lax.ppermute(across, ('gy', 'gz'), route)]
  transfers between devices with their start and end apart: 31 -> 31, of which waited for: 15 -> 12; matrix products, arithmetic and copies ran while one was open for 0% -> 0% of each run, Pallas kernels for 19% -> 19%
where the time goes in v17:
time: 71.7 us; the launch traced here: 71.5 us
  starting transfers between devices  36.1 us (50%)
  waiting for transfers between devices  17.2 us (24%)
  Pallas kernels  15.5 us (22%)
  local copies, waits for them, and re-layouts  1.54 us (2%)
  between operations  0.97 us (1%)
    ppermute x20, starting transfers between devices, swapped(): lax.ppermute(block, axis, [(i, i ^ bit) for i in range(lax.axis_size(axis...  23.5 us
    pallas_call x8, Pallas kernels, call(): pl.pallas_call(kernel, out_shape=arrays, in_specs=[VMEM] * len(args), out...  15.5 us
    ppermute x20, waiting for transfers between devices, swapped(): lax.ppermute(block, axis, [(i, i ^ bit) for i in range(lax.axis_size(axis...  10.2 us
    ppermute x5, starting transfers between devices, crossed(): return lax.ppermute(block, 'section', [(0, 1), (1, 0)])  5.71 us
    ppermute x3, waiting for transfers between devices, spread(): got.append(lax.ppermute(blocks[turn], 'gy', route))  5.34 us
    ppermute x3, starting transfers between devices, spread(): got.append(lax.ppermute(blocks[turn], 'gy', route))  4.39 us
    ppermute x2, starting transfers between devices, around(): across = lax.ppermute(across, ('gy', 'gz'), route)  1.86 us
    ppermute x2, waiting for transfers between devices, around(): across = lax.ppermute(across, ('gy', 'gz'), route)  1.59 us
  transfers between devices with their start and end apart: 31, of which 12 were waited for; matrix products, arithmetic and copies ran while one was open for 0% of the time, Pallas kernels for 19%

profile of v17, /device:TPU:0, one launch (start us, length us, event | category | flops | bytes accessed | tf_op | source)
XLA Modules:
  0.0 71.5 jit_solution(16880205214108131395)
XLA Ops:
  0.7 1.2 %copy_bitcast_fusion = (f32[1,2,64,2,2,128]{5,2,3,4,1,0:T(8,128)S(1)}, f32[1,2,64,2,2,128]{5,2,3,4,1,0:T(8,128)S(1)}) fusion(f32[2,64,2,2,128]{4,3,2,1,0:T(2,128)} %param.7, f32[2,64,2,2,128]{4,3,2,1,0:T(2,128)} %param.4), kind=kLoop, calls=%fused_computation.1 | loop fusion | bytes 1048576 | tf_op jit(solution)/shard_map/stack | solution.py:446
  1.9 0.2 copy.17.rows
  2.2 0.5 collective-permute-start
  2.7 0.7 collective-permute-start.1
  3.4 0.3 pack.1
  3.7 0.0 collective-permute-done.1.inner
  3.7 0.1 windows.1
  3.8 2.7 %collective-permute-start.2 = (f32[14,64,128]{2,1,0:T(8,128)S(1)}, f32[14,64,128]{2,1,0:T(8,128)S(1)}, u32[]{:S(2)}, u32[]{:S(2)}) collective-permute-start(f32[14,64,128]{2,1,0:T(8,128)S(1)} %get-tuple-element.61), channel_id=1, source_target_pairs={{0,16},{16,0},{1,17},{17,1},{2,18},{18,2},{3,19},{19,3},{4,20},{20... | collective-permute-start | bytes 1376264 | tf_op jit(solution)/shard_map/ppermute | solution.py:422
  6.5 1.6 %collective-permute-start.3 = (f32[2,88,128]{2,1,0:T(8,128)S(1)}, f32[2,88,128]{2,1,0:T(8,128)S(1)}, u32[]{:S(2)}, u32[]{:S(2)}) collective-permute-start(f32[2,88,128]{2,1,0:T(8,128)S(1)} %get-tuple-element.63), channel_id=1, source_target_pairs={{0,4},{4,0},{8,12},{12,8},{1,5},{5,1},{9,13},{13,9},{2,6},{6,2},{1... | collective-permute-start | bytes 270344 | tf_op jit(solution)/shard_map/ppermute | solution.py:410
  8.1 2.6 %collective-permute-start.5 = (f32[2,88,128]{2,1,0:T(8,128)S(1)}, f32[2,88,128]{2,1,0:T(8,128)S(1)}, u32[]{:S(2)}, u32[]{:S(2)}) collective-permute-start(f32[2,88,128]{2,1,0:T(8,128)S(1)} %get-tuple-element.64), channel_id=1, source_target_pairs={{0,8},{4,12},{8,0},{12,4},{1,9},{5,13},{9,1},{13,5},{2,10},{6,14},... | collective-permute-start | bytes 270344 | tf_op jit(solution)/shard_map/ppermute | solution.py:410
  10.7 0.2 collective-permute-start.6
  10.9 0.7 %own_table.1 = (bf16[2,1920,256]{2,1,0:T(8,128)(2,1)S(1)}, bf16[2,1920,256]{2,1,0:T(8,128)(2,1)S(1)}, f32[2,8,128]{2,1,0:T(8,128)S(1)}) custom-call(f32[28,64,128]{2,1,0:T(8,128)S(1)} %get-tuple-element.53.refs_0_), custom_call_target="tpu_custom_call" | custom-call | bytes 1024 | tf_op jit(solution)/shard_map/own_table/pallas_call | solution.py:24
  11.6 0.0 collective-permute-done.3.refs_1_
  11.7 0.4 collective-permute-start.4
  12.0 2.6 %collective-permute-done.5.refs_2_ = f32[2,88,128]{2,1,0:T(8,128)S(1)} collective-permute-done((f32[2,88,128]{2,1,0:T(8,128)S(1)}, f32[2,88,128]{2,1,0:T(8,128)S(1)}, u32[]{:S(2)}, u32[]{:S(2)}) %collective-permute-start.5) | collective-permute-done | bytes 90144 | tf_op jit(solution)/shard_map/ppermute | solution.py:410
  14.6 0.5 collective-permute-start.8
  15.1 2.8 %collective-permute-done.6.refs_3_ = f32[2,88,128]{2,1,0:T(8,128)S(1)} collective-permute-done((f32[2,88,128]{2,1,0:T(8,128)S(1)}, f32[2,88,128]{2,1,0:T(8,128)S(1)}, u32[]{:S(2)}, u32[]{:S(2)}) %collective-permute-start.6) | collective-permute-done | bytes 90144 | tf_op jit(solution)/shard_map/ppermute | solution.py:410
  17.9 0.5 collective-permute-start.9
  18.5 1.8 %collective-permute-start.7 = (f32[14,64,128]{2,1,0:T(8,128)S(1)}, f32[14,64,128]{2,1,0:T(8,128)S(1)}, u32[]{:S(2)}, u32[]{:S(2)}) collective-permute-start(f32[14,64,128]{2,1,0:T(8,128)S(1)} %collective-permute-done.2.refs_0_), channel_id=1, source_target_pairs={{0,1},{1,0},{2,3},{3,2},{4,5},{5,4},{6,7},{7,6},{8,9},{9,8},{10,11... | collective-permute-start | bytes 1376264 | tf_op jit(solution)/shard_map/ppermute | solution.py:418
  20.3 1.6 %collective-permute-start.10 = (f32[3,2,40,128]{3,2,1,0:T(8,128)S(1)}, f32[3,2,40,128]{3,2,1,0:T(8,128)S(1)}, u32[]{:S(2)}, u32[]{:S(2)}) collective-permute-start(f32[3,2,40,128]{3,2,1,0:T(8,128)S(1)} %pad_maximum_fusion.5), channel_id=1, source_target_pairs={{0,16},{16,0},{1,17},{17,1},{2,18},{18,2},{3,19},{19,3},{4,20},{20... | collective-permute-start | bytes 368648 | tf_op jit(solution)/shard_map/ppermute | solution.py:422
  21.9 0.8 %far_table.1 = (bf16[2,1920,256]{2,1,0:T(8,128)(2,1)S(1)}, bf16[2,1920,256]{2,1,0:T(8,128)(2,1)S(1)}, f32[2,8,128]{2,1,0:T(8,128)S(1)}) custom-call(f32[14,64,128]{2,1,0:T(8,128)S(1)} %collective-permute-done.2.refs_0_, f32[14,64,128]{2,1,0:T(8,128)S(1)} %collective-permute-done.7.refs_1_), custom_call_target="tpu_custom_call" | custom-call | bytes 1024 | tf_op jit(solution)/shard_map/far_table/pallas_call | solution.py:24
  22.7 0.0 collective-permute-done.9.refs_7_
  22.7 4.5 %forward.1 = (bf16[5,2,480,256]{3,2,1,0:T(8,128)(2,1)S(1)}, f32[4,2,384,128]{3,2,1,0:T(8,128)S(1)}, f32[2,2,32,128]{3,2,1,0:T(8,128)S(1)}, f32[2,2,32,128]{3,2,1...) custom-call(bf16[2,1920,256]{2,1,0:T(8,128)(2,1)S(1)} %get-tuple-element.68.own, ...), custom_call_target="tpu_custom_call" | custom-call | bytes 1024 | tf_op jit(solution)/shard_map/forward/pallas_call | solution.py:24
  27.2 2.7 %collective-permute-start.11 = (f32[2,2,2,32,128]{4,3,2,1,0:T(8,128)S(1)}, f32[2,2,2,32,128]{4,3,2,1,0:T(8,128)S(1)}, u32[]{:S(2)}, u32[]{:S(2)}) collective-permute-start(f32[2,2,2,32,128]{4,3,2,1,0:T(8,128)S(1)} %pad_maximum_fusion.4), channel_id=1, source_target_pairs={{0,8},{4,12},{8,0},{12,4},{1,9},{5,13},{9,1},{13,5},{2,10},{6,14},... | collective-permute-start | bytes 393224 | tf_op jit(solution)/shard_map/ppermute | solution.py:418
  29.9 0.0 collective-permute-done.10.refs_5_
  29.9 6.5 %backward.1 = (f32[2,2,32,128]{3,2,1,0:T(8,128)S(1)}, f32[2,2,32,128]{3,2,1,0:T(8,128)S(1)}, f32[2,2,32,128]{3,2,1,0:T(8,128)S(1)}, f32[2,2,32,128]{3,2,1,0:T(8,128)S(1)}, f32[28,64,128]{2,1,0:T(8,128)S(1)}) custom-call(bf16[2,1920,256]{2,1,0:T(8,128)(2,1)S(1)} %get-tuple-element.54.own, bf16[2,1920,256]{2,1,0:T(8,128)(2,1)S(1)} %get-tuple-element.67.other, ...), custom_call_target="tpu_custom_call" | custom-call | flops 4076863488 | bytes 1024 | tf_op jit(solution)/shard_map/backward/pallas_call | solution.py:24
  36.5 0.2 collective-permute-done.11
  36.7 0.1 fusion
  36.7 0.1 collective-permute-start.12
  36.8 0.5 collective-permute-start.13
  37.3 1.0 %collective-permute-done.12 = f32[448,128]{1,0:T(8,128)S(1)} collective-permute-done((f32[448,128]{1,0:T(8,128)S(1)}, f32[448,128]{1,0:T(8,128)S(1)}, u32[]{:S(2)}, u32[]{:S(2)}) %collective-permute-start.12) | collective-permute-done | bytes 229408 | tf_op jit(solution)/shard_map/ppermute | solution.py:418
  38.3 0.3 collective-permute-done.13
  38.7 2.5 %collective-permute-start.14 = (f32[224,128]{1,0:T(8,128)S(1)}, f32[224,128]{1,0:T(8,128)S(1)}, u32[]{:S(2)}, u32[]{:S(2)}) collective-permute-start(f32[224,128]{1,0:T(8,128)S(1)} %slice.139), channel_id=1, source_target_pairs={{0,2},{1,3},{2,0},{3,1},{4,6},{5,7},{6,4},{7,5},{8,10},{9,11},{10,... | collective-permute-start | bytes 344072 | tf_op jit(solution)/shard_map/ppermute | solution.py:418
  41.2 0.1 collective-permute-start.19
  41.3 1.1 %collective-permute-start.16 = (f32[3,2,2,32,128]{4,3,2,1,0:T(8,128)S(1)}, f32[3,2,2,32,128]{4,3,2,1,0:T(8,128)S(1)}, u32[]{:S(2)}, u32[]{:S(2)}) collective-permute-start(f32[3,2,2,32,128]{4,3,2,1,0:T(8,128)S(1)} %pad_maximum_fusion.3), channel_id=1, source_target_pairs={{0,4},{4,0},{8,12},{12,8},{1,5},{5,1},{9,13},{13,9},{2,6},{6,2},{1... | collective-permute-start | bytes 589832 | tf_op jit(solution)/shard_map/ppermute | solution.py:418
  42.3 2.7 %collective-permute-start.17 = (f32[2,2,32,128]{3,2,1,0:T(8,128)S(1)}, f32[2,2,32,128]{3,2,1,0:T(8,128)S(1)}, u32[]{:S(2)}, u32[]{:S(2)}) collective-permute-start(f32[2,2,32,128]{3,2,1,0:T(8,128)S(1)} %get-tuple-element.90), channel_id=1, source_target_pairs={{0,8},{4,12},{8,0},{12,4},{1,9},{5,13},{9,1},{13,5},{2,10},{6,14},... | collective-permute-start | bytes 196616 | tf_op jit(solution)/shard_map/ppermute | solution.py:418
  45.0 0.7 collective-permute-start.18
  45.7 1.4 %collective-permute-done.19 = f32[224,128]{1,0:T(8,128)S(1)} collective-permute-done((f32[224,128]{1,0:T(8,128)S(1)}, f32[224,128]{1,0:T(8,128)S(1)}, u32[]{:S(2)}, u32[]{:S(2)}) %collective-permute-start.19) | collective-permute-done | bytes 114720 | tf_op jit(solution)/shard_map/ppermute | solution.py:418
  47.1 0.8 %collective-permute-start.20 = (f32[112,128]{1,0:T(8,128)S(1)}, f32[112,128]{1,0:T(8,128)S(1)}, u32[]{:S(2)}, u32[]{:S(2)}) collective-permute-start(f32[112,128]{1,0:T(8,128)S(1)} %slice_select_fusion), channel_id=1, source_target_pairs={{0,4},{4,0},{8,12},{12,8},{1,5},{5,1},{9,13},{13,9},{2,6},{6,2},{1... | collective-permute-start | bytes 172040 | tf_op jit(solution)/shard_map/ppermute | solution.py:418
  47.9 1.4 %collective-permute-start.15 = (f32[112,128]{1,0:T(8,128)S(1)}, f32[112,128]{1,0:T(8,128)S(1)}, u32[]{:S(2)}, u32[]{:S(2)}) collective-permute-start(f32[112,128]{1,0:T(8,128)S(1)} %slice_select_fusion.1), channel_id=1, source_target_pairs={{0,4},{4,0},{8,12},{12,8},{1,5},{5,1},{9,13},{13,9},{2,6},{6,2},{1... | collective-permute-start | bytes 172040 | tf_op jit(solution)/shard_map/ppermute | solution.py:418
  49.3 2.8 %collective-permute-done.20 = f32[112,128]{1,0:T(8,128)S(1)} collective-permute-done((f32[112,128]{1,0:T(8,128)S(1)}, f32[112,128]{1,0:T(8,128)S(1)}, u32[]{:S(2)}, u32[]{:S(2)}) %collective-permute-start.20) | collective-permute-done | bytes 57376 | tf_op jit(solution)/shard_map/ppermute | solution.py:418
  52.1 2.6 %collective-permute-start.21 = (f32[112,128]{1,0:T(8,128)S(1)}, f32[112,128]{1,0:T(8,128)S(1)}, u32[]{:S(2)}, u32[]{:S(2)}) collective-permute-start(f32[112,128]{1,0:T(8,128)S(1)} %select_add_fusion), channel_id=1, source_target_pairs={{0,8},{4,12},{8,0},{12,4},{1,9},{5,13},{9,1},{13,5},{2,10},{6,14},... | collective-permute-start | bytes 172040 | tf_op jit(solution)/shard_map/ppermute | solution.py:418
  54.7 0.0 collective-permute-done.15
  54.7 0.0 collective-permute-done.17.refs_6_
  54.8 0.7 collective-permute-start.25
  55.5 3.2 %collective-permute-done.21 = f32[112,128]{1,0:T(8,128)S(1)} collective-permute-done((f32[112,128]{1,0:T(8,128)S(1)}, f32[112,128]{1,0:T(8,128)S(1)}, u32[]{:S(2)}, u32[]{:S(2)}) %collective-permute-start.21) | collective-permute-done | bytes 57376 | tf_op jit(solution)/shard_map/ppermute | solution.py:418
  58.6 0.9 %collective-permute-start.24 = (f32[112,128]{1,0:T(8,128)S(1)}, f32[112,128]{1,0:T(8,128)S(1)}, u32[]{:S(2)}, u32[]{:S(2)}) collective-permute-start(f32[112,128]{1,0:T(8,128)S(1)} %add.39), channel_id=1, source_target_pairs={{0,6},{1,7},{2,4},{3,5},{4,2},{5,3},{6,0},{7,1},{8,14},{9,15},{10,... | collective-permute-start | bytes 172040 | tf_op jit(solution)/shard_map/ppermute | solution.py:431
  59.6 1.0 %collective-permute-start.23 = (f32[112,128]{1,0:T(8,128)S(1)}, f32[112,128]{1,0:T(8,128)S(1)}, u32[]{:S(2)}, u32[]{:S(2)}) collective-permute-start(f32[112,128]{1,0:T(8,128)S(1)} %add.39), channel_id=1, source_target_pairs={{0,2},{1,3},{2,0},{3,1},{4,6},{5,7},{6,4},{7,5},{8,10},{9,11},{10,... | collective-permute-start | bytes 172040 | tf_op jit(solution)/shard_map/ppermute | solution.py:418
  60.6 1.6 %collective-permute-start.22 = (f32[112,128]{1,0:T(8,128)S(1)}, f32[112,128]{1,0:T(8,128)S(1)}, u32[]{:S(2)}, u32[]{:S(2)}) collective-permute-start(f32[112,128]{1,0:T(8,128)S(1)} %add.39), channel_id=1, source_target_pairs={{0,4},{4,0},{8,12},{12,8},{1,5},{5,1},{9,13},{13,9},{2,6},{6,2},{1... | collective-permute-start | bytes 172040 | tf_op jit(solution)/shard_map/ppermute | solution.py:418
  62.2 0.0 collective-permute-done.25
  62.2 0.9 %collective-permute-start.28 = (f32[112,128]{1,0:T(8,128)S(1)}, f32[112,128]{1,0:T(8,128)S(1)}, u32[]{:S(2)}, u32[]{:S(2)}) collective-permute-start(f32[112,128]{1,0:T(8,128)S(1)} %add.40), channel_id=1, source_target_pairs={{0,6},{1,7},{2,4},{3,5},{4,2},{5,3},{6,0},{7,1},{8,14},{9,15},{10,... | collective-permute-start | bytes 172040 | tf_op jit(solution)/shard_map/ppermute | solution.py:431
  63.1 1.0 %collective-permute-start.27 = (f32[112,128]{1,0:T(8,128)S(1)}, f32[112,128]{1,0:T(8,128)S(1)}, u32[]{:S(2)}, u32[]{:S(2)}) collective-permute-start(f32[112,128]{1,0:T(8,128)S(1)} %add.40), channel_id=1, source_target_pairs={{0,2},{1,3},{2,0},{3,1},{4,6},{5,7},{6,4},{7,5},{8,10},{9,11},{10,... | collective-permute-start | bytes 172040 | tf_op jit(solution)/shard_map/ppermute | solution.py:418
  64.2 0.0 collective-permute-done.24
  64.2 1.6 %collective-permute-start.26 = (f32[112,128]{1,0:T(8,128)S(1)}, f32[112,128]{1,0:T(8,128)S(1)}, u32[]{:S(2)}, u32[]{:S(2)}) collective-permute-start(f32[112,128]{1,0:T(8,128)S(1)} %add.40), channel_id=1, source_target_pairs={{0,4},{4,0},{8,12},{12,8},{1,5},{5,1},{9,13},{13,9},{2,6},{6,2},{1... | collective-permute-start | bytes 172040 | tf_op jit(solution)/shard_map/ppermute | solution.py:418
  65.8 0.0 collective-permute-done.23
  65.8 0.0 collective-permute-done.22
  65.8 0.1 collective-permute-start.29
  65.9 1.6 %collective-permute-done.28 = f32[112,128]{1,0:T(8,128)S(1)} collective-permute-done((f32[112,128]{1,0:T(8,128)S(1)}, f32[112,128]{1,0:T(8,128)S(1)}, u32[]{:S(2)}, u32[]{:S(2)}) %collective-permute-start.28) | collective-permute-done | bytes 57376 | tf_op jit(solution)/shard_map/ppermute | solution.py:431
  67.5 0.5 collective-permute-done.27
  67.9 0.4 collective-permute-done.26
  68.4 0.1 collective-permute-start.30
  68.5 1.0 %restore.1 = (f32[512,128]{1,0:T(8,128)}, f32[512,128]{1,0:T(8,128)}) custom-call(f32[2,2,32,128]{3,2,1,0:T(8,128)S(1)} %get-tuple-element.86.refs_0_, f32[2,2,32,128]{3,2,1,0:T(8,128)S(1)} %get-tuple-element.110.refs_1_, f32[2,2,32,128]{3,2,1,0:T(8,128)S(1)} %get-tuple-element.111.refs_2_, f32[2,2,32,128]{3,2,1,0:T(8,128)S(1)} %get-tuple-element.109.refs_3_, ...), custom_call_target="tpu_custom_call" | custom-call | bytes 1024 | tf_op jit(solution)/shard_map/restore/pallas_call | solution.py:24
  69.4 0.5 collective-permute-done.30.refs_3_
  69.9 1.6 %unpack.1 = (f32[2,27,64,64]{3,2,1,0:T(8,128)}, f32[2,64]{1,0:T(2,128)}) custom-call(f32[448,128]{1,0:T(8,128)S(1)} %pad_maximum_fusion.1.refs_0_, f32[448,128]{1,0:T(8,128)S(1)} %pad_maximum_fusion.2.refs_1_, f32[448,128]{1,0:T(8,128)S(1)} %collective-permute-done.29.refs_2_, f32[448,128]{1,0:T(8,128)S(1)} %collective-permute-done.30.refs_3_), custom_call_target="tpu_custom_call" | custom-call | bytes 1024 | tf_op jit(solution)/shard_map/unpack/pallas_call | solution.py:24
  (40 shorter events, 0.4 us)
Async XLA Ops:
  0.6 2.7 %copy-start = (f32[2,27,64,64]{3,2,1,0:T(8,128)S(1)}, f32[2,27,64,64]{3,2,1,0:T(8,128)}, u32[]{:S(2)}) copy-start(f32[2,27,64,64]{3,2,1,0:T(8,128)} %weights.1) | copy-start | bytes 2654212
  0.6 2.7 %copy-start.1 = (f32[2,64]{1,0:T(2,128)S(1)}, f32[2,64]{1,0:T(2,128)}, u32[]{:S(2)}) copy-start(f32[2,64]{1,0:T(2,128)} %biases.1) | copy-start | bytes 1540
  2.2 1.5 %collective-permute-start = (f32[2,2,2,8,128]{4,3,2,1,0:T(8,128)S(1)}, f32[2,2,2,8,128]{4,3,2,1,0:T(8,128)S(1)}, u32[]{:S(2)}, u32[]{:S(2)}) collective-permute-start(f32[2,2,2,8,128]{4,3,2,1,0:T(8,128)S(1)} %get-tuple-element.107), channel_id=1, source_target_pairs={{0,1},{1,0},{2,3},{3,2},{4,5},{5,4},{6,7},{7,6},{8,9},{9,8},{10,11... | collective-permute-start | bytes 98312 | tf_op jit(solution)/shard_map/ppermute | solution.py:418
  2.7 1.0 %collective-permute-start.1 = (f32[2,2,2,8,128]{4,3,2,1,0:T(8,128)S(1)}, f32[2,2,2,8,128]{4,3,2,1,0:T(8,128)S(1)}, u32[]{:S(2)}, u32[]{:S(2)}) collective-permute-start(f32[2,2,2,8,128]{4,3,2,1,0:T(8,128)S(1)} %get-tuple-element.106), channel_id=1, source_target_pairs={{1,2},{2,1},{5,6},{6,5},{9,10},{10,9},{13,14},{14,13},{17,18},{18,... | collective-permute-start | bytes 98312 | tf_op jit(solution)/shard_map/ppermute | solution.py:456
  3.8 14.6 %collective-permute-start.2 = (f32[14,64,128]{2,1,0:T(8,128)S(1)}, f32[14,64,128]{2,1,0:T(8,128)S(1)}, u32[]{:S(2)}, u32[]{:S(2)}) collective-permute-start(f32[14,64,128]{2,1,0:T(8,128)S(1)} %get-tuple-element.61), channel_id=1, source_target_pairs={{0,16},{16,0},{1,17},{17,1},{2,18},{18,2},{3,19},{19,3},{4,20},{20... | collective-permute-start | bytes 1376264 | tf_op jit(solution)/shard_map/ppermute | solution.py:422
  6.5 5.1 %collective-permute-start.3 = (f32[2,88,128]{2,1,0:T(8,128)S(1)}, f32[2,88,128]{2,1,0:T(8,128)S(1)}, u32[]{:S(2)}, u32[]{:S(2)}) collective-permute-start(f32[2,88,128]{2,1,0:T(8,128)S(1)} %get-tuple-element.63), channel_id=1, source_target_pairs={{0,4},{4,0},{8,12},{12,8},{1,5},{5,1},{9,13},{13,9},{2,6},{6,2},{1... | collective-permute-start | bytes 270344 | tf_op jit(solution)/shard_map/ppermute | solution.py:410
  8.1 6.5 %collective-permute-start.5 = (f32[2,88,128]{2,1,0:T(8,128)S(1)}, f32[2,88,128]{2,1,0:T(8,128)S(1)}, u32[]{:S(2)}, u32[]{:S(2)}) collective-permute-start(f32[2,88,128]{2,1,0:T(8,128)S(1)} %get-tuple-element.64), channel_id=1, source_target_pairs={{0,8},{4,12},{8,0},{12,4},{1,9},{5,13},{9,1},{13,5},{2,10},{6,14},... | collective-permute-start | bytes 270344 | tf_op jit(solution)/shard_map/ppermute | solution.py:410
  10.7 7.2 %collective-permute-start.6 = (f32[2,88,128]{2,1,0:T(8,128)S(1)}, f32[2,88,128]{2,1,0:T(8,128)S(1)}, u32[]{:S(2)}, u32[]{:S(2)}) collective-permute-start(f32[2,88,128]{2,1,0:T(8,128)S(1)} %get-tuple-element.65), channel_id=1, source_target_pairs={{0,12},{4,8},{8,4},{12,0},{1,13},{5,9},{9,5},{13,1},{2,14},{6,10},... | collective-permute-start | bytes 270344 | tf_op jit(solution)/shard_map/ppermute | solution.py:410
  11.7 6.8 %collective-permute-start.4 = (f32[2,48,128]{2,1,0:T(8,128)S(1)}, f32[2,48,128]{2,1,0:T(8,128)S(1)}, u32[]{:S(2)}, u32[]{:S(2)}) collective-permute-start(f32[2,48,128]{2,1,0:T(8,128)S(1)} %slice.128), channel_id=1, source_target_pairs={{0,16},{16,0},{1,17},{17,1},{2,18},{18,2},{3,19},{19,3},{4,20},{20... | collective-permute-start | bytes 147464 | tf_op jit(solution)/shard_map/ppermute | solution.py:422
  14.6 8.0 %collective-permute-start.8 = (f32[2,48,128]{2,1,0:T(8,128)S(1)}, f32[2,48,128]{2,1,0:T(8,128)S(1)}, u32[]{:S(2)}, u32[]{:S(2)}) collective-permute-start(f32[2,48,128]{2,1,0:T(8,128)S(1)} %slice.129), channel_id=1, source_target_pairs={{0,16},{16,0},{1,17},{17,1},{2,18},{18,2},{3,19},{19,3},{4,20},{20... | collective-permute-start | bytes 147464 | tf_op jit(solution)/shard_map/ppermute | solution.py:422
  17.9 4.8 %collective-permute-start.9 = (f32[2,48,128]{2,1,0:T(8,128)S(1)}, f32[2,48,128]{2,1,0:T(8,128)S(1)}, u32[]{:S(2)}, u32[]{:S(2)}) collective-permute-start(f32[2,48,128]{2,1,0:T(8,128)S(1)} %slice.130), channel_id=1, source_target_pairs={{0,16},{16,0},{1,17},{17,1},{2,18},{18,2},{3,19},{19,3},{4,20},{20... | collective-permute-start | bytes 147464 | tf_op jit(solution)/shard_map/ppermute | solution.py:422
  18.5 3.4 %collective-permute-start.7 = (f32[14,64,128]{2,1,0:T(8,128)S(1)}, f32[14,64,128]{2,1,0:T(8,128)S(1)}, u32[]{:S(2)}, u32[]{:S(2)}) collective-permute-start(f32[14,64,128]{2,1,0:T(8,128)S(1)} %collective-permute-done.2.refs_0_), channel_id=1, source_target_pairs={{0,1},{1,0},{2,3},{3,2},{4,5},{5,4},{6,7},{7,6},{8,9},{9,8},{10,11... | collective-permute-start | bytes 1376264 | tf_op jit(solution)/shard_map/ppermute | solution.py:418
  20.3 9.6 %collective-permute-start.10 = (f32[3,2,40,128]{3,2,1,0:T(8,128)S(1)}, f32[3,2,40,128]{3,2,1,0:T(8,128)S(1)}, u32[]{:S(2)}, u32[]{:S(2)}) collective-permute-start(f32[3,2,40,128]{3,2,1,0:T(8,128)S(1)} %pad_maximum_fusion.5), channel_id=1, source_target_pairs={{0,16},{16,0},{1,17},{17,1},{2,18},{18,2},{3,19},{19,3},{4,20},{20... | collective-permute-start | bytes 368648 | tf_op jit(solution)/shard_map/ppermute | solution.py:422
  27.2 9.5 %collective-permute-start.11 = (f32[2,2,2,32,128]{4,3,2,1,0:T(8,128)S(1)}, f32[2,2,2,32,128]{4,3,2,1,0:T(8,128)S(1)}, u32[]{:S(2)}, u32[]{:S(2)}) collective-permute-start(f32[2,2,2,32,128]{4,3,2,1,0:T(8,128)S(1)} %pad_maximum_fusion.4), channel_id=1, source_target_pairs={{0,8},{4,12},{8,0},{12,4},{1,9},{5,13},{9,1},{13,5},{2,10},{6,14},... | collective-permute-start | bytes 393224 | tf_op jit(solution)/shard_map/ppermute | solution.py:418
  36.7 1.6 %collective-permute-start.12 = (f32[448,128]{1,0:T(8,128)S(1)}, f32[448,128]{1,0:T(8,128)S(1)}, u32[]{:S(2)}, u32[]{:S(2)}) collective-permute-start(f32[448,128]{1,0:T(8,128)S(1)} %bitcast.49), channel_id=1, source_target_pairs={{0,1},{1,0},{2,3},{3,2},{4,5},{5,4},{6,7},{7,6},{8,9},{9,8},{10,11... | collective-permute-start | bytes 688136 | tf_op jit(solution)/shard_map/ppermute | solution.py:418
  36.8 1.8 %collective-permute-start.13 = (f32[448,128]{1,0:T(8,128)S(1)}, f32[448,128]{1,0:T(8,128)S(1)}, u32[]{:S(2)}, u32[]{:S(2)}) collective-permute-start(f32[448,128]{1,0:T(8,128)S(1)} %bitcast.48), channel_id=1, source_target_pairs={{0,1},{1,0},{2,3},{3,2},{4,5},{5,4},{6,7},{7,6},{8,9},{9,8},{10,11... | collective-permute-start | bytes 688136 | tf_op jit(solution)/shard_map/ppermute | solution.py:418
  38.7 9.2 %collective-permute-start.14 = (f32[224,128]{1,0:T(8,128)S(1)}, f32[224,128]{1,0:T(8,128)S(1)}, u32[]{:S(2)}, u32[]{:S(2)}) collective-permute-start(f32[224,128]{1,0:T(8,128)S(1)} %slice.139), channel_id=1, source_target_pairs={{0,2},{1,3},{2,0},{3,1},{4,6},{5,7},{6,4},{7,5},{8,10},{9,11},{10,... | collective-permute-start | bytes 344072 | tf_op jit(solution)/shard_map/ppermute | solution.py:418
  41.2 5.9 %collective-permute-start.19 = (f32[224,128]{1,0:T(8,128)S(1)}, f32[224,128]{1,0:T(8,128)S(1)}, u32[]{:S(2)}, u32[]{:S(2)}) collective-permute-start(f32[224,128]{1,0:T(8,128)S(1)} %slice.123), channel_id=1, source_target_pairs={{0,2},{1,3},{2,0},{3,1},{4,6},{5,7},{6,4},{7,5},{8,10},{9,11},{10,... | collective-permute-start | bytes 344072 | tf_op jit(solution)/shard_map/ppermute | solution.py:418
  41.3 13.5 %collective-permute-start.16 = (f32[3,2,2,32,128]{4,3,2,1,0:T(8,128)S(1)}, f32[3,2,2,32,128]{4,3,2,1,0:T(8,128)S(1)}, u32[]{:S(2)}, u32[]{:S(2)}) collective-permute-start(f32[3,2,2,32,128]{4,3,2,1,0:T(8,128)S(1)} %pad_maximum_fusion.3), channel_id=1, source_target_pairs={{0,4},{4,0},{8,12},{12,8},{1,5},{5,1},{9,13},{13,9},{2,6},{6,2},{1... | collective-permute-start | bytes 589832 | tf_op jit(solution)/shard_map/ppermute | solution.py:418
  42.3 12.4 %collective-permute-start.17 = (f32[2,2,32,128]{3,2,1,0:T(8,128)S(1)}, f32[2,2,32,128]{3,2,1,0:T(8,128)S(1)}, u32[]{:S(2)}, u32[]{:S(2)}) collective-permute-start(f32[2,2,32,128]{3,2,1,0:T(8,128)S(1)} %get-tuple-element.90), channel_id=1, source_target_pairs={{0,8},{4,12},{8,0},{12,4},{1,9},{5,13},{9,1},{13,5},{2,10},{6,14},... | collective-permute-start | bytes 196616 | tf_op jit(solution)/shard_map/ppermute | solution.py:418
  45.0 9.7 %collective-permute-start.18 = (f32[2,2,32,128]{3,2,1,0:T(8,128)S(1)}, f32[2,2,32,128]{3,2,1,0:T(8,128)S(1)}, u32[]{:S(2)}, u32[]{:S(2)}) collective-permute-start(f32[2,2,32,128]{3,2,1,0:T(8,128)S(1)} %get-tuple-element.91), channel_id=1, source_target_pairs={{0,12},{4,8},{8,4},{12,0},{1,13},{5,9},{9,5},{13,1},{2,14},{6,10},... | collective-permute-start | bytes 196616 | tf_op jit(solution)/shard_map/ppermute | solution.py:418
  47.1 5.0 %collective-permute-start.20 = (f32[112,128]{1,0:T(8,128)S(1)}, f32[112,128]{1,0:T(8,128)S(1)}, u32[]{:S(2)}, u32[]{:S(2)}) collective-permute-start(f32[112,128]{1,0:T(8,128)S(1)} %slice_select_fusion), channel_id=1, source_target_pairs={{0,4},{4,0},{8,12},{12,8},{1,5},{5,1},{9,13},{13,9},{2,6},{6,2},{1... | collective-permute-start | bytes 172040 | tf_op jit(solution)/shard_map/ppermute | solution.py:418
  47.9 6.8 %collective-permute-start.15 = (f32[112,128]{1,0:T(8,128)S(1)}, f32[112,128]{1,0:T(8,128)S(1)}, u32[]{:S(2)}, u32[]{:S(2)}) collective-permute-start(f32[112,128]{1,0:T(8,128)S(1)} %slice_select_fusion.1), channel_id=1, source_target_pairs={{0,4},{4,0},{8,12},{12,8},{1,5},{5,1},{9,13},{13,9},{2,6},{6,2},{1... | collective-permute-start | bytes 172040 | tf_op jit(solution)/shard_map/ppermute | solution.py:418
  52.1 6.5 %collective-permute-start.21 = (f32[112,128]{1,0:T(8,128)S(1)}, f32[112,128]{1,0:T(8,128)S(1)}, u32[]{:S(2)}, u32[]{:S(2)}) collective-permute-start(f32[112,128]{1,0:T(8,128)S(1)} %select_add_fusion), channel_id=1, source_target_pairs={{0,8},{4,12},{8,0},{12,4},{1,9},{5,13},{9,1},{13,5},{2,10},{6,14},... | collective-permute-start | bytes 172040 | tf_op jit(solution)/shard_map/ppermute | solution.py:418
  54.8 7.4 %collective-permute-start.25 = (f32[112,128]{1,0:T(8,128)S(1)}, f32[112,128]{1,0:T(8,128)S(1)}, u32[]{:S(2)}, u32[]{:S(2)}) collective-permute-start(f32[112,128]{1,0:T(8,128)S(1)} %select_add_fusion.1), channel_id=1, source_target_pairs={{0,8},{4,12},{8,0},{12,4},{1,9},{5,13},{9,1},{13,5},{2,10},{6,14},... | collective-permute-start | bytes 172040 | tf_op jit(solution)/shard_map/ppermute | solution.py:418
  58.6 5.5 %collective-permute-start.24 = (f32[112,128]{1,0:T(8,128)S(1)}, f32[112,128]{1,0:T(8,128)S(1)}, u32[]{:S(2)}, u32[]{:S(2)}) collective-permute-start(f32[112,128]{1,0:T(8,128)S(1)} %add.39), channel_id=1, source_target_pairs={{0,6},{1,7},{2,4},{3,5},{4,2},{5,3},{6,0},{7,1},{8,14},{9,15},{10,... | collective-permute-start | bytes 172040 | tf_op jit(solution)/shard_map/ppermute | solution.py:431
  59.6 6.2 %collective-permute-start.23 = (f32[112,128]{1,0:T(8,128)S(1)}, f32[112,128]{1,0:T(8,128)S(1)}, u32[]{:S(2)}, u32[]{:S(2)}) collective-permute-start(f32[112,128]{1,0:T(8,128)S(1)} %add.39), channel_id=1, source_target_pairs={{0,2},{1,3},{2,0},{3,1},{4,6},{5,7},{6,4},{7,5},{8,10},{9,11},{10,... | collective-permute-start | bytes 172040 | tf_op jit(solution)/shard_map/ppermute | solution.py:418
  60.6 5.2 %collective-permute-start.22 = (f32[112,128]{1,0:T(8,128)S(1)}, f32[112,128]{1,0:T(8,128)S(1)}, u32[]{:S(2)}, u32[]{:S(2)}) collective-permute-start(f32[112,128]{1,0:T(8,128)S(1)} %add.39), channel_id=1, source_target_pairs={{0,4},{4,0},{8,12},{12,8},{1,5},{5,1},{9,13},{13,9},{2,6},{6,2},{1... | collective-permute-start | bytes 172040 | tf_op jit(solution)/shard_map/ppermute | solution.py:418
  62.2 5.3 %collective-permute-start.28 = (f32[112,128]{1,0:T(8,128)S(1)}, f32[112,128]{1,0:T(8,128)S(1)}, u32[]{:S(2)}, u32[]{:S(2)}) collective-permute-start(f32[112,128]{1,0:T(8,128)S(1)} %add.40), channel_id=1, source_target_pairs={{0,6},{1,7},{2,4},{3,5},{4,2},{5,3},{6,0},{7,1},{8,14},{9,15},{10,... | collective-permute-start | bytes 172040 | tf_op jit(solution)/shard_map/ppermute | solution.py:431
  63.1 4.8 %collective-permute-start.27 = (f32[112,128]{1,0:T(8,128)S(1)}, f32[112,128]{1,0:T(8,128)S(1)}, u32[]{:S(2)}, u32[]{:S(2)}) collective-permute-start(f32[112,128]{1,0:T(8,128)S(1)} %add.40), channel_id=1, source_target_pairs={{0,2},{1,3},{2,0},{3,1},{4,6},{5,7},{6,4},{7,5},{8,10},{9,11},{10,... | collective-permute-start | bytes 172040 | tf_op jit(solution)/shard_map/ppermute | solution.py:418
  64.2 4.2 %collective-permute-start.26 = (f32[112,128]{1,0:T(8,128)S(1)}, f32[112,128]{1,0:T(8,128)S(1)}, u32[]{:S(2)}, u32[]{:S(2)}) collective-permute-start(f32[112,128]{1,0:T(8,128)S(1)} %add.40), channel_id=1, source_target_pairs={{0,4},{4,0},{8,12},{12,8},{1,5},{5,1},{9,13},{13,9},{2,6},{6,2},{1... | collective-permute-start | bytes 172040 | tf_op jit(solution)/shard_map/ppermute | solution.py:418
  65.8 3.7 %collective-permute-start.29 = (f32[448,128]{1,0:T(8,128)S(1)}, f32[448,128]{1,0:T(8,128)S(1)}, u32[]{:S(2)}, u32[]{:S(2)}) collective-permute-start(f32[448,128]{1,0:T(8,128)S(1)} %pad_maximum_fusion.1.refs_0_), channel_id=1, source_target_pairs={{0,1},{1,0},{2,3},{3,2},{4,5},{5,4},{6,7},{7,6},{8,9},{9,8},{10,11... | collective-permute-start | bytes 688136 | tf_op jit(solution)/shard_map/ppermute | solution.py:418
  68.4 1.6 %collective-permute-start.30 = (f32[448,128]{1,0:T(8,128)S(1)}, f32[448,128]{1,0:T(8,128)S(1)}, u32[]{:S(2)}, u32[]{:S(2)}) collective-permute-start(f32[448,128]{1,0:T(8,128)S(1)} %pad_maximum_fusion.2.refs_1_), channel_id=1, source_target_pairs={{0,1},{1,0},{2,3},{3,2},{4,5},{5,4},{6,7},{7,6},{8,9},{9,8},{10,11... | collective-permute-start | bytes 688136 | tf_op jit(solution)/shard_map/ppermute | solution.py:418
